TPU v7x, 32 devices: a whole 2x2x4 slice. The times are simulated.
32 devices in a mesh: dx: 2 (over y), dy: 16 (over z, x, core).
Axes of the slice: x: 2, y: 2, z: 4, core: 2. Of those that a mesh axis runs over, the one named last changes fastest.
Arguments:
- vectors: bfloat16 [2, 16, 256, 16, 128], P(None, 'dx', 'dy'), may hold values from -6 to 6
- resident: bfloat16 [16, 256, 16, 512], P('dx', 'dy'), may hold values from -6 to 6
- inv_mass: float32 [16, 256, 16], P('dx', 'dy'), may hold values from 0.26 to 1.3
- potential: float32 [16, 256, 16], P('dx', 'dy'), may hold values from -0.4 to 0.4
- cell_matrix: bfloat16 [729, 729], replicated, may hold values from -1 to 1.3, as said below
- connectivity: int32 [2, 16, 4, 729], P('dx', 'dy'), may hold values from 0 to 2447, as said below
Outputs:
- filtered: float32 [2, 16, 256, 16, 128], P(None, 'dx', 'dy')
- margin: float32 [512, 256], P('dy')
Inputs may be any that keep to these rules, and one draw needn't show every extreme that they name: `connectivity`: cell c of a device, with c = (cx * 2 + cy) * 2 + cz, covers the extended nodes with i from cx * 8 to cx * 8 + 8, j from cy * 8 to cy * 8 + 8, and k from cz * 8 to cz * 8 + 8 taken modulo 2 * 8; its 729 entries name each of these nodes once, in an order that may differ from cell to cell. `cell_matrix`: Symmetric.
All inputs are finite; a program needn't handle non-finite values.
Results may differ from a plain program's by a relative error of at most 0.0055.
Values may be sent and summed in bfloat16 or wider, within the bound.
No kernel may reach another device: no remote copies, remote signals or barrier semaphores. Data moves between devices by JAX's collectives and lax.ppermute only.
A program may use at most 64 MiB of HBM per device.

v0:
```python
import math

import jax
import jax.numpy as jnp
from jax import lax
from jax.sharding import PartitionSpec as P

BLOCKS = 2
DEGREE = 3


center_shift = 1.2
half_width = 2.0


def from_behind(value, axis, steps):
    count = lax.axis_size(axis)
    pairs = [(source, (source + steps) % count) for source in range(count)]
    return lax.ppermute(value, axis, pairs)


def body(vectors, resident, inv_mass, potential, cell_matrix, connectivity):
    node_index = connectivity.reshape(-1)
    cell_count = connectivity.shape[2]
    node_count = connectivity.shape[3]
    extent_x, extent_y, extent_z = inv_mass.shape
    ext_rows = (extent_x + 1) * (extent_y + 1) * extent_z
    total_nodes = extent_x * extent_y * extent_z * lax.axis_size("dx") * lax.axis_size("dy")
    norm_scale = 1.0 / math.sqrt(total_nodes)
    resident_rows = resident.reshape(-1, resident.shape[-1])
    res_count = resident.shape[-1]

    def apply_hamiltonian(values):
        vec_width = values.shape[-1]
        scaled = (values * inv_mass[..., None]).astype(jnp.bfloat16)
        upper_x = from_behind(scaled[:1], "dx", -1)
        grown = jnp.concatenate([scaled, upper_x], axis=0)
        upper_y = from_behind(grown[:, :1], "dy", -1)
        grown = jnp.concatenate([grown, upper_y], axis=1)
        picked = jnp.take(grown.reshape(-1, vec_width), node_index, axis=0).reshape(
            cell_count, node_count, vec_width
        )
        product = jnp.einsum("il,clw->ciw", cell_matrix, picked, preferred_element_type=jnp.float32)
        summed = jax.ops.segment_sum(
            product.reshape(-1, vec_width), node_index, num_segments=ext_rows
        )
        summed = summed.reshape(extent_x + 1, extent_y + 1, extent_z, vec_width)
        from_lower_y = from_behind(summed[:, extent_y:], "dy", 1)
        folded = summed[:, :extent_y].at[:, 0:1].add(from_lower_y)
        from_lower_x = from_behind(folded[extent_x:], "dx", 1)
        folded = folded[:extent_x].at[0:1].add(from_lower_x)
        return inv_mass[..., None] * folded + potential[..., None] * values

    stacked = jnp.concatenate([vectors[block_id] for block_id in range(BLOCKS)], axis=-1).astype(
        jnp.float32
    )
    image = apply_hamiltonian(stacked)
    older = stacked
    current = (image - center_shift * stacked) / half_width
    for degree_id in range(1, DEGREE):
        image = apply_hamiltonian(current)
        newer = 2.0 * (image - center_shift * current) / half_width - older
        older = current
        current = newer
    vec_width = current.shape[-1]
    rounded = current.astype(jnp.bfloat16).reshape(-1, vec_width)
    local = lax.dot_general(
        resident_rows, rounded, (((0,), (0,)), ((), ())), preferred_element_type=jnp.float32
    )
    local = local * norm_scale
    summed = lax.psum(local, ("dx", "dy"))
    owned = res_count // lax.axis_size("dy")
    margin = lax.dynamic_slice_in_dim(summed, lax.axis_index("dy") * owned, owned, 0)
    filtered = jnp.stack(jnp.split(current, BLOCKS, axis=-1))
    return (filtered, margin)


def solution(mesh):
    return jax.shard_map(
        body,
        mesh=mesh,
        in_specs=(
            P(None, "dx", "dy", None, None),
            P("dx", "dy", None, None),
            P("dx", "dy", None),
            P("dx", "dy", None),
            P(),
            P("dx", "dy", None, None),
        ),
        out_specs=(P(None, "dx", "dy", None, None), P("dy", None)),
        check_vma=False,
    )
```

profile of v0, /device:TPU:0, one launch (start us, length us, event | category | flops | bytes accessed | tf_op | source)
XLA Modules:
  0.0 358.0 jit_solution(12512269076755641155)
XLA Ops:
  7.2 1.5 slice_bitcast_fusion.3
  10.0 3.0 collective-permute-start
  13.1 3.4 collective-permute-done
  16.5 3.4 collective-permute-start.1
  21.9 1.4 pad_maximum_fusion.1
  23.3 9.7 %gather_fusion = bf16[2916,256]{1,0:T(8,128)(2,1)} fusion(bf16[2448,256]{1,0:T(8,128)(2,1)S(1)} %bitcast.42, s32[3072]{0:T(1024)} %pad_clamp_fusion), kind=kCustom, calls=%fused_computation.clone | custom fusion | bytes 2997648 | tf_op jit(solution)/shard_map/jit(_take)/gather | solution.py:40
  32.9 3.5 broadcast_select_fusion
  36.4 3.0 reshape.257
  39.4 4.4 %convolution_bitcast_fusion.2 = f32[4,729,256]{2,1,0:T(8,128)} fusion(bf16[4,729,256]{2,1,0:T(8,128)(2,1)} %reshape.257, bf16[729,729]{1,0:T(8,128)(2,1)S(1)} %copy-done.22), kind=kOutput, calls=%fused_computation.19 | convolution fusion | flops 1088391168 | bytes 5541858 | tf_op jit(solution)/shard_map/il,clw->ciw/dot_general | solution.py:43
  43.8 3.9 %reshape.296 = f32[2916,256]{1,0:T(8,128)} reshape(f32[4,729,256]{2,1,0:T(8,128)} %convolution_bitcast_fusion.2) | data formatting | bytes 5971968 | tf_op jit(solution)/shard_map/reshape | solution.py:45
  47.7 17.5 %scatter_custom_fusion = f32[2448,256]{1,0:T(8,128)} fusion(s32[2916]{0:T(1024)} %copy-done.20, f32[2916,256]{1,0:T(8,128)} %reshape.296, f32[]{:T(128)} %constant.157.clone.1), kind=kCustom, calls=%fused_computation.30 | custom fusion | flops 746496 | bytes 2507264 | tf_op jit(solution)/shard_map/scatter-add | solution.py:44
  66.1 1.9 slice.273
  68.0 5.4 %collective-permute-done.2 = f32[9,1,16,256]{3,2,1,0:T(8,128)S(1)} collective-permute-done((f32[9,1,16,256]{3,2,1,0:T(8,128)S(1)}, f32[9,1,16,256]{3,2,1,0:T(8,128)S(1)}, u32[]{:S(2)}, u32[]{:S(2)}) %collective-permute-start.2) | collective-permute-done | bytes 147488 | tf_op jit(solution)/shard_map/ppermute | solution.py:19
  74.4 1.6 collective-permute-start.3
  76.2 5.8 %collective-permute-done.3 = f32[1,16,16,256]{3,2,1,0:T(8,128)S(1)} collective-permute-done((f32[1,16,16,256]{3,2,1,0:T(8,128)S(1)}, f32[1,16,16,256]{3,2,1,0:T(8,128)S(1)}, u32[]{:S(2)}, u32[]{:S(2)}) %collective-permute-start.3) | collective-permute-done | bytes 262176 | tf_op jit(solution)/shard_map/ppermute | solution.py:19
  83.4 1.6 collective-permute-start.4
  85.0 3.4 collective-permute-done.4
  88.7 2.0 collective-permute-done.5
  90.9 9.5 %gather_fusion.1 = bf16[2916,256]{1,0:T(8,128)(2,1)} fusion(bf16[2448,256]{1,0:T(8,128)(2,1)S(1)} %bitcast.43, s32[3072]{0:T(1024)S(1)} %copy-done.19), kind=kCustom, calls=%fused_computation.1.clone | custom fusion | bytes 2997648 | tf_op jit(solution)/shard_map/jit(_take)/gather | solution.py:40
  100.4 3.5 broadcast_select_fusion.1
  103.9 3.1 reshape.261
  107.0 4.3 %convolution_bitcast_fusion.1 = f32[4,729,256]{2,1,0:T(8,128)} fusion(bf16[4,729,256]{2,1,0:T(8,128)(2,1)} %reshape.261, bf16[729,729]{1,0:T(8,128)(2,1)S(1)} %copy-done.23), kind=kOutput, calls=%fused_computation.18 | convolution fusion | flops 1088391168 | bytes 5541858 | tf_op jit(solution)/shard_map/il,clw->ciw/dot_general | solution.py:43
  111.3 3.9 %reshape.304 = f32[2916,256]{1,0:T(8,128)} reshape(f32[4,729,256]{2,1,0:T(8,128)} %convolution_bitcast_fusion.1) | data formatting | bytes 5971968 | tf_op jit(solution)/shard_map/reshape | solution.py:45
  115.2 17.4 %scatter_custom_fusion.1 = f32[2448,256]{1,0:T(8,128)} fusion(s32[2916]{0:T(1024)} %copy-done.20, f32[2916,256]{1,0:T(8,128)} %reshape.304, f32[]{:T(128)} %constant.157.clone.1), kind=kCustom, calls=%fused_computation.28 | custom fusion | flops 746496 | bytes 2507264 | tf_op jit(solution)/shard_map/scatter-add | solution.py:44
  133.6 1.9 slice.280
  135.5 5.4 %collective-permute-done.6 = f32[9,1,16,256]{3,2,1,0:T(8,128)S(1)} collective-permute-done((f32[9,1,16,256]{3,2,1,0:T(8,128)S(1)}, f32[9,1,16,256]{3,2,1,0:T(8,128)S(1)}, u32[]{:S(2)}, u32[]{:S(2)}) %collective-permute-start.6) | collective-permute-done | bytes 147488 | tf_op jit(solution)/shard_map/ppermute | solution.py:19
  141.9 1.6 collective-permute-start.7
  143.7 6.0 %collective-permute-done.7 = f32[1,16,16,256]{3,2,1,0:T(8,128)S(1)} collective-permute-done((f32[1,16,16,256]{3,2,1,0:T(8,128)S(1)}, f32[1,16,16,256]{3,2,1,0:T(8,128)S(1)}, u32[]{:S(2)}, u32[]{:S(2)}) %collective-permute-start.7) | collective-permute-done | bytes 262176 | tf_op jit(solution)/shard_map/ppermute | solution.py:19
  151.0 1.6 collective-permute-start.8
  152.6 3.4 collective-permute-done.8
  156.4 2.0 collective-permute-done.9
  158.5 9.7 %gather_fusion.2 = bf16[2916,256]{1,0:T(8,128)(2,1)} fusion(bf16[2448,256]{1,0:T(8,128)(2,1)S(1)} %bitcast.41, s32[3072]{0:T(1024)} %pad_clamp_fusion), kind=kCustom, calls=%fused_computation.2.clone | custom fusion | bytes 2997648 | tf_op jit(solution)/shard_map/jit(_take)/gather | solution.py:40
  168.2 3.5 broadcast_select_fusion.2
  171.7 3.0 reshape.265
  174.7 4.3 %convolution_bitcast_fusion = f32[4,729,256]{2,1,0:T(8,128)} fusion(bf16[4,729,256]{2,1,0:T(8,128)(2,1)} %reshape.265, bf16[729,729]{1,0:T(8,128)(2,1)S(1)} %copy-done.24), kind=kOutput, calls=%fused_computation.17 | convolution fusion | flops 1088391168 | bytes 5541858 | tf_op jit(solution)/shard_map/il,clw->ciw/dot_general | solution.py:43
  179.0 4.0 %reshape.312 = f32[2916,256]{1,0:T(8,128)} reshape(f32[4,729,256]{2,1,0:T(8,128)} %convolution_bitcast_fusion) | data formatting | bytes 5971968 | tf_op jit(solution)/shard_map/reshape | solution.py:45
  183.0 17.5 %scatter_custom_fusion.2 = f32[2448,256]{1,0:T(8,128)} fusion(s32[2916]{0:T(1024)} %copy-done.20, f32[2916,256]{1,0:T(8,128)} %reshape.312, f32[]{:T(128)} %constant.157.clone.1), kind=kCustom, calls=%fused_computation.26 | custom fusion | flops 746496 | bytes 2507264 | tf_op jit(solution)/shard_map/scatter-add | solution.py:44
  201.4 1.9 slice.287
  203.3 5.4 %collective-permute-done.10 = f32[9,1,16,256]{3,2,1,0:T(8,128)S(1)} collective-permute-done((f32[9,1,16,256]{3,2,1,0:T(8,128)S(1)}, f32[9,1,16,256]{3,2,1,0:T(8,128)S(1)}, u32[]{:S(2)}, u32[]{:S(2)}) %collective-permute-start.10) | collective-permute-done | bytes 147488 | tf_op jit(solution)/shard_map/ppermute | solution.py:19
  209.7 1.4 copy-done.14
  211.1 1.6 collective-permute-start.11
  212.7 2.0 slice.290
  214.7 2.9 collective-permute-done.11
  218.6 1.7 multiply_subtract_fusion
  221.6 1.5 fusion.10
  223.2 1.7 slice_bitcast_fusion.1
  224.8 1.5 pad_maximum_fusion
  226.3 123.1 %all-reduce.2.cloned.1.call-done = f32[512,256]{0,1:T(8,128)} async-done(((f32[512,256]{0,1:T(8,128)}), f32[512,256]{0,1:T(8,128)}) %all-reduce.2.cloned.1.call-update) | async-done | bytes 524304 | tf_op jit(solution)/shard_map/psum | solution.py:71
  (90 shorter events, 17.1 us)
Async XLA Ops:
  7.2 214.4 %copy-start = (bf16[8,16,16,512]{3,2,1,0:T(8,128)(2,1)S(1)}, bf16[8,16,16,512]{3,2,1,0:T(8,128)(2,1)}, u32[]{:S(2)}) copy-start(bf16[8,16,16,512]{3,2,1,0:T(8,128)(2,1)} %param.21) | copy-start | bytes 6291460
  7.2 2.4 copy-start.17
  7.2 5.8 %copy-start.21 = (s32[1,1,4,729]{3,2,1,0:T(4,128)S(1)}, s32[1,1,4,729]{3,2,1,0:T(4,128)}, u32[]{:S(2)}) copy-start(s32[1,1,4,729]{3,2,1,0:T(4,128)} %param.25) | copy-start | bytes 34996
  7.2 342.2 %all-reduce.2.cloned.1.call-start = ((), (), s32[]{:S(2)}) async-start(), calls=%async_computation | async-start | bytes 1048576 | tf_op jit(solution)/shard_map/psum | solution.py:71
  8.8 0.8 copy-start.6
  8.8 1.2 copy-start.10
  10.0 10.6 %copy-start.15 = (bf16[8,16,16,256]{3,2,1,0:T(8,128)(2,1)}, bf16[8,16,16,256]{3,2,1,0:T(8,128)(2,1)S(1)}, u32[]{:S(2)}) copy-start(bf16[8,16,16,256]{3,2,1,0:T(8,128)(2,1)S(1)} %fusion) | copy-start | bytes 3145732
  10.0 6.5 %collective-permute-start = (bf16[1,16,16,256]{3,2,1,0:T(8,128)(2,1)S(1)}, bf16[1,16,16,256]{3,2,1,0:T(8,128)(2,1)S(1)}, u32[]{:S(2)}, u32[]{:S(2)}) collective-permute-start(bf16[1,16,16,256]{3,2,1,0:T(8,128)(2,1)S(1)} %slice.272), channel_id=1, source_target_pairs={{0,16},{16,0},{1,17},{17,1},{2,18},{18,2},{3,19},{19,3},{4,20},{20... | collective-permute-start | bytes 393224 | tf_op jit(solution)/shard_map/ppermute | solution.py:19
  13.1 7.4 %copy-start.20 = (s32[2916]{0:T(1024)}, s32[2916]{0:T(1024)S(1)}, u32[]{:S(2)}) copy-start(s32[2916]{0:T(1024)S(1)} %reshape.310) | copy-start | bytes 34996
  16.5 5.4 %collective-permute-start.1 = (bf16[9,1,16,256]{3,2,1,0:T(8,128)(2,1)S(1)}, bf16[9,1,16,256]{3,2,1,0:T(8,128)(2,1)S(1)}, u32[]{:S(2)}, u32[]{:S(2)}) collective-permute-start(bf16[9,1,16,256]{3,2,1,0:T(8,128)(2,1)S(1)} %pad_maximum_fusion.7), channel_id=1, source_target_pairs={{0,15},{1,0},{2,1},{3,2},{4,3},{5,4},{6,5},{7,6},{8,7},{9,8},{10,9... | collective-permute-start | bytes 221192 | tf_op jit(solution)/shard_map/ppermute | solution.py:19
  36.4 3.0 copy-start.22
  66.1 7.4 %collective-permute-start.2 = (f32[9,1,16,256]{3,2,1,0:T(8,128)S(1)}, f32[9,1,16,256]{3,2,1,0:T(8,128)S(1)}, u32[]{:S(2)}, u32[]{:S(2)}) collective-permute-start(f32[9,1,16,256]{3,2,1,0:T(8,128)S(1)} %slice.275), channel_id=1, source_target_pairs={{0,1},{1,2},{2,3},{3,4},{4,5},{5,6},{6,7},{7,8},{8,9},{9,10},{10,1... | collective-permute-start | bytes 442376 | tf_op jit(solution)/shard_map/ppermute | solution.py:19
  74.4 7.6 %collective-permute-start.3 = (f32[1,16,16,256]{3,2,1,0:T(8,128)S(1)}, f32[1,16,16,256]{3,2,1,0:T(8,128)S(1)}, u32[]{:S(2)}, u32[]{:S(2)}) collective-permute-start(f32[1,16,16,256]{3,2,1,0:T(8,128)S(1)} %slice.278), channel_id=1, source_target_pairs={{0,16},{16,0},{1,17},{17,1},{2,18},{18,2},{3,19},{19,3},{4,20},{20... | collective-permute-start | bytes 786440 | tf_op jit(solution)/shard_map/ppermute | solution.py:19
  76.0 6.1 %copy-start.7 = (bf16[8,16,16,128]{3,2,1,0:T(8,128)(2,1)S(1)}, bf16[8,16,16,128]{3,2,1,0:T(8,128)(2,1)}, u32[]{:S(2)}) copy-start(bf16[8,16,16,128]{3,2,1,0:T(8,128)(2,1)} %copy-done.6) | copy-start | bytes 1572868
  76.0 6.1 %copy-start.11 = (bf16[8,16,16,128]{3,2,1,0:T(8,128)(2,1)S(1)}, bf16[8,16,16,128]{3,2,1,0:T(8,128)(2,1)}, u32[]{:S(2)}) copy-start(bf16[8,16,16,128]{3,2,1,0:T(8,128)(2,1)} %copy-done.10) | copy-start | bytes 1572868
  76.0 6.1 %copy-start.18 = (f32[8,16,16]{2,1,0:T(8,128)S(1)}, f32[8,16,16]{2,1,0:T(8,128)}, u32[]{:S(2)}) copy-start(f32[8,16,16]{2,1,0:T(8,128)} %param.23) | copy-start | bytes 24580
  82.1 1.3 copy-start.1
  83.4 7.4 %copy-start.19 = (s32[3072]{0:T(1024)S(1)}, s32[3072]{0:T(1024)}, u32[]{:S(2)}) copy-start(s32[3072]{0:T(1024)} %pad_clamp_fusion) | copy-start | bytes 36868
  83.4 5.0 %collective-permute-start.4 = (bf16[1,16,16,256]{3,2,1,0:T(8,128)(2,1)S(1)}, bf16[1,16,16,256]{3,2,1,0:T(8,128)(2,1)S(1)}, u32[]{:S(2)}, u32[]{:S(2)}) collective-permute-start(bf16[1,16,16,256]{3,2,1,0:T(8,128)(2,1)S(1)} %slice.279), channel_id=1, source_target_pairs={{0,16},{16,0},{1,17},{17,1},{2,18},{18,2},{3,19},{19,3},{4,20},{20... | collective-permute-start | bytes 393224 | tf_op jit(solution)/shard_map/ppermute | solution.py:19
  88.5 2.2 collective-permute-start.5
  103.9 3.1 copy-start.23
  133.6 7.4 %collective-permute-start.6 = (f32[9,1,16,256]{3,2,1,0:T(8,128)S(1)}, f32[9,1,16,256]{3,2,1,0:T(8,128)S(1)}, u32[]{:S(2)}, u32[]{:S(2)}) collective-permute-start(f32[9,1,16,256]{3,2,1,0:T(8,128)S(1)} %slice.282), channel_id=1, source_target_pairs={{0,1},{1,2},{2,3},{3,4},{4,5},{5,6},{6,7},{7,8},{8,9},{9,10},{10,1... | collective-permute-start | bytes 442376 | tf_op jit(solution)/shard_map/ppermute | solution.py:19
  141.9 7.8 %collective-permute-start.7 = (f32[1,16,16,256]{3,2,1,0:T(8,128)S(1)}, f32[1,16,16,256]{3,2,1,0:T(8,128)S(1)}, u32[]{:S(2)}, u32[]{:S(2)}) collective-permute-start(f32[1,16,16,256]{3,2,1,0:T(8,128)S(1)} %slice.285), channel_id=1, source_target_pairs={{0,16},{16,0},{1,17},{17,1},{2,18},{18,2},{3,19},{19,3},{4,20},{20... | collective-permute-start | bytes 786440 | tf_op jit(solution)/shard_map/ppermute | solution.py:19
  143.5 6.2 %copy-start.2 = (f32[8,16,16,256]{3,2,1,0:T(8,128)S(1)}, f32[8,16,16,256]{3,2,1,0:T(8,128)}, u32[]{:S(2)}) copy-start(f32[8,16,16,256]{3,2,1,0:T(8,128)} %copy-done.1) | copy-start | bytes 6291460
  143.5 6.2 %copy-start.8 = (bf16[8,16,16,128]{3,2,1,0:T(8,128)(2,1)S(1)}, bf16[8,16,16,128]{3,2,1,0:T(8,128)(2,1)}, u32[]{:S(2)}) copy-start(bf16[8,16,16,128]{3,2,1,0:T(8,128)(2,1)} %copy-done.6) | copy-start | bytes 1572868
  143.5 6.2 %copy-start.12 = (bf16[8,16,16,128]{3,2,1,0:T(8,128)(2,1)S(1)}, bf16[8,16,16,128]{3,2,1,0:T(8,128)(2,1)}, u32[]{:S(2)}) copy-start(bf16[8,16,16,128]{3,2,1,0:T(8,128)(2,1)} %copy-done.10) | copy-start | bytes 1572868
  149.7 1.3 copy-start.4
  151.0 5.0 %collective-permute-start.8 = (bf16[1,16,16,256]{3,2,1,0:T(8,128)(2,1)S(1)}, bf16[1,16,16,256]{3,2,1,0:T(8,128)(2,1)S(1)}, u32[]{:S(2)}, u32[]{:S(2)}) collective-permute-start(bf16[1,16,16,256]{3,2,1,0:T(8,128)(2,1)S(1)} %slice.286), channel_id=1, source_target_pairs={{0,16},{16,0},{1,17},{17,1},{2,18},{18,2},{3,19},{19,3},{4,20},{20... | collective-permute-start | bytes 393224 | tf_op jit(solution)/shard_map/ppermute | solution.py:19
  156.1 2.3 collective-permute-start.9
  171.7 3.0 copy-start.24
  201.3 7.4 %collective-permute-start.10 = (f32[9,1,16,256]{3,2,1,0:T(8,128)S(1)}, f32[9,1,16,256]{3,2,1,0:T(8,128)S(1)}, u32[]{:S(2)}, u32[]{:S(2)}) collective-permute-start(f32[9,1,16,256]{3,2,1,0:T(8,128)S(1)} %slice.289), channel_id=1, source_target_pairs={{0,1},{1,2},{2,3},{3,4},{4,5},{5,6},{6,7},{7,8},{8,9},{9,10},{10,1... | collective-permute-start | bytes 442376 | tf_op jit(solution)/shard_map/ppermute | solution.py:19
  209.7 1.4 copy-start.14
  211.1 7.5 %copy-start.13 = (bf16[8,16,16,128]{3,2,1,0:T(8,128)(2,1)S(1)}, bf16[8,16,16,128]{3,2,1,0:T(8,128)(2,1)}, u32[]{:S(2)}) copy-start(bf16[8,16,16,128]{3,2,1,0:T(8,128)(2,1)} %copy-done.10) | copy-start | bytes 1572868
  211.1 6.4 %collective-permute-start.11 = (f32[1,16,16,256]{3,2,1,0:T(8,128)S(1)}, f32[1,16,16,256]{3,2,1,0:T(8,128)S(1)}, u32[]{:S(2)}, u32[]{:S(2)}) collective-permute-start(f32[1,16,16,256]{3,2,1,0:T(8,128)S(1)} %slice.292), channel_id=1, source_target_pairs={{0,16},{16,0},{1,17},{17,1},{2,18},{18,2},{3,19},{19,3},{4,20},{20... | collective-permute-start | bytes 786440 | tf_op jit(solution)/shard_map/ppermute | solution.py:19
  212.7 5.8 %copy-start.3 = (f32[8,16,16,256]{3,2,1,0:T(8,128)S(1)}, f32[8,16,16,256]{3,2,1,0:T(8,128)}, u32[]{:S(2)}) copy-start(f32[8,16,16,256]{3,2,1,0:T(8,128)} %copy-done.1) | copy-start | bytes 6291460
  212.7 5.9 %copy-start.5 = (f32[8,16,16,256]{3,2,1,0:T(8,128)S(1)}, f32[8,16,16,256]{3,2,1,0:T(8,128)}, u32[]{:S(2)}) copy-start(f32[8,16,16,256]{3,2,1,0:T(8,128)} %copy-done.4) | copy-start | bytes 6291460
  212.7 5.9 %copy-start.9 = (bf16[8,16,16,128]{3,2,1,0:T(8,128)(2,1)S(1)}, bf16[8,16,16,128]{3,2,1,0:T(8,128)(2,1)}, u32[]{:S(2)}) copy-start(bf16[8,16,16,128]{3,2,1,0:T(8,128)(2,1)} %copy-done.6) | copy-start | bytes 1572868
  220.3 1.3 copy-start.16
Sparse Core Ops, SparseCore 0:
  223.3 126.0 all-reduce.1
where the time goes:
time: 359 us; the launch traced here: 358 us
  waiting for transfers between devices  170 us (47%)
  other arithmetic  74.7 us (21%)
  local copies, waits for them, and re-layouts  69.4 us (19%)
  starting transfers between devices  15.1 us (4%)
  matrix products  14.6 us (4%)
  between operations  14.5 us (4%)
    psum x1, waiting for transfers between devices, body(): summed = lax.psum(local, ('dx', 'dy'))  123 us
    scatter-add x3, other arithmetic, apply_hamiltonian(): jax.ops.segment_sum(product.reshape(-1, vec_width), node_index, num_segme...  52.4 us
    ppermute x12, waiting for transfers between devices, from_behind(): return lax.ppermute(value, axis, pairs)  46.5 us
    gather x3, local copies, waits for them, and re-layouts, apply_hamiltonian(): jnp.take(grown.reshape(-1, vec_width), node_index, axis=0)  28.9 us
    ppermute x12, starting transfers between devices, from_behind(): return lax.ppermute(value, axis, pairs)  15 us
    dot_general x3, matrix products, apply_hamiltonian(): jnp.einsum('il,clw->ciw', cell_matrix, picked, preferred_element_type=jnp...  13 us
    reshape x3, local copies, waits for them, and re-layouts, apply_hamiltonian(): product.reshape(-1, vec_width)  11.7 us
    select_n x4, other arithmetic, apply_hamiltonian(): jnp.take(grown.reshape(-1, vec_width), node_index, axis=0)  10.5 us
  transfers between devices with their start and end apart: 13, of which 13 were waited for; matrix products, arithmetic and copies ran while one was open for 3% of the time, Pallas kernels for 0%

commit v1 on v0

v1 whole, which is shorter than its diff:
```python
import functools
import math

import jax
import jax.numpy as jnp
from jax import lax
from jax.experimental import pallas as pl
from jax.experimental.pallas import tpu as pltpu
from jax.sharding import PartitionSpec as P

LANES = 128
SUB = 16
VMEM_LIMIT = 40 * 1024 * 1024

center_shift = 1.2
half_width = 2.0


def round_up(value, step):
    return -(-value // step) * step


class Sizes:
    def __init__(self, vectors, inv_mass, connectivity):
        self.blocks = vectors.shape[0]
        self.width = vectors.shape[-1]
        self.full = self.blocks * self.width
        self.ex, self.ey, self.ez = inv_mass.shape
        self.cells, self.nodes = connectivity.shape[2:]
        self.n1 = round(self.nodes ** (1.0 / 3.0))
        self.p = self.n1 - 1
        self.cx, self.cy, self.cz = self.ex // self.p, self.ey // self.p, self.ez // self.p
        self.gx, self.gy, self.gz = self.ex + 1, self.ey + 1, self.ez
        self.main = self.n1 * self.n1 * self.p
        self.rows = round_up(self.nodes, SUB)
        self.depth = round_up(self.nodes, LANES)
        self.ext = (self.blocks, self.gx, self.gy, self.gz, self.width)
        self.own = (self.blocks, self.ex, self.ey, self.ez, self.width)

    def cell_origins(self):
        for a in range(self.cx):
            for b in range(self.cy):
                for c in range(self.cz):
                    yield a * self.p, b * self.p, c * self.p


def send(value, steps_x, steps_y):
    nx, ny = lax.axis_size("dx"), lax.axis_size("dy")
    pairs = [
        (a * ny + b, ((a + steps_x) % nx) * ny + (b + steps_y) % ny)
        for a in range(nx)
        for b in range(ny)
    ]
    return lax.ppermute(value, ("dx", "dy"), pairs)


def swap_x(value):
    if lax.axis_size("dx") == 2:
        return send(value, 1, 0)
    return jnp.stack([send(value[0], -1, 0), send(value[1], 1, 0)])


def swap_y(near, far):
    ny = lax.axis_size("dy")
    near_pairs = [(b, b + 1 if b % 2 == 0 else b - 1) for b in range(ny)]
    far_pairs = [(b, (b - 1 if b % 2 == 0 else b + 1) % ny) for b in range(ny)]
    far = lax.ppermute(far, "dy", far_pairs)
    near = lax.ppermute(near, "dy", near_pairs)
    return near, far


def order_kernel(sz, origins, conn_ref, matrix_ref, out_ref):
    f32, bf16 = jnp.float32, jnp.bfloat16
    for cell, (x0, y0, z0) in enumerate(origins):
        conn = conn_ref[cell].astype(f32)
        li = jnp.floor((conn + 0.5) * (1.0 / (sz.gy * sz.gz)))
        rest = conn - li * (sz.gy * sz.gz)
        lj = jnp.floor((rest + 0.5) * (1.0 / sz.gz))
        lk = rest - lj * sz.gz - z0
        lk = jnp.where(lk < 0, lk + sz.gz, lk)
        column = (li - x0) * sz.n1 + (lj - y0)
        index = jnp.where(lk < sz.p, column * sz.p + lk, sz.main + column).astype(jnp.int32)
        place = lax.broadcasted_iota(jnp.int32, (sz.depth, sz.nodes), 0)
        pick = (place == index).astype(f32).astype(bf16)
        half = jnp.dot(pick[: sz.rows], matrix_ref[...], preferred_element_type=f32)
        whole = lax.dot_general(
            half.astype(bf16), pick, (((1,), (1,)), ((), ())), preferred_element_type=f32
        )
        out_ref[cell] = whole.astype(bf16)


def cell_products(sz, u_ref, mat_refs, rhs_ref, edge_ref, acc_ref):
    n1, p, width = sz.n1, sz.p, sz.width
    flat = sz.gx * sz.gy * sz.gz
    u_flat = u_ref.reshape(sz.blocks * flat, width)
    acc_flat = acc_ref.reshape(sz.blocks * flat, width)
    acc_ref[...] = jnp.zeros_like(acc_ref)
    tail = sz.nodes // 8 * 8
    rhs_ref[tail:, :] = jnp.zeros((sz.depth - tail, sz.full), jnp.float32)
    matrices = [ref.at[c] for ref in mat_refs for c in range(ref.shape[0])]
    for matrix, (x0, y0, z0) in zip(matrices, sz.cell_origins()):
        x1, y1, z1 = x0 + n1, y0 + n1, z0 + p
        wrap = z1 % sz.gz
        edges = []
        for b in range(sz.blocks):
            lanes = slice(b * width, (b + 1) * width)
            rhs_ref[: sz.main, lanes] = u_ref[b, x0:x1, y0:y1, z0:z1].reshape(sz.main, width)
            for i in range(n1):
                start = b * flat + ((x0 + i) * sz.gy + y0) * sz.gz + wrap
                edge = slice(i * n1, (i + 1) * n1)
                edges.append((pl.ds(start, n1, stride=sz.gz), edge, lanes))
        for rows, edge, lanes in edges:
            rhs_ref[sz.main + edge.start : sz.main + edge.stop, lanes] = u_flat[rows]
        product = jnp.dot(
            matrix[...], rhs_ref[...].astype(jnp.bfloat16), preferred_element_type=jnp.float32
        )
        for b in range(sz.blocks):
            lanes = slice(b * width, (b + 1) * width)
            acc_ref[b, x0:x1, y0:y1, z0:z1] += product[: sz.main, lanes].reshape(n1, n1, p, width)
        edge_ref[...] = product[sz.main :]
        for rows, edge, lanes in edges:
            acc_flat[rows] = acc_flat[rows] + edge_ref[edge, lanes]


def write_messages(sz, even, acc_ref, corner, face, side):
    end_x, end_y = sz.gx - 1, sz.gy - 1
    near = jnp.where(even, end_y, 0)
    for slot, j in enumerate((near, end_y - near)):
        for b in range(sz.blocks):
            corner[0, slot, b] = acc_ref[b, 0, j].astype(corner.dtype)
            corner[1, slot, b] = acc_ref[b, end_x, j].astype(corner.dtype)
            side[slot, b] = acc_ref[b, :, j]
    for b in range(sz.blocks):
        face[0, b] = acc_ref[b, 0, 1:end_y].astype(face.dtype)
        face[1, b] = acc_ref[b, end_x, 1:end_y].astype(face.dtype)


def side_kernel(sz, side_ref, corner_ref, near_ref, far_ref):
    for slot, out in enumerate((near_ref, far_ref)):
        for i in range(sz.gx):
            value = side_ref[slot, :, i]
            if i == 0:
                value = value + corner_ref[1, slot].astype(jnp.float32)
            if i == sz.gx - 1:
                value = value + corner_ref[0, slot].astype(jnp.float32)
            out[:, i] = value.astype(out.dtype)


def summed_at(sz, even, i, j, acc_ref, corner, face, near, far):
    f32 = jnp.float32
    total = acc_ref[:, i, j]
    end_x, end_y = sz.gx - 1, sz.gy - 1
    side = 1 if i == 0 else 0 if i == end_x else None
    if j in (0, end_y):
        is_near = even if j == end_y else jnp.logical_not(even)
        if side is not None:
            total = total + jnp.where(
                is_near, corner[side, 0].astype(f32), corner[side, 1].astype(f32)
            )
        total = total + jnp.where(is_near, near[:, i].astype(f32), far[:, i].astype(f32))
    elif side is not None:
        total = total + face[side, :, j - 1].astype(f32)
    return total


def first_kernel(
    sz, n_mat, even_ref, vec_ref, from_x, from_y, own_inv, own_pot, *refs
):
    mats = refs[:n_mat]
    x_ref, inv_ref, pot_ref, acc_ref, corner, face, side, u_ref, rhs_ref, edge_ref = refs[n_mat:]
    even = even_ref[0] == 0
    inv_ref[: sz.ex, : sz.ey] = own_inv[...]
    pot_ref[: sz.ex, : sz.ey] = own_pot[...]

    def fields(parts):
        parts = parts.astype(jnp.float32)
        for at, ref in enumerate((inv_ref, pot_ref)):
            total = sum(parts[..., 3 * at + k : 3 * at + k + 1] for k in range(3))
            yield ref, jnp.broadcast_to(total, parts.shape)

    for j in range(sz.ey):
        for ref, value in fields(from_x[sz.blocks, j]):
            ref[sz.ex, j] = value
    for i in range(sz.gx):
        for ref, value in fields(from_y[sz.blocks, i]):
            ref[i, sz.ey] = value
    x_ref[:, : sz.ex, : sz.ey] = vec_ref[...]
    x_ref[:, sz.ex, : sz.ey] = from_x[: sz.blocks]
    x_ref[:, :, sz.ey] = from_y[: sz.blocks]
    for i in range(sz.gx):
        for j in range(sz.gy):
            u_ref[:, i, j] = x_ref[:, i, j].astype(jnp.float32) * inv_ref[i, j]
    cell_products(sz, u_ref, mats, rhs_ref, edge_ref, acc_ref)
    write_messages(sz, even, acc_ref, corner, face, side)


def second_kernel(
    sz, n_mat, even_ref, x_ref, sum_ref, corner_in, face_in, near_in, far_in, inv_ref, pot_ref, *refs
):
    mats = refs[:n_mat]
    y_ref, acc_ref, corner, face, side, u_ref, rhs_ref, edge_ref = refs[n_mat:]
    even = even_ref[0] == 0
    for i in range(sz.gx):
        for j in range(sz.gy):
            total = summed_at(sz, even, i, j, sum_ref, corner_in, face_in, near_in, far_in)
            old = x_ref[:, i, j].astype(jnp.float32)
            inv = inv_ref[i, j]
            image = inv * total + pot_ref[i, j] * old
            new = (image - center_shift * old) / half_width
            y_ref[:, i, j] = new
            u_ref[:, i, j] = inv * new
    cell_products(sz, u_ref, mats, rhs_ref, edge_ref, acc_ref)
    write_messages(sz, even, acc_ref, corner, face, side)


def third_kernel(
    sz, n_mat, even_ref, x_ref, y_ref, sum_ref, corner_in, face_in, near_in, far_in, inv_ref, pot_ref,
    *refs,
):
    mats = refs[:n_mat]
    part_ref, corner, face, side, new_ref, acc_ref, u_ref, rhs_ref, edge_ref = refs[n_mat:]
    even = even_ref[0] == 0
    for i in range(sz.gx):
        for j in range(sz.gy):
            total = summed_at(sz, even, i, j, sum_ref, corner_in, face_in, near_in, far_in)
            old = y_ref[:, i, j]
            inv = inv_ref[i, j]
            image = inv * total + pot_ref[i, j] * old
            new = 2.0 * (image - center_shift * old) / half_width - x_ref[:, i, j].astype(jnp.float32)
            new_ref[:, i, j] = new
            u_ref[:, i, j] = inv * new
    cell_products(sz, u_ref, mats, rhs_ref, edge_ref, acc_ref)
    corner[...] = acc_ref[:, sz.ex, sz.ey].astype(corner.dtype)
    face[...] = acc_ref[:, sz.ex, : sz.ey].astype(face.dtype)
    side[...] = acc_ref[:, : sz.ex, sz.ey].astype(side.dtype)
    for i in range(sz.ex):
        for j in range(sz.ey):
            new = new_ref[:, i, j]
            image = inv_ref[i, j] * acc_ref[:, i, j] + pot_ref[i, j] * new
            part_ref[:, i, j] = 2.0 * (image - center_shift * new) / half_width - y_ref[:, i, j]


def last_side_kernel(sz, side_ref, corner_ref, out_ref):
    for i in range(sz.ex):
        value = side_ref[:, i]
        if i == 0:
            value = value + corner_ref[...].astype(jnp.float32)
        out_ref[:, i] = value.astype(out_ref.dtype)


def last_kernel(sz, part_ref, face, side, inv_ref, out_ref, rounded_ref):
    gain = 2.0 / half_width
    for i in range(sz.ex):
        for j in range(sz.ey):
            value = part_ref[:, i, j]
            more = None
            if i == 0:
                more = face[:, j].astype(jnp.float32)
            if j == 0:
                term = side[:, i].astype(jnp.float32)
                more = term if more is None else more + term
            if more is not None:
                value = value + gain * (inv_ref[i, j] * more)
            for b in range(sz.blocks):
                lanes = slice(b * sz.width, (b + 1) * sz.width)
                rounded_ref[i, j, :, lanes] = value[b].astype(jnp.bfloat16)
            out_ref[:, i, j] = value


def call(kernel, name, flops, out_shape, scratch, operands, scalar_first=False):
    size = sum(math.prod(s.shape) * jnp.dtype(s.dtype).itemsize for s in (*operands, *out_shape))
    whole = pl.BlockSpec(memory_space=pltpu.VMEM)
    specs = [whole] * len(operands)
    if scalar_first:
        specs[0] = pl.BlockSpec(memory_space=pltpu.SMEM)
    return pl.pallas_call(
        kernel,
        in_specs=specs,
        out_specs=[whole] * len(out_shape),
        out_shape=out_shape,
        scratch_shapes=scratch,
        compiler_params=pltpu.CompilerParams(vmem_limit_bytes=VMEM_LIMIT),
        cost_estimate=pl.CostEstimate(flops=flops, bytes_accessed=size, transcendentals=0),
        name=name,
    )(*operands)


def field_parts(fields, width):
    parts = []
    for at in range(fields.shape[0]):
        rest = fields[at]
        for _ in range(3):
            part = lax.reduce_precision(rest, 8, 7)
            rest = rest - part
            parts.append(part.astype(jnp.bfloat16))
    stacked = jnp.stack(parts, axis=-1)
    pads = [(0, 0)] * (stacked.ndim - 1) + [(0, width - len(parts))]
    return jnp.pad(stacked, pads)[None]


def body(vectors, resident, inv_mass, potential, cell_matrix, connectivity):
    sz = Sizes(vectors, inv_mass, connectivity)
    bf16, f32 = jnp.bfloat16, jnp.float32
    nx, ny = lax.axis_size("dx"), lax.axis_size("dy")
    norm_scale = 1.0 / math.sqrt(sz.ex * sz.ey * sz.ez * nx * ny)
    ext, own, full, width = sz.ext, sz.own, sz.full, sz.width

    def like(shape, dtype):
        return jax.ShapeDtypeStruct(shape, dtype)

    fields = jnp.stack([inv_mass, potential])
    to_x = jnp.concatenate([vectors[:, 0], field_parts(fields[:, 0], width)])
    from_x = send(to_x, -1, 0)
    to_y = jnp.concatenate([vectors[:, :, 0], field_parts(fields[:, :, 0], width)])
    to_y = jnp.concatenate([to_y, from_x[:, None, 0]], axis=1)
    from_y = send(to_y, 0, -1)

    conn = connectivity.reshape(sz.cells, 1, sz.nodes)
    origins = list(sz.cell_origins())
    halves = 2 if sz.cells % 2 == 0 else 1
    step = sz.cells // halves
    matrices = []
    for at in range(0, sz.cells, step):
        matrices += call(
            functools.partial(order_kernel, sz, origins[at : at + step]), "order_cells",
            4 * step * sz.depth**3, [like((step, sz.rows, sz.depth), bf16)], [],
            [conn[at : at + step], cell_matrix],
        )
    own_inv = jnp.broadcast_to(inv_mass[..., None], inv_mass.shape + (width,))
    own_pot = jnp.broadcast_to(potential[..., None], inv_mass.shape + (width,))
    parity = jnp.reshape(lax.axis_index("dy") % 2, (1,)).astype(jnp.int32)

    messages = [
        like((2, 2, sz.blocks, sz.ez, width), bf16),
        like((2, sz.blocks, sz.gy - 2, sz.ez, width), bf16),
        like((2, sz.blocks, sz.gx, sz.ez, width), f32),
    ]
    scratch = [
        pltpu.VMEM(ext, f32),
        pltpu.VMEM((sz.depth, full), f32),
        pltpu.VMEM((sz.rows - sz.main, full), f32),
    ]
    flops = 2 * sz.cells * sz.rows * sz.depth * full
    field_ext = like(ext[1:], f32)

    def exchange(corner, face, side):
        corner = swap_x(corner)
        face = swap_x(face)
        near, far = call(
            functools.partial(side_kernel, sz), "sides", 0,
            [like((sz.blocks, sz.gx, sz.ez, width), bf16)] * 2, [], [side, corner],
        )
        return (corner, face, *swap_y(near, far))

    x_ext, inv_b, pot_b, part, *sent = call(
        functools.partial(first_kernel, sz, len(matrices)), "first", flops,
        [like(ext, bf16), field_ext, field_ext, like(ext, f32)] + messages, scratch,
        [parity, vectors, from_x, from_y, own_inv, own_pot, *matrices], True,
    )
    y1, part, *sent = call(
        functools.partial(second_kernel, sz, len(matrices)), "second", flops,
        [like(ext, f32), like(ext, f32)] + messages, scratch,
        [parity, x_ext, part, *exchange(*sent), inv_b, pot_b, *matrices], True,
    )
    part, corner, face, side = call(
        functools.partial(third_kernel, sz, len(matrices)), "third", flops,
        [
            like(own, f32), like((sz.blocks, sz.ez, width), bf16),
            like((sz.blocks, sz.ey, sz.ez, width), bf16), like((sz.blocks, sz.ex, sz.ez, width), f32),
        ],
        [pltpu.VMEM(ext, f32), pltpu.VMEM(ext, f32)] + scratch,
        [parity, x_ext, y1, part, *exchange(*sent), inv_b, pot_b, *matrices], True,
    )
    corner = send(corner, 1, 0)
    face = send(face, 1, 0)
    (side,) = call(
        functools.partial(last_side_kernel, sz), "last_side", 0,
        [like((sz.blocks, sz.ex, sz.ez, width), bf16)], [], [side, corner],
    )
    side = send(side, 0, 1)
    filtered, rounded = call(
        functools.partial(last_kernel, sz), "last", 0,
        [like(own, f32), like(own[1:4] + (full,), bf16)], [],
        [part, face, side, inv_b],
    )
    local = lax.dot_general(
        resident.reshape(-1, resident.shape[-1]), rounded.reshape(-1, full),
        (((0,), (0,)), ((), ())), preferred_element_type=f32,
    )
    local = (local * norm_scale).astype(bf16).reshape(ny, -1, full)
    pieces = lax.all_to_all(local, "dy", 0, 0)
    mine = jnp.sum(pieces.astype(f32), axis=0)
    total = mine
    for steps in range(1, nx):
        total = total + send(mine, steps, 0)
    return (filtered, total)


def solution(mesh):
    return jax.shard_map(
        body,
        mesh=mesh,
        in_specs=(
            P(None, "dx", "dy", None, None),
            P("dx", "dy", None, None),
            P("dx", "dy", None),
            P("dx", "dy", None),
            P(),
            P("dx", "dy", None, None),
        ),
        out_specs=(P(None, "dx", "dy", None, None), P("dy", None)),
        check_vma=False,
    )
```

time: 359 us -> 106 us (0.30)
  waiting for transfers between devices: 170 us -> 27.9 us
  other arithmetic: 74.7 us -> 5.79 us
  local copies, waits for them, and re-layouts: 69.4 us -> 14.1 us
  Pallas kernels: 0 us -> 22.2 us
  matrix products: 14.6 us -> 0.72 us
  between operations: 14.5 us -> 0.84 us
  blocking collectives: 0 us -> 12.6 us
  starting transfers between devices: 15.1 us -> 20.7 us
    psum x1 -> x0, waiting for transfers between devices: 123 us -> none  [body(): summed = lax.psum(local, ('dx', 'dy'))]
    scatter-add x9 -> x0, other arithmetic: 56.2 us -> none  [the longest x3 52.4 us: apply_hamiltonian(): jax.ops.segment_sum(product.reshape(-1, vec_width), node_index, num_segme...]
    gather x3 -> x0, local copies, waits for them, and re-layouts: 28.9 us -> none  [apply_hamiltonian(): jnp.take(grown.reshape(-1, vec_width), node_index, axis=0)]
    pallas_call x0 -> x9, Pallas kernels: none -> 22.2 us  [call(): pl.pallas_call(kernel, in_specs=specs, out_specs=[whole] * len(out_shape)...]
    reshape x6 -> x0, local copies, waits for them, and re-layouts: 20.8 us -> none  [the longest x3 11.7 us: apply_hamiltonian(): product.reshape(-1, vec_width)]
    ppermute x12 -> x14, waiting for transfers between devices: 46.5 us -> 27.9 us  [the longest x10 21.8 us: send(): return lax.ppermute(value, ('dx', 'dy'), pairs)]
    dot_general x4 -> x1, matrix products: 14.6 us -> 0.72 us  [body(): lax.dot_general(resident.reshape(-1, resident.shape[-1]), rounded.reshape...]
    all_to_all x0 -> x1, blocking collectives: none -> 12.6 us  [body(): pieces = lax.all_to_all(local, 'dy', 0, 0)]
  transfers between devices with their start and end apart: 13 -> 14, of which waited for: 13 -> 7; matrix products, arithmetic and copies ran while one was open for 3% -> 2% of each run, Pallas kernels for 0% -> 7%
where the time goes in v1:
time: 106 us; the launch traced here: 105 us
  waiting for transfers between devices  27.9 us (26%)
  Pallas kernels  22.2 us (21%)
  starting transfers between devices  20.7 us (20%)
  local copies, waits for them, and re-layouts  14.1 us (13%)
  blocking collectives  12.6 us (12%)
  other arithmetic  5.79 us (5%)
    pallas_call x9, Pallas kernels, call(): pl.pallas_call(kernel, in_specs=specs, out_specs=[whole] * len(out_shape)...  22.2 us
    ppermute x10, waiting for transfers between devices, send(): return lax.ppermute(value, ('dx', 'dy'), pairs)  21.8 us
    ppermute x10, starting transfers between devices, send(): return lax.ppermute(value, ('dx', 'dy'), pairs)  13.6 us
    all_to_all x1, blocking collectives, body(): pieces = lax.all_to_all(local, 'dy', 0, 0)  12.6 us
    unnamed x20, local copies, waits for them, and re-layouts  8.81 us
    ppermute x2, starting transfers between devices, swap_y(): far = lax.ppermute(far, 'dy', far_pairs)  6.93 us
    ppermute x2, waiting for transfers between devices, swap_y(): far = lax.ppermute(far, 'dy', far_pairs)  6.14 us
    unnamed x10, other arithmetic  3.72 us
  transfers between devices with their start and end apart: 14, of which 7 were waited for; matrix products, arithmetic and copies ran while one was open for 2% of the time, Pallas kernels for 7%

profile of v1, /device:TPU:0, one launch (start us, length us, event | category | flops | bytes accessed | tf_op | source)
XLA Modules:
  0.0 104.8 jit_solution(8947845768750754980)
XLA Ops:
  0.6 0.8 constant_dynamic-update-slice_fusion.5
  1.5 0.7 constant_dynamic-update-slice_fusion.4
  2.2 0.7 constant_dynamic-update-slice_fusion.3
  2.9 0.7 constant_dynamic-update-slice_fusion.2
  3.6 0.7 constant_dynamic-update-slice_fusion.1
  4.3 0.7 constant_dynamic-update-slice_fusion
  5.0 0.2 copy.30
  5.2 0.9 slice_bitcast_fusion
  6.2 3.0 %collective-permute-start = (bf16[3,16,16,128]{3,2,1,0:T(8,128)(2,1)S(1)}, bf16[3,16,16,128]{3,2,1,0:T(8,128)(2,1)S(1)}, u32[]{:S(2)}, u32[]{:S(2)}) collective-permute-start(bf16[3,16,16,128]{3,2,1,0:T(8,128)(2,1)S(1)} %pad_maximum_fusion), channel_id=1, source_target_pairs={{0,16},{1,17},{2,18},{3,19},{4,20},{5,21},{6,22},{7,23},{8,24},{9,... | collective-permute-start | bytes 589832 | tf_op jit(solution)/shard_map/ppermute | solution.py:54
  9.2 0.8 slice.60
  10.0 0.8 slice.61
  10.8 0.8 fusion.11
  11.6 0.1 copy.32
  11.8 1.2 %copy-done.8 = bf16[729,729]{1,0:T(8,128)(2,1)S(1)} copy-done((bf16[729,729]{1,0:T(8,128)(2,1)S(1)}, bf16[729,729]{1,0:T(8,128)(2,1)}, u32[]{:S(2)}) %copy-start.8) | copy-done | bytes 1062906
  13.0 3.8 %order_cells.3.refs_1_ = bf16[2,736,768]{2,1,0:T(8,128)(2,1)S(1)} custom-call(s32[2,1,729]{2,1,0:T(1,128)S(1)} %get-tuple-element.48.conn_ref, bf16[729,729]{1,0:T(8,128)(2,1)S(1)} %copy-done.8), custom_call_target="tpu_custom_call" | custom-call | flops 3623878656 | bytes 3329706 | tf_op jit(solution)/shard_map/order_cells/pallas_call | solution.py:276
  16.9 1.4 %copy-done.1 = bf16[2,736,768]{2,1,0:T(8,128)(2,1)} copy-done((bf16[2,736,768]{2,1,0:T(8,128)(2,1)}, bf16[2,736,768]{2,1,0:T(8,128)(2,1)S(1)}, u32[]{:S(2)}) %copy-start.1) | copy-done | bytes 2261016
  18.3 0.7 pad_maximum_fusion.1
  19.0 3.7 %collective-permute-start.1 = (bf16[3,9,16,128]{3,2,1,0:T(8,128)(2,1)}, bf16[3,9,16,128]{3,2,1,0:T(8,128)(2,1)S(1)}, u32[]{:S(2)}, u32[]{:S(2)}) collective-permute-start(bf16[3,9,16,128]{3,2,1,0:T(8,128)(2,1)} %pad_maximum_fusion.1), channel_id=1, source_target_pairs={{0,15},{1,0},{2,1},{3,2},{4,3},{5,4},{6,5},{7,6},{8,7},{9,8},{10,9... | collective-permute-start | bytes 331784 | tf_op jit(solution)/shard_map/ppermute | solution.py:54
  22.7 3.8 %order_cells.2.refs_0_ = bf16[2,736,768]{2,1,0:T(8,128)(2,1)S(1)} custom-call(s32[2,1,729]{2,1,0:T(1,128)S(1)} %get-tuple-element.49.conn_ref, bf16[729,729]{1,0:T(8,128)(2,1)S(1)} %copy-done.8), custom_call_target="tpu_custom_call" | custom-call | flops 3623878656 | bytes 3329706 | tf_op jit(solution)/shard_map/order_cells/pallas_call | solution.py:276
  26.5 1.4 %copy-done.3 = bf16[2,736,768]{2,1,0:T(8,128)(2,1)} copy-done((bf16[2,736,768]{2,1,0:T(8,128)(2,1)}, bf16[2,736,768]{2,1,0:T(8,128)(2,1)S(1)}, u32[]{:S(2)}) %copy-start.3) | copy-done | bytes 2261016
  27.9 0.3 broadcast_in_dim.20.own_inv
  28.2 1.2 %broadcast_in_dim.21.own_pot = f32[8,16,16,128]{3,2,1,0:T(8,128)S(1)} broadcast(f32[8,16,16]{2,1,0:T(8,128)} %param.9), dimensions={0,1,2} | broadcast | bytes 1056768 | tf_op jit(solution)/shard_map/broadcast_in_dim | solution.py:330
  29.4 1.6 %copy-done.2 = bf16[2,736,768]{2,1,0:T(8,128)(2,1)S(1)} copy-done((bf16[2,736,768]{2,1,0:T(8,128)(2,1)S(1)}, bf16[2,736,768]{2,1,0:T(8,128)(2,1)}, u32[]{:S(2)}) %copy-start.2) | copy-done | bytes 2261016
  31.0 1.6 %copy-done.4 = bf16[2,736,768]{2,1,0:T(8,128)(2,1)S(1)} copy-done((bf16[2,736,768]{2,1,0:T(8,128)(2,1)S(1)}, bf16[2,736,768]{2,1,0:T(8,128)(2,1)}, u32[]{:S(2)}) %copy-start.4) | copy-done | bytes 2261016
  32.7 3.7 %first.1 = (bf16[2,9,17,16,128]{4,3,2,1,0:T(8,128)(2,1)S(1)}, f32[9,17,16,128]{3,2,1,0:T(8,128)S(1)}, f32[9,17,16,128]{3,2,1,0:T(8,128)S(1)}, f32[2,9,17,16,128]...) custom-call(s32[1]{0:T(128)} %bitcast.even_ref, ...), custom_call_target="tpu_custom_call" | custom-call | flops 1157627904 | bytes 14815236 | tf_op jit(solution)/shard_map/first/pallas_call | solution.py:276
  36.4 0.5 collective-permute-start.3
  36.9 1.5 %collective-permute-start.2 = (bf16[2,2,2,16,128]{4,3,2,1,0:T(8,128)(2,1)S(1)}, bf16[2,2,2,16,128]{4,3,2,1,0:T(8,128)(2,1)S(1)}, u32[]{:S(2)}, u32[]{:S(2)}) collective-permute-start(bf16[2,2,2,16,128]{4,3,2,1,0:T(8,128)(2,1)S(1)} %get-tuple-element.26), channel_id=1, source_target_pairs={{0,16},{1,17},{2,18},{3,19},{4,20},{5,21},{6,22},{7,23},{8,24},{9,... | collective-permute-start | bytes 98312 | tf_op jit(solution)/shard_map/ppermute | solution.py:54
  38.4 4.5 %collective-permute-done.2.corner_ref.corner_in = bf16[2,2,2,16,128]{4,3,2,1,0:T(8,128)(2,1)S(1)} collective-permute-done((bf16[2,2,2,16,128]{4,3,2,1,0:T(8,128)(2,1)S(1)}, bf16[2,2,2,16,128]{4,3,2,1,0:T(8,128)(2,1)S(1)}, u32[]{:S(2)}, u32[]{:S(2)}) %collective-permute-start.2) | collective-permute-done | bytes 32800 | tf_op jit(solution)/shard_map/ppermute | solution.py:54
  43.1 3.6 %collective-permute-start.5 = (bf16[2,9,16,128]{3,2,1,0:T(8,128)(2,1)S(1)}, bf16[2,9,16,128]{3,2,1,0:T(8,128)(2,1)S(1)}, u32[]{:S(2)}, u32[]{:S(2)}) collective-permute-start(bf16[2,9,16,128]{3,2,1,0:T(8,128)(2,1)S(1)} %get-tuple-element.30), channel_id=1, source_target_pairs={{0,15},{1,2},{2,1},{3,4},{4,3},{5,6},{6,5},{7,8},{8,7},{9,10},{10,... | collective-permute-start | bytes 221192 | tf_op jit(solution)/shard_map/ppermute | solution.py:67
  46.6 3.0 %collective-permute-done.5.far_in = bf16[2,9,16,128]{3,2,1,0:T(8,128)(2,1)S(1)} collective-permute-done((bf16[2,9,16,128]{3,2,1,0:T(8,128)(2,1)S(1)}, bf16[2,9,16,128]{3,2,1,0:T(8,128)(2,1)S(1)}, u32[]{:S(2)}, u32[]{:S(2)}) %collective-permute-start.5) | collective-permute-done | bytes 73760 | tf_op jit(solution)/shard_map/ppermute | solution.py:67
  49.6 4.2 %second.1 = (f32[2,9,17,16,128]{4,3,2,1,0:T(8,128)S(1)}, f32[2,9,17,16,128]{4,3,2,1,0:T(8,128)S(1)}, bf16[2,2,2,16,128]{4,3,2,1,0:T(8,128)(2,1)S(1)}, bf16[2,2,1...) custom-call(s32[1]{0:T(128)} %bitcast.even_ref, bf16[2,9,17,16,128]{4,3,2,1,0:T(8,128)(2,1)S(1)} %get-tuple-element.24.x_ref, ...), custom_call_target="tpu_custom_call" | custom-call | flops 1157627904 | bytes 16801796 | tf_op jit(solution)/shard_map/second/pallas_call | solution.py:276
  53.8 1.5 %copy-done.6 = f32[2,9,17,16,128]{4,3,2,1,0:T(8,128)} copy-done((f32[2,9,17,16,128]{4,3,2,1,0:T(8,128)}, f32[2,9,17,16,128]{4,3,2,1,0:T(8,128)S(1)}, u32[]{:S(2)}) %copy-start.6) | copy-done | bytes 2506776
  55.3 0.5 collective-permute-start.7
  55.8 1.5 %collective-permute-start.6 = (bf16[2,2,2,16,128]{4,3,2,1,0:T(8,128)(2,1)S(1)}, bf16[2,2,2,16,128]{4,3,2,1,0:T(8,128)(2,1)S(1)}, u32[]{:S(2)}, u32[]{:S(2)}) collective-permute-start(bf16[2,2,2,16,128]{4,3,2,1,0:T(8,128)(2,1)S(1)} %get-tuple-element.35), channel_id=1, source_target_pairs={{0,16},{1,17},{2,18},{3,19},{4,20},{5,21},{6,22},{7,23},{8,24},{9,... | collective-permute-start | bytes 98312 | tf_op jit(solution)/shard_map/ppermute | solution.py:54
  57.3 4.5 %collective-permute-done.6.corner_ref.corner_in = bf16[2,2,2,16,128]{4,3,2,1,0:T(8,128)(2,1)S(1)} collective-permute-done((bf16[2,2,2,16,128]{4,3,2,1,0:T(8,128)(2,1)S(1)}, bf16[2,2,2,16,128]{4,3,2,1,0:T(8,128)(2,1)S(1)}, u32[]{:S(2)}, u32[]{:S(2)}) %collective-permute-start.6) | collective-permute-done | bytes 32800 | tf_op jit(solution)/shard_map/ppermute | solution.py:54
  62.0 3.4 %collective-permute-start.9 = (bf16[2,9,16,128]{3,2,1,0:T(8,128)(2,1)S(1)}, bf16[2,9,16,128]{3,2,1,0:T(8,128)(2,1)S(1)}, u32[]{:S(2)}, u32[]{:S(2)}) collective-permute-start(bf16[2,9,16,128]{3,2,1,0:T(8,128)(2,1)S(1)} %get-tuple-element.39), channel_id=1, source_target_pairs={{0,15},{1,2},{2,1},{3,4},{4,3},{5,6},{6,5},{7,8},{8,7},{9,10},{10,... | collective-permute-start | bytes 221192 | tf_op jit(solution)/shard_map/ppermute | solution.py:67
  65.3 3.2 %collective-permute-done.9.far_in = bf16[2,9,16,128]{3,2,1,0:T(8,128)(2,1)S(1)} collective-permute-done((bf16[2,9,16,128]{3,2,1,0:T(8,128)(2,1)S(1)}, bf16[2,9,16,128]{3,2,1,0:T(8,128)(2,1)S(1)}, u32[]{:S(2)}, u32[]{:S(2)}) %collective-permute-start.9) | collective-permute-done | bytes 73760 | tf_op jit(solution)/shard_map/ppermute | solution.py:67
  68.5 5.0 %third.1 = (f32[2,8,16,16,128]{4,3,2,1,0:T(8,128)S(1)}, bf16[2,16,128]{2,1,0:T(8,128)(2,1)S(1)}, bf16[2,16,16,128]{3,2,1,0:T(8,128)(2,1)S(1)}, f32[2,8,16,128]{3,2,1,0:T(8,128)S(1)}) custom-call(s32[1]{0:T(128)} %bitcast.even_ref, bf16[2,9,17,16,128]{4,3,2,1,0:T(8,128)(2,1)S(1)} %get-tuple-element.24.x_ref, ...), custom_call_target="tpu_custom_call" | custom-call | flops 1157627904 | bytes 16089092 | tf_op jit(solution)/shard_map/third/pallas_call | solution.py:276
  73.5 0.6 collective-permute-start.10
  74.1 1.5 %collective-permute-start.11 = (bf16[2,16,128]{2,1,0:T(8,128)(2,1)S(1)}, bf16[2,16,128]{2,1,0:T(8,128)(2,1)S(1)}, u32[]{:S(2)}, u32[]{:S(2)}) collective-permute-start(bf16[2,16,128]{2,1,0:T(8,128)(2,1)S(1)} %get-tuple-element.43), channel_id=1, source_target_pairs={{0,16},{1,17},{2,18},{3,19},{4,20},{5,21},{6,22},{7,23},{8,24},{9,... | collective-permute-start | bytes 24584 | tf_op jit(solution)/shard_map/ppermute | solution.py:54
  75.6 3.0 %collective-permute-done.11.corner_ref = bf16[2,16,128]{2,1,0:T(8,128)(2,1)S(1)} collective-permute-done((bf16[2,16,128]{2,1,0:T(8,128)(2,1)S(1)}, bf16[2,16,128]{2,1,0:T(8,128)(2,1)S(1)}, u32[]{:S(2)}, u32[]{:S(2)}) %collective-permute-start.11) | collective-permute-done | bytes 8224 | tf_op jit(solution)/shard_map/ppermute | solution.py:54
  78.7 6.4 %collective-permute-done.12.side = bf16[2,8,16,128]{3,2,1,0:T(8,128)(2,1)S(1)} collective-permute-done((bf16[2,8,16,128]{3,2,1,0:T(8,128)(2,1)S(1)}, bf16[2,8,16,128]{3,2,1,0:T(8,128)(2,1)S(1)}, u32[]{:S(2)}, u32[]{:S(2)}) %collective-permute-start.12) | collective-permute-done | bytes 65568 | tf_op jit(solution)/shard_map/ppermute | solution.py:54
  85.1 1.6 %last.1 = (f32[2,8,16,16,128]{4,3,2,1,0:T(8,128)}, bf16[8,16,16,256]{3,2,1,0:T(8,128)(2,1)S(1)}) custom-call(f32[2,8,16,16,128]{4,3,2,1,0:T(8,128)S(1)} %get-tuple-element.40.part_ref, bf16[2,16,16,128]{3,2,1,0:T(8,128)(2,1)S(1)} %collective-permute-done.10.face, bf16[2,8,16,128]{3,2,1,0:T(8,128)(2,1)S(1)} %collective-permute-done.12.side, ...), custom_call_target="tpu_custom_call" | custom-call | bytes 6692864 | tf_op jit(solution)/shard_map/last/pallas_call | solution.py:276
  86.7 0.7 fusion.2
  87.5 12.6 %all_to_all.5 = bf16[16,32,256]{2,1,0:T(8,128)(2,1)S(1)} all-to-all(bf16[16,32,256]{2,1,0:T(8,128)(2,1)S(1)} %bitcast.68), channel_id=1, replica_groups=mesh['dx'=2,'dy'=16] {'dy'}, dimensions={0} | all-to-all | bytes 524288 | tf_op jit(solution)/shard_map/all_to_all | solution.py:391
  100.2 0.7 collective-permute-start.13
  100.9 3.3 %collective-permute-done.13 = f32[32,256]{1,0:T(8,128)S(1)} collective-permute-done((f32[32,256]{1,0:T(8,128)S(1)}, f32[32,256]{1,0:T(8,128)S(1)}, u32[]{:S(2)}, u32[]{:S(2)}) %collective-permute-start.13) | collective-permute-done | bytes 32800 | tf_op jit(solution)/shard_map/ppermute | solution.py:54
  104.2 0.6 add.12
  (41 shorter events, 0.6 us)
Async XLA Ops:
  0.6 86.0 %copy-start = (bf16[8,16,16,512]{3,2,1,0:T(8,128)(2,1)S(1)}, bf16[8,16,16,512]{3,2,1,0:T(8,128)(2,1)}, u32[]{:S(2)}) copy-start(bf16[8,16,16,512]{3,2,1,0:T(8,128)(2,1)} %param.7) | copy-start | bytes 6291460
  6.2 12.1 %collective-permute-start = (bf16[3,16,16,128]{3,2,1,0:T(8,128)(2,1)S(1)}, bf16[3,16,16,128]{3,2,1,0:T(8,128)(2,1)S(1)}, u32[]{:S(2)}, u32[]{:S(2)}) collective-permute-start(bf16[3,16,16,128]{3,2,1,0:T(8,128)(2,1)S(1)} %pad_maximum_fusion), channel_id=1, source_target_pairs={{0,16},{1,17},{2,18},{3,19},{4,20},{5,21},{6,22},{7,23},{8,24},{9,... | collective-permute-start | bytes 589832 | tf_op jit(solution)/shard_map/ppermute | solution.py:54
  11.8 1.3 %copy-start.8 = (bf16[729,729]{1,0:T(8,128)(2,1)S(1)}, bf16[729,729]{1,0:T(8,128)(2,1)}, u32[]{:S(2)}) copy-start(bf16[729,729]{1,0:T(8,128)(2,1)} %matrix_ref.3) | copy-start | bytes 3188650
  13.0 5.2 %copy-start.7 = (bf16[2,8,16,16,128]{4,3,2,1,0:T(8,128)(2,1)S(1)}, bf16[2,8,16,16,128]{4,3,2,1,0:T(8,128)(2,1)}, u32[]{:S(2)}) copy-start(bf16[2,8,16,16,128]{4,3,2,1,0:T(8,128)(2,1)} %vec_ref.1) | copy-start | bytes 3145732
  16.9 1.4 %copy-start.1 = (bf16[2,736,768]{2,1,0:T(8,128)(2,1)}, bf16[2,736,768]{2,1,0:T(8,128)(2,1)S(1)}, u32[]{:S(2)}) copy-start(bf16[2,736,768]{2,1,0:T(8,128)(2,1)S(1)} %order_cells.3.refs_1_) | copy-start | bytes 6782980
  19.0 8.9 %collective-permute-start.1 = (bf16[3,9,16,128]{3,2,1,0:T(8,128)(2,1)}, bf16[3,9,16,128]{3,2,1,0:T(8,128)(2,1)S(1)}, u32[]{:S(2)}, u32[]{:S(2)}) collective-permute-start(bf16[3,9,16,128]{3,2,1,0:T(8,128)(2,1)} %pad_maximum_fusion.1), channel_id=1, source_target_pairs={{0,15},{1,0},{2,1},{3,2},{4,3},{5,4},{6,5},{7,6},{8,7},{9,8},{10,9... | collective-permute-start | bytes 331784 | tf_op jit(solution)/shard_map/ppermute | solution.py:54
  22.7 5.2 %copy-start.9 = (f32[8,16,16]{2,1,0:T(8,128)S(1)}, f32[8,16,16]{2,1,0:T(8,128)}, u32[]{:S(2)}) copy-start(f32[8,16,16]{2,1,0:T(8,128)} %param.8) | copy-start | bytes 24580
  26.5 1.4 %copy-start.3 = (bf16[2,736,768]{2,1,0:T(8,128)(2,1)}, bf16[2,736,768]{2,1,0:T(8,128)(2,1)S(1)}, u32[]{:S(2)}) copy-start(bf16[2,736,768]{2,1,0:T(8,128)(2,1)S(1)} %order_cells.2.refs_0_) | copy-start | bytes 6782980
  29.4 1.6 %copy-start.2 = (bf16[2,736,768]{2,1,0:T(8,128)(2,1)S(1)}, bf16[2,736,768]{2,1,0:T(8,128)(2,1)}, u32[]{:S(2)}) copy-start(bf16[2,736,768]{2,1,0:T(8,128)(2,1)} %copy-done.1) | copy-start | bytes 6782980
  31.0 1.6 %copy-start.4 = (bf16[2,736,768]{2,1,0:T(8,128)(2,1)S(1)}, bf16[2,736,768]{2,1,0:T(8,128)(2,1)}, u32[]{:S(2)}) copy-start(bf16[2,736,768]{2,1,0:T(8,128)(2,1)} %copy-done.3) | copy-start | bytes 6782980
  32.7 16.9 %copy-start.5 = (bf16[2,736,768]{2,1,0:T(8,128)(2,1)S(1)}, bf16[2,736,768]{2,1,0:T(8,128)(2,1)}, u32[]{:S(2)}) copy-start(bf16[2,736,768]{2,1,0:T(8,128)(2,1)} %copy-done.3) | copy-start | bytes 6782980
  36.4 13.2 %collective-permute-start.3 = (bf16[2,2,15,16,128]{4,3,2,1,0:T(8,128)(2,1)S(1)}, bf16[2,2,15,16,128]{4,3,2,1,0:T(8,128)(2,1)S(1)}, u32[]{:S(2)}, u32[]{:S(2)}) collective-permute-start(bf16[2,2,15,16,128]{4,3,2,1,0:T(8,128)(2,1)S(1)} %get-tuple-element.27), channel_id=1, source_target_pairs={{0,16},{1,17},{2,18},{3,19},{4,20},{5,21},{6,22},{7,23},{8,24},{9,... | collective-permute-start | bytes 737288 | tf_op jit(solution)/shard_map/ppermute | solution.py:54
  36.9 6.0 %collective-permute-start.2 = (bf16[2,2,2,16,128]{4,3,2,1,0:T(8,128)(2,1)S(1)}, bf16[2,2,2,16,128]{4,3,2,1,0:T(8,128)(2,1)S(1)}, u32[]{:S(2)}, u32[]{:S(2)}) collective-permute-start(bf16[2,2,2,16,128]{4,3,2,1,0:T(8,128)(2,1)S(1)} %get-tuple-element.26), channel_id=1, source_target_pairs={{0,16},{1,17},{2,18},{3,19},{4,20},{5,21},{6,22},{7,23},{8,24},{9,... | collective-permute-start | bytes 98312 | tf_op jit(solution)/shard_map/ppermute | solution.py:54
  43.0 3.7 %collective-permute-start.4 = (bf16[2,9,16,128]{3,2,1,0:T(8,128)(2,1)S(1)}, bf16[2,9,16,128]{3,2,1,0:T(8,128)(2,1)S(1)}, u32[]{:S(2)}, u32[]{:S(2)}) collective-permute-start(bf16[2,9,16,128]{3,2,1,0:T(8,128)(2,1)S(1)} %get-tuple-element.29), channel_id=1, source_target_pairs={{0,1},{1,0},{2,3},{3,2},{4,5},{5,4},{6,7},{7,6},{8,9},{9,8},{10,11... | collective-permute-start | bytes 221192 | tf_op jit(solution)/shard_map/ppermute | solution.py:68
  43.1 6.5 %collective-permute-start.5 = (bf16[2,9,16,128]{3,2,1,0:T(8,128)(2,1)S(1)}, bf16[2,9,16,128]{3,2,1,0:T(8,128)(2,1)S(1)}, u32[]{:S(2)}, u32[]{:S(2)}) collective-permute-start(bf16[2,9,16,128]{3,2,1,0:T(8,128)(2,1)S(1)} %get-tuple-element.30), channel_id=1, source_target_pairs={{0,15},{1,2},{2,1},{3,4},{4,3},{5,6},{6,5},{7,8},{8,7},{9,10},{10,... | collective-permute-start | bytes 221192 | tf_op jit(solution)/shard_map/ppermute | solution.py:67
  53.8 1.5 %copy-start.6 = (f32[2,9,17,16,128]{4,3,2,1,0:T(8,128)}, f32[2,9,17,16,128]{4,3,2,1,0:T(8,128)S(1)}, u32[]{:S(2)}) copy-start(f32[2,9,17,16,128]{4,3,2,1,0:T(8,128)S(1)} %get-tuple-element.34.sum_ref) | copy-start | bytes 7520260
  55.3 13.2 %collective-permute-start.7 = (bf16[2,2,15,16,128]{4,3,2,1,0:T(8,128)(2,1)S(1)}, bf16[2,2,15,16,128]{4,3,2,1,0:T(8,128)(2,1)S(1)}, u32[]{:S(2)}, u32[]{:S(2)}) collective-permute-start(bf16[2,2,15,16,128]{4,3,2,1,0:T(8,128)(2,1)S(1)} %get-tuple-element.36), channel_id=1, source_target_pairs={{0,16},{1,17},{2,18},{3,19},{4,20},{5,21},{6,22},{7,23},{8,24},{9,... | collective-permute-start | bytes 737288 | tf_op jit(solution)/shard_map/ppermute | solution.py:54
  55.8 6.0 %collective-permute-start.6 = (bf16[2,2,2,16,128]{4,3,2,1,0:T(8,128)(2,1)S(1)}, bf16[2,2,2,16,128]{4,3,2,1,0:T(8,128)(2,1)S(1)}, u32[]{:S(2)}, u32[]{:S(2)}) collective-permute-start(bf16[2,2,2,16,128]{4,3,2,1,0:T(8,128)(2,1)S(1)} %get-tuple-element.35), channel_id=1, source_target_pairs={{0,16},{1,17},{2,18},{3,19},{4,20},{5,21},{6,22},{7,23},{8,24},{9,... | collective-permute-start | bytes 98312 | tf_op jit(solution)/shard_map/ppermute | solution.py:54
  61.9 3.4 %collective-permute-start.8 = (bf16[2,9,16,128]{3,2,1,0:T(8,128)(2,1)S(1)}, bf16[2,9,16,128]{3,2,1,0:T(8,128)(2,1)S(1)}, u32[]{:S(2)}, u32[]{:S(2)}) collective-permute-start(bf16[2,9,16,128]{3,2,1,0:T(8,128)(2,1)S(1)} %get-tuple-element.38), channel_id=1, source_target_pairs={{0,1},{1,0},{2,3},{3,2},{4,5},{5,4},{6,7},{7,6},{8,9},{9,8},{10,11... | collective-permute-start | bytes 221192 | tf_op jit(solution)/shard_map/ppermute | solution.py:68
  62.0 6.5 %collective-permute-start.9 = (bf16[2,9,16,128]{3,2,1,0:T(8,128)(2,1)S(1)}, bf16[2,9,16,128]{3,2,1,0:T(8,128)(2,1)S(1)}, u32[]{:S(2)}, u32[]{:S(2)}) collective-permute-start(bf16[2,9,16,128]{3,2,1,0:T(8,128)(2,1)S(1)} %get-tuple-element.39), channel_id=1, source_target_pairs={{0,15},{1,2},{2,1},{3,4},{4,3},{5,6},{6,5},{7,8},{8,7},{9,10},{10,... | collective-permute-start | bytes 221192 | tf_op jit(solution)/shard_map/ppermute | solution.py:67
  73.5 11.6 %collective-permute-start.10 = (bf16[2,16,16,128]{3,2,1,0:T(8,128)(2,1)S(1)}, bf16[2,16,16,128]{3,2,1,0:T(8,128)(2,1)S(1)}, u32[]{:S(2)}, u32[]{:S(2)}) collective-permute-start(bf16[2,16,16,128]{3,2,1,0:T(8,128)(2,1)S(1)} %get-tuple-element.41), channel_id=1, source_target_pairs={{0,16},{1,17},{2,18},{3,19},{4,20},{5,21},{6,22},{7,23},{8,24},{9,... | collective-permute-start | bytes 393224 | tf_op jit(solution)/shard_map/ppermute | solution.py:54
  74.1 4.5 %collective-permute-start.11 = (bf16[2,16,128]{2,1,0:T(8,128)(2,1)S(1)}, bf16[2,16,128]{2,1,0:T(8,128)(2,1)S(1)}, u32[]{:S(2)}, u32[]{:S(2)}) collective-permute-start(bf16[2,16,128]{2,1,0:T(8,128)(2,1)S(1)} %get-tuple-element.43), channel_id=1, source_target_pairs={{0,16},{1,17},{2,18},{3,19},{4,20},{5,21},{6,22},{7,23},{8,24},{9,... | collective-permute-start | bytes 24584 | tf_op jit(solution)/shard_map/ppermute | solution.py:54
  78.6 6.4 %collective-permute-start.12 = (bf16[2,8,16,128]{3,2,1,0:T(8,128)(2,1)S(1)}, bf16[2,8,16,128]{3,2,1,0:T(8,128)(2,1)S(1)}, u32[]{:S(2)}, u32[]{:S(2)}) collective-permute-start(bf16[2,8,16,128]{3,2,1,0:T(8,128)(2,1)S(1)} %last_side.1), channel_id=1, source_target_pairs={{0,1},{1,2},{2,3},{3,4},{4,5},{5,6},{6,7},{7,8},{8,9},{9,10},{10,1... | collective-permute-start | bytes 196616 | tf_op jit(solution)/shard_map/ppermute | solution.py:54
  100.2 4.0 %collective-permute-start.13 = (f32[32,256]{1,0:T(8,128)S(1)}, f32[32,256]{1,0:T(8,128)S(1)}, u32[]{:S(2)}, u32[]{:S(2)}) collective-permute-start(f32[32,256]{1,0:T(8,128)S(1)} %convert_reduce_fusion), channel_id=1, source_target_pairs={{0,16},{1,17},{2,18},{3,19},{4,20},{5,21},{6,22},{7,23},{8,24},{9,... | collective-permute-start | bytes 98312 | tf_op jit(solution)/shard_map/ppermute | solution.py:54

commit v2 on v1

--- a/solution.py
+++ b/solution.py
@@ -10,7 +10,7 @@
 
 LANES = 128
 SUB = 16
-VMEM_LIMIT = 40 * 1024 * 1024
+VMEM_LIMIT = 28 * 1024 * 1024
 
 center_shift = 1.2
 half_width = 2.0
@@ -69,10 +69,12 @@
     return near, far
 
 
-def order_kernel(sz, origins, conn_ref, matrix_ref, out_ref):
+def order_kernel(sz, first, count, conn_ref, matrix_ref, out_ref):
     f32, bf16 = jnp.float32, jnp.bfloat16
-    for cell, (x0, y0, z0) in enumerate(origins):
-        conn = conn_ref[cell].astype(f32)
+    for slot in range(count):
+        cell = first + slot
+        x0, y0, z0 = list(sz.cell_origins())[cell]
+        conn = conn_ref[cell : cell + 1, :].astype(f32)
         li = jnp.floor((conn + 0.5) * (1.0 / (sz.gy * sz.gz)))
         rest = conn - li * (sz.gy * sz.gz)
         lj = jnp.floor((rest + 0.5) * (1.0 / sz.gz))
@@ -86,7 +88,7 @@
         whole = lax.dot_general(
             half.astype(bf16), pick, (((1,), (1,)), ((), ())), preferred_element_type=f32
         )
-        out_ref[cell] = whole.astype(bf16)
+        out_ref[slot] = whole.astype(bf16)
 
 
 def cell_products(sz, u_ref, mat_refs, rhs_ref, edge_ref, acc_ref):
@@ -135,7 +137,8 @@
         face[1, b] = acc_ref[b, end_x, 1:end_y].astype(face.dtype)
 
 
-def side_kernel(sz, side_ref, corner_ref, near_ref, far_ref):
+def side_kernel(sz, side_ref, corner_ref, face_in, near_ref, far_ref, face_out):
+    del face_in, face_out
     for slot, out in enumerate((near_ref, far_ref)):
         for i in range(sz.gx):
             value = side_ref[slot, :, i]
@@ -161,6 +164,28 @@
     elif side is not None:
         total = total + face[side, :, j - 1].astype(f32)
     return total
+
+
+def field_row(inv, pot):
+    lane = lax.broadcasted_iota(jnp.int32, inv.shape, inv.ndim - 1)
+    row = jnp.zeros_like(inv)
+    for at, rest in enumerate((inv, pot)):
+        for k in range(3):
+            part = rest.astype(jnp.bfloat16).astype(jnp.float32)
+            rest = rest - part
+            row = jnp.where(lane == 3 * at + k, part, row)
+    return row.astype(jnp.bfloat16)
+
+
+def pack_x_kernel(sz, vec_ref, inv_ref, pot_ref, out_ref):
+    out_ref[: sz.blocks] = vec_ref[...]
+    out_ref[sz.blocks] = field_row(inv_ref[...], pot_ref[...])
+
+
+def pack_y_kernel(sz, vec_ref, inv_ref, pot_ref, from_x, out_ref):
+    out_ref[: sz.blocks, : sz.ex] = vec_ref[:, :, 0]
+    out_ref[sz.blocks, : sz.ex] = field_row(inv_ref[:, 0], pot_ref[:, 0])
+    out_ref[:, sz.ex] = from_x[:, 0]
 
 
 def first_kernel(
@@ -240,7 +265,8 @@
             part_ref[:, i, j] = 2.0 * (image - center_shift * new) / half_width - y_ref[:, i, j]
 
 
-def last_side_kernel(sz, side_ref, corner_ref, out_ref):
+def last_side_kernel(sz, side_ref, corner_ref, face_in, out_ref, face_out):
+    del face_in, face_out
     for i in range(sz.ex):
         value = side_ref[:, i]
         if i == 0:
@@ -267,7 +293,8 @@
             out_ref[:, i, j] = value
 
 
-def call(kernel, name, flops, out_shape, scratch, operands, scalar_first=False):
+def call(kernel, name, flops, out_shape, scratch, operands, scalar_first=False, aliases=None):
+    out_shape = [jax.ShapeDtypeStruct(s.shape, s.dtype) for s in out_shape]
     size = sum(math.prod(s.shape) * jnp.dtype(s.dtype).itemsize for s in (*operands, *out_shape))
     whole = pl.BlockSpec(memory_space=pltpu.VMEM)
     specs = [whole] * len(operands)
@@ -279,23 +306,11 @@
         out_specs=[whole] * len(out_shape),
         out_shape=out_shape,
         scratch_shapes=scratch,
+        input_output_aliases=aliases or {},
         compiler_params=pltpu.CompilerParams(vmem_limit_bytes=VMEM_LIMIT),
         cost_estimate=pl.CostEstimate(flops=flops, bytes_accessed=size, transcendentals=0),
         name=name,
     )(*operands)
-
-
-def field_parts(fields, width):
-    parts = []
-    for at in range(fields.shape[0]):
-        rest = fields[at]
-        for _ in range(3):
-            part = lax.reduce_precision(rest, 8, 7)
-            rest = rest - part
-            parts.append(part.astype(jnp.bfloat16))
-    stacked = jnp.stack(parts, axis=-1)
-    pads = [(0, 0)] * (stacked.ndim - 1) + [(0, width - len(parts))]
-    return jnp.pad(stacked, pads)[None]
 
 
 def body(vectors, resident, inv_mass, potential, cell_matrix, connectivity):
@@ -308,26 +323,30 @@
     def like(shape, dtype):
         return jax.ShapeDtypeStruct(shape, dtype)
 
-    fields = jnp.stack([inv_mass, potential])
-    to_x = jnp.concatenate([vectors[:, 0], field_parts(fields[:, 0], width)])
+    own_inv = jnp.broadcast_to(inv_mass[..., None], inv_mass.shape + (width,))
+    own_pot = jnp.broadcast_to(potential[..., None], inv_mass.shape + (width,))
+    (to_x,) = call(
+        functools.partial(pack_x_kernel, sz), "pack_x", 0,
+        [like((sz.blocks + 1, sz.ey, sz.ez, width), bf16)], [],
+        [vectors[:, 0], own_inv[0], own_pot[0]],
+    )
     from_x = send(to_x, -1, 0)
-    to_y = jnp.concatenate([vectors[:, :, 0], field_parts(fields[:, :, 0], width)])
-    to_y = jnp.concatenate([to_y, from_x[:, None, 0]], axis=1)
+    (to_y,) = call(
+        functools.partial(pack_y_kernel, sz), "pack_y", 0,
+        [like((sz.blocks + 1, sz.gx, sz.ez, width), bf16)], [], [vectors, own_inv, own_pot, from_x],
+    )
     from_y = send(to_y, 0, -1)
 
-    conn = connectivity.reshape(sz.cells, 1, sz.nodes)
-    origins = list(sz.cell_origins())
+    conn = connectivity.reshape(sz.cells, sz.nodes)
     halves = 2 if sz.cells % 2 == 0 else 1
     step = sz.cells // halves
     matrices = []
     for at in range(0, sz.cells, step):
         matrices += call(
-            functools.partial(order_kernel, sz, origins[at : at + step]), "order_cells",
+            functools.partial(order_kernel, sz, at, step), "order_cells",
             4 * step * sz.depth**3, [like((step, sz.rows, sz.depth), bf16)], [],
-            [conn[at : at + step], cell_matrix],
+            [conn, cell_matrix],
         )
-    own_inv = jnp.broadcast_to(inv_mass[..., None], inv_mass.shape + (width,))
-    own_pot = jnp.broadcast_to(potential[..., None], inv_mass.shape + (width,))
     parity = jnp.reshape(lax.axis_index("dy") % 2, (1,)).astype(jnp.int32)
 
     messages = [
@@ -345,11 +364,12 @@
 
     def exchange(corner, face, side):
         corner = swap_x(corner)
+        near, far, face = call(
+            functools.partial(side_kernel, sz), "sides", 0,
+            [like((sz.blocks, sz.gx, sz.ez, width), bf16)] * 2 + [face], [], [side, corner, face],
+            aliases={2: 2},
+        )
         face = swap_x(face)
-        near, far = call(
-            functools.partial(side_kernel, sz), "sides", 0,
-            [like((sz.blocks, sz.gx, sz.ez, width), bf16)] * 2, [], [side, corner],
-        )
         return (corner, face, *swap_y(near, far))
 
     x_ext, inv_b, pot_b, part, *sent = call(
@@ -372,11 +392,12 @@
         [parity, x_ext, y1, part, *exchange(*sent), inv_b, pot_b, *matrices], True,
     )
     corner = send(corner, 1, 0)
+    side, face = call(
+        functools.partial(last_side_kernel, sz), "last_side", 0,
+        [like((sz.blocks, sz.ex, sz.ez, width), bf16), face], [], [side, corner, face],
+        aliases={2: 1},
+    )
     face = send(face, 1, 0)
-    (side,) = call(
-        functools.partial(last_side_kernel, sz), "last_side", 0,
-        [like((sz.blocks, sz.ex, sz.ez, width), bf16)], [], [side, corner],
-    )
     side = send(side, 0, 1)
     filtered, rounded = call(
         functools.partial(last_kernel, sz), "last", 0,

time: 106 us -> 93.3 us (0.88)
  starting transfers between devices: 20.7 us -> 14.6 us
  other arithmetic: 5.79 us -> 0.66 us
  Pallas kernels: 22.2 us -> 18 us
  waiting for transfers between devices: 27.9 us -> 30.7 us
    ppermute x2, starting transfers between devices: 6.93 us -> 0.88 us  [swap_y(): far = lax.ppermute(far, 'dy', far_pairs)]
    ppermute x2, waiting for transfers between devices: 6.14 us -> 10.4 us  [swap_y(): far = lax.ppermute(far, 'dy', far_pairs)]
    pallas_call x9 -> x11, Pallas kernels: 22.2 us -> 18 us  [call(): pl.pallas_call(kernel, in_specs=specs, out_specs=[whole] * len(out_shape)...]
    unnamed x10 -> x0, other arithmetic: 3.72 us -> none
    ppermute x10, waiting for transfers between devices: 21.8 us -> 18.6 us  [send(): return lax.ppermute(value, ('dx', 'dy'), pairs)]
    unnamed x20 -> x34, local copies, waits for them, and re-layouts: 8.81 us -> 11.3 us
    slice x5 -> x0, local copies, waits for them, and re-layouts: 2.33 us -> none  [the longest x2 1.52 us: field_parts(): rest = fields[at]]
    ppermute x2, waiting for transfers between devices: 0.01 us -> 1.65 us  [swap_y(): near = lax.ppermute(near, 'dy', near_pairs)]
  transfers between devices with their start and end apart: 14 -> 14, of which waited for: 7 -> 9; matrix products, arithmetic and copies ran while one was open for 2% -> 0% of each run, Pallas kernels for 7% -> 8%
where the time goes in v2:
time: 93.3 us; the launch traced here: 92.9 us
  waiting for transfers between devices  30.7 us (33%)
  Pallas kernels  18 us (19%)
  local copies, waits for them, and re-layouts  14.7 us (16%)
  starting transfers between devices  14.6 us (16%)
  blocking collectives  12.6 us (14%)
    ppermute x10, waiting for transfers between devices, send(): return lax.ppermute(value, ('dx', 'dy'), pairs)  18.6 us
    pallas_call x11, Pallas kernels, call(): pl.pallas_call(kernel, in_specs=specs, out_specs=[whole] * len(out_shape)...  18 us
    ppermute x10, starting transfers between devices, send(): return lax.ppermute(value, ('dx', 'dy'), pairs)  13.8 us
    all_to_all x1, blocking collectives, body(): pieces = lax.all_to_all(local, 'dy', 0, 0)  12.6 us
    unnamed x34, local copies, waits for them, and re-layouts  11.3 us
    ppermute x2, waiting for transfers between devices, swap_y(): far = lax.ppermute(far, 'dy', far_pairs)  10.4 us
  transfers between devices with their start and end apart: 14, of which 9 were waited for; matrix products, arithmetic and copies ran while one was open for 0% of the time, Pallas kernels for 8%

profile of v2, /device:TPU:0, one launch (start us, length us, event | category | flops | bytes accessed | tf_op | source)
XLA Modules:
  0.0 92.9 jit_solution(7101739044935466052)
XLA Ops:
  0.6 0.8 slice_bitcast_fusion.2
  1.5 0.7 slice_bitcast_fusion.1
  2.2 0.9 slice_bitcast_fusion.vec_ref
  3.2 0.1 broadcast_in_dim.21.inv_ref
  3.3 0.1 pack_x.1
  3.4 3.0 %collective-permute-start = (bf16[3,16,16,128]{3,2,1,0:T(8,128)(2,1)S(1)}, bf16[3,16,16,128]{3,2,1,0:T(8,128)(2,1)S(1)}, u32[]{:S(2)}, u32[]{:S(2)}) collective-permute-start(bf16[3,16,16,128]{3,2,1,0:T(8,128)(2,1)S(1)} %pack_x.1), channel_id=1, source_target_pairs={{0,16},{1,17},{2,18},{3,19},{4,20},{5,21},{6,22},{7,23},{8,24},{9,... | collective-permute-start | bytes 589832 | tf_op jit(solution)/shard_map/ppermute | solution.py:54
  6.4 1.3 %copy-done.11 = bf16[729,729]{1,0:T(8,128)(2,1)S(1)} copy-done((bf16[729,729]{1,0:T(8,128)(2,1)S(1)}, bf16[729,729]{1,0:T(8,128)(2,1)}, u32[]{:S(2)}) %copy-start.11) | copy-done | bytes 1062906
  7.7 0.7 copy-done.13
  8.4 3.8 %order_cells.3.refs_1_ = bf16[2,736,768]{2,1,0:T(8,128)(2,1)S(1)} custom-call(s32[4,729]{1,0:T(4,128)S(1)} %bitcast.25, bf16[729,729]{1,0:T(8,128)(2,1)S(1)} %copy-done.11), custom_call_target="tpu_custom_call" | custom-call | flops 3623878656 | bytes 3335538 | tf_op jit(solution)/shard_map/order_cells/pallas_call | solution.py:303
  12.2 1.4 %copy-done.1 = bf16[2,736,768]{2,1,0:T(8,128)(2,1)} copy-done((bf16[2,736,768]{2,1,0:T(8,128)(2,1)}, bf16[2,736,768]{2,1,0:T(8,128)(2,1)S(1)}, u32[]{:S(2)}) %copy-start.1) | copy-done | bytes 2261016
  13.6 0.3 broadcast_in_dim.24.inv_ref.own_inv
  14.0 0.3 broadcast_in_dim.25.pot_ref.own_pot
  14.3 0.5 copy-done.9
  14.8 0.8 pack_y.1
  15.6 0.3 copy-done.7
  15.8 3.7 %collective-permute-start.1 = (bf16[3,9,16,128]{3,2,1,0:T(8,128)(2,1)}, bf16[3,9,16,128]{3,2,1,0:T(8,128)(2,1)S(1)}, u32[]{:S(2)}, u32[]{:S(2)}) collective-permute-start(bf16[3,9,16,128]{3,2,1,0:T(8,128)(2,1)} %pack_y.1), channel_id=1, source_target_pairs={{0,15},{1,0},{2,1},{3,2},{4,3},{5,4},{6,5},{7,6},{8,7},{9,8},{10,9... | collective-permute-start | bytes 331784 | tf_op jit(solution)/shard_map/ppermute | solution.py:54
  19.5 3.8 %order_cells.2.refs_0_ = bf16[2,736,768]{2,1,0:T(8,128)(2,1)S(1)} custom-call(s32[4,729]{1,0:T(4,128)S(1)} %bitcast.26, bf16[729,729]{1,0:T(8,128)(2,1)S(1)} %copy-done.12), custom_call_target="tpu_custom_call" | custom-call | flops 3623878656 | bytes 3335538 | tf_op jit(solution)/shard_map/order_cells/pallas_call | solution.py:303
  23.3 1.4 %copy-done.4 = bf16[2,736,768]{2,1,0:T(8,128)(2,1)} copy-done((bf16[2,736,768]{2,1,0:T(8,128)(2,1)}, bf16[2,736,768]{2,1,0:T(8,128)(2,1)S(1)}, u32[]{:S(2)}) %copy-start.4) | copy-done | bytes 2261016
  24.7 1.6 %copy-done.2 = bf16[2,736,768]{2,1,0:T(8,128)(2,1)S(1)} copy-done((bf16[2,736,768]{2,1,0:T(8,128)(2,1)S(1)}, bf16[2,736,768]{2,1,0:T(8,128)(2,1)}, u32[]{:S(2)}) %copy-start.2) | copy-done | bytes 2261016
  26.4 1.6 %copy-done.5 = bf16[2,736,768]{2,1,0:T(8,128)(2,1)S(1)} copy-done((bf16[2,736,768]{2,1,0:T(8,128)(2,1)S(1)}, bf16[2,736,768]{2,1,0:T(8,128)(2,1)}, u32[]{:S(2)}) %copy-start.5) | copy-done | bytes 2261016
  28.0 1.2 %copy-done.8 = f32[8,16,16,128]{3,2,1,0:T(8,128)S(1)} copy-done((f32[8,16,16,128]{3,2,1,0:T(8,128)S(1)}, f32[8,16,16,128]{3,2,1,0:T(8,128)}, u32[]{:S(2)}) %copy-start.8) | copy-done | bytes 1048600
  29.3 1.2 %copy-done.10 = bf16[2,8,16,16,128]{4,3,2,1,0:T(8,128)(2,1)S(1)} copy-done((bf16[2,8,16,16,128]{4,3,2,1,0:T(8,128)(2,1)S(1)}, bf16[2,8,16,16,128]{4,3,2,1,0:T(8,128)(2,1)}, u32[]{:S(2)}) %copy-start.10) | copy-done | bytes 1048600
  30.5 2.2 %first.1 = (bf16[2,9,17,16,128]{4,3,2,1,0:T(8,128)(2,1)S(1)}, f32[9,17,16,128]{3,2,1,0:T(8,128)S(1)}, f32[9,17,16,128]{3,2,1,0:T(8,128)S(1)}, f32[2,9,17,16,128]...) custom-call(s32[1]{0:T(128)} %bitcast.even_ref, ...), custom_call_target="tpu_custom_call" | custom-call | flops 1157627904 | bytes 14815236 | tf_op jit(solution)/shard_map/first/pallas_call | solution.py:303
  32.7 0.6 collective-permute-start.2
  33.2 3.8 %collective-permute-done.2.corner_ref.corner_in = bf16[2,2,2,16,128]{4,3,2,1,0:T(8,128)(2,1)S(1)} collective-permute-done((bf16[2,2,2,16,128]{4,3,2,1,0:T(8,128)(2,1)S(1)}, bf16[2,2,2,16,128]{4,3,2,1,0:T(8,128)(2,1)S(1)}, u32[]{:S(2)}, u32[]{:S(2)}) %collective-permute-start.2) | collective-permute-done | bytes 32800 | tf_op jit(solution)/shard_map/ppermute | solution.py:54
  37.1 0.6 collective-permute-start.3
  37.7 0.5 collective-permute-start.5
  38.2 0.7 collective-permute-done.4.near_in
  38.9 5.2 %collective-permute-done.5.far_in = bf16[2,9,16,128]{3,2,1,0:T(8,128)(2,1)S(1)} collective-permute-done((bf16[2,9,16,128]{3,2,1,0:T(8,128)(2,1)S(1)}, bf16[2,9,16,128]{3,2,1,0:T(8,128)(2,1)S(1)}, u32[]{:S(2)}, u32[]{:S(2)}) %collective-permute-start.5) | collective-permute-done | bytes 73760 | tf_op jit(solution)/shard_map/ppermute | solution.py:67
  44.1 2.5 %second.1 = (f32[2,9,17,16,128]{4,3,2,1,0:T(8,128)S(1)}, f32[2,9,17,16,128]{4,3,2,1,0:T(8,128)S(1)}, bf16[2,2,2,16,128]{4,3,2,1,0:T(8,128)(2,1)S(1)}, bf16[2,2,1...) custom-call(s32[1]{0:T(128)} %bitcast.even_ref, bf16[2,9,17,16,128]{4,3,2,1,0:T(8,128)(2,1)S(1)} %get-tuple-element.28.x_ref, ...), custom_call_target="tpu_custom_call" | custom-call | flops 1157627904 | bytes 16801796 | tf_op jit(solution)/shard_map/second/pallas_call | solution.py:303
  46.6 1.6 %collective-permute-start.6 = (bf16[2,2,2,16,128]{4,3,2,1,0:T(8,128)(2,1)S(1)}, bf16[2,2,2,16,128]{4,3,2,1,0:T(8,128)(2,1)S(1)}, u32[]{:S(2)}, u32[]{:S(2)}) collective-permute-start(bf16[2,2,2,16,128]{4,3,2,1,0:T(8,128)(2,1)S(1)} %get-tuple-element.40), channel_id=1, source_target_pairs={{0,16},{1,17},{2,18},{3,19},{4,20},{5,21},{6,22},{7,23},{8,24},{9,... | collective-permute-start | bytes 98312 | tf_op jit(solution)/shard_map/ppermute | solution.py:54
  48.2 2.8 %collective-permute-done.6.corner_ref.corner_in = bf16[2,2,2,16,128]{4,3,2,1,0:T(8,128)(2,1)S(1)} collective-permute-done((bf16[2,2,2,16,128]{4,3,2,1,0:T(8,128)(2,1)S(1)}, bf16[2,2,2,16,128]{4,3,2,1,0:T(8,128)(2,1)S(1)}, u32[]{:S(2)}, u32[]{:S(2)}) %collective-permute-start.6) | collective-permute-done | bytes 32800 | tf_op jit(solution)/shard_map/ppermute | solution.py:54
  51.0 1.6 %collective-permute-start.7 = (bf16[2,2,15,16,128]{4,3,2,1,0:T(8,128)(2,1)S(1)}, bf16[2,2,15,16,128]{4,3,2,1,0:T(8,128)(2,1)S(1)}, u32[]{:S(2)}, u32[]{:S(2)}) collective-permute-start(bf16[2,2,15,16,128]{4,3,2,1,0:T(8,128)(2,1)S(1)} %get-tuple-element.43), channel_id=1, source_target_pairs={{0,16},{1,17},{2,18},{3,19},{4,20},{5,21},{6,22},{7,23},{8,24},{9,... | collective-permute-start | bytes 737288 | tf_op jit(solution)/shard_map/ppermute | solution.py:54
  52.5 0.3 collective-permute-start.9
  52.9 0.9 %collective-permute-done.8.near_in = bf16[2,9,16,128]{3,2,1,0:T(8,128)(2,1)S(1)} collective-permute-done((bf16[2,9,16,128]{3,2,1,0:T(8,128)(2,1)S(1)}, bf16[2,9,16,128]{3,2,1,0:T(8,128)(2,1)S(1)}, u32[]{:S(2)}, u32[]{:S(2)}) %collective-permute-start.8) | collective-permute-done | bytes 73760 | tf_op jit(solution)/shard_map/ppermute | solution.py:68
  53.8 5.2 %collective-permute-done.9.far_in = bf16[2,9,16,128]{3,2,1,0:T(8,128)(2,1)S(1)} collective-permute-done((bf16[2,9,16,128]{3,2,1,0:T(8,128)(2,1)S(1)}, bf16[2,9,16,128]{3,2,1,0:T(8,128)(2,1)S(1)}, u32[]{:S(2)}, u32[]{:S(2)}) %collective-permute-start.9) | collective-permute-done | bytes 73760 | tf_op jit(solution)/shard_map/ppermute | solution.py:67
  59.0 3.3 %third.1 = (f32[2,8,16,16,128]{4,3,2,1,0:T(8,128)S(1)}, bf16[2,16,128]{2,1,0:T(8,128)(2,1)S(1)}, bf16[2,16,16,128]{3,2,1,0:T(8,128)(2,1)S(1)}, f32[2,8,16,128]{3,2,1,0:T(8,128)S(1)}) custom-call(s32[1]{0:T(128)} %bitcast.even_ref, bf16[2,9,17,16,128]{4,3,2,1,0:T(8,128)(2,1)S(1)} %get-tuple-element.28.x_ref, ...), custom_call_target="tpu_custom_call" | custom-call | flops 1157627904 | bytes 16089092 | tf_op jit(solution)/shard_map/third/pallas_call | solution.py:303
  62.3 0.6 collective-permute-start.10
  62.9 3.2 %collective-permute-done.10.corner_ref = bf16[2,16,128]{2,1,0:T(8,128)(2,1)S(1)} collective-permute-done((bf16[2,16,128]{2,1,0:T(8,128)(2,1)S(1)}, bf16[2,16,128]{2,1,0:T(8,128)(2,1)S(1)}, u32[]{:S(2)}, u32[]{:S(2)}) %collective-permute-start.10) | collective-permute-done | bytes 8224 | tf_op jit(solution)/shard_map/ppermute | solution.py:54
  66.1 0.6 collective-permute-start.11
  66.7 6.4 %collective-permute-done.12.side = bf16[2,8,16,128]{3,2,1,0:T(8,128)(2,1)S(1)} collective-permute-done((bf16[2,8,16,128]{3,2,1,0:T(8,128)(2,1)S(1)}, bf16[2,8,16,128]{3,2,1,0:T(8,128)(2,1)S(1)}, u32[]{:S(2)}, u32[]{:S(2)}) %collective-permute-start.12) | collective-permute-done | bytes 65568 | tf_op jit(solution)/shard_map/ppermute | solution.py:54
  73.1 1.6 %last.1 = (f32[2,8,16,16,128]{4,3,2,1,0:T(8,128)}, bf16[8,16,16,256]{3,2,1,0:T(8,128)(2,1)S(1)}) custom-call(f32[2,8,16,16,128]{4,3,2,1,0:T(8,128)S(1)} %get-tuple-element.46.part_ref, bf16[2,16,16,128]{3,2,1,0:T(8,128)(2,1)S(1)} %collective-permute-done.11.face, bf16[2,8,16,128]{3,2,1,0:T(8,128)(2,1)S(1)} %collective-permute-done.12.side, ...), custom_call_target="tpu_custom_call" | custom-call | bytes 6692864 | tf_op jit(solution)/shard_map/last/pallas_call | solution.py:303
  74.7 0.7 fusion.2
  75.4 0.1 copy.13
  75.6 12.6 %all_to_all.5 = bf16[16,32,256]{2,1,0:T(8,128)(2,1)S(1)} all-to-all(bf16[16,32,256]{2,1,0:T(8,128)(2,1)S(1)} %bitcast.27), channel_id=1, replica_groups=mesh['dx'=2,'dy'=16] {'dy'}, dimensions={0} | all-to-all | bytes 524288 | tf_op jit(solution)/shard_map/all_to_all | solution.py:412
  88.3 1.6 %collective-permute-start.13 = (f32[32,256]{1,0:T(8,128)S(1)}, f32[32,256]{1,0:T(8,128)S(1)}, u32[]{:S(2)}, u32[]{:S(2)}) collective-permute-start(f32[32,256]{1,0:T(8,128)S(1)} %convert_reduce_fusion), channel_id=1, source_target_pairs={{0,16},{1,17},{2,18},{3,19},{4,20},{5,21},{6,22},{7,23},{8,24},{9,... | collective-permute-start | bytes 98312 | tf_op jit(solution)/shard_map/ppermute | solution.py:54
  89.8 2.4 %collective-permute-done.13 = f32[32,256]{1,0:T(8,128)S(1)} collective-permute-done((f32[32,256]{1,0:T(8,128)S(1)}, f32[32,256]{1,0:T(8,128)S(1)}, u32[]{:S(2)}, u32[]{:S(2)}) %collective-permute-start.13) | collective-permute-done | bytes 32800 | tf_op jit(solution)/shard_map/ppermute | solution.py:54
  92.2 0.6 add.8
  (37 shorter events, 0.3 us)
Async XLA Ops:
  0.6 74.1 %copy-start = (bf16[8,16,16,512]{3,2,1,0:T(8,128)(2,1)S(1)}, bf16[8,16,16,512]{3,2,1,0:T(8,128)(2,1)}, u32[]{:S(2)}) copy-start(bf16[8,16,16,512]{3,2,1,0:T(8,128)(2,1)} %param.7) | copy-start | bytes 6291460
  3.4 10.2 %collective-permute-start = (bf16[3,16,16,128]{3,2,1,0:T(8,128)(2,1)S(1)}, bf16[3,16,16,128]{3,2,1,0:T(8,128)(2,1)S(1)}, u32[]{:S(2)}, u32[]{:S(2)}) collective-permute-start(bf16[3,16,16,128]{3,2,1,0:T(8,128)(2,1)S(1)} %pack_x.1), channel_id=1, source_target_pairs={{0,16},{1,17},{2,18},{3,19},{4,20},{5,21},{6,22},{7,23},{8,24},{9,... | collective-permute-start | bytes 589832 | tf_op jit(solution)/shard_map/ppermute | solution.py:54
  6.4 1.3 %copy-start.11 = (bf16[729,729]{1,0:T(8,128)(2,1)S(1)}, bf16[729,729]{1,0:T(8,128)(2,1)}, u32[]{:S(2)}) copy-start(bf16[729,729]{1,0:T(8,128)(2,1)} %matrix_ref.3) | copy-start | bytes 3188650
  7.7 0.7 copy-start.13
  8.4 5.2 %copy-start.15 = (f32[8,16,16]{2,1,0:T(8,128)S(1)}, f32[8,16,16]{2,1,0:T(8,128)}, u32[]{:S(2)}) copy-start(f32[8,16,16]{2,1,0:T(8,128)} %param.8) | copy-start | bytes 24580
  8.4 5.6 %copy-start.16 = (f32[8,16,16]{2,1,0:T(8,128)S(1)}, f32[8,16,16]{2,1,0:T(8,128)}, u32[]{:S(2)}) copy-start(f32[8,16,16]{2,1,0:T(8,128)} %param.9) | copy-start | bytes 24580
  12.2 1.4 %copy-start.1 = (bf16[2,736,768]{2,1,0:T(8,128)(2,1)}, bf16[2,736,768]{2,1,0:T(8,128)(2,1)S(1)}, u32[]{:S(2)}) copy-start(bf16[2,736,768]{2,1,0:T(8,128)(2,1)S(1)} %order_cells.3.refs_1_) | copy-start | bytes 6782980
  13.6 1.2 %copy-start.9 = (bf16[2,8,16,16,128]{4,3,2,1,0:T(8,128)(2,1)S(1)}, bf16[2,8,16,16,128]{4,3,2,1,0:T(8,128)(2,1)}, u32[]{:S(2)}) copy-start(bf16[2,8,16,16,128]{4,3,2,1,0:T(8,128)(2,1)} %vec_ref.3) | copy-start | bytes 3145732
  14.0 5.6 %copy-start.12 = (bf16[729,729]{1,0:T(8,128)(2,1)S(1)}, bf16[729,729]{1,0:T(8,128)(2,1)}, u32[]{:S(2)}) copy-start(bf16[729,729]{1,0:T(8,128)(2,1)} %matrix_ref.3) | copy-start | bytes 3188650
  14.0 5.6 %copy-start.14 = (s32[1,1,4,729]{3,2,1,0:T(4,128)S(1)}, s32[1,1,4,729]{3,2,1,0:T(4,128)}, u32[]{:S(2)}) copy-start(s32[1,1,4,729]{3,2,1,0:T(4,128)} %param.11) | copy-start | bytes 34996
  14.8 1.0 %copy-start.7 = (f32[8,16,16,128]{3,2,1,0:T(8,128)}, f32[8,16,16,128]{3,2,1,0:T(8,128)S(1)}, u32[]{:S(2)}) copy-start(f32[8,16,16,128]{3,2,1,0:T(8,128)S(1)} %broadcast_in_dim.25.pot_ref.own_pot) | copy-start | bytes 3145732
  15.8 8.9 %collective-permute-start.1 = (bf16[3,9,16,128]{3,2,1,0:T(8,128)(2,1)}, bf16[3,9,16,128]{3,2,1,0:T(8,128)(2,1)S(1)}, u32[]{:S(2)}, u32[]{:S(2)}) collective-permute-start(bf16[3,9,16,128]{3,2,1,0:T(8,128)(2,1)} %pack_y.1), channel_id=1, source_target_pairs={{0,15},{1,0},{2,1},{3,2},{4,3},{5,4},{6,5},{7,6},{8,7},{9,8},{10,9... | collective-permute-start | bytes 331784 | tf_op jit(solution)/shard_map/ppermute | solution.py:54
  23.3 1.4 %copy-start.4 = (bf16[2,736,768]{2,1,0:T(8,128)(2,1)}, bf16[2,736,768]{2,1,0:T(8,128)(2,1)S(1)}, u32[]{:S(2)}) copy-start(bf16[2,736,768]{2,1,0:T(8,128)(2,1)S(1)} %order_cells.2.refs_0_) | copy-start | bytes 6782980
  24.7 1.6 %copy-start.2 = (bf16[2,736,768]{2,1,0:T(8,128)(2,1)S(1)}, bf16[2,736,768]{2,1,0:T(8,128)(2,1)}, u32[]{:S(2)}) copy-start(bf16[2,736,768]{2,1,0:T(8,128)(2,1)} %copy-done.1) | copy-start | bytes 6782980
  26.4 1.6 %copy-start.5 = (bf16[2,736,768]{2,1,0:T(8,128)(2,1)S(1)}, bf16[2,736,768]{2,1,0:T(8,128)(2,1)}, u32[]{:S(2)}) copy-start(bf16[2,736,768]{2,1,0:T(8,128)(2,1)} %copy-done.4) | copy-start | bytes 6782980
  28.0 1.2 %copy-start.8 = (f32[8,16,16,128]{3,2,1,0:T(8,128)S(1)}, f32[8,16,16,128]{3,2,1,0:T(8,128)}, u32[]{:S(2)}) copy-start(f32[8,16,16,128]{3,2,1,0:T(8,128)} %copy-done.7) | copy-start | bytes 3145732
  29.2 1.2 %copy-start.10 = (bf16[2,8,16,16,128]{4,3,2,1,0:T(8,128)(2,1)S(1)}, bf16[2,8,16,16,128]{4,3,2,1,0:T(8,128)(2,1)}, u32[]{:S(2)}) copy-start(bf16[2,8,16,16,128]{4,3,2,1,0:T(8,128)(2,1)} %vec_ref.3) | copy-start | bytes 3145732
  30.5 13.7 %copy-start.3 = (bf16[2,736,768]{2,1,0:T(8,128)(2,1)S(1)}, bf16[2,736,768]{2,1,0:T(8,128)(2,1)}, u32[]{:S(2)}) copy-start(bf16[2,736,768]{2,1,0:T(8,128)(2,1)} %copy-done.1) | copy-start | bytes 6782980
  30.5 13.7 %copy-start.6 = (bf16[2,736,768]{2,1,0:T(8,128)(2,1)S(1)}, bf16[2,736,768]{2,1,0:T(8,128)(2,1)}, u32[]{:S(2)}) copy-start(bf16[2,736,768]{2,1,0:T(8,128)(2,1)} %copy-done.4) | copy-start | bytes 6782980
  32.7 4.4 %collective-permute-start.2 = (bf16[2,2,2,16,128]{4,3,2,1,0:T(8,128)(2,1)S(1)}, bf16[2,2,2,16,128]{4,3,2,1,0:T(8,128)(2,1)S(1)}, u32[]{:S(2)}, u32[]{:S(2)}) collective-permute-start(bf16[2,2,2,16,128]{4,3,2,1,0:T(8,128)(2,1)S(1)} %get-tuple-element.30), channel_id=1, source_target_pairs={{0,16},{1,17},{2,18},{3,19},{4,20},{5,21},{6,22},{7,23},{8,24},{9,... | collective-permute-start | bytes 98312 | tf_op jit(solution)/shard_map/ppermute | solution.py:54
  37.1 7.1 %collective-permute-start.3 = (bf16[2,2,15,16,128]{4,3,2,1,0:T(8,128)(2,1)S(1)}, bf16[2,2,15,16,128]{4,3,2,1,0:T(8,128)(2,1)S(1)}, u32[]{:S(2)}, u32[]{:S(2)}) collective-permute-start(bf16[2,2,15,16,128]{4,3,2,1,0:T(8,128)(2,1)S(1)} %get-tuple-element.33), channel_id=1, source_target_pairs={{0,16},{1,17},{2,18},{3,19},{4,20},{5,21},{6,22},{7,23},{8,24},{9,... | collective-permute-start | bytes 737288 | tf_op jit(solution)/shard_map/ppermute | solution.py:54
  37.7 1.3 %collective-permute-start.4 = (bf16[2,9,16,128]{3,2,1,0:T(8,128)(2,1)S(1)}, bf16[2,9,16,128]{3,2,1,0:T(8,128)(2,1)S(1)}, u32[]{:S(2)}, u32[]{:S(2)}) collective-permute-start(bf16[2,9,16,128]{3,2,1,0:T(8,128)(2,1)S(1)} %get-tuple-element.34), channel_id=1, source_target_pairs={{0,1},{1,0},{2,3},{3,2},{4,5},{5,4},{6,7},{7,6},{8,9},{9,8},{10,11... | collective-permute-start | bytes 221192 | tf_op jit(solution)/shard_map/ppermute | solution.py:68
  37.7 6.5 %collective-permute-start.5 = (bf16[2,9,16,128]{3,2,1,0:T(8,128)(2,1)S(1)}, bf16[2,9,16,128]{3,2,1,0:T(8,128)(2,1)S(1)}, u32[]{:S(2)}, u32[]{:S(2)}) collective-permute-start(bf16[2,9,16,128]{3,2,1,0:T(8,128)(2,1)S(1)} %get-tuple-element.35), channel_id=1, source_target_pairs={{0,15},{1,2},{2,1},{3,4},{4,3},{5,6},{6,5},{7,8},{8,7},{9,10},{10,... | collective-permute-start | bytes 221192 | tf_op jit(solution)/shard_map/ppermute | solution.py:67
  46.6 4.3 %collective-permute-start.6 = (bf16[2,2,2,16,128]{4,3,2,1,0:T(8,128)(2,1)S(1)}, bf16[2,2,2,16,128]{4,3,2,1,0:T(8,128)(2,1)S(1)}, u32[]{:S(2)}, u32[]{:S(2)}) collective-permute-start(bf16[2,2,2,16,128]{4,3,2,1,0:T(8,128)(2,1)S(1)} %get-tuple-element.40), channel_id=1, source_target_pairs={{0,16},{1,17},{2,18},{3,19},{4,20},{5,21},{6,22},{7,23},{8,24},{9,... | collective-permute-start | bytes 98312 | tf_op jit(solution)/shard_map/ppermute | solution.py:54
  51.0 8.0 %collective-permute-start.7 = (bf16[2,2,15,16,128]{4,3,2,1,0:T(8,128)(2,1)S(1)}, bf16[2,2,15,16,128]{4,3,2,1,0:T(8,128)(2,1)S(1)}, u32[]{:S(2)}, u32[]{:S(2)}) collective-permute-start(bf16[2,2,15,16,128]{4,3,2,1,0:T(8,128)(2,1)S(1)} %get-tuple-element.43), channel_id=1, source_target_pairs={{0,16},{1,17},{2,18},{3,19},{4,20},{5,21},{6,22},{7,23},{8,24},{9,... | collective-permute-start | bytes 737288 | tf_op jit(solution)/shard_map/ppermute | solution.py:54
  52.5 1.3 %collective-permute-start.8 = (bf16[2,9,16,128]{3,2,1,0:T(8,128)(2,1)S(1)}, bf16[2,9,16,128]{3,2,1,0:T(8,128)(2,1)S(1)}, u32[]{:S(2)}, u32[]{:S(2)}) collective-permute-start(bf16[2,9,16,128]{3,2,1,0:T(8,128)(2,1)S(1)} %get-tuple-element.44), channel_id=1, source_target_pairs={{0,1},{1,0},{2,3},{3,2},{4,5},{5,4},{6,7},{7,6},{8,9},{9,8},{10,11... | collective-permute-start | bytes 221192 | tf_op jit(solution)/shard_map/ppermute | solution.py:68
  52.5 6.5 %collective-permute-start.9 = (bf16[2,9,16,128]{3,2,1,0:T(8,128)(2,1)S(1)}, bf16[2,9,16,128]{3,2,1,0:T(8,128)(2,1)S(1)}, u32[]{:S(2)}, u32[]{:S(2)}) collective-permute-start(bf16[2,9,16,128]{3,2,1,0:T(8,128)(2,1)S(1)} %get-tuple-element.45), channel_id=1, source_target_pairs={{0,15},{1,2},{2,1},{3,4},{4,3},{5,6},{6,5},{7,8},{8,7},{9,10},{10,... | collective-permute-start | bytes 221192 | tf_op jit(solution)/shard_map/ppermute | solution.py:67
  62.3 3.8 %collective-permute-start.10 = (bf16[2,16,128]{2,1,0:T(8,128)(2,1)S(1)}, bf16[2,16,128]{2,1,0:T(8,128)(2,1)S(1)}, u32[]{:S(2)}, u32[]{:S(2)}) collective-permute-start(bf16[2,16,128]{2,1,0:T(8,128)(2,1)S(1)} %get-tuple-element.48), channel_id=1, source_target_pairs={{0,16},{1,17},{2,18},{3,19},{4,20},{5,21},{6,22},{7,23},{8,24},{9,... | collective-permute-start | bytes 24584 | tf_op jit(solution)/shard_map/ppermute | solution.py:54
  66.1 7.0 %collective-permute-start.11 = (bf16[2,16,16,128]{3,2,1,0:T(8,128)(2,1)S(1)}, bf16[2,16,16,128]{3,2,1,0:T(8,128)(2,1)S(1)}, u32[]{:S(2)}, u32[]{:S(2)}) collective-permute-start(bf16[2,16,16,128]{3,2,1,0:T(8,128)(2,1)S(1)} %get-tuple-element.50), channel_id=1, source_target_pairs={{0,16},{1,17},{2,18},{3,19},{4,20},{5,21},{6,22},{7,23},{8,24},{9,... | collective-permute-start | bytes 393224 | tf_op jit(solution)/shard_map/ppermute | solution.py:54
  66.7 6.4 %collective-permute-start.12 = (bf16[2,8,16,128]{3,2,1,0:T(8,128)(2,1)S(1)}, bf16[2,8,16,128]{3,2,1,0:T(8,128)(2,1)S(1)}, u32[]{:S(2)}, u32[]{:S(2)}) collective-permute-start(bf16[2,8,16,128]{3,2,1,0:T(8,128)(2,1)S(1)} %get-tuple-element.51), channel_id=1, source_target_pairs={{0,1},{1,2},{2,3},{3,4},{4,5},{5,6},{6,7},{7,8},{8,9},{9,10},{10,1... | collective-permute-start | bytes 196616 | tf_op jit(solution)/shard_map/ppermute | solution.py:54
  88.3 4.0 %collective-permute-start.13 = (f32[32,256]{1,0:T(8,128)S(1)}, f32[32,256]{1,0:T(8,128)S(1)}, u32[]{:S(2)}, u32[]{:S(2)}) collective-permute-start(f32[32,256]{1,0:T(8,128)S(1)} %convert_reduce_fusion), channel_id=1, source_target_pairs={{0,16},{1,17},{2,18},{3,19},{4,20},{5,21},{6,22},{7,23},{8,24},{9,... | collective-permute-start | bytes 98312 | tf_op jit(solution)/shard_map/ppermute | solution.py:54

commit v3 on v2

--- a/solution.py
+++ b/solution.py
@@ -10,7 +10,7 @@
 
 LANES = 128
 SUB = 16
-VMEM_LIMIT = 28 * 1024 * 1024
+VMEM_LIMIT = 16 * 1024 * 1024
 
 center_shift = 1.2
 half_width = 2.0
@@ -21,10 +21,11 @@
 
 
 class Sizes:
-    def __init__(self, vectors, inv_mass, connectivity):
+    def __init__(self, vectors, resident, inv_mass, connectivity):
         self.blocks = vectors.shape[0]
         self.width = vectors.shape[-1]
         self.full = self.blocks * self.width
+        self.groups = resident.shape[-1] // LANES
         self.ex, self.ey, self.ez = inv_mass.shape
         self.cells, self.nodes = connectivity.shape[2:]
         self.n1 = round(self.nodes ** (1.0 / 3.0))
@@ -129,8 +130,8 @@
     near = jnp.where(even, end_y, 0)
     for slot, j in enumerate((near, end_y - near)):
         for b in range(sz.blocks):
-            corner[0, slot, b] = acc_ref[b, 0, j].astype(corner.dtype)
-            corner[1, slot, b] = acc_ref[b, end_x, j].astype(corner.dtype)
+            corner[0, slot * sz.blocks + b] = acc_ref[b, 0, j].astype(corner.dtype)
+            corner[1, slot * sz.blocks + b] = acc_ref[b, end_x, j].astype(corner.dtype)
             side[slot, b] = acc_ref[b, :, j]
     for b in range(sz.blocks):
         face[0, b] = acc_ref[b, 0, 1:end_y].astype(face.dtype)
@@ -140,12 +141,13 @@
 def side_kernel(sz, side_ref, corner_ref, face_in, near_ref, far_ref, face_out):
     del face_in, face_out
     for slot, out in enumerate((near_ref, far_ref)):
+        pair = slice(slot * sz.blocks, (slot + 1) * sz.blocks)
         for i in range(sz.gx):
             value = side_ref[slot, :, i]
             if i == 0:
-                value = value + corner_ref[1, slot].astype(jnp.float32)
+                value = value + corner_ref[1, pair].astype(jnp.float32)
             if i == sz.gx - 1:
-                value = value + corner_ref[0, slot].astype(jnp.float32)
+                value = value + corner_ref[0, pair].astype(jnp.float32)
             out[:, i] = value.astype(out.dtype)
 
 
@@ -158,7 +160,8 @@
         is_near = even if j == end_y else jnp.logical_not(even)
         if side is not None:
             total = total + jnp.where(
-                is_near, corner[side, 0].astype(f32), corner[side, 1].astype(f32)
+                is_near, corner[side, : sz.blocks].astype(f32),
+                corner[side, sz.blocks : 2 * sz.blocks].astype(f32),
             )
         total = total + jnp.where(is_near, near[:, i].astype(f32), far[:, i].astype(f32))
     elif side is not None:
@@ -177,22 +180,86 @@
     return row.astype(jnp.bfloat16)
 
 
-def pack_x_kernel(sz, vec_ref, inv_ref, pot_ref, out_ref):
-    out_ref[: sz.blocks] = vec_ref[...]
-    out_ref[sz.blocks] = field_row(inv_ref[...], pot_ref[...])
-
-
-def pack_y_kernel(sz, vec_ref, inv_ref, pot_ref, from_x, out_ref):
-    out_ref[: sz.blocks, : sz.ex] = vec_ref[:, :, 0]
-    out_ref[sz.blocks, : sz.ex] = field_row(inv_ref[:, 0], pot_ref[:, 0])
-    out_ref[:, sz.ex] = from_x[:, 0]
+def field_rows(sz, inv, pot, count):
+    inv, pot = inv.T, pot.T
+    shape = (sz.ez, sz.width)
+    for at in range(count):
+        yield at, field_row(
+            jnp.broadcast_to(inv[:, at : at + 1], shape), jnp.broadcast_to(pot[:, at : at + 1], shape)
+        )
+
+
+def pack_x_kernel(
+    sz, vec_hbm, inv_hbm, pot_hbm, mat_hbm, conn_hbm, out_ref, mat_ref, conn_ref, field_ref, sems
+):
+    loads = [
+        pltpu.make_async_copy(mat_hbm, mat_ref, sems.at[2 + sz.blocks]),
+        pltpu.make_async_copy(conn_hbm, conn_ref, sems.at[3 + sz.blocks]),
+    ]
+    copies = [
+        pltpu.make_async_copy(inv_hbm.at[0], field_ref.at[0], sems.at[0]),
+        pltpu.make_async_copy(pot_hbm.at[0], field_ref.at[1], sems.at[1]),
+    ]
+    for b in range(sz.blocks):
+        copies.append(pltpu.make_async_copy(vec_hbm.at[b, 0], out_ref.at[b], sems.at[2 + b]))
+    copies += loads
+    for copy in copies:
+        copy.start()
+    for copy in copies[:2]:
+        copy.wait()
+    for j, row in field_rows(sz, field_ref[0], field_ref[1], sz.ey):
+        out_ref[sz.blocks, j] = row
+    for copy in copies[2:]:
+        copy.wait()
+
+
+def pack_y_kernel(sz, vec_hbm, res_hbm, inv_hbm, pot_hbm, from_x, out_ref, res_ref, field_ref, sems):
+    base = (sz.blocks + 1) * sz.gx
+    copies = [
+        pltpu.make_async_copy(inv_hbm.at[:, 0], field_ref.at[0], sems.at[0]),
+        pltpu.make_async_copy(pot_hbm.at[:, 0], field_ref.at[1], sems.at[1]),
+        pltpu.make_async_copy(res_hbm.at[0], res_ref, sems.at[2]),
+    ]
+    for b in range(sz.blocks):
+        rows = pl.ds(b * sz.gx, sz.ex)
+        copies.append(pltpu.make_async_copy(vec_hbm.at[b, :, 0], out_ref.at[rows], sems.at[3 + b]))
+    for g in range(sz.groups):
+        rows = pl.ds(base + g * sz.ex, sz.ex)
+        lanes = pl.ds(g * LANES, LANES)
+        copies.append(
+            pltpu.make_async_copy(
+                res_hbm.at[:, 0, :, lanes], out_ref.at[rows], sems.at[3 + sz.blocks + g]
+            )
+        )
+    for copy in copies:
+        copy.start()
+    for copy in copies[:2]:
+        copy.wait()
+    for i, row in field_rows(sz, field_ref[0], field_ref[1], sz.ex):
+        out_ref[sz.blocks * sz.gx + i] = row
+    for b in range(sz.blocks + 1):
+        out_ref[b * sz.gx + sz.ex] = from_x[b, 0]
+    for copy in copies[2:]:
+        copy.wait()
+
+
+def resident_rows_kernel(sz, from_y, corner, out_ref):
+    base = (sz.blocks + 1) * sz.gx
+    for g in range(sz.groups):
+        lanes = slice(g * LANES, (g + 1) * LANES)
+        for i in range(sz.ex):
+            out_ref[i, :, lanes] = from_y[base + g * sz.ex + i]
+        out_ref[sz.ex, :, lanes] = corner[0, 2 * sz.blocks + g]
 
 
 def first_kernel(
-    sz, n_mat, even_ref, vec_ref, from_x, from_y, own_inv, own_pot, *refs
+    sz, n_mat, even_ref, vec_ref, from_x, from_y, own_inv, own_pot, res_in, *refs
 ):
+    del res_in
     mats = refs[:n_mat]
-    x_ref, inv_ref, pot_ref, acc_ref, corner, face, side, u_ref, rhs_ref, edge_ref = refs[n_mat:]
+    res_out, x_ref, inv_ref, pot_ref, acc_ref, corner, face, side = refs[n_mat : n_mat + 8]
+    u_ref, rhs_ref, edge_ref = refs[n_mat + 8 :]
+    del res_out
     even = even_ref[0] == 0
     inv_ref[: sz.ex, : sz.ey] = own_inv[...]
     pot_ref[: sz.ex, : sz.ey] = own_pot[...]
@@ -207,16 +274,21 @@
         for ref, value in fields(from_x[sz.blocks, j]):
             ref[sz.ex, j] = value
     for i in range(sz.gx):
-        for ref, value in fields(from_y[sz.blocks, i]):
+        for ref, value in fields(from_y[sz.blocks * sz.gx + i]):
             ref[i, sz.ey] = value
     x_ref[:, : sz.ex, : sz.ey] = vec_ref[...]
     x_ref[:, sz.ex, : sz.ey] = from_x[: sz.blocks]
-    x_ref[:, :, sz.ey] = from_y[: sz.blocks]
+    for b in range(sz.blocks):
+        x_ref[b, :, sz.ey] = from_y[b * sz.gx : (b + 1) * sz.gx]
     for i in range(sz.gx):
         for j in range(sz.gy):
             u_ref[:, i, j] = x_ref[:, i, j].astype(jnp.float32) * inv_ref[i, j]
     cell_products(sz, u_ref, mats, rhs_ref, edge_ref, acc_ref)
     write_messages(sz, even, acc_ref, corner, face, side)
+    base = (sz.blocks + 1) * sz.gx
+    for g in range(sz.groups):
+        corner[0, 2 * sz.blocks + g] = from_y[base + g * sz.ex]
+        corner[1, 2 * sz.blocks + g] = jnp.zeros((sz.ez, sz.width), corner.dtype)
 
 
 def second_kernel(
@@ -238,12 +310,18 @@
     write_messages(sz, even, acc_ref, corner, face, side)
 
 
+def put_lanes(sz, ref, at, value):
+    for b in range(sz.blocks):
+        ref[at, :, b * sz.width : (b + 1) * sz.width] = value[b]
+
+
 def third_kernel(
     sz, n_mat, even_ref, x_ref, y_ref, sum_ref, corner_in, face_in, near_in, far_in, inv_ref, pot_ref,
     *refs,
 ):
     mats = refs[:n_mat]
-    part_ref, corner, face, side, new_ref, acc_ref, u_ref, rhs_ref, edge_ref = refs[n_mat:]
+    part_ref, corner, face, side, own_rows, face_rows, side_rows = refs[n_mat : n_mat + 7]
+    new_ref, acc_ref, u_ref, rhs_ref, edge_ref = refs[n_mat + 7 :]
     even = even_ref[0] == 0
     for i in range(sz.gx):
         for j in range(sz.gy):
@@ -255,14 +333,27 @@
             new_ref[:, i, j] = new
             u_ref[:, i, j] = inv * new
     cell_products(sz, u_ref, mats, rhs_ref, edge_ref, acc_ref)
-    corner[...] = acc_ref[:, sz.ex, sz.ey].astype(corner.dtype)
-    face[...] = acc_ref[:, sz.ex, : sz.ey].astype(face.dtype)
-    side[...] = acc_ref[:, : sz.ex, sz.ey].astype(side.dtype)
-    for i in range(sz.ex):
-        for j in range(sz.ey):
-            new = new_ref[:, i, j]
-            image = inv_ref[i, j] * acc_ref[:, i, j] + pot_ref[i, j] * new
-            part_ref[:, i, j] = 2.0 * (image - center_shift * new) / half_width - y_ref[:, i, j]
+    gain = 2.0 / half_width
+    for i in range(sz.gx):
+        for j in range(sz.gy):
+            if i == sz.ex or j == sz.ey:
+                value = gain * (inv_ref[i, j] * acc_ref[:, i, j])
+                rounded = value.astype(face.dtype)
+                if j == sz.ey:
+                    put_lanes(sz, side_rows, i, rounded)
+                    if i == sz.ex:
+                        corner[...] = rounded
+                    else:
+                        side[:, i] = value
+                else:
+                    put_lanes(sz, face_rows, j, rounded)
+                    face[:, j] = rounded
+            else:
+                new = new_ref[:, i, j]
+                image = inv_ref[i, j] * acc_ref[:, i, j] + pot_ref[i, j] * new
+                value = 2.0 * (image - center_shift * new) / half_width - y_ref[:, i, j]
+                part_ref[:, i, j] = value
+                put_lanes(sz, own_rows, i * sz.ey + j, value.astype(face.dtype))
 
 
 def last_side_kernel(sz, side_ref, corner_ref, face_in, out_ref, face_out):
@@ -274,8 +365,7 @@
         out_ref[:, i] = value.astype(out_ref.dtype)
 
 
-def last_kernel(sz, part_ref, face, side, inv_ref, out_ref, rounded_ref):
-    gain = 2.0 / half_width
+def last_kernel(sz, part_ref, face, side, out_ref):
     for i in range(sz.ex):
         for j in range(sz.ey):
             value = part_ref[:, i, j]
@@ -286,20 +376,21 @@
                 term = side[:, i].astype(jnp.float32)
                 more = term if more is None else more + term
             if more is not None:
-                value = value + gain * (inv_ref[i, j] * more)
-            for b in range(sz.blocks):
-                lanes = slice(b * sz.width, (b + 1) * sz.width)
-                rounded_ref[i, j, :, lanes] = value[b].astype(jnp.bfloat16)
+                value = value + more
             out_ref[:, i, j] = value
 
 
-def call(kernel, name, flops, out_shape, scratch, operands, scalar_first=False, aliases=None):
+def call(kernel, name, flops, out_shape, scratch, operands, scalar_first=False, aliases=None,
+         hbm=0):
     out_shape = [jax.ShapeDtypeStruct(s.shape, s.dtype) for s in out_shape]
     size = sum(math.prod(s.shape) * jnp.dtype(s.dtype).itemsize for s in (*operands, *out_shape))
     whole = pl.BlockSpec(memory_space=pltpu.VMEM)
-    specs = [whole] * len(operands)
+    specs = [pl.BlockSpec(memory_space=pltpu.HBM)] * hbm + [whole] * (len(operands) - hbm)
     if scalar_first:
         specs[0] = pl.BlockSpec(memory_space=pltpu.SMEM)
+    operands = [pltpu.with_memory_space_constraint(a, pltpu.HBM) for a in operands[:hbm]] + list(
+        operands[hbm:]
+    )
     return pl.pallas_call(
         kernel,
         in_specs=specs,
@@ -314,7 +405,7 @@
 
 
 def body(vectors, resident, inv_mass, potential, cell_matrix, connectivity):
-    sz = Sizes(vectors, inv_mass, connectivity)
+    sz = Sizes(vectors, resident, inv_mass, connectivity)
     bf16, f32 = jnp.bfloat16, jnp.float32
     nx, ny = lax.axis_size("dx"), lax.axis_size("dy")
     norm_scale = 1.0 / math.sqrt(sz.ex * sz.ey * sz.ez * nx * ny)
@@ -325,19 +416,29 @@
 
     own_inv = jnp.broadcast_to(inv_mass[..., None], inv_mass.shape + (width,))
     own_pot = jnp.broadcast_to(potential[..., None], inv_mass.shape + (width,))
-    (to_x,) = call(
+    conn = connectivity.reshape(sz.cells, sz.nodes)
+    to_x, cell_matrix, conn = call(
         functools.partial(pack_x_kernel, sz), "pack_x", 0,
-        [like((sz.blocks + 1, sz.ey, sz.ez, width), bf16)], [],
-        [vectors[:, 0], own_inv[0], own_pot[0]],
+        [like((sz.blocks + 1, sz.ey, sz.ez, width), bf16), cell_matrix, conn],
+        [pltpu.VMEM((2, sz.ey, sz.ez), f32), pltpu.SemaphoreType.DMA((4 + sz.blocks,))],
+        [vectors, inv_mass, potential, cell_matrix, conn], hbm=5,
     )
     from_x = send(to_x, -1, 0)
-    (to_y,) = call(
+    to_y, res_face = call(
         functools.partial(pack_y_kernel, sz), "pack_y", 0,
-        [like((sz.blocks + 1, sz.gx, sz.ez, width), bf16)], [], [vectors, own_inv, own_pot, from_x],
+        [
+            like(((sz.blocks + 1) * sz.gx + sz.groups * sz.ex, sz.ez, width), bf16),
+            like(resident.shape[1:], bf16),
+        ],
+        [
+            pltpu.VMEM((2, sz.ex, sz.ez), f32),
+            pltpu.SemaphoreType.DMA((3 + sz.blocks + sz.groups,)),
+        ],
+        [vectors, resident, inv_mass, potential, from_x], hbm=4,
     )
     from_y = send(to_y, 0, -1)
-
-    conn = connectivity.reshape(sz.cells, sz.nodes)
+    res_x = send(res_face, -1, 0)
+
     halves = 2 if sz.cells % 2 == 0 else 1
     step = sz.cells // halves
     matrices = []
@@ -350,7 +451,7 @@
     parity = jnp.reshape(lax.axis_index("dy") % 2, (1,)).astype(jnp.int32)
 
     messages = [
-        like((2, 2, sz.blocks, sz.ez, width), bf16),
+        like((2, 2 * sz.blocks, sz.ez, width), bf16),
         like((2, sz.blocks, sz.gy - 2, sz.ez, width), bf16),
         like((2, sz.blocks, sz.gx, sz.ez, width), f32),
     ]
@@ -372,41 +473,40 @@
         face = swap_x(face)
         return (corner, face, *swap_y(near, far))
 
-    x_ext, inv_b, pot_b, part, *sent = call(
+    first_corner = like((2, 2 * sz.blocks + sz.groups, sz.ez, width), bf16)
+    res_x, x_ext, inv_b, pot_b, part, *sent = call(
         functools.partial(first_kernel, sz, len(matrices)), "first", flops,
-        [like(ext, bf16), field_ext, field_ext, like(ext, f32)] + messages, scratch,
-        [parity, vectors, from_x, from_y, own_inv, own_pot, *matrices], True,
+        [res_x, like(ext, bf16), field_ext, field_ext, like(ext, f32), first_corner] + messages[1:],
+        scratch, [parity, vectors, from_x, from_y, own_inv, own_pot, res_x, *matrices], True,
+        aliases={6: 0},
+    )
+    got = exchange(*sent)
+    (res_y,) = call(
+        functools.partial(resident_rows_kernel, sz), "resident_rows", 0,
+        [like((sz.gx,) + resident.shape[2:], bf16)], [], [from_y, got[0]],
     )
     y1, part, *sent = call(
         functools.partial(second_kernel, sz, len(matrices)), "second", flops,
         [like(ext, f32), like(ext, f32)] + messages, scratch,
-        [parity, x_ext, part, *exchange(*sent), inv_b, pot_b, *matrices], True,
-    )
-    part, corner, face, side = call(
+        [parity, x_ext, part, *got, inv_b, pot_b, *matrices], True,
+    )
+    part, corner, face, side, *rows = call(
         functools.partial(third_kernel, sz, len(matrices)), "third", flops,
         [
             like(own, f32), like((sz.blocks, sz.ez, width), bf16),
             like((sz.blocks, sz.ey, sz.ez, width), bf16), like((sz.blocks, sz.ex, sz.ez, width), f32),
+            like((sz.ex * sz.ey, sz.ez, full), bf16), like((sz.ey, sz.ez, full), bf16),
+            like((sz.gx, sz.ez, full), bf16),
         ],
         [pltpu.VMEM(ext, f32), pltpu.VMEM(ext, f32)] + scratch,
         [parity, x_ext, y1, part, *exchange(*sent), inv_b, pot_b, *matrices], True,
     )
-    corner = send(corner, 1, 0)
-    side, face = call(
-        functools.partial(last_side_kernel, sz), "last_side", 0,
-        [like((sz.blocks, sz.ex, sz.ez, width), bf16), face], [], [side, corner, face],
-        aliases={2: 1},
-    )
-    face = send(face, 1, 0)
-    side = send(side, 0, 1)
-    filtered, rounded = call(
-        functools.partial(last_kernel, sz), "last", 0,
-        [like(own, f32), like(own[1:4] + (full,), bf16)], [],
-        [part, face, side, inv_b],
-    )
-    local = lax.dot_general(
-        resident.reshape(-1, resident.shape[-1]), rounded.reshape(-1, full),
-        (((0,), (0,)), ((), ())), preferred_element_type=f32,
+    local = sum(
+        lax.dot_general(
+            many.reshape(-1, many.shape[-1]), few.reshape(-1, full), (((0,), (0,)), ((), ())),
+            preferred_element_type=f32,
+        )
+        for many, few in zip((resident, res_x, res_y), rows)
     )
     local = (local * norm_scale).astype(bf16).reshape(ny, -1, full)
     pieces = lax.all_to_all(local, "dy", 0, 0)
@@ -414,6 +514,17 @@
     total = mine
     for steps in range(1, nx):
         total = total + send(mine, steps, 0)
+    corner = send(corner, 1, 0)
+    side, face = call(
+        functools.partial(last_side_kernel, sz), "last_side", 0,
+        [like((sz.blocks, sz.ex, sz.ez, width), bf16), face], [], [side, corner, face],
+        aliases={2: 1},
+    )
+    face = send(face, 1, 0)
+    side = send(side, 0, 1)
+    (filtered,) = call(
+        functools.partial(last_kernel, sz), "last", 0, [like(own, f32)], [], [part, face, side]
+    )
     return (filtered, total)
 
 

time: 93.3 us -> 76.2 us (0.82)
  local copies, waits for them, and re-layouts: 14.7 us -> 1.53 us
  blocking collectives: 12.6 us -> 0 us
  starting transfers between devices: 14.6 us -> 25 us
  waiting for transfers between devices: 30.7 us -> 26.9 us
  Pallas kernels: 18 us -> 19.7 us
    all_to_all x1 -> x0, blocking collectives: 12.6 us -> none  [body(): pieces = lax.all_to_all(local, 'dy', 0, 0)]
    unnamed x34 -> x8, local copies, waits for them, and re-layouts: 11.3 us -> 0.02 us
    all_to_all x0 -> x1, waiting for transfers between devices: none -> 5.78 us  [body(): pieces = lax.all_to_all(local, 'dy', 0, 0)]
    ppermute x10 -> x11, waiting for transfers between devices: 18.6 us -> 13.8 us  [send(): return lax.ppermute(value, ('dx', 'dy'), pairs)]
    ppermute x2, starting transfers between devices: 0.88 us -> 5.53 us  [swap_y(): far = lax.ppermute(far, 'dy', far_pairs)]
    all_to_all x0 -> x1, starting transfers between devices: none -> 4.27 us  [body(): pieces = lax.all_to_all(local, 'dy', 0, 0)]
    ppermute x2, waiting for transfers between devices: 10.4 us -> 7.37 us  [swap_y(): far = lax.ppermute(far, 'dy', far_pairs)]
    pallas_call x11 -> x12, Pallas kernels: 18 us -> 19.7 us  [call(): pl.pallas_call(kernel, in_specs=specs, out_specs=[whole] * len(out_shape)...]
  transfers between devices with their start and end apart: 14 -> 16, of which waited for: 9 -> 9; matrix products, arithmetic and copies ran while one was open for 0% -> 0% of each run, Pallas kernels for 8% -> 12%
where the time goes in v3:
time: 76.2 us; the launch traced here: 75.9 us
  waiting for transfers between devices  26.9 us (35%)
  starting transfers between devices  25 us (33%)
  Pallas kernels  19.7 us (26%)
  local copies, waits for them, and re-layouts  1.53 us (2%)
  matrix products  1.27 us (2%)
  between operations  0.79 us (1%)
    pallas_call x12, Pallas kernels, call(): pl.pallas_call(kernel, in_specs=specs, out_specs=[whole] * len(out_shape)...  19.7 us
    ppermute x11, starting transfers between devices, send(): return lax.ppermute(value, ('dx', 'dy'), pairs)  15.2 us
    ppermute x11, waiting for transfers between devices, send(): return lax.ppermute(value, ('dx', 'dy'), pairs)  13.8 us
    ppermute x2, waiting for transfers between devices, swap_y(): far = lax.ppermute(far, 'dy', far_pairs)  7.37 us
    all_to_all x1, waiting for transfers between devices, body(): pieces = lax.all_to_all(local, 'dy', 0, 0)  5.78 us
    ppermute x2, starting transfers between devices, swap_y(): far = lax.ppermute(far, 'dy', far_pairs)  5.53 us
    all_to_all x1, starting transfers between devices, body(): pieces = lax.all_to_all(local, 'dy', 0, 0)  4.27 us
  transfers between devices with their start and end apart: 16, of which 9 were waited for; matrix products, arithmetic and copies ran while one was open for 0% of the time, Pallas kernels for 12%

profile of v3, /device:TPU:0, one launch (start us, length us, event | category | flops | bytes accessed | tf_op | source)
XLA Modules:
  0.0 75.9 jit_solution(16132632187848620656)
XLA Ops:
  0.6 1.4 %pack_x.1 = (bf16[3,16,16,128]{3,2,1,0:T(8,128)(2,1)S(1)}, bf16[729,729]{1,0:T(8,128)(2,1)S(1)}, s32[4,729]{1,0:T(4,128)S(1)}) custom-call(bf16[2,8,16,16,128]{4,3,2,1,0:T(8,128)(2,1)} %vec_ref.1, f32[8,16,16]{2,1,0:T(8,128)} %inv_hbm.3, f32[8,16,16]{2,1,0:T(8,128)} %pot_hbm.3, bf16[729,729]{1,0:T(8,128)(2,1)} %mat_hbm.1, s32[4,729]{1,0:T(4,128)} %bitcast.27), custom_call_target="tpu_custom_call" | custom-call | bytes 3410660 | tf_op jit(solution)/shard_map/pack_x/pallas_call | solution.py:394
  2.1 3.0 %collective-permute-start = (bf16[3,16,16,128]{3,2,1,0:T(8,128)(2,1)S(1)}, bf16[3,16,16,128]{3,2,1,0:T(8,128)(2,1)S(1)}, u32[]{:S(2)}, u32[]{:S(2)}) collective-permute-start(bf16[3,16,16,128]{3,2,1,0:T(8,128)(2,1)S(1)} %get-tuple-element.35), channel_id=1, source_target_pairs={{0,16},{1,17},{2,18},{3,19},{4,20},{5,21},{6,22},{7,23},{8,24},{9,... | collective-permute-start | bytes 589832 | tf_op jit(solution)/shard_map/ppermute | solution.py:55
  5.1 3.8 %order_cells.3.refs_1_ = bf16[2,736,768]{2,1,0:T(8,128)(2,1)S(1)} custom-call(s32[4,729]{1,0:T(4,128)S(1)} %get-tuple-element.38.conn_ref, bf16[729,729]{1,0:T(8,128)(2,1)S(1)} %get-tuple-element.39.matrix_ref), custom_call_target="tpu_custom_call" | custom-call | flops 3623878656 | bytes 3335538 | tf_op jit(solution)/shard_map/order_cells/pallas_call | solution.py:394
  8.9 1.1 %collective-permute-done.from_x = bf16[3,16,16,128]{3,2,1,0:T(8,128)(2,1)S(1)} collective-permute-done((bf16[3,16,16,128]{3,2,1,0:T(8,128)(2,1)S(1)}, bf16[3,16,16,128]{3,2,1,0:T(8,128)(2,1)S(1)}, u32[]{:S(2)}, u32[]{:S(2)}) %collective-permute-start) | collective-permute-done | bytes 196640 | tf_op jit(solution)/shard_map/ppermute | solution.py:55
  10.0 1.1 %pack_y.1 = (bf16[59,16,128]{2,1,0:T(8,128)(2,1)S(1)}, bf16[16,16,512]{2,1,0:T(8,128)(2,1)S(1)}) custom-call(bf16[2,8,16,16,128]{4,3,2,1,0:T(8,128)(2,1)} %vec_ref.1, bf16[8,16,16,512]{3,2,1,0:T(8,128)(2,1)} %res_hbm.1, f32[8,16,16]{2,1,0:T(8,128)} %inv_hbm.3, f32[8,16,16]{2,1,0:T(8,128)} %pot_hbm.3, bf16[3,16,16,128]{3,2,1,0:T(8,128)(2,1)S(1)} %collective-permute-done.from_x), custom_call_target="tpu_custom_call" | custom-call | bytes 3862528 | tf_op jit(solution)/shard_map/pack_y/pallas_call | solution.py:394
  11.1 3.6 %collective-permute-start.1 = (bf16[59,16,128]{2,1,0:T(8,128)(2,1)S(1)}, bf16[59,16,128]{2,1,0:T(8,128)(2,1)S(1)}, u32[]{:S(2)}, u32[]{:S(2)}) collective-permute-start(bf16[59,16,128]{2,1,0:T(8,128)(2,1)S(1)} %get-tuple-element.36), channel_id=1, source_target_pairs={{0,15},{1,0},{2,1},{3,2},{4,3},{5,4},{6,5},{7,6},{8,7},{9,8},{10,9... | collective-permute-start | bytes 725000 | tf_op jit(solution)/shard_map/ppermute | solution.py:55
  14.6 1.5 %collective-permute-start.2 = (bf16[16,16,512]{2,1,0:T(8,128)(2,1)S(1)}, bf16[16,16,512]{2,1,0:T(8,128)(2,1)S(1)}, u32[]{:S(2)}, u32[]{:S(2)}) collective-permute-start(bf16[16,16,512]{2,1,0:T(8,128)(2,1)S(1)} %get-tuple-element.37), channel_id=1, source_target_pairs={{0,16},{1,17},{2,18},{3,19},{4,20},{5,21},{6,22},{7,23},{8,24},{9,... | collective-permute-start | bytes 786440 | tf_op jit(solution)/shard_map/ppermute | solution.py:55
  16.1 3.8 %order_cells.2.refs_0_ = bf16[2,736,768]{2,1,0:T(8,128)(2,1)S(1)} custom-call(s32[4,729]{1,0:T(4,128)S(1)} %get-tuple-element.38.conn_ref, bf16[729,729]{1,0:T(8,128)(2,1)S(1)} %get-tuple-element.39.matrix_ref), custom_call_target="tpu_custom_call" | custom-call | flops 3623878656 | bytes 3335538 | tf_op jit(solution)/shard_map/order_cells/pallas_call | solution.py:394
  19.9 0.0 copy-start
  20.0 0.0 collective-permute-done.1.from_y
  20.0 1.0 %collective-permute-done.2.res_in = bf16[16,16,512]{2,1,0:T(8,128)(2,1)S(1)} collective-permute-done((bf16[16,16,512]{2,1,0:T(8,128)(2,1)S(1)}, bf16[16,16,512]{2,1,0:T(8,128)(2,1)S(1)}, u32[]{:S(2)}, u32[]{:S(2)}) %collective-permute-start.2) | collective-permute-done | bytes 262176 | tf_op jit(solution)/shard_map/ppermute | solution.py:55
  21.0 0.3 broadcast_in_dim.4.own_inv
  21.4 0.3 broadcast_in_dim.5.own_pot
  21.7 2.2 %first.1 = (bf16[16,16,512]{2,1,0:T(8,128)(2,1)S(1)}, bf16[2,9,17,16,128]{4,3,2,1,0:T(8,128)(2,1)S(1)}, f32[9,17,16,128]{3,2,1,0:T(8,128)S(1)}, f32[9,17,16,128]...) custom-call(s32[1]{0:T(128)} %bitcast.even_ref, ...), custom_call_target="tpu_custom_call", output_to_operand_aliasing={{0}: (6, {})} | custom-call | flops 1157627904 | bytes 15503364 | tf_op jit(solution)/shard_map/first/pallas_call | solution.py:394
  23.9 1.6 %collective-permute-start.3 = (bf16[2,8,16,128]{3,2,1,0:T(8,128)(2,1)S(1)}, bf16[2,8,16,128]{3,2,1,0:T(8,128)(2,1)S(1)}, u32[]{:S(2)}, u32[]{:S(2)}) collective-permute-start(bf16[2,8,16,128]{3,2,1,0:T(8,128)(2,1)S(1)} %get-tuple-element.42), channel_id=1, source_target_pairs={{0,16},{1,17},{2,18},{3,19},{4,20},{5,21},{6,22},{7,23},{8,24},{9,... | collective-permute-start | bytes 196616 | tf_op jit(solution)/shard_map/ppermute | solution.py:55
  25.5 3.5 %collective-permute-done.3.corner_ref.corner_in.corner = bf16[2,8,16,128]{3,2,1,0:T(8,128)(2,1)S(1)} collective-permute-done((bf16[2,8,16,128]{3,2,1,0:T(8,128)(2,1)S(1)}, bf16[2,8,16,128]{3,2,1,0:T(8,128)(2,1)S(1)}, u32[]{:S(2)}, u32[]{:S(2)}) %collective-permute-start.3) | collective-permute-done | bytes 65568 | tf_op jit(solution)/shard_map/ppermute | solution.py:55
  29.0 1.6 %collective-permute-start.4 = (bf16[2,2,15,16,128]{4,3,2,1,0:T(8,128)(2,1)S(1)}, bf16[2,2,15,16,128]{4,3,2,1,0:T(8,128)(2,1)S(1)}, u32[]{:S(2)}, u32[]{:S(2)}) collective-permute-start(bf16[2,2,15,16,128]{4,3,2,1,0:T(8,128)(2,1)S(1)} %get-tuple-element.45), channel_id=1, source_target_pairs={{0,16},{1,17},{2,18},{3,19},{4,20},{5,21},{6,22},{7,23},{8,24},{9,... | collective-permute-start | bytes 737288 | tf_op jit(solution)/shard_map/ppermute | solution.py:55
  30.6 0.0 collective-permute-start.5
  30.6 3.1 %collective-permute-start.6 = (bf16[2,9,16,128]{3,2,1,0:T(8,128)(2,1)S(1)}, bf16[2,9,16,128]{3,2,1,0:T(8,128)(2,1)S(1)}, u32[]{:S(2)}, u32[]{:S(2)}) collective-permute-start(bf16[2,9,16,128]{3,2,1,0:T(8,128)(2,1)S(1)} %get-tuple-element.47), channel_id=1, source_target_pairs={{0,15},{1,2},{2,1},{3,4},{4,3},{5,6},{6,5},{7,8},{8,7},{9,10},{10,... | collective-permute-start | bytes 221192 | tf_op jit(solution)/shard_map/ppermute | solution.py:68
  33.8 0.0 collective-permute-done.5.near_in
  33.8 3.3 %collective-permute-done.6.far_in = bf16[2,9,16,128]{3,2,1,0:T(8,128)(2,1)S(1)} collective-permute-done((bf16[2,9,16,128]{3,2,1,0:T(8,128)(2,1)S(1)}, bf16[2,9,16,128]{3,2,1,0:T(8,128)(2,1)S(1)}, u32[]{:S(2)}, u32[]{:S(2)}) %collective-permute-start.6) | collective-permute-done | bytes 73760 | tf_op jit(solution)/shard_map/ppermute | solution.py:68
  37.1 0.0 collective-permute-done.4.face_in
  37.1 2.5 %second.1 = (f32[2,9,17,16,128]{4,3,2,1,0:T(8,128)S(1)}, f32[2,9,17,16,128]{4,3,2,1,0:T(8,128)S(1)}, bf16[2,4,16,128]{3,2,1,0:T(8,128)(2,1)S(1)}, bf16[2,2,15,16...) custom-call(s32[1]{0:T(128)} %bitcast.even_ref, bf16[2,9,17,16,128]{4,3,2,1,0:T(8,128)(2,1)S(1)} %get-tuple-element.40.x_ref, ...), custom_call_target="tpu_custom_call" | custom-call | flops 1157627904 | bytes 16834564 | tf_op jit(solution)/shard_map/second/pallas_call | solution.py:394
  39.6 0.5 collective-permute-start.7
  40.1 3.8 %collective-permute-done.7.corner_ref.corner_in = bf16[2,4,16,128]{3,2,1,0:T(8,128)(2,1)S(1)} collective-permute-done((bf16[2,4,16,128]{3,2,1,0:T(8,128)(2,1)S(1)}, bf16[2,4,16,128]{3,2,1,0:T(8,128)(2,1)S(1)}, u32[]{:S(2)}, u32[]{:S(2)}) %collective-permute-start.7) | collective-permute-done | bytes 32800 | tf_op jit(solution)/shard_map/ppermute | solution.py:55
  44.0 0.5 collective-permute-start.8
  44.5 0.0 collective-permute-start.9
  44.5 2.4 %collective-permute-start.10 = (bf16[2,9,16,128]{3,2,1,0:T(8,128)(2,1)S(1)}, bf16[2,9,16,128]{3,2,1,0:T(8,128)(2,1)S(1)}, u32[]{:S(2)}, u32[]{:S(2)}) collective-permute-start(bf16[2,9,16,128]{3,2,1,0:T(8,128)(2,1)S(1)} %get-tuple-element.57), channel_id=1, source_target_pairs={{0,15},{1,2},{2,1},{3,4},{4,3},{5,6},{6,5},{7,8},{8,7},{9,10},{10,... | collective-permute-start | bytes 221192 | tf_op jit(solution)/shard_map/ppermute | solution.py:68
  46.9 0.0 collective-permute-done.9.near_in
  46.9 4.0 %collective-permute-done.10.far_in = bf16[2,9,16,128]{3,2,1,0:T(8,128)(2,1)S(1)} collective-permute-done((bf16[2,9,16,128]{3,2,1,0:T(8,128)(2,1)S(1)}, bf16[2,9,16,128]{3,2,1,0:T(8,128)(2,1)S(1)}, u32[]{:S(2)}, u32[]{:S(2)}) %collective-permute-start.10) | collective-permute-done | bytes 73760 | tf_op jit(solution)/shard_map/ppermute | solution.py:68
  51.0 0.0 collective-permute-done.8.face_in
  51.0 3.3 %third.1 = (f32[2,8,16,16,128]{4,3,2,1,0:T(8,128)S(1)}, bf16[2,16,128]{2,1,0:T(8,128)(2,1)S(1)}, bf16[2,16,16,128]{3,2,1,0:T(8,128)(2,1)S(1)}, f32[2,8,16,128]{3...) custom-call(s32[1]{0:T(128)} %bitcast.even_ref, ...), custom_call_target="tpu_custom_call" | custom-call | flops 1157627904 | bytes 17342468 | tf_op jit(solution)/shard_map/third/pallas_call | solution.py:394
  54.3 0.3 convolution_bitcast_fusion.1
  54.6 0.3 convolution_bitcast_fusion
  54.9 0.7 fusion.3
  55.6 0.8 %copy.16 = bf16[512,256]{1,0:T(8,128)(2,1)} copy(bf16[512,256]{0,1:T(8,128)(2,1)S(1)} %fusion.3) | data formatting | bytes 524288 | tf_op jit(solution)/shard_map/convert_element_type | solution.py:511
  56.4 4.3 %all-to-all-start = ((bf16[16,32,256]{2,1,0:T(8,128)(2,1)}), bf16[16,32,256]{2,1,0:T(8,128)(2,1)S(1)}, u32[]{:S(2)}, u32[]{:S(2)}) async-start(bf16[16,32,256]{2,1,0:T(8,128)(2,1)} %bitcast.7), calls=%async_computation | async-start | bytes 524288 | tf_op jit(solution)/shard_map/all_to_all | solution.py:512
  60.7 0.9 %collective-permute-start.11 = (bf16[2,16,128]{2,1,0:T(8,128)(2,1)S(1)}, bf16[2,16,128]{2,1,0:T(8,128)(2,1)S(1)}, u32[]{:S(2)}, u32[]{:S(2)}) collective-permute-start(bf16[2,16,128]{2,1,0:T(8,128)(2,1)S(1)} %get-tuple-element.60), channel_id=1, source_target_pairs={{0,16},{1,17},{2,18},{3,19},{4,20},{5,21},{6,22},{7,23},{8,24},{9,... | collective-permute-start | bytes 24584 | tf_op jit(solution)/shard_map/ppermute | solution.py:55
  61.7 2.8 %collective-permute-done.11.corner_ref = bf16[2,16,128]{2,1,0:T(8,128)(2,1)S(1)} collective-permute-done((bf16[2,16,128]{2,1,0:T(8,128)(2,1)S(1)}, bf16[2,16,128]{2,1,0:T(8,128)(2,1)S(1)}, u32[]{:S(2)}, u32[]{:S(2)}) %collective-permute-start.11) | collective-permute-done | bytes 8224 | tf_op jit(solution)/shard_map/ppermute | solution.py:55
  64.4 0.1 collective-permute-start.13
  64.5 0.9 %collective-permute-start.12 = (bf16[2,16,16,128]{3,2,1,0:T(8,128)(2,1)S(1)}, bf16[2,16,16,128]{3,2,1,0:T(8,128)(2,1)S(1)}, u32[]{:S(2)}, u32[]{:S(2)}) collective-permute-start(bf16[2,16,16,128]{3,2,1,0:T(8,128)(2,1)S(1)} %get-tuple-element.62), channel_id=1, source_target_pairs={{0,16},{1,17},{2,18},{3,19},{4,20},{5,21},{6,22},{7,23},{8,24},{9,... | collective-permute-start | bytes 393224 | tf_op jit(solution)/shard_map/ppermute | solution.py:55
  65.5 5.8 %all-to-all-done = bf16[16,32,256]{2,1,0:T(8,128)(2,1)S(1)} async-done(((bf16[16,32,256]{2,1,0:T(8,128)(2,1)}), bf16[16,32,256]{2,1,0:T(8,128)(2,1)S(1)}, u32[]{:S(2)}, u32[]{:S(2)}) %all-to-all-start) | async-done | bytes 262176 | tf_op jit(solution)/shard_map/all_to_all | solution.py:512
  71.3 0.9 %collective-permute-start.14 = (f32[32,256]{1,0:T(8,128)S(1)}, f32[32,256]{1,0:T(8,128)S(1)}, u32[]{:S(2)}, u32[]{:S(2)}) collective-permute-start(f32[32,256]{1,0:T(8,128)S(1)} %convert_reduce_fusion), channel_id=1, source_target_pairs={{0,16},{1,17},{2,18},{3,19},{4,20},{5,21},{6,22},{7,23},{8,24},{9,... | collective-permute-start | bytes 98312 | tf_op jit(solution)/shard_map/ppermute | solution.py:55
  72.2 0.0 collective-permute-done.13.side
  72.2 0.0 collective-permute-done.12.face
  72.2 1.5 %last.1 = f32[2,8,16,16,128]{4,3,2,1,0:T(8,128)} custom-call(f32[2,8,16,16,128]{4,3,2,1,0:T(8,128)S(1)} %get-tuple-element.58.part_ref, bf16[2,16,16,128]{3,2,1,0:T(8,128)(2,1)S(1)} %collective-permute-done.12.face, bf16[2,8,16,128]{3,2,1,0:T(8,128)(2,1)S(1)} %collective-permute-done.13.side), custom_call_target="tpu_custom_call" | custom-call | bytes 4390912 | tf_op jit(solution)/shard_map/last/pallas_call | solution.py:394
  73.7 1.6 %collective-permute-done.14 = f32[32,256]{1,0:T(8,128)S(1)} collective-permute-done((f32[32,256]{1,0:T(8,128)S(1)}, f32[32,256]{1,0:T(8,128)S(1)}, u32[]{:S(2)}, u32[]{:S(2)}) %collective-permute-start.14) | collective-permute-done | bytes 32800 | tf_op jit(solution)/shard_map/ppermute | solution.py:55
  75.3 0.6 add.16
  (12 shorter events, 0.1 us)
Async XLA Ops:
  2.1 7.9 %collective-permute-start = (bf16[3,16,16,128]{3,2,1,0:T(8,128)(2,1)S(1)}, bf16[3,16,16,128]{3,2,1,0:T(8,128)(2,1)S(1)}, u32[]{:S(2)}, u32[]{:S(2)}) collective-permute-start(bf16[3,16,16,128]{3,2,1,0:T(8,128)(2,1)S(1)} %get-tuple-element.35), channel_id=1, source_target_pairs={{0,16},{1,17},{2,18},{3,19},{4,20},{5,21},{6,22},{7,23},{8,24},{9,... | collective-permute-start | bytes 589832 | tf_op jit(solution)/shard_map/ppermute | solution.py:55
  11.1 8.9 %collective-permute-start.1 = (bf16[59,16,128]{2,1,0:T(8,128)(2,1)S(1)}, bf16[59,16,128]{2,1,0:T(8,128)(2,1)S(1)}, u32[]{:S(2)}, u32[]{:S(2)}) collective-permute-start(bf16[59,16,128]{2,1,0:T(8,128)(2,1)S(1)} %get-tuple-element.36), channel_id=1, source_target_pairs={{0,15},{1,0},{2,1},{3,2},{4,3},{5,4},{6,5},{7,6},{8,7},{9,8},{10,9... | collective-permute-start | bytes 725000 | tf_op jit(solution)/shard_map/ppermute | solution.py:55
  14.6 6.4 %copy-start.2 = (f32[8,16,16]{2,1,0:T(8,128)S(1)}, f32[8,16,16]{2,1,0:T(8,128)}, u32[]{:S(2)}) copy-start(f32[8,16,16]{2,1,0:T(8,128)} %inv_hbm.3) | copy-start | bytes 24580
  14.6 6.7 %copy-start.3 = (f32[8,16,16]{2,1,0:T(8,128)S(1)}, f32[8,16,16]{2,1,0:T(8,128)}, u32[]{:S(2)}) copy-start(f32[8,16,16]{2,1,0:T(8,128)} %pot_hbm.3) | copy-start | bytes 24580
  14.6 6.4 %collective-permute-start.2 = (bf16[16,16,512]{2,1,0:T(8,128)(2,1)S(1)}, bf16[16,16,512]{2,1,0:T(8,128)(2,1)S(1)}, u32[]{:S(2)}, u32[]{:S(2)}) collective-permute-start(bf16[16,16,512]{2,1,0:T(8,128)(2,1)S(1)} %get-tuple-element.37), channel_id=1, source_target_pairs={{0,16},{1,17},{2,18},{3,19},{4,20},{5,21},{6,22},{7,23},{8,24},{9,... | collective-permute-start | bytes 786440 | tf_op jit(solution)/shard_map/ppermute | solution.py:55
  19.9 1.7 %copy-start = (bf16[2,8,16,16,128]{4,3,2,1,0:T(8,128)(2,1)S(1)}, bf16[2,8,16,16,128]{4,3,2,1,0:T(8,128)(2,1)}, u32[]{:S(2)}) copy-start(bf16[2,8,16,16,128]{4,3,2,1,0:T(8,128)(2,1)} %vec_ref.1) | copy-start | bytes 3145732
  23.9 5.1 %collective-permute-start.3 = (bf16[2,8,16,128]{3,2,1,0:T(8,128)(2,1)S(1)}, bf16[2,8,16,128]{3,2,1,0:T(8,128)(2,1)S(1)}, u32[]{:S(2)}, u32[]{:S(2)}) collective-permute-start(bf16[2,8,16,128]{3,2,1,0:T(8,128)(2,1)S(1)} %get-tuple-element.42), channel_id=1, source_target_pairs={{0,16},{1,17},{2,18},{3,19},{4,20},{5,21},{6,22},{7,23},{8,24},{9,... | collective-permute-start | bytes 196616 | tf_op jit(solution)/shard_map/ppermute | solution.py:55
  29.0 8.1 %collective-permute-start.4 = (bf16[2,2,15,16,128]{4,3,2,1,0:T(8,128)(2,1)S(1)}, bf16[2,2,15,16,128]{4,3,2,1,0:T(8,128)(2,1)S(1)}, u32[]{:S(2)}, u32[]{:S(2)}) collective-permute-start(bf16[2,2,15,16,128]{4,3,2,1,0:T(8,128)(2,1)S(1)} %get-tuple-element.45), channel_id=1, source_target_pairs={{0,16},{1,17},{2,18},{3,19},{4,20},{5,21},{6,22},{7,23},{8,24},{9,... | collective-permute-start | bytes 737288 | tf_op jit(solution)/shard_map/ppermute | solution.py:55
  30.6 3.2 %collective-permute-start.5 = (bf16[2,9,16,128]{3,2,1,0:T(8,128)(2,1)S(1)}, bf16[2,9,16,128]{3,2,1,0:T(8,128)(2,1)S(1)}, u32[]{:S(2)}, u32[]{:S(2)}) collective-permute-start(bf16[2,9,16,128]{3,2,1,0:T(8,128)(2,1)S(1)} %get-tuple-element.46), channel_id=1, source_target_pairs={{0,1},{1,0},{2,3},{3,2},{4,5},{5,4},{6,7},{7,6},{8,9},{9,8},{10,11... | collective-permute-start | bytes 221192 | tf_op jit(solution)/shard_map/ppermute | solution.py:69
  30.6 6.5 %collective-permute-start.6 = (bf16[2,9,16,128]{3,2,1,0:T(8,128)(2,1)S(1)}, bf16[2,9,16,128]{3,2,1,0:T(8,128)(2,1)S(1)}, u32[]{:S(2)}, u32[]{:S(2)}) collective-permute-start(bf16[2,9,16,128]{3,2,1,0:T(8,128)(2,1)S(1)} %get-tuple-element.47), channel_id=1, source_target_pairs={{0,15},{1,2},{2,1},{3,4},{4,3},{5,6},{6,5},{7,8},{8,7},{9,10},{10,... | collective-permute-start | bytes 221192 | tf_op jit(solution)/shard_map/ppermute | solution.py:68
  39.6 4.3 %collective-permute-start.7 = (bf16[2,4,16,128]{3,2,1,0:T(8,128)(2,1)S(1)}, bf16[2,4,16,128]{3,2,1,0:T(8,128)(2,1)S(1)}, u32[]{:S(2)}, u32[]{:S(2)}) collective-permute-start(bf16[2,4,16,128]{3,2,1,0:T(8,128)(2,1)S(1)} %get-tuple-element.52), channel_id=1, source_target_pairs={{0,16},{1,17},{2,18},{3,19},{4,20},{5,21},{6,22},{7,23},{8,24},{9,... | collective-permute-start | bytes 98312 | tf_op jit(solution)/shard_map/ppermute | solution.py:55
  44.0 7.0 %collective-permute-start.8 = (bf16[2,2,15,16,128]{4,3,2,1,0:T(8,128)(2,1)S(1)}, bf16[2,2,15,16,128]{4,3,2,1,0:T(8,128)(2,1)S(1)}, u32[]{:S(2)}, u32[]{:S(2)}) collective-permute-start(bf16[2,2,15,16,128]{4,3,2,1,0:T(8,128)(2,1)S(1)} %get-tuple-element.55), channel_id=1, source_target_pairs={{0,16},{1,17},{2,18},{3,19},{4,20},{5,21},{6,22},{7,23},{8,24},{9,... | collective-permute-start | bytes 737288 | tf_op jit(solution)/shard_map/ppermute | solution.py:55
  44.5 2.4 %collective-permute-start.9 = (bf16[2,9,16,128]{3,2,1,0:T(8,128)(2,1)S(1)}, bf16[2,9,16,128]{3,2,1,0:T(8,128)(2,1)S(1)}, u32[]{:S(2)}, u32[]{:S(2)}) collective-permute-start(bf16[2,9,16,128]{3,2,1,0:T(8,128)(2,1)S(1)} %get-tuple-element.56), channel_id=1, source_target_pairs={{0,1},{1,0},{2,3},{3,2},{4,5},{5,4},{6,7},{7,6},{8,9},{9,8},{10,11... | collective-permute-start | bytes 221192 | tf_op jit(solution)/shard_map/ppermute | solution.py:69
  44.5 6.5 %collective-permute-start.10 = (bf16[2,9,16,128]{3,2,1,0:T(8,128)(2,1)S(1)}, bf16[2,9,16,128]{3,2,1,0:T(8,128)(2,1)S(1)}, u32[]{:S(2)}, u32[]{:S(2)}) collective-permute-start(bf16[2,9,16,128]{3,2,1,0:T(8,128)(2,1)S(1)} %get-tuple-element.57), channel_id=1, source_target_pairs={{0,15},{1,2},{2,1},{3,4},{4,3},{5,6},{6,5},{7,8},{8,7},{9,10},{10,... | collective-permute-start | bytes 221192 | tf_op jit(solution)/shard_map/ppermute | solution.py:68
  51.0 3.9 %copy-start.1 = (bf16[8,16,16,512]{3,2,1,0:T(8,128)(2,1)S(1)}, bf16[8,16,16,512]{3,2,1,0:T(8,128)(2,1)}, u32[]{:S(2)}) copy-start(bf16[8,16,16,512]{3,2,1,0:T(8,128)(2,1)} %res_hbm.1) | copy-start | bytes 6291460
  56.4 14.8 %all-to-all-start = ((bf16[16,32,256]{2,1,0:T(8,128)(2,1)}), bf16[16,32,256]{2,1,0:T(8,128)(2,1)S(1)}, u32[]{:S(2)}, u32[]{:S(2)}) async-start(bf16[16,32,256]{2,1,0:T(8,128)(2,1)} %bitcast.7), calls=%async_computation | async-start | bytes 524288 | tf_op jit(solution)/shard_map/all_to_all | solution.py:512
  60.7 3.7 %collective-permute-start.11 = (bf16[2,16,128]{2,1,0:T(8,128)(2,1)S(1)}, bf16[2,16,128]{2,1,0:T(8,128)(2,1)S(1)}, u32[]{:S(2)}, u32[]{:S(2)}) collective-permute-start(bf16[2,16,128]{2,1,0:T(8,128)(2,1)S(1)} %get-tuple-element.60), channel_id=1, source_target_pairs={{0,16},{1,17},{2,18},{3,19},{4,20},{5,21},{6,22},{7,23},{8,24},{9,... | collective-permute-start | bytes 24584 | tf_op jit(solution)/shard_map/ppermute | solution.py:55
  64.4 7.8 %collective-permute-start.13 = (bf16[2,8,16,128]{3,2,1,0:T(8,128)(2,1)S(1)}, bf16[2,8,16,128]{3,2,1,0:T(8,128)(2,1)S(1)}, u32[]{:S(2)}, u32[]{:S(2)}) collective-permute-start(bf16[2,8,16,128]{3,2,1,0:T(8,128)(2,1)S(1)} %get-tuple-element.63), channel_id=1, source_target_pairs={{0,1},{1,2},{2,3},{3,4},{4,5},{5,6},{6,7},{7,8},{8,9},{9,10},{10,1... | collective-permute-start | bytes 196616 | tf_op jit(solution)/shard_map/ppermute | solution.py:55
  64.5 7.7 %collective-permute-start.12 = (bf16[2,16,16,128]{3,2,1,0:T(8,128)(2,1)S(1)}, bf16[2,16,16,128]{3,2,1,0:T(8,128)(2,1)S(1)}, u32[]{:S(2)}, u32[]{:S(2)}) collective-permute-start(bf16[2,16,16,128]{3,2,1,0:T(8,128)(2,1)S(1)} %get-tuple-element.62), channel_id=1, source_target_pairs={{0,16},{1,17},{2,18},{3,19},{4,20},{5,21},{6,22},{7,23},{8,24},{9,... | collective-permute-start | bytes 393224 | tf_op jit(solution)/shard_map/ppermute | solution.py:55
  71.3 4.0 %collective-permute-start.14 = (f32[32,256]{1,0:T(8,128)S(1)}, f32[32,256]{1,0:T(8,128)S(1)}, u32[]{:S(2)}, u32[]{:S(2)}) collective-permute-start(f32[32,256]{1,0:T(8,128)S(1)} %convert_reduce_fusion), channel_id=1, source_target_pairs={{0,16},{1,17},{2,18},{3,19},{4,20},{5,21},{6,22},{7,23},{8,24},{9,... | collective-permute-start | bytes 98312 | tf_op jit(solution)/shard_map/ppermute | solution.py:55

commit v4 on v0

v4 whole, which is shorter than its diff:
```python
import functools
import math

import jax
import jax.numpy as jnp
from jax import lax
from jax.experimental import pallas as pl
from jax.experimental.pallas import tpu as pltpu
from jax.sharding import PartitionSpec as P

LANES = 128
SUB = 16
VMEM_LIMIT = 16 * 1024 * 1024

center_shift = 1.2
half_width = 2.0
gain = 2.0 / half_width

f32, bf16 = jnp.float32, jnp.bfloat16


def round_up(value, step):
    return -(-value // step) * step


class Sizes:
    def __init__(self, vectors, resident, inv_mass, connectivity):
        self.blocks = vectors.shape[0]
        self.width = vectors.shape[-1]
        self.full = self.blocks * self.width
        self.groups = resident.shape[-1] // LANES
        self.ex, self.ey, self.ez = inv_mass.shape
        self.cells, self.nodes = connectivity.shape[2:]
        self.n1 = round(self.nodes ** (1.0 / 3.0))
        self.p = self.n1 - 1
        self.cx, self.cy, self.cz = self.ex // self.p, self.ey // self.p, self.ez // self.p
        self.gx, self.gy, self.gz = self.ex + 1, self.ey + 1, self.ez
        self.edge = (self.blocks, self.ez, self.width)
        self.origins = [
            (a * self.p, b * self.p, c * self.p)
            for a in range(self.cx)
            for b in range(self.cy)
            for c in range(self.cz)
        ]
        self.most = max(len(self.cell_corners(cell)) for cell in range(self.cells))
        self.base = round_up(self.most * self.n1, 8)
        plain = self.n1 * self.n1 - min(len(self.cell_corners(cell)) for cell in range(self.cells))
        self.tail = self.base + plain * self.p
        self.rows = round_up(self.tail + plain, SUB)
        self.depth = round_up(self.rows, LANES)
        self.own_edges = self.ex * self.ey
        self.edges = round_up(self.own_edges + self.ey + self.gx, LANES // self.ez)

    def corner(self, i, j):
        if i in (0, self.ex) and j in (0, self.ey):
            return 2 * (i // self.ex) + j // self.ey
        return None

    def cell_corners(self, cell):
        x0, y0, _ = self.origins[cell]
        return [
            (i, j)
            for i in range(self.n1)
            for j in range(self.n1)
            if self.corner(x0 + i, y0 + j) is not None
        ]

    def runs(self, cell):
        corners = self.cell_corners(cell)
        place = 0
        for i in range(self.n1):
            js = [j for j in range(self.n1) if (i, j) not in corners]
            while js:
                count = 1
                while count < len(js) and js[count] == js[0] + count:
                    count += 1
                yield place, i, js[0], count
                place += count
                js = js[count:]


def send(value, steps_x, steps_y):
    nx, ny = lax.axis_size("dx"), lax.axis_size("dy")
    pairs = [
        (a * ny + b, ((a + steps_x) % nx) * ny + (b + steps_y) % ny)
        for a in range(nx)
        for b in range(ny)
    ]
    return lax.ppermute(value, ("dx", "dy"), pairs)


def swap_x(value):
    if lax.axis_size("dx") == 2:
        return send(value, 1, 0)
    return jnp.stack([send(value[0], -1, 0), send(value[1], 1, 0)])


def swap_y(near, far):
    ny = lax.axis_size("dy")
    near_pairs = [(b, b + 1 if b % 2 == 0 else b - 1) for b in range(ny)]
    far_pairs = [(b, (b - 1 if b % 2 == 0 else b + 1) % ny) for b in range(ny)]
    far = lax.ppermute(far, "dy", far_pairs)
    near = lax.ppermute(near, "dy", near_pairs)
    return near, far


def order_kernel(sz, first, count, conn_ref, matrix_ref, out_ref):
    for slot in range(count):
        cell = first + slot
        x0, y0, z0 = sz.origins[cell]
        conn = conn_ref[cell : cell + 1, :].astype(f32)
        li = jnp.floor((conn + 0.5) * (1.0 / (sz.gy * sz.gz)))
        rest = conn - li * (sz.gy * sz.gz)
        lj = jnp.floor((rest + 0.5) * (1.0 / sz.gz))
        lk = rest - lj * sz.gz - z0
        lk = jnp.where(lk < 0, lk + sz.gz, lk)
        column = (li - x0) * sz.n1 + (lj - y0)
        corners = [i * sz.n1 + j for i, j in sz.cell_corners(cell)]
        place = column
        for at in corners:
            place = place - jnp.where(column > at, 1.0, 0.0)
        index = jnp.where(lk < sz.p, sz.base + place * sz.p + lk, sz.tail + place)
        for rank, at in enumerate(corners):
            special = jnp.where(lk < sz.p, rank * sz.p + lk, len(corners) * sz.p + rank)
            index = jnp.where(column == at, special, index)
        index = index.astype(jnp.int32)
        row = lax.broadcasted_iota(jnp.int32, (sz.depth, sz.nodes), 0)
        pick = (row == index).astype(f32).astype(bf16)
        half = jnp.dot(pick[: sz.rows], matrix_ref[...], preferred_element_type=f32)
        whole = lax.dot_general(
            half.astype(bf16), pick, (((1,), (1,)), ((), ())), preferred_element_type=f32
        )
        out_ref[slot] = whole.astype(bf16)


def field_row(inv, pot):
    lane = lax.broadcasted_iota(jnp.int32, inv.shape, inv.ndim - 1)
    row = jnp.zeros_like(inv)
    for at, rest in enumerate((inv, pot)):
        for k in range(3):
            part = rest.astype(bf16).astype(f32)
            rest = rest - part
            row = jnp.where(lane == 3 * at + k, part, row)
    return row.astype(bf16)


def field_rows(sz, inv, pot, count):
    inv, pot = inv.T, pot.T
    shape = (sz.ez, sz.width)
    for at in range(count):
        yield at, field_row(
            jnp.broadcast_to(inv[:, at : at + 1], shape), jnp.broadcast_to(pot[:, at : at + 1], shape)
        )


def fields_of(row):
    row = row.astype(f32)
    return [
        jnp.broadcast_to(sum(row[:, 3 * at + k : 3 * at + k + 1] for k in range(3)), row.shape)
        for at in range(2)
    ]


def pack_kernel(
    sz, vec_hbm, res_hbm, inv_hbm, pot_hbm, mat_hbm, conn_hbm,
    to_x, to_y, mat_ref, conn_ref, at_x, at_y, sems,
):
    slabs = sz.blocks + 1
    pairs = [
        (inv_hbm.at[0], at_x.at[0]), (pot_hbm.at[0], at_x.at[1]),
        (inv_hbm.at[:, 0], at_y.at[0]), (pot_hbm.at[:, 0], at_y.at[1]),
    ]
    for b in range(sz.blocks):
        pairs.append((vec_hbm.at[b, 0], to_x.at[pl.ds(b * sz.ey, sz.ey)]))
        pairs.append((vec_hbm.at[b, :, 0], to_y.at[pl.ds(b * sz.ex, sz.ex)]))
    for g in range(sz.groups):
        lanes = pl.ds(g * LANES, LANES)
        pairs.append((res_hbm.at[0, :, :, lanes], to_x.at[pl.ds((slabs + g) * sz.ey, sz.ey)]))
        pairs.append((res_hbm.at[:, 0, :, lanes], to_y.at[pl.ds((slabs + g) * sz.ex, sz.ex)]))
    pairs += [(mat_hbm, mat_ref), (conn_hbm, conn_ref)]
    copies = [pltpu.make_async_copy(a, b, sems.at[k]) for k, (a, b) in enumerate(pairs)]
    for copy in copies:
        copy.start()
    for copy in copies[:4]:
        copy.wait()
    for j, row in field_rows(sz, at_x[0], at_x[1], sz.ey):
        to_x[sz.blocks * sz.ey + j] = row
    for i, row in field_rows(sz, at_y[0], at_y[1], sz.ex):
        to_y[sz.blocks * sz.ex + i] = row
    for copy in copies[4:]:
        copy.wait()


def ghost_corner_kernel(sz, from_y, out_ref):
    for part in range(out_ref.shape[0]):
        out_ref[part] = from_y[part * sz.ex]


def turn_kernel(sz, res_ref, from_x, from_y, corner, out_ref):
    slabs = sz.blocks + 1
    own = sz.own_edges * sz.ez
    for g in range(sz.groups):
        lanes = slice(g * LANES, (g + 1) * LANES)
        out_ref[lanes, :own] = res_ref[:, lanes].T
        ghost_x = from_x[(slabs + g) * sz.ey : (slabs + g + 1) * sz.ey]
        ghost_y = from_y[(slabs + g) * sz.ex : (slabs + g + 1) * sz.ex]
        rest = sz.edges - sz.own_edges - sz.ey - sz.gx
        parts = [ghost_x, ghost_y, corner[slabs + g : slabs + g + 1]]
        if rest:
            parts.append(jnp.zeros((rest, sz.ez, LANES), bf16))
        ghosts = jnp.concatenate(parts, axis=0)
        out_ref[lanes, own:] = ghosts.reshape(-1, LANES).T


class Nodes:
    def __init__(self, sz, vec, from_x, from_y, own_inv, own_pot, ghost_x, ghost_y, corners=None):
        self.sz, self.vec, self.from_x, self.from_y = sz, vec, from_x, from_y
        self.own, self.ghost_x, self.ghost_y, self.corners = (own_inv, own_pot), ghost_x, ghost_y, corners

    def x(self, i, j):
        sz = self.sz
        if i < sz.ex and j < sz.ey:
            return self.vec[:, i, j].astype(f32)
        if i == sz.ex:
            parts = [self.from_x[b * sz.ey + j] for b in range(sz.blocks)]
        else:
            parts = [self.from_y[b * sz.ex + i] for b in range(sz.blocks)]
        return jnp.stack(parts).astype(f32)

    def field(self, at, i, j):
        sz = self.sz
        if i < sz.ex and j < sz.ey:
            return self.own[at][i, j]
        if i < sz.ex:
            return self.ghost_y[at, i]
        if j < sz.ey:
            return self.ghost_x[at, j]
        return self.corners[at]

    def inv(self, i, j):
        return self.field(0, i, j)

    def pot(self, i, j):
        return self.field(1, i, j)


class Sums:
    def __init__(self, sz, even, acc, face, near, far, corner=None):
        self.sz, self.even, self.acc, self.face = sz, even, acc, face
        self.near, self.far, self.corner = near, far, corner

    def at(self, i, j):
        sz = self.sz
        total = self.acc[:, i, j]
        side = 1 if i == 0 else 0 if i == sz.ex else None
        if side is not None:
            total = total + self.face[side, :, j].astype(f32)
        if j in (0, sz.ey):
            is_near = self.even if j == sz.ey else jnp.logical_not(self.even)
            total = total + jnp.where(is_near, self.near[:, i].astype(f32), self.far[:, i].astype(f32))
            if side is not None:
                total = total + jnp.where(
                    is_near, self.corner[side, 0].astype(f32), self.corner[side, 1].astype(f32)
                )
        return total


def plain_edges(sz):
    return [(i, j) for i in range(sz.gx) for j in range(sz.gy) if sz.corner(i, j) is None]


def corner_edges(sz):
    return [(i, j) for i in (0, sz.ex) for j in (0, sz.ey)]


def main_products(sz, u_ref, mat_refs, rhs_ref, out_ref):
    width = sz.width
    flat = sz.gx * sz.gy * sz.gz
    u_flat = u_ref.reshape(sz.blocks * flat, width)
    matrices = [ref.at[c] for ref in mat_refs for c in range(ref.shape[0])]
    rhs_ref[: sz.base] = jnp.zeros((sz.base, sz.full), f32)
    last = sz.nodes // 8 * 8
    rhs_ref[last:] = jnp.zeros((sz.depth - last, sz.full), f32)
    for cell, (x0, y0, z0) in enumerate(sz.origins):
        z1 = z0 + sz.p
        wrap = z1 % sz.gz
        for b in range(sz.blocks):
            lanes = slice(b * width, (b + 1) * width)
            for place, i, j, count in sz.runs(cell):
                row = sz.base + place * sz.p
                rhs_ref[row : row + count * sz.p, lanes] = u_ref[
                    b, x0 + i, y0 + j : y0 + j + count, z0:z1
                ].reshape(count * sz.p, width)
        for b in range(sz.blocks):
            lanes = slice(b * width, (b + 1) * width)
            for place, i, j, count in sz.runs(cell):
                start = b * flat + ((x0 + i) * sz.gy + y0 + j) * sz.gz + wrap
                rhs_ref[sz.tail + place : sz.tail + place + count, lanes] = u_flat[
                    pl.ds(start, count, stride=sz.gz)
                ]
        out_ref[cell] = jnp.dot(
            matrices[cell][...], rhs_ref[...].astype(bf16), preferred_element_type=f32
        )


def corner_products(sz, u_corner, prod_ref, mat_refs, small_ref, tail_ref, acc_ref):
    width = sz.width
    flat = sz.gx * sz.gy * sz.gz
    acc_flat = acc_ref.reshape(sz.blocks * flat, width)
    matrices = [ref.at[c] for ref in mat_refs for c in range(ref.shape[0])]
    small_ref[...] = jnp.zeros_like(small_ref)
    touched = set()
    for cell, (x0, y0, z0) in enumerate(sz.origins):
        z1 = z0 + sz.p
        wrap = z1 % sz.gz
        corners = sz.cell_corners(cell)
        for rank, (i, j) in enumerate(corners):
            value = u_corner[sz.corner(x0 + i, y0 + j)]
            last = len(corners) * sz.p + rank
            for b in range(sz.blocks):
                lanes = slice(b * width, (b + 1) * width)
                small_ref[rank * sz.p : (rank + 1) * sz.p, lanes] = value[b, z0:z1]
                small_ref[last : last + 1, lanes] = value[b, wrap : wrap + 1]
        total = prod_ref[cell] + jnp.dot(
            matrices[cell][:, : small_ref.shape[0]], small_ref[...].astype(bf16),
            preferred_element_type=f32,
        )
        tail_ref[cell, : sz.base] = total[: sz.base]
        tail_ref[cell, sz.base :] = total[sz.tail :]
        spans = [(rank * sz.p, i, j, 1) for rank, (i, j) in enumerate(corners)]
        spans += [(sz.base + place * sz.p, i, j, count) for place, i, j, count in sz.runs(cell)]
        for row, i, j, count in spans:
            for at in range(count):
                part = total[row + at * sz.p : row + (at + 1) * sz.p]
                key = (x0 + i, y0 + j + at, z0)
                for b in range(sz.blocks):
                    value = part[:, b * width : (b + 1) * width]
                    if key in touched:
                        value = acc_ref[b, key[0], key[1], z0:z1] + value
                    acc_ref[b, key[0], key[1], z0:z1] = value
                touched.add(key)
    for cell, (x0, y0, z0) in enumerate(sz.origins):
        wrap = (z0 + sz.p) % sz.gz
        corners = sz.cell_corners(cell)
        spans = [(len(corners) * sz.p + rank, i, j, 1) for rank, (i, j) in enumerate(corners)]
        spans += [(sz.base + place, i, j, count) for place, i, j, count in sz.runs(cell)]
        for row, i, j, count in spans:
            for b in range(sz.blocks):
                start = b * flat + ((x0 + i) * sz.gy + y0 + j) * sz.gz + wrap
                rows = pl.ds(start, count, stride=sz.gz) if count > 1 else pl.ds(start, 1)
                lanes = slice(b * width, (b + 1) * width)
                acc_flat[rows] = acc_flat[rows] + tail_ref[cell, row : row + count, lanes]


def write_messages(sz, even, acc_ref, face, near, far):
    at_near = jnp.where(even, sz.ey, 0)
    for b in range(sz.blocks):
        face[0, b] = acc_ref[b, 0].astype(bf16)
        face[1, b] = acc_ref[b, sz.ex].astype(bf16)
        near[b] = acc_ref[b, :, at_near].astype(bf16)
        far[b] = acc_ref[b, :, sz.ey - at_near].astype(bf16)


def corner_pack_kernel(sz, near, far, out_ref):
    for side, i in enumerate((0, sz.ex)):
        for slot, ref in enumerate((near, far)):
            out_ref[side, slot] = ref[:, i]


def first_main(sz, n_mat, vec, from_x, from_y, own_inv, own_pot, *refs):
    mats = refs[:n_mat]
    prod_ref, ghost_x, ghost_y, u_ref, rhs_ref = refs[n_mat:]
    for j in range(sz.ey):
        ghost_x[0, j], ghost_x[1, j] = fields_of(from_x[sz.blocks * sz.ey + j])
    for i in range(sz.ex):
        ghost_y[0, i], ghost_y[1, i] = fields_of(from_y[sz.blocks * sz.ex + i])
    nodes = Nodes(sz, vec, from_x, from_y, own_inv, own_pot, ghost_x, ghost_y)
    for i, j in plain_edges(sz):
        u_ref[:, i, j] = nodes.x(i, j) * nodes.inv(i, j)
    main_products(sz, u_ref, mats, rhs_ref, prod_ref)


def first_corner(sz, n_mat, even_ref, vec, from_x, from_y, corner, own_inv, own_pot, ghost_x, ghost_y,
                 prod_ref, *refs):
    mats = refs[:n_mat]
    acc_ref, face, near, far, last_x, last_field, small_ref, tail_ref = refs[n_mat:]
    last_field[0], last_field[1] = fields_of(corner[sz.blocks])
    for b in range(sz.blocks):
        last_x[b] = corner[b].astype(f32)
    nodes = Nodes(sz, vec, from_x, from_y, own_inv, own_pot, ghost_x, ghost_y, last_field)
    u_corner = []
    for i, j in corner_edges(sz):
        x = last_x[...] if (i, j) == (sz.ex, sz.ey) else nodes.x(i, j)
        u_corner.append(x * nodes.inv(i, j))
    corner_products(sz, u_corner, prod_ref, mats, small_ref, tail_ref, acc_ref)
    write_messages(sz, even_ref[0] == 0, acc_ref, face, near, far)


def second_main(sz, n_mat, even_ref, vec, from_x, from_y, own_inv, own_pot, ghost_x, ghost_y,
                acc_in, face_in, near_in, far_in, *refs):
    mats = refs[:n_mat]
    prod_ref, y_ref, u_ref, rhs_ref = refs[n_mat:]
    nodes = Nodes(sz, vec, from_x, from_y, own_inv, own_pot, ghost_x, ghost_y)
    sums = Sums(sz, even_ref[0] == 0, acc_in, face_in, near_in, far_in)
    for i, j in plain_edges(sz):
        old, inv = nodes.x(i, j), nodes.inv(i, j)
        image = inv * sums.at(i, j) + nodes.pot(i, j) * old
        new = (image - center_shift * old) / half_width
        y_ref[:, i, j] = new
        u_ref[:, i, j] = inv * new
    main_products(sz, u_ref, mats, rhs_ref, prod_ref)


def second_corner(sz, n_mat, even_ref, vec, from_x, from_y, own_inv, own_pot, ghost_x, ghost_y, last_x,
                  last_field, acc_in, face_in, near_in, far_in, corner_in, prod_ref, *refs):
    mats = refs[:n_mat]
    acc_ref, face, near, far, y_corner, small_ref, tail_ref = refs[n_mat:]
    even = even_ref[0] == 0
    nodes = Nodes(sz, vec, from_x, from_y, own_inv, own_pot, ghost_x, ghost_y, last_field)
    sums = Sums(sz, even, acc_in, face_in, near_in, far_in, corner_in)
    u_corner = []
    for at, (i, j) in enumerate(corner_edges(sz)):
        old = last_x[...] if (i, j) == (sz.ex, sz.ey) else nodes.x(i, j)
        inv = nodes.inv(i, j)
        image = inv * sums.at(i, j) + nodes.pot(i, j) * old
        new = (image - center_shift * old) / half_width
        y_corner[at] = new
        u_corner.append(inv * new)
    corner_products(sz, u_corner, prod_ref, mats, small_ref, tail_ref, acc_ref)
    write_messages(sz, even, acc_ref, face, near, far)


def third_main(sz, n_mat, even_ref, vec, from_x, from_y, own_inv, own_pot, ghost_x, ghost_y,
               acc_in, face_in, near_in, far_in, y_ref, *refs):
    mats = refs[:n_mat]
    prod_ref, new_ref, u_ref, rhs_ref = refs[n_mat:]
    nodes = Nodes(sz, vec, from_x, from_y, own_inv, own_pot, ghost_x, ghost_y)
    sums = Sums(sz, even_ref[0] == 0, acc_in, face_in, near_in, far_in)
    for i, j in plain_edges(sz):
        old, inv = y_ref[:, i, j], nodes.inv(i, j)
        image = inv * sums.at(i, j) + nodes.pot(i, j) * old
        new = 2.0 * (image - center_shift * old) / half_width - nodes.x(i, j)
        new_ref[:, i, j] = new
        u_ref[:, i, j] = inv * new
    main_products(sz, u_ref, mats, rhs_ref, prod_ref)


def third_corner(sz, n_mat, norm_scale, even_ref, vec, from_x, from_y, own_inv, own_pot, ghost_x, ghost_y,
                 last_x, last_field, acc_in, face_in, near_in, far_in, corner_in, prod_ref, y_ref,
                 y_corner, new_ref, turned, *refs):
    mats = refs[:n_mat]
    part_ref, face, side, corner, margin = refs[n_mat : n_mat + 5]
    acc_ref, rows_ref, small_ref, tail_ref = refs[n_mat + 5 :]
    nodes = Nodes(sz, vec, from_x, from_y, own_inv, own_pot, ghost_x, ghost_y, last_field)
    sums = Sums(sz, even_ref[0] == 0, acc_in, face_in, near_in, far_in, corner_in)
    u_corner, new_corner = [], []
    for at, (i, j) in enumerate(corner_edges(sz)):
        x = last_x[...] if (i, j) == (sz.ex, sz.ey) else nodes.x(i, j)
        old, inv = y_corner[at], nodes.inv(i, j)
        image = inv * sums.at(i, j) + nodes.pot(i, j) * old
        new_corner.append(2.0 * (image - center_shift * old) / half_width - x)
        u_corner.append(inv * new_corner[-1])
    corner_products(sz, u_corner, prod_ref, mats, small_ref, tail_ref, acc_ref)

    def put_row(at, value):
        for b in range(sz.blocks):
            rows_ref[at, :, b * sz.width : (b + 1) * sz.width] = value[b]

    for i in range(sz.gx):
        for j in range(sz.gy):
            acc, inv = acc_ref[:, i, j], nodes.inv(i, j)
            if i == sz.ex or j == sz.ey:
                value = gain * (inv * acc)
                rounded = value.astype(bf16)
                if j < sz.ey:
                    put_row(sz.own_edges + j, rounded)
                    face[:, j] = rounded
                else:
                    put_row(sz.own_edges + sz.ey + i, rounded)
                    if i < sz.ex:
                        side[:, i] = value
                    else:
                        corner[...] = rounded
                continue
            at = sz.corner(i, j)
            old = y_ref[:, i, j] if at is None else y_corner[at]
            new = new_ref[:, i, j] if at is None else new_corner[at]
            image = inv * acc + nodes.pot(i, j) * new
            value = 2.0 * (image - center_shift * new) / half_width - old
            part_ref[:, i, j] = value
            put_row(i * sz.ey + j, value.astype(bf16))
    for at in range(sz.own_edges + sz.ey + sz.gx, sz.edges):
        rows_ref[at] = jnp.zeros((sz.ez, sz.full), bf16)
    local = jnp.dot(
        turned[...], rows_ref[...].reshape(sz.edges * sz.ez, sz.full), preferred_element_type=f32
    )
    margin[...] = (local * norm_scale).astype(bf16)


def last_side_kernel(sz, side_ref, corner_ref, face_in, out_ref, face_out):
    del face_in, face_out
    for i in range(sz.ex):
        value = side_ref[:, i]
        if i == 0:
            value = value + corner_ref[...].astype(f32)
        out_ref[:, i] = value.astype(out_ref.dtype)


def last_kernel(sz, part_ref, face, side, out_ref):
    for i in range(sz.ex):
        for j in range(sz.ey):
            value = part_ref[:, i, j]
            if i == 0:
                value = value + face[:, j].astype(f32)
            if j == 0:
                value = value + side[:, i].astype(f32)
            out_ref[:, i, j] = value


def like(shape, dtype):
    return jax.ShapeDtypeStruct(shape, dtype)


def call(kernel, name, flops, out_shape, scratch, operands, hbm=0, scalar_first=False, aliases=None):
    out_shape = [like(s.shape, s.dtype) for s in out_shape]
    size = sum(math.prod(s.shape) * jnp.dtype(s.dtype).itemsize for s in (*operands, *out_shape))
    whole = pl.BlockSpec(memory_space=pltpu.VMEM)
    specs = [pl.BlockSpec(memory_space=pltpu.HBM)] * hbm + [whole] * (len(operands) - hbm)
    if scalar_first:
        specs[0] = pl.BlockSpec(memory_space=pltpu.SMEM)
    operands = [pltpu.with_memory_space_constraint(a, pltpu.HBM) for a in operands[:hbm]] + list(
        operands[hbm:]
    )
    return pl.pallas_call(
        kernel,
        in_specs=specs,
        out_specs=[whole] * len(out_shape),
        out_shape=out_shape,
        scratch_shapes=scratch,
        input_output_aliases=aliases or {},
        compiler_params=pltpu.CompilerParams(vmem_limit_bytes=VMEM_LIMIT),
        cost_estimate=pl.CostEstimate(flops=flops, bytes_accessed=size, transcendentals=0),
        name=name,
    )(*operands)


def body(vectors, resident, inv_mass, potential, cell_matrix, connectivity):
    sz = Sizes(vectors, resident, inv_mass, connectivity)
    nx, ny = lax.axis_size("dx"), lax.axis_size("dy")
    norm_scale = 1.0 / math.sqrt(sz.ex * sz.ey * sz.ez * nx * ny)
    blocks, ez, width, full = sz.blocks, sz.ez, sz.width, sz.full
    res_count = resident.shape[-1]
    tile = (ez, width)
    parts = blocks + 1 + sz.groups

    conn = connectivity.reshape(sz.cells, sz.nodes)
    to_x, to_y, cell_matrix, conn = call(
        functools.partial(pack_kernel, sz), "pack", 0,
        [like((parts * sz.ey,) + tile, bf16), like((parts * sz.ex,) + tile, bf16), cell_matrix, conn],
        [
            pltpu.VMEM((2, sz.ey, ez), f32), pltpu.VMEM((2, sz.ex, ez), f32),
            pltpu.SemaphoreType.DMA((6 + 2 * blocks + 2 * sz.groups,)),
        ],
        [vectors, resident, inv_mass, potential, cell_matrix, conn], hbm=6,
    )
    from_x = send(to_x, -1, 0)
    from_y = send(to_y, 0, -1)

    halves = 2 if sz.cells % 2 == 0 else 1
    step = sz.cells // halves
    mats = []
    for at in range(0, sz.cells, step):
        mats += call(
            functools.partial(order_kernel, sz, at, step), "order_cells",
            4 * step * sz.depth**3, [like((step, sz.rows, sz.depth), bf16)], [], [conn, cell_matrix],
        )
    own_inv = jnp.broadcast_to(inv_mass[..., None], inv_mass.shape + (width,))
    own_pot = jnp.broadcast_to(potential[..., None], inv_mass.shape + (width,))
    parity = jnp.reshape(lax.axis_index("dy") % 2, (1,)).astype(jnp.int32)
    (ghost_corner,) = call(
        functools.partial(ghost_corner_kernel, sz), "ghost_corner", 0,
        [like((parts,) + tile, bf16)], [], [from_y],
    )
    ghost_corner = send(ghost_corner, -1, 0)

    grid = (blocks, sz.gx, sz.gy) + tile
    own = (blocks, sz.ex, sz.ey) + tile
    products = like((sz.cells, sz.rows, full), f32)
    messages = [
        like((2, blocks, sz.gy) + tile, bf16),
        like((blocks, sz.gx) + tile, bf16),
        like((blocks, sz.gx) + tile, bf16),
    ]
    main_scratch = [pltpu.VMEM(grid, f32), pltpu.VMEM((sz.depth, full), f32)]
    corner_scratch = [
        pltpu.VMEM((LANES, full), f32),
        pltpu.VMEM((sz.cells, sz.base + sz.rows - sz.tail, full), f32),
    ]
    n_mat = len(mats)
    flops = 2 * sz.cells * sz.rows * sz.depth * full
    small_flops = 2 * sz.cells * sz.rows * LANES * full

    def exchange(face, near, far):
        face = swap_x(face)
        near, far = swap_y(near, far)
        (corner,) = call(
            functools.partial(corner_pack_kernel, sz), "corner_pack", 0,
            [like((2, 2) + sz.edge, bf16)], [], [near, far],
        )
        return [face, near, far], swap_x(corner)

    prod, ghost_x, ghost_y = call(
        functools.partial(first_main, sz, n_mat), "first_main", flops,
        [products, like((2, sz.ey) + tile, f32), like((2, sz.ex) + tile, f32)], main_scratch,
        [vectors, from_x, from_y, own_inv, own_pot, *mats],
    )
    acc, face, near, far, last_x, last_field = call(
        functools.partial(first_corner, sz, n_mat), "first_corner", small_flops,
        [like(grid, f32), *messages, like(sz.edge, f32), like((2,) + tile, f32)], corner_scratch,
        [
            parity, vectors, from_x, from_y, ghost_corner, own_inv, own_pot, ghost_x, ghost_y, prod, *mats,
        ],
        scalar_first=True,
    )
    (turned,) = call(
        functools.partial(turn_kernel, sz), "turn_residents", flops // 2,
        [like((res_count, sz.edges * ez), bf16)], [],
        [resident.reshape(-1, res_count), from_x, from_y, ghost_corner],
    )
    got, corner = exchange(face, near, far)
    state = [vectors, from_x, from_y, own_inv, own_pot, ghost_x, ghost_y]
    ends = [last_x, last_field]
    prod, y1 = call(
        functools.partial(second_main, sz, n_mat), "second_main", flops,
        [products, like(grid, f32)], main_scratch,
        [parity, *state, acc, *got, *mats], scalar_first=True,
    )
    acc, face, near, far, y1_corner = call(
        functools.partial(second_corner, sz, n_mat), "second_corner", small_flops,
        [like(grid, f32), *messages, like((4,) + sz.edge, f32)], corner_scratch,
        [parity, *state, *ends, acc, *got, corner, prod, *mats], scalar_first=True,
    )
    got, corner = exchange(face, near, far)
    prod, y2 = call(
        functools.partial(third_main, sz, n_mat), "third_main", flops,
        [products, like(grid, f32)], main_scratch,
        [parity, *state, acc, *got, y1, *mats], scalar_first=True,
    )
    part, face, side, corner, local = call(
        functools.partial(third_corner, sz, n_mat, norm_scale), "third_corner",
        small_flops + 2 * res_count * sz.edges * ez * full,
        [
            like(own, f32), like((blocks, sz.ey) + tile, bf16), like((blocks, sz.ex) + tile, f32),
            like(sz.edge, bf16), like((res_count, full), bf16),
        ],
        [pltpu.VMEM(grid, f32), pltpu.VMEM((sz.edges, ez, full), bf16)] + corner_scratch,
        [parity, *state, *ends, acc, *got, corner, prod, y1, y1_corner, y2, turned, *mats],
        scalar_first=True,
    )

    pieces = lax.all_to_all(local.reshape(ny, -1, full), "dy", 0, 0)
    mine = jnp.sum(pieces.astype(f32), axis=0)
    margin = mine
    for steps in range(1, nx):
        margin = margin + send(mine, steps, 0)

    corner = send(corner, 1, 0)
    side, face = call(
        functools.partial(last_side_kernel, sz), "last_side", 0,
        [like((blocks, sz.ex) + tile, bf16), face], [], [side, corner, face], aliases={2: 1},
    )
    face = send(face, 1, 0)
    side = send(side, 0, 1)
    (filtered,) = call(
        functools.partial(last_kernel, sz), "last", 0, [like(own, f32)], [], [part, face, side]
    )
    return (filtered, margin)


def solution(mesh):
    return jax.shard_map(
        body,
        mesh=mesh,
        in_specs=(
            P(None, "dx", "dy", None, None),
            P("dx", "dy", None, None),
            P("dx", "dy", None),
            P("dx", "dy", None),
            P(),
            P("dx", "dy", None, None),
        ),
        out_specs=(P(None, "dx", "dy", None, None), P("dy", None)),
        check_vma=False,
    )
```

time: 359 us -> 71.7 us (0.20)
  waiting for transfers between devices: 170 us -> 21.8 us
  other arithmetic: 74.7 us -> 0.66 us
  local copies, waits for them, and re-layouts: 69.4 us -> 4.85 us
  Pallas kernels: 0 us -> 23.2 us
  matrix products: 14.6 us -> 0 us
  between operations: 14.5 us -> 0.82 us
  starting transfers between devices: 15.1 us -> 20.1 us
    psum x1 -> x0, waiting for transfers between devices: 123 us -> none  [body(): summed = lax.psum(local, ('dx', 'dy'))]
    scatter-add x9 -> x0, other arithmetic: 56.2 us -> none  [the longest x3 52.4 us: apply_hamiltonian(): jax.ops.segment_sum(product.reshape(-1, vec_width), node_index, num_segme...]
    ppermute x12 -> x15, waiting for transfers between devices: 46.5 us -> 15.7 us  [the longest x2 8.97 us: swap_y(): far = lax.ppermute(far, 'dy', far_pairs)]
    gather x3 -> x0, local copies, waits for them, and re-layouts: 28.9 us -> none  [apply_hamiltonian(): jnp.take(grown.reshape(-1, vec_width), node_index, axis=0)]
    pallas_call x0 -> x15, Pallas kernels: none -> 23.2 us  [call(): pl.pallas_call(kernel, in_specs=specs, out_specs=[whole] * len(out_shape)...]
    reshape x6 -> x0, local copies, waits for them, and re-layouts: 20.8 us -> none  [the longest x3 11.7 us: apply_hamiltonian(): product.reshape(-1, vec_width)]
    dot_general x4 -> x0, matrix products: 14.6 us -> none  [the longest x3 13 us: apply_hamiltonian(): jnp.einsum('il,clw->ciw', cell_matrix, picked, preferred_element_type=jnp...]
    slice x15 -> x0, local copies, waits for them, and re-layouts: 10.8 us -> none  [the longest x3 5.63 us: apply_hamiltonian(): folded = summed[:, :extent_y].at[:, 0:1].add(from_lower_y)]
  transfers between devices with their start and end apart: 13 -> 16, of which waited for: 13 -> 8; matrix products, arithmetic and copies ran while one was open for 3% -> 1% of each run, Pallas kernels for 0% -> 22%
where the time goes in v4:
time: 71.7 us; the launch traced here: 71.4 us
  Pallas kernels  23.2 us (32%)
  waiting for transfers between devices  21.8 us (30%)
  starting transfers between devices  20.1 us (28%)
  local copies, waits for them, and re-layouts  4.85 us (7%)
  between operations  0.82 us (1%)
    pallas_call x15, Pallas kernels, call(): pl.pallas_call(kernel, in_specs=specs, out_specs=[whole] * len(out_shape)...  23.2 us
    ppermute x11, starting transfers between devices, send(): return lax.ppermute(value, ('dx', 'dy'), pairs)  13.5 us
    ppermute x2, waiting for transfers between devices, swap_y(): far = lax.ppermute(far, 'dy', far_pairs)  8.97 us
    ppermute x11, waiting for transfers between devices, send(): return lax.ppermute(value, ('dx', 'dy'), pairs)  6.69 us
    all_to_all x1, waiting for transfers between devices, body(): pieces = lax.all_to_all(local.reshape(ny, -1, full), 'dy', 0, 0)  6.12 us
    unnamed x16, local copies, waits for them, and re-layouts  4.18 us
    all_to_all x1, starting transfers between devices, body(): pieces = lax.all_to_all(local.reshape(ny, -1, full), 'dy', 0, 0)  3.53 us
    ppermute x2, starting transfers between devices, swap_y(): far = lax.ppermute(far, 'dy', far_pairs)  3.05 us
  transfers between devices with their start and end apart: 16, of which 8 were waited for; matrix products, arithmetic and copies ran while one was open for 1% of the time, Pallas kernels for 22%

profile of v4, /device:TPU:0, one launch (start us, length us, event | category | flops | bytes accessed | tf_op | source)
XLA Modules:
  0.0 71.4 jit_solution(3787973032147817418)
XLA Ops:
  0.6 2.5 %pack.1 = (bf16[112,16,128]{2,1,0:T(8,128)(2,1)S(1)}, bf16[56,16,128]{2,1,0:T(8,128)(2,1)}, bf16[729,729]{1,0:T(8,128)(2,1)S(1)}, s32[4,729]{1,0:T(4,128)S(1)}) custom-call(bf16[2,8,16,16,128]{4,3,2,1,0:T(8,128)(2,1)} %vec.11, bf16[8,16,16,512]{3,2,1,0:T(8,128)(2,1)} %res_hbm.1, f32[8,16,16]{2,1,0:T(8,128)} %inv_hbm.1, f32[8,16,16]{2,1,0:T(8,128)} %pot_hbm.1, ...), custom_call_target="tpu_custom_call" | custom-call | bytes 5999332 | tf_op jit(solution)/shard_map/pack/pallas_call | solution.py:534
  3.1 0.0 copy-start.4
  3.1 5.5 %collective-permute-start.1 = (bf16[56,16,128]{2,1,0:T(8,128)(2,1)}, bf16[56,16,128]{2,1,0:T(8,128)(2,1)S(1)}, u32[]{:S(2)}, u32[]{:S(2)}) collective-permute-start(bf16[56,16,128]{2,1,0:T(8,128)(2,1)} %get-tuple-element.32), channel_id=1, source_target_pairs={{0,15},{1,0},{2,1},{3,2},{4,3},{5,4},{6,5},{7,6},{8,7},{9,8},{10,9... | collective-permute-start | bytes 688136 | tf_op jit(solution)/shard_map/ppermute | solution.py:89
  8.6 1.5 %collective-permute-start = (bf16[112,16,128]{2,1,0:T(8,128)(2,1)S(1)}, bf16[112,16,128]{2,1,0:T(8,128)(2,1)S(1)}, u32[]{:S(2)}, u32[]{:S(2)}) collective-permute-start(bf16[112,16,128]{2,1,0:T(8,128)(2,1)S(1)} %get-tuple-element.31), channel_id=1, source_target_pairs={{0,16},{1,17},{2,18},{3,19},{4,20},{5,21},{6,22},{7,23},{8,24},{9,... | collective-permute-start | bytes 1376264 | tf_op jit(solution)/shard_map/ppermute | solution.py:89
  10.1 3.8 %order_cells.3.refs_1_ = bf16[2,736,768]{2,1,0:T(8,128)(2,1)S(1)} custom-call(s32[4,729]{1,0:T(4,128)S(1)} %get-tuple-element.33.conn_ref, bf16[729,729]{1,0:T(8,128)(2,1)S(1)} %get-tuple-element.34.matrix_ref), custom_call_target="tpu_custom_call" | custom-call | flops 3623878656 | bytes 3335538 | tf_op jit(solution)/shard_map/order_cells/pallas_call | solution.py:534
  13.9 0.0 copy-start.5
  14.0 1.2 %copy-done.5 = bf16[729,729]{1,0:T(8,128)(2,1)S(1)} copy-done((bf16[729,729]{1,0:T(8,128)(2,1)S(1)}, bf16[729,729]{1,0:T(8,128)(2,1)}, u32[]{:S(2)}) %copy-start.5) | copy-done | bytes 1062906
  15.2 3.8 %order_cells.2.refs_0_ = bf16[2,736,768]{2,1,0:T(8,128)(2,1)S(1)} custom-call(s32[4,729]{1,0:T(4,128)S(1)} %get-tuple-element.33.conn_ref, bf16[729,729]{1,0:T(8,128)(2,1)S(1)} %copy-done.5), custom_call_target="tpu_custom_call" | custom-call | flops 3623878656 | bytes 3335538 | tf_op jit(solution)/shard_map/order_cells/pallas_call | solution.py:534
  19.0 0.0 copy-start
  19.0 0.0 collective-permute-done.1.from_y
  19.0 0.6 collective-permute-start.2
  19.6 0.0 collective-permute-done.from_x
  19.6 0.3 broadcast_in_dim.4.own_inv
  20.0 0.3 broadcast_in_dim.5.own_pot
  20.3 1.5 %first_main.1 = (f32[4,736,256]{2,1,0:T(8,128)S(1)}, f32[2,16,16,128]{3,2,1,0:T(8,128)S(1)}, f32[2,8,16,128]{3,2,1,0:T(8,128)S(1)}) custom-call(bf16[2,8,16,16,128]{4,3,2,1,0:T(8,128)(2,1)S(1)} %copy-done, bf16[112,16,128]{2,1,0:T(8,128)(2,1)S(1)} %collective-permute-done.from_x, bf16[56,16,128]{2,1,0:T(8,128)(2,1)S(1)} %collective-permute-done.1.from_y, ...), custom_call_target="tpu_custom_call" | custom-call | flops 1157627904 | bytes 11763712 | tf_op jit(solution)/shard_map/first_main/pallas_call | solution.py:534
  21.9 1.4 %collective-permute-done.2.corner = bf16[7,16,128]{2,1,0:T(8,128)(2,1)S(1)} collective-permute-done((bf16[7,16,128]{2,1,0:T(8,128)(2,1)S(1)}, bf16[7,16,128]{2,1,0:T(8,128)(2,1)S(1)}, u32[]{:S(2)}, u32[]{:S(2)}) %collective-permute-start.2) | collective-permute-done | bytes 28704 | tf_op jit(solution)/shard_map/ppermute | solution.py:89
  23.3 0.8 %first_corner.1 = (f32[2,9,17,16,128]{4,3,2,1,0:T(8,128)S(1)}, bf16[2,2,17,16,128]{4,3,2,1,0:T(8,128)(2,1)S(1)}, bf16[2,9,16,128]{3,2,1,0:T(8,128)(2,1)S(1)}, bf...) custom-call(s32[1]{0:T(128)} %bitcast.even_ref, ...), custom_call_target="tpu_custom_call" | custom-call | flops 192937984 | bytes 14757892 | tf_op jit(solution)/shard_map/first_corner/pallas_call | solution.py:534
  24.1 0.6 collective-permute-start.3
  24.7 0.0 collective-permute-start.4
  24.7 2.5 %collective-permute-start.5 = (bf16[2,9,16,128]{3,2,1,0:T(8,128)(2,1)S(1)}, bf16[2,9,16,128]{3,2,1,0:T(8,128)(2,1)S(1)}, u32[]{:S(2)}, u32[]{:S(2)}) collective-permute-start(bf16[2,9,16,128]{3,2,1,0:T(8,128)(2,1)S(1)} %get-tuple-element.43), channel_id=1, source_target_pairs={{0,15},{1,2},{2,1},{3,4},{4,3},{5,6},{6,5},{7,8},{8,7},{9,10},{10,... | collective-permute-start | bytes 221192 | tf_op jit(solution)/shard_map/ppermute | solution.py:102
  27.2 0.0 collective-permute-done.4.near.near_in
  27.2 4.0 %collective-permute-done.5.far.far_in = bf16[2,9,16,128]{3,2,1,0:T(8,128)(2,1)S(1)} collective-permute-done((bf16[2,9,16,128]{3,2,1,0:T(8,128)(2,1)S(1)}, bf16[2,9,16,128]{3,2,1,0:T(8,128)(2,1)S(1)}, u32[]{:S(2)}, u32[]{:S(2)}) %collective-permute-start.5) | collective-permute-done | bytes 73760 | tf_op jit(solution)/shard_map/ppermute | solution.py:102
  31.2 1.5 %collective-permute-start.6 = (bf16[2,2,2,16,128]{4,3,2,1,0:T(8,128)(2,1)S(1)}, bf16[2,2,2,16,128]{4,3,2,1,0:T(8,128)(2,1)S(1)}, u32[]{:S(2)}, u32[]{:S(2)}) collective-permute-start(bf16[2,2,2,16,128]{4,3,2,1,0:T(8,128)(2,1)S(1)} %corner_pack.2), channel_id=1, source_target_pairs={{0,16},{1,17},{2,18},{3,19},{4,20},{5,21},{6,22},{7,23},{8,24},{9,... | collective-permute-start | bytes 98312 | tf_op jit(solution)/shard_map/ppermute | solution.py:89
  32.7 0.0 collective-permute-done.3.face_in
  32.7 2.0 %second_main.1 = (f32[4,736,256]{2,1,0:T(8,128)S(1)}, f32[2,9,17,16,128]{4,3,2,1,0:T(8,128)S(1)}) custom-call(s32[1]{0:T(128)} %bitcast.even_ref, bf16[2,8,16,16,128]{4,3,2,1,0:T(8,128)(2,1)S(1)} %copy-done, bf16[112,16,128]{2,1,0:T(8,128)(2,1)S(1)} %collective-permute-done.from_x, bf16[56,16,128]{2,1,0:T(8,128)(2,1)S(1)} %collective-permute-done.1.from_y, ...), custom_call_target="tpu_custom_call" | custom-call | flops 1157627904 | bytes 17203204 | tf_op jit(solution)/shard_map/second_main/pallas_call | solution.py:534
  34.6 0.4 collective-permute-done.6.corner_in
  35.1 0.9 %second_corner.1 = (f32[2,9,17,16,128]{4,3,2,1,0:T(8,128)S(1)}, bf16[2,2,17,16,128]{4,3,2,1,0:T(8,128)(2,1)S(1)}, bf16[2,9,16,128]{3,2,1,0:T(8,128)(2,1)S(1)}, b...) custom-call(s32[1]{0:T(128)} %bitcast.even_ref, bf16[2,8,16,16,128]{4,3,2,1,0:T(8,128)(2,1)S(1)} %copy-done, ...), custom_call_target="tpu_custom_call" | custom-call | flops 192937984 | bytes 17760260 | tf_op jit(solution)/shard_map/second_corner/pallas_call | solution.py:534
  36.0 1.6 %collective-permute-start.7 = (bf16[2,2,17,16,128]{4,3,2,1,0:T(8,128)(2,1)S(1)}, bf16[2,2,17,16,128]{4,3,2,1,0:T(8,128)(2,1)S(1)}, u32[]{:S(2)}, u32[]{:S(2)}) collective-permute-start(bf16[2,2,17,16,128]{4,3,2,1,0:T(8,128)(2,1)S(1)} %get-tuple-element.46), channel_id=1, source_target_pairs={{0,16},{1,17},{2,18},{3,19},{4,20},{5,21},{6,22},{7,23},{8,24},{9,... | collective-permute-start | bytes 835592 | tf_op jit(solution)/shard_map/ppermute | solution.py:89
  37.6 0.0 collective-permute-start.8
  37.6 0.5 collective-permute-start.9
  38.1 0.9 %turn_residents.1.turned = bf16[512,2560]{1,0:T(8,128)(2,1)S(1)} custom-call(bf16[2048,512]{1,0:T(8,128)(2,1)S(1)} %bitcast.4, bf16[112,16,128]{2,1,0:T(8,128)(2,1)S(1)} %collective-permute-done.from_x, bf16[56,16,128]{2,1,0:T(8,128)(2,1)S(1)} %collective-permute-done.1.from_y, bf16[7,16,128]{2,1,0:T(8,128)(2,1)S(1)} %collective-permute-done.2.corner), custom_call_target="tpu_custom_call" | custom-call | flops 578813952 | bytes 5435392 | tf_op jit(solution)/shard_map/turn_residents/pallas_call | solution.py:534
  39.0 5.0 %collective-permute-done.9.far.far_in = bf16[2,9,16,128]{3,2,1,0:T(8,128)(2,1)S(1)} collective-permute-done((bf16[2,9,16,128]{3,2,1,0:T(8,128)(2,1)S(1)}, bf16[2,9,16,128]{3,2,1,0:T(8,128)(2,1)S(1)}, u32[]{:S(2)}, u32[]{:S(2)}) %collective-permute-start.9) | collective-permute-done | bytes 73760 | tf_op jit(solution)/shard_map/ppermute | solution.py:102
  44.0 0.5 collective-permute-start.10
  44.5 2.1 %third_main.1 = (f32[4,736,256]{2,1,0:T(8,128)S(1)}, f32[2,9,17,16,128]{4,3,2,1,0:T(8,128)S(1)}) custom-call(s32[1]{0:T(128)} %bitcast.even_ref, bf16[2,8,16,16,128]{4,3,2,1,0:T(8,128)(2,1)S(1)} %copy-done, bf16[112,16,128]{2,1,0:T(8,128)(2,1)S(1)} %collective-permute-done.from_x, bf16[56,16,128]{2,1,0:T(8,128)(2,1)S(1)} %collective-permute-done.1.from_y, ...), custom_call_target="tpu_custom_call" | custom-call | flops 1157627904 | bytes 19709956 | tf_op jit(solution)/shard_map/third_main/pallas_call | solution.py:534
  46.7 1.3 %collective-permute-done.10.corner_in = bf16[2,2,2,16,128]{4,3,2,1,0:T(8,128)(2,1)S(1)} collective-permute-done((bf16[2,2,2,16,128]{4,3,2,1,0:T(8,128)(2,1)S(1)}, bf16[2,2,2,16,128]{4,3,2,1,0:T(8,128)(2,1)S(1)}, u32[]{:S(2)}, u32[]{:S(2)}) %collective-permute-start.10) | collective-permute-done | bytes 32800 | tf_op jit(solution)/shard_map/ppermute | solution.py:89
  48.0 3.4 %third_corner.1 = (f32[2,8,16,16,128]{4,3,2,1,0:T(8,128)S(1)}, bf16[2,16,16,128]{3,2,1,0:T(8,128)(2,1)S(1)}, f32[2,8,16,128]{3,2,1,0:T(8,128)S(1)}, bf16[2,16,128]{2,1,0:T(8,128)(2,1)S(1)}, bf16[512,256]{1,0:T(8,128)(2,1)}) custom-call(s32[1]{0:T(128)} %bitcast.even_ref, bf16[2,8,16,16,128]{4,3,2,1,0:T(8,128)(2,1)S(1)} %copy-done, ...), custom_call_target="tpu_custom_call" | custom-call | flops 864026624 | bytes 25092100 | tf_op jit(solution)/shard_map/third_corner/pallas_call | solution.py:534
  51.4 1.3 %copy-done.2 = f32[2,8,16,16,128]{4,3,2,1,0:T(8,128)} copy-done((f32[2,8,16,16,128]{4,3,2,1,0:T(8,128)}, f32[2,8,16,16,128]{4,3,2,1,0:T(8,128)S(1)}, u32[]{:S(2)}) %copy-start.2) | copy-done | bytes 2097176
  52.7 3.5 %all-to-all-start = ((bf16[16,32,256]{2,1,0:T(8,128)(2,1)}), bf16[16,32,256]{2,1,0:T(8,128)(2,1)S(1)}, u32[]{:S(2)}, u32[]{:S(2)}) async-start(bf16[16,32,256]{2,1,0:T(8,128)(2,1)} %bitcast.3), calls=%async_computation | async-start | bytes 524288 | tf_op jit(solution)/shard_map/all_to_all | solution.py:661
  56.3 0.6 collective-permute-start.11
  56.8 3.1 %collective-permute-done.11.corner_ref = bf16[2,16,128]{2,1,0:T(8,128)(2,1)S(1)} collective-permute-done((bf16[2,16,128]{2,1,0:T(8,128)(2,1)S(1)}, bf16[2,16,128]{2,1,0:T(8,128)(2,1)S(1)}, u32[]{:S(2)}, u32[]{:S(2)}) %collective-permute-start.11) | collective-permute-done | bytes 8224 | tf_op jit(solution)/shard_map/ppermute | solution.py:89
  60.0 0.1 collective-permute-start.13
  60.1 0.6 collective-permute-start.12
  60.6 6.1 %all-to-all-done = bf16[16,32,256]{2,1,0:T(8,128)(2,1)S(1)} async-done(((bf16[16,32,256]{2,1,0:T(8,128)(2,1)}), bf16[16,32,256]{2,1,0:T(8,128)(2,1)S(1)}, u32[]{:S(2)}, u32[]{:S(2)}) %all-to-all-start) | async-done | bytes 262176 | tf_op jit(solution)/shard_map/all_to_all | solution.py:661
  66.8 0.6 collective-permute-start.14
  67.4 1.6 %copy-done.3 = f32[2,8,16,16,128]{4,3,2,1,0:T(8,128)S(1)} copy-done((f32[2,8,16,16,128]{4,3,2,1,0:T(8,128)S(1)}, f32[2,8,16,16,128]{4,3,2,1,0:T(8,128)}, u32[]{:S(2)}) %copy-start.3) | copy-done | bytes 2097176
  68.9 1.5 %last.1 = f32[2,8,16,16,128]{4,3,2,1,0:T(8,128)} custom-call(f32[2,8,16,16,128]{4,3,2,1,0:T(8,128)S(1)} %copy-done.3, bf16[2,16,16,128]{3,2,1,0:T(8,128)(2,1)S(1)} %collective-permute-done.12.face, bf16[2,8,16,128]{3,2,1,0:T(8,128)(2,1)S(1)} %collective-permute-done.13.side), custom_call_target="tpu_custom_call" | custom-call | bytes 4390912 | tf_op jit(solution)/shard_map/last/pallas_call | solution.py:534
  70.4 0.4 collective-permute-done.14
  70.8 0.6 add.8
  (19 shorter events, 0.1 us)
Async XLA Ops:
  3.1 10.8 %copy-start.4 = (bf16[729,729]{1,0:T(8,128)(2,1)}, bf16[729,729]{1,0:T(8,128)(2,1)S(1)}, u32[]{:S(2)}) copy-start(bf16[729,729]{1,0:T(8,128)(2,1)S(1)} %get-tuple-element.34.matrix_ref) | copy-start | bytes 3188650
  3.1 15.9 %collective-permute-start.1 = (bf16[56,16,128]{2,1,0:T(8,128)(2,1)}, bf16[56,16,128]{2,1,0:T(8,128)(2,1)S(1)}, u32[]{:S(2)}, u32[]{:S(2)}) collective-permute-start(bf16[56,16,128]{2,1,0:T(8,128)(2,1)} %get-tuple-element.32), channel_id=1, source_target_pairs={{0,15},{1,0},{2,1},{3,2},{4,3},{5,4},{6,5},{7,6},{8,7},{9,8},{10,9... | collective-permute-start | bytes 688136 | tf_op jit(solution)/shard_map/ppermute | solution.py:89
  8.6 11.0 %collective-permute-start = (bf16[112,16,128]{2,1,0:T(8,128)(2,1)S(1)}, bf16[112,16,128]{2,1,0:T(8,128)(2,1)S(1)}, u32[]{:S(2)}, u32[]{:S(2)}) collective-permute-start(bf16[112,16,128]{2,1,0:T(8,128)(2,1)S(1)} %get-tuple-element.31), channel_id=1, source_target_pairs={{0,16},{1,17},{2,18},{3,19},{4,20},{5,21},{6,22},{7,23},{8,24},{9,... | collective-permute-start | bytes 1376264 | tf_op jit(solution)/shard_map/ppermute | solution.py:89
  13.9 1.3 %copy-start.5 = (bf16[729,729]{1,0:T(8,128)(2,1)S(1)}, bf16[729,729]{1,0:T(8,128)(2,1)}, u32[]{:S(2)}) copy-start(bf16[729,729]{1,0:T(8,128)(2,1)} %copy-done.4) | copy-start | bytes 3188650
  15.2 4.4 %copy-start.6 = (f32[8,16,16]{2,1,0:T(8,128)S(1)}, f32[8,16,16]{2,1,0:T(8,128)}, u32[]{:S(2)}) copy-start(f32[8,16,16]{2,1,0:T(8,128)} %inv_hbm.1) | copy-start | bytes 24580
  15.2 4.8 %copy-start.7 = (f32[8,16,16]{2,1,0:T(8,128)S(1)}, f32[8,16,16]{2,1,0:T(8,128)}, u32[]{:S(2)}) copy-start(f32[8,16,16]{2,1,0:T(8,128)} %pot_hbm.1) | copy-start | bytes 24580
  19.0 1.3 %copy-start = (bf16[2,8,16,16,128]{4,3,2,1,0:T(8,128)(2,1)S(1)}, bf16[2,8,16,16,128]{4,3,2,1,0:T(8,128)(2,1)}, u32[]{:S(2)}) copy-start(bf16[2,8,16,16,128]{4,3,2,1,0:T(8,128)(2,1)} %vec.11) | copy-start | bytes 3145732
  19.0 4.2 %collective-permute-start.2 = (bf16[7,16,128]{2,1,0:T(8,128)(2,1)S(1)}, bf16[7,16,128]{2,1,0:T(8,128)(2,1)S(1)}, u32[]{:S(2)}, u32[]{:S(2)}) collective-permute-start(bf16[7,16,128]{2,1,0:T(8,128)(2,1)S(1)} %ghost_corner.1), channel_id=1, source_target_pairs={{0,16},{1,17},{2,18},{3,19},{4,20},{5,21},{6,22},{7,23},{8,24},{9,... | collective-permute-start | bytes 86024 | tf_op jit(solution)/shard_map/ppermute | solution.py:89
  24.1 8.6 %collective-permute-start.3 = (bf16[2,2,17,16,128]{4,3,2,1,0:T(8,128)(2,1)S(1)}, bf16[2,2,17,16,128]{4,3,2,1,0:T(8,128)(2,1)S(1)}, u32[]{:S(2)}, u32[]{:S(2)}) collective-permute-start(bf16[2,2,17,16,128]{4,3,2,1,0:T(8,128)(2,1)S(1)} %get-tuple-element.41), channel_id=1, source_target_pairs={{0,16},{1,17},{2,18},{3,19},{4,20},{5,21},{6,22},{7,23},{8,24},{9,... | collective-permute-start | bytes 835592 | tf_op jit(solution)/shard_map/ppermute | solution.py:89
  24.7 2.5 %collective-permute-start.4 = (bf16[2,9,16,128]{3,2,1,0:T(8,128)(2,1)S(1)}, bf16[2,9,16,128]{3,2,1,0:T(8,128)(2,1)S(1)}, u32[]{:S(2)}, u32[]{:S(2)}) collective-permute-start(bf16[2,9,16,128]{3,2,1,0:T(8,128)(2,1)S(1)} %get-tuple-element.42), channel_id=1, source_target_pairs={{0,1},{1,0},{2,3},{3,2},{4,5},{5,4},{6,7},{7,6},{8,9},{9,8},{10,11... | collective-permute-start | bytes 221192 | tf_op jit(solution)/shard_map/ppermute | solution.py:103
  24.7 6.5 %collective-permute-start.5 = (bf16[2,9,16,128]{3,2,1,0:T(8,128)(2,1)S(1)}, bf16[2,9,16,128]{3,2,1,0:T(8,128)(2,1)S(1)}, u32[]{:S(2)}, u32[]{:S(2)}) collective-permute-start(bf16[2,9,16,128]{3,2,1,0:T(8,128)(2,1)S(1)} %get-tuple-element.43), channel_id=1, source_target_pairs={{0,15},{1,2},{2,1},{3,4},{4,3},{5,6},{6,5},{7,8},{8,7},{9,10},{10,... | collective-permute-start | bytes 221192 | tf_op jit(solution)/shard_map/ppermute | solution.py:102
  31.2 3.9 %collective-permute-start.6 = (bf16[2,2,2,16,128]{4,3,2,1,0:T(8,128)(2,1)S(1)}, bf16[2,2,2,16,128]{4,3,2,1,0:T(8,128)(2,1)S(1)}, u32[]{:S(2)}, u32[]{:S(2)}) collective-permute-start(bf16[2,2,2,16,128]{4,3,2,1,0:T(8,128)(2,1)S(1)} %corner_pack.2), channel_id=1, source_target_pairs={{0,16},{1,17},{2,18},{3,19},{4,20},{5,21},{6,22},{7,23},{8,24},{9,... | collective-permute-start | bytes 98312 | tf_op jit(solution)/shard_map/ppermute | solution.py:89
  35.1 3.0 %copy-start.1 = (bf16[8,16,16,512]{3,2,1,0:T(8,128)(2,1)S(1)}, bf16[8,16,16,512]{3,2,1,0:T(8,128)(2,1)}, u32[]{:S(2)}) copy-start(bf16[8,16,16,512]{3,2,1,0:T(8,128)(2,1)} %res_hbm.1) | copy-start | bytes 6291460
  36.0 8.6 %collective-permute-start.7 = (bf16[2,2,17,16,128]{4,3,2,1,0:T(8,128)(2,1)S(1)}, bf16[2,2,17,16,128]{4,3,2,1,0:T(8,128)(2,1)S(1)}, u32[]{:S(2)}, u32[]{:S(2)}) collective-permute-start(bf16[2,2,17,16,128]{4,3,2,1,0:T(8,128)(2,1)S(1)} %get-tuple-element.46), channel_id=1, source_target_pairs={{0,16},{1,17},{2,18},{3,19},{4,20},{5,21},{6,22},{7,23},{8,24},{9,... | collective-permute-start | bytes 835592 | tf_op jit(solution)/shard_map/ppermute | solution.py:89
  37.6 1.4 %collective-permute-start.8 = (bf16[2,9,16,128]{3,2,1,0:T(8,128)(2,1)S(1)}, bf16[2,9,16,128]{3,2,1,0:T(8,128)(2,1)S(1)}, u32[]{:S(2)}, u32[]{:S(2)}) collective-permute-start(bf16[2,9,16,128]{3,2,1,0:T(8,128)(2,1)S(1)} %get-tuple-element.47), channel_id=1, source_target_pairs={{0,1},{1,0},{2,3},{3,2},{4,5},{5,4},{6,7},{7,6},{8,9},{9,8},{10,11... | collective-permute-start | bytes 221192 | tf_op jit(solution)/shard_map/ppermute | solution.py:103
  37.6 6.5 %collective-permute-start.9 = (bf16[2,9,16,128]{3,2,1,0:T(8,128)(2,1)S(1)}, bf16[2,9,16,128]{3,2,1,0:T(8,128)(2,1)S(1)}, u32[]{:S(2)}, u32[]{:S(2)}) collective-permute-start(bf16[2,9,16,128]{3,2,1,0:T(8,128)(2,1)S(1)} %get-tuple-element.48), channel_id=1, source_target_pairs={{0,15},{1,2},{2,1},{3,4},{4,3},{5,6},{6,5},{7,8},{8,7},{9,10},{10,... | collective-permute-start | bytes 221192 | tf_op jit(solution)/shard_map/ppermute | solution.py:102
  44.0 3.9 %collective-permute-start.10 = (bf16[2,2,2,16,128]{4,3,2,1,0:T(8,128)(2,1)S(1)}, bf16[2,2,2,16,128]{4,3,2,1,0:T(8,128)(2,1)S(1)}, u32[]{:S(2)}, u32[]{:S(2)}) collective-permute-start(bf16[2,2,2,16,128]{4,3,2,1,0:T(8,128)(2,1)S(1)} %corner_pack.3), channel_id=1, source_target_pairs={{0,16},{1,17},{2,18},{3,19},{4,20},{5,21},{6,22},{7,23},{8,24},{9,... | collective-permute-start | bytes 98312 | tf_op jit(solution)/shard_map/ppermute | solution.py:89
  51.4 1.3 %copy-start.2 = (f32[2,8,16,16,128]{4,3,2,1,0:T(8,128)}, f32[2,8,16,16,128]{4,3,2,1,0:T(8,128)S(1)}, u32[]{:S(2)}) copy-start(f32[2,8,16,16,128]{4,3,2,1,0:T(8,128)S(1)} %get-tuple-element.53.part_ref) | copy-start | bytes 6291460
  52.7 14.0 %all-to-all-start = ((bf16[16,32,256]{2,1,0:T(8,128)(2,1)}), bf16[16,32,256]{2,1,0:T(8,128)(2,1)S(1)}, u32[]{:S(2)}, u32[]{:S(2)}) async-start(bf16[16,32,256]{2,1,0:T(8,128)(2,1)} %bitcast.3), calls=%async_computation | async-start | bytes 524288 | tf_op jit(solution)/shard_map/all_to_all | solution.py:661
  56.3 3.7 %collective-permute-start.11 = (bf16[2,16,128]{2,1,0:T(8,128)(2,1)S(1)}, bf16[2,16,128]{2,1,0:T(8,128)(2,1)S(1)}, u32[]{:S(2)}, u32[]{:S(2)}) collective-permute-start(bf16[2,16,128]{2,1,0:T(8,128)(2,1)S(1)} %get-tuple-element.55), channel_id=1, source_target_pairs={{0,16},{1,17},{2,18},{3,19},{4,20},{5,21},{6,22},{7,23},{8,24},{9,... | collective-permute-start | bytes 24584 | tf_op jit(solution)/shard_map/ppermute | solution.py:89
  60.0 7.4 %collective-permute-start.13 = (bf16[2,8,16,128]{3,2,1,0:T(8,128)(2,1)S(1)}, bf16[2,8,16,128]{3,2,1,0:T(8,128)(2,1)S(1)}, u32[]{:S(2)}, u32[]{:S(2)}) collective-permute-start(bf16[2,8,16,128]{3,2,1,0:T(8,128)(2,1)S(1)} %get-tuple-element.58), channel_id=1, source_target_pairs={{0,1},{1,2},{2,3},{3,4},{4,5},{5,6},{6,7},{7,8},{8,9},{9,10},{10,1... | collective-permute-start | bytes 196616 | tf_op jit(solution)/shard_map/ppermute | solution.py:89
  60.1 7.3 %collective-permute-start.12 = (bf16[2,16,16,128]{3,2,1,0:T(8,128)(2,1)S(1)}, bf16[2,16,16,128]{3,2,1,0:T(8,128)(2,1)S(1)}, u32[]{:S(2)}, u32[]{:S(2)}) collective-permute-start(bf16[2,16,16,128]{3,2,1,0:T(8,128)(2,1)S(1)} %get-tuple-element.57), channel_id=1, source_target_pairs={{0,16},{1,17},{2,18},{3,19},{4,20},{5,21},{6,22},{7,23},{8,24},{9,... | collective-permute-start | bytes 393224 | tf_op jit(solution)/shard_map/ppermute | solution.py:89
  66.8 4.0 %collective-permute-start.14 = (f32[32,256]{1,0:T(8,128)S(1)}, f32[32,256]{1,0:T(8,128)S(1)}, u32[]{:S(2)}, u32[]{:S(2)}) collective-permute-start(f32[32,256]{1,0:T(8,128)S(1)} %convert_reduce_fusion), channel_id=1, source_target_pairs={{0,16},{1,17},{2,18},{3,19},{4,20},{5,21},{6,22},{7,23},{8,24},{9,... | collective-permute-start | bytes 98312 | tf_op jit(solution)/shard_map/ppermute | solution.py:89
  67.4 1.6 %copy-start.3 = (f32[2,8,16,16,128]{4,3,2,1,0:T(8,128)S(1)}, f32[2,8,16,16,128]{4,3,2,1,0:T(8,128)}, u32[]{:S(2)}) copy-start(f32[2,8,16,16,128]{4,3,2,1,0:T(8,128)} %copy-done.2) | copy-start | bytes 6291460

commit v5 on v4

--- a/solution.py
+++ b/solution.py
@@ -9,6 +9,7 @@
 from jax.sharding import PartitionSpec as P
 
 LANES = 128
+TILE = 256
 SUB = 16
 VMEM_LIMIT = 16 * 1024 * 1024
 
@@ -28,7 +29,8 @@
         self.blocks = vectors.shape[0]
         self.width = vectors.shape[-1]
         self.full = self.blocks * self.width
-        self.groups = resident.shape[-1] // LANES
+        self.res = resident.shape[-1]
+        self.wide = self.res + self.full + self.width
         self.ex, self.ey, self.ez = inv_mass.shape
         self.cells, self.nodes = connectivity.shape[2:]
         self.n1 = round(self.nodes ** (1.0 / 3.0))
@@ -104,9 +106,8 @@
     return near, far
 
 
-def order_kernel(sz, first, count, conn_ref, matrix_ref, out_ref):
-    for slot in range(count):
-        cell = first + slot
+def order_kernel(sz, conn_ref, matrix_ref, out_ref):
+    for cell in range(sz.cells):
         x0, y0, z0 = sz.origins[cell]
         conn = conn_ref[cell : cell + 1, :].astype(f32)
         li = jnp.floor((conn + 0.5) * (1.0 / (sz.gy * sz.gz)))
@@ -127,10 +128,19 @@
         row = lax.broadcasted_iota(jnp.int32, (sz.depth, sz.nodes), 0)
         pick = (row == index).astype(f32).astype(bf16)
         half = jnp.dot(pick[: sz.rows], matrix_ref[...], preferred_element_type=f32)
-        whole = lax.dot_general(
-            half.astype(bf16), pick, (((1,), (1,)), ((), ())), preferred_element_type=f32
-        )
-        out_ref[slot] = whole.astype(bf16)
+        half = half.astype(bf16)
+        cuts = list(range(0, sz.depth, TILE)) + [sz.depth]
+        for r0, r1 in zip(cuts[:-1], cuts[1:]):
+            r1 = min(r1, sz.rows)
+            block = lax.dot_general(
+                half[r0:r1], pick[r0:], (((1,), (1,)), ((), ())), preferred_element_type=f32
+            ).astype(bf16)
+            out_ref[cell, r0:r1, r0:] = block
+            for c0, c1 in zip(cuts[:-1], cuts[1:]):
+                if c0 > r0:
+                    mirror = block[:, c0 - r0 : c1 - r0].T
+                    c1 = min(c1, sz.rows)
+                    out_ref[cell, c0:c1, r0:r1] = mirror[: c1 - c0]
 
 
 def field_row(inv, pot):
@@ -165,18 +175,16 @@
     sz, vec_hbm, res_hbm, inv_hbm, pot_hbm, mat_hbm, conn_hbm,
     to_x, to_y, mat_ref, conn_ref, at_x, at_y, sems,
 ):
-    slabs = sz.blocks + 1
     pairs = [
         (inv_hbm.at[0], at_x.at[0]), (pot_hbm.at[0], at_x.at[1]),
         (inv_hbm.at[:, 0], at_y.at[0]), (pot_hbm.at[:, 0], at_y.at[1]),
+        (res_hbm.at[0], to_x.at[:, :, pl.ds(0, sz.res)]),
+        (res_hbm.at[:, 0], to_y.at[:, :, pl.ds(0, sz.res)]),
     ]
     for b in range(sz.blocks):
-        pairs.append((vec_hbm.at[b, 0], to_x.at[pl.ds(b * sz.ey, sz.ey)]))
-        pairs.append((vec_hbm.at[b, :, 0], to_y.at[pl.ds(b * sz.ex, sz.ex)]))
-    for g in range(sz.groups):
-        lanes = pl.ds(g * LANES, LANES)
-        pairs.append((res_hbm.at[0, :, :, lanes], to_x.at[pl.ds((slabs + g) * sz.ey, sz.ey)]))
-        pairs.append((res_hbm.at[:, 0, :, lanes], to_y.at[pl.ds((slabs + g) * sz.ex, sz.ex)]))
+        lanes = pl.ds(sz.res + b * sz.width, sz.width)
+        pairs.append((vec_hbm.at[b, 0], to_x.at[:, :, lanes]))
+        pairs.append((vec_hbm.at[b, :, 0], to_y.at[:, :, lanes]))
     pairs += [(mat_hbm, mat_ref), (conn_hbm, conn_ref)]
     copies = [pltpu.make_async_copy(a, b, sems.at[k]) for k, (a, b) in enumerate(pairs)]
     for copy in copies:
@@ -184,34 +192,31 @@
     for copy in copies[:4]:
         copy.wait()
     for j, row in field_rows(sz, at_x[0], at_x[1], sz.ey):
-        to_x[sz.blocks * sz.ey + j] = row
+        to_x[j, :, sz.res + sz.full :] = row
     for i, row in field_rows(sz, at_y[0], at_y[1], sz.ex):
-        to_y[sz.blocks * sz.ex + i] = row
+        to_y[i, :, sz.res + sz.full :] = row
     for copy in copies[4:]:
         copy.wait()
 
 
-def ghost_corner_kernel(sz, from_y, out_ref):
-    for part in range(out_ref.shape[0]):
-        out_ref[part] = from_y[part * sz.ex]
-
-
 def turn_kernel(sz, res_ref, from_x, from_y, corner, out_ref):
-    slabs = sz.blocks + 1
     own = sz.own_edges * sz.ez
-    for g in range(sz.groups):
-        lanes = slice(g * LANES, (g + 1) * LANES)
+    for g in range(0, sz.res, LANES):
+        lanes = slice(g, g + LANES)
         out_ref[lanes, :own] = res_ref[:, lanes].T
-        ghost_x = from_x[(slabs + g) * sz.ey : (slabs + g + 1) * sz.ey]
-        ghost_y = from_y[(slabs + g) * sz.ex : (slabs + g + 1) * sz.ex]
         rest = sz.edges - sz.own_edges - sz.ey - sz.gx
-        parts = [ghost_x, ghost_y, corner[slabs + g : slabs + g + 1]]
+        parts = [from_x[:, :, lanes], from_y[:, :, lanes], corner[:, :, lanes]]
         if rest:
             parts.append(jnp.zeros((rest, sz.ez, LANES), bf16))
         ghosts = jnp.concatenate(parts, axis=0)
         out_ref[lanes, own:] = ghosts.reshape(-1, LANES).T
 
 
+def vectors_of(sz, edge):
+    lanes = [slice(sz.res + b * sz.width, sz.res + (b + 1) * sz.width) for b in range(sz.blocks)]
+    return jnp.stack([edge[:, at] for at in lanes]).astype(f32)
+
+
 class Nodes:
     def __init__(self, sz, vec, from_x, from_y, own_inv, own_pot, ghost_x, ghost_y, corners=None):
         self.sz, self.vec, self.from_x, self.from_y = sz, vec, from_x, from_y
@@ -221,11 +226,7 @@
         sz = self.sz
         if i < sz.ex and j < sz.ey:
             return self.vec[:, i, j].astype(f32)
-        if i == sz.ex:
-            parts = [self.from_x[b * sz.ey + j] for b in range(sz.blocks)]
-        else:
-            parts = [self.from_y[b * sz.ex + i] for b in range(sz.blocks)]
-        return jnp.stack(parts).astype(f32)
+        return vectors_of(sz, self.from_x[j] if i == sz.ex else self.from_y[i])
 
     def field(self, at, i, j):
         sz = self.sz
@@ -265,41 +266,45 @@
         return total
 
 
-def plain_edges(sz):
-    return [(i, j) for i in range(sz.gx) for j in range(sz.gy) if sz.corner(i, j) is None]
-
-
 def corner_edges(sz):
     return [(i, j) for i in (0, sz.ex) for j in (0, sz.ey)]
 
 
-def main_products(sz, u_ref, mat_refs, rhs_ref, out_ref):
+def main_products(sz, prepare, u_ref, mat_refs, rhs_ref, out_ref):
     width = sz.width
     flat = sz.gx * sz.gy * sz.gz
     u_flat = u_ref.reshape(sz.blocks * flat, width)
     matrices = [ref.at[c] for ref in mat_refs for c in range(ref.shape[0])]
-    rhs_ref[: sz.base] = jnp.zeros((sz.base, sz.full), f32)
     last = sz.nodes // 8 * 8
-    rhs_ref[last:] = jnp.zeros((sz.depth - last, sz.full), f32)
+    ready = set()
     for cell, (x0, y0, z0) in enumerate(sz.origins):
+        slot = cell % 2
+        if cell < 2:
+            rhs_ref[slot, : sz.base] = jnp.zeros((sz.base, sz.full), f32)
+            rhs_ref[slot, last:] = jnp.zeros((sz.depth - last, sz.full), f32)
+        for place, i, j, count in sz.runs(cell):
+            for at in range(j, j + count):
+                if (x0 + i, y0 + at) not in ready:
+                    prepare(x0 + i, y0 + at)
+                    ready.add((x0 + i, y0 + at))
         z1 = z0 + sz.p
         wrap = z1 % sz.gz
         for b in range(sz.blocks):
             lanes = slice(b * width, (b + 1) * width)
             for place, i, j, count in sz.runs(cell):
                 row = sz.base + place * sz.p
-                rhs_ref[row : row + count * sz.p, lanes] = u_ref[
+                rhs_ref[slot, row : row + count * sz.p, lanes] = u_ref[
                     b, x0 + i, y0 + j : y0 + j + count, z0:z1
                 ].reshape(count * sz.p, width)
         for b in range(sz.blocks):
             lanes = slice(b * width, (b + 1) * width)
             for place, i, j, count in sz.runs(cell):
                 start = b * flat + ((x0 + i) * sz.gy + y0 + j) * sz.gz + wrap
-                rhs_ref[sz.tail + place : sz.tail + place + count, lanes] = u_flat[
+                rhs_ref[slot, sz.tail + place : sz.tail + place + count, lanes] = u_flat[
                     pl.ds(start, count, stride=sz.gz)
                 ]
         out_ref[cell] = jnp.dot(
-            matrices[cell][...], rhs_ref[...].astype(bf16), preferred_element_type=f32
+            matrices[cell][...], rhs_ref[slot].astype(bf16), preferred_element_type=f32
         )
 
 
@@ -371,22 +376,23 @@
     mats = refs[:n_mat]
     prod_ref, ghost_x, ghost_y, u_ref, rhs_ref = refs[n_mat:]
     for j in range(sz.ey):
-        ghost_x[0, j], ghost_x[1, j] = fields_of(from_x[sz.blocks * sz.ey + j])
+        ghost_x[0, j], ghost_x[1, j] = fields_of(from_x[j, :, sz.res + sz.full :])
     for i in range(sz.ex):
-        ghost_y[0, i], ghost_y[1, i] = fields_of(from_y[sz.blocks * sz.ex + i])
+        ghost_y[0, i], ghost_y[1, i] = fields_of(from_y[i, :, sz.res + sz.full :])
     nodes = Nodes(sz, vec, from_x, from_y, own_inv, own_pot, ghost_x, ghost_y)
-    for i, j in plain_edges(sz):
+
+    def prepare(i, j):
         u_ref[:, i, j] = nodes.x(i, j) * nodes.inv(i, j)
-    main_products(sz, u_ref, mats, rhs_ref, prod_ref)
+
+    main_products(sz, prepare, u_ref, mats, rhs_ref, prod_ref)
 
 
 def first_corner(sz, n_mat, even_ref, vec, from_x, from_y, corner, own_inv, own_pot, ghost_x, ghost_y,
                  prod_ref, *refs):
     mats = refs[:n_mat]
     acc_ref, face, near, far, last_x, last_field, small_ref, tail_ref = refs[n_mat:]
-    last_field[0], last_field[1] = fields_of(corner[sz.blocks])
-    for b in range(sz.blocks):
-        last_x[b] = corner[b].astype(f32)
+    last_field[0], last_field[1] = fields_of(corner[0, :, sz.res + sz.full :])
+    last_x[...] = vectors_of(sz, corner[0])
     nodes = Nodes(sz, vec, from_x, from_y, own_inv, own_pot, ghost_x, ghost_y, last_field)
     u_corner = []
     for i, j in corner_edges(sz):
@@ -402,13 +408,15 @@
     prod_ref, y_ref, u_ref, rhs_ref = refs[n_mat:]
     nodes = Nodes(sz, vec, from_x, from_y, own_inv, own_pot, ghost_x, ghost_y)
     sums = Sums(sz, even_ref[0] == 0, acc_in, face_in, near_in, far_in)
-    for i, j in plain_edges(sz):
+
+    def prepare(i, j):
         old, inv = nodes.x(i, j), nodes.inv(i, j)
         image = inv * sums.at(i, j) + nodes.pot(i, j) * old
         new = (image - center_shift * old) / half_width
         y_ref[:, i, j] = new
         u_ref[:, i, j] = inv * new
-    main_products(sz, u_ref, mats, rhs_ref, prod_ref)
+
+    main_products(sz, prepare, u_ref, mats, rhs_ref, prod_ref)
 
 
 def second_corner(sz, n_mat, even_ref, vec, from_x, from_y, own_inv, own_pot, ghost_x, ghost_y, last_x,
@@ -436,21 +444,23 @@
     prod_ref, new_ref, u_ref, rhs_ref = refs[n_mat:]
     nodes = Nodes(sz, vec, from_x, from_y, own_inv, own_pot, ghost_x, ghost_y)
     sums = Sums(sz, even_ref[0] == 0, acc_in, face_in, near_in, far_in)
-    for i, j in plain_edges(sz):
+
+    def prepare(i, j):
         old, inv = y_ref[:, i, j], nodes.inv(i, j)
         image = inv * sums.at(i, j) + nodes.pot(i, j) * old
         new = 2.0 * (image - center_shift * old) / half_width - nodes.x(i, j)
         new_ref[:, i, j] = new
         u_ref[:, i, j] = inv * new
-    main_products(sz, u_ref, mats, rhs_ref, prod_ref)
+
+    main_products(sz, prepare, u_ref, mats, rhs_ref, prod_ref)
 
 
 def third_corner(sz, n_mat, norm_scale, even_ref, vec, from_x, from_y, own_inv, own_pot, ghost_x, ghost_y,
                  last_x, last_field, acc_in, face_in, near_in, far_in, corner_in, prod_ref, y_ref,
                  y_corner, new_ref, turned, *refs):
     mats = refs[:n_mat]
-    part_ref, face, side, corner, margin = refs[n_mat : n_mat + 5]
-    acc_ref, rows_ref, small_ref, tail_ref = refs[n_mat + 5 :]
+    out_hbm, edge_x, edge_y, face, side, corner, margin = refs[n_mat : n_mat + 7]
+    part_ref, sem, acc_ref, rows_ref, small_ref, tail_ref = refs[n_mat + 7 :]
     nodes = Nodes(sz, vec, from_x, from_y, own_inv, own_pot, ghost_x, ghost_y, last_field)
     sums = Sums(sz, even_ref[0] == 0, acc_in, face_in, near_in, far_in, corner_in)
     u_corner, new_corner = [], []
@@ -488,13 +498,20 @@
             image = inv * acc + nodes.pot(i, j) * new
             value = 2.0 * (image - center_shift * new) / half_width - old
             part_ref[:, i, j] = value
+            if i == 0:
+                edge_x[:, j] = value
+            elif j == 0:
+                edge_y[:, i - 1] = value
             put_row(i * sz.ey + j, value.astype(bf16))
+    copy = pltpu.make_async_copy(part_ref, out_hbm, sem)
+    copy.start()
     for at in range(sz.own_edges + sz.ey + sz.gx, sz.edges):
         rows_ref[at] = jnp.zeros((sz.ez, sz.full), bf16)
     local = jnp.dot(
         turned[...], rows_ref[...].reshape(sz.edges * sz.ez, sz.full), preferred_element_type=f32
     )
     margin[...] = (local * norm_scale).astype(bf16)
+    copy.wait()
 
 
 def last_side_kernel(sz, side_ref, corner_ref, face_in, out_ref, face_out):
@@ -506,35 +523,46 @@
         out_ref[:, i] = value.astype(out_ref.dtype)
 
 
-def last_kernel(sz, part_ref, face, side, out_ref):
-    for i in range(sz.ex):
-        for j in range(sz.ey):
-            value = part_ref[:, i, j]
-            if i == 0:
-                value = value + face[:, j].astype(f32)
-            if j == 0:
-                value = value + side[:, i].astype(f32)
-            out_ref[:, i, j] = value
+def last_kernel(sz, old_hbm, edge_x, edge_y, face, side, out_hbm, at_x, at_y, sems):
+    del old_hbm
+    for j in range(sz.ey):
+        value = edge_x[:, j] + face[:, j].astype(f32)
+        if j == 0:
+            value = value + side[:, 0].astype(f32)
+        at_x[:, j] = value
+    for i in range(1, sz.ex):
+        at_y[:, i - 1] = edge_y[:, i - 1] + side[:, i].astype(f32)
+    copies = [
+        pltpu.make_async_copy(at_x, out_hbm.at[:, 0], sems.at[0]),
+        pltpu.make_async_copy(at_y, out_hbm.at[:, pl.ds(1, sz.ex - 1), 0], sems.at[1]),
+    ]
+    for copy in copies:
+        copy.start()
+    for copy in copies:
+        copy.wait()
 
 
 def like(shape, dtype):
     return jax.ShapeDtypeStruct(shape, dtype)
 
 
-def call(kernel, name, flops, out_shape, scratch, operands, hbm=0, scalar_first=False, aliases=None):
+def call(kernel, name, flops, out_shape, scratch, operands, hbm=0, scalar_first=False, aliases=None,
+         out_hbm=0):
     out_shape = [like(s.shape, s.dtype) for s in out_shape]
     size = sum(math.prod(s.shape) * jnp.dtype(s.dtype).itemsize for s in (*operands, *out_shape))
     whole = pl.BlockSpec(memory_space=pltpu.VMEM)
     specs = [pl.BlockSpec(memory_space=pltpu.HBM)] * hbm + [whole] * (len(operands) - hbm)
     if scalar_first:
         specs[0] = pl.BlockSpec(memory_space=pltpu.SMEM)
+    out_specs = [pl.BlockSpec(memory_space=pltpu.HBM)] * out_hbm + [whole] * (len(out_shape) - out_hbm)
+    out_shape = [pltpu.HBM(s.shape, s.dtype) for s in out_shape[:out_hbm]] + out_shape[out_hbm:]
     operands = [pltpu.with_memory_space_constraint(a, pltpu.HBM) for a in operands[:hbm]] + list(
         operands[hbm:]
     )
     return pl.pallas_call(
         kernel,
         in_specs=specs,
-        out_specs=[whole] * len(out_shape),
+        out_specs=out_specs,
         out_shape=out_shape,
         scratch_shapes=scratch,
         input_output_aliases=aliases or {},
@@ -551,37 +579,28 @@
     blocks, ez, width, full = sz.blocks, sz.ez, sz.width, sz.full
     res_count = resident.shape[-1]
     tile = (ez, width)
-    parts = blocks + 1 + sz.groups
 
     conn = connectivity.reshape(sz.cells, sz.nodes)
     to_x, to_y, cell_matrix, conn = call(
         functools.partial(pack_kernel, sz), "pack", 0,
-        [like((parts * sz.ey,) + tile, bf16), like((parts * sz.ex,) + tile, bf16), cell_matrix, conn],
+        [like((sz.ey, ez, sz.wide), bf16), like((sz.ex, ez, sz.wide), bf16), cell_matrix, conn],
         [
             pltpu.VMEM((2, sz.ey, ez), f32), pltpu.VMEM((2, sz.ex, ez), f32),
-            pltpu.SemaphoreType.DMA((6 + 2 * blocks + 2 * sz.groups,)),
+            pltpu.SemaphoreType.DMA((8 + 2 * blocks,)),
         ],
         [vectors, resident, inv_mass, potential, cell_matrix, conn], hbm=6,
     )
     from_x = send(to_x, -1, 0)
     from_y = send(to_y, 0, -1)
 
-    halves = 2 if sz.cells % 2 == 0 else 1
-    step = sz.cells // halves
-    mats = []
-    for at in range(0, sz.cells, step):
-        mats += call(
-            functools.partial(order_kernel, sz, at, step), "order_cells",
-            4 * step * sz.depth**3, [like((step, sz.rows, sz.depth), bf16)], [], [conn, cell_matrix],
-        )
+    mats = call(
+        functools.partial(order_kernel, sz), "order_cells", 4 * sz.cells * sz.depth**3,
+        [like((sz.cells, sz.rows, sz.depth), bf16)], [], [conn, cell_matrix],
+    )
     own_inv = jnp.broadcast_to(inv_mass[..., None], inv_mass.shape + (width,))
     own_pot = jnp.broadcast_to(potential[..., None], inv_mass.shape + (width,))
     parity = jnp.reshape(lax.axis_index("dy") % 2, (1,)).astype(jnp.int32)
-    (ghost_corner,) = call(
-        functools.partial(ghost_corner_kernel, sz), "ghost_corner", 0,
-        [like((parts,) + tile, bf16)], [], [from_y],
-    )
-    ghost_corner = send(ghost_corner, -1, 0)
+    ghost_corner = send(from_y[:1], -1, 0)
 
     grid = (blocks, sz.gx, sz.gy) + tile
     own = (blocks, sz.ex, sz.ey) + tile
@@ -591,7 +610,7 @@
         like((blocks, sz.gx) + tile, bf16),
         like((blocks, sz.gx) + tile, bf16),
     ]
-    main_scratch = [pltpu.VMEM(grid, f32), pltpu.VMEM((sz.depth, full), f32)]
+    main_scratch = [pltpu.VMEM(grid, f32), pltpu.VMEM((2, sz.depth, full), f32)]
     corner_scratch = [
         pltpu.VMEM((LANES, full), f32),
         pltpu.VMEM((sz.cells, sz.base + sz.rows - sz.tail, full), f32),
@@ -646,16 +665,17 @@
         [products, like(grid, f32)], main_scratch,
         [parity, *state, acc, *got, y1, *mats], scalar_first=True,
     )
-    part, face, side, corner, local = call(
+    filtered, edge_x, edge_y, face, side, corner, local = call(
         functools.partial(third_corner, sz, n_mat, norm_scale), "third_corner",
         small_flops + 2 * res_count * sz.edges * ez * full,
         [
-            like(own, f32), like((blocks, sz.ey) + tile, bf16), like((blocks, sz.ex) + tile, f32),
+            like(own, f32), like((blocks, sz.ey) + tile, f32), like((blocks, sz.ex - 1) + tile, f32),
+            like((blocks, sz.ey) + tile, bf16), like((blocks, sz.ex) + tile, f32),
             like(sz.edge, bf16), like((res_count, full), bf16),
         ],
-        [pltpu.VMEM(grid, f32), pltpu.VMEM((sz.edges, ez, full), bf16)] + corner_scratch,
+        [pltpu.VMEM(own, f32), pltpu.SemaphoreType.DMA, pltpu.VMEM(grid, f32), pltpu.VMEM((sz.edges, ez, full), bf16)] + corner_scratch,
         [parity, *state, *ends, acc, *got, corner, prod, y1, y1_corner, y2, turned, *mats],
-        scalar_first=True,
+        scalar_first=True, out_hbm=1,
     )
 
     pieces = lax.all_to_all(local.reshape(ny, -1, full), "dy", 0, 0)
@@ -672,7 +692,12 @@
     face = send(face, 1, 0)
     side = send(side, 0, 1)
     (filtered,) = call(
-        functools.partial(last_kernel, sz), "last", 0, [like(own, f32)], [], [part, face, side]
+        functools.partial(last_kernel, sz), "last", 0, [like(own, f32)],
+        [
+            pltpu.VMEM((blocks, sz.ey) + tile, f32), pltpu.VMEM((blocks, sz.ex - 1) + tile, f32),
+            pltpu.SemaphoreType.DMA((2,)),
+        ],
+        [filtered, edge_x, edge_y, face, side], hbm=1, out_hbm=1, aliases={0: 0},
     )
     return (filtered, margin)
 

time: 71.7 us -> 72.2 us (level)
  starting transfers between devices: 20.1 us -> 23.6 us
  waiting for transfers between devices: 21.8 us -> 19.1 us
    ppermute x11, starting transfers between devices: 13.5 us -> 16.6 us  [send(): return lax.ppermute(value, ('dx', 'dy'), pairs)]
    ppermute x11, waiting for transfers between devices: 6.69 us -> 5.47 us  [send(): return lax.ppermute(value, ('dx', 'dy'), pairs)]
    all_to_all x1, waiting for transfers between devices: 6.12 us -> 5.09 us  [body(): pieces = lax.all_to_all(local.reshape(ny, -1, full), 'dy', 0, 0)]
    pallas_call x15 -> x13, Pallas kernels: 23.2 us -> 22.6 us  [call(): pl.pallas_call(kernel, in_specs=specs, out_specs=out_specs, out_shape=out...]
  transfers between devices with their start and end apart: 16 -> 16, of which waited for: 8 -> 7; matrix products, arithmetic and copies ran while one was open for 1% -> 1% of each run, Pallas kernels for 22% -> 20%
where the time goes in v5:
time: 72.2 us; the launch traced here: 71.8 us
  starting transfers between devices  23.6 us (33%)
  Pallas kernels  22.6 us (31%)
  waiting for transfers between devices  19.1 us (26%)
  local copies, waits for them, and re-layouts  5.02 us (7%)
  between operations  0.81 us (1%)
    pallas_call x13, Pallas kernels, call(): pl.pallas_call(kernel, in_specs=specs, out_specs=out_specs, out_shape=out...  22.6 us
    ppermute x11, starting transfers between devices, send(): return lax.ppermute(value, ('dx', 'dy'), pairs)  16.6 us
    ppermute x2, waiting for transfers between devices, swap_y(): far = lax.ppermute(far, 'dy', far_pairs)  8.57 us
    ppermute x11, waiting for transfers between devices, send(): return lax.ppermute(value, ('dx', 'dy'), pairs)  5.47 us
    all_to_all x1, waiting for transfers between devices, body(): pieces = lax.all_to_all(local.reshape(ny, -1, full), 'dy', 0, 0)  5.09 us
    unnamed x16, local copies, waits for them, and re-layouts  4.35 us
    all_to_all x1, starting transfers between devices, body(): pieces = lax.all_to_all(local.reshape(ny, -1, full), 'dy', 0, 0)  3.54 us
    ppermute x2, starting transfers between devices, swap_y(): far = lax.ppermute(far, 'dy', far_pairs)  3.46 us
  transfers between devices with their start and end apart: 16, of which 7 were waited for; matrix products, arithmetic and copies ran while one was open for 1% of the time, Pallas kernels for 20%

profile of v5, /device:TPU:0, one launch (start us, length us, event | category | flops | bytes accessed | tf_op | source)
XLA Modules:
  0.0 71.8 jit_solution(3137504889127334182)
XLA Ops:
  0.6 1.7 %pack.1 = (bf16[16,16,896]{2,1,0:T(8,128)(2,1)S(1)}, bf16[8,16,896]{2,1,0:T(8,128)(2,1)S(1)}, bf16[729,729]{1,0:T(8,128)(2,1)S(1)}, s32[4,729]{1,0:T(4,128)S(1)}) custom-call(bf16[2,8,16,16,128]{4,3,2,1,0:T(8,128)(2,1)} %vec.11, bf16[8,16,16,512]{3,2,1,0:T(8,128)(2,1)} %res_hbm.1, f32[8,16,16]{2,1,0:T(8,128)} %inv_hbm.1, f32[8,16,16]{2,1,0:T(8,128)} %pot_hbm.1, ...), custom_call_target="tpu_custom_call" | custom-call | bytes 5999332 | tf_op jit(solution)/shard_map/pack/pallas_call | solution.py:562
  2.3 5.5 %collective-permute-start.1 = (bf16[8,16,896]{2,1,0:T(8,128)(2,1)S(1)}, bf16[8,16,896]{2,1,0:T(8,128)(2,1)S(1)}, u32[]{:S(2)}, u32[]{:S(2)}) collective-permute-start(bf16[8,16,896]{2,1,0:T(8,128)(2,1)S(1)} %get-tuple-element.34), channel_id=1, source_target_pairs={{0,15},{1,0},{2,1},{3,2},{4,3},{5,4},{6,5},{7,6},{8,7},{9,8},{10,9... | collective-permute-start | bytes 688136 | tf_op jit(solution)/shard_map/ppermute | solution.py:91
  7.8 1.5 %collective-permute-start = (bf16[16,16,896]{2,1,0:T(8,128)(2,1)S(1)}, bf16[16,16,896]{2,1,0:T(8,128)(2,1)S(1)}, u32[]{:S(2)}, u32[]{:S(2)}) collective-permute-start(bf16[16,16,896]{2,1,0:T(8,128)(2,1)S(1)} %get-tuple-element.33), channel_id=1, source_target_pairs={{0,16},{1,17},{2,18},{3,19},{4,20},{5,21},{6,22},{7,23},{8,24},{9,... | collective-permute-start | bytes 1376264 | tf_op jit(solution)/shard_map/ppermute | solution.py:91
  9.3 7.4 %order_cells.1.refs_0_ = bf16[4,736,768]{2,1,0:T(8,128)(2,1)S(1)} custom-call(s32[4,729]{1,0:T(4,128)S(1)} %get-tuple-element.35.conn_ref, bf16[729,729]{1,0:T(8,128)(2,1)S(1)} %get-tuple-element.36.matrix_ref), custom_call_target="tpu_custom_call" | custom-call | flops 7247757312 | bytes 5596530 | tf_op jit(solution)/shard_map/order_cells/pallas_call | solution.py:562
  16.7 0.0 copy-start
  16.7 2.0 %copy-done = bf16[4,736,768]{2,1,0:T(8,128)(2,1)} copy-done((bf16[4,736,768]{2,1,0:T(8,128)(2,1)}, bf16[4,736,768]{2,1,0:T(8,128)(2,1)S(1)}, u32[]{:S(2)}) %copy-start) | copy-done | bytes 4522008
  18.7 0.0 collective-permute-done.1.from_y
  18.7 0.6 collective-permute-start.2
  19.3 0.0 collective-permute-done.from_x
  19.3 0.3 broadcast_in_dim.4.own_inv
  19.7 0.3 broadcast_in_dim.5.own_pot
  20.0 2.3 %copy-done.1 = bf16[4,736,768]{2,1,0:T(8,128)(2,1)S(1)} copy-done((bf16[4,736,768]{2,1,0:T(8,128)(2,1)S(1)}, bf16[4,736,768]{2,1,0:T(8,128)(2,1)}, u32[]{:S(2)}) %copy-start.1) | copy-done | bytes 4522008
  22.3 1.5 %first_main.1 = (f32[4,736,256]{2,1,0:T(8,128)S(1)}, f32[2,16,16,128]{3,2,1,0:T(8,128)S(1)}, f32[2,8,16,128]{3,2,1,0:T(8,128)S(1)}) custom-call(bf16[2,8,16,16,128]{4,3,2,1,0:T(8,128)(2,1)S(1)} %copy-done.2, bf16[16,16,896]{2,1,0:T(8,128)(2,1)S(1)} %collective-permute-done.from_x, bf16[8,16,896]{2,1,0:T(8,128)(2,1)S(1)} %collective-permute-done.1.from_y, ...), custom_call_target="tpu_custom_call" | custom-call | flops 1157627904 | bytes 11763712 | tf_op jit(solution)/shard_map/first_main/pallas_call | solution.py:562
  23.8 0.0 collective-permute-done.2.corner
  23.8 0.9 %first_corner.1 = (f32[2,9,17,16,128]{4,3,2,1,0:T(8,128)S(1)}, bf16[2,2,17,16,128]{4,3,2,1,0:T(8,128)(2,1)S(1)}, bf16[2,9,16,128]{3,2,1,0:T(8,128)(2,1)S(1)}, bf...) custom-call(s32[1]{0:T(128)} %bitcast.even_ref, ...), custom_call_target="tpu_custom_call" | custom-call | flops 192937984 | bytes 14757892 | tf_op jit(solution)/shard_map/first_corner/pallas_call | solution.py:562
  24.6 1.6 %collective-permute-start.3 = (bf16[2,2,17,16,128]{4,3,2,1,0:T(8,128)(2,1)S(1)}, bf16[2,2,17,16,128]{4,3,2,1,0:T(8,128)(2,1)S(1)}, u32[]{:S(2)}, u32[]{:S(2)}) collective-permute-start(bf16[2,2,17,16,128]{4,3,2,1,0:T(8,128)(2,1)S(1)} %get-tuple-element.43), channel_id=1, source_target_pairs={{0,16},{1,17},{2,18},{3,19},{4,20},{5,21},{6,22},{7,23},{8,24},{9,... | collective-permute-start | bytes 835592 | tf_op jit(solution)/shard_map/ppermute | solution.py:91
  26.2 0.0 collective-permute-start.4
  26.2 2.1 %collective-permute-start.5 = (bf16[2,9,16,128]{3,2,1,0:T(8,128)(2,1)S(1)}, bf16[2,9,16,128]{3,2,1,0:T(8,128)(2,1)S(1)}, u32[]{:S(2)}, u32[]{:S(2)}) collective-permute-start(bf16[2,9,16,128]{3,2,1,0:T(8,128)(2,1)S(1)} %get-tuple-element.45), channel_id=1, source_target_pairs={{0,15},{1,2},{2,1},{3,4},{4,3},{5,6},{6,5},{7,8},{8,7},{9,10},{10,... | collective-permute-start | bytes 221192 | tf_op jit(solution)/shard_map/ppermute | solution.py:104
  28.3 0.0 collective-permute-done.4.near.near_in
  28.3 4.4 %collective-permute-done.5.far.far_in = bf16[2,9,16,128]{3,2,1,0:T(8,128)(2,1)S(1)} collective-permute-done((bf16[2,9,16,128]{3,2,1,0:T(8,128)(2,1)S(1)}, bf16[2,9,16,128]{3,2,1,0:T(8,128)(2,1)S(1)}, u32[]{:S(2)}, u32[]{:S(2)}) %collective-permute-start.5) | collective-permute-done | bytes 73760 | tf_op jit(solution)/shard_map/ppermute | solution.py:104
  32.7 0.5 collective-permute-start.6
  33.2 0.0 collective-permute-done.3.face_in
  33.2 1.9 %second_main.1 = (f32[4,736,256]{2,1,0:T(8,128)S(1)}, f32[2,9,17,16,128]{4,3,2,1,0:T(8,128)S(1)}) custom-call(s32[1]{0:T(128)} %bitcast.even_ref, bf16[2,8,16,16,128]{4,3,2,1,0:T(8,128)(2,1)S(1)} %copy-done.2, bf16[16,16,896]{2,1,0:T(8,128)(2,1)S(1)} %collective-permute-done.from_x, bf16[8,16,896]{2,1,0:T(8,128)(2,1)S(1)} %collective-permute-done.1.from_y, ...), custom_call_target="tpu_custom_call" | custom-call | flops 1157627904 | bytes 17203204 | tf_op jit(solution)/shard_map/second_main/pallas_call | solution.py:562
  35.1 1.5 %collective-permute-done.6.corner_in = bf16[2,2,2,16,128]{4,3,2,1,0:T(8,128)(2,1)S(1)} collective-permute-done((bf16[2,2,2,16,128]{4,3,2,1,0:T(8,128)(2,1)S(1)}, bf16[2,2,2,16,128]{4,3,2,1,0:T(8,128)(2,1)S(1)}, u32[]{:S(2)}, u32[]{:S(2)}) %collective-permute-start.6) | collective-permute-done | bytes 32800 | tf_op jit(solution)/shard_map/ppermute | solution.py:91
  36.6 0.9 %second_corner.1 = (f32[2,9,17,16,128]{4,3,2,1,0:T(8,128)S(1)}, bf16[2,2,17,16,128]{4,3,2,1,0:T(8,128)(2,1)S(1)}, bf16[2,9,16,128]{3,2,1,0:T(8,128)(2,1)S(1)}, b...) custom-call(s32[1]{0:T(128)} %bitcast.even_ref, bf16[2,8,16,16,128]{4,3,2,1,0:T(8,128)(2,1)S(1)} %copy-done.2, ...), custom_call_target="tpu_custom_call" | custom-call | flops 192937984 | bytes 17760260 | tf_op jit(solution)/shard_map/second_corner/pallas_call | solution.py:562
  37.5 0.6 collective-permute-start.7
  38.1 0.0 collective-permute-start.8
  38.1 1.4 %collective-permute-start.9 = (bf16[2,9,16,128]{3,2,1,0:T(8,128)(2,1)S(1)}, bf16[2,9,16,128]{3,2,1,0:T(8,128)(2,1)S(1)}, u32[]{:S(2)}, u32[]{:S(2)}) collective-permute-start(bf16[2,9,16,128]{3,2,1,0:T(8,128)(2,1)S(1)} %get-tuple-element.50), channel_id=1, source_target_pairs={{0,15},{1,2},{2,1},{3,4},{4,3},{5,6},{6,5},{7,8},{8,7},{9,10},{10,... | collective-permute-start | bytes 221192 | tf_op jit(solution)/shard_map/ppermute | solution.py:104
  39.4 0.9 %turn_residents.1.turned = bf16[512,2560]{1,0:T(8,128)(2,1)S(1)} custom-call(bf16[2048,512]{1,0:T(8,128)(2,1)S(1)} %bitcast.6, bf16[16,16,896]{2,1,0:T(8,128)(2,1)S(1)} %collective-permute-done.from_x, bf16[8,16,896]{2,1,0:T(8,128)(2,1)S(1)} %collective-permute-done.1.from_y, bf16[1,16,896]{2,1,0:T(8,128)(2,1)S(1)} %collective-permute-done.2.corner), custom_call_target="tpu_custom_call" | custom-call | flops 578813952 | bytes 5435392 | tf_op jit(solution)/shard_map/turn_residents/pallas_call | solution.py:562
  40.3 0.0 collective-permute-done.8.near.near_in
  40.4 4.2 %collective-permute-done.9.far.far_in = bf16[2,9,16,128]{3,2,1,0:T(8,128)(2,1)S(1)} collective-permute-done((bf16[2,9,16,128]{3,2,1,0:T(8,128)(2,1)S(1)}, bf16[2,9,16,128]{3,2,1,0:T(8,128)(2,1)S(1)}, u32[]{:S(2)}, u32[]{:S(2)}) %collective-permute-start.9) | collective-permute-done | bytes 73760 | tf_op jit(solution)/shard_map/ppermute | solution.py:104
  44.6 1.5 %collective-permute-start.10 = (bf16[2,2,2,16,128]{4,3,2,1,0:T(8,128)(2,1)S(1)}, bf16[2,2,2,16,128]{4,3,2,1,0:T(8,128)(2,1)S(1)}, u32[]{:S(2)}, u32[]{:S(2)}) collective-permute-start(bf16[2,2,2,16,128]{4,3,2,1,0:T(8,128)(2,1)S(1)} %corner_pack.3), channel_id=1, source_target_pairs={{0,16},{1,17},{2,18},{3,19},{4,20},{5,21},{6,22},{7,23},{8,24},{9,... | collective-permute-start | bytes 98312 | tf_op jit(solution)/shard_map/ppermute | solution.py:91
  46.1 0.0 collective-permute-done.7.face_in
  46.1 2.1 %third_main.1 = (f32[4,736,256]{2,1,0:T(8,128)S(1)}, f32[2,9,17,16,128]{4,3,2,1,0:T(8,128)S(1)}) custom-call(s32[1]{0:T(128)} %bitcast.even_ref, bf16[2,8,16,16,128]{4,3,2,1,0:T(8,128)(2,1)S(1)} %copy-done.2, bf16[16,16,896]{2,1,0:T(8,128)(2,1)S(1)} %collective-permute-done.from_x, bf16[8,16,896]{2,1,0:T(8,128)(2,1)S(1)} %collective-permute-done.1.from_y, ...), custom_call_target="tpu_custom_call" | custom-call | flops 1157627904 | bytes 19709956 | tf_op jit(solution)/shard_map/third_main/pallas_call | solution.py:562
  48.2 0.2 collective-permute-done.10.corner_in
  48.5 4.7 %third_corner.1 = (f32[2,8,16,16,128]{4,3,2,1,0:T(8,128)}, f32[2,16,16,128]{3,2,1,0:T(8,128)S(1)}, f32[2,7,16,128]{3,2,1,0:T(8,128)S(1)}, bf16[2,16,16,128]{3,2,...) custom-call(s32[1]{0:T(128)} %bitcast.even_ref, ...), custom_call_target="tpu_custom_call" | custom-call | flops 864026624 | bytes 25468932 | tf_op jit(solution)/shard_map/third_corner/pallas_call | solution.py:562
  53.2 3.5 %all-to-all-start = ((bf16[16,32,256]{2,1,0:T(8,128)(2,1)}), bf16[16,32,256]{2,1,0:T(8,128)(2,1)S(1)}, u32[]{:S(2)}, u32[]{:S(2)}) async-start(bf16[16,32,256]{2,1,0:T(8,128)(2,1)} %bitcast.3), calls=%async_computation | async-start | bytes 524288 | tf_op jit(solution)/shard_map/all_to_all | solution.py:681
  56.7 1.6 %collective-permute-start.11 = (bf16[2,16,128]{2,1,0:T(8,128)(2,1)S(1)}, bf16[2,16,128]{2,1,0:T(8,128)(2,1)S(1)}, u32[]{:S(2)}, u32[]{:S(2)}) collective-permute-start(bf16[2,16,128]{2,1,0:T(8,128)(2,1)S(1)} %get-tuple-element.59), channel_id=1, source_target_pairs={{0,16},{1,17},{2,18},{3,19},{4,20},{5,21},{6,22},{7,23},{8,24},{9,... | collective-permute-start | bytes 24584 | tf_op jit(solution)/shard_map/ppermute | solution.py:91
  58.3 2.1 %collective-permute-done.11.corner_ref = bf16[2,16,128]{2,1,0:T(8,128)(2,1)S(1)} collective-permute-done((bf16[2,16,128]{2,1,0:T(8,128)(2,1)S(1)}, bf16[2,16,128]{2,1,0:T(8,128)(2,1)S(1)}, u32[]{:S(2)}, u32[]{:S(2)}) %collective-permute-start.11) | collective-permute-done | bytes 8224 | tf_op jit(solution)/shard_map/ppermute | solution.py:91
  60.5 0.1 collective-permute-start.13
  60.5 1.6 %collective-permute-start.12 = (bf16[2,16,16,128]{3,2,1,0:T(8,128)(2,1)S(1)}, bf16[2,16,16,128]{3,2,1,0:T(8,128)(2,1)S(1)}, u32[]{:S(2)}, u32[]{:S(2)}) collective-permute-start(bf16[2,16,16,128]{3,2,1,0:T(8,128)(2,1)S(1)} %get-tuple-element.61), channel_id=1, source_target_pairs={{0,16},{1,17},{2,18},{3,19},{4,20},{5,21},{6,22},{7,23},{8,24},{9,... | collective-permute-start | bytes 393224 | tf_op jit(solution)/shard_map/ppermute | solution.py:91
  62.1 5.1 %all-to-all-done = bf16[16,32,256]{2,1,0:T(8,128)(2,1)S(1)} async-done(((bf16[16,32,256]{2,1,0:T(8,128)(2,1)}), bf16[16,32,256]{2,1,0:T(8,128)(2,1)S(1)}, u32[]{:S(2)}, u32[]{:S(2)}) %all-to-all-start) | async-done | bytes 262176 | tf_op jit(solution)/shard_map/all_to_all | solution.py:681
  67.2 1.6 %collective-permute-start.14 = (f32[32,256]{1,0:T(8,128)S(1)}, f32[32,256]{1,0:T(8,128)S(1)}, u32[]{:S(2)}, u32[]{:S(2)}) collective-permute-start(f32[32,256]{1,0:T(8,128)S(1)} %convert_reduce_fusion), channel_id=1, source_target_pairs={{0,16},{1,17},{2,18},{3,19},{4,20},{5,21},{6,22},{7,23},{8,24},{9,... | collective-permute-start | bytes 98312 | tf_op jit(solution)/shard_map/ppermute | solution.py:91
  68.8 0.0 collective-permute-done.13.side
  68.8 0.0 collective-permute-done.12.face
  68.8 0.8 %last.1 = f32[2,8,16,16,128]{4,3,2,1,0:T(8,128)} custom-call(f32[2,8,16,16,128]{4,3,2,1,0:T(8,128)} %get-tuple-element.55.old_hbm, f32[2,16,16,128]{3,2,1,0:T(8,128)S(1)} %get-tuple-element.56.edge_x, f32[2,7,16,128]{3,2,1,0:T(8,128)S(1)} %get-tuple-element.57.edge_y, ...), custom_call_target="tpu_custom_call", output_to_operand_aliasing={{}: (0, {})} | custom-call | bytes 4767744 | tf_op jit(solution)/shard_map/last/pallas_call | solution.py:562
  69.6 1.6 %collective-permute-done.14 = f32[32,256]{1,0:T(8,128)S(1)} collective-permute-done((f32[32,256]{1,0:T(8,128)S(1)}, f32[32,256]{1,0:T(8,128)S(1)}, u32[]{:S(2)}, u32[]{:S(2)}) %collective-permute-start.14) | collective-permute-done | bytes 32800 | tf_op jit(solution)/shard_map/ppermute | solution.py:91
  71.2 0.6 add.8
  (19 shorter events, 0.1 us)
Async XLA Ops:
  2.3 16.4 %collective-permute-start.1 = (bf16[8,16,896]{2,1,0:T(8,128)(2,1)S(1)}, bf16[8,16,896]{2,1,0:T(8,128)(2,1)S(1)}, u32[]{:S(2)}, u32[]{:S(2)}) collective-permute-start(bf16[8,16,896]{2,1,0:T(8,128)(2,1)S(1)} %get-tuple-element.34), channel_id=1, source_target_pairs={{0,15},{1,0},{2,1},{3,2},{4,3},{5,4},{6,5},{7,6},{8,7},{9,8},{10,9... | collective-permute-start | bytes 688136 | tf_op jit(solution)/shard_map/ppermute | solution.py:91
  7.8 11.5 %collective-permute-start = (bf16[16,16,896]{2,1,0:T(8,128)(2,1)S(1)}, bf16[16,16,896]{2,1,0:T(8,128)(2,1)S(1)}, u32[]{:S(2)}, u32[]{:S(2)}) collective-permute-start(bf16[16,16,896]{2,1,0:T(8,128)(2,1)S(1)} %get-tuple-element.33), channel_id=1, source_target_pairs={{0,16},{1,17},{2,18},{3,19},{4,20},{5,21},{6,22},{7,23},{8,24},{9,... | collective-permute-start | bytes 1376264 | tf_op jit(solution)/shard_map/ppermute | solution.py:91
  9.3 10.0 %copy-start.4 = (f32[8,16,16]{2,1,0:T(8,128)S(1)}, f32[8,16,16]{2,1,0:T(8,128)}, u32[]{:S(2)}) copy-start(f32[8,16,16]{2,1,0:T(8,128)} %inv_hbm.1) | copy-start | bytes 24580
  9.3 10.4 %copy-start.5 = (f32[8,16,16]{2,1,0:T(8,128)S(1)}, f32[8,16,16]{2,1,0:T(8,128)}, u32[]{:S(2)}) copy-start(f32[8,16,16]{2,1,0:T(8,128)} %pot_hbm.1) | copy-start | bytes 24580
  16.7 2.1 %copy-start = (bf16[4,736,768]{2,1,0:T(8,128)(2,1)}, bf16[4,736,768]{2,1,0:T(8,128)(2,1)S(1)}, u32[]{:S(2)}) copy-start(bf16[4,736,768]{2,1,0:T(8,128)(2,1)S(1)} %order_cells.1.refs_0_) | copy-start | bytes 13565956
  18.7 1.3 %copy-start.2 = (bf16[2,8,16,16,128]{4,3,2,1,0:T(8,128)(2,1)S(1)}, bf16[2,8,16,16,128]{4,3,2,1,0:T(8,128)(2,1)}, u32[]{:S(2)}) copy-start(bf16[2,8,16,16,128]{4,3,2,1,0:T(8,128)(2,1)} %vec.11) | copy-start | bytes 3145732
  18.7 5.0 %collective-permute-start.2 = (bf16[1,16,896]{2,1,0:T(8,128)(2,1)S(1)}, bf16[1,16,896]{2,1,0:T(8,128)(2,1)S(1)}, u32[]{:S(2)}, u32[]{:S(2)}) collective-permute-start(bf16[1,16,896]{2,1,0:T(8,128)(2,1)S(1)} %slice.4), channel_id=1, source_target_pairs={{0,16},{1,17},{2,18},{3,19},{4,20},{5,21},{6,22},{7,23},{8,24},{9,... | collective-permute-start | bytes 86024 | tf_op jit(solution)/shard_map/ppermute | solution.py:91
  20.0 2.3 %copy-start.1 = (bf16[4,736,768]{2,1,0:T(8,128)(2,1)S(1)}, bf16[4,736,768]{2,1,0:T(8,128)(2,1)}, u32[]{:S(2)}) copy-start(bf16[4,736,768]{2,1,0:T(8,128)(2,1)} %copy-done) | copy-start | bytes 13565956
  24.6 8.6 %collective-permute-start.3 = (bf16[2,2,17,16,128]{4,3,2,1,0:T(8,128)(2,1)S(1)}, bf16[2,2,17,16,128]{4,3,2,1,0:T(8,128)(2,1)S(1)}, u32[]{:S(2)}, u32[]{:S(2)}) collective-permute-start(bf16[2,2,17,16,128]{4,3,2,1,0:T(8,128)(2,1)S(1)} %get-tuple-element.43), channel_id=1, source_target_pairs={{0,16},{1,17},{2,18},{3,19},{4,20},{5,21},{6,22},{7,23},{8,24},{9,... | collective-permute-start | bytes 835592 | tf_op jit(solution)/shard_map/ppermute | solution.py:91
  26.2 2.1 %collective-permute-start.4 = (bf16[2,9,16,128]{3,2,1,0:T(8,128)(2,1)S(1)}, bf16[2,9,16,128]{3,2,1,0:T(8,128)(2,1)S(1)}, u32[]{:S(2)}, u32[]{:S(2)}) collective-permute-start(bf16[2,9,16,128]{3,2,1,0:T(8,128)(2,1)S(1)} %get-tuple-element.44), channel_id=1, source_target_pairs={{0,1},{1,0},{2,3},{3,2},{4,5},{5,4},{6,7},{7,6},{8,9},{9,8},{10,11... | collective-permute-start | bytes 221192 | tf_op jit(solution)/shard_map/ppermute | solution.py:105
  26.2 6.5 %collective-permute-start.5 = (bf16[2,9,16,128]{3,2,1,0:T(8,128)(2,1)S(1)}, bf16[2,9,16,128]{3,2,1,0:T(8,128)(2,1)S(1)}, u32[]{:S(2)}, u32[]{:S(2)}) collective-permute-start(bf16[2,9,16,128]{3,2,1,0:T(8,128)(2,1)S(1)} %get-tuple-element.45), channel_id=1, source_target_pairs={{0,15},{1,2},{2,1},{3,4},{4,3},{5,6},{6,5},{7,8},{8,7},{9,10},{10,... | collective-permute-start | bytes 221192 | tf_op jit(solution)/shard_map/ppermute | solution.py:104
  32.7 3.9 %collective-permute-start.6 = (bf16[2,2,2,16,128]{4,3,2,1,0:T(8,128)(2,1)S(1)}, bf16[2,2,2,16,128]{4,3,2,1,0:T(8,128)(2,1)S(1)}, u32[]{:S(2)}, u32[]{:S(2)}) collective-permute-start(bf16[2,2,2,16,128]{4,3,2,1,0:T(8,128)(2,1)S(1)} %corner_pack.2), channel_id=1, source_target_pairs={{0,16},{1,17},{2,18},{3,19},{4,20},{5,21},{6,22},{7,23},{8,24},{9,... | collective-permute-start | bytes 98312 | tf_op jit(solution)/shard_map/ppermute | solution.py:91
  33.2 12.9 %slice-start = ((s8[4521984]{0:T(1024)(128)(4,1)}), s8[4194304]{0:T(1024)(128)(4,1)S(1)}, s32[]{:S(2)}) async-start(s8[4521984]{0:T(1024)(128)(4,1)} %bitcast.4), calls=%async_computation.1 | async-start | bytes 8388608
  36.6 2.8 %copy-start.3 = (bf16[8,16,16,512]{3,2,1,0:T(8,128)(2,1)S(1)}, bf16[8,16,16,512]{3,2,1,0:T(8,128)(2,1)}, u32[]{:S(2)}) copy-start(bf16[8,16,16,512]{3,2,1,0:T(8,128)(2,1)} %res_hbm.1) | copy-start | bytes 6291460
  36.6 9.5 %slice-start.1 = ((s8[4521984]{0:T(1024)(128)(4,1)}), s8[327680]{0:T(1024)(128)(4,1)S(1)}, s32[]{:S(2)}) async-start(s8[4521984]{0:T(1024)(128)(4,1)} %bitcast.4), calls=%async_computation.2 | async-start | bytes 655360
  37.5 8.6 %collective-permute-start.7 = (bf16[2,2,17,16,128]{4,3,2,1,0:T(8,128)(2,1)S(1)}, bf16[2,2,17,16,128]{4,3,2,1,0:T(8,128)(2,1)S(1)}, u32[]{:S(2)}, u32[]{:S(2)}) collective-permute-start(bf16[2,2,17,16,128]{4,3,2,1,0:T(8,128)(2,1)S(1)} %get-tuple-element.48), channel_id=1, source_target_pairs={{0,16},{1,17},{2,18},{3,19},{4,20},{5,21},{6,22},{7,23},{8,24},{9,... | collective-permute-start | bytes 835592 | tf_op jit(solution)/shard_map/ppermute | solution.py:91
  38.1 2.3 %collective-permute-start.8 = (bf16[2,9,16,128]{3,2,1,0:T(8,128)(2,1)S(1)}, bf16[2,9,16,128]{3,2,1,0:T(8,128)(2,1)S(1)}, u32[]{:S(2)}, u32[]{:S(2)}) collective-permute-start(bf16[2,9,16,128]{3,2,1,0:T(8,128)(2,1)S(1)} %get-tuple-element.49), channel_id=1, source_target_pairs={{0,1},{1,0},{2,3},{3,2},{4,5},{5,4},{6,7},{7,6},{8,9},{9,8},{10,11... | collective-permute-start | bytes 221192 | tf_op jit(solution)/shard_map/ppermute | solution.py:105
  38.1 6.5 %collective-permute-start.9 = (bf16[2,9,16,128]{3,2,1,0:T(8,128)(2,1)S(1)}, bf16[2,9,16,128]{3,2,1,0:T(8,128)(2,1)S(1)}, u32[]{:S(2)}, u32[]{:S(2)}) collective-permute-start(bf16[2,9,16,128]{3,2,1,0:T(8,128)(2,1)S(1)} %get-tuple-element.50), channel_id=1, source_target_pairs={{0,15},{1,2},{2,1},{3,4},{4,3},{5,6},{6,5},{7,8},{8,7},{9,10},{10,... | collective-permute-start | bytes 221192 | tf_op jit(solution)/shard_map/ppermute | solution.py:104
  44.6 3.9 %collective-permute-start.10 = (bf16[2,2,2,16,128]{4,3,2,1,0:T(8,128)(2,1)S(1)}, bf16[2,2,2,16,128]{4,3,2,1,0:T(8,128)(2,1)S(1)}, u32[]{:S(2)}, u32[]{:S(2)}) collective-permute-start(bf16[2,2,2,16,128]{4,3,2,1,0:T(8,128)(2,1)S(1)} %corner_pack.3), channel_id=1, source_target_pairs={{0,16},{1,17},{2,18},{3,19},{4,20},{5,21},{6,22},{7,23},{8,24},{9,... | collective-permute-start | bytes 98312 | tf_op jit(solution)/shard_map/ppermute | solution.py:91
  53.2 14.0 %all-to-all-start = ((bf16[16,32,256]{2,1,0:T(8,128)(2,1)}), bf16[16,32,256]{2,1,0:T(8,128)(2,1)S(1)}, u32[]{:S(2)}, u32[]{:S(2)}) async-start(bf16[16,32,256]{2,1,0:T(8,128)(2,1)} %bitcast.3), calls=%async_computation | async-start | bytes 524288 | tf_op jit(solution)/shard_map/all_to_all | solution.py:681
  56.7 3.7 %collective-permute-start.11 = (bf16[2,16,128]{2,1,0:T(8,128)(2,1)S(1)}, bf16[2,16,128]{2,1,0:T(8,128)(2,1)S(1)}, u32[]{:S(2)}, u32[]{:S(2)}) collective-permute-start(bf16[2,16,128]{2,1,0:T(8,128)(2,1)S(1)} %get-tuple-element.59), channel_id=1, source_target_pairs={{0,16},{1,17},{2,18},{3,19},{4,20},{5,21},{6,22},{7,23},{8,24},{9,... | collective-permute-start | bytes 24584 | tf_op jit(solution)/shard_map/ppermute | solution.py:91
  60.5 8.4 %collective-permute-start.13 = (bf16[2,8,16,128]{3,2,1,0:T(8,128)(2,1)S(1)}, bf16[2,8,16,128]{3,2,1,0:T(8,128)(2,1)S(1)}, u32[]{:S(2)}, u32[]{:S(2)}) collective-permute-start(bf16[2,8,16,128]{3,2,1,0:T(8,128)(2,1)S(1)} %get-tuple-element.62), channel_id=1, source_target_pairs={{0,1},{1,2},{2,3},{3,4},{4,5},{5,6},{6,7},{7,8},{8,9},{9,10},{10,1... | collective-permute-start | bytes 196616 | tf_op jit(solution)/shard_map/ppermute | solution.py:91
  60.5 8.3 %collective-permute-start.12 = (bf16[2,16,16,128]{3,2,1,0:T(8,128)(2,1)S(1)}, bf16[2,16,16,128]{3,2,1,0:T(8,128)(2,1)S(1)}, u32[]{:S(2)}, u32[]{:S(2)}) collective-permute-start(bf16[2,16,16,128]{3,2,1,0:T(8,128)(2,1)S(1)} %get-tuple-element.61), channel_id=1, source_target_pairs={{0,16},{1,17},{2,18},{3,19},{4,20},{5,21},{6,22},{7,23},{8,24},{9,... | collective-permute-start | bytes 393224 | tf_op jit(solution)/shard_map/ppermute | solution.py:91
  67.2 4.0 %collective-permute-start.14 = (f32[32,256]{1,0:T(8,128)S(1)}, f32[32,256]{1,0:T(8,128)S(1)}, u32[]{:S(2)}, u32[]{:S(2)}) collective-permute-start(f32[32,256]{1,0:T(8,128)S(1)} %convert_reduce_fusion), channel_id=1, source_target_pairs={{0,16},{1,17},{2,18},{3,19},{4,20},{5,21},{6,22},{7,23},{8,24},{9,... | collective-permute-start | bytes 98312 | tf_op jit(solution)/shard_map/ppermute | solution.py:91

commit v6 on v5

--- a/solution.py
+++ b/solution.py
@@ -97,13 +97,16 @@
     return jnp.stack([send(value[0], -1, 0), send(value[1], 1, 0)])
 
 
+def send_near(value):
+    pairs = [(b, b + 1 if b % 2 == 0 else b - 1) for b in range(lax.axis_size("dy"))]
+    return lax.ppermute(value, "dy", pairs)
+
+
 def swap_y(near, far):
     ny = lax.axis_size("dy")
-    near_pairs = [(b, b + 1 if b % 2 == 0 else b - 1) for b in range(ny)]
     far_pairs = [(b, (b - 1 if b % 2 == 0 else b + 1) % ny) for b in range(ny)]
     far = lax.ppermute(far, "dy", far_pairs)
-    near = lax.ppermute(near, "dy", near_pairs)
-    return near, far
+    return send_near(near), far
 
 
 def order_kernel(sz, conn_ref, matrix_ref, out_ref):
@@ -199,17 +202,25 @@
         copy.wait()
 
 
-def turn_kernel(sz, res_ref, from_x, from_y, corner, out_ref):
+def turn_kernel(sz, pieces, res_ref, from_x, from_y, corner, out_ref):
     own = sz.own_edges * sz.ez
+    share = sz.res // out_ref.shape[0] // pieces
+
+    def put(g, columns, value):
+        for at in range(0, LANES, share):
+            owner = (g + at) // share
+            row = owner // 2 * share
+            out_ref[owner % 2, row : row + share, columns] = value[at : at + share]
+
     for g in range(0, sz.res, LANES):
         lanes = slice(g, g + LANES)
-        out_ref[lanes, :own] = res_ref[:, lanes].T
+        put(g, slice(0, own), res_ref[:, lanes].T)
         rest = sz.edges - sz.own_edges - sz.ey - sz.gx
         parts = [from_x[:, :, lanes], from_y[:, :, lanes], corner[:, :, lanes]]
         if rest:
             parts.append(jnp.zeros((rest, sz.ez, LANES), bf16))
         ghosts = jnp.concatenate(parts, axis=0)
-        out_ref[lanes, own:] = ghosts.reshape(-1, LANES).T
+        put(g, slice(own, sz.edges * sz.ez), ghosts.reshape(-1, LANES).T)
 
 
 def vectors_of(sz, edge):
@@ -459,8 +470,8 @@
                  last_x, last_field, acc_in, face_in, near_in, far_in, corner_in, prod_ref, y_ref,
                  y_corner, new_ref, turned, *refs):
     mats = refs[:n_mat]
-    out_hbm, edge_x, edge_y, face, side, corner, margin = refs[n_mat : n_mat + 7]
-    part_ref, sem, acc_ref, rows_ref, small_ref, tail_ref = refs[n_mat + 7 :]
+    out_hbm, edge_x, edge_y, face, side, corner, give, keep = refs[n_mat : n_mat + 8]
+    part_ref, sem, acc_ref, rows_ref, small_ref, tail_ref = refs[n_mat + 8 :]
     nodes = Nodes(sz, vec, from_x, from_y, own_inv, own_pot, ghost_x, ghost_y, last_field)
     sums = Sums(sz, even_ref[0] == 0, acc_in, face_in, near_in, far_in, corner_in)
     u_corner, new_corner = [], []
@@ -476,6 +487,7 @@
         for b in range(sz.blocks):
             rows_ref[at, :, b * sz.width : (b + 1) * sz.width] = value[b]
 
+    copies = []
     for i in range(sz.gx):
         for j in range(sz.gy):
             acc, inv = acc_ref[:, i, j], nodes.inv(i, j)
@@ -503,15 +515,18 @@
             elif j == 0:
                 edge_y[:, i - 1] = value
             put_row(i * sz.ey + j, value.astype(bf16))
-    copy = pltpu.make_async_copy(part_ref, out_hbm, sem)
-    copy.start()
+        if i < sz.ex:
+            copies.append(pltpu.make_async_copy(part_ref.at[:, i], out_hbm.at[:, i], sem.at[i]))
+            copies[-1].start()
     for at in range(sz.own_edges + sz.ey + sz.gx, sz.edges):
         rows_ref[at] = jnp.zeros((sz.ez, sz.full), bf16)
-    local = jnp.dot(
-        turned[...], rows_ref[...].reshape(sz.edges * sz.ez, sz.full), preferred_element_type=f32
-    )
-    margin[...] = (local * norm_scale).astype(bf16)
-    copy.wait()
+    rows = rows_ref[...].reshape(sz.edges * sz.ez, sz.full)
+    mine = even_ref[0]
+    for half, out in ((1 - mine, give), (mine, keep)):
+        local = jnp.dot(turned[half], rows, preferred_element_type=f32)
+        out[...] = (local * norm_scale).astype(out.dtype)
+    for copy in copies:
+        copy.wait()
 
 
 def last_side_kernel(sz, side_ref, corner_ref, face_in, out_ref, face_out):
@@ -546,8 +561,14 @@
     return jax.ShapeDtypeStruct(shape, dtype)
 
 
+class Pinned:
+    def __init__(self, value):
+        self.value, self.shape, self.dtype = value, value.shape, value.dtype
+
+
 def call(kernel, name, flops, out_shape, scratch, operands, hbm=0, scalar_first=False, aliases=None,
          out_hbm=0):
+    pinned = [isinstance(s, Pinned) for s in out_shape]
     out_shape = [like(s.shape, s.dtype) for s in out_shape]
     size = sum(math.prod(s.shape) * jnp.dtype(s.dtype).itemsize for s in (*operands, *out_shape))
     whole = pl.BlockSpec(memory_space=pltpu.VMEM)
@@ -556,10 +577,12 @@
         specs[0] = pl.BlockSpec(memory_space=pltpu.SMEM)
     out_specs = [pl.BlockSpec(memory_space=pltpu.HBM)] * out_hbm + [whole] * (len(out_shape) - out_hbm)
     out_shape = [pltpu.HBM(s.shape, s.dtype) for s in out_shape[:out_hbm]] + out_shape[out_hbm:]
+    out_shape = [pltpu.VMEM(s.shape, s.dtype) if p else s for s, p in zip(out_shape, pinned)]
     operands = [pltpu.with_memory_space_constraint(a, pltpu.HBM) for a in operands[:hbm]] + list(
-        operands[hbm:]
-    )
-    return pl.pallas_call(
+        pltpu.with_memory_space_constraint(a.value, pltpu.VMEM) if isinstance(a, Pinned) else a
+        for a in operands[hbm:]
+    )
+    results = pl.pallas_call(
         kernel,
         in_specs=specs,
         out_specs=out_specs,
@@ -570,6 +593,7 @@
         cost_estimate=pl.CostEstimate(flops=flops, bytes_accessed=size, transcendentals=0),
         name=name,
     )(*operands)
+    return [Pinned(r) if p else r for r, p in zip(results, pinned)]
 
 
 def body(vectors, resident, inv_mass, potential, cell_matrix, connectivity):
@@ -583,7 +607,7 @@
     conn = connectivity.reshape(sz.cells, sz.nodes)
     to_x, to_y, cell_matrix, conn = call(
         functools.partial(pack_kernel, sz), "pack", 0,
-        [like((sz.ey, ez, sz.wide), bf16), like((sz.ex, ez, sz.wide), bf16), cell_matrix, conn],
+        [like((sz.ey, ez, sz.wide), bf16), like((sz.ex, ez, sz.wide), bf16), Pinned(cell_matrix), conn],
         [
             pltpu.VMEM((2, sz.ey, ez), f32), pltpu.VMEM((2, sz.ex, ez), f32),
             pltpu.SemaphoreType.DMA((8 + 2 * blocks,)),
@@ -595,7 +619,7 @@
 
     mats = call(
         functools.partial(order_kernel, sz), "order_cells", 4 * sz.cells * sz.depth**3,
-        [like((sz.cells, sz.rows, sz.depth), bf16)], [], [conn, cell_matrix],
+        [Pinned(like((sz.cells, sz.rows, sz.depth), bf16))], [], [conn, cell_matrix],
     )
     own_inv = jnp.broadcast_to(inv_mass[..., None], inv_mass.shape + (width,))
     own_pot = jnp.broadcast_to(potential[..., None], inv_mass.shape + (width,))
@@ -604,7 +628,8 @@
 
     grid = (blocks, sz.gx, sz.gy) + tile
     own = (blocks, sz.ex, sz.ey) + tile
-    products = like((sz.cells, sz.rows, full), f32)
+    products = Pinned(like((sz.cells, sz.rows, full), f32))
+    state_grid = Pinned(like(grid, f32))
     messages = [
         like((2, blocks, sz.gy) + tile, bf16),
         like((blocks, sz.gx) + tile, bf16),
@@ -635,15 +660,15 @@
     )
     acc, face, near, far, last_x, last_field = call(
         functools.partial(first_corner, sz, n_mat), "first_corner", small_flops,
-        [like(grid, f32), *messages, like(sz.edge, f32), like((2,) + tile, f32)], corner_scratch,
+        [state_grid, *messages, like(sz.edge, f32), like((2,) + tile, f32)], corner_scratch,
         [
             parity, vectors, from_x, from_y, ghost_corner, own_inv, own_pot, ghost_x, ghost_y, prod, *mats,
         ],
         scalar_first=True,
     )
     (turned,) = call(
-        functools.partial(turn_kernel, sz), "turn_residents", flops // 2,
-        [like((res_count, sz.edges * ez), bf16)], [],
+        functools.partial(turn_kernel, sz, ny // 2), "turn_residents", flops // 2,
+        [like((2, res_count // 2, sz.edges * ez), bf16)], [],
         [resident.reshape(-1, res_count), from_x, from_y, ghost_corner],
     )
     got, corner = exchange(face, near, far)
@@ -651,38 +676,38 @@
     ends = [last_x, last_field]
     prod, y1 = call(
         functools.partial(second_main, sz, n_mat), "second_main", flops,
-        [products, like(grid, f32)], main_scratch,
+        [products, state_grid], main_scratch,
         [parity, *state, acc, *got, *mats], scalar_first=True,
     )
     acc, face, near, far, y1_corner = call(
         functools.partial(second_corner, sz, n_mat), "second_corner", small_flops,
-        [like(grid, f32), *messages, like((4,) + sz.edge, f32)], corner_scratch,
+        [state_grid, *messages, like((4,) + sz.edge, f32)], corner_scratch,
         [parity, *state, *ends, acc, *got, corner, prod, *mats], scalar_first=True,
     )
     got, corner = exchange(face, near, far)
     prod, y2 = call(
         functools.partial(third_main, sz, n_mat), "third_main", flops,
-        [products, like(grid, f32)], main_scratch,
+        [products, state_grid], main_scratch,
         [parity, *state, acc, *got, y1, *mats], scalar_first=True,
     )
-    filtered, edge_x, edge_y, face, side, corner, local = call(
+    filtered, edge_x, edge_y, face, side, corner, give, keep = call(
         functools.partial(third_corner, sz, n_mat, norm_scale), "third_corner",
         small_flops + 2 * res_count * sz.edges * ez * full,
         [
             like(own, f32), like((blocks, sz.ey) + tile, f32), like((blocks, sz.ex - 1) + tile, f32),
             like((blocks, sz.ey) + tile, bf16), like((blocks, sz.ex) + tile, f32),
-            like(sz.edge, bf16), like((res_count, full), bf16),
+            like(sz.edge, bf16), like((res_count // 2, full), bf16), like((res_count // 2, full), f32),
         ],
-        [pltpu.VMEM(own, f32), pltpu.SemaphoreType.DMA, pltpu.VMEM(grid, f32), pltpu.VMEM((sz.edges, ez, full), bf16)] + corner_scratch,
+        [pltpu.VMEM(own, f32), pltpu.SemaphoreType.DMA((sz.ex,)), pltpu.VMEM(grid, f32), pltpu.VMEM((sz.edges, ez, full), bf16)] + corner_scratch,
         [parity, *state, *ends, acc, *got, corner, prod, y1, y1_corner, y2, turned, *mats],
         scalar_first=True, out_hbm=1,
     )
 
-    pieces = lax.all_to_all(local.reshape(ny, -1, full), "dy", 0, 0)
-    mine = jnp.sum(pieces.astype(f32), axis=0)
-    margin = mine
-    for steps in range(1, nx):
-        margin = margin + send(mine, steps, 0)
+    mine = (keep + send_near(give).astype(f32)).astype(bf16).reshape(1, ny // 2, -1, full)
+    mine = jnp.broadcast_to(mine, (nx,) + mine.shape[1:]).reshape(nx * ny // 2, -1, full)
+    groups = [[a * ny + b for a in range(nx) for b in range(c, ny, 2)] for c in range(2)]
+    pieces = lax.all_to_all(mine, ("dx", "dy"), 0, 0, axis_index_groups=groups)
+    margin = jnp.sum(pieces.astype(f32), axis=0)
 
     corner = send(corner, 1, 0)
     side, face = call(

time: 72.2 us -> 71 us (0.983)
  Pallas kernels: 22.6 us -> 20.7 us
  starting transfers between devices: 23.6 us -> 22.3 us
  waiting for transfers between devices: 19.1 us -> 20.4 us
    all_to_all x1, waiting for transfers between devices: 5.09 us -> 0.01 us  [body(): pieces = lax.all_to_all(mine, ('dx', 'dy'), 0, 0, axis_index_groups=groups)]
    ppermute x11 -> x10, waiting for transfers between devices: 5.47 us -> 10.5 us  [send(): return lax.ppermute(value, ('dx', 'dy'), pairs)]
    pallas_call x13, Pallas kernels: 22.6 us -> 20.7 us  [call(): pl.pallas_call(kernel, in_specs=specs, out_specs=out_specs, out_shape=out...]
    ppermute x2 -> x3, waiting for transfers between devices: 0.01 us -> 1.34 us  [send_near(): return lax.ppermute(value, 'dy', pairs)]
    ppermute x11 -> x10, starting transfers between devices: 16.6 us -> 15.3 us  [send(): return lax.ppermute(value, ('dx', 'dy'), pairs)]
  transfers between devices with their start and end apart: 16 -> 16, of which waited for: 7 -> 7; matrix products, arithmetic and copies ran while one was open for 1% -> 1% of each run, Pallas kernels for 20% -> 21%
where the time goes in v6:
time: 71 us; the launch traced here: 70.7 us
  starting transfers between devices  22.3 us (31%)
  Pallas kernels  20.7 us (29%)
  waiting for transfers between devices  20.4 us (29%)
  local copies, waits for them, and re-layouts  5.74 us (8%)
  between operations  0.82 us (1%)
    pallas_call x13, Pallas kernels, call(): pl.pallas_call(kernel, in_specs=specs, out_specs=out_specs, out_shape=out...  20.7 us
    ppermute x10, starting transfers between devices, send(): return lax.ppermute(value, ('dx', 'dy'), pairs)  15.3 us
    ppermute x10, waiting for transfers between devices, send(): return lax.ppermute(value, ('dx', 'dy'), pairs)  10.5 us
    ppermute x2, waiting for transfers between devices, swap_y(): far = lax.ppermute(far, 'dy', far_pairs)  8.57 us
    unnamed x16, local copies, waits for them, and re-layouts  4.35 us
    all_to_all x1, starting transfers between devices, body(): pieces = lax.all_to_all(mine, ('dx', 'dy'), 0, 0, axis_index_groups=groups)  3.53 us
    ppermute x2, starting transfers between devices, swap_y(): far = lax.ppermute(far, 'dy', far_pairs)  3.46 us
  transfers between devices with their start and end apart: 16, of which 7 were waited for; matrix products, arithmetic and copies ran while one was open for 1% of the time, Pallas kernels for 21%

profile of v6, /device:TPU:0, one launch (start us, length us, event | category | flops | bytes accessed | tf_op | source)
XLA Modules:
  0.0 70.7 jit_solution(10028857556177515485)
XLA Ops:
  0.6 1.7 %pack.1 = (bf16[16,16,896]{2,1,0:T(8,128)(2,1)S(1)}, bf16[8,16,896]{2,1,0:T(8,128)(2,1)S(1)}, bf16[729,729]{1,0:T(8,128)(2,1)S(1)}, s32[4,729]{1,0:T(4,128)S(1)}) custom-call(bf16[2,8,16,16,128]{4,3,2,1,0:T(8,128)(2,1)} %vec.11, bf16[8,16,16,512]{3,2,1,0:T(8,128)(2,1)} %res_hbm.1, f32[8,16,16]{2,1,0:T(8,128)} %inv_hbm.1, f32[8,16,16]{2,1,0:T(8,128)} %pot_hbm.1, ...), custom_call_target="tpu_custom_call" | custom-call | bytes 5999332 | tf_op jit(solution)/shard_map/pack/pallas_call | solution.py:585
  2.3 5.5 %collective-permute-start.1 = (bf16[8,16,896]{2,1,0:T(8,128)(2,1)S(1)}, bf16[8,16,896]{2,1,0:T(8,128)(2,1)S(1)}, u32[]{:S(2)}, u32[]{:S(2)}) collective-permute-start(bf16[8,16,896]{2,1,0:T(8,128)(2,1)S(1)} %get-tuple-element.35), channel_id=1, source_target_pairs={{0,15},{1,0},{2,1},{3,2},{4,3},{5,4},{6,5},{7,6},{8,7},{9,8},{10,9... | collective-permute-start | bytes 688136 | tf_op jit(solution)/shard_map/ppermute | solution.py:91
  7.8 1.5 %collective-permute-start = (bf16[16,16,896]{2,1,0:T(8,128)(2,1)S(1)}, bf16[16,16,896]{2,1,0:T(8,128)(2,1)S(1)}, u32[]{:S(2)}, u32[]{:S(2)}) collective-permute-start(bf16[16,16,896]{2,1,0:T(8,128)(2,1)S(1)} %get-tuple-element.34), channel_id=1, source_target_pairs={{0,16},{1,17},{2,18},{3,19},{4,20},{5,21},{6,22},{7,23},{8,24},{9,... | collective-permute-start | bytes 1376264 | tf_op jit(solution)/shard_map/ppermute | solution.py:91
  9.3 7.4 %order_cells.1.refs_0_ = bf16[4,736,768]{2,1,0:T(8,128)(2,1)S(1)} custom-call(s32[4,729]{1,0:T(4,128)S(1)} %get-tuple-element.36.conn_ref, bf16[729,729]{1,0:T(8,128)(2,1)S(1)} %get-tuple-element.37.matrix_ref), custom_call_target="tpu_custom_call" | custom-call | flops 7247757312 | bytes 5596530 | tf_op jit(solution)/shard_map/order_cells/pallas_call | solution.py:585
  16.7 2.0 %copy-done = bf16[4,736,768]{2,1,0:T(8,128)(2,1)} copy-done((bf16[4,736,768]{2,1,0:T(8,128)(2,1)}, bf16[4,736,768]{2,1,0:T(8,128)(2,1)S(1)}, u32[]{:S(2)}) %copy-start) | copy-done | bytes 4522008
  18.7 0.0 collective-permute-done.1.from_y
  18.7 0.6 collective-permute-start.2
  19.3 0.0 collective-permute-done.from_x
  19.3 0.3 broadcast_in_dim.8.own_inv
  19.7 0.3 broadcast_in_dim.9.own_pot
  20.0 2.3 %copy-done.1 = bf16[4,736,768]{2,1,0:T(8,128)(2,1)S(1)} copy-done((bf16[4,736,768]{2,1,0:T(8,128)(2,1)S(1)}, bf16[4,736,768]{2,1,0:T(8,128)(2,1)}, u32[]{:S(2)}) %copy-start.1) | copy-done | bytes 4522008
  22.3 1.5 %first_main.1 = (f32[4,736,256]{2,1,0:T(8,128)S(1)}, f32[2,16,16,128]{3,2,1,0:T(8,128)S(1)}, f32[2,8,16,128]{3,2,1,0:T(8,128)S(1)}) custom-call(bf16[2,8,16,16,128]{4,3,2,1,0:T(8,128)(2,1)S(1)} %copy-done.2, bf16[16,16,896]{2,1,0:T(8,128)(2,1)S(1)} %collective-permute-done.from_x, bf16[8,16,896]{2,1,0:T(8,128)(2,1)S(1)} %collective-permute-done.1.from_y, ...), custom_call_target="tpu_custom_call" | custom-call | flops 1157627904 | bytes 11763712 | tf_op jit(solution)/shard_map/first_main/pallas_call | solution.py:585
  23.8 0.0 collective-permute-done.2.corner
  23.8 0.9 %first_corner.1 = (f32[2,9,17,16,128]{4,3,2,1,0:T(8,128)S(1)}, bf16[2,2,17,16,128]{4,3,2,1,0:T(8,128)(2,1)S(1)}, bf16[2,9,16,128]{3,2,1,0:T(8,128)(2,1)S(1)}, bf...) custom-call(s32[1]{0:T(128)} %bitcast.even_ref, ...), custom_call_target="tpu_custom_call" | custom-call | flops 192937984 | bytes 14757892 | tf_op jit(solution)/shard_map/first_corner/pallas_call | solution.py:585
  24.6 1.6 %collective-permute-start.3 = (bf16[2,2,17,16,128]{4,3,2,1,0:T(8,128)(2,1)S(1)}, bf16[2,2,17,16,128]{4,3,2,1,0:T(8,128)(2,1)S(1)}, u32[]{:S(2)}, u32[]{:S(2)}) collective-permute-start(bf16[2,2,17,16,128]{4,3,2,1,0:T(8,128)(2,1)S(1)} %get-tuple-element.44), channel_id=1, source_target_pairs={{0,16},{1,17},{2,18},{3,19},{4,20},{5,21},{6,22},{7,23},{8,24},{9,... | collective-permute-start | bytes 835592 | tf_op jit(solution)/shard_map/ppermute | solution.py:91
  26.2 0.0 collective-permute-start.4
  26.2 2.1 %collective-permute-start.5 = (bf16[2,9,16,128]{3,2,1,0:T(8,128)(2,1)S(1)}, bf16[2,9,16,128]{3,2,1,0:T(8,128)(2,1)S(1)}, u32[]{:S(2)}, u32[]{:S(2)}) collective-permute-start(bf16[2,9,16,128]{3,2,1,0:T(8,128)(2,1)S(1)} %get-tuple-element.46), channel_id=1, source_target_pairs={{0,15},{1,2},{2,1},{3,4},{4,3},{5,6},{6,5},{7,8},{8,7},{9,10},{10,... | collective-permute-start | bytes 221192 | tf_op jit(solution)/shard_map/ppermute | solution.py:108
  28.3 0.0 collective-permute-done.4.near.near_in
  28.3 4.4 %collective-permute-done.5.far.far_in = bf16[2,9,16,128]{3,2,1,0:T(8,128)(2,1)S(1)} collective-permute-done((bf16[2,9,16,128]{3,2,1,0:T(8,128)(2,1)S(1)}, bf16[2,9,16,128]{3,2,1,0:T(8,128)(2,1)S(1)}, u32[]{:S(2)}, u32[]{:S(2)}) %collective-permute-start.5) | collective-permute-done | bytes 73760 | tf_op jit(solution)/shard_map/ppermute | solution.py:108
  32.7 0.5 collective-permute-start.6
  33.2 0.0 collective-permute-done.3.face_in
  33.2 1.9 %second_main.1 = (f32[4,736,256]{2,1,0:T(8,128)S(1)}, f32[2,9,17,16,128]{4,3,2,1,0:T(8,128)S(1)}) custom-call(s32[1]{0:T(128)} %bitcast.even_ref, bf16[2,8,16,16,128]{4,3,2,1,0:T(8,128)(2,1)S(1)} %copy-done.2, bf16[16,16,896]{2,1,0:T(8,128)(2,1)S(1)} %collective-permute-done.from_x, bf16[8,16,896]{2,1,0:T(8,128)(2,1)S(1)} %collective-permute-done.1.from_y, ...), custom_call_target="tpu_custom_call" | custom-call | flops 1157627904 | bytes 17203204 | tf_op jit(solution)/shard_map/second_main/pallas_call | solution.py:585
  35.1 1.5 %collective-permute-done.6.corner_in = bf16[2,2,2,16,128]{4,3,2,1,0:T(8,128)(2,1)S(1)} collective-permute-done((bf16[2,2,2,16,128]{4,3,2,1,0:T(8,128)(2,1)S(1)}, bf16[2,2,2,16,128]{4,3,2,1,0:T(8,128)(2,1)S(1)}, u32[]{:S(2)}, u32[]{:S(2)}) %collective-permute-start.6) | collective-permute-done | bytes 32800 | tf_op jit(solution)/shard_map/ppermute | solution.py:91
  36.6 0.9 %second_corner.1 = (f32[2,9,17,16,128]{4,3,2,1,0:T(8,128)S(1)}, bf16[2,2,17,16,128]{4,3,2,1,0:T(8,128)(2,1)S(1)}, bf16[2,9,16,128]{3,2,1,0:T(8,128)(2,1)S(1)}, b...) custom-call(s32[1]{0:T(128)} %bitcast.even_ref, bf16[2,8,16,16,128]{4,3,2,1,0:T(8,128)(2,1)S(1)} %copy-done.2, ...), custom_call_target="tpu_custom_call" | custom-call | flops 192937984 | bytes 17760260 | tf_op jit(solution)/shard_map/second_corner/pallas_call | solution.py:585
  37.5 0.6 collective-permute-start.7
  38.1 0.0 collective-permute-start.8
  38.1 1.4 %collective-permute-start.9 = (bf16[2,9,16,128]{3,2,1,0:T(8,128)(2,1)S(1)}, bf16[2,9,16,128]{3,2,1,0:T(8,128)(2,1)S(1)}, u32[]{:S(2)}, u32[]{:S(2)}) collective-permute-start(bf16[2,9,16,128]{3,2,1,0:T(8,128)(2,1)S(1)} %get-tuple-element.51), channel_id=1, source_target_pairs={{0,15},{1,2},{2,1},{3,4},{4,3},{5,6},{6,5},{7,8},{8,7},{9,10},{10,... | collective-permute-start | bytes 221192 | tf_op jit(solution)/shard_map/ppermute | solution.py:108
  39.4 0.9 %turn_residents.1.turned = bf16[2,256,2560]{2,1,0:T(8,128)(2,1)S(1)} custom-call(bf16[2048,512]{1,0:T(8,128)(2,1)S(1)} %bitcast.7, bf16[16,16,896]{2,1,0:T(8,128)(2,1)S(1)} %collective-permute-done.from_x, bf16[8,16,896]{2,1,0:T(8,128)(2,1)S(1)} %collective-permute-done.1.from_y, bf16[1,16,896]{2,1,0:T(8,128)(2,1)S(1)} %collective-permute-done.2.corner), custom_call_target="tpu_custom_call" | custom-call | flops 578813952 | bytes 5435392 | tf_op jit(solution)/shard_map/turn_residents/pallas_call | solution.py:585
  40.3 0.0 collective-permute-done.8.near.near_in
  40.4 4.2 %collective-permute-done.9.far.far_in = bf16[2,9,16,128]{3,2,1,0:T(8,128)(2,1)S(1)} collective-permute-done((bf16[2,9,16,128]{3,2,1,0:T(8,128)(2,1)S(1)}, bf16[2,9,16,128]{3,2,1,0:T(8,128)(2,1)S(1)}, u32[]{:S(2)}, u32[]{:S(2)}) %collective-permute-start.9) | collective-permute-done | bytes 73760 | tf_op jit(solution)/shard_map/ppermute | solution.py:108
  44.6 1.5 %collective-permute-start.10 = (bf16[2,2,2,16,128]{4,3,2,1,0:T(8,128)(2,1)S(1)}, bf16[2,2,2,16,128]{4,3,2,1,0:T(8,128)(2,1)S(1)}, u32[]{:S(2)}, u32[]{:S(2)}) collective-permute-start(bf16[2,2,2,16,128]{4,3,2,1,0:T(8,128)(2,1)S(1)} %corner_pack.3), channel_id=1, source_target_pairs={{0,16},{1,17},{2,18},{3,19},{4,20},{5,21},{6,22},{7,23},{8,24},{9,... | collective-permute-start | bytes 98312 | tf_op jit(solution)/shard_map/ppermute | solution.py:91
  46.1 0.0 collective-permute-done.7.face_in
  46.1 2.1 %third_main.1 = (f32[4,736,256]{2,1,0:T(8,128)S(1)}, f32[2,9,17,16,128]{4,3,2,1,0:T(8,128)S(1)}) custom-call(s32[1]{0:T(128)} %bitcast.even_ref, bf16[2,8,16,16,128]{4,3,2,1,0:T(8,128)(2,1)S(1)} %copy-done.2, bf16[16,16,896]{2,1,0:T(8,128)(2,1)S(1)} %collective-permute-done.from_x, bf16[8,16,896]{2,1,0:T(8,128)(2,1)S(1)} %collective-permute-done.1.from_y, ...), custom_call_target="tpu_custom_call" | custom-call | flops 1157627904 | bytes 19709956 | tf_op jit(solution)/shard_map/third_main/pallas_call | solution.py:585
  48.2 0.2 collective-permute-done.10.corner_in
  48.5 2.8 %third_corner.1 = (f32[2,8,16,16,128]{4,3,2,1,0:T(8,128)}, f32[2,16,16,128]{3,2,1,0:T(8,128)S(1)}, f32[2,7,16,128]{3,2,1,0:T(8,128)S(1)}, bf16[2,16,16,128]{3,2,...) custom-call(s32[1]{0:T(128)} %bitcast.even_ref, ...), custom_call_target="tpu_custom_call" | custom-call | flops 864026624 | bytes 25600004 | tf_op jit(solution)/shard_map/third_corner/pallas_call | solution.py:585
  51.3 0.1 collective-permute-start.14
  51.3 1.3 %collective-permute-done.14 = bf16[256,256]{1,0:T(8,128)(2,1)S(1)} collective-permute-done((bf16[256,256]{1,0:T(8,128)(2,1)S(1)}, bf16[256,256]{1,0:T(8,128)(2,1)S(1)}, u32[]{:S(2)}, u32[]{:S(2)}) %collective-permute-start.14) | collective-permute-done | bytes 131104 | tf_op jit(solution)/shard_map/ppermute | solution.py:102
  52.7 0.7 %broadcast_in_dim.22 = bf16[2,8,32,256]{3,2,1,0:T(8,128)(2,1)} broadcast(bf16[8,32,256]{2,1,0:T(8,128)(2,1)S(1)} %bitcast.8), dimensions={1,2,3} | broadcast | bytes 393216 | tf_op jit(solution)/shard_map/broadcast_in_dim | solution.py:707
  53.4 3.5 %all-to-all-start = ((bf16[16,32,256]{2,1,0:T(8,128)(2,1)}), bf16[16,32,256]{2,1,0:T(8,128)(2,1)S(1)}, u32[]{:S(2)}, u32[]{:S(2)}) async-start(bf16[16,32,256]{2,1,0:T(8,128)(2,1)} %bitcast.4), calls=%async_computation | async-start | bytes 524288 | tf_op jit(solution)/shard_map/all_to_all | solution.py:709
  57.0 1.9 %collective-permute-start.11 = (bf16[2,16,128]{2,1,0:T(8,128)(2,1)S(1)}, bf16[2,16,128]{2,1,0:T(8,128)(2,1)S(1)}, u32[]{:S(2)}, u32[]{:S(2)}) collective-permute-start(bf16[2,16,128]{2,1,0:T(8,128)(2,1)S(1)} %get-tuple-element.60), channel_id=1, source_target_pairs={{0,16},{1,17},{2,18},{3,19},{4,20},{5,21},{6,22},{7,23},{8,24},{9,... | collective-permute-start | bytes 24584 | tf_op jit(solution)/shard_map/ppermute | solution.py:91
  58.9 2.4 %collective-permute-done.11.corner_ref = bf16[2,16,128]{2,1,0:T(8,128)(2,1)S(1)} collective-permute-done((bf16[2,16,128]{2,1,0:T(8,128)(2,1)S(1)}, bf16[2,16,128]{2,1,0:T(8,128)(2,1)S(1)}, u32[]{:S(2)}, u32[]{:S(2)}) %collective-permute-start.11) | collective-permute-done | bytes 8224 | tf_op jit(solution)/shard_map/ppermute | solution.py:91
  61.2 1.6 %collective-permute-start.12 = (bf16[2,16,16,128]{3,2,1,0:T(8,128)(2,1)S(1)}, bf16[2,16,16,128]{3,2,1,0:T(8,128)(2,1)S(1)}, u32[]{:S(2)}, u32[]{:S(2)}) collective-permute-start(bf16[2,16,16,128]{3,2,1,0:T(8,128)(2,1)S(1)} %get-tuple-element.62), channel_id=1, source_target_pairs={{0,16},{1,17},{2,18},{3,19},{4,20},{5,21},{6,22},{7,23},{8,24},{9,... | collective-permute-start | bytes 393224 | tf_op jit(solution)/shard_map/ppermute | solution.py:91
  62.8 0.0 collective-permute-start.13
  62.9 6.4 %collective-permute-done.13.side = bf16[2,8,16,128]{3,2,1,0:T(8,128)(2,1)S(1)} collective-permute-done((bf16[2,8,16,128]{3,2,1,0:T(8,128)(2,1)S(1)}, bf16[2,8,16,128]{3,2,1,0:T(8,128)(2,1)S(1)}, u32[]{:S(2)}, u32[]{:S(2)}) %collective-permute-start.13) | collective-permute-done | bytes 65568 | tf_op jit(solution)/shard_map/ppermute | solution.py:91
  69.2 0.0 collective-permute-done.12.face
  69.2 0.8 %last.1 = f32[2,8,16,16,128]{4,3,2,1,0:T(8,128)} custom-call(f32[2,8,16,16,128]{4,3,2,1,0:T(8,128)} %get-tuple-element.56.old_hbm, f32[2,16,16,128]{3,2,1,0:T(8,128)S(1)} %get-tuple-element.57.edge_x, f32[2,7,16,128]{3,2,1,0:T(8,128)S(1)} %get-tuple-element.58.edge_y, ...), custom_call_target="tpu_custom_call", output_to_operand_aliasing={{}: (0, {})} | custom-call | bytes 4767744 | tf_op jit(solution)/shard_map/last/pallas_call | solution.py:585
  70.0 0.0 all-to-all-done
  70.0 0.7 convert_reduce_fusion
  (20 shorter events, 0.1 us)
Async XLA Ops:
  2.3 16.4 %collective-permute-start.1 = (bf16[8,16,896]{2,1,0:T(8,128)(2,1)S(1)}, bf16[8,16,896]{2,1,0:T(8,128)(2,1)S(1)}, u32[]{:S(2)}, u32[]{:S(2)}) collective-permute-start(bf16[8,16,896]{2,1,0:T(8,128)(2,1)S(1)} %get-tuple-element.35), channel_id=1, source_target_pairs={{0,15},{1,0},{2,1},{3,2},{4,3},{5,4},{6,5},{7,6},{8,7},{9,8},{10,9... | collective-permute-start | bytes 688136 | tf_op jit(solution)/shard_map/ppermute | solution.py:91
  7.8 11.5 %collective-permute-start = (bf16[16,16,896]{2,1,0:T(8,128)(2,1)S(1)}, bf16[16,16,896]{2,1,0:T(8,128)(2,1)S(1)}, u32[]{:S(2)}, u32[]{:S(2)}) collective-permute-start(bf16[16,16,896]{2,1,0:T(8,128)(2,1)S(1)} %get-tuple-element.34), channel_id=1, source_target_pairs={{0,16},{1,17},{2,18},{3,19},{4,20},{5,21},{6,22},{7,23},{8,24},{9,... | collective-permute-start | bytes 1376264 | tf_op jit(solution)/shard_map/ppermute | solution.py:91
  9.3 10.0 %copy-start.4 = (f32[8,16,16]{2,1,0:T(8,128)S(1)}, f32[8,16,16]{2,1,0:T(8,128)}, u32[]{:S(2)}) copy-start(f32[8,16,16]{2,1,0:T(8,128)} %inv_hbm.1) | copy-start | bytes 24580
  9.3 10.4 %copy-start.5 = (f32[8,16,16]{2,1,0:T(8,128)S(1)}, f32[8,16,16]{2,1,0:T(8,128)}, u32[]{:S(2)}) copy-start(f32[8,16,16]{2,1,0:T(8,128)} %pot_hbm.1) | copy-start | bytes 24580
  16.7 2.1 %copy-start = (bf16[4,736,768]{2,1,0:T(8,128)(2,1)}, bf16[4,736,768]{2,1,0:T(8,128)(2,1)S(1)}, u32[]{:S(2)}) copy-start(bf16[4,736,768]{2,1,0:T(8,128)(2,1)S(1)} %order_cells.1.refs_0_) | copy-start | bytes 13565956
  18.7 1.3 %copy-start.2 = (bf16[2,8,16,16,128]{4,3,2,1,0:T(8,128)(2,1)S(1)}, bf16[2,8,16,16,128]{4,3,2,1,0:T(8,128)(2,1)}, u32[]{:S(2)}) copy-start(bf16[2,8,16,16,128]{4,3,2,1,0:T(8,128)(2,1)} %vec.11) | copy-start | bytes 3145732
  18.7 5.0 %collective-permute-start.2 = (bf16[1,16,896]{2,1,0:T(8,128)(2,1)S(1)}, bf16[1,16,896]{2,1,0:T(8,128)(2,1)S(1)}, u32[]{:S(2)}, u32[]{:S(2)}) collective-permute-start(bf16[1,16,896]{2,1,0:T(8,128)(2,1)S(1)} %slice.4), channel_id=1, source_target_pairs={{0,16},{1,17},{2,18},{3,19},{4,20},{5,21},{6,22},{7,23},{8,24},{9,... | collective-permute-start | bytes 86024 | tf_op jit(solution)/shard_map/ppermute | solution.py:91
  20.0 2.3 %copy-start.1 = (bf16[4,736,768]{2,1,0:T(8,128)(2,1)S(1)}, bf16[4,736,768]{2,1,0:T(8,128)(2,1)}, u32[]{:S(2)}) copy-start(bf16[4,736,768]{2,1,0:T(8,128)(2,1)} %copy-done) | copy-start | bytes 13565956
  24.6 8.6 %collective-permute-start.3 = (bf16[2,2,17,16,128]{4,3,2,1,0:T(8,128)(2,1)S(1)}, bf16[2,2,17,16,128]{4,3,2,1,0:T(8,128)(2,1)S(1)}, u32[]{:S(2)}, u32[]{:S(2)}) collective-permute-start(bf16[2,2,17,16,128]{4,3,2,1,0:T(8,128)(2,1)S(1)} %get-tuple-element.44), channel_id=1, source_target_pairs={{0,16},{1,17},{2,18},{3,19},{4,20},{5,21},{6,22},{7,23},{8,24},{9,... | collective-permute-start | bytes 835592 | tf_op jit(solution)/shard_map/ppermute | solution.py:91
  26.2 2.1 %collective-permute-start.4 = (bf16[2,9,16,128]{3,2,1,0:T(8,128)(2,1)S(1)}, bf16[2,9,16,128]{3,2,1,0:T(8,128)(2,1)S(1)}, u32[]{:S(2)}, u32[]{:S(2)}) collective-permute-start(bf16[2,9,16,128]{3,2,1,0:T(8,128)(2,1)S(1)} %get-tuple-element.45), channel_id=1, source_target_pairs={{0,1},{1,0},{2,3},{3,2},{4,5},{5,4},{6,7},{7,6},{8,9},{9,8},{10,11... | collective-permute-start | bytes 221192 | tf_op jit(solution)/shard_map/ppermute | solution.py:102
  26.2 6.5 %collective-permute-start.5 = (bf16[2,9,16,128]{3,2,1,0:T(8,128)(2,1)S(1)}, bf16[2,9,16,128]{3,2,1,0:T(8,128)(2,1)S(1)}, u32[]{:S(2)}, u32[]{:S(2)}) collective-permute-start(bf16[2,9,16,128]{3,2,1,0:T(8,128)(2,1)S(1)} %get-tuple-element.46), channel_id=1, source_target_pairs={{0,15},{1,2},{2,1},{3,4},{4,3},{5,6},{6,5},{7,8},{8,7},{9,10},{10,... | collective-permute-start | bytes 221192 | tf_op jit(solution)/shard_map/ppermute | solution.py:108
  32.7 3.9 %collective-permute-start.6 = (bf16[2,2,2,16,128]{4,3,2,1,0:T(8,128)(2,1)S(1)}, bf16[2,2,2,16,128]{4,3,2,1,0:T(8,128)(2,1)S(1)}, u32[]{:S(2)}, u32[]{:S(2)}) collective-permute-start(bf16[2,2,2,16,128]{4,3,2,1,0:T(8,128)(2,1)S(1)} %corner_pack.2), channel_id=1, source_target_pairs={{0,16},{1,17},{2,18},{3,19},{4,20},{5,21},{6,22},{7,23},{8,24},{9,... | collective-permute-start | bytes 98312 | tf_op jit(solution)/shard_map/ppermute | solution.py:91
  33.2 12.9 %slice-start = ((s8[4521984]{0:T(1024)(128)(4,1)}), s8[4194304]{0:T(1024)(128)(4,1)S(1)}, s32[]{:S(2)}) async-start(s8[4521984]{0:T(1024)(128)(4,1)} %bitcast.5), calls=%async_computation.1 | async-start | bytes 8388608
  36.6 2.8 %copy-start.3 = (bf16[8,16,16,512]{3,2,1,0:T(8,128)(2,1)S(1)}, bf16[8,16,16,512]{3,2,1,0:T(8,128)(2,1)}, u32[]{:S(2)}) copy-start(bf16[8,16,16,512]{3,2,1,0:T(8,128)(2,1)} %res_hbm.1) | copy-start | bytes 6291460
  36.6 9.5 %slice-start.1 = ((s8[4521984]{0:T(1024)(128)(4,1)}), s8[327680]{0:T(1024)(128)(4,1)S(1)}, s32[]{:S(2)}) async-start(s8[4521984]{0:T(1024)(128)(4,1)} %bitcast.5), calls=%async_computation.2 | async-start | bytes 655360
  37.5 8.6 %collective-permute-start.7 = (bf16[2,2,17,16,128]{4,3,2,1,0:T(8,128)(2,1)S(1)}, bf16[2,2,17,16,128]{4,3,2,1,0:T(8,128)(2,1)S(1)}, u32[]{:S(2)}, u32[]{:S(2)}) collective-permute-start(bf16[2,2,17,16,128]{4,3,2,1,0:T(8,128)(2,1)S(1)} %get-tuple-element.49), channel_id=1, source_target_pairs={{0,16},{1,17},{2,18},{3,19},{4,20},{5,21},{6,22},{7,23},{8,24},{9,... | collective-permute-start | bytes 835592 | tf_op jit(solution)/shard_map/ppermute | solution.py:91
  38.1 2.3 %collective-permute-start.8 = (bf16[2,9,16,128]{3,2,1,0:T(8,128)(2,1)S(1)}, bf16[2,9,16,128]{3,2,1,0:T(8,128)(2,1)S(1)}, u32[]{:S(2)}, u32[]{:S(2)}) collective-permute-start(bf16[2,9,16,128]{3,2,1,0:T(8,128)(2,1)S(1)} %get-tuple-element.50), channel_id=1, source_target_pairs={{0,1},{1,0},{2,3},{3,2},{4,5},{5,4},{6,7},{7,6},{8,9},{9,8},{10,11... | collective-permute-start | bytes 221192 | tf_op jit(solution)/shard_map/ppermute | solution.py:102
  38.1 6.5 %collective-permute-start.9 = (bf16[2,9,16,128]{3,2,1,0:T(8,128)(2,1)S(1)}, bf16[2,9,16,128]{3,2,1,0:T(8,128)(2,1)S(1)}, u32[]{:S(2)}, u32[]{:S(2)}) collective-permute-start(bf16[2,9,16,128]{3,2,1,0:T(8,128)(2,1)S(1)} %get-tuple-element.51), channel_id=1, source_target_pairs={{0,15},{1,2},{2,1},{3,4},{4,3},{5,6},{6,5},{7,8},{8,7},{9,10},{10,... | collective-permute-start | bytes 221192 | tf_op jit(solution)/shard_map/ppermute | solution.py:108
  44.6 3.9 %collective-permute-start.10 = (bf16[2,2,2,16,128]{4,3,2,1,0:T(8,128)(2,1)S(1)}, bf16[2,2,2,16,128]{4,3,2,1,0:T(8,128)(2,1)S(1)}, u32[]{:S(2)}, u32[]{:S(2)}) collective-permute-start(bf16[2,2,2,16,128]{4,3,2,1,0:T(8,128)(2,1)S(1)} %corner_pack.3), channel_id=1, source_target_pairs={{0,16},{1,17},{2,18},{3,19},{4,20},{5,21},{6,22},{7,23},{8,24},{9,... | collective-permute-start | bytes 98312 | tf_op jit(solution)/shard_map/ppermute | solution.py:91
  51.3 1.4 %collective-permute-start.14 = (bf16[256,256]{1,0:T(8,128)(2,1)S(1)}, bf16[256,256]{1,0:T(8,128)(2,1)S(1)}, u32[]{:S(2)}, u32[]{:S(2)}) collective-permute-start(bf16[256,256]{1,0:T(8,128)(2,1)S(1)} %get-tuple-element.65), channel_id=1, source_target_pairs={{0,1},{1,0},{2,3},{3,2},{4,5},{5,4},{6,7},{7,6},{8,9},{9,8},{10,11... | collective-permute-start | bytes 393224 | tf_op jit(solution)/shard_map/ppermute | solution.py:102
  53.4 16.6 %all-to-all-start = ((bf16[16,32,256]{2,1,0:T(8,128)(2,1)}), bf16[16,32,256]{2,1,0:T(8,128)(2,1)S(1)}, u32[]{:S(2)}, u32[]{:S(2)}) async-start(bf16[16,32,256]{2,1,0:T(8,128)(2,1)} %bitcast.4), calls=%async_computation | async-start | bytes 524288 | tf_op jit(solution)/shard_map/all_to_all | solution.py:709
  57.0 4.2 %collective-permute-start.11 = (bf16[2,16,128]{2,1,0:T(8,128)(2,1)S(1)}, bf16[2,16,128]{2,1,0:T(8,128)(2,1)S(1)}, u32[]{:S(2)}, u32[]{:S(2)}) collective-permute-start(bf16[2,16,128]{2,1,0:T(8,128)(2,1)S(1)} %get-tuple-element.60), channel_id=1, source_target_pairs={{0,16},{1,17},{2,18},{3,19},{4,20},{5,21},{6,22},{7,23},{8,24},{9,... | collective-permute-start | bytes 24584 | tf_op jit(solution)/shard_map/ppermute | solution.py:91
  61.2 8.0 %collective-permute-start.12 = (bf16[2,16,16,128]{3,2,1,0:T(8,128)(2,1)S(1)}, bf16[2,16,16,128]{3,2,1,0:T(8,128)(2,1)S(1)}, u32[]{:S(2)}, u32[]{:S(2)}) collective-permute-start(bf16[2,16,16,128]{3,2,1,0:T(8,128)(2,1)S(1)} %get-tuple-element.62), channel_id=1, source_target_pairs={{0,16},{1,17},{2,18},{3,19},{4,20},{5,21},{6,22},{7,23},{8,24},{9,... | collective-permute-start | bytes 393224 | tf_op jit(solution)/shard_map/ppermute | solution.py:91
  62.8 6.4 %collective-permute-start.13 = (bf16[2,8,16,128]{3,2,1,0:T(8,128)(2,1)S(1)}, bf16[2,8,16,128]{3,2,1,0:T(8,128)(2,1)S(1)}, u32[]{:S(2)}, u32[]{:S(2)}) collective-permute-start(bf16[2,8,16,128]{3,2,1,0:T(8,128)(2,1)S(1)} %get-tuple-element.63), channel_id=1, source_target_pairs={{0,1},{1,2},{2,3},{3,4},{4,5},{5,6},{6,7},{7,8},{8,9},{9,10},{10,1... | collective-permute-start | bytes 196616 | tf_op jit(solution)/shard_map/ppermute | solution.py:91

commit v7 on v6

--- a/solution.py
+++ b/solution.py
@@ -11,7 +11,7 @@
 LANES = 128
 TILE = 256
 SUB = 16
-VMEM_LIMIT = 16 * 1024 * 1024
+VMEM_LIMIT = 12 * 1024 * 1024
 
 center_shift = 1.2
 half_width = 2.0
@@ -109,7 +109,7 @@
     return send_near(near), far
 
 
-def order_kernel(sz, conn_ref, matrix_ref, out_ref):
+def order_kernel(sz, conn_ref, matrix_ref, *out_refs):
     for cell in range(sz.cells):
         x0, y0, z0 = sz.origins[cell]
         conn = conn_ref[cell : cell + 1, :].astype(f32)
@@ -138,12 +138,12 @@
             block = lax.dot_general(
                 half[r0:r1], pick[r0:], (((1,), (1,)), ((), ())), preferred_element_type=f32
             ).astype(bf16)
-            out_ref[cell, r0:r1, r0:] = block
+            out_refs[cell][r0:r1, r0:] = block
             for c0, c1 in zip(cuts[:-1], cuts[1:]):
                 if c0 > r0:
                     mirror = block[:, c0 - r0 : c1 - r0].T
                     c1 = min(c1, sz.rows)
-                    out_ref[cell, c0:c1, r0:r1] = mirror[: c1 - c0]
+                    out_refs[cell][c0:c1, r0:r1] = mirror[: c1 - c0]
 
 
 def field_row(inv, pot):
@@ -285,7 +285,6 @@
     width = sz.width
     flat = sz.gx * sz.gy * sz.gz
     u_flat = u_ref.reshape(sz.blocks * flat, width)
-    matrices = [ref.at[c] for ref in mat_refs for c in range(ref.shape[0])]
     last = sz.nodes // 8 * 8
     ready = set()
     for cell, (x0, y0, z0) in enumerate(sz.origins):
@@ -315,7 +314,7 @@
                     pl.ds(start, count, stride=sz.gz)
                 ]
         out_ref[cell] = jnp.dot(
-            matrices[cell][...], rhs_ref[slot].astype(bf16), preferred_element_type=f32
+            mat_refs[cell][...], rhs_ref[slot].astype(bf16), preferred_element_type=f32
         )
 
 
@@ -323,7 +322,6 @@
     width = sz.width
     flat = sz.gx * sz.gy * sz.gz
     acc_flat = acc_ref.reshape(sz.blocks * flat, width)
-    matrices = [ref.at[c] for ref in mat_refs for c in range(ref.shape[0])]
     small_ref[...] = jnp.zeros_like(small_ref)
     touched = set()
     for cell, (x0, y0, z0) in enumerate(sz.origins):
@@ -338,7 +336,7 @@
                 small_ref[rank * sz.p : (rank + 1) * sz.p, lanes] = value[b, z0:z1]
                 small_ref[last : last + 1, lanes] = value[b, wrap : wrap + 1]
         total = prod_ref[cell] + jnp.dot(
-            matrices[cell][:, : small_ref.shape[0]], small_ref[...].astype(bf16),
+            mat_refs[cell][:, : small_ref.shape[0]], small_ref[...].astype(bf16),
             preferred_element_type=f32,
         )
         tail_ref[cell, : sz.base] = total[: sz.base]
@@ -466,22 +464,29 @@
     main_products(sz, prepare, u_ref, mats, rhs_ref, prod_ref)
 
 
-def third_corner(sz, n_mat, norm_scale, even_ref, vec, from_x, from_y, own_inv, own_pot, ghost_x, ghost_y,
-                 last_x, last_field, acc_in, face_in, near_in, far_in, corner_in, prod_ref, y_ref,
-                 y_corner, new_ref, turned, *refs):
+def third_corner(sz, n_mat, even_ref, vec, from_x, from_y, own_inv, own_pot, ghost_x, ghost_y,
+                 last_x, last_field, acc_in, face_in, near_in, far_in, corner_in, prod_ref, y_corner, *refs):
     mats = refs[:n_mat]
-    out_hbm, edge_x, edge_y, face, side, corner, give, keep = refs[n_mat : n_mat + 8]
-    part_ref, sem, acc_ref, rows_ref, small_ref, tail_ref = refs[n_mat + 8 :]
+    acc_ref, new_corner, face, small_ref, tail_ref = refs[n_mat:]
     nodes = Nodes(sz, vec, from_x, from_y, own_inv, own_pot, ghost_x, ghost_y, last_field)
     sums = Sums(sz, even_ref[0] == 0, acc_in, face_in, near_in, far_in, corner_in)
-    u_corner, new_corner = [], []
+    u_corner = []
     for at, (i, j) in enumerate(corner_edges(sz)):
         x = last_x[...] if (i, j) == (sz.ex, sz.ey) else nodes.x(i, j)
         old, inv = y_corner[at], nodes.inv(i, j)
         image = inv * sums.at(i, j) + nodes.pot(i, j) * old
-        new_corner.append(2.0 * (image - center_shift * old) / half_width - x)
-        u_corner.append(inv * new_corner[-1])
+        new = 2.0 * (image - center_shift * old) / half_width - x
+        new_corner[at] = new
+        u_corner.append(inv * new)
     corner_products(sz, u_corner, prod_ref, mats, small_ref, tail_ref, acc_ref)
+    for j in range(sz.gy):
+        face[:, j] = (gain * (nodes.inv(sz.ex, j) * acc_ref[:, sz.ex, j])).astype(bf16)
+
+
+def third_end(sz, norm_scale, even_ref, own_inv, own_pot, ghost_x, ghost_y, last_field, acc_ref, y_ref,
+              y_corner, new_ref, new_corner, turned, *refs):
+    out_hbm, edge_x, edge_y, side, give, keep, part_ref, sem, rows_ref = refs
+    nodes = Nodes(sz, None, None, None, own_inv, own_pot, ghost_x, ghost_y, last_field)
 
     def put_row(at, value):
         for b in range(sz.blocks):
@@ -496,13 +501,10 @@
                 rounded = value.astype(bf16)
                 if j < sz.ey:
                     put_row(sz.own_edges + j, rounded)
-                    face[:, j] = rounded
                 else:
                     put_row(sz.own_edges + sz.ey + i, rounded)
                     if i < sz.ex:
                         side[:, i] = value
-                    else:
-                        corner[...] = rounded
                 continue
             at = sz.corner(i, j)
             old = y_ref[:, i, j] if at is None else y_corner[at]
@@ -529,13 +531,18 @@
         copy.wait()
 
 
-def last_side_kernel(sz, side_ref, corner_ref, face_in, out_ref, face_out):
-    del face_in, face_out
+def ready_kernel(sz, keep, taken, side_ref, face, pieces, out_ref):
     for i in range(sz.ex):
         value = side_ref[:, i]
         if i == 0:
-            value = value + corner_ref[...].astype(f32)
+            value = value + face[:, sz.ey].astype(f32)
         out_ref[:, i] = value.astype(out_ref.dtype)
+    rows = pieces.shape[2]
+    for at in range(pieces.shape[1]):
+        span = slice(at * rows, (at + 1) * rows)
+        value = (keep[span] + taken[span].astype(f32)).astype(pieces.dtype)
+        for copy in range(pieces.shape[0]):
+            pieces[copy, at] = value
 
 
 def last_kernel(sz, old_hbm, edge_x, edge_y, face, side, out_hbm, at_x, at_y, sems):
@@ -619,7 +626,7 @@
 
     mats = call(
         functools.partial(order_kernel, sz), "order_cells", 4 * sz.cells * sz.depth**3,
-        [Pinned(like((sz.cells, sz.rows, sz.depth), bf16))], [], [conn, cell_matrix],
+        [Pinned(like((sz.rows, sz.depth), bf16))] * sz.cells, [], [conn, cell_matrix],
     )
     own_inv = jnp.broadcast_to(inv_mass[..., None], inv_mass.shape + (width,))
     own_pot = jnp.broadcast_to(potential[..., None], inv_mass.shape + (width,))
@@ -690,31 +697,38 @@
         [products, state_grid], main_scratch,
         [parity, *state, acc, *got, y1, *mats], scalar_first=True,
     )
-    filtered, edge_x, edge_y, face, side, corner, give, keep = call(
-        functools.partial(third_corner, sz, n_mat, norm_scale), "third_corner",
-        small_flops + 2 * res_count * sz.edges * ez * full,
+    acc, new_corner, face = call(
+        functools.partial(third_corner, sz, n_mat), "third_corner", small_flops,
+        [state_grid, like((4,) + sz.edge, f32), like((blocks, sz.gy) + tile, bf16)], corner_scratch,
+        [parity, *state, *ends, acc, *got, corner, prod, y1_corner, *mats], scalar_first=True,
+    )
+    face = send(face, 1, 0)
+    filtered, edge_x, edge_y, side, give, keep = call(
+        functools.partial(third_end, sz, norm_scale), "third_end", 2 * res_count * sz.edges * ez * full,
         [
             like(own, f32), like((blocks, sz.ey) + tile, f32), like((blocks, sz.ex - 1) + tile, f32),
-            like((blocks, sz.ey) + tile, bf16), like((blocks, sz.ex) + tile, f32),
-            like(sz.edge, bf16), like((res_count // 2, full), bf16), like((res_count // 2, full), f32),
+            like((blocks, sz.ex) + tile, f32), like((res_count // 2, full), bf16), like((res_count // 2, full), f32),
         ],
-        [pltpu.VMEM(own, f32), pltpu.SemaphoreType.DMA((sz.ex,)), pltpu.VMEM(grid, f32), pltpu.VMEM((sz.edges, ez, full), bf16)] + corner_scratch,
-        [parity, *state, *ends, acc, *got, corner, prod, y1, y1_corner, y2, turned, *mats],
+        [
+            pltpu.VMEM(own, f32), pltpu.SemaphoreType.DMA((sz.ex,)),
+            pltpu.VMEM((sz.edges, ez, full), bf16),
+        ],
+        [
+            parity, own_inv, own_pot, ghost_x, ghost_y, last_field, acc, y1, y1_corner, y2, new_corner, turned,
+        ],
         scalar_first=True, out_hbm=1,
     )
 
-    mine = (keep + send_near(give).astype(f32)).astype(bf16).reshape(1, ny // 2, -1, full)
-    mine = jnp.broadcast_to(mine, (nx,) + mine.shape[1:]).reshape(nx * ny // 2, -1, full)
+    pieces, side = call(
+        functools.partial(ready_kernel, sz), "ready", 0,
+        [like((nx, ny // 2, res_count // ny, full), bf16), like((blocks, sz.ex) + tile, bf16)],
+        [], [keep, send_near(give), side, face],
+    )
+    pieces = pieces.reshape(nx * ny // 2, -1, full)
     groups = [[a * ny + b for a in range(nx) for b in range(c, ny, 2)] for c in range(2)]
-    pieces = lax.all_to_all(mine, ("dx", "dy"), 0, 0, axis_index_groups=groups)
+    pieces = lax.all_to_all(pieces, ("dx", "dy"), 0, 0, axis_index_groups=groups)
     margin = jnp.sum(pieces.astype(f32), axis=0)
 
-    corner = send(corner, 1, 0)
-    side, face = call(
-        functools.partial(last_side_kernel, sz), "last_side", 0,
-        [like((blocks, sz.ex) + tile, bf16), face], [], [side, corner, face], aliases={2: 1},
-    )
-    face = send(face, 1, 0)
     side = send(side, 0, 1)
     (filtered,) = call(
         functools.partial(last_kernel, sz), "last", 0, [like(own, f32)],

time: 71 us -> 78 us (1.099)
  Pallas kernels: 20.7 us -> 30 us
  waiting for transfers between devices: 20.4 us -> 17.2 us
  starting transfers between devices: 22.3 us -> 23.1 us
    pallas_call x13 -> x14, Pallas kernels: 20.7 us -> 30 us  [call(): pl.pallas_call(kernel, in_specs=specs, out_specs=out_specs, out_shape=out...]
    ppermute x2, waiting for transfers between devices: 8.57 us -> 6.11 us  [swap_y(): far = lax.ppermute(far, 'dy', far_pairs)]
    ppermute x10 -> x9, starting transfers between devices: 15.3 us -> 12.9 us  [send(): return lax.ppermute(value, ('dx', 'dy'), pairs)]
    ppermute x10 -> x9, waiting for transfers between devices: 10.5 us -> 8.27 us  [send(): return lax.ppermute(value, ('dx', 'dy'), pairs)]
    all_to_all x1, starting transfers between devices: 3.53 us -> 5.24 us  [body(): lax.all_to_all(pieces, ('dx', 'dy'), 0, 0, axis_index_groups=groups)]
    ppermute x2, starting transfers between devices: 3.46 us -> 4.9 us  [swap_y(): far = lax.ppermute(far, 'dy', far_pairs)]
    all_to_all x1, waiting for transfers between devices: 0.01 us -> 1.43 us  [body(): lax.all_to_all(pieces, ('dx', 'dy'), 0, 0, axis_index_groups=groups)]
    unnamed x16 -> x14, local copies, waits for them, and re-layouts: 4.35 us -> 3.28 us
  transfers between devices with their start and end apart: 16 -> 15, of which waited for: 7 -> 7; matrix products, arithmetic and copies ran while one was open for 1% -> 3% of each run, Pallas kernels for 21% -> 27%
where the time goes in v7:
time: 78 us; the launch traced here: 77.4 us
  Pallas kernels  30 us (38%)
  starting transfers between devices  23.1 us (30%)
  waiting for transfers between devices  17.2 us (22%)
  local copies, waits for them, and re-layouts  5.7 us (7%)
  between operations  0.82 us (1%)
    pallas_call x14, Pallas kernels, call(): pl.pallas_call(kernel, in_specs=specs, out_specs=out_specs, out_shape=out...  30 us
    ppermute x9, starting transfers between devices, send(): return lax.ppermute(value, ('dx', 'dy'), pairs)  12.9 us
    ppermute x9, waiting for transfers between devices, send(): return lax.ppermute(value, ('dx', 'dy'), pairs)  8.27 us
    ppermute x2, waiting for transfers between devices, swap_y(): far = lax.ppermute(far, 'dy', far_pairs)  6.11 us
    all_to_all x1, starting transfers between devices, body(): lax.all_to_all(pieces, ('dx', 'dy'), 0, 0, axis_index_groups=groups)  5.24 us
    ppermute x2, starting transfers between devices, swap_y(): far = lax.ppermute(far, 'dy', far_pairs)  4.9 us
    unnamed x14, local copies, waits for them, and re-layouts  3.28 us
  transfers between devices with their start and end apart: 15, of which 7 were waited for; matrix products, arithmetic and copies ran while one was open for 3% of the time, Pallas kernels for 27%

profile of v7, /device:TPU:0, one launch (start us, length us, event | category | flops | bytes accessed | tf_op | source)
XLA Modules:
  0.0 77.4 jit_solution(4731467158056009421)
XLA Ops:
  0.6 2.5 %pack.1 = (bf16[16,16,896]{2,1,0:T(8,128)(2,1)}, bf16[8,16,896]{2,1,0:T(8,128)(2,1)}, bf16[729,729]{1,0:T(8,128)(2,1)S(1)}, s32[4,729]{1,0:T(4,128)S(1)}) custom-call(bf16[2,8,16,16,128]{4,3,2,1,0:T(8,128)(2,1)} %vec.11, bf16[8,16,16,512]{3,2,1,0:T(8,128)(2,1)} %res_hbm.1, f32[8,16,16]{2,1,0:T(8,128)} %inv_hbm.1, f32[8,16,16]{2,1,0:T(8,128)} %pot_hbm.1, ...), custom_call_target="tpu_custom_call" | custom-call | bytes 5999332 | tf_op jit(solution)/shard_map/pack/pallas_call | solution.py:592
  3.2 5.5 %collective-permute-start.1 = (bf16[8,16,896]{2,1,0:T(8,128)(2,1)}, bf16[8,16,896]{2,1,0:T(8,128)(2,1)S(1)}, u32[]{:S(2)}, u32[]{:S(2)}) collective-permute-start(bf16[8,16,896]{2,1,0:T(8,128)(2,1)} %get-tuple-element.40), channel_id=1, source_target_pairs={{0,15},{1,0},{2,1},{3,2},{4,3},{5,4},{6,5},{7,6},{8,7},{9,8},{10,9... | collective-permute-start | bytes 688136 | tf_op jit(solution)/shard_map/ppermute | solution.py:91
  8.6 1.5 %collective-permute-start = (bf16[16,16,896]{2,1,0:T(8,128)(2,1)}, bf16[16,16,896]{2,1,0:T(8,128)(2,1)}, u32[]{:S(2)}, u32[]{:S(2)}) collective-permute-start(bf16[16,16,896]{2,1,0:T(8,128)(2,1)} %get-tuple-element.39), channel_id=1, source_target_pairs={{0,16},{1,17},{2,18},{3,19},{4,20},{5,21},{6,22},{7,23},{8,24},{9,... | collective-permute-start | bytes 1376264 | tf_op jit(solution)/shard_map/ppermute | solution.py:91
  10.1 7.4 %order_cells.1 = (bf16[736,768]{1,0:T(8,128)(2,1)S(1)}, bf16[736,768]{1,0:T(8,128)(2,1)S(1)}, bf16[736,768]{1,0:T(8,128)(2,1)S(1)}, bf16[736,768]{1,0:T(8,128)(2,1)S(1)}) custom-call(s32[4,729]{1,0:T(4,128)S(1)} %get-tuple-element.41.conn_ref, bf16[729,729]{1,0:T(8,128)(2,1)S(1)} %get-tuple-element.42.matrix_ref), custom_call_target="tpu_custom_call" | custom-call | flops 7247757312 | bytes 5596530 | tf_op jit(solution)/shard_map/order_cells/pallas_call | solution.py:592
  17.5 0.0 copy-start.1
  17.5 1.0 %copy-done.1 = bf16[736,768]{1,0:T(8,128)(2,1)} copy-done((bf16[736,768]{1,0:T(8,128)(2,1)}, bf16[736,768]{1,0:T(8,128)(2,1)S(1)}, u32[]{:S(2)}) %copy-start.1) | copy-done | bytes 1130520
  18.5 1.0 %copy-done.3 = bf16[736,768]{1,0:T(8,128)(2,1)} copy-done((bf16[736,768]{1,0:T(8,128)(2,1)}, bf16[736,768]{1,0:T(8,128)(2,1)S(1)}, u32[]{:S(2)}) %copy-start.3) | copy-done | bytes 1130520
  19.5 0.0 collective-permute-done.1.from_y
  19.5 0.6 collective-permute-start.2
  20.1 0.0 collective-permute-done.from_x
  20.1 1.2 %broadcast_in_dim.4.own_inv = f32[8,16,16,128]{3,2,1,0:T(8,128)S(1)} broadcast(f32[8,16,16]{2,1,0:T(8,128)} %inv_hbm.1), dimensions={0,1,2} | broadcast | bytes 1056768 | tf_op jit(solution)/shard_map/broadcast_in_dim | solution.py:631
  21.4 1.2 %broadcast_in_dim.5.own_pot = f32[8,16,16,128]{3,2,1,0:T(8,128)S(1)} broadcast(f32[8,16,16]{2,1,0:T(8,128)} %pot_hbm.1), dimensions={0,1,2} | broadcast | bytes 1056768 | tf_op jit(solution)/shard_map/broadcast_in_dim | solution.py:632
  22.6 1.2 %copy-done.4 = bf16[736,768]{1,0:T(8,128)(2,1)S(1)} copy-done((bf16[736,768]{1,0:T(8,128)(2,1)S(1)}, bf16[736,768]{1,0:T(8,128)(2,1)}, u32[]{:S(2)}) %copy-start.4) | copy-done | bytes 1130520
  23.8 2.5 %first_main.1 = (f32[4,736,256]{2,1,0:T(8,128)S(1)}, f32[2,16,16,128]{3,2,1,0:T(8,128)S(1)}, f32[2,8,16,128]{3,2,1,0:T(8,128)S(1)}) custom-call(bf16[2,8,16,16,128]{4,3,2,1,0:T(8,128)(2,1)S(1)} %copy-done, bf16[16,16,896]{2,1,0:T(8,128)(2,1)} %collective-permute-done.from_x, bf16[8,16,896]{2,1,0:T(8,128)(2,1)S(1)} %collective-permute-done.1.from_y, ...), custom_call_target="tpu_custom_call" | custom-call | flops 1157627904 | bytes 11763712 | tf_op jit(solution)/shard_map/first_main/pallas_call | solution.py:592
  26.3 0.0 collective-permute-done.2.corner
  26.3 2.0 %first_corner.1 = (f32[2,9,17,16,128]{4,3,2,1,0:T(8,128)S(1)}, bf16[2,2,17,16,128]{4,3,2,1,0:T(8,128)(2,1)S(1)}, bf16[2,9,16,128]{3,2,1,0:T(8,128)(2,1)S(1)}, bf...) custom-call(s32[1]{0:T(128)} %bitcast.even_ref, ...), custom_call_target="tpu_custom_call" | custom-call | flops 192937984 | bytes 14757892 | tf_op jit(solution)/shard_map/first_corner/pallas_call | solution.py:592
  28.3 1.5 %collective-permute-start.3 = (bf16[2,2,17,16,128]{4,3,2,1,0:T(8,128)(2,1)S(1)}, bf16[2,2,17,16,128]{4,3,2,1,0:T(8,128)(2,1)S(1)}, u32[]{:S(2)}, u32[]{:S(2)}) collective-permute-start(bf16[2,2,17,16,128]{4,3,2,1,0:T(8,128)(2,1)S(1)} %get-tuple-element.53), channel_id=1, source_target_pairs={{0,16},{1,17},{2,18},{3,19},{4,20},{5,21},{6,22},{7,23},{8,24},{9,... | collective-permute-start | bytes 835592 | tf_op jit(solution)/shard_map/ppermute | solution.py:91
  29.8 0.0 collective-permute-start.4
  29.8 2.7 %collective-permute-start.5 = (bf16[2,9,16,128]{3,2,1,0:T(8,128)(2,1)S(1)}, bf16[2,9,16,128]{3,2,1,0:T(8,128)(2,1)S(1)}, u32[]{:S(2)}, u32[]{:S(2)}) collective-permute-start(bf16[2,9,16,128]{3,2,1,0:T(8,128)(2,1)S(1)} %get-tuple-element.55), channel_id=1, source_target_pairs={{0,15},{1,2},{2,1},{3,4},{4,3},{5,6},{6,5},{7,8},{8,7},{9,10},{10,... | collective-permute-start | bytes 221192 | tf_op jit(solution)/shard_map/ppermute | solution.py:108
  32.5 0.0 collective-permute-done.4.near.near_in
  32.5 3.7 %collective-permute-done.5.far.far_in = bf16[2,9,16,128]{3,2,1,0:T(8,128)(2,1)S(1)} collective-permute-done((bf16[2,9,16,128]{3,2,1,0:T(8,128)(2,1)S(1)}, bf16[2,9,16,128]{3,2,1,0:T(8,128)(2,1)S(1)}, u32[]{:S(2)}, u32[]{:S(2)}) %collective-permute-start.5) | collective-permute-done | bytes 73760 | tf_op jit(solution)/shard_map/ppermute | solution.py:108
  36.3 0.6 collective-permute-start.6
  36.9 0.0 collective-permute-done.3.face_in
  36.9 2.9 %second_main.1 = (f32[4,736,256]{2,1,0:T(8,128)S(1)}, f32[2,9,17,16,128]{4,3,2,1,0:T(8,128)S(1)}) custom-call(s32[1]{0:T(128)} %bitcast.even_ref, bf16[2,8,16,16,128]{4,3,2,1,0:T(8,128)(2,1)S(1)} %copy-done, bf16[16,16,896]{2,1,0:T(8,128)(2,1)} %collective-permute-done.from_x, bf16[8,16,896]{2,1,0:T(8,128)(2,1)S(1)} %collective-permute-done.1.from_y, ...), custom_call_target="tpu_custom_call" | custom-call | flops 1157627904 | bytes 17203204 | tf_op jit(solution)/shard_map/second_main/pallas_call | solution.py:592
  39.8 0.4 collective-permute-done.6.corner_in
  40.2 2.0 %second_corner.1 = (f32[2,9,17,16,128]{4,3,2,1,0:T(8,128)S(1)}, bf16[2,2,17,16,128]{4,3,2,1,0:T(8,128)(2,1)S(1)}, bf16[2,9,16,128]{3,2,1,0:T(8,128)(2,1)S(1)}, b...) custom-call(s32[1]{0:T(128)} %bitcast.even_ref, bf16[2,8,16,16,128]{4,3,2,1,0:T(8,128)(2,1)S(1)} %copy-done, ...), custom_call_target="tpu_custom_call" | custom-call | flops 192937984 | bytes 17760260 | tf_op jit(solution)/shard_map/second_corner/pallas_call | solution.py:592
  42.3 1.1 %collective-permute-start.7 = (bf16[2,2,17,16,128]{4,3,2,1,0:T(8,128)(2,1)S(1)}, bf16[2,2,17,16,128]{4,3,2,1,0:T(8,128)(2,1)S(1)}, u32[]{:S(2)}, u32[]{:S(2)}) collective-permute-start(bf16[2,2,17,16,128]{4,3,2,1,0:T(8,128)(2,1)S(1)} %get-tuple-element.58), channel_id=1, source_target_pairs={{0,16},{1,17},{2,18},{3,19},{4,20},{5,21},{6,22},{7,23},{8,24},{9,... | collective-permute-start | bytes 835592 | tf_op jit(solution)/shard_map/ppermute | solution.py:91
  43.4 2.2 %collective-permute-start.9 = (bf16[2,9,16,128]{3,2,1,0:T(8,128)(2,1)S(1)}, bf16[2,9,16,128]{3,2,1,0:T(8,128)(2,1)S(1)}, u32[]{:S(2)}, u32[]{:S(2)}) collective-permute-start(bf16[2,9,16,128]{3,2,1,0:T(8,128)(2,1)S(1)} %get-tuple-element.60), channel_id=1, source_target_pairs={{0,15},{1,2},{2,1},{3,4},{4,3},{5,6},{6,5},{7,8},{8,7},{9,10},{10,... | collective-permute-start | bytes 221192 | tf_op jit(solution)/shard_map/ppermute | solution.py:108
  45.6 1.9 %turn_residents.1.turned = bf16[2,256,2560]{2,1,0:T(8,128)(2,1)S(1)} custom-call(bf16[2048,512]{1,0:T(8,128)(2,1)S(1)} %bitcast.4, bf16[16,16,896]{2,1,0:T(8,128)(2,1)} %collective-permute-done.from_x, bf16[8,16,896]{2,1,0:T(8,128)(2,1)S(1)} %collective-permute-done.1.from_y, bf16[1,16,896]{2,1,0:T(8,128)(2,1)S(1)} %collective-permute-done.2.corner), custom_call_target="tpu_custom_call" | custom-call | flops 578813952 | bytes 5435392 | tf_op jit(solution)/shard_map/turn_residents/pallas_call | solution.py:592
  47.5 0.0 collective-permute-done.8.near.near_in
  47.5 2.4 %collective-permute-done.9.far.far_in = bf16[2,9,16,128]{3,2,1,0:T(8,128)(2,1)S(1)} collective-permute-done((bf16[2,9,16,128]{3,2,1,0:T(8,128)(2,1)S(1)}, bf16[2,9,16,128]{3,2,1,0:T(8,128)(2,1)S(1)}, u32[]{:S(2)}, u32[]{:S(2)}) %collective-permute-start.9) | collective-permute-done | bytes 73760 | tf_op jit(solution)/shard_map/ppermute | solution.py:108
  49.9 1.0 %collective-permute-start.10 = (bf16[2,2,2,16,128]{4,3,2,1,0:T(8,128)(2,1)S(1)}, bf16[2,2,2,16,128]{4,3,2,1,0:T(8,128)(2,1)S(1)}, u32[]{:S(2)}, u32[]{:S(2)}) collective-permute-start(bf16[2,2,2,16,128]{4,3,2,1,0:T(8,128)(2,1)S(1)} %corner_pack.3), channel_id=1, source_target_pairs={{0,16},{1,17},{2,18},{3,19},{4,20},{5,21},{6,22},{7,23},{8,24},{9,... | collective-permute-start | bytes 98312 | tf_op jit(solution)/shard_map/ppermute | solution.py:91
  50.8 0.0 collective-permute-done.7.face_in
  50.8 3.1 %third_main.1 = (f32[4,736,256]{2,1,0:T(8,128)S(1)}, f32[2,9,17,16,128]{4,3,2,1,0:T(8,128)S(1)}) custom-call(s32[1]{0:T(128)} %bitcast.even_ref, bf16[2,8,16,16,128]{4,3,2,1,0:T(8,128)(2,1)S(1)} %copy-done, bf16[16,16,896]{2,1,0:T(8,128)(2,1)} %collective-permute-done.from_x, bf16[8,16,896]{2,1,0:T(8,128)(2,1)S(1)} %collective-permute-done.1.from_y, ...), custom_call_target="tpu_custom_call" | custom-call | flops 1157627904 | bytes 19709956 | tf_op jit(solution)/shard_map/third_main/pallas_call | solution.py:592
  54.0 0.0 collective-permute-done.10.corner_in
  54.0 1.9 %third_corner.1 = (f32[2,9,17,16,128]{4,3,2,1,0:T(8,128)S(1)}, f32[4,2,16,128]{3,2,1,0:T(8,128)S(1)}, bf16[2,17,16,128]{3,2,1,0:T(8,128)(2,1)S(1)}) custom-call(s32[1]{0:T(128)} %bitcast.even_ref, bf16[2,8,16,16,128]{4,3,2,1,0:T(8,128)(2,1)S(1)} %copy-done, bf16[16,16,896]{2,1,0:T(8,128)(2,1)} %collective-permute-done.from_x, ...), custom_call_target="tpu_custom_call" | custom-call | flops 192937984 | bytes 17539076 | tf_op jit(solution)/shard_map/third_corner/pallas_call | solution.py:592
  55.9 1.1 %collective-permute-start.11 = (bf16[2,17,16,128]{3,2,1,0:T(8,128)(2,1)S(1)}, bf16[2,17,16,128]{3,2,1,0:T(8,128)(2,1)S(1)}, u32[]{:S(2)}, u32[]{:S(2)}) collective-permute-start(bf16[2,17,16,128]{3,2,1,0:T(8,128)(2,1)S(1)} %get-tuple-element.70), channel_id=1, source_target_pairs={{0,16},{1,17},{2,18},{3,19},{4,20},{5,21},{6,22},{7,23},{8,24},{9,... | collective-permute-start | bytes 417800 | tf_op jit(solution)/shard_map/ppermute | solution.py:91
  57.0 2.3 %third_end.1 = (f32[2,8,16,16,128]{4,3,2,1,0:T(8,128)}, f32[2,16,16,128]{3,2,1,0:T(8,128)S(1)}, f32[2,7,16,128]{3,2,1,0:T(8,128)S(1)}, f32[2,8,16,128]{3,2,1,0:T...) custom-call(s32[1]{0:T(128)} %bitcast.even_ref, f32[8,16,16,128]{3,2,1,0:T(8,128)S(1)} %broadcast_in_dim.4.own_inv, ...), custom_call_target="tpu_custom_call" | custom-call | flops 671088640 | bytes 15777796 | tf_op jit(solution)/shard_map/third_end/pallas_call | solution.py:592
  59.3 0.1 collective-permute-start.12
  59.3 1.3 %collective-permute-done.12.taken = bf16[256,256]{1,0:T(8,128)(2,1)S(1)} collective-permute-done((bf16[256,256]{1,0:T(8,128)(2,1)S(1)}, bf16[256,256]{1,0:T(8,128)(2,1)S(1)}, u32[]{:S(2)}, u32[]{:S(2)}) %collective-permute-start.12) | collective-permute-done | bytes 131104 | tf_op jit(solution)/shard_map/ppermute | solution.py:102
  60.7 0.3 collective-permute-done.11.face
  61.0 0.7 ready.1
  61.7 5.2 %all-to-all-start = ((bf16[16,32,256]{2,1,0:T(8,128)(2,1)}), bf16[16,32,256]{2,1,0:T(8,128)(2,1)S(1)}, u32[]{:S(2)}, u32[]{:S(2)}) async-start(bf16[16,32,256]{2,1,0:T(8,128)(2,1)} %bitcast.3), calls=%async_computation | async-start | bytes 524288 | tf_op jit(solution)/shard_map/all_to_all | solution.py:729
  67.0 0.1 collective-permute-start.13
  67.0 7.5 %collective-permute-done.13.side = bf16[2,8,16,128]{3,2,1,0:T(8,128)(2,1)S(1)} collective-permute-done((bf16[2,8,16,128]{3,2,1,0:T(8,128)(2,1)S(1)}, bf16[2,8,16,128]{3,2,1,0:T(8,128)(2,1)S(1)}, u32[]{:S(2)}, u32[]{:S(2)}) %collective-permute-start.13) | collective-permute-done | bytes 65568 | tf_op jit(solution)/shard_map/ppermute | solution.py:91
  74.6 0.8 %last.1 = f32[2,8,16,16,128]{4,3,2,1,0:T(8,128)} custom-call(f32[2,8,16,16,128]{4,3,2,1,0:T(8,128)} %get-tuple-element.67.old_hbm, f32[2,16,16,128]{3,2,1,0:T(8,128)S(1)} %get-tuple-element.68.edge_x, f32[2,7,16,128]{3,2,1,0:T(8,128)S(1)} %get-tuple-element.69.edge_y, ...), custom_call_target="tpu_custom_call", output_to_operand_aliasing={{}: (0, {})} | custom-call | bytes 4775936 | tf_op jit(solution)/shard_map/last/pallas_call | solution.py:592
  75.3 1.4 %all-to-all-done = bf16[16,32,256]{2,1,0:T(8,128)(2,1)S(1)} async-done(((bf16[16,32,256]{2,1,0:T(8,128)(2,1)}), bf16[16,32,256]{2,1,0:T(8,128)(2,1)S(1)}, u32[]{:S(2)}, u32[]{:S(2)}) %all-to-all-start) | async-done | bytes 262176 | tf_op jit(solution)/shard_map/all_to_all | solution.py:729
  76.8 0.7 convert_reduce_fusion
  (14 shorter events, 0.0 us)
Async XLA Ops:
  3.2 16.4 %collective-permute-start.1 = (bf16[8,16,896]{2,1,0:T(8,128)(2,1)}, bf16[8,16,896]{2,1,0:T(8,128)(2,1)S(1)}, u32[]{:S(2)}, u32[]{:S(2)}) collective-permute-start(bf16[8,16,896]{2,1,0:T(8,128)(2,1)} %get-tuple-element.40), channel_id=1, source_target_pairs={{0,15},{1,0},{2,1},{3,2},{4,3},{5,4},{6,5},{7,6},{8,7},{9,8},{10,9... | collective-permute-start | bytes 688136 | tf_op jit(solution)/shard_map/ppermute | solution.py:91
  8.6 11.5 %collective-permute-start = (bf16[16,16,896]{2,1,0:T(8,128)(2,1)}, bf16[16,16,896]{2,1,0:T(8,128)(2,1)}, u32[]{:S(2)}, u32[]{:S(2)}) collective-permute-start(bf16[16,16,896]{2,1,0:T(8,128)(2,1)} %get-tuple-element.39), channel_id=1, source_target_pairs={{0,16},{1,17},{2,18},{3,19},{4,20},{5,21},{6,22},{7,23},{8,24},{9,... | collective-permute-start | bytes 1376264 | tf_op jit(solution)/shard_map/ppermute | solution.py:91
  17.5 1.0 %copy-start.1 = (bf16[736,768]{1,0:T(8,128)(2,1)}, bf16[736,768]{1,0:T(8,128)(2,1)S(1)}, u32[]{:S(2)}) copy-start(bf16[736,768]{1,0:T(8,128)(2,1)S(1)} %get-tuple-element.45.refs_2_) | copy-start | bytes 3391492
  18.5 1.0 %copy-start.3 = (bf16[736,768]{1,0:T(8,128)(2,1)}, bf16[736,768]{1,0:T(8,128)(2,1)S(1)}, u32[]{:S(2)}) copy-start(bf16[736,768]{1,0:T(8,128)(2,1)S(1)} %get-tuple-element.46.refs_3_) | copy-start | bytes 3391492
  19.5 3.0 %copy-start = (bf16[2,8,16,16,128]{4,3,2,1,0:T(8,128)(2,1)S(1)}, bf16[2,8,16,16,128]{4,3,2,1,0:T(8,128)(2,1)}, u32[]{:S(2)}) copy-start(bf16[2,8,16,16,128]{4,3,2,1,0:T(8,128)(2,1)} %vec.11) | copy-start | bytes 3145732
  19.5 3.0 %copy-start.2 = (bf16[736,768]{1,0:T(8,128)(2,1)S(1)}, bf16[736,768]{1,0:T(8,128)(2,1)}, u32[]{:S(2)}) copy-start(bf16[736,768]{1,0:T(8,128)(2,1)} %copy-done.1) | copy-start | bytes 3391492
  19.5 6.8 %collective-permute-start.2 = (bf16[1,16,896]{2,1,0:T(8,128)(2,1)S(1)}, bf16[1,16,896]{2,1,0:T(8,128)(2,1)S(1)}, u32[]{:S(2)}, u32[]{:S(2)}) collective-permute-start(bf16[1,16,896]{2,1,0:T(8,128)(2,1)S(1)} %slice.4), channel_id=1, source_target_pairs={{0,16},{1,17},{2,18},{3,19},{4,20},{5,21},{6,22},{7,23},{8,24},{9,... | collective-permute-start | bytes 86024 | tf_op jit(solution)/shard_map/ppermute | solution.py:91
  22.6 1.3 %copy-start.4 = (bf16[736,768]{1,0:T(8,128)(2,1)S(1)}, bf16[736,768]{1,0:T(8,128)(2,1)}, u32[]{:S(2)}) copy-start(bf16[736,768]{1,0:T(8,128)(2,1)} %copy-done.3) | copy-start | bytes 3391492
  26.3 10.5 %copy-start.5 = (bf16[736,768]{1,0:T(8,128)(2,1)S(1)}, bf16[736,768]{1,0:T(8,128)(2,1)}, u32[]{:S(2)}) copy-start(bf16[736,768]{1,0:T(8,128)(2,1)} %copy-done.3) | copy-start | bytes 3391492
  28.3 8.6 %collective-permute-start.3 = (bf16[2,2,17,16,128]{4,3,2,1,0:T(8,128)(2,1)S(1)}, bf16[2,2,17,16,128]{4,3,2,1,0:T(8,128)(2,1)S(1)}, u32[]{:S(2)}, u32[]{:S(2)}) collective-permute-start(bf16[2,2,17,16,128]{4,3,2,1,0:T(8,128)(2,1)S(1)} %get-tuple-element.53), channel_id=1, source_target_pairs={{0,16},{1,17},{2,18},{3,19},{4,20},{5,21},{6,22},{7,23},{8,24},{9,... | collective-permute-start | bytes 835592 | tf_op jit(solution)/shard_map/ppermute | solution.py:91
  29.8 2.7 %collective-permute-start.4 = (bf16[2,9,16,128]{3,2,1,0:T(8,128)(2,1)S(1)}, bf16[2,9,16,128]{3,2,1,0:T(8,128)(2,1)S(1)}, u32[]{:S(2)}, u32[]{:S(2)}) collective-permute-start(bf16[2,9,16,128]{3,2,1,0:T(8,128)(2,1)S(1)} %get-tuple-element.54), channel_id=1, source_target_pairs={{0,1},{1,0},{2,3},{3,2},{4,5},{5,4},{6,7},{7,6},{8,9},{9,8},{10,11... | collective-permute-start | bytes 221192 | tf_op jit(solution)/shard_map/ppermute | solution.py:102
  29.8 6.5 %collective-permute-start.5 = (bf16[2,9,16,128]{3,2,1,0:T(8,128)(2,1)S(1)}, bf16[2,9,16,128]{3,2,1,0:T(8,128)(2,1)S(1)}, u32[]{:S(2)}, u32[]{:S(2)}) collective-permute-start(bf16[2,9,16,128]{3,2,1,0:T(8,128)(2,1)S(1)} %get-tuple-element.55), channel_id=1, source_target_pairs={{0,15},{1,2},{2,1},{3,4},{4,3},{5,6},{6,5},{7,8},{8,7},{9,10},{10,... | collective-permute-start | bytes 221192 | tf_op jit(solution)/shard_map/ppermute | solution.py:108
  36.3 3.9 %collective-permute-start.6 = (bf16[2,2,2,16,128]{4,3,2,1,0:T(8,128)(2,1)S(1)}, bf16[2,2,2,16,128]{4,3,2,1,0:T(8,128)(2,1)S(1)}, u32[]{:S(2)}, u32[]{:S(2)}) collective-permute-start(bf16[2,2,2,16,128]{4,3,2,1,0:T(8,128)(2,1)S(1)} %corner_pack.2), channel_id=1, source_target_pairs={{0,16},{1,17},{2,18},{3,19},{4,20},{5,21},{6,22},{7,23},{8,24},{9,... | collective-permute-start | bytes 98312 | tf_op jit(solution)/shard_map/ppermute | solution.py:91
  40.2 5.4 %copy-start.6 = (bf16[8,16,16,512]{3,2,1,0:T(8,128)(2,1)S(1)}, bf16[8,16,16,512]{3,2,1,0:T(8,128)(2,1)}, u32[]{:S(2)}) copy-start(bf16[8,16,16,512]{3,2,1,0:T(8,128)(2,1)} %res_hbm.1) | copy-start | bytes 6291460
  42.3 8.6 %collective-permute-start.7 = (bf16[2,2,17,16,128]{4,3,2,1,0:T(8,128)(2,1)S(1)}, bf16[2,2,17,16,128]{4,3,2,1,0:T(8,128)(2,1)S(1)}, u32[]{:S(2)}, u32[]{:S(2)}) collective-permute-start(bf16[2,2,17,16,128]{4,3,2,1,0:T(8,128)(2,1)S(1)} %get-tuple-element.58), channel_id=1, source_target_pairs={{0,16},{1,17},{2,18},{3,19},{4,20},{5,21},{6,22},{7,23},{8,24},{9,... | collective-permute-start | bytes 835592 | tf_op jit(solution)/shard_map/ppermute | solution.py:91
  43.4 4.1 %collective-permute-start.8 = (bf16[2,9,16,128]{3,2,1,0:T(8,128)(2,1)S(1)}, bf16[2,9,16,128]{3,2,1,0:T(8,128)(2,1)S(1)}, u32[]{:S(2)}, u32[]{:S(2)}) collective-permute-start(bf16[2,9,16,128]{3,2,1,0:T(8,128)(2,1)S(1)} %get-tuple-element.59), channel_id=1, source_target_pairs={{0,1},{1,0},{2,3},{3,2},{4,5},{5,4},{6,7},{7,6},{8,9},{9,8},{10,11... | collective-permute-start | bytes 221192 | tf_op jit(solution)/shard_map/ppermute | solution.py:102
  43.4 6.5 %collective-permute-start.9 = (bf16[2,9,16,128]{3,2,1,0:T(8,128)(2,1)S(1)}, bf16[2,9,16,128]{3,2,1,0:T(8,128)(2,1)S(1)}, u32[]{:S(2)}, u32[]{:S(2)}) collective-permute-start(bf16[2,9,16,128]{3,2,1,0:T(8,128)(2,1)S(1)} %get-tuple-element.60), channel_id=1, source_target_pairs={{0,15},{1,2},{2,1},{3,4},{4,3},{5,6},{6,5},{7,8},{8,7},{9,10},{10,... | collective-permute-start | bytes 221192 | tf_op jit(solution)/shard_map/ppermute | solution.py:108
  49.9 4.1 %collective-permute-start.10 = (bf16[2,2,2,16,128]{4,3,2,1,0:T(8,128)(2,1)S(1)}, bf16[2,2,2,16,128]{4,3,2,1,0:T(8,128)(2,1)S(1)}, u32[]{:S(2)}, u32[]{:S(2)}) collective-permute-start(bf16[2,2,2,16,128]{4,3,2,1,0:T(8,128)(2,1)S(1)} %corner_pack.3), channel_id=1, source_target_pairs={{0,16},{1,17},{2,18},{3,19},{4,20},{5,21},{6,22},{7,23},{8,24},{9,... | collective-permute-start | bytes 98312 | tf_op jit(solution)/shard_map/ppermute | solution.py:91
  55.9 5.1 %collective-permute-start.11 = (bf16[2,17,16,128]{3,2,1,0:T(8,128)(2,1)S(1)}, bf16[2,17,16,128]{3,2,1,0:T(8,128)(2,1)S(1)}, u32[]{:S(2)}, u32[]{:S(2)}) collective-permute-start(bf16[2,17,16,128]{3,2,1,0:T(8,128)(2,1)S(1)} %get-tuple-element.70), channel_id=1, source_target_pairs={{0,16},{1,17},{2,18},{3,19},{4,20},{5,21},{6,22},{7,23},{8,24},{9,... | collective-permute-start | bytes 417800 | tf_op jit(solution)/shard_map/ppermute | solution.py:91
  59.3 1.4 %collective-permute-start.12 = (bf16[256,256]{1,0:T(8,128)(2,1)S(1)}, bf16[256,256]{1,0:T(8,128)(2,1)S(1)}, u32[]{:S(2)}, u32[]{:S(2)}) collective-permute-start(bf16[256,256]{1,0:T(8,128)(2,1)S(1)} %get-tuple-element.72), channel_id=1, source_target_pairs={{0,1},{1,0},{2,3},{3,2},{4,5},{5,4},{6,7},{7,6},{8,9},{9,8},{10,11... | collective-permute-start | bytes 393224 | tf_op jit(solution)/shard_map/ppermute | solution.py:102
  61.7 15.1 %all-to-all-start = ((bf16[16,32,256]{2,1,0:T(8,128)(2,1)}), bf16[16,32,256]{2,1,0:T(8,128)(2,1)S(1)}, u32[]{:S(2)}, u32[]{:S(2)}) async-start(bf16[16,32,256]{2,1,0:T(8,128)(2,1)} %bitcast.3), calls=%async_computation | async-start | bytes 524288 | tf_op jit(solution)/shard_map/all_to_all | solution.py:729
  67.0 7.6 %collective-permute-start.13 = (bf16[2,8,16,128]{3,2,1,0:T(8,128)(2,1)S(1)}, bf16[2,8,16,128]{3,2,1,0:T(8,128)(2,1)S(1)}, u32[]{:S(2)}, u32[]{:S(2)}) collective-permute-start(bf16[2,8,16,128]{3,2,1,0:T(8,128)(2,1)S(1)} %get-tuple-element.74), channel_id=1, source_target_pairs={{0,1},{1,2},{2,3},{3,4},{4,5},{5,6},{6,7},{7,8},{8,9},{9,10},{10,1... | collective-permute-start | bytes 196616 | tf_op jit(solution)/shard_map/ppermute | solution.py:91

commit v8 on v7

--- a/solution.py
+++ b/solution.py
@@ -11,7 +11,7 @@
 LANES = 128
 TILE = 256
 SUB = 16
-VMEM_LIMIT = 12 * 1024 * 1024
+VMEM_LIMIT = 16 * 1024 * 1024
 
 center_shift = 1.2
 half_width = 2.0
@@ -109,7 +109,12 @@
     return send_near(near), far
 
 
+def cell_matrices(refs):
+    return [ref.at[at] for ref in refs for at in range(ref.shape[0])]
+
+
 def order_kernel(sz, conn_ref, matrix_ref, *out_refs):
+    matrices = cell_matrices(out_refs)
     for cell in range(sz.cells):
         x0, y0, z0 = sz.origins[cell]
         conn = conn_ref[cell : cell + 1, :].astype(f32)
@@ -138,12 +143,12 @@
             block = lax.dot_general(
                 half[r0:r1], pick[r0:], (((1,), (1,)), ((), ())), preferred_element_type=f32
             ).astype(bf16)
-            out_refs[cell][r0:r1, r0:] = block
+            matrices[cell][r0:r1, r0:] = block
             for c0, c1 in zip(cuts[:-1], cuts[1:]):
                 if c0 > r0:
                     mirror = block[:, c0 - r0 : c1 - r0].T
                     c1 = min(c1, sz.rows)
-                    out_refs[cell][c0:c1, r0:r1] = mirror[: c1 - c0]
+                    matrices[cell][c0:c1, r0:r1] = mirror[: c1 - c0]
 
 
 def field_row(inv, pot):
@@ -202,9 +207,15 @@
         copy.wait()
 
 
-def turn_kernel(sz, pieces, res_ref, from_x, from_y, corner, out_ref):
+def turn_kernel(sz, pieces, res_hbm, from_x, from_y, corner, out_ref, res_ref, sems):
     own = sz.own_edges * sz.ez
     share = sz.res // out_ref.shape[0] // pieces
+    copies = [
+        pltpu.make_async_copy(res_hbm.at[:, pl.ds(g, LANES)], res_ref.at[:, pl.ds(g, LANES)], sems.at[at])
+        for at, g in enumerate(range(0, sz.res, LANES))
+    ]
+    for copy in copies:
+        copy.start()
 
     def put(g, columns, value):
         for at in range(0, LANES, share):
@@ -214,6 +225,7 @@
 
     for g in range(0, sz.res, LANES):
         lanes = slice(g, g + LANES)
+        copies[g // LANES].wait()
         put(g, slice(0, own), res_ref[:, lanes].T)
         rest = sz.edges - sz.own_edges - sz.ey - sz.gx
         parts = [from_x[:, :, lanes], from_y[:, :, lanes], corner[:, :, lanes]]
@@ -286,6 +298,7 @@
     flat = sz.gx * sz.gy * sz.gz
     u_flat = u_ref.reshape(sz.blocks * flat, width)
     last = sz.nodes // 8 * 8
+    matrices = cell_matrices(mat_refs)
     ready = set()
     for cell, (x0, y0, z0) in enumerate(sz.origins):
         slot = cell % 2
@@ -314,7 +327,7 @@
                     pl.ds(start, count, stride=sz.gz)
                 ]
         out_ref[cell] = jnp.dot(
-            mat_refs[cell][...], rhs_ref[slot].astype(bf16), preferred_element_type=f32
+            matrices[cell][...], rhs_ref[slot].astype(bf16), preferred_element_type=f32
         )
 
 
@@ -323,6 +336,7 @@
     flat = sz.gx * sz.gy * sz.gz
     acc_flat = acc_ref.reshape(sz.blocks * flat, width)
     small_ref[...] = jnp.zeros_like(small_ref)
+    matrices = cell_matrices(mat_refs)
     touched = set()
     for cell, (x0, y0, z0) in enumerate(sz.origins):
         z1 = z0 + sz.p
@@ -336,7 +350,7 @@
                 small_ref[rank * sz.p : (rank + 1) * sz.p, lanes] = value[b, z0:z1]
                 small_ref[last : last + 1, lanes] = value[b, wrap : wrap + 1]
         total = prod_ref[cell] + jnp.dot(
-            mat_refs[cell][:, : small_ref.shape[0]], small_ref[...].astype(bf16),
+            matrices[cell][:, : small_ref.shape[0]], small_ref[...].astype(bf16),
             preferred_element_type=f32,
         )
         tail_ref[cell, : sz.base] = total[: sz.base]
@@ -624,9 +638,10 @@
     from_x = send(to_x, -1, 0)
     from_y = send(to_y, 0, -1)
 
+    halves = 2 if sz.cells % 2 == 0 else 1
     mats = call(
         functools.partial(order_kernel, sz), "order_cells", 4 * sz.cells * sz.depth**3,
-        [Pinned(like((sz.rows, sz.depth), bf16))] * sz.cells, [], [conn, cell_matrix],
+        [Pinned(like((sz.cells // halves, sz.rows, sz.depth), bf16))] * halves, [], [conn, cell_matrix],
     )
     own_inv = jnp.broadcast_to(inv_mass[..., None], inv_mass.shape + (width,))
     own_pot = jnp.broadcast_to(potential[..., None], inv_mass.shape + (width,))
@@ -675,8 +690,12 @@
     )
     (turned,) = call(
         functools.partial(turn_kernel, sz, ny // 2), "turn_residents", flops // 2,
-        [like((2, res_count // 2, sz.edges * ez), bf16)], [],
-        [resident.reshape(-1, res_count), from_x, from_y, ghost_corner],
+        [like((2, res_count // 2, sz.edges * ez), bf16)],
+        [
+            pltpu.VMEM((sz.own_edges * ez, res_count), bf16),
+            pltpu.SemaphoreType.DMA((res_count // LANES,)),
+        ],
+        [resident.reshape(-1, res_count), from_x, from_y, ghost_corner], hbm=1,
     )
     got, corner = exchange(face, near, far)
     state = [vectors, from_x, from_y, own_inv, own_pot, ghost_x, ghost_y]

time: 78 us -> 76.6 us (0.982)
  waiting for transfers between devices: 17.2 us -> 14.6 us
  starting transfers between devices: 23.1 us -> 25.1 us
  local copies, waits for them, and re-layouts: 5.7 us -> 3.83 us
  Pallas kernels: 30 us -> 30.9 us
    ppermute x2, waiting for transfers between devices: 6.11 us -> 3.55 us  [swap_y(): far = lax.ppermute(far, 'dy', far_pairs)]
    unnamed x14 -> x6, local copies, waits for them, and re-layouts: 3.28 us -> 1.39 us
    ppermute x2, starting transfers between devices: 4.9 us -> 6.21 us  [swap_y(): far = lax.ppermute(far, 'dy', far_pairs)]
    pallas_call x14, Pallas kernels: 30 us -> 30.9 us  [call(): pl.pallas_call(kernel, in_specs=specs, out_specs=out_specs, out_shape=out...]
  transfers between devices with their start and end apart: 15 -> 15, of which waited for: 7 -> 7; matrix products, arithmetic and copies ran while one was open for 3% -> 3% of each run, Pallas kernels for 27% -> 29%
where the time goes in v8:
time: 76.6 us; the launch traced here: 76 us
  Pallas kernels  30.9 us (40%)
  starting transfers between devices  25.1 us (33%)
  waiting for transfers between devices  14.6 us (19%)
  local copies, waits for them, and re-layouts  3.83 us (5%)
  between operations  0.81 us (1%)
    pallas_call x14, Pallas kernels, call(): pl.pallas_call(kernel, in_specs=specs, out_specs=out_specs, out_shape=out...  30.9 us
    ppermute x9, starting transfers between devices, send(): return lax.ppermute(value, ('dx', 'dy'), pairs)  12.9 us
    ppermute x9, waiting for transfers between devices, send(): return lax.ppermute(value, ('dx', 'dy'), pairs)  8.32 us
    ppermute x2, starting transfers between devices, swap_y(): far = lax.ppermute(far, 'dy', far_pairs)  6.21 us
    all_to_all x1, starting transfers between devices, body(): lax.all_to_all(pieces, ('dx', 'dy'), 0, 0, axis_index_groups=groups)  5.91 us
    ppermute x2, waiting for transfers between devices, swap_y(): far = lax.ppermute(far, 'dy', far_pairs)  3.55 us
  transfers between devices with their start and end apart: 15, of which 7 were waited for; matrix products, arithmetic and copies ran while one was open for 3% of the time, Pallas kernels for 29%

profile of v8, /device:TPU:0, one launch (start us, length us, event | category | flops | bytes accessed | tf_op | source)
XLA Modules:
  0.0 76.0 jit_solution(11944287034606334623)
XLA Ops:
  0.6 2.5 %pack.1 = (bf16[16,16,896]{2,1,0:T(8,128)(2,1)}, bf16[8,16,896]{2,1,0:T(8,128)(2,1)}, bf16[729,729]{1,0:T(8,128)(2,1)S(1)}, s32[4,729]{1,0:T(4,128)S(1)}) custom-call(bf16[2,8,16,16,128]{4,3,2,1,0:T(8,128)(2,1)} %vec.11, bf16[8,16,16,512]{3,2,1,0:T(8,128)(2,1)} %res_hbm.1, f32[8,16,16]{2,1,0:T(8,128)} %inv_hbm.1, f32[8,16,16]{2,1,0:T(8,128)} %pot_hbm.1, ...), custom_call_target="tpu_custom_call" | custom-call | bytes 5999332 | tf_op jit(solution)/shard_map/pack/pallas_call | solution.py:606
  3.1 5.5 %collective-permute-start.1 = (bf16[8,16,896]{2,1,0:T(8,128)(2,1)}, bf16[8,16,896]{2,1,0:T(8,128)(2,1)S(1)}, u32[]{:S(2)}, u32[]{:S(2)}) collective-permute-start(bf16[8,16,896]{2,1,0:T(8,128)(2,1)} %get-tuple-element.38), channel_id=1, source_target_pairs={{0,15},{1,0},{2,1},{3,2},{4,3},{5,4},{6,5},{7,6},{8,7},{9,8},{10,9... | collective-permute-start | bytes 688136 | tf_op jit(solution)/shard_map/ppermute | solution.py:91
  8.6 1.5 %collective-permute-start = (bf16[16,16,896]{2,1,0:T(8,128)(2,1)}, bf16[16,16,896]{2,1,0:T(8,128)(2,1)}, u32[]{:S(2)}, u32[]{:S(2)}) collective-permute-start(bf16[16,16,896]{2,1,0:T(8,128)(2,1)} %get-tuple-element.37), channel_id=1, source_target_pairs={{0,16},{1,17},{2,18},{3,19},{4,20},{5,21},{6,22},{7,23},{8,24},{9,... | collective-permute-start | bytes 1376264 | tf_op jit(solution)/shard_map/ppermute | solution.py:91
  10.1 7.4 %order_cells.1 = (bf16[2,736,768]{2,1,0:T(8,128)(2,1)S(1)}, bf16[2,736,768]{2,1,0:T(8,128)(2,1)S(1)}) custom-call(s32[4,729]{1,0:T(4,128)S(1)} %get-tuple-element.39.conn_ref, bf16[729,729]{1,0:T(8,128)(2,1)S(1)} %get-tuple-element.40.matrix_ref), custom_call_target="tpu_custom_call" | custom-call | flops 7247757312 | bytes 5596530 | tf_op jit(solution)/shard_map/order_cells/pallas_call | solution.py:606
  17.5 0.0 copy-start
  17.5 1.4 %copy-done = bf16[2,736,768]{2,1,0:T(8,128)(2,1)} copy-done((bf16[2,736,768]{2,1,0:T(8,128)(2,1)}, bf16[2,736,768]{2,1,0:T(8,128)(2,1)S(1)}, u32[]{:S(2)}) %copy-start) | copy-done | bytes 2261016
  18.9 0.0 collective-permute-done.1.from_y
  18.9 0.6 collective-permute-start.2
  19.5 0.0 collective-permute-done.from_x
  19.5 1.3 %broadcast_in_dim.4.own_inv = f32[8,16,16,128]{3,2,1,0:T(8,128)S(1)} broadcast(f32[8,16,16]{2,1,0:T(8,128)} %inv_hbm.1), dimensions={0,1,2} | broadcast | bytes 1056768 | tf_op jit(solution)/shard_map/broadcast_in_dim | solution.py:646
  20.7 1.2 %broadcast_in_dim.5.own_pot = f32[8,16,16,128]{3,2,1,0:T(8,128)S(1)} broadcast(f32[8,16,16]{2,1,0:T(8,128)} %pot_hbm.1), dimensions={0,1,2} | broadcast | bytes 1056768 | tf_op jit(solution)/shard_map/broadcast_in_dim | solution.py:647
  21.9 0.0 copy-done.2
  21.9 2.5 %first_main.1 = (f32[4,736,256]{2,1,0:T(8,128)S(1)}, f32[2,16,16,128]{3,2,1,0:T(8,128)S(1)}, f32[2,8,16,128]{3,2,1,0:T(8,128)S(1)}) custom-call(bf16[2,8,16,16,128]{4,3,2,1,0:T(8,128)(2,1)S(1)} %copy-done.2, bf16[16,16,896]{2,1,0:T(8,128)(2,1)} %collective-permute-done.from_x, bf16[8,16,896]{2,1,0:T(8,128)(2,1)S(1)} %collective-permute-done.1.from_y, ...), custom_call_target="tpu_custom_call" | custom-call | flops 1157627904 | bytes 11763712 | tf_op jit(solution)/shard_map/first_main/pallas_call | solution.py:606
  24.4 0.0 collective-permute-done.2.corner
  24.4 1.9 %first_corner.1 = (f32[2,9,17,16,128]{4,3,2,1,0:T(8,128)S(1)}, bf16[2,2,17,16,128]{4,3,2,1,0:T(8,128)(2,1)S(1)}, bf16[2,9,16,128]{3,2,1,0:T(8,128)(2,1)S(1)}, bf...) custom-call(s32[1]{0:T(128)} %bitcast.even_ref, ...), custom_call_target="tpu_custom_call" | custom-call | flops 192937984 | bytes 14757892 | tf_op jit(solution)/shard_map/first_corner/pallas_call | solution.py:606
  26.3 1.5 %collective-permute-start.3 = (bf16[2,2,17,16,128]{4,3,2,1,0:T(8,128)(2,1)S(1)}, bf16[2,2,17,16,128]{4,3,2,1,0:T(8,128)(2,1)S(1)}, u32[]{:S(2)}, u32[]{:S(2)}) collective-permute-start(bf16[2,2,17,16,128]{4,3,2,1,0:T(8,128)(2,1)S(1)} %get-tuple-element.49), channel_id=1, source_target_pairs={{0,16},{1,17},{2,18},{3,19},{4,20},{5,21},{6,22},{7,23},{8,24},{9,... | collective-permute-start | bytes 835592 | tf_op jit(solution)/shard_map/ppermute | solution.py:91
  27.8 0.0 collective-permute-start.4
  27.8 3.4 %collective-permute-start.5 = (bf16[2,9,16,128]{3,2,1,0:T(8,128)(2,1)S(1)}, bf16[2,9,16,128]{3,2,1,0:T(8,128)(2,1)S(1)}, u32[]{:S(2)}, u32[]{:S(2)}) collective-permute-start(bf16[2,9,16,128]{3,2,1,0:T(8,128)(2,1)S(1)} %get-tuple-element.51), channel_id=1, source_target_pairs={{0,15},{1,2},{2,1},{3,4},{4,3},{5,6},{6,5},{7,8},{8,7},{9,10},{10,... | collective-permute-start | bytes 221192 | tf_op jit(solution)/shard_map/ppermute | solution.py:108
  31.2 0.0 collective-permute-done.4.near.near_in
  31.2 3.1 %collective-permute-done.5.far.far_in = bf16[2,9,16,128]{3,2,1,0:T(8,128)(2,1)S(1)} collective-permute-done((bf16[2,9,16,128]{3,2,1,0:T(8,128)(2,1)S(1)}, bf16[2,9,16,128]{3,2,1,0:T(8,128)(2,1)S(1)}, u32[]{:S(2)}, u32[]{:S(2)}) %collective-permute-start.5) | collective-permute-done | bytes 73760 | tf_op jit(solution)/shard_map/ppermute | solution.py:108
  34.3 0.6 collective-permute-start.6
  34.9 0.0 collective-permute-done.3.face_in
  34.9 2.9 %second_main.1 = (f32[4,736,256]{2,1,0:T(8,128)S(1)}, f32[2,9,17,16,128]{4,3,2,1,0:T(8,128)S(1)}) custom-call(s32[1]{0:T(128)} %bitcast.even_ref, bf16[2,8,16,16,128]{4,3,2,1,0:T(8,128)(2,1)S(1)} %copy-done.2, bf16[16,16,896]{2,1,0:T(8,128)(2,1)} %collective-permute-done.from_x, bf16[8,16,896]{2,1,0:T(8,128)(2,1)S(1)} %collective-permute-done.1.from_y, ...), custom_call_target="tpu_custom_call" | custom-call | flops 1157627904 | bytes 17203204 | tf_op jit(solution)/shard_map/second_main/pallas_call | solution.py:606
  37.8 0.4 collective-permute-done.6.corner_in
  38.2 1.9 %second_corner.1 = (f32[2,9,17,16,128]{4,3,2,1,0:T(8,128)S(1)}, bf16[2,2,17,16,128]{4,3,2,1,0:T(8,128)(2,1)S(1)}, bf16[2,9,16,128]{3,2,1,0:T(8,128)(2,1)S(1)}, b...) custom-call(s32[1]{0:T(128)} %bitcast.even_ref, bf16[2,8,16,16,128]{4,3,2,1,0:T(8,128)(2,1)S(1)} %copy-done.2, ...), custom_call_target="tpu_custom_call" | custom-call | flops 192937984 | bytes 17760260 | tf_op jit(solution)/shard_map/second_corner/pallas_call | solution.py:606
  40.1 1.1 %collective-permute-start.7 = (bf16[2,2,17,16,128]{4,3,2,1,0:T(8,128)(2,1)S(1)}, bf16[2,2,17,16,128]{4,3,2,1,0:T(8,128)(2,1)S(1)}, u32[]{:S(2)}, u32[]{:S(2)}) collective-permute-start(bf16[2,2,17,16,128]{4,3,2,1,0:T(8,128)(2,1)S(1)} %get-tuple-element.54), channel_id=1, source_target_pairs={{0,16},{1,17},{2,18},{3,19},{4,20},{5,21},{6,22},{7,23},{8,24},{9,... | collective-permute-start | bytes 835592 | tf_op jit(solution)/shard_map/ppermute | solution.py:91
  41.2 0.0 collective-permute-start.8
  41.2 2.8 %collective-permute-start.9 = (bf16[2,9,16,128]{3,2,1,0:T(8,128)(2,1)S(1)}, bf16[2,9,16,128]{3,2,1,0:T(8,128)(2,1)S(1)}, u32[]{:S(2)}, u32[]{:S(2)}) collective-permute-start(bf16[2,9,16,128]{3,2,1,0:T(8,128)(2,1)S(1)} %get-tuple-element.56), channel_id=1, source_target_pairs={{0,15},{1,2},{2,1},{3,4},{4,3},{5,6},{6,5},{7,8},{8,7},{9,10},{10,... | collective-permute-start | bytes 221192 | tf_op jit(solution)/shard_map/ppermute | solution.py:108
  44.0 3.2 %turn_residents.1.turned = bf16[2,256,2560]{2,1,0:T(8,128)(2,1)S(1)} custom-call(bf16[2048,512]{1,0:T(8,128)(2,1)} %bitcast.4, bf16[16,16,896]{2,1,0:T(8,128)(2,1)} %collective-permute-done.from_x, bf16[8,16,896]{2,1,0:T(8,128)(2,1)S(1)} %collective-permute-done.1.from_y, bf16[1,16,896]{2,1,0:T(8,128)(2,1)S(1)} %collective-permute-done.2.corner), custom_call_target="tpu_custom_call" | custom-call | flops 578813952 | bytes 5435392 | tf_op jit(solution)/shard_map/turn_residents/pallas_call | solution.py:606
  47.2 0.0 collective-permute-done.8.near.near_in
  47.2 0.5 collective-permute-done.9.far.far_in
  47.7 1.0 %collective-permute-start.10 = (bf16[2,2,2,16,128]{4,3,2,1,0:T(8,128)(2,1)S(1)}, bf16[2,2,2,16,128]{4,3,2,1,0:T(8,128)(2,1)S(1)}, u32[]{:S(2)}, u32[]{:S(2)}) collective-permute-start(bf16[2,2,2,16,128]{4,3,2,1,0:T(8,128)(2,1)S(1)} %corner_pack.3), channel_id=1, source_target_pairs={{0,16},{1,17},{2,18},{3,19},{4,20},{5,21},{6,22},{7,23},{8,24},{9,... | collective-permute-start | bytes 98312 | tf_op jit(solution)/shard_map/ppermute | solution.py:91
  48.7 0.0 collective-permute-done.7.face_in
  48.7 3.1 %third_main.1 = (f32[4,736,256]{2,1,0:T(8,128)S(1)}, f32[2,9,17,16,128]{4,3,2,1,0:T(8,128)S(1)}) custom-call(s32[1]{0:T(128)} %bitcast.even_ref, bf16[2,8,16,16,128]{4,3,2,1,0:T(8,128)(2,1)S(1)} %copy-done.2, bf16[16,16,896]{2,1,0:T(8,128)(2,1)} %collective-permute-done.from_x, bf16[8,16,896]{2,1,0:T(8,128)(2,1)S(1)} %collective-permute-done.1.from_y, ...), custom_call_target="tpu_custom_call" | custom-call | flops 1157627904 | bytes 19709956 | tf_op jit(solution)/shard_map/third_main/pallas_call | solution.py:606
  51.8 0.0 collective-permute-done.10.corner_in
  51.8 1.9 %third_corner.1 = (f32[2,9,17,16,128]{4,3,2,1,0:T(8,128)S(1)}, f32[4,2,16,128]{3,2,1,0:T(8,128)S(1)}, bf16[2,17,16,128]{3,2,1,0:T(8,128)(2,1)S(1)}) custom-call(s32[1]{0:T(128)} %bitcast.even_ref, bf16[2,8,16,16,128]{4,3,2,1,0:T(8,128)(2,1)S(1)} %copy-done.2, bf16[16,16,896]{2,1,0:T(8,128)(2,1)} %collective-permute-done.from_x, ...), custom_call_target="tpu_custom_call" | custom-call | flops 192937984 | bytes 17539076 | tf_op jit(solution)/shard_map/third_corner/pallas_call | solution.py:606
  53.7 1.1 %collective-permute-start.11 = (bf16[2,17,16,128]{3,2,1,0:T(8,128)(2,1)S(1)}, bf16[2,17,16,128]{3,2,1,0:T(8,128)(2,1)S(1)}, u32[]{:S(2)}, u32[]{:S(2)}) collective-permute-start(bf16[2,17,16,128]{3,2,1,0:T(8,128)(2,1)S(1)} %get-tuple-element.66), channel_id=1, source_target_pairs={{0,16},{1,17},{2,18},{3,19},{4,20},{5,21},{6,22},{7,23},{8,24},{9,... | collective-permute-start | bytes 417800 | tf_op jit(solution)/shard_map/ppermute | solution.py:91
  54.8 2.3 %third_end.1 = (f32[2,8,16,16,128]{4,3,2,1,0:T(8,128)}, f32[2,16,16,128]{3,2,1,0:T(8,128)S(1)}, f32[2,7,16,128]{3,2,1,0:T(8,128)S(1)}, f32[2,8,16,128]{3,2,1,0:T...) custom-call(s32[1]{0:T(128)} %bitcast.even_ref, f32[8,16,16,128]{3,2,1,0:T(8,128)S(1)} %broadcast_in_dim.4.own_inv, ...), custom_call_target="tpu_custom_call" | custom-call | flops 671088640 | bytes 15777796 | tf_op jit(solution)/shard_map/third_end/pallas_call | solution.py:606
  57.1 0.1 collective-permute-start.12
  57.2 1.3 %collective-permute-done.12.taken = bf16[256,256]{1,0:T(8,128)(2,1)S(1)} collective-permute-done((bf16[256,256]{1,0:T(8,128)(2,1)S(1)}, bf16[256,256]{1,0:T(8,128)(2,1)S(1)}, u32[]{:S(2)}, u32[]{:S(2)}) %collective-permute-start.12) | collective-permute-done | bytes 131104 | tf_op jit(solution)/shard_map/ppermute | solution.py:102
  58.5 0.3 collective-permute-done.11.face
  58.8 0.7 ready.1
  59.5 5.9 %all-to-all-start = ((bf16[16,32,256]{2,1,0:T(8,128)(2,1)}), bf16[16,32,256]{2,1,0:T(8,128)(2,1)S(1)}, u32[]{:S(2)}, u32[]{:S(2)}) async-start(bf16[16,32,256]{2,1,0:T(8,128)(2,1)} %bitcast.3), calls=%async_computation | async-start | bytes 524288 | tf_op jit(solution)/shard_map/all_to_all | solution.py:748
  65.5 0.1 collective-permute-start.13
  65.5 7.6 %collective-permute-done.13.side = bf16[2,8,16,128]{3,2,1,0:T(8,128)(2,1)S(1)} collective-permute-done((bf16[2,8,16,128]{3,2,1,0:T(8,128)(2,1)S(1)}, bf16[2,8,16,128]{3,2,1,0:T(8,128)(2,1)S(1)}, u32[]{:S(2)}, u32[]{:S(2)}) %collective-permute-start.13) | collective-permute-done | bytes 65568 | tf_op jit(solution)/shard_map/ppermute | solution.py:91
  73.1 0.8 %last.1 = f32[2,8,16,16,128]{4,3,2,1,0:T(8,128)} custom-call(f32[2,8,16,16,128]{4,3,2,1,0:T(8,128)} %get-tuple-element.63.old_hbm, f32[2,16,16,128]{3,2,1,0:T(8,128)S(1)} %get-tuple-element.64.edge_x, f32[2,7,16,128]{3,2,1,0:T(8,128)S(1)} %get-tuple-element.65.edge_y, ...), custom_call_target="tpu_custom_call", output_to_operand_aliasing={{}: (0, {})} | custom-call | bytes 4775936 | tf_op jit(solution)/shard_map/last/pallas_call | solution.py:606
  73.9 1.4 %all-to-all-done = bf16[16,32,256]{2,1,0:T(8,128)(2,1)S(1)} async-done(((bf16[16,32,256]{2,1,0:T(8,128)(2,1)}), bf16[16,32,256]{2,1,0:T(8,128)(2,1)S(1)}, u32[]{:S(2)}, u32[]{:S(2)}) %all-to-all-start) | async-done | bytes 262176 | tf_op jit(solution)/shard_map/all_to_all | solution.py:748
  75.3 0.7 convert_reduce_fusion
  (6 shorter events, 0.0 us)
Async XLA Ops:
  3.1 15.7 %collective-permute-start.1 = (bf16[8,16,896]{2,1,0:T(8,128)(2,1)}, bf16[8,16,896]{2,1,0:T(8,128)(2,1)S(1)}, u32[]{:S(2)}, u32[]{:S(2)}) collective-permute-start(bf16[8,16,896]{2,1,0:T(8,128)(2,1)} %get-tuple-element.38), channel_id=1, source_target_pairs={{0,15},{1,0},{2,1},{3,2},{4,3},{5,4},{6,5},{7,6},{8,7},{9,8},{10,9... | collective-permute-start | bytes 688136 | tf_op jit(solution)/shard_map/ppermute | solution.py:91
  8.6 10.9 %collective-permute-start = (bf16[16,16,896]{2,1,0:T(8,128)(2,1)}, bf16[16,16,896]{2,1,0:T(8,128)(2,1)}, u32[]{:S(2)}, u32[]{:S(2)}) collective-permute-start(bf16[16,16,896]{2,1,0:T(8,128)(2,1)} %get-tuple-element.37), channel_id=1, source_target_pairs={{0,16},{1,17},{2,18},{3,19},{4,20},{5,21},{6,22},{7,23},{8,24},{9,... | collective-permute-start | bytes 1376264 | tf_op jit(solution)/shard_map/ppermute | solution.py:91
  10.1 11.8 %copy-start.2 = (bf16[2,8,16,16,128]{4,3,2,1,0:T(8,128)(2,1)S(1)}, bf16[2,8,16,16,128]{4,3,2,1,0:T(8,128)(2,1)}, u32[]{:S(2)}) copy-start(bf16[2,8,16,16,128]{4,3,2,1,0:T(8,128)(2,1)} %vec.11) | copy-start | bytes 3145732
  17.5 1.4 %copy-start = (bf16[2,736,768]{2,1,0:T(8,128)(2,1)}, bf16[2,736,768]{2,1,0:T(8,128)(2,1)S(1)}, u32[]{:S(2)}) copy-start(bf16[2,736,768]{2,1,0:T(8,128)(2,1)S(1)} %get-tuple-element.42.refs_1_) | copy-start | bytes 6782980
  18.9 3.0 %copy-start.1 = (bf16[2,736,768]{2,1,0:T(8,128)(2,1)S(1)}, bf16[2,736,768]{2,1,0:T(8,128)(2,1)}, u32[]{:S(2)}) copy-start(bf16[2,736,768]{2,1,0:T(8,128)(2,1)} %copy-done) | copy-start | bytes 6782980
  18.9 5.5 %collective-permute-start.2 = (bf16[1,16,896]{2,1,0:T(8,128)(2,1)S(1)}, bf16[1,16,896]{2,1,0:T(8,128)(2,1)S(1)}, u32[]{:S(2)}, u32[]{:S(2)}) collective-permute-start(bf16[1,16,896]{2,1,0:T(8,128)(2,1)S(1)} %slice.4), channel_id=1, source_target_pairs={{0,16},{1,17},{2,18},{3,19},{4,20},{5,21},{6,22},{7,23},{8,24},{9,... | collective-permute-start | bytes 86024 | tf_op jit(solution)/shard_map/ppermute | solution.py:91
  26.3 8.6 %collective-permute-start.3 = (bf16[2,2,17,16,128]{4,3,2,1,0:T(8,128)(2,1)S(1)}, bf16[2,2,17,16,128]{4,3,2,1,0:T(8,128)(2,1)S(1)}, u32[]{:S(2)}, u32[]{:S(2)}) collective-permute-start(bf16[2,2,17,16,128]{4,3,2,1,0:T(8,128)(2,1)S(1)} %get-tuple-element.49), channel_id=1, source_target_pairs={{0,16},{1,17},{2,18},{3,19},{4,20},{5,21},{6,22},{7,23},{8,24},{9,... | collective-permute-start | bytes 835592 | tf_op jit(solution)/shard_map/ppermute | solution.py:91
  27.8 3.4 %collective-permute-start.4 = (bf16[2,9,16,128]{3,2,1,0:T(8,128)(2,1)S(1)}, bf16[2,9,16,128]{3,2,1,0:T(8,128)(2,1)S(1)}, u32[]{:S(2)}, u32[]{:S(2)}) collective-permute-start(bf16[2,9,16,128]{3,2,1,0:T(8,128)(2,1)S(1)} %get-tuple-element.50), channel_id=1, source_target_pairs={{0,1},{1,0},{2,3},{3,2},{4,5},{5,4},{6,7},{7,6},{8,9},{9,8},{10,11... | collective-permute-start | bytes 221192 | tf_op jit(solution)/shard_map/ppermute | solution.py:102
  27.8 6.5 %collective-permute-start.5 = (bf16[2,9,16,128]{3,2,1,0:T(8,128)(2,1)S(1)}, bf16[2,9,16,128]{3,2,1,0:T(8,128)(2,1)S(1)}, u32[]{:S(2)}, u32[]{:S(2)}) collective-permute-start(bf16[2,9,16,128]{3,2,1,0:T(8,128)(2,1)S(1)} %get-tuple-element.51), channel_id=1, source_target_pairs={{0,15},{1,2},{2,1},{3,4},{4,3},{5,6},{6,5},{7,8},{8,7},{9,10},{10,... | collective-permute-start | bytes 221192 | tf_op jit(solution)/shard_map/ppermute | solution.py:108
  34.3 3.9 %collective-permute-start.6 = (bf16[2,2,2,16,128]{4,3,2,1,0:T(8,128)(2,1)S(1)}, bf16[2,2,2,16,128]{4,3,2,1,0:T(8,128)(2,1)S(1)}, u32[]{:S(2)}, u32[]{:S(2)}) collective-permute-start(bf16[2,2,2,16,128]{4,3,2,1,0:T(8,128)(2,1)S(1)} %corner_pack.2), channel_id=1, source_target_pairs={{0,16},{1,17},{2,18},{3,19},{4,20},{5,21},{6,22},{7,23},{8,24},{9,... | collective-permute-start | bytes 98312 | tf_op jit(solution)/shard_map/ppermute | solution.py:91
  40.1 8.6 %collective-permute-start.7 = (bf16[2,2,17,16,128]{4,3,2,1,0:T(8,128)(2,1)S(1)}, bf16[2,2,17,16,128]{4,3,2,1,0:T(8,128)(2,1)S(1)}, u32[]{:S(2)}, u32[]{:S(2)}) collective-permute-start(bf16[2,2,17,16,128]{4,3,2,1,0:T(8,128)(2,1)S(1)} %get-tuple-element.54), channel_id=1, source_target_pairs={{0,16},{1,17},{2,18},{3,19},{4,20},{5,21},{6,22},{7,23},{8,24},{9,... | collective-permute-start | bytes 835592 | tf_op jit(solution)/shard_map/ppermute | solution.py:91
  41.2 6.0 %collective-permute-start.8 = (bf16[2,9,16,128]{3,2,1,0:T(8,128)(2,1)S(1)}, bf16[2,9,16,128]{3,2,1,0:T(8,128)(2,1)S(1)}, u32[]{:S(2)}, u32[]{:S(2)}) collective-permute-start(bf16[2,9,16,128]{3,2,1,0:T(8,128)(2,1)S(1)} %get-tuple-element.55), channel_id=1, source_target_pairs={{0,1},{1,0},{2,3},{3,2},{4,5},{5,4},{6,7},{7,6},{8,9},{9,8},{10,11... | collective-permute-start | bytes 221192 | tf_op jit(solution)/shard_map/ppermute | solution.py:102
  41.2 6.5 %collective-permute-start.9 = (bf16[2,9,16,128]{3,2,1,0:T(8,128)(2,1)S(1)}, bf16[2,9,16,128]{3,2,1,0:T(8,128)(2,1)S(1)}, u32[]{:S(2)}, u32[]{:S(2)}) collective-permute-start(bf16[2,9,16,128]{3,2,1,0:T(8,128)(2,1)S(1)} %get-tuple-element.56), channel_id=1, source_target_pairs={{0,15},{1,2},{2,1},{3,4},{4,3},{5,6},{6,5},{7,8},{8,7},{9,10},{10,... | collective-permute-start | bytes 221192 | tf_op jit(solution)/shard_map/ppermute | solution.py:108
  47.7 4.1 %collective-permute-start.10 = (bf16[2,2,2,16,128]{4,3,2,1,0:T(8,128)(2,1)S(1)}, bf16[2,2,2,16,128]{4,3,2,1,0:T(8,128)(2,1)S(1)}, u32[]{:S(2)}, u32[]{:S(2)}) collective-permute-start(bf16[2,2,2,16,128]{4,3,2,1,0:T(8,128)(2,1)S(1)} %corner_pack.3), channel_id=1, source_target_pairs={{0,16},{1,17},{2,18},{3,19},{4,20},{5,21},{6,22},{7,23},{8,24},{9,... | collective-permute-start | bytes 98312 | tf_op jit(solution)/shard_map/ppermute | solution.py:91
  53.7 5.1 %collective-permute-start.11 = (bf16[2,17,16,128]{3,2,1,0:T(8,128)(2,1)S(1)}, bf16[2,17,16,128]{3,2,1,0:T(8,128)(2,1)S(1)}, u32[]{:S(2)}, u32[]{:S(2)}) collective-permute-start(bf16[2,17,16,128]{3,2,1,0:T(8,128)(2,1)S(1)} %get-tuple-element.66), channel_id=1, source_target_pairs={{0,16},{1,17},{2,18},{3,19},{4,20},{5,21},{6,22},{7,23},{8,24},{9,... | collective-permute-start | bytes 417800 | tf_op jit(solution)/shard_map/ppermute | solution.py:91
  57.1 1.4 %collective-permute-start.12 = (bf16[256,256]{1,0:T(8,128)(2,1)S(1)}, bf16[256,256]{1,0:T(8,128)(2,1)S(1)}, u32[]{:S(2)}, u32[]{:S(2)}) collective-permute-start(bf16[256,256]{1,0:T(8,128)(2,1)S(1)} %get-tuple-element.68), channel_id=1, source_target_pairs={{0,1},{1,0},{2,3},{3,2},{4,5},{5,4},{6,7},{7,6},{8,9},{9,8},{10,11... | collective-permute-start | bytes 393224 | tf_op jit(solution)/shard_map/ppermute | solution.py:102
  59.5 15.8 %all-to-all-start = ((bf16[16,32,256]{2,1,0:T(8,128)(2,1)}), bf16[16,32,256]{2,1,0:T(8,128)(2,1)S(1)}, u32[]{:S(2)}, u32[]{:S(2)}) async-start(bf16[16,32,256]{2,1,0:T(8,128)(2,1)} %bitcast.3), calls=%async_computation | async-start | bytes 524288 | tf_op jit(solution)/shard_map/all_to_all | solution.py:748
  65.5 7.6 %collective-permute-start.13 = (bf16[2,8,16,128]{3,2,1,0:T(8,128)(2,1)S(1)}, bf16[2,8,16,128]{3,2,1,0:T(8,128)(2,1)S(1)}, u32[]{:S(2)}, u32[]{:S(2)}) collective-permute-start(bf16[2,8,16,128]{3,2,1,0:T(8,128)(2,1)S(1)} %get-tuple-element.70), channel_id=1, source_target_pairs={{0,1},{1,2},{2,3},{3,4},{4,5},{5,6},{6,7},{7,8},{8,9},{9,10},{10,1... | collective-permute-start | bytes 196616 | tf_op jit(solution)/shard_map/ppermute | solution.py:91

commit v9 on v7

--- a/solution.py
+++ b/solution.py
@@ -11,7 +11,7 @@
 LANES = 128
 TILE = 256
 SUB = 16
-VMEM_LIMIT = 12 * 1024 * 1024
+VMEM_LIMIT = 16 * 1024 * 1024
 
 center_shift = 1.2
 half_width = 2.0
@@ -109,7 +109,12 @@
     return send_near(near), far
 
 
+def cell_matrices(refs):
+    return [ref.at[at] for ref in refs for at in range(ref.shape[0])]
+
+
 def order_kernel(sz, conn_ref, matrix_ref, *out_refs):
+    matrices = cell_matrices(out_refs)
     for cell in range(sz.cells):
         x0, y0, z0 = sz.origins[cell]
         conn = conn_ref[cell : cell + 1, :].astype(f32)
@@ -138,12 +143,12 @@
             block = lax.dot_general(
                 half[r0:r1], pick[r0:], (((1,), (1,)), ((), ())), preferred_element_type=f32
             ).astype(bf16)
-            out_refs[cell][r0:r1, r0:] = block
+            matrices[cell][r0:r1, r0:] = block
             for c0, c1 in zip(cuts[:-1], cuts[1:]):
                 if c0 > r0:
                     mirror = block[:, c0 - r0 : c1 - r0].T
                     c1 = min(c1, sz.rows)
-                    out_refs[cell][c0:c1, r0:r1] = mirror[: c1 - c0]
+                    matrices[cell][c0:c1, r0:r1] = mirror[: c1 - c0]
 
 
 def field_row(inv, pot):
@@ -286,6 +291,7 @@
     flat = sz.gx * sz.gy * sz.gz
     u_flat = u_ref.reshape(sz.blocks * flat, width)
     last = sz.nodes // 8 * 8
+    matrices = cell_matrices(mat_refs)
     ready = set()
     for cell, (x0, y0, z0) in enumerate(sz.origins):
         slot = cell % 2
@@ -314,7 +320,7 @@
                     pl.ds(start, count, stride=sz.gz)
                 ]
         out_ref[cell] = jnp.dot(
-            mat_refs[cell][...], rhs_ref[slot].astype(bf16), preferred_element_type=f32
+            matrices[cell][...], rhs_ref[slot].astype(bf16), preferred_element_type=f32
         )
 
 
@@ -323,6 +329,7 @@
     flat = sz.gx * sz.gy * sz.gz
     acc_flat = acc_ref.reshape(sz.blocks * flat, width)
     small_ref[...] = jnp.zeros_like(small_ref)
+    matrices = cell_matrices(mat_refs)
     touched = set()
     for cell, (x0, y0, z0) in enumerate(sz.origins):
         z1 = z0 + sz.p
@@ -336,7 +343,7 @@
                 small_ref[rank * sz.p : (rank + 1) * sz.p, lanes] = value[b, z0:z1]
                 small_ref[last : last + 1, lanes] = value[b, wrap : wrap + 1]
         total = prod_ref[cell] + jnp.dot(
-            mat_refs[cell][:, : small_ref.shape[0]], small_ref[...].astype(bf16),
+            matrices[cell][:, : small_ref.shape[0]], small_ref[...].astype(bf16),
             preferred_element_type=f32,
         )
         tail_ref[cell, : sz.base] = total[: sz.base]
@@ -568,14 +575,8 @@
     return jax.ShapeDtypeStruct(shape, dtype)
 
 
-class Pinned:
-    def __init__(self, value):
-        self.value, self.shape, self.dtype = value, value.shape, value.dtype
-
-
 def call(kernel, name, flops, out_shape, scratch, operands, hbm=0, scalar_first=False, aliases=None,
          out_hbm=0):
-    pinned = [isinstance(s, Pinned) for s in out_shape]
     out_shape = [like(s.shape, s.dtype) for s in out_shape]
     size = sum(math.prod(s.shape) * jnp.dtype(s.dtype).itemsize for s in (*operands, *out_shape))
     whole = pl.BlockSpec(memory_space=pltpu.VMEM)
@@ -584,12 +585,10 @@
         specs[0] = pl.BlockSpec(memory_space=pltpu.SMEM)
     out_specs = [pl.BlockSpec(memory_space=pltpu.HBM)] * out_hbm + [whole] * (len(out_shape) - out_hbm)
     out_shape = [pltpu.HBM(s.shape, s.dtype) for s in out_shape[:out_hbm]] + out_shape[out_hbm:]
-    out_shape = [pltpu.VMEM(s.shape, s.dtype) if p else s for s, p in zip(out_shape, pinned)]
     operands = [pltpu.with_memory_space_constraint(a, pltpu.HBM) for a in operands[:hbm]] + list(
-        pltpu.with_memory_space_constraint(a.value, pltpu.VMEM) if isinstance(a, Pinned) else a
-        for a in operands[hbm:]
-    )
-    results = pl.pallas_call(
+        operands[hbm:]
+    )
+    return pl.pallas_call(
         kernel,
         in_specs=specs,
         out_specs=out_specs,
@@ -600,7 +599,6 @@
         cost_estimate=pl.CostEstimate(flops=flops, bytes_accessed=size, transcendentals=0),
         name=name,
     )(*operands)
-    return [Pinned(r) if p else r for r, p in zip(results, pinned)]
 
 
 def body(vectors, resident, inv_mass, potential, cell_matrix, connectivity):
@@ -614,7 +612,7 @@
     conn = connectivity.reshape(sz.cells, sz.nodes)
     to_x, to_y, cell_matrix, conn = call(
         functools.partial(pack_kernel, sz), "pack", 0,
-        [like((sz.ey, ez, sz.wide), bf16), like((sz.ex, ez, sz.wide), bf16), Pinned(cell_matrix), conn],
+        [like((sz.ey, ez, sz.wide), bf16), like((sz.ex, ez, sz.wide), bf16), cell_matrix, conn],
         [
             pltpu.VMEM((2, sz.ey, ez), f32), pltpu.VMEM((2, sz.ex, ez), f32),
             pltpu.SemaphoreType.DMA((8 + 2 * blocks,)),
@@ -624,9 +622,10 @@
     from_x = send(to_x, -1, 0)
     from_y = send(to_y, 0, -1)
 
+    halves = 2 if sz.cells % 2 == 0 else 1
     mats = call(
         functools.partial(order_kernel, sz), "order_cells", 4 * sz.cells * sz.depth**3,
-        [Pinned(like((sz.rows, sz.depth), bf16))] * sz.cells, [], [conn, cell_matrix],
+        [like((sz.cells // halves, sz.rows, sz.depth), bf16)] * halves, [], [conn, cell_matrix],
     )
     own_inv = jnp.broadcast_to(inv_mass[..., None], inv_mass.shape + (width,))
     own_pot = jnp.broadcast_to(potential[..., None], inv_mass.shape + (width,))
@@ -635,8 +634,8 @@
 
     grid = (blocks, sz.gx, sz.gy) + tile
     own = (blocks, sz.ex, sz.ey) + tile
-    products = Pinned(like((sz.cells, sz.rows, full), f32))
-    state_grid = Pinned(like(grid, f32))
+    products = like((sz.cells, sz.rows, full), f32)
+    state_grid = like(grid, f32)
     messages = [
         like((2, blocks, sz.gy) + tile, bf16),
         like((blocks, sz.gx) + tile, bf16),

time: 78 us -> 76.7 us (0.983)
  starting transfers between devices: 23.1 us -> 25.1 us
  local copies, waits for them, and re-layouts: 5.7 us -> 3.85 us
  waiting for transfers between devices: 17.2 us -> 15.9 us
    unnamed x14 -> x8, local copies, waits for them, and re-layouts: 3.28 us -> 1.41 us
    ppermute x2, waiting for transfers between devices: 6.11 us -> 4.83 us  [swap_y(): far = lax.ppermute(far, 'dy', far_pairs)]
    ppermute x2, starting transfers between devices: 4.9 us -> 6.18 us  [swap_y(): far = lax.ppermute(far, 'dy', far_pairs)]
where the time goes in v9:
time: 76.7 us; the launch traced here: 76.1 us
  Pallas kernels  29.8 us (39%)
  starting transfers between devices  25.1 us (33%)
  waiting for transfers between devices  15.9 us (21%)
  local copies, waits for them, and re-layouts  3.85 us (5%)
  between operations  0.8 us (1%)
    pallas_call x14, Pallas kernels, call(): pl.pallas_call(kernel, in_specs=specs, out_specs=out_specs, out_shape=out...  29.8 us
    ppermute x9, starting transfers between devices, send(): return lax.ppermute(value, ('dx', 'dy'), pairs)  12.9 us
    ppermute x9, waiting for transfers between devices, send(): return lax.ppermute(value, ('dx', 'dy'), pairs)  8.33 us
    ppermute x2, starting transfers between devices, swap_y(): far = lax.ppermute(far, 'dy', far_pairs)  6.18 us
    all_to_all x1, starting transfers between devices, body(): lax.all_to_all(pieces, ('dx', 'dy'), 0, 0, axis_index_groups=groups)  5.89 us
    ppermute x2, waiting for transfers between devices, swap_y(): far = lax.ppermute(far, 'dy', far_pairs)  4.83 us
  transfers between devices with their start and end apart: 15, of which 7 were waited for; matrix products, arithmetic and copies ran while one was open for 3% of the time, Pallas kernels for 27%

profile of v9, /device:TPU:0, one launch (start us, length us, event | category | flops | bytes accessed | tf_op | source)
XLA Modules:
  0.0 76.1 jit_solution(12862110843827827083)
XLA Ops:
  0.6 2.5 %pack.1 = (bf16[16,16,896]{2,1,0:T(8,128)(2,1)}, bf16[8,16,896]{2,1,0:T(8,128)(2,1)}, bf16[729,729]{1,0:T(8,128)(2,1)S(1)}, s32[4,729]{1,0:T(4,128)S(1)}) custom-call(bf16[2,8,16,16,128]{4,3,2,1,0:T(8,128)(2,1)} %vec.11, bf16[8,16,16,512]{3,2,1,0:T(8,128)(2,1)} %res_hbm.1, f32[8,16,16]{2,1,0:T(8,128)} %inv_hbm.1, f32[8,16,16]{2,1,0:T(8,128)} %pot_hbm.1, ...), custom_call_target="tpu_custom_call" | custom-call | bytes 5999332 | tf_op jit(solution)/shard_map/pack/pallas_call | solution.py:591
  3.1 5.5 %collective-permute-start.1 = (bf16[8,16,896]{2,1,0:T(8,128)(2,1)}, bf16[8,16,896]{2,1,0:T(8,128)(2,1)S(1)}, u32[]{:S(2)}, u32[]{:S(2)}) collective-permute-start(bf16[8,16,896]{2,1,0:T(8,128)(2,1)} %get-tuple-element.38), channel_id=1, source_target_pairs={{0,15},{1,0},{2,1},{3,2},{4,3},{5,4},{6,5},{7,6},{8,7},{9,8},{10,9... | collective-permute-start | bytes 688136 | tf_op jit(solution)/shard_map/ppermute | solution.py:91
  8.6 1.5 %collective-permute-start = (bf16[16,16,896]{2,1,0:T(8,128)(2,1)}, bf16[16,16,896]{2,1,0:T(8,128)(2,1)}, u32[]{:S(2)}, u32[]{:S(2)}) collective-permute-start(bf16[16,16,896]{2,1,0:T(8,128)(2,1)} %get-tuple-element.37), channel_id=1, source_target_pairs={{0,16},{1,17},{2,18},{3,19},{4,20},{5,21},{6,22},{7,23},{8,24},{9,... | collective-permute-start | bytes 1376264 | tf_op jit(solution)/shard_map/ppermute | solution.py:91
  10.1 7.4 %order_cells.1 = (bf16[2,736,768]{2,1,0:T(8,128)(2,1)S(1)}, bf16[2,736,768]{2,1,0:T(8,128)(2,1)S(1)}) custom-call(s32[4,729]{1,0:T(4,128)S(1)} %get-tuple-element.39.conn_ref, bf16[729,729]{1,0:T(8,128)(2,1)S(1)} %get-tuple-element.40.matrix_ref), custom_call_target="tpu_custom_call" | custom-call | flops 7247757312 | bytes 5596530 | tf_op jit(solution)/shard_map/order_cells/pallas_call | solution.py:591
  17.5 0.0 copy-start
  17.5 1.4 %copy-done = bf16[2,736,768]{2,1,0:T(8,128)(2,1)} copy-done((bf16[2,736,768]{2,1,0:T(8,128)(2,1)}, bf16[2,736,768]{2,1,0:T(8,128)(2,1)S(1)}, u32[]{:S(2)}) %copy-start) | copy-done | bytes 2261016
  18.9 0.0 collective-permute-done.1.from_y
  18.9 0.6 collective-permute-start.2
  19.5 0.0 collective-permute-done.from_x
  19.5 1.3 %broadcast_in_dim.4.own_inv = f32[8,16,16,128]{3,2,1,0:T(8,128)S(1)} broadcast(f32[8,16,16]{2,1,0:T(8,128)} %inv_hbm.1), dimensions={0,1,2} | broadcast | bytes 1056768 | tf_op jit(solution)/shard_map/broadcast_in_dim | solution.py:630
  20.8 1.2 %broadcast_in_dim.5.own_pot = f32[8,16,16,128]{3,2,1,0:T(8,128)S(1)} broadcast(f32[8,16,16]{2,1,0:T(8,128)} %pot_hbm.1), dimensions={0,1,2} | broadcast | bytes 1056768 | tf_op jit(solution)/shard_map/broadcast_in_dim | solution.py:631
  21.9 0.0 copy-done.2
  22.0 2.5 %first_main.1 = (f32[4,736,256]{2,1,0:T(8,128)S(1)}, f32[2,16,16,128]{3,2,1,0:T(8,128)S(1)}, f32[2,8,16,128]{3,2,1,0:T(8,128)S(1)}) custom-call(bf16[2,8,16,16,128]{4,3,2,1,0:T(8,128)(2,1)S(1)} %copy-done.2, bf16[16,16,896]{2,1,0:T(8,128)(2,1)} %collective-permute-done.from_x, bf16[8,16,896]{2,1,0:T(8,128)(2,1)S(1)} %collective-permute-done.1.from_y, ...), custom_call_target="tpu_custom_call" | custom-call | flops 1157627904 | bytes 11763712 | tf_op jit(solution)/shard_map/first_main/pallas_call | solution.py:591
  24.4 0.0 collective-permute-done.2.corner
  24.4 1.9 %first_corner.1 = (f32[2,9,17,16,128]{4,3,2,1,0:T(8,128)S(1)}, bf16[2,2,17,16,128]{4,3,2,1,0:T(8,128)(2,1)S(1)}, bf16[2,9,16,128]{3,2,1,0:T(8,128)(2,1)S(1)}, bf...) custom-call(s32[1]{0:T(128)} %bitcast.even_ref, ...), custom_call_target="tpu_custom_call" | custom-call | flops 192937984 | bytes 14757892 | tf_op jit(solution)/shard_map/first_corner/pallas_call | solution.py:591
  26.3 1.5 %collective-permute-start.3 = (bf16[2,2,17,16,128]{4,3,2,1,0:T(8,128)(2,1)S(1)}, bf16[2,2,17,16,128]{4,3,2,1,0:T(8,128)(2,1)S(1)}, u32[]{:S(2)}, u32[]{:S(2)}) collective-permute-start(bf16[2,2,17,16,128]{4,3,2,1,0:T(8,128)(2,1)S(1)} %get-tuple-element.49), channel_id=1, source_target_pairs={{0,16},{1,17},{2,18},{3,19},{4,20},{5,21},{6,22},{7,23},{8,24},{9,... | collective-permute-start | bytes 835592 | tf_op jit(solution)/shard_map/ppermute | solution.py:91
  27.8 0.0 collective-permute-start.4
  27.8 3.4 %collective-permute-start.5 = (bf16[2,9,16,128]{3,2,1,0:T(8,128)(2,1)S(1)}, bf16[2,9,16,128]{3,2,1,0:T(8,128)(2,1)S(1)}, u32[]{:S(2)}, u32[]{:S(2)}) collective-permute-start(bf16[2,9,16,128]{3,2,1,0:T(8,128)(2,1)S(1)} %get-tuple-element.51), channel_id=1, source_target_pairs={{0,15},{1,2},{2,1},{3,4},{4,3},{5,6},{6,5},{7,8},{8,7},{9,10},{10,... | collective-permute-start | bytes 221192 | tf_op jit(solution)/shard_map/ppermute | solution.py:108
  31.2 0.0 collective-permute-done.4.near.near_in
  31.2 3.1 %collective-permute-done.5.far.far_in = bf16[2,9,16,128]{3,2,1,0:T(8,128)(2,1)S(1)} collective-permute-done((bf16[2,9,16,128]{3,2,1,0:T(8,128)(2,1)S(1)}, bf16[2,9,16,128]{3,2,1,0:T(8,128)(2,1)S(1)}, u32[]{:S(2)}, u32[]{:S(2)}) %collective-permute-start.5) | collective-permute-done | bytes 73760 | tf_op jit(solution)/shard_map/ppermute | solution.py:108
  34.3 0.6 collective-permute-start.6
  34.9 0.0 collective-permute-done.3.face_in
  34.9 2.9 %second_main.1 = (f32[4,736,256]{2,1,0:T(8,128)S(1)}, f32[2,9,17,16,128]{4,3,2,1,0:T(8,128)S(1)}) custom-call(s32[1]{0:T(128)} %bitcast.even_ref, bf16[2,8,16,16,128]{4,3,2,1,0:T(8,128)(2,1)S(1)} %copy-done.2, bf16[16,16,896]{2,1,0:T(8,128)(2,1)} %collective-permute-done.from_x, bf16[8,16,896]{2,1,0:T(8,128)(2,1)S(1)} %collective-permute-done.1.from_y, ...), custom_call_target="tpu_custom_call" | custom-call | flops 1157627904 | bytes 17203204 | tf_op jit(solution)/shard_map/second_main/pallas_call | solution.py:591
  37.8 0.4 collective-permute-done.6.corner_in
  38.2 2.1 %second_corner.1 = (f32[2,9,17,16,128]{4,3,2,1,0:T(8,128)S(1)}, bf16[2,2,17,16,128]{4,3,2,1,0:T(8,128)(2,1)S(1)}, bf16[2,9,16,128]{3,2,1,0:T(8,128)(2,1)S(1)}, b...) custom-call(s32[1]{0:T(128)} %bitcast.even_ref, bf16[2,8,16,16,128]{4,3,2,1,0:T(8,128)(2,1)S(1)} %copy-done.2, ...), custom_call_target="tpu_custom_call" | custom-call | flops 192937984 | bytes 17760260 | tf_op jit(solution)/shard_map/second_corner/pallas_call | solution.py:591
  40.3 1.1 %collective-permute-start.7 = (bf16[2,2,17,16,128]{4,3,2,1,0:T(8,128)(2,1)S(1)}, bf16[2,2,17,16,128]{4,3,2,1,0:T(8,128)(2,1)S(1)}, u32[]{:S(2)}, u32[]{:S(2)}) collective-permute-start(bf16[2,2,17,16,128]{4,3,2,1,0:T(8,128)(2,1)S(1)} %get-tuple-element.54), channel_id=1, source_target_pairs={{0,16},{1,17},{2,18},{3,19},{4,20},{5,21},{6,22},{7,23},{8,24},{9,... | collective-permute-start | bytes 835592 | tf_op jit(solution)/shard_map/ppermute | solution.py:91
  41.4 0.0 collective-permute-start.8
  41.4 2.8 %collective-permute-start.9 = (bf16[2,9,16,128]{3,2,1,0:T(8,128)(2,1)S(1)}, bf16[2,9,16,128]{3,2,1,0:T(8,128)(2,1)S(1)}, u32[]{:S(2)}, u32[]{:S(2)}) collective-permute-start(bf16[2,9,16,128]{3,2,1,0:T(8,128)(2,1)S(1)} %get-tuple-element.56), channel_id=1, source_target_pairs={{0,15},{1,2},{2,1},{3,4},{4,3},{5,6},{6,5},{7,8},{8,7},{9,10},{10,... | collective-permute-start | bytes 221192 | tf_op jit(solution)/shard_map/ppermute | solution.py:108
  44.2 1.9 %turn_residents.1.turned = bf16[2,256,2560]{2,1,0:T(8,128)(2,1)S(1)} custom-call(bf16[2048,512]{1,0:T(8,128)(2,1)S(1)} %bitcast.4, bf16[16,16,896]{2,1,0:T(8,128)(2,1)} %collective-permute-done.from_x, bf16[8,16,896]{2,1,0:T(8,128)(2,1)S(1)} %collective-permute-done.1.from_y, bf16[1,16,896]{2,1,0:T(8,128)(2,1)S(1)} %collective-permute-done.2.corner), custom_call_target="tpu_custom_call" | custom-call | flops 578813952 | bytes 5435392 | tf_op jit(solution)/shard_map/turn_residents/pallas_call | solution.py:591
  46.1 0.0 collective-permute-done.8.near.near_in
  46.1 1.7 %collective-permute-done.9.far.far_in = bf16[2,9,16,128]{3,2,1,0:T(8,128)(2,1)S(1)} collective-permute-done((bf16[2,9,16,128]{3,2,1,0:T(8,128)(2,1)S(1)}, bf16[2,9,16,128]{3,2,1,0:T(8,128)(2,1)S(1)}, u32[]{:S(2)}, u32[]{:S(2)}) %collective-permute-start.9) | collective-permute-done | bytes 73760 | tf_op jit(solution)/shard_map/ppermute | solution.py:108
  47.9 1.0 %collective-permute-start.10 = (bf16[2,2,2,16,128]{4,3,2,1,0:T(8,128)(2,1)S(1)}, bf16[2,2,2,16,128]{4,3,2,1,0:T(8,128)(2,1)S(1)}, u32[]{:S(2)}, u32[]{:S(2)}) collective-permute-start(bf16[2,2,2,16,128]{4,3,2,1,0:T(8,128)(2,1)S(1)} %corner_pack.3), channel_id=1, source_target_pairs={{0,16},{1,17},{2,18},{3,19},{4,20},{5,21},{6,22},{7,23},{8,24},{9,... | collective-permute-start | bytes 98312 | tf_op jit(solution)/shard_map/ppermute | solution.py:91
  48.8 0.0 collective-permute-done.7.face_in
  48.8 3.1 %third_main.1 = (f32[4,736,256]{2,1,0:T(8,128)S(1)}, f32[2,9,17,16,128]{4,3,2,1,0:T(8,128)S(1)}) custom-call(s32[1]{0:T(128)} %bitcast.even_ref, bf16[2,8,16,16,128]{4,3,2,1,0:T(8,128)(2,1)S(1)} %copy-done.2, bf16[16,16,896]{2,1,0:T(8,128)(2,1)} %collective-permute-done.from_x, bf16[8,16,896]{2,1,0:T(8,128)(2,1)S(1)} %collective-permute-done.1.from_y, ...), custom_call_target="tpu_custom_call" | custom-call | flops 1157627904 | bytes 19709956 | tf_op jit(solution)/shard_map/third_main/pallas_call | solution.py:591
  52.0 0.0 collective-permute-done.10.corner_in
  52.0 1.9 %third_corner.1 = (f32[2,9,17,16,128]{4,3,2,1,0:T(8,128)S(1)}, f32[4,2,16,128]{3,2,1,0:T(8,128)S(1)}, bf16[2,17,16,128]{3,2,1,0:T(8,128)(2,1)S(1)}) custom-call(s32[1]{0:T(128)} %bitcast.even_ref, bf16[2,8,16,16,128]{4,3,2,1,0:T(8,128)(2,1)S(1)} %copy-done.2, bf16[16,16,896]{2,1,0:T(8,128)(2,1)} %collective-permute-done.from_x, ...), custom_call_target="tpu_custom_call" | custom-call | flops 192937984 | bytes 17539076 | tf_op jit(solution)/shard_map/third_corner/pallas_call | solution.py:591
  53.9 1.1 %collective-permute-start.11 = (bf16[2,17,16,128]{3,2,1,0:T(8,128)(2,1)S(1)}, bf16[2,17,16,128]{3,2,1,0:T(8,128)(2,1)S(1)}, u32[]{:S(2)}, u32[]{:S(2)}) collective-permute-start(bf16[2,17,16,128]{3,2,1,0:T(8,128)(2,1)S(1)} %get-tuple-element.66), channel_id=1, source_target_pairs={{0,16},{1,17},{2,18},{3,19},{4,20},{5,21},{6,22},{7,23},{8,24},{9,... | collective-permute-start | bytes 417800 | tf_op jit(solution)/shard_map/ppermute | solution.py:91
  55.0 2.3 %third_end.1 = (f32[2,8,16,16,128]{4,3,2,1,0:T(8,128)}, f32[2,16,16,128]{3,2,1,0:T(8,128)S(1)}, f32[2,7,16,128]{3,2,1,0:T(8,128)S(1)}, f32[2,8,16,128]{3,2,1,0:T...) custom-call(s32[1]{0:T(128)} %bitcast.even_ref, f32[8,16,16,128]{3,2,1,0:T(8,128)S(1)} %broadcast_in_dim.4.own_inv, ...), custom_call_target="tpu_custom_call" | custom-call | flops 671088640 | bytes 15777796 | tf_op jit(solution)/shard_map/third_end/pallas_call | solution.py:591
  57.2 0.1 collective-permute-start.12
  57.3 1.3 %collective-permute-done.12.taken = bf16[256,256]{1,0:T(8,128)(2,1)S(1)} collective-permute-done((bf16[256,256]{1,0:T(8,128)(2,1)S(1)}, bf16[256,256]{1,0:T(8,128)(2,1)S(1)}, u32[]{:S(2)}, u32[]{:S(2)}) %collective-permute-start.12) | collective-permute-done | bytes 131104 | tf_op jit(solution)/shard_map/ppermute | solution.py:102
  58.7 0.3 collective-permute-done.11.face
  59.0 0.7 ready.1
  59.7 5.9 %all-to-all-start = ((bf16[16,32,256]{2,1,0:T(8,128)(2,1)}), bf16[16,32,256]{2,1,0:T(8,128)(2,1)S(1)}, u32[]{:S(2)}, u32[]{:S(2)}) async-start(bf16[16,32,256]{2,1,0:T(8,128)(2,1)} %bitcast.3), calls=%async_computation | async-start | bytes 524288 | tf_op jit(solution)/shard_map/all_to_all | solution.py:728
  65.6 0.1 collective-permute-start.13
  65.7 7.6 %collective-permute-done.13.side = bf16[2,8,16,128]{3,2,1,0:T(8,128)(2,1)S(1)} collective-permute-done((bf16[2,8,16,128]{3,2,1,0:T(8,128)(2,1)S(1)}, bf16[2,8,16,128]{3,2,1,0:T(8,128)(2,1)S(1)}, u32[]{:S(2)}, u32[]{:S(2)}) %collective-permute-start.13) | collective-permute-done | bytes 65568 | tf_op jit(solution)/shard_map/ppermute | solution.py:91
  73.2 0.8 %last.1 = f32[2,8,16,16,128]{4,3,2,1,0:T(8,128)} custom-call(f32[2,8,16,16,128]{4,3,2,1,0:T(8,128)} %get-tuple-element.63.old_hbm, f32[2,16,16,128]{3,2,1,0:T(8,128)S(1)} %get-tuple-element.64.edge_x, f32[2,7,16,128]{3,2,1,0:T(8,128)S(1)} %get-tuple-element.65.edge_y, ...), custom_call_target="tpu_custom_call", output_to_operand_aliasing={{}: (0, {})} | custom-call | bytes 4775936 | tf_op jit(solution)/shard_map/last/pallas_call | solution.py:591
  74.0 1.4 %all-to-all-done = bf16[16,32,256]{2,1,0:T(8,128)(2,1)S(1)} async-done(((bf16[16,32,256]{2,1,0:T(8,128)(2,1)}), bf16[16,32,256]{2,1,0:T(8,128)(2,1)S(1)}, u32[]{:S(2)}, u32[]{:S(2)}) %all-to-all-start) | async-done | bytes 262176 | tf_op jit(solution)/shard_map/all_to_all | solution.py:728
  75.5 0.7 convert_reduce_fusion
  (8 shorter events, 0.0 us)
Async XLA Ops:
  3.1 15.8 %collective-permute-start.1 = (bf16[8,16,896]{2,1,0:T(8,128)(2,1)}, bf16[8,16,896]{2,1,0:T(8,128)(2,1)S(1)}, u32[]{:S(2)}, u32[]{:S(2)}) collective-permute-start(bf16[8,16,896]{2,1,0:T(8,128)(2,1)} %get-tuple-element.38), channel_id=1, source_target_pairs={{0,15},{1,0},{2,1},{3,2},{4,3},{5,4},{6,5},{7,6},{8,7},{9,8},{10,9... | collective-permute-start | bytes 688136 | tf_op jit(solution)/shard_map/ppermute | solution.py:91
  8.6 10.9 %collective-permute-start = (bf16[16,16,896]{2,1,0:T(8,128)(2,1)}, bf16[16,16,896]{2,1,0:T(8,128)(2,1)}, u32[]{:S(2)}, u32[]{:S(2)}) collective-permute-start(bf16[16,16,896]{2,1,0:T(8,128)(2,1)} %get-tuple-element.37), channel_id=1, source_target_pairs={{0,16},{1,17},{2,18},{3,19},{4,20},{5,21},{6,22},{7,23},{8,24},{9,... | collective-permute-start | bytes 1376264 | tf_op jit(solution)/shard_map/ppermute | solution.py:91
  10.1 11.8 %copy-start.2 = (bf16[2,8,16,16,128]{4,3,2,1,0:T(8,128)(2,1)S(1)}, bf16[2,8,16,16,128]{4,3,2,1,0:T(8,128)(2,1)}, u32[]{:S(2)}) copy-start(bf16[2,8,16,16,128]{4,3,2,1,0:T(8,128)(2,1)} %vec.11) | copy-start | bytes 3145732
  17.5 1.4 %copy-start = (bf16[2,736,768]{2,1,0:T(8,128)(2,1)}, bf16[2,736,768]{2,1,0:T(8,128)(2,1)S(1)}, u32[]{:S(2)}) copy-start(bf16[2,736,768]{2,1,0:T(8,128)(2,1)S(1)} %get-tuple-element.42.refs_1_) | copy-start | bytes 6782980
  18.9 3.0 %copy-start.1 = (bf16[2,736,768]{2,1,0:T(8,128)(2,1)S(1)}, bf16[2,736,768]{2,1,0:T(8,128)(2,1)}, u32[]{:S(2)}) copy-start(bf16[2,736,768]{2,1,0:T(8,128)(2,1)} %copy-done) | copy-start | bytes 6782980
  18.9 5.5 %collective-permute-start.2 = (bf16[1,16,896]{2,1,0:T(8,128)(2,1)S(1)}, bf16[1,16,896]{2,1,0:T(8,128)(2,1)S(1)}, u32[]{:S(2)}, u32[]{:S(2)}) collective-permute-start(bf16[1,16,896]{2,1,0:T(8,128)(2,1)S(1)} %slice.4), channel_id=1, source_target_pairs={{0,16},{1,17},{2,18},{3,19},{4,20},{5,21},{6,22},{7,23},{8,24},{9,... | collective-permute-start | bytes 86024 | tf_op jit(solution)/shard_map/ppermute | solution.py:91
  26.3 8.6 %collective-permute-start.3 = (bf16[2,2,17,16,128]{4,3,2,1,0:T(8,128)(2,1)S(1)}, bf16[2,2,17,16,128]{4,3,2,1,0:T(8,128)(2,1)S(1)}, u32[]{:S(2)}, u32[]{:S(2)}) collective-permute-start(bf16[2,2,17,16,128]{4,3,2,1,0:T(8,128)(2,1)S(1)} %get-tuple-element.49), channel_id=1, source_target_pairs={{0,16},{1,17},{2,18},{3,19},{4,20},{5,21},{6,22},{7,23},{8,24},{9,... | collective-permute-start | bytes 835592 | tf_op jit(solution)/shard_map/ppermute | solution.py:91
  27.8 3.4 %collective-permute-start.4 = (bf16[2,9,16,128]{3,2,1,0:T(8,128)(2,1)S(1)}, bf16[2,9,16,128]{3,2,1,0:T(8,128)(2,1)S(1)}, u32[]{:S(2)}, u32[]{:S(2)}) collective-permute-start(bf16[2,9,16,128]{3,2,1,0:T(8,128)(2,1)S(1)} %get-tuple-element.50), channel_id=1, source_target_pairs={{0,1},{1,0},{2,3},{3,2},{4,5},{5,4},{6,7},{7,6},{8,9},{9,8},{10,11... | collective-permute-start | bytes 221192 | tf_op jit(solution)/shard_map/ppermute | solution.py:102
  27.8 6.5 %collective-permute-start.5 = (bf16[2,9,16,128]{3,2,1,0:T(8,128)(2,1)S(1)}, bf16[2,9,16,128]{3,2,1,0:T(8,128)(2,1)S(1)}, u32[]{:S(2)}, u32[]{:S(2)}) collective-permute-start(bf16[2,9,16,128]{3,2,1,0:T(8,128)(2,1)S(1)} %get-tuple-element.51), channel_id=1, source_target_pairs={{0,15},{1,2},{2,1},{3,4},{4,3},{5,6},{6,5},{7,8},{8,7},{9,10},{10,... | collective-permute-start | bytes 221192 | tf_op jit(solution)/shard_map/ppermute | solution.py:108
  34.3 3.9 %collective-permute-start.6 = (bf16[2,2,2,16,128]{4,3,2,1,0:T(8,128)(2,1)S(1)}, bf16[2,2,2,16,128]{4,3,2,1,0:T(8,128)(2,1)S(1)}, u32[]{:S(2)}, u32[]{:S(2)}) collective-permute-start(bf16[2,2,2,16,128]{4,3,2,1,0:T(8,128)(2,1)S(1)} %corner_pack.2), channel_id=1, source_target_pairs={{0,16},{1,17},{2,18},{3,19},{4,20},{5,21},{6,22},{7,23},{8,24},{9,... | collective-permute-start | bytes 98312 | tf_op jit(solution)/shard_map/ppermute | solution.py:91
  38.2 6.0 %copy-start.3 = (bf16[8,16,16,512]{3,2,1,0:T(8,128)(2,1)S(1)}, bf16[8,16,16,512]{3,2,1,0:T(8,128)(2,1)}, u32[]{:S(2)}) copy-start(bf16[8,16,16,512]{3,2,1,0:T(8,128)(2,1)} %res_hbm.1) | copy-start | bytes 6291460
  40.3 8.6 %collective-permute-start.7 = (bf16[2,2,17,16,128]{4,3,2,1,0:T(8,128)(2,1)S(1)}, bf16[2,2,17,16,128]{4,3,2,1,0:T(8,128)(2,1)S(1)}, u32[]{:S(2)}, u32[]{:S(2)}) collective-permute-start(bf16[2,2,17,16,128]{4,3,2,1,0:T(8,128)(2,1)S(1)} %get-tuple-element.54), channel_id=1, source_target_pairs={{0,16},{1,17},{2,18},{3,19},{4,20},{5,21},{6,22},{7,23},{8,24},{9,... | collective-permute-start | bytes 835592 | tf_op jit(solution)/shard_map/ppermute | solution.py:91
  41.4 4.7 %collective-permute-start.8 = (bf16[2,9,16,128]{3,2,1,0:T(8,128)(2,1)S(1)}, bf16[2,9,16,128]{3,2,1,0:T(8,128)(2,1)S(1)}, u32[]{:S(2)}, u32[]{:S(2)}) collective-permute-start(bf16[2,9,16,128]{3,2,1,0:T(8,128)(2,1)S(1)} %get-tuple-element.55), channel_id=1, source_target_pairs={{0,1},{1,0},{2,3},{3,2},{4,5},{5,4},{6,7},{7,6},{8,9},{9,8},{10,11... | collective-permute-start | bytes 221192 | tf_op jit(solution)/shard_map/ppermute | solution.py:102
  41.4 6.5 %collective-permute-start.9 = (bf16[2,9,16,128]{3,2,1,0:T(8,128)(2,1)S(1)}, bf16[2,9,16,128]{3,2,1,0:T(8,128)(2,1)S(1)}, u32[]{:S(2)}, u32[]{:S(2)}) collective-permute-start(bf16[2,9,16,128]{3,2,1,0:T(8,128)(2,1)S(1)} %get-tuple-element.56), channel_id=1, source_target_pairs={{0,15},{1,2},{2,1},{3,4},{4,3},{5,6},{6,5},{7,8},{8,7},{9,10},{10,... | collective-permute-start | bytes 221192 | tf_op jit(solution)/shard_map/ppermute | solution.py:108
  47.9 4.1 %collective-permute-start.10 = (bf16[2,2,2,16,128]{4,3,2,1,0:T(8,128)(2,1)S(1)}, bf16[2,2,2,16,128]{4,3,2,1,0:T(8,128)(2,1)S(1)}, u32[]{:S(2)}, u32[]{:S(2)}) collective-permute-start(bf16[2,2,2,16,128]{4,3,2,1,0:T(8,128)(2,1)S(1)} %corner_pack.3), channel_id=1, source_target_pairs={{0,16},{1,17},{2,18},{3,19},{4,20},{5,21},{6,22},{7,23},{8,24},{9,... | collective-permute-start | bytes 98312 | tf_op jit(solution)/shard_map/ppermute | solution.py:91
  53.9 5.1 %collective-permute-start.11 = (bf16[2,17,16,128]{3,2,1,0:T(8,128)(2,1)S(1)}, bf16[2,17,16,128]{3,2,1,0:T(8,128)(2,1)S(1)}, u32[]{:S(2)}, u32[]{:S(2)}) collective-permute-start(bf16[2,17,16,128]{3,2,1,0:T(8,128)(2,1)S(1)} %get-tuple-element.66), channel_id=1, source_target_pairs={{0,16},{1,17},{2,18},{3,19},{4,20},{5,21},{6,22},{7,23},{8,24},{9,... | collective-permute-start | bytes 417800 | tf_op jit(solution)/shard_map/ppermute | solution.py:91
  57.2 1.4 %collective-permute-start.12 = (bf16[256,256]{1,0:T(8,128)(2,1)S(1)}, bf16[256,256]{1,0:T(8,128)(2,1)S(1)}, u32[]{:S(2)}, u32[]{:S(2)}) collective-permute-start(bf16[256,256]{1,0:T(8,128)(2,1)S(1)} %get-tuple-element.68), channel_id=1, source_target_pairs={{0,1},{1,0},{2,3},{3,2},{4,5},{5,4},{6,7},{7,6},{8,9},{9,8},{10,11... | collective-permute-start | bytes 393224 | tf_op jit(solution)/shard_map/ppermute | solution.py:102
  59.7 15.7 %all-to-all-start = ((bf16[16,32,256]{2,1,0:T(8,128)(2,1)}), bf16[16,32,256]{2,1,0:T(8,128)(2,1)S(1)}, u32[]{:S(2)}, u32[]{:S(2)}) async-start(bf16[16,32,256]{2,1,0:T(8,128)(2,1)} %bitcast.3), calls=%async_computation | async-start | bytes 524288 | tf_op jit(solution)/shard_map/all_to_all | solution.py:728
  65.6 7.6 %collective-permute-start.13 = (bf16[2,8,16,128]{3,2,1,0:T(8,128)(2,1)S(1)}, bf16[2,8,16,128]{3,2,1,0:T(8,128)(2,1)S(1)}, u32[]{:S(2)}, u32[]{:S(2)}) collective-permute-start(bf16[2,8,16,128]{3,2,1,0:T(8,128)(2,1)S(1)} %get-tuple-element.70), channel_id=1, source_target_pairs={{0,1},{1,2},{2,3},{3,4},{4,5},{5,6},{6,7},{7,8},{8,9},{9,10},{10,1... | collective-permute-start | bytes 196616 | tf_op jit(solution)/shard_map/ppermute | solution.py:91

commit v10 on v6

--- a/solution.py
+++ b/solution.py
@@ -109,8 +109,9 @@
     return send_near(near), far
 
 
-def order_kernel(sz, conn_ref, matrix_ref, out_ref):
-    for cell in range(sz.cells):
+def order_kernel(sz, first, conn_ref, matrix_ref, out_ref):
+    for slot in range(out_ref.shape[0]):
+        cell = first + slot
         x0, y0, z0 = sz.origins[cell]
         conn = conn_ref[cell : cell + 1, :].astype(f32)
         li = jnp.floor((conn + 0.5) * (1.0 / (sz.gy * sz.gz)))
@@ -138,12 +139,12 @@
             block = lax.dot_general(
                 half[r0:r1], pick[r0:], (((1,), (1,)), ((), ())), preferred_element_type=f32
             ).astype(bf16)
-            out_ref[cell, r0:r1, r0:] = block
+            out_ref[slot, r0:r1, r0:] = block
             for c0, c1 in zip(cuts[:-1], cuts[1:]):
                 if c0 > r0:
                     mirror = block[:, c0 - r0 : c1 - r0].T
                     c1 = min(c1, sz.rows)
-                    out_ref[cell, c0:c1, r0:r1] = mirror[: c1 - c0]
+                    out_ref[slot, c0:c1, r0:r1] = mirror[: c1 - c0]
 
 
 def field_row(inv, pot):
@@ -470,8 +471,8 @@
                  last_x, last_field, acc_in, face_in, near_in, far_in, corner_in, prod_ref, y_ref,
                  y_corner, new_ref, turned, *refs):
     mats = refs[:n_mat]
-    out_hbm, edge_x, edge_y, face, side, corner, give, keep = refs[n_mat : n_mat + 8]
-    part_ref, sem, acc_ref, rows_ref, small_ref, tail_ref = refs[n_mat + 8 :]
+    out_hbm, edge_x, edge_y, face, side, give, keep = refs[n_mat : n_mat + 7]
+    part_ref, sem, acc_ref, rows_ref, small_ref, tail_ref = refs[n_mat + 7 :]
     nodes = Nodes(sz, vec, from_x, from_y, own_inv, own_pot, ghost_x, ghost_y, last_field)
     sums = Sums(sz, even_ref[0] == 0, acc_in, face_in, near_in, far_in, corner_in)
     u_corner, new_corner = [], []
@@ -494,15 +495,11 @@
             if i == sz.ex or j == sz.ey:
                 value = gain * (inv * acc)
                 rounded = value.astype(bf16)
-                if j < sz.ey:
-                    put_row(sz.own_edges + j, rounded)
+                if i == sz.ex:
                     face[:, j] = rounded
                 else:
-                    put_row(sz.own_edges + sz.ey + i, rounded)
-                    if i < sz.ex:
-                        side[:, i] = value
-                    else:
-                        corner[...] = rounded
+                    side[:, i] = value
+                put_row(sz.own_edges + (j if j < sz.ey else sz.ey + i), rounded)
                 continue
             at = sz.corner(i, j)
             old = y_ref[:, i, j] if at is None else y_corner[at]
@@ -529,12 +526,20 @@
         copy.wait()
 
 
-def last_side_kernel(sz, side_ref, corner_ref, face_in, out_ref, face_out):
-    del face_in, face_out
+def pieces_kernel(keep, taken, pieces):
+    rows = pieces.shape[2]
+    for at in range(pieces.shape[1]):
+        span = slice(at * rows, (at + 1) * rows)
+        value = (keep[span] + taken[span].astype(f32)).astype(pieces.dtype)
+        for copy in range(pieces.shape[0]):
+            pieces[copy, at] = value
+
+
+def last_side_kernel(sz, side_ref, face, out_ref):
     for i in range(sz.ex):
         value = side_ref[:, i]
         if i == 0:
-            value = value + corner_ref[...].astype(f32)
+            value = value + face[:, sz.ey].astype(f32)
         out_ref[:, i] = value.astype(out_ref.dtype)
 
 
@@ -561,14 +566,8 @@
     return jax.ShapeDtypeStruct(shape, dtype)
 
 
-class Pinned:
-    def __init__(self, value):
-        self.value, self.shape, self.dtype = value, value.shape, value.dtype
-
-
 def call(kernel, name, flops, out_shape, scratch, operands, hbm=0, scalar_first=False, aliases=None,
          out_hbm=0):
-    pinned = [isinstance(s, Pinned) for s in out_shape]
     out_shape = [like(s.shape, s.dtype) for s in out_shape]
     size = sum(math.prod(s.shape) * jnp.dtype(s.dtype).itemsize for s in (*operands, *out_shape))
     whole = pl.BlockSpec(memory_space=pltpu.VMEM)
@@ -577,12 +576,10 @@
         specs[0] = pl.BlockSpec(memory_space=pltpu.SMEM)
     out_specs = [pl.BlockSpec(memory_space=pltpu.HBM)] * out_hbm + [whole] * (len(out_shape) - out_hbm)
     out_shape = [pltpu.HBM(s.shape, s.dtype) for s in out_shape[:out_hbm]] + out_shape[out_hbm:]
-    out_shape = [pltpu.VMEM(s.shape, s.dtype) if p else s for s, p in zip(out_shape, pinned)]
     operands = [pltpu.with_memory_space_constraint(a, pltpu.HBM) for a in operands[:hbm]] + list(
-        pltpu.with_memory_space_constraint(a.value, pltpu.VMEM) if isinstance(a, Pinned) else a
-        for a in operands[hbm:]
-    )
-    results = pl.pallas_call(
+        operands[hbm:]
+    )
+    return pl.pallas_call(
         kernel,
         in_specs=specs,
         out_specs=out_specs,
@@ -593,7 +590,6 @@
         cost_estimate=pl.CostEstimate(flops=flops, bytes_accessed=size, transcendentals=0),
         name=name,
     )(*operands)
-    return [Pinned(r) if p else r for r, p in zip(results, pinned)]
 
 
 def body(vectors, resident, inv_mass, potential, cell_matrix, connectivity):
@@ -605,9 +601,9 @@
     tile = (ez, width)
 
     conn = connectivity.reshape(sz.cells, sz.nodes)
-    to_x, to_y, cell_matrix, conn = call(
+    to_x, to_y, loaded, conn = call(
         functools.partial(pack_kernel, sz), "pack", 0,
-        [like((sz.ey, ez, sz.wide), bf16), like((sz.ex, ez, sz.wide), bf16), Pinned(cell_matrix), conn],
+        [like((sz.ey, ez, sz.wide), bf16), like((sz.ex, ez, sz.wide), bf16), cell_matrix, conn],
         [
             pltpu.VMEM((2, sz.ey, ez), f32), pltpu.VMEM((2, sz.ex, ez), f32),
             pltpu.SemaphoreType.DMA((8 + 2 * blocks,)),
@@ -617,10 +613,14 @@
     from_x = send(to_x, -1, 0)
     from_y = send(to_y, 0, -1)
 
-    mats = call(
-        functools.partial(order_kernel, sz), "order_cells", 4 * sz.cells * sz.depth**3,
-        [Pinned(like((sz.cells, sz.rows, sz.depth), bf16))], [], [conn, cell_matrix],
-    )
+    halves = 2 if sz.cells % 2 == 0 else 1
+    step = sz.cells // halves
+    mats = []
+    for at in range(0, sz.cells, step):
+        mats += call(
+            functools.partial(order_kernel, sz, at), "order_cells", 4 * step * sz.depth**3,
+            [like((step, sz.rows, sz.depth), bf16)], [], [conn, loaded if at == 0 else cell_matrix],
+        )
     own_inv = jnp.broadcast_to(inv_mass[..., None], inv_mass.shape + (width,))
     own_pot = jnp.broadcast_to(potential[..., None], inv_mass.shape + (width,))
     parity = jnp.reshape(lax.axis_index("dy") % 2, (1,)).astype(jnp.int32)
@@ -628,8 +628,8 @@
 
     grid = (blocks, sz.gx, sz.gy) + tile
     own = (blocks, sz.ex, sz.ey) + tile
-    products = Pinned(like((sz.cells, sz.rows, full), f32))
-    state_grid = Pinned(like(grid, f32))
+    products = like((sz.cells, sz.rows, full), f32)
+    state_grid = like(grid, f32)
     messages = [
         like((2, blocks, sz.gy) + tile, bf16),
         like((blocks, sz.gx) + tile, bf16),
@@ -690,31 +690,33 @@
         [products, state_grid], main_scratch,
         [parity, *state, acc, *got, y1, *mats], scalar_first=True,
     )
-    filtered, edge_x, edge_y, face, side, corner, give, keep = call(
+    filtered, edge_x, edge_y, face, side, give, keep = call(
         functools.partial(third_corner, sz, n_mat, norm_scale), "third_corner",
         small_flops + 2 * res_count * sz.edges * ez * full,
         [
             like(own, f32), like((blocks, sz.ey) + tile, f32), like((blocks, sz.ex - 1) + tile, f32),
-            like((blocks, sz.ey) + tile, bf16), like((blocks, sz.ex) + tile, f32),
-            like(sz.edge, bf16), like((res_count // 2, full), bf16), like((res_count // 2, full), f32),
+            like((blocks, sz.gy) + tile, bf16), like((blocks, sz.ex) + tile, f32),
+            like((res_count // 2, full), bf16), like((res_count // 2, full), f32),
         ],
         [pltpu.VMEM(own, f32), pltpu.SemaphoreType.DMA((sz.ex,)), pltpu.VMEM(grid, f32), pltpu.VMEM((sz.edges, ez, full), bf16)] + corner_scratch,
         [parity, *state, *ends, acc, *got, corner, prod, y1, y1_corner, y2, turned, *mats],
         scalar_first=True, out_hbm=1,
     )
 
-    mine = (keep + send_near(give).astype(f32)).astype(bf16).reshape(1, ny // 2, -1, full)
-    mine = jnp.broadcast_to(mine, (nx,) + mine.shape[1:]).reshape(nx * ny // 2, -1, full)
+    (pieces,) = call(
+        pieces_kernel, "pieces", 0, [like((nx, ny // 2, res_count // ny, full), bf16)], [],
+        [keep, send_near(give)],
+    )
+    pieces = pieces.reshape(nx * ny // 2, -1, full)
     groups = [[a * ny + b for a in range(nx) for b in range(c, ny, 2)] for c in range(2)]
-    pieces = lax.all_to_all(mine, ("dx", "dy"), 0, 0, axis_index_groups=groups)
+    pieces = lax.all_to_all(pieces, ("dx", "dy"), 0, 0, axis_index_groups=groups)
     margin = jnp.sum(pieces.astype(f32), axis=0)
 
-    corner = send(corner, 1, 0)
-    side, face = call(
+    face = send(face, 1, 0)
+    (side,) = call(
         functools.partial(last_side_kernel, sz), "last_side", 0,
-        [like((blocks, sz.ex) + tile, bf16), face], [], [side, corner, face], aliases={2: 1},
-    )
-    face = send(face, 1, 0)
+        [like((blocks, sz.ex) + tile, bf16)], [], [side, face],
+    )
     side = send(side, 0, 1)
     (filtered,) = call(
         functools.partial(last_kernel, sz), "last", 0, [like(own, f32)],

time: 71 us -> 73.4 us (1.034)
  waiting for transfers between devices: 20.4 us -> 25.9 us
  local copies, waits for them, and re-layouts: 5.74 us -> 2.94 us
  starting transfers between devices: 22.3 us -> 20.3 us
  Pallas kernels: 20.7 us -> 22.4 us
    ppermute x10 -> x9, waiting for transfers between devices: 10.5 us -> 15.7 us  [send(): return lax.ppermute(value, ('dx', 'dy'), pairs)]
    unnamed x16, local copies, waits for them, and re-layouts: 4.35 us -> 2.27 us
    pallas_call x13 -> x15, Pallas kernels: 20.7 us -> 22.4 us  [call(): pl.pallas_call(kernel, in_specs=specs, out_specs=out_specs, out_shape=out...]
    ppermute x10 -> x9, starting transfers between devices: 15.3 us -> 13.6 us  [send(): return lax.ppermute(value, ('dx', 'dy'), pairs)]
  transfers between devices with their start and end apart: 16 -> 15, of which waited for: 7 -> 8; matrix products, arithmetic and copies ran while one was open for 1% -> 1% of each run, Pallas kernels for 21% -> 20%
where the time goes in v10:
time: 73.4 us; the launch traced here: 73.1 us
  waiting for transfers between devices  25.9 us (35%)
  Pallas kernels  22.4 us (31%)
  starting transfers between devices  20.3 us (28%)
  local copies, waits for them, and re-layouts  2.94 us (4%)
  between operations  0.86 us (1%)
    pallas_call x15, Pallas kernels, call(): pl.pallas_call(kernel, in_specs=specs, out_specs=out_specs, out_shape=out...  22.4 us
    ppermute x9, waiting for transfers between devices, send(): return lax.ppermute(value, ('dx', 'dy'), pairs)  15.7 us
    ppermute x9, starting transfers between devices, send(): return lax.ppermute(value, ('dx', 'dy'), pairs)  13.6 us
    ppermute x2, waiting for transfers between devices, swap_y(): far = lax.ppermute(far, 'dy', far_pairs)  8.94 us
    all_to_all x1, starting transfers between devices, body(): lax.all_to_all(pieces, ('dx', 'dy'), 0, 0, axis_index_groups=groups)  3.53 us
    ppermute x2, starting transfers between devices, swap_y(): far = lax.ppermute(far, 'dy', far_pairs)  3.09 us
    unnamed x16, local copies, waits for them, and re-layouts  2.27 us
  transfers between devices with their start and end apart: 15, of which 8 were waited for; matrix products, arithmetic and copies ran while one was open for 1% of the time, Pallas kernels for 20%

profile of v10, /device:TPU:0, one launch (start us, length us, event | category | flops | bytes accessed | tf_op | source)
XLA Modules:
  0.0 73.1 jit_solution(5497985545166907908)
XLA Ops:
  0.6 2.4 %pack.1 = (bf16[16,16,896]{2,1,0:T(8,128)(2,1)S(1)}, bf16[8,16,896]{2,1,0:T(8,128)(2,1)}, bf16[729,729]{1,0:T(8,128)(2,1)S(1)}, s32[4,729]{1,0:T(4,128)S(1)}) custom-call(bf16[2,8,16,16,128]{4,3,2,1,0:T(8,128)(2,1)} %vec.11, bf16[8,16,16,512]{3,2,1,0:T(8,128)(2,1)} %res_hbm.1, f32[8,16,16]{2,1,0:T(8,128)} %inv_hbm.1, f32[8,16,16]{2,1,0:T(8,128)} %pot_hbm.1, ...), custom_call_target="tpu_custom_call" | custom-call | bytes 5999332 | tf_op jit(solution)/shard_map/pack/pallas_call | solution.py:582
  3.1 0.0 copy-start.3
  3.1 1.0 %copy-done.3 = bf16[729,729]{1,0:T(8,128)(2,1)} copy-done((bf16[729,729]{1,0:T(8,128)(2,1)}, bf16[729,729]{1,0:T(8,128)(2,1)S(1)}, u32[]{:S(2)}) %copy-start.3) | copy-done | bytes 1062906
  4.1 5.4 %collective-permute-start.1 = (bf16[8,16,896]{2,1,0:T(8,128)(2,1)}, bf16[8,16,896]{2,1,0:T(8,128)(2,1)S(1)}, u32[]{:S(2)}, u32[]{:S(2)}) collective-permute-start(bf16[8,16,896]{2,1,0:T(8,128)(2,1)} %get-tuple-element.32), channel_id=1, source_target_pairs={{0,15},{1,0},{2,1},{3,2},{4,3},{5,4},{6,5},{7,6},{8,7},{9,8},{10,9... | collective-permute-start | bytes 688136 | tf_op jit(solution)/shard_map/ppermute | solution.py:91
  9.5 1.5 %collective-permute-start = (bf16[16,16,896]{2,1,0:T(8,128)(2,1)S(1)}, bf16[16,16,896]{2,1,0:T(8,128)(2,1)S(1)}, u32[]{:S(2)}, u32[]{:S(2)}) collective-permute-start(bf16[16,16,896]{2,1,0:T(8,128)(2,1)S(1)} %get-tuple-element.31), channel_id=1, source_target_pairs={{0,16},{1,17},{2,18},{3,19},{4,20},{5,21},{6,22},{7,23},{8,24},{9,... | collective-permute-start | bytes 1376264 | tf_op jit(solution)/shard_map/ppermute | solution.py:91
  11.0 3.8 %order_cells.3.refs_1_ = bf16[2,736,768]{2,1,0:T(8,128)(2,1)S(1)} custom-call(s32[4,729]{1,0:T(4,128)S(1)} %get-tuple-element.33.conn_ref, bf16[729,729]{1,0:T(8,128)(2,1)S(1)} %copy-done.2), custom_call_target="tpu_custom_call" | custom-call | flops 3623878656 | bytes 3335538 | tf_op jit(solution)/shard_map/order_cells/pallas_call | solution.py:582
  14.8 0.0 copy-start.4
  14.8 1.2 %copy-done.4 = bf16[729,729]{1,0:T(8,128)(2,1)S(1)} copy-done((bf16[729,729]{1,0:T(8,128)(2,1)S(1)}, bf16[729,729]{1,0:T(8,128)(2,1)}, u32[]{:S(2)}) %copy-start.4) | copy-done | bytes 1062906
  16.1 3.8 %order_cells.2.refs_0_ = bf16[2,736,768]{2,1,0:T(8,128)(2,1)S(1)} custom-call(s32[4,729]{1,0:T(4,128)S(1)} %get-tuple-element.33.conn_ref, bf16[729,729]{1,0:T(8,128)(2,1)S(1)} %copy-done.4), custom_call_target="tpu_custom_call" | custom-call | flops 3623878656 | bytes 3335538 | tf_op jit(solution)/shard_map/order_cells/pallas_call | solution.py:582
  19.9 0.0 copy-start
  19.9 0.0 collective-permute-done.1.from_y
  19.9 0.6 collective-permute-start.2
  20.5 0.0 collective-permute-done.from_x
  20.5 0.3 broadcast_in_dim.4.own_inv
  20.9 0.3 broadcast_in_dim.5.own_pot
  21.2 1.5 %first_main.1 = (f32[4,736,256]{2,1,0:T(8,128)S(1)}, f32[2,16,16,128]{3,2,1,0:T(8,128)S(1)}, f32[2,8,16,128]{3,2,1,0:T(8,128)S(1)}) custom-call(bf16[2,8,16,16,128]{4,3,2,1,0:T(8,128)(2,1)S(1)} %copy-done, bf16[16,16,896]{2,1,0:T(8,128)(2,1)S(1)} %collective-permute-done.from_x, bf16[8,16,896]{2,1,0:T(8,128)(2,1)S(1)} %collective-permute-done.1.from_y, ...), custom_call_target="tpu_custom_call" | custom-call | flops 1157627904 | bytes 11763712 | tf_op jit(solution)/shard_map/first_main/pallas_call | solution.py:582
  22.7 1.5 %collective-permute-done.2.corner = bf16[1,16,896]{2,1,0:T(8,128)(2,1)S(1)} collective-permute-done((bf16[1,16,896]{2,1,0:T(8,128)(2,1)S(1)}, bf16[1,16,896]{2,1,0:T(8,128)(2,1)S(1)}, u32[]{:S(2)}, u32[]{:S(2)}) %collective-permute-start.2) | collective-permute-done | bytes 28704 | tf_op jit(solution)/shard_map/ppermute | solution.py:91
  24.2 0.8 %first_corner.1 = (f32[2,9,17,16,128]{4,3,2,1,0:T(8,128)S(1)}, bf16[2,2,17,16,128]{4,3,2,1,0:T(8,128)(2,1)S(1)}, bf16[2,9,16,128]{3,2,1,0:T(8,128)(2,1)S(1)}, bf...) custom-call(s32[1]{0:T(128)} %bitcast.even_ref, ...), custom_call_target="tpu_custom_call" | custom-call | flops 192937984 | bytes 14757892 | tf_op jit(solution)/shard_map/first_corner/pallas_call | solution.py:582
  25.0 0.5 collective-permute-start.3
  25.5 0.0 collective-permute-start.4
  25.5 2.6 %collective-permute-start.5 = (bf16[2,9,16,128]{3,2,1,0:T(8,128)(2,1)S(1)}, bf16[2,9,16,128]{3,2,1,0:T(8,128)(2,1)S(1)}, u32[]{:S(2)}, u32[]{:S(2)}) collective-permute-start(bf16[2,9,16,128]{3,2,1,0:T(8,128)(2,1)S(1)} %get-tuple-element.43), channel_id=1, source_target_pairs={{0,15},{1,2},{2,1},{3,4},{4,3},{5,6},{6,5},{7,8},{8,7},{9,10},{10,... | collective-permute-start | bytes 221192 | tf_op jit(solution)/shard_map/ppermute | solution.py:108
  28.1 0.0 collective-permute-done.4.near.near_in
  28.1 3.9 %collective-permute-done.5.far.far_in = bf16[2,9,16,128]{3,2,1,0:T(8,128)(2,1)S(1)} collective-permute-done((bf16[2,9,16,128]{3,2,1,0:T(8,128)(2,1)S(1)}, bf16[2,9,16,128]{3,2,1,0:T(8,128)(2,1)S(1)}, u32[]{:S(2)}, u32[]{:S(2)}) %collective-permute-start.5) | collective-permute-done | bytes 73760 | tf_op jit(solution)/shard_map/ppermute | solution.py:108
  32.0 1.6 %collective-permute-start.6 = (bf16[2,2,2,16,128]{4,3,2,1,0:T(8,128)(2,1)S(1)}, bf16[2,2,2,16,128]{4,3,2,1,0:T(8,128)(2,1)S(1)}, u32[]{:S(2)}, u32[]{:S(2)}) collective-permute-start(bf16[2,2,2,16,128]{4,3,2,1,0:T(8,128)(2,1)S(1)} %corner_pack.2), channel_id=1, source_target_pairs={{0,16},{1,17},{2,18},{3,19},{4,20},{5,21},{6,22},{7,23},{8,24},{9,... | collective-permute-start | bytes 98312 | tf_op jit(solution)/shard_map/ppermute | solution.py:91
  33.6 0.0 collective-permute-done.3.face_in
  33.6 2.0 %second_main.1 = (f32[4,736,256]{2,1,0:T(8,128)S(1)}, f32[2,9,17,16,128]{4,3,2,1,0:T(8,128)S(1)}) custom-call(s32[1]{0:T(128)} %bitcast.even_ref, bf16[2,8,16,16,128]{4,3,2,1,0:T(8,128)(2,1)S(1)} %copy-done, bf16[16,16,896]{2,1,0:T(8,128)(2,1)S(1)} %collective-permute-done.from_x, bf16[8,16,896]{2,1,0:T(8,128)(2,1)S(1)} %collective-permute-done.1.from_y, ...), custom_call_target="tpu_custom_call" | custom-call | flops 1157627904 | bytes 17203204 | tf_op jit(solution)/shard_map/second_main/pallas_call | solution.py:582
  35.6 0.3 collective-permute-done.6.corner_in
  35.9 0.9 %second_corner.1 = (f32[2,9,17,16,128]{4,3,2,1,0:T(8,128)S(1)}, bf16[2,2,17,16,128]{4,3,2,1,0:T(8,128)(2,1)S(1)}, bf16[2,9,16,128]{3,2,1,0:T(8,128)(2,1)S(1)}, b...) custom-call(s32[1]{0:T(128)} %bitcast.even_ref, bf16[2,8,16,16,128]{4,3,2,1,0:T(8,128)(2,1)S(1)} %copy-done, ...), custom_call_target="tpu_custom_call" | custom-call | flops 192937984 | bytes 17760260 | tf_op jit(solution)/shard_map/second_corner/pallas_call | solution.py:582
  36.8 1.7 %collective-permute-start.7 = (bf16[2,2,17,16,128]{4,3,2,1,0:T(8,128)(2,1)S(1)}, bf16[2,2,17,16,128]{4,3,2,1,0:T(8,128)(2,1)S(1)}, u32[]{:S(2)}, u32[]{:S(2)}) collective-permute-start(bf16[2,2,17,16,128]{4,3,2,1,0:T(8,128)(2,1)S(1)} %get-tuple-element.46), channel_id=1, source_target_pairs={{0,16},{1,17},{2,18},{3,19},{4,20},{5,21},{6,22},{7,23},{8,24},{9,... | collective-permute-start | bytes 835592 | tf_op jit(solution)/shard_map/ppermute | solution.py:91
  38.5 0.5 collective-permute-start.9
  39.0 0.9 %turn_residents.1.turned = bf16[2,256,2560]{2,1,0:T(8,128)(2,1)S(1)} custom-call(bf16[2048,512]{1,0:T(8,128)(2,1)S(1)} %bitcast.4, bf16[16,16,896]{2,1,0:T(8,128)(2,1)S(1)} %collective-permute-done.from_x, bf16[8,16,896]{2,1,0:T(8,128)(2,1)S(1)} %collective-permute-done.1.from_y, bf16[1,16,896]{2,1,0:T(8,128)(2,1)S(1)} %collective-permute-done.2.corner), custom_call_target="tpu_custom_call" | custom-call | flops 578813952 | bytes 5435392 | tf_op jit(solution)/shard_map/turn_residents/pallas_call | solution.py:582
  39.9 0.0 collective-permute-done.8.near.near_in
  39.9 5.0 %collective-permute-done.9.far.far_in = bf16[2,9,16,128]{3,2,1,0:T(8,128)(2,1)S(1)} collective-permute-done((bf16[2,9,16,128]{3,2,1,0:T(8,128)(2,1)S(1)}, bf16[2,9,16,128]{3,2,1,0:T(8,128)(2,1)S(1)}, u32[]{:S(2)}, u32[]{:S(2)}) %collective-permute-start.9) | collective-permute-done | bytes 73760 | tf_op jit(solution)/shard_map/ppermute | solution.py:108
  44.9 0.4 collective-permute-start.10
  45.4 0.0 collective-permute-done.7.face_in
  45.4 2.1 %third_main.1 = (f32[4,736,256]{2,1,0:T(8,128)S(1)}, f32[2,9,17,16,128]{4,3,2,1,0:T(8,128)S(1)}) custom-call(s32[1]{0:T(128)} %bitcast.even_ref, bf16[2,8,16,16,128]{4,3,2,1,0:T(8,128)(2,1)S(1)} %copy-done, bf16[16,16,896]{2,1,0:T(8,128)(2,1)S(1)} %collective-permute-done.from_x, bf16[8,16,896]{2,1,0:T(8,128)(2,1)S(1)} %collective-permute-done.1.from_y, ...), custom_call_target="tpu_custom_call" | custom-call | flops 1157627904 | bytes 19709956 | tf_op jit(solution)/shard_map/third_main/pallas_call | solution.py:582
  47.4 1.4 %collective-permute-done.10.corner_in = bf16[2,2,2,16,128]{4,3,2,1,0:T(8,128)(2,1)S(1)} collective-permute-done((bf16[2,2,2,16,128]{4,3,2,1,0:T(8,128)(2,1)S(1)}, bf16[2,2,2,16,128]{4,3,2,1,0:T(8,128)(2,1)S(1)}, u32[]{:S(2)}, u32[]{:S(2)}) %collective-permute-start.10) | collective-permute-done | bytes 32800 | tf_op jit(solution)/shard_map/ppermute | solution.py:91
  48.9 2.7 %third_corner.1 = (f32[2,8,16,16,128]{4,3,2,1,0:T(8,128)}, f32[2,16,16,128]{3,2,1,0:T(8,128)S(1)}, f32[2,7,16,128]{3,2,1,0:T(8,128)S(1)}, bf16[2,17,16,128]{3,2,...) custom-call(s32[1]{0:T(128)} %bitcast.even_ref, ...), custom_call_target="tpu_custom_call" | custom-call | flops 864026624 | bytes 25600004 | tf_op jit(solution)/shard_map/third_corner/pallas_call | solution.py:582
  51.6 0.1 collective-permute-start.13
  51.6 1.3 %collective-permute-done.13.taken = bf16[256,256]{1,0:T(8,128)(2,1)S(1)} collective-permute-done((bf16[256,256]{1,0:T(8,128)(2,1)S(1)}, bf16[256,256]{1,0:T(8,128)(2,1)S(1)}, u32[]{:S(2)}, u32[]{:S(2)}) %collective-permute-start.13) | collective-permute-done | bytes 131104 | tf_op jit(solution)/shard_map/ppermute | solution.py:102
  53.0 0.7 %pieces.1 = bf16[2,8,32,256]{3,2,1,0:T(8,128)(2,1)} custom-call(f32[256,256]{1,0:T(8,128)S(1)} %get-tuple-element.58.keep, bf16[256,256]{1,0:T(8,128)(2,1)S(1)} %collective-permute-done.13.taken), custom_call_target="tpu_custom_call" | custom-call | bytes 655360 | tf_op jit(solution)/shard_map/pieces/pallas_call | solution.py:582
  53.7 3.5 %all-to-all-start = ((bf16[16,32,256]{2,1,0:T(8,128)(2,1)}), bf16[16,32,256]{2,1,0:T(8,128)(2,1)S(1)}, u32[]{:S(2)}, u32[]{:S(2)}) async-start(bf16[16,32,256]{2,1,0:T(8,128)(2,1)} %bitcast.3), calls=%async_computation | async-start | bytes 524288 | tf_op jit(solution)/shard_map/all_to_all | solution.py:712
  57.3 1.9 %collective-permute-start.11 = (bf16[2,17,16,128]{3,2,1,0:T(8,128)(2,1)}, bf16[2,17,16,128]{3,2,1,0:T(8,128)(2,1)S(1)}, u32[]{:S(2)}, u32[]{:S(2)}) collective-permute-start(bf16[2,17,16,128]{3,2,1,0:T(8,128)(2,1)} %copy-done.5), channel_id=1, source_target_pairs={{0,16},{1,17},{2,18},{3,19},{4,20},{5,21},{6,22},{7,23},{8,24},{9,... | collective-permute-start | bytes 417800 | tf_op jit(solution)/shard_map/ppermute | solution.py:91
  59.2 6.0 %collective-permute-done.11.face = bf16[2,17,16,128]{3,2,1,0:T(8,128)(2,1)S(1)} collective-permute-done((bf16[2,17,16,128]{3,2,1,0:T(8,128)(2,1)}, bf16[2,17,16,128]{3,2,1,0:T(8,128)(2,1)S(1)}, u32[]{:S(2)}, u32[]{:S(2)}) %collective-permute-start.11) | collective-permute-done | bytes 139296 | tf_op jit(solution)/shard_map/ppermute | solution.py:91
  65.2 0.1 collective-permute-start.12
  65.3 6.4 %collective-permute-done.12.side = bf16[2,8,16,128]{3,2,1,0:T(8,128)(2,1)S(1)} collective-permute-done((bf16[2,8,16,128]{3,2,1,0:T(8,128)(2,1)S(1)}, bf16[2,8,16,128]{3,2,1,0:T(8,128)(2,1)S(1)}, u32[]{:S(2)}, u32[]{:S(2)}) %collective-permute-start.12) | collective-permute-done | bytes 65568 | tf_op jit(solution)/shard_map/ppermute | solution.py:91
  71.7 0.8 %last.1 = f32[2,8,16,16,128]{4,3,2,1,0:T(8,128)} custom-call(f32[2,8,16,16,128]{4,3,2,1,0:T(8,128)} %get-tuple-element.53.old_hbm, f32[2,16,16,128]{3,2,1,0:T(8,128)S(1)} %get-tuple-element.54.edge_x, f32[2,7,16,128]{3,2,1,0:T(8,128)S(1)} %get-tuple-element.55.edge_y, ...), custom_call_target="tpu_custom_call", output_to_operand_aliasing={{}: (0, {})} | custom-call | bytes 4775936 | tf_op jit(solution)/shard_map/last/pallas_call | solution.py:582
  72.5 0.7 convert_reduce_fusion
  (17 shorter events, 0.0 us)
Async XLA Ops:
  0.6 10.4 %copy-start.2 = (bf16[729,729]{1,0:T(8,128)(2,1)S(1)}, bf16[729,729]{1,0:T(8,128)(2,1)}, u32[]{:S(2)}) copy-start(bf16[729,729]{1,0:T(8,128)(2,1)} %matrix_ref.1) | copy-start | bytes 3188650
  3.1 1.0 %copy-start.3 = (bf16[729,729]{1,0:T(8,128)(2,1)}, bf16[729,729]{1,0:T(8,128)(2,1)S(1)}, u32[]{:S(2)}) copy-start(bf16[729,729]{1,0:T(8,128)(2,1)S(1)} %get-tuple-element.34.matrix_ref) | copy-start | bytes 3188650
  4.1 15.8 %collective-permute-start.1 = (bf16[8,16,896]{2,1,0:T(8,128)(2,1)}, bf16[8,16,896]{2,1,0:T(8,128)(2,1)S(1)}, u32[]{:S(2)}, u32[]{:S(2)}) collective-permute-start(bf16[8,16,896]{2,1,0:T(8,128)(2,1)} %get-tuple-element.32), channel_id=1, source_target_pairs={{0,15},{1,0},{2,1},{3,2},{4,3},{5,4},{6,5},{7,6},{8,7},{9,8},{10,9... | collective-permute-start | bytes 688136 | tf_op jit(solution)/shard_map/ppermute | solution.py:91
  9.5 11.0 %collective-permute-start = (bf16[16,16,896]{2,1,0:T(8,128)(2,1)S(1)}, bf16[16,16,896]{2,1,0:T(8,128)(2,1)S(1)}, u32[]{:S(2)}, u32[]{:S(2)}) collective-permute-start(bf16[16,16,896]{2,1,0:T(8,128)(2,1)S(1)} %get-tuple-element.31), channel_id=1, source_target_pairs={{0,16},{1,17},{2,18},{3,19},{4,20},{5,21},{6,22},{7,23},{8,24},{9,... | collective-permute-start | bytes 1376264 | tf_op jit(solution)/shard_map/ppermute | solution.py:91
  14.8 1.3 %copy-start.4 = (bf16[729,729]{1,0:T(8,128)(2,1)S(1)}, bf16[729,729]{1,0:T(8,128)(2,1)}, u32[]{:S(2)}) copy-start(bf16[729,729]{1,0:T(8,128)(2,1)} %copy-done.3) | copy-start | bytes 3188650
  16.1 4.4 %copy-start.6 = (f32[8,16,16]{2,1,0:T(8,128)S(1)}, f32[8,16,16]{2,1,0:T(8,128)}, u32[]{:S(2)}) copy-start(f32[8,16,16]{2,1,0:T(8,128)} %inv_hbm.1) | copy-start | bytes 24580
  16.1 4.7 %copy-start.7 = (f32[8,16,16]{2,1,0:T(8,128)S(1)}, f32[8,16,16]{2,1,0:T(8,128)}, u32[]{:S(2)}) copy-start(f32[8,16,16]{2,1,0:T(8,128)} %pot_hbm.1) | copy-start | bytes 24580
  19.9 1.3 %copy-start = (bf16[2,8,16,16,128]{4,3,2,1,0:T(8,128)(2,1)S(1)}, bf16[2,8,16,16,128]{4,3,2,1,0:T(8,128)(2,1)}, u32[]{:S(2)}) copy-start(bf16[2,8,16,16,128]{4,3,2,1,0:T(8,128)(2,1)} %vec.11) | copy-start | bytes 3145732
  19.9 4.2 %collective-permute-start.2 = (bf16[1,16,896]{2,1,0:T(8,128)(2,1)S(1)}, bf16[1,16,896]{2,1,0:T(8,128)(2,1)S(1)}, u32[]{:S(2)}, u32[]{:S(2)}) collective-permute-start(bf16[1,16,896]{2,1,0:T(8,128)(2,1)S(1)} %slice.4), channel_id=1, source_target_pairs={{0,16},{1,17},{2,18},{3,19},{4,20},{5,21},{6,22},{7,23},{8,24},{9,... | collective-permute-start | bytes 86024 | tf_op jit(solution)/shard_map/ppermute | solution.py:91
  25.0 8.6 %collective-permute-start.3 = (bf16[2,2,17,16,128]{4,3,2,1,0:T(8,128)(2,1)S(1)}, bf16[2,2,17,16,128]{4,3,2,1,0:T(8,128)(2,1)S(1)}, u32[]{:S(2)}, u32[]{:S(2)}) collective-permute-start(bf16[2,2,17,16,128]{4,3,2,1,0:T(8,128)(2,1)S(1)} %get-tuple-element.41), channel_id=1, source_target_pairs={{0,16},{1,17},{2,18},{3,19},{4,20},{5,21},{6,22},{7,23},{8,24},{9,... | collective-permute-start | bytes 835592 | tf_op jit(solution)/shard_map/ppermute | solution.py:91
  25.5 2.6 %collective-permute-start.4 = (bf16[2,9,16,128]{3,2,1,0:T(8,128)(2,1)S(1)}, bf16[2,9,16,128]{3,2,1,0:T(8,128)(2,1)S(1)}, u32[]{:S(2)}, u32[]{:S(2)}) collective-permute-start(bf16[2,9,16,128]{3,2,1,0:T(8,128)(2,1)S(1)} %get-tuple-element.42), channel_id=1, source_target_pairs={{0,1},{1,0},{2,3},{3,2},{4,5},{5,4},{6,7},{7,6},{8,9},{9,8},{10,11... | collective-permute-start | bytes 221192 | tf_op jit(solution)/shard_map/ppermute | solution.py:102
  25.5 6.5 %collective-permute-start.5 = (bf16[2,9,16,128]{3,2,1,0:T(8,128)(2,1)S(1)}, bf16[2,9,16,128]{3,2,1,0:T(8,128)(2,1)S(1)}, u32[]{:S(2)}, u32[]{:S(2)}) collective-permute-start(bf16[2,9,16,128]{3,2,1,0:T(8,128)(2,1)S(1)} %get-tuple-element.43), channel_id=1, source_target_pairs={{0,15},{1,2},{2,1},{3,4},{4,3},{5,6},{6,5},{7,8},{8,7},{9,10},{10,... | collective-permute-start | bytes 221192 | tf_op jit(solution)/shard_map/ppermute | solution.py:108
  32.0 3.9 %collective-permute-start.6 = (bf16[2,2,2,16,128]{4,3,2,1,0:T(8,128)(2,1)S(1)}, bf16[2,2,2,16,128]{4,3,2,1,0:T(8,128)(2,1)S(1)}, u32[]{:S(2)}, u32[]{:S(2)}) collective-permute-start(bf16[2,2,2,16,128]{4,3,2,1,0:T(8,128)(2,1)S(1)} %corner_pack.2), channel_id=1, source_target_pairs={{0,16},{1,17},{2,18},{3,19},{4,20},{5,21},{6,22},{7,23},{8,24},{9,... | collective-permute-start | bytes 98312 | tf_op jit(solution)/shard_map/ppermute | solution.py:91
  35.9 3.1 %copy-start.1 = (bf16[8,16,16,512]{3,2,1,0:T(8,128)(2,1)S(1)}, bf16[8,16,16,512]{3,2,1,0:T(8,128)(2,1)}, u32[]{:S(2)}) copy-start(bf16[8,16,16,512]{3,2,1,0:T(8,128)(2,1)} %res_hbm.1) | copy-start | bytes 6291460
  36.8 8.6 %collective-permute-start.7 = (bf16[2,2,17,16,128]{4,3,2,1,0:T(8,128)(2,1)S(1)}, bf16[2,2,17,16,128]{4,3,2,1,0:T(8,128)(2,1)S(1)}, u32[]{:S(2)}, u32[]{:S(2)}) collective-permute-start(bf16[2,2,17,16,128]{4,3,2,1,0:T(8,128)(2,1)S(1)} %get-tuple-element.46), channel_id=1, source_target_pairs={{0,16},{1,17},{2,18},{3,19},{4,20},{5,21},{6,22},{7,23},{8,24},{9,... | collective-permute-start | bytes 835592 | tf_op jit(solution)/shard_map/ppermute | solution.py:91
  38.5 1.4 %collective-permute-start.8 = (bf16[2,9,16,128]{3,2,1,0:T(8,128)(2,1)S(1)}, bf16[2,9,16,128]{3,2,1,0:T(8,128)(2,1)S(1)}, u32[]{:S(2)}, u32[]{:S(2)}) collective-permute-start(bf16[2,9,16,128]{3,2,1,0:T(8,128)(2,1)S(1)} %get-tuple-element.47), channel_id=1, source_target_pairs={{0,1},{1,0},{2,3},{3,2},{4,5},{5,4},{6,7},{7,6},{8,9},{9,8},{10,11... | collective-permute-start | bytes 221192 | tf_op jit(solution)/shard_map/ppermute | solution.py:102
  38.5 6.5 %collective-permute-start.9 = (bf16[2,9,16,128]{3,2,1,0:T(8,128)(2,1)S(1)}, bf16[2,9,16,128]{3,2,1,0:T(8,128)(2,1)S(1)}, u32[]{:S(2)}, u32[]{:S(2)}) collective-permute-start(bf16[2,9,16,128]{3,2,1,0:T(8,128)(2,1)S(1)} %get-tuple-element.48), channel_id=1, source_target_pairs={{0,15},{1,2},{2,1},{3,4},{4,3},{5,6},{6,5},{7,8},{8,7},{9,10},{10,... | collective-permute-start | bytes 221192 | tf_op jit(solution)/shard_map/ppermute | solution.py:108
  44.9 3.9 %collective-permute-start.10 = (bf16[2,2,2,16,128]{4,3,2,1,0:T(8,128)(2,1)S(1)}, bf16[2,2,2,16,128]{4,3,2,1,0:T(8,128)(2,1)S(1)}, u32[]{:S(2)}, u32[]{:S(2)}) collective-permute-start(bf16[2,2,2,16,128]{4,3,2,1,0:T(8,128)(2,1)S(1)} %corner_pack.3), channel_id=1, source_target_pairs={{0,16},{1,17},{2,18},{3,19},{4,20},{5,21},{6,22},{7,23},{8,24},{9,... | collective-permute-start | bytes 98312 | tf_op jit(solution)/shard_map/ppermute | solution.py:91
  51.6 2.2 %copy-start.5 = (bf16[2,17,16,128]{3,2,1,0:T(8,128)(2,1)}, bf16[2,17,16,128]{3,2,1,0:T(8,128)(2,1)S(1)}, u32[]{:S(2)}) copy-start(bf16[2,17,16,128]{3,2,1,0:T(8,128)(2,1)S(1)} %get-tuple-element.56) | copy-start | bytes 417796
  51.6 1.4 %collective-permute-start.13 = (bf16[256,256]{1,0:T(8,128)(2,1)S(1)}, bf16[256,256]{1,0:T(8,128)(2,1)S(1)}, u32[]{:S(2)}, u32[]{:S(2)}) collective-permute-start(bf16[256,256]{1,0:T(8,128)(2,1)S(1)} %get-tuple-element.59), channel_id=1, source_target_pairs={{0,1},{1,0},{2,3},{3,2},{4,5},{5,4},{6,7},{7,6},{8,9},{9,8},{10,11... | collective-permute-start | bytes 393224 | tf_op jit(solution)/shard_map/ppermute | solution.py:102
  53.7 18.7 %all-to-all-start = ((bf16[16,32,256]{2,1,0:T(8,128)(2,1)}), bf16[16,32,256]{2,1,0:T(8,128)(2,1)S(1)}, u32[]{:S(2)}, u32[]{:S(2)}) async-start(bf16[16,32,256]{2,1,0:T(8,128)(2,1)} %bitcast.3), calls=%async_computation | async-start | bytes 524288 | tf_op jit(solution)/shard_map/all_to_all | solution.py:712
  57.3 7.9 %collective-permute-start.11 = (bf16[2,17,16,128]{3,2,1,0:T(8,128)(2,1)}, bf16[2,17,16,128]{3,2,1,0:T(8,128)(2,1)S(1)}, u32[]{:S(2)}, u32[]{:S(2)}) collective-permute-start(bf16[2,17,16,128]{3,2,1,0:T(8,128)(2,1)} %copy-done.5), channel_id=1, source_target_pairs={{0,16},{1,17},{2,18},{3,19},{4,20},{5,21},{6,22},{7,23},{8,24},{9,... | collective-permute-start | bytes 417800 | tf_op jit(solution)/shard_map/ppermute | solution.py:91
  65.2 6.4 %collective-permute-start.12 = (bf16[2,8,16,128]{3,2,1,0:T(8,128)(2,1)S(1)}, bf16[2,8,16,128]{3,2,1,0:T(8,128)(2,1)S(1)}, u32[]{:S(2)}, u32[]{:S(2)}) collective-permute-start(bf16[2,8,16,128]{3,2,1,0:T(8,128)(2,1)S(1)} %last_side.1), channel_id=1, source_target_pairs={{0,1},{1,2},{2,3},{3,4},{4,5},{5,6},{6,7},{7,8},{8,9},{9,10},{10,1... | collective-permute-start | bytes 196616 | tf_op jit(solution)/shard_map/ppermute | solution.py:91

commit v11 on v10

--- a/solution.py
+++ b/solution.py
@@ -109,7 +109,12 @@
     return send_near(near), far
 
 
-def order_kernel(sz, first, conn_ref, matrix_ref, out_ref):
+def order_kernel(sz, first, matrix_ref, conn_ref, out_ref, *load):
+    copy = None
+    if load:
+        copy = pltpu.make_async_copy(matrix_ref, *load)
+        copy.start()
+        matrix_ref = load[0]
     for slot in range(out_ref.shape[0]):
         cell = first + slot
         x0, y0, z0 = sz.origins[cell]
@@ -131,6 +136,8 @@
         index = index.astype(jnp.int32)
         row = lax.broadcasted_iota(jnp.int32, (sz.depth, sz.nodes), 0)
         pick = (row == index).astype(f32).astype(bf16)
+        if copy is not None and slot == 0:
+            copy.wait()
         half = jnp.dot(pick[: sz.rows], matrix_ref[...], preferred_element_type=f32)
         half = half.astype(bf16)
         cuts = list(range(0, sz.depth, TILE)) + [sz.depth]
@@ -176,8 +183,7 @@
 
 
 def pack_kernel(
-    sz, vec_hbm, res_hbm, inv_hbm, pot_hbm, mat_hbm, conn_hbm,
-    to_x, to_y, mat_ref, conn_ref, at_x, at_y, sems,
+    sz, vec_hbm, res_hbm, inv_hbm, pot_hbm, conn_hbm, to_x, to_y, conn_ref, at_x, at_y, sems
 ):
     pairs = [
         (inv_hbm.at[0], at_x.at[0]), (pot_hbm.at[0], at_x.at[1]),
@@ -189,7 +195,7 @@
         lanes = pl.ds(sz.res + b * sz.width, sz.width)
         pairs.append((vec_hbm.at[b, 0], to_x.at[:, :, lanes]))
         pairs.append((vec_hbm.at[b, :, 0], to_y.at[:, :, lanes]))
-    pairs += [(mat_hbm, mat_ref), (conn_hbm, conn_ref)]
+    pairs.append((conn_hbm, conn_ref))
     copies = [pltpu.make_async_copy(a, b, sems.at[k]) for k, (a, b) in enumerate(pairs)]
     for copy in copies:
         copy.start()
@@ -471,8 +477,8 @@
                  last_x, last_field, acc_in, face_in, near_in, far_in, corner_in, prod_ref, y_ref,
                  y_corner, new_ref, turned, *refs):
     mats = refs[:n_mat]
-    out_hbm, edge_x, edge_y, face, side, give, keep = refs[n_mat : n_mat + 7]
-    part_ref, sem, acc_ref, rows_ref, small_ref, tail_ref = refs[n_mat + 7 :]
+    out_hbm, edge_x, edge_y, face, side, corner, give, keep = refs[n_mat : n_mat + 8]
+    part_ref, sem, acc_ref, rows_ref, small_ref, tail_ref = refs[n_mat + 8 :]
     nodes = Nodes(sz, vec, from_x, from_y, own_inv, own_pot, ghost_x, ghost_y, last_field)
     sums = Sums(sz, even_ref[0] == 0, acc_in, face_in, near_in, far_in, corner_in)
     u_corner, new_corner = [], []
@@ -495,10 +501,12 @@
             if i == sz.ex or j == sz.ey:
                 value = gain * (inv * acc)
                 rounded = value.astype(bf16)
-                if i == sz.ex:
+                if j < sz.ey:
                     face[:, j] = rounded
+                elif i < sz.ex:
+                    side[:, i] = value
                 else:
-                    side[:, i] = value
+                    corner[...] = rounded
                 put_row(sz.own_edges + (j if j < sz.ey else sz.ey + i), rounded)
                 continue
             at = sz.corner(i, j)
@@ -535,11 +543,12 @@
             pieces[copy, at] = value
 
 
-def last_side_kernel(sz, side_ref, face, out_ref):
+def last_side_kernel(sz, side_ref, corner_ref, face_in, out_ref, face_out):
+    del face_in, face_out
     for i in range(sz.ex):
         value = side_ref[:, i]
         if i == 0:
-            value = value + face[:, sz.ey].astype(f32)
+            value = value + corner_ref[...].astype(f32)
         out_ref[:, i] = value.astype(out_ref.dtype)
 
 
@@ -601,14 +610,14 @@
     tile = (ez, width)
 
     conn = connectivity.reshape(sz.cells, sz.nodes)
-    to_x, to_y, loaded, conn = call(
+    to_x, to_y, conn = call(
         functools.partial(pack_kernel, sz), "pack", 0,
-        [like((sz.ey, ez, sz.wide), bf16), like((sz.ex, ez, sz.wide), bf16), cell_matrix, conn],
+        [like((sz.ey, ez, sz.wide), bf16), like((sz.ex, ez, sz.wide), bf16), conn],
         [
             pltpu.VMEM((2, sz.ey, ez), f32), pltpu.VMEM((2, sz.ex, ez), f32),
-            pltpu.SemaphoreType.DMA((8 + 2 * blocks,)),
+            pltpu.SemaphoreType.DMA((7 + 2 * blocks,)),
         ],
-        [vectors, resident, inv_mass, potential, cell_matrix, conn], hbm=6,
+        [vectors, resident, inv_mass, potential, conn], hbm=5,
     )
     from_x = send(to_x, -1, 0)
     from_y = send(to_y, 0, -1)
@@ -619,7 +628,9 @@
     for at in range(0, sz.cells, step):
         mats += call(
             functools.partial(order_kernel, sz, at), "order_cells", 4 * step * sz.depth**3,
-            [like((step, sz.rows, sz.depth), bf16)], [], [conn, loaded if at == 0 else cell_matrix],
+            [like((step, sz.rows, sz.depth), bf16)],
+            [pltpu.VMEM(cell_matrix.shape, bf16), pltpu.SemaphoreType.DMA] if at == 0 else [],
+            [cell_matrix, conn], hbm=1 if at == 0 else 0,
         )
     own_inv = jnp.broadcast_to(inv_mass[..., None], inv_mass.shape + (width,))
     own_pot = jnp.broadcast_to(potential[..., None], inv_mass.shape + (width,))
@@ -690,12 +701,12 @@
         [products, state_grid], main_scratch,
         [parity, *state, acc, *got, y1, *mats], scalar_first=True,
     )
-    filtered, edge_x, edge_y, face, side, give, keep = call(
+    filtered, edge_x, edge_y, face, side, corner, give, keep = call(
         functools.partial(third_corner, sz, n_mat, norm_scale), "third_corner",
         small_flops + 2 * res_count * sz.edges * ez * full,
         [
             like(own, f32), like((blocks, sz.ey) + tile, f32), like((blocks, sz.ex - 1) + tile, f32),
-            like((blocks, sz.gy) + tile, bf16), like((blocks, sz.ex) + tile, f32),
+            like((blocks, sz.ey) + tile, bf16), like((blocks, sz.ex) + tile, f32), like(sz.edge, bf16),
             like((res_count // 2, full), bf16), like((res_count // 2, full), f32),
         ],
         [pltpu.VMEM(own, f32), pltpu.SemaphoreType.DMA((sz.ex,)), pltpu.VMEM(grid, f32), pltpu.VMEM((sz.edges, ez, full), bf16)] + corner_scratch,
@@ -712,11 +723,12 @@
     pieces = lax.all_to_all(pieces, ("dx", "dy"), 0, 0, axis_index_groups=groups)
     margin = jnp.sum(pieces.astype(f32), axis=0)
 
+    corner = send(corner, 1, 0)
+    side, face = call(
+        functools.partial(last_side_kernel, sz), "last_side", 0,
+        [like((blocks, sz.ex) + tile, bf16), face], [], [side, corner, face], aliases={2: 1},
+    )
     face = send(face, 1, 0)
-    (side,) = call(
-        functools.partial(last_side_kernel, sz), "last_side", 0,
-        [like((blocks, sz.ex) + tile, bf16)], [], [side, face],
-    )
     side = send(side, 0, 1)
     (filtered,) = call(
         functools.partial(last_kernel, sz), "last", 0, [like(own, f32)],

time: 73.4 us -> 71.3 us (0.971)
  waiting for transfers between devices: 25.9 us -> 22.4 us
  starting transfers between devices: 20.3 us -> 21.8 us
  local copies, waits for them, and re-layouts: 2.94 us -> 1.6 us
  Pallas kernels: 22.4 us -> 23.6 us
    ppermute x9 -> x10, waiting for transfers between devices: 15.7 us -> 12 us  [send(): return lax.ppermute(value, ('dx', 'dy'), pairs)]
    ppermute x9 -> x10, starting transfers between devices: 13.6 us -> 15.3 us  [send(): return lax.ppermute(value, ('dx', 'dy'), pairs)]
    unnamed x16 -> x14, local copies, waits for them, and re-layouts: 2.27 us -> 0.93 us
    pallas_call x15, Pallas kernels: 22.4 us -> 23.6 us  [call(): pl.pallas_call(kernel, in_specs=specs, out_specs=out_specs, out_shape=out...]
  transfers between devices with their start and end apart: 15 -> 16, of which waited for: 8 -> 8; matrix products, arithmetic and copies ran while one was open for 1% -> 1% of each run, Pallas kernels for 20% -> 23%
where the time goes in v11:
time: 71.3 us; the launch traced here: 70.9 us
  Pallas kernels  23.6 us (33%)
  waiting for transfers between devices  22.4 us (31%)
  starting transfers between devices  21.8 us (31%)
  local copies, waits for them, and re-layouts  1.6 us (2%)
  between operations  0.85 us (1%)
    pallas_call x15, Pallas kernels, call(): pl.pallas_call(kernel, in_specs=specs, out_specs=out_specs, out_shape=out...  23.6 us
    ppermute x10, starting transfers between devices, send(): return lax.ppermute(value, ('dx', 'dy'), pairs)  15.3 us
    ppermute x10, waiting for transfers between devices, send(): return lax.ppermute(value, ('dx', 'dy'), pairs)  12 us
    ppermute x2, waiting for transfers between devices, swap_y(): far = lax.ppermute(far, 'dy', far_pairs)  9.09 us
    all_to_all x1, starting transfers between devices, body(): lax.all_to_all(pieces, ('dx', 'dy'), 0, 0, axis_index_groups=groups)  3.53 us
    ppermute x2, starting transfers between devices, swap_y(): far = lax.ppermute(far, 'dy', far_pairs)  2.94 us
  transfers between devices with their start and end apart: 16, of which 8 were waited for; matrix products, arithmetic and copies ran while one was open for 1% of the time, Pallas kernels for 23%

profile of v11, /device:TPU:0, one launch (start us, length us, event | category | flops | bytes accessed | tf_op | source)
XLA Modules:
  0.0 70.9 jit_solution(10052145482940787676)
XLA Ops:
  0.6 0.0 copy-start.4
  0.6 2.0 %pack.1 = (bf16[16,16,896]{2,1,0:T(8,128)(2,1)S(1)}, bf16[8,16,896]{2,1,0:T(8,128)(2,1)}, s32[4,729]{1,0:T(4,128)S(1)}) custom-call(bf16[2,8,16,16,128]{4,3,2,1,0:T(8,128)(2,1)} %vec.11, bf16[8,16,16,512]{3,2,1,0:T(8,128)(2,1)} %res_hbm.1, f32[8,16,16]{2,1,0:T(8,128)} %inv_hbm.1, f32[8,16,16]{2,1,0:T(8,128)} %pot_hbm.1, s32[4,729]{1,0:T(4,128)} %bitcast.5), custom_call_target="tpu_custom_call" | custom-call | bytes 3873568 | tf_op jit(solution)/shard_map/pack/pallas_call | solution.py:591
  2.6 5.5 %collective-permute-start.1 = (bf16[8,16,896]{2,1,0:T(8,128)(2,1)}, bf16[8,16,896]{2,1,0:T(8,128)(2,1)S(1)}, u32[]{:S(2)}, u32[]{:S(2)}) collective-permute-start(bf16[8,16,896]{2,1,0:T(8,128)(2,1)} %get-tuple-element.34), channel_id=1, source_target_pairs={{0,15},{1,0},{2,1},{3,2},{4,3},{5,4},{6,5},{7,6},{8,7},{9,8},{10,9... | collective-permute-start | bytes 688136 | tf_op jit(solution)/shard_map/ppermute | solution.py:91
  8.1 1.5 %collective-permute-start = (bf16[16,16,896]{2,1,0:T(8,128)(2,1)S(1)}, bf16[16,16,896]{2,1,0:T(8,128)(2,1)S(1)}, u32[]{:S(2)}, u32[]{:S(2)}) collective-permute-start(bf16[16,16,896]{2,1,0:T(8,128)(2,1)S(1)} %get-tuple-element.33), channel_id=1, source_target_pairs={{0,16},{1,17},{2,18},{3,19},{4,20},{5,21},{6,22},{7,23},{8,24},{9,... | collective-permute-start | bytes 1376264 | tf_op jit(solution)/shard_map/ppermute | solution.py:91
  9.6 3.8 %order_cells.3.refs_1_ = bf16[2,736,768]{2,1,0:T(8,128)(2,1)S(1)} custom-call(bf16[729,729]{1,0:T(8,128)(2,1)S(1)} %copy-done.4, s32[4,729]{1,0:T(4,128)S(1)} %get-tuple-element.35.conn_ref), custom_call_target="tpu_custom_call" | custom-call | flops 3623878656 | bytes 3335538 | tf_op jit(solution)/shard_map/order_cells/pallas_call | solution.py:591
  13.4 0.0 copy-start.5
  13.4 0.0 copy-start.6
  13.4 5.1 %order_cells.2.refs_0_ = bf16[2,736,768]{2,1,0:T(8,128)(2,1)S(1)} custom-call(bf16[729,729]{1,0:T(8,128)(2,1)} %matrix_ref.3, s32[4,729]{1,0:T(4,128)S(1)} %get-tuple-element.35.conn_ref), custom_call_target="tpu_custom_call" | custom-call | flops 3623878656 | bytes 3335538 | tf_op jit(solution)/shard_map/order_cells/pallas_call | solution.py:591
  18.5 0.0 copy-start
  18.6 0.0 collective-permute-done.1.from_y
  18.6 0.6 collective-permute-start.2
  19.2 0.0 collective-permute-done.from_x
  19.2 0.3 broadcast_in_dim.4.own_inv
  19.5 0.3 broadcast_in_dim.5.own_pot
  19.9 1.5 %first_main.1 = (f32[4,736,256]{2,1,0:T(8,128)S(1)}, f32[2,16,16,128]{3,2,1,0:T(8,128)S(1)}, f32[2,8,16,128]{3,2,1,0:T(8,128)S(1)}) custom-call(bf16[2,8,16,16,128]{4,3,2,1,0:T(8,128)(2,1)S(1)} %copy-done, bf16[16,16,896]{2,1,0:T(8,128)(2,1)S(1)} %collective-permute-done.from_x, bf16[8,16,896]{2,1,0:T(8,128)(2,1)S(1)} %collective-permute-done.1.from_y, ...), custom_call_target="tpu_custom_call" | custom-call | flops 1157627904 | bytes 11763712 | tf_op jit(solution)/shard_map/first_main/pallas_call | solution.py:591
  21.3 1.5 %collective-permute-done.2.corner = bf16[1,16,896]{2,1,0:T(8,128)(2,1)S(1)} collective-permute-done((bf16[1,16,896]{2,1,0:T(8,128)(2,1)S(1)}, bf16[1,16,896]{2,1,0:T(8,128)(2,1)S(1)}, u32[]{:S(2)}, u32[]{:S(2)}) %collective-permute-start.2) | collective-permute-done | bytes 28704 | tf_op jit(solution)/shard_map/ppermute | solution.py:91
  22.8 0.8 %first_corner.1 = (f32[2,9,17,16,128]{4,3,2,1,0:T(8,128)S(1)}, bf16[2,2,17,16,128]{4,3,2,1,0:T(8,128)(2,1)S(1)}, bf16[2,9,16,128]{3,2,1,0:T(8,128)(2,1)S(1)}, bf...) custom-call(s32[1]{0:T(128)} %bitcast.even_ref, ...), custom_call_target="tpu_custom_call" | custom-call | flops 192937984 | bytes 14757892 | tf_op jit(solution)/shard_map/first_corner/pallas_call | solution.py:591
  23.7 0.5 collective-permute-start.3
  24.1 0.0 collective-permute-start.4
  24.2 2.5 %collective-permute-start.5 = (bf16[2,9,16,128]{3,2,1,0:T(8,128)(2,1)S(1)}, bf16[2,9,16,128]{3,2,1,0:T(8,128)(2,1)S(1)}, u32[]{:S(2)}, u32[]{:S(2)}) collective-permute-start(bf16[2,9,16,128]{3,2,1,0:T(8,128)(2,1)S(1)} %get-tuple-element.44), channel_id=1, source_target_pairs={{0,15},{1,2},{2,1},{3,4},{4,3},{5,6},{6,5},{7,8},{8,7},{9,10},{10,... | collective-permute-start | bytes 221192 | tf_op jit(solution)/shard_map/ppermute | solution.py:108
  26.7 0.0 collective-permute-done.4.near.near_in
  26.7 4.0 %collective-permute-done.5.far.far_in = bf16[2,9,16,128]{3,2,1,0:T(8,128)(2,1)S(1)} collective-permute-done((bf16[2,9,16,128]{3,2,1,0:T(8,128)(2,1)S(1)}, bf16[2,9,16,128]{3,2,1,0:T(8,128)(2,1)S(1)}, u32[]{:S(2)}, u32[]{:S(2)}) %collective-permute-start.5) | collective-permute-done | bytes 73760 | tf_op jit(solution)/shard_map/ppermute | solution.py:108
  30.6 1.6 %collective-permute-start.6 = (bf16[2,2,2,16,128]{4,3,2,1,0:T(8,128)(2,1)S(1)}, bf16[2,2,2,16,128]{4,3,2,1,0:T(8,128)(2,1)S(1)}, u32[]{:S(2)}, u32[]{:S(2)}) collective-permute-start(bf16[2,2,2,16,128]{4,3,2,1,0:T(8,128)(2,1)S(1)} %corner_pack.2), channel_id=1, source_target_pairs={{0,16},{1,17},{2,18},{3,19},{4,20},{5,21},{6,22},{7,23},{8,24},{9,... | collective-permute-start | bytes 98312 | tf_op jit(solution)/shard_map/ppermute | solution.py:91
  32.3 0.0 collective-permute-done.3.face_in
  32.3 1.9 %second_main.1 = (f32[4,736,256]{2,1,0:T(8,128)S(1)}, f32[2,9,17,16,128]{4,3,2,1,0:T(8,128)S(1)}) custom-call(s32[1]{0:T(128)} %bitcast.even_ref, bf16[2,8,16,16,128]{4,3,2,1,0:T(8,128)(2,1)S(1)} %copy-done, bf16[16,16,896]{2,1,0:T(8,128)(2,1)S(1)} %collective-permute-done.from_x, bf16[8,16,896]{2,1,0:T(8,128)(2,1)S(1)} %collective-permute-done.1.from_y, ...), custom_call_target="tpu_custom_call" | custom-call | flops 1157627904 | bytes 17203204 | tf_op jit(solution)/shard_map/second_main/pallas_call | solution.py:591
  34.2 0.3 collective-permute-done.6.corner_in
  34.5 0.9 %second_corner.1 = (f32[2,9,17,16,128]{4,3,2,1,0:T(8,128)S(1)}, bf16[2,2,17,16,128]{4,3,2,1,0:T(8,128)(2,1)S(1)}, bf16[2,9,16,128]{3,2,1,0:T(8,128)(2,1)S(1)}, b...) custom-call(s32[1]{0:T(128)} %bitcast.even_ref, bf16[2,8,16,16,128]{4,3,2,1,0:T(8,128)(2,1)S(1)} %copy-done, ...), custom_call_target="tpu_custom_call" | custom-call | flops 192937984 | bytes 17760260 | tf_op jit(solution)/shard_map/second_corner/pallas_call | solution.py:591
  35.4 1.7 %collective-permute-start.7 = (bf16[2,2,17,16,128]{4,3,2,1,0:T(8,128)(2,1)S(1)}, bf16[2,2,17,16,128]{4,3,2,1,0:T(8,128)(2,1)S(1)}, u32[]{:S(2)}, u32[]{:S(2)}) collective-permute-start(bf16[2,2,17,16,128]{4,3,2,1,0:T(8,128)(2,1)S(1)} %get-tuple-element.47), channel_id=1, source_target_pairs={{0,16},{1,17},{2,18},{3,19},{4,20},{5,21},{6,22},{7,23},{8,24},{9,... | collective-permute-start | bytes 835592 | tf_op jit(solution)/shard_map/ppermute | solution.py:91
  37.1 0.0 collective-permute-start.8
  37.1 0.4 collective-permute-start.9
  37.6 0.9 %turn_residents.1.turned = bf16[2,256,2560]{2,1,0:T(8,128)(2,1)S(1)} custom-call(bf16[2048,512]{1,0:T(8,128)(2,1)S(1)} %bitcast.4, bf16[16,16,896]{2,1,0:T(8,128)(2,1)S(1)} %collective-permute-done.from_x, bf16[8,16,896]{2,1,0:T(8,128)(2,1)S(1)} %collective-permute-done.1.from_y, bf16[1,16,896]{2,1,0:T(8,128)(2,1)S(1)} %collective-permute-done.2.corner), custom_call_target="tpu_custom_call" | custom-call | flops 578813952 | bytes 5435392 | tf_op jit(solution)/shard_map/turn_residents/pallas_call | solution.py:591
  38.5 5.1 %collective-permute-done.9.far.far_in = bf16[2,9,16,128]{3,2,1,0:T(8,128)(2,1)S(1)} collective-permute-done((bf16[2,9,16,128]{3,2,1,0:T(8,128)(2,1)S(1)}, bf16[2,9,16,128]{3,2,1,0:T(8,128)(2,1)S(1)}, u32[]{:S(2)}, u32[]{:S(2)}) %collective-permute-start.9) | collective-permute-done | bytes 73760 | tf_op jit(solution)/shard_map/ppermute | solution.py:108
  43.6 0.4 collective-permute-start.10
  44.0 2.1 %third_main.1 = (f32[4,736,256]{2,1,0:T(8,128)S(1)}, f32[2,9,17,16,128]{4,3,2,1,0:T(8,128)S(1)}) custom-call(s32[1]{0:T(128)} %bitcast.even_ref, bf16[2,8,16,16,128]{4,3,2,1,0:T(8,128)(2,1)S(1)} %copy-done, bf16[16,16,896]{2,1,0:T(8,128)(2,1)S(1)} %collective-permute-done.from_x, bf16[8,16,896]{2,1,0:T(8,128)(2,1)S(1)} %collective-permute-done.1.from_y, ...), custom_call_target="tpu_custom_call" | custom-call | flops 1157627904 | bytes 19709956 | tf_op jit(solution)/shard_map/third_main/pallas_call | solution.py:591
  46.1 1.4 %collective-permute-done.10.corner_in = bf16[2,2,2,16,128]{4,3,2,1,0:T(8,128)(2,1)S(1)} collective-permute-done((bf16[2,2,2,16,128]{4,3,2,1,0:T(8,128)(2,1)S(1)}, bf16[2,2,2,16,128]{4,3,2,1,0:T(8,128)(2,1)S(1)}, u32[]{:S(2)}, u32[]{:S(2)}) %collective-permute-start.10) | collective-permute-done | bytes 32800 | tf_op jit(solution)/shard_map/ppermute | solution.py:91
  47.5 3.1 %third_corner.1 = (f32[2,8,16,16,128]{4,3,2,1,0:T(8,128)}, f32[2,16,16,128]{3,2,1,0:T(8,128)S(1)}, f32[2,7,16,128]{3,2,1,0:T(8,128)S(1)}, bf16[2,16,16,128]{3,2,...) custom-call(s32[1]{0:T(128)} %bitcast.even_ref, ...), custom_call_target="tpu_custom_call" | custom-call | flops 864026624 | bytes 25600004 | tf_op jit(solution)/shard_map/third_corner/pallas_call | solution.py:591
  50.6 0.1 collective-permute-start.14
  50.7 1.3 %collective-permute-done.14.taken = bf16[256,256]{1,0:T(8,128)(2,1)S(1)} collective-permute-done((bf16[256,256]{1,0:T(8,128)(2,1)S(1)}, bf16[256,256]{1,0:T(8,128)(2,1)S(1)}, u32[]{:S(2)}, u32[]{:S(2)}) %collective-permute-start.14) | collective-permute-done | bytes 131104 | tf_op jit(solution)/shard_map/ppermute | solution.py:102
  52.0 0.7 %pieces.1 = bf16[2,8,32,256]{3,2,1,0:T(8,128)(2,1)} custom-call(f32[256,256]{1,0:T(8,128)S(1)} %get-tuple-element.62.keep, bf16[256,256]{1,0:T(8,128)(2,1)S(1)} %collective-permute-done.14.taken), custom_call_target="tpu_custom_call" | custom-call | bytes 655360 | tf_op jit(solution)/shard_map/pieces/pallas_call | solution.py:591
  52.8 3.5 %all-to-all-start = ((bf16[16,32,256]{2,1,0:T(8,128)(2,1)}), bf16[16,32,256]{2,1,0:T(8,128)(2,1)S(1)}, u32[]{:S(2)}, u32[]{:S(2)}) async-start(bf16[16,32,256]{2,1,0:T(8,128)(2,1)} %bitcast.3), calls=%async_computation | async-start | bytes 524288 | tf_op jit(solution)/shard_map/all_to_all | solution.py:723
  56.3 1.9 %collective-permute-start.11 = (bf16[2,16,128]{2,1,0:T(8,128)(2,1)S(1)}, bf16[2,16,128]{2,1,0:T(8,128)(2,1)S(1)}, u32[]{:S(2)}, u32[]{:S(2)}) collective-permute-start(bf16[2,16,128]{2,1,0:T(8,128)(2,1)S(1)} %get-tuple-element.58), channel_id=1, source_target_pairs={{0,16},{1,17},{2,18},{3,19},{4,20},{5,21},{6,22},{7,23},{8,24},{9,... | collective-permute-start | bytes 24584 | tf_op jit(solution)/shard_map/ppermute | solution.py:91
  58.2 2.4 %collective-permute-done.11.corner_ref = bf16[2,16,128]{2,1,0:T(8,128)(2,1)S(1)} collective-permute-done((bf16[2,16,128]{2,1,0:T(8,128)(2,1)S(1)}, bf16[2,16,128]{2,1,0:T(8,128)(2,1)S(1)}, u32[]{:S(2)}, u32[]{:S(2)}) %collective-permute-start.11) | collective-permute-done | bytes 8224 | tf_op jit(solution)/shard_map/ppermute | solution.py:91
  60.6 1.6 %collective-permute-start.12 = (bf16[2,16,16,128]{3,2,1,0:T(8,128)(2,1)S(1)}, bf16[2,16,16,128]{3,2,1,0:T(8,128)(2,1)S(1)}, u32[]{:S(2)}, u32[]{:S(2)}) collective-permute-start(bf16[2,16,16,128]{3,2,1,0:T(8,128)(2,1)S(1)} %get-tuple-element.60), channel_id=1, source_target_pairs={{0,16},{1,17},{2,18},{3,19},{4,20},{5,21},{6,22},{7,23},{8,24},{9,... | collective-permute-start | bytes 393224 | tf_op jit(solution)/shard_map/ppermute | solution.py:91
  62.2 6.4 %collective-permute-done.13.side = bf16[2,8,16,128]{3,2,1,0:T(8,128)(2,1)S(1)} collective-permute-done((bf16[2,8,16,128]{3,2,1,0:T(8,128)(2,1)S(1)}, bf16[2,8,16,128]{3,2,1,0:T(8,128)(2,1)S(1)}, u32[]{:S(2)}, u32[]{:S(2)}) %collective-permute-start.13) | collective-permute-done | bytes 65568 | tf_op jit(solution)/shard_map/ppermute | solution.py:91
  68.6 0.9 %copy-done.3 = f32[2,7,16,128]{3,2,1,0:T(8,128)S(1)} copy-done((f32[2,7,16,128]{3,2,1,0:T(8,128)S(1)}, f32[2,7,16,128]{3,2,1,0:T(8,128)}, u32[]{:S(2)}) %copy-start.3) | copy-done | bytes 114712
  69.5 0.8 %last.1 = f32[2,8,16,16,128]{4,3,2,1,0:T(8,128)} custom-call(f32[2,8,16,16,128]{4,3,2,1,0:T(8,128)} %get-tuple-element.54.old_hbm, f32[2,16,16,128]{3,2,1,0:T(8,128)S(1)} %get-tuple-element.55.edge_x, f32[2,7,16,128]{3,2,1,0:T(8,128)S(1)} %copy-done.3, bf16[2,16,16,128]{3,2,1,0:T(8,128)(2,1)S(1)} %collective-permute-done.12.face, ...), custom_call_target="tpu_custom_call", output_to_operand_aliasing={{}: (0, {})} | custom-call | bytes 4767744 | tf_op jit(solution)/shard_map/last/pallas_call | solution.py:591
  70.3 0.0 all-to-all-done
  70.3 0.7 convert_reduce_fusion
  (17 shorter events, 0.0 us)
Async XLA Ops:
  0.6 9.0 %copy-start.4 = (bf16[729,729]{1,0:T(8,128)(2,1)S(1)}, bf16[729,729]{1,0:T(8,128)(2,1)}, u32[]{:S(2)}) copy-start(bf16[729,729]{1,0:T(8,128)(2,1)} %matrix_ref.3) | copy-start | bytes 3188650
  2.6 15.9 %collective-permute-start.1 = (bf16[8,16,896]{2,1,0:T(8,128)(2,1)}, bf16[8,16,896]{2,1,0:T(8,128)(2,1)S(1)}, u32[]{:S(2)}, u32[]{:S(2)}) collective-permute-start(bf16[8,16,896]{2,1,0:T(8,128)(2,1)} %get-tuple-element.34), channel_id=1, source_target_pairs={{0,15},{1,0},{2,1},{3,2},{4,3},{5,4},{6,5},{7,6},{8,7},{9,8},{10,9... | collective-permute-start | bytes 688136 | tf_op jit(solution)/shard_map/ppermute | solution.py:91
  8.1 11.1 %collective-permute-start = (bf16[16,16,896]{2,1,0:T(8,128)(2,1)S(1)}, bf16[16,16,896]{2,1,0:T(8,128)(2,1)S(1)}, u32[]{:S(2)}, u32[]{:S(2)}) collective-permute-start(bf16[16,16,896]{2,1,0:T(8,128)(2,1)S(1)} %get-tuple-element.33), channel_id=1, source_target_pairs={{0,16},{1,17},{2,18},{3,19},{4,20},{5,21},{6,22},{7,23},{8,24},{9,... | collective-permute-start | bytes 1376264 | tf_op jit(solution)/shard_map/ppermute | solution.py:91
  13.4 5.7 %copy-start.5 = (f32[8,16,16]{2,1,0:T(8,128)S(1)}, f32[8,16,16]{2,1,0:T(8,128)}, u32[]{:S(2)}) copy-start(f32[8,16,16]{2,1,0:T(8,128)} %inv_hbm.1) | copy-start | bytes 24580
  13.4 6.1 %copy-start.6 = (f32[8,16,16]{2,1,0:T(8,128)S(1)}, f32[8,16,16]{2,1,0:T(8,128)}, u32[]{:S(2)}) copy-start(f32[8,16,16]{2,1,0:T(8,128)} %pot_hbm.1) | copy-start | bytes 24580
  18.5 1.3 %copy-start = (bf16[2,8,16,16,128]{4,3,2,1,0:T(8,128)(2,1)S(1)}, bf16[2,8,16,16,128]{4,3,2,1,0:T(8,128)(2,1)}, u32[]{:S(2)}) copy-start(bf16[2,8,16,16,128]{4,3,2,1,0:T(8,128)(2,1)} %vec.11) | copy-start | bytes 3145732
  18.6 4.2 %collective-permute-start.2 = (bf16[1,16,896]{2,1,0:T(8,128)(2,1)S(1)}, bf16[1,16,896]{2,1,0:T(8,128)(2,1)S(1)}, u32[]{:S(2)}, u32[]{:S(2)}) collective-permute-start(bf16[1,16,896]{2,1,0:T(8,128)(2,1)S(1)} %slice.4), channel_id=1, source_target_pairs={{0,16},{1,17},{2,18},{3,19},{4,20},{5,21},{6,22},{7,23},{8,24},{9,... | collective-permute-start | bytes 86024 | tf_op jit(solution)/shard_map/ppermute | solution.py:91
  23.7 8.6 %collective-permute-start.3 = (bf16[2,2,17,16,128]{4,3,2,1,0:T(8,128)(2,1)S(1)}, bf16[2,2,17,16,128]{4,3,2,1,0:T(8,128)(2,1)S(1)}, u32[]{:S(2)}, u32[]{:S(2)}) collective-permute-start(bf16[2,2,17,16,128]{4,3,2,1,0:T(8,128)(2,1)S(1)} %get-tuple-element.42), channel_id=1, source_target_pairs={{0,16},{1,17},{2,18},{3,19},{4,20},{5,21},{6,22},{7,23},{8,24},{9,... | collective-permute-start | bytes 835592 | tf_op jit(solution)/shard_map/ppermute | solution.py:91
  24.1 2.5 %collective-permute-start.4 = (bf16[2,9,16,128]{3,2,1,0:T(8,128)(2,1)S(1)}, bf16[2,9,16,128]{3,2,1,0:T(8,128)(2,1)S(1)}, u32[]{:S(2)}, u32[]{:S(2)}) collective-permute-start(bf16[2,9,16,128]{3,2,1,0:T(8,128)(2,1)S(1)} %get-tuple-element.43), channel_id=1, source_target_pairs={{0,1},{1,0},{2,3},{3,2},{4,5},{5,4},{6,7},{7,6},{8,9},{9,8},{10,11... | collective-permute-start | bytes 221192 | tf_op jit(solution)/shard_map/ppermute | solution.py:102
  24.2 6.5 %collective-permute-start.5 = (bf16[2,9,16,128]{3,2,1,0:T(8,128)(2,1)S(1)}, bf16[2,9,16,128]{3,2,1,0:T(8,128)(2,1)S(1)}, u32[]{:S(2)}, u32[]{:S(2)}) collective-permute-start(bf16[2,9,16,128]{3,2,1,0:T(8,128)(2,1)S(1)} %get-tuple-element.44), channel_id=1, source_target_pairs={{0,15},{1,2},{2,1},{3,4},{4,3},{5,6},{6,5},{7,8},{8,7},{9,10},{10,... | collective-permute-start | bytes 221192 | tf_op jit(solution)/shard_map/ppermute | solution.py:108
  30.6 3.9 %collective-permute-start.6 = (bf16[2,2,2,16,128]{4,3,2,1,0:T(8,128)(2,1)S(1)}, bf16[2,2,2,16,128]{4,3,2,1,0:T(8,128)(2,1)S(1)}, u32[]{:S(2)}, u32[]{:S(2)}) collective-permute-start(bf16[2,2,2,16,128]{4,3,2,1,0:T(8,128)(2,1)S(1)} %corner_pack.2), channel_id=1, source_target_pairs={{0,16},{1,17},{2,18},{3,19},{4,20},{5,21},{6,22},{7,23},{8,24},{9,... | collective-permute-start | bytes 98312 | tf_op jit(solution)/shard_map/ppermute | solution.py:91
  34.5 3.0 %copy-start.1 = (bf16[8,16,16,512]{3,2,1,0:T(8,128)(2,1)S(1)}, bf16[8,16,16,512]{3,2,1,0:T(8,128)(2,1)}, u32[]{:S(2)}) copy-start(bf16[8,16,16,512]{3,2,1,0:T(8,128)(2,1)} %res_hbm.1) | copy-start | bytes 6291460
  35.4 8.6 %collective-permute-start.7 = (bf16[2,2,17,16,128]{4,3,2,1,0:T(8,128)(2,1)S(1)}, bf16[2,2,17,16,128]{4,3,2,1,0:T(8,128)(2,1)S(1)}, u32[]{:S(2)}, u32[]{:S(2)}) collective-permute-start(bf16[2,2,17,16,128]{4,3,2,1,0:T(8,128)(2,1)S(1)} %get-tuple-element.47), channel_id=1, source_target_pairs={{0,16},{1,17},{2,18},{3,19},{4,20},{5,21},{6,22},{7,23},{8,24},{9,... | collective-permute-start | bytes 835592 | tf_op jit(solution)/shard_map/ppermute | solution.py:91
  37.1 1.3 %collective-permute-start.8 = (bf16[2,9,16,128]{3,2,1,0:T(8,128)(2,1)S(1)}, bf16[2,9,16,128]{3,2,1,0:T(8,128)(2,1)S(1)}, u32[]{:S(2)}, u32[]{:S(2)}) collective-permute-start(bf16[2,9,16,128]{3,2,1,0:T(8,128)(2,1)S(1)} %get-tuple-element.48), channel_id=1, source_target_pairs={{0,1},{1,0},{2,3},{3,2},{4,5},{5,4},{6,7},{7,6},{8,9},{9,8},{10,11... | collective-permute-start | bytes 221192 | tf_op jit(solution)/shard_map/ppermute | solution.py:102
  37.1 6.5 %collective-permute-start.9 = (bf16[2,9,16,128]{3,2,1,0:T(8,128)(2,1)S(1)}, bf16[2,9,16,128]{3,2,1,0:T(8,128)(2,1)S(1)}, u32[]{:S(2)}, u32[]{:S(2)}) collective-permute-start(bf16[2,9,16,128]{3,2,1,0:T(8,128)(2,1)S(1)} %get-tuple-element.49), channel_id=1, source_target_pairs={{0,15},{1,2},{2,1},{3,4},{4,3},{5,6},{6,5},{7,8},{8,7},{9,10},{10,... | collective-permute-start | bytes 221192 | tf_op jit(solution)/shard_map/ppermute | solution.py:108
  43.6 3.9 %collective-permute-start.10 = (bf16[2,2,2,16,128]{4,3,2,1,0:T(8,128)(2,1)S(1)}, bf16[2,2,2,16,128]{4,3,2,1,0:T(8,128)(2,1)S(1)}, u32[]{:S(2)}, u32[]{:S(2)}) collective-permute-start(bf16[2,2,2,16,128]{4,3,2,1,0:T(8,128)(2,1)S(1)} %corner_pack.3), channel_id=1, source_target_pairs={{0,16},{1,17},{2,18},{3,19},{4,20},{5,21},{6,22},{7,23},{8,24},{9,... | collective-permute-start | bytes 98312 | tf_op jit(solution)/shard_map/ppermute | solution.py:91
  50.6 2.2 %copy-start.2 = (f32[2,7,16,128]{3,2,1,0:T(8,128)}, f32[2,7,16,128]{3,2,1,0:T(8,128)S(1)}, u32[]{:S(2)}) copy-start(f32[2,7,16,128]{3,2,1,0:T(8,128)S(1)} %get-tuple-element.56.edge_y) | copy-start | bytes 344068
  50.6 1.4 %collective-permute-start.14 = (bf16[256,256]{1,0:T(8,128)(2,1)S(1)}, bf16[256,256]{1,0:T(8,128)(2,1)S(1)}, u32[]{:S(2)}, u32[]{:S(2)}) collective-permute-start(bf16[256,256]{1,0:T(8,128)(2,1)S(1)} %get-tuple-element.63), channel_id=1, source_target_pairs={{0,1},{1,0},{2,3},{3,2},{4,5},{5,4},{6,7},{7,6},{8,9},{9,8},{10,11... | collective-permute-start | bytes 393224 | tf_op jit(solution)/shard_map/ppermute | solution.py:102
  52.8 17.5 %all-to-all-start = ((bf16[16,32,256]{2,1,0:T(8,128)(2,1)}), bf16[16,32,256]{2,1,0:T(8,128)(2,1)S(1)}, u32[]{:S(2)}, u32[]{:S(2)}) async-start(bf16[16,32,256]{2,1,0:T(8,128)(2,1)} %bitcast.3), calls=%async_computation | async-start | bytes 524288 | tf_op jit(solution)/shard_map/all_to_all | solution.py:723
  56.3 4.2 %collective-permute-start.11 = (bf16[2,16,128]{2,1,0:T(8,128)(2,1)S(1)}, bf16[2,16,128]{2,1,0:T(8,128)(2,1)S(1)}, u32[]{:S(2)}, u32[]{:S(2)}) collective-permute-start(bf16[2,16,128]{2,1,0:T(8,128)(2,1)S(1)} %get-tuple-element.58), channel_id=1, source_target_pairs={{0,16},{1,17},{2,18},{3,19},{4,20},{5,21},{6,22},{7,23},{8,24},{9,... | collective-permute-start | bytes 24584 | tf_op jit(solution)/shard_map/ppermute | solution.py:91
  60.6 8.0 %collective-permute-start.12 = (bf16[2,16,16,128]{3,2,1,0:T(8,128)(2,1)S(1)}, bf16[2,16,16,128]{3,2,1,0:T(8,128)(2,1)S(1)}, u32[]{:S(2)}, u32[]{:S(2)}) collective-permute-start(bf16[2,16,16,128]{3,2,1,0:T(8,128)(2,1)S(1)} %get-tuple-element.60), channel_id=1, source_target_pairs={{0,16},{1,17},{2,18},{3,19},{4,20},{5,21},{6,22},{7,23},{8,24},{9,... | collective-permute-start | bytes 393224 | tf_op jit(solution)/shard_map/ppermute | solution.py:91
  62.2 6.4 %collective-permute-start.13 = (bf16[2,8,16,128]{3,2,1,0:T(8,128)(2,1)S(1)}, bf16[2,8,16,128]{3,2,1,0:T(8,128)(2,1)S(1)}, u32[]{:S(2)}, u32[]{:S(2)}) collective-permute-start(bf16[2,8,16,128]{3,2,1,0:T(8,128)(2,1)S(1)} %get-tuple-element.61), channel_id=1, source_target_pairs={{0,1},{1,2},{2,3},{3,4},{4,5},{5,6},{6,7},{7,8},{8,9},{9,10},{10,1... | collective-permute-start | bytes 196616 | tf_op jit(solution)/shard_map/ppermute | solution.py:91
  68.6 0.9 %copy-start.3 = (f32[2,7,16,128]{3,2,1,0:T(8,128)S(1)}, f32[2,7,16,128]{3,2,1,0:T(8,128)}, u32[]{:S(2)}) copy-start(f32[2,7,16,128]{3,2,1,0:T(8,128)} %copy-done.2) | copy-start | bytes 344068

commit v12 on v11

--- a/solution.py
+++ b/solution.py
@@ -30,7 +30,7 @@
         self.width = vectors.shape[-1]
         self.full = self.blocks * self.width
         self.res = resident.shape[-1]
-        self.wide = self.res + self.full + self.width
+        self.wide = self.full + self.width
         self.ex, self.ey, self.ez = inv_mass.shape
         self.cells, self.nodes = connectivity.shape[2:]
         self.n1 = round(self.nodes ** (1.0 / 3.0))
@@ -109,12 +109,7 @@
     return send_near(near), far
 
 
-def order_kernel(sz, first, matrix_ref, conn_ref, out_ref, *load):
-    copy = None
-    if load:
-        copy = pltpu.make_async_copy(matrix_ref, *load)
-        copy.start()
-        matrix_ref = load[0]
+def order_kernel(sz, first, matrix_ref, conn_ref, out_ref):
     for slot in range(out_ref.shape[0]):
         cell = first + slot
         x0, y0, z0 = sz.origins[cell]
@@ -136,8 +131,6 @@
         index = index.astype(jnp.int32)
         row = lax.broadcasted_iota(jnp.int32, (sz.depth, sz.nodes), 0)
         pick = (row == index).astype(f32).astype(bf16)
-        if copy is not None and slot == 0:
-            copy.wait()
         half = jnp.dot(pick[: sz.rows], matrix_ref[...], preferred_element_type=f32)
         half = half.astype(bf16)
         cuts = list(range(0, sz.depth, TILE)) + [sz.depth]
@@ -183,16 +176,16 @@
 
 
 def pack_kernel(
-    sz, vec_hbm, res_hbm, inv_hbm, pot_hbm, conn_hbm, to_x, to_y, conn_ref, at_x, at_y, sems
+    sz, vec_hbm, res_hbm, inv_hbm, pot_hbm, conn_hbm, to_x, to_y, res_x, conn_ref, at_x, at_y, sems
 ):
     pairs = [
         (inv_hbm.at[0], at_x.at[0]), (pot_hbm.at[0], at_x.at[1]),
         (inv_hbm.at[:, 0], at_y.at[0]), (pot_hbm.at[:, 0], at_y.at[1]),
-        (res_hbm.at[0], to_x.at[:, :, pl.ds(0, sz.res)]),
-        (res_hbm.at[:, 0], to_y.at[:, :, pl.ds(0, sz.res)]),
+        (res_hbm.at[0], res_x),
+        (res_hbm.at[:, 0], to_y.at[:, :, pl.ds(sz.wide, sz.res)]),
     ]
     for b in range(sz.blocks):
-        lanes = pl.ds(sz.res + b * sz.width, sz.width)
+        lanes = pl.ds(b * sz.width, sz.width)
         pairs.append((vec_hbm.at[b, 0], to_x.at[:, :, lanes]))
         pairs.append((vec_hbm.at[b, :, 0], to_y.at[:, :, lanes]))
     pairs.append((conn_hbm, conn_ref))
@@ -202,14 +195,14 @@
     for copy in copies[:4]:
         copy.wait()
     for j, row in field_rows(sz, at_x[0], at_x[1], sz.ey):
-        to_x[j, :, sz.res + sz.full :] = row
+        to_x[j, :, sz.full : sz.wide] = row
     for i, row in field_rows(sz, at_y[0], at_y[1], sz.ex):
-        to_y[i, :, sz.res + sz.full :] = row
+        to_y[i, :, sz.full : sz.wide] = row
     for copy in copies[4:]:
         copy.wait()
 
 
-def turn_kernel(sz, pieces, res_ref, from_x, from_y, corner, out_ref):
+def turn_kernel(sz, pieces, res_ref, res_x, from_y, corner, out_ref):
     own = sz.own_edges * sz.ez
     share = sz.res // out_ref.shape[0] // pieces
 
@@ -223,7 +216,8 @@
         lanes = slice(g, g + LANES)
         put(g, slice(0, own), res_ref[:, lanes].T)
         rest = sz.edges - sz.own_edges - sz.ey - sz.gx
-        parts = [from_x[:, :, lanes], from_y[:, :, lanes], corner[:, :, lanes]]
+        tail = slice(sz.wide + g, sz.wide + g + LANES)
+        parts = [res_x[:, :, lanes], from_y[:, :, tail], corner[:, :, tail]]
         if rest:
             parts.append(jnp.zeros((rest, sz.ez, LANES), bf16))
         ghosts = jnp.concatenate(parts, axis=0)
@@ -231,7 +225,7 @@
 
 
 def vectors_of(sz, edge):
-    lanes = [slice(sz.res + b * sz.width, sz.res + (b + 1) * sz.width) for b in range(sz.blocks)]
+    lanes = [slice(b * sz.width, (b + 1) * sz.width) for b in range(sz.blocks)]
     return jnp.stack([edge[:, at] for at in lanes]).astype(f32)
 
 
@@ -394,9 +388,9 @@
     mats = refs[:n_mat]
     prod_ref, ghost_x, ghost_y, u_ref, rhs_ref = refs[n_mat:]
     for j in range(sz.ey):
-        ghost_x[0, j], ghost_x[1, j] = fields_of(from_x[j, :, sz.res + sz.full :])
+        ghost_x[0, j], ghost_x[1, j] = fields_of(from_x[j, :, sz.full : sz.wide])
     for i in range(sz.ex):
-        ghost_y[0, i], ghost_y[1, i] = fields_of(from_y[i, :, sz.res + sz.full :])
+        ghost_y[0, i], ghost_y[1, i] = fields_of(from_y[i, :, sz.full : sz.wide])
     nodes = Nodes(sz, vec, from_x, from_y, own_inv, own_pot, ghost_x, ghost_y)
 
     def prepare(i, j):
@@ -405,11 +399,12 @@
     main_products(sz, prepare, u_ref, mats, rhs_ref, prod_ref)
 
 
-def first_corner(sz, n_mat, even_ref, vec, from_x, from_y, corner, own_inv, own_pot, ghost_x, ghost_y,
-                 prod_ref, *refs):
+def first_corner(sz, n_mat, even_ref, res_in, vec, from_x, from_y, corner, own_inv, own_pot, ghost_x,
+                 ghost_y, prod_ref, *refs):
     mats = refs[:n_mat]
-    acc_ref, face, near, far, last_x, last_field, small_ref, tail_ref = refs[n_mat:]
-    last_field[0], last_field[1] = fields_of(corner[0, :, sz.res + sz.full :])
+    res_out, acc_ref, face, near, far, last_x, last_field, small_ref, tail_ref = refs[n_mat:]
+    del res_in, res_out
+    last_field[0], last_field[1] = fields_of(corner[0, :, sz.full : sz.wide])
     last_x[...] = vectors_of(sz, corner[0])
     nodes = Nodes(sz, vec, from_x, from_y, own_inv, own_pot, ghost_x, ghost_y, last_field)
     u_corner = []
@@ -473,12 +468,12 @@
     main_products(sz, prepare, u_ref, mats, rhs_ref, prod_ref)
 
 
-def third_corner(sz, n_mat, norm_scale, even_ref, vec, from_x, from_y, own_inv, own_pot, ghost_x, ghost_y,
+def third_corner(sz, n_mat, even_ref, vec, from_x, from_y, own_inv, own_pot, ghost_x, ghost_y,
                  last_x, last_field, acc_in, face_in, near_in, far_in, corner_in, prod_ref, y_ref,
-                 y_corner, new_ref, turned, *refs):
+                 y_corner, new_ref, *refs):
     mats = refs[:n_mat]
-    out_hbm, edge_x, edge_y, face, side, corner, give, keep = refs[n_mat : n_mat + 8]
-    part_ref, sem, acc_ref, rows_ref, small_ref, tail_ref = refs[n_mat + 8 :]
+    out_hbm, edge_x, edge_y, face, side, corner, rows_ref = refs[n_mat : n_mat + 7]
+    part_ref, sem, acc_ref, small_ref, tail_ref = refs[n_mat + 7 :]
     nodes = Nodes(sz, vec, from_x, from_y, own_inv, own_pot, ghost_x, ghost_y, last_field)
     sums = Sums(sz, even_ref[0] == 0, acc_in, face_in, near_in, far_in, corner_in)
     u_corner, new_corner = [], []
@@ -525,26 +520,26 @@
             copies[-1].start()
     for at in range(sz.own_edges + sz.ey + sz.gx, sz.edges):
         rows_ref[at] = jnp.zeros((sz.ez, sz.full), bf16)
+    for copy in copies:
+        copy.wait()
+
+
+def margin_kernel(sz, norm_scale, even_ref, turned, rows_ref, give, keep):
     rows = rows_ref[...].reshape(sz.edges * sz.ez, sz.full)
     mine = even_ref[0]
     for half, out in ((1 - mine, give), (mine, keep)):
         local = jnp.dot(turned[half], rows, preferred_element_type=f32)
         out[...] = (local * norm_scale).astype(out.dtype)
-    for copy in copies:
-        copy.wait()
-
-
-def pieces_kernel(keep, taken, pieces):
+
+
+def ready_kernel(sz, keep, taken, side_ref, corner_ref, face_in, pieces, out_ref, face_out):
+    del face_in, face_out
     rows = pieces.shape[2]
     for at in range(pieces.shape[1]):
         span = slice(at * rows, (at + 1) * rows)
         value = (keep[span] + taken[span].astype(f32)).astype(pieces.dtype)
         for copy in range(pieces.shape[0]):
             pieces[copy, at] = value
-
-
-def last_side_kernel(sz, side_ref, corner_ref, face_in, out_ref, face_out):
-    del face_in, face_out
     for i in range(sz.ex):
         value = side_ref[:, i]
         if i == 0:
@@ -552,7 +547,7 @@
         out_ref[:, i] = value.astype(out_ref.dtype)
 
 
-def last_kernel(sz, old_hbm, edge_x, edge_y, face, side, out_hbm, at_x, at_y, sems):
+def last_kernel(sz, old_hbm, edge_x, edge_y, face, side, pieces, out_hbm, margin, at_x, at_y, sems):
     del old_hbm
     for j in range(sz.ey):
         value = edge_x[:, j] + face[:, j].astype(f32)
@@ -567,6 +562,7 @@
     ]
     for copy in copies:
         copy.start()
+    margin[...] = sum(pieces[at].astype(f32) for at in range(pieces.shape[0]))
     for copy in copies:
         copy.wait()
 
@@ -584,6 +580,9 @@
     if scalar_first:
         specs[0] = pl.BlockSpec(memory_space=pltpu.SMEM)
     out_specs = [pl.BlockSpec(memory_space=pltpu.HBM)] * out_hbm + [whole] * (len(out_shape) - out_hbm)
+    for source, target in (aliases or {}).items():
+        if source >= hbm:
+            specs[source] = out_specs[target] = pl.BlockSpec(memory_space=pl.ANY)
     out_shape = [pltpu.HBM(s.shape, s.dtype) for s in out_shape[:out_hbm]] + out_shape[out_hbm:]
     operands = [pltpu.with_memory_space_constraint(a, pltpu.HBM) for a in operands[:hbm]] + list(
         operands[hbm:]
@@ -610,9 +609,12 @@
     tile = (ez, width)
 
     conn = connectivity.reshape(sz.cells, sz.nodes)
-    to_x, to_y, conn = call(
+    to_x, to_y, res_x, conn = call(
         functools.partial(pack_kernel, sz), "pack", 0,
-        [like((sz.ey, ez, sz.wide), bf16), like((sz.ex, ez, sz.wide), bf16), conn],
+        [
+            like((sz.ey, ez, sz.wide), bf16), like((sz.ex, ez, sz.wide + sz.res), bf16),
+            like((sz.ey, ez, sz.res), bf16), conn,
+        ],
         [
             pltpu.VMEM((2, sz.ey, ez), f32), pltpu.VMEM((2, sz.ex, ez), f32),
             pltpu.SemaphoreType.DMA((7 + 2 * blocks,)),
@@ -621,6 +623,7 @@
     )
     from_x = send(to_x, -1, 0)
     from_y = send(to_y, 0, -1)
+    res_x = send(res_x, -1, 0)
 
     halves = 2 if sz.cells % 2 == 0 else 1
     step = sz.cells // halves
@@ -629,8 +632,7 @@
         mats += call(
             functools.partial(order_kernel, sz, at), "order_cells", 4 * step * sz.depth**3,
             [like((step, sz.rows, sz.depth), bf16)],
-            [pltpu.VMEM(cell_matrix.shape, bf16), pltpu.SemaphoreType.DMA] if at == 0 else [],
-            [cell_matrix, conn], hbm=1 if at == 0 else 0,
+            [], [cell_matrix, conn],
         )
     own_inv = jnp.broadcast_to(inv_mass[..., None], inv_mass.shape + (width,))
     own_pot = jnp.broadcast_to(potential[..., None], inv_mass.shape + (width,))
@@ -669,18 +671,19 @@
         [products, like((2, sz.ey) + tile, f32), like((2, sz.ex) + tile, f32)], main_scratch,
         [vectors, from_x, from_y, own_inv, own_pot, *mats],
     )
-    acc, face, near, far, last_x, last_field = call(
+    res_x, acc, face, near, far, last_x, last_field = call(
         functools.partial(first_corner, sz, n_mat), "first_corner", small_flops,
-        [state_grid, *messages, like(sz.edge, f32), like((2,) + tile, f32)], corner_scratch,
+        [res_x, state_grid, *messages, like(sz.edge, f32), like((2,) + tile, f32)], corner_scratch,
         [
-            parity, vectors, from_x, from_y, ghost_corner, own_inv, own_pot, ghost_x, ghost_y, prod, *mats,
+            parity, res_x, vectors, from_x, from_y, ghost_corner, own_inv, own_pot, ghost_x, ghost_y, prod,
+            *mats,
         ],
-        scalar_first=True,
+        scalar_first=True, aliases={1: 0},
     )
     (turned,) = call(
         functools.partial(turn_kernel, sz, ny // 2), "turn_residents", flops // 2,
         [like((2, res_count // 2, sz.edges * ez), bf16)], [],
-        [resident.reshape(-1, res_count), from_x, from_y, ghost_corner],
+        [resident.reshape(-1, res_count), res_x, from_y, ghost_corner],
     )
     got, corner = exchange(face, near, far)
     state = [vectors, from_x, from_y, own_inv, own_pot, ghost_x, ghost_y]
@@ -701,42 +704,42 @@
         [products, state_grid], main_scratch,
         [parity, *state, acc, *got, y1, *mats], scalar_first=True,
     )
-    filtered, edge_x, edge_y, face, side, corner, give, keep = call(
-        functools.partial(third_corner, sz, n_mat, norm_scale), "third_corner",
-        small_flops + 2 * res_count * sz.edges * ez * full,
+    filtered, edge_x, edge_y, face, side, corner, rows = call(
+        functools.partial(third_corner, sz, n_mat), "third_corner", small_flops,
         [
             like(own, f32), like((blocks, sz.ey) + tile, f32), like((blocks, sz.ex - 1) + tile, f32),
             like((blocks, sz.ey) + tile, bf16), like((blocks, sz.ex) + tile, f32), like(sz.edge, bf16),
-            like((res_count // 2, full), bf16), like((res_count // 2, full), f32),
+            like((sz.edges, ez, full), bf16),
         ],
-        [pltpu.VMEM(own, f32), pltpu.SemaphoreType.DMA((sz.ex,)), pltpu.VMEM(grid, f32), pltpu.VMEM((sz.edges, ez, full), bf16)] + corner_scratch,
-        [parity, *state, *ends, acc, *got, corner, prod, y1, y1_corner, y2, turned, *mats],
+        [pltpu.VMEM(own, f32), pltpu.SemaphoreType.DMA((sz.ex,)), pltpu.VMEM(grid, f32)] + corner_scratch,
+        [parity, *state, *ends, acc, *got, corner, prod, y1, y1_corner, y2, *mats],
         scalar_first=True, out_hbm=1,
     )
-
-    (pieces,) = call(
-        pieces_kernel, "pieces", 0, [like((nx, ny // 2, res_count // ny, full), bf16)], [],
-        [keep, send_near(give)],
+    corner = send(corner, 1, 0)
+    give, keep = call(
+        functools.partial(margin_kernel, sz, norm_scale), "margin", 2 * res_count * sz.edges * ez * full,
+        [like((res_count // 2, full), bf16), like((res_count // 2, full), f32)], [],
+        [parity, turned, rows], scalar_first=True,
+    )
+
+    pieces, side, face = call(
+        functools.partial(ready_kernel, sz), "ready", 0,
+        [like((nx, ny // 2, res_count // ny, full), bf16), like((blocks, sz.ex) + tile, bf16), face],
+        [], [keep, send_near(give), side, corner, face], aliases={4: 2},
     )
     pieces = pieces.reshape(nx * ny // 2, -1, full)
     groups = [[a * ny + b for a in range(nx) for b in range(c, ny, 2)] for c in range(2)]
     pieces = lax.all_to_all(pieces, ("dx", "dy"), 0, 0, axis_index_groups=groups)
-    margin = jnp.sum(pieces.astype(f32), axis=0)
-
-    corner = send(corner, 1, 0)
-    side, face = call(
-        functools.partial(last_side_kernel, sz), "last_side", 0,
-        [like((blocks, sz.ex) + tile, bf16), face], [], [side, corner, face], aliases={2: 1},
-    )
+
     face = send(face, 1, 0)
     side = send(side, 0, 1)
-    (filtered,) = call(
-        functools.partial(last_kernel, sz), "last", 0, [like(own, f32)],
+    filtered, margin = call(
+        functools.partial(last_kernel, sz), "last", 0, [like(own, f32), like(pieces.shape[1:], f32)],
         [
             pltpu.VMEM((blocks, sz.ey) + tile, f32), pltpu.VMEM((blocks, sz.ex - 1) + tile, f32),
             pltpu.SemaphoreType.DMA((2,)),
         ],
-        [filtered, edge_x, edge_y, face, side], hbm=1, out_hbm=1, aliases={0: 0},
+        [filtered, edge_x, edge_y, face, side, pieces], hbm=1, out_hbm=1, aliases={0: 0},
     )
     return (filtered, margin)
 

time: 71.3 us -> 80.1 us (1.12)
  Pallas kernels: 23.6 us -> 30.3 us
  local copies, waits for them, and re-layouts: 1.6 us -> 6.26 us
  starting transfers between devices: 21.8 us -> 20.6 us
  waiting for transfers between devices: 22.4 us -> 21.4 us
    pallas_call x15, Pallas kernels: 23.6 us -> 30.3 us  [call(): pl.pallas_call(kernel, in_specs=specs, out_specs=out_specs, out_shape=out...]
    unnamed x14 -> x20, local copies, waits for them, and re-layouts: 0.93 us -> 3.91 us
    ppermute x10 -> x11, waiting for transfers between devices: 12 us -> 9.74 us  [send(): return lax.ppermute(value, ('dx', 'dy'), pairs)]
    ppermute x2, starting transfers between devices: 2.94 us -> 0.75 us  [swap_y(): far = lax.ppermute(far, 'dy', far_pairs)]
    all_to_all x1, waiting for transfers between devices: 0.01 us -> 1.29 us  [body(): lax.all_to_all(pieces, ('dx', 'dy'), 0, 0, axis_index_groups=groups)]
    ppermute x10 -> x11, starting transfers between devices: 15.3 us -> 16.2 us  [send(): return lax.ppermute(value, ('dx', 'dy'), pairs)]
    broadcast_in_dim x1, local copies, waits for them, and re-layouts: 0.33 us -> 1.17 us  [body(): own_pot = jnp.broadcast_to(potential[..., None], inv_mass.shape + (width,))]
    broadcast_in_dim x1, local copies, waits for them, and re-layouts: 0.33 us -> 1.17 us  [body(): own_inv = jnp.broadcast_to(inv_mass[..., None], inv_mass.shape + (width,))]
  transfers between devices with their start and end apart: 16 -> 17, of which waited for: 8 -> 6; matrix products, arithmetic and copies ran while one was open for 1% -> 3% of each run, Pallas kernels for 23% -> 22%
where the time goes in v12:
time: 80.1 us; the launch traced here: 79.5 us
  Pallas kernels  30.3 us (38%)
  waiting for transfers between devices  21.4 us (27%)
  starting transfers between devices  20.6 us (26%)
  local copies, waits for them, and re-layouts  6.26 us (8%)
  between operations  1.02 us (1%)
    pallas_call x15, Pallas kernels, call(): pl.pallas_call(kernel, in_specs=specs, out_specs=out_specs, out_shape=out...  30.3 us
    ppermute x11, starting transfers between devices, send(): return lax.ppermute(value, ('dx', 'dy'), pairs)  16.2 us
    ppermute x2, waiting for transfers between devices, swap_y(): far = lax.ppermute(far, 'dy', far_pairs)  9.82 us
    ppermute x11, waiting for transfers between devices, send(): return lax.ppermute(value, ('dx', 'dy'), pairs)  9.74 us
    unnamed x20, local copies, waits for them, and re-layouts  3.91 us
    all_to_all x1, starting transfers between devices, body(): lax.all_to_all(pieces, ('dx', 'dy'), 0, 0, axis_index_groups=groups)  3.53 us
  transfers between devices with their start and end apart: 17, of which 6 were waited for; matrix products, arithmetic and copies ran while one was open for 3% of the time, Pallas kernels for 22%

profile of v12, /device:TPU:0, one launch (start us, length us, event | category | flops | bytes accessed | tf_op | source)
XLA Modules:
  0.0 79.5 jit_solution(17965883921743313289)
XLA Ops:
  0.6 2.1 %pack.1 = (bf16[16,16,384]{2,1,0:T(8,128)(2,1)}, bf16[8,16,896]{2,1,0:T(8,128)(2,1)}, bf16[16,16,512]{2,1,0:T(8,128)(2,1)}, s32[4,729]{1,0:T(4,128)S(1)}) custom-call(bf16[2,8,16,16,128]{4,3,2,1,0:T(8,128)(2,1)} %vec.11, bf16[8,16,16,512]{3,2,1,0:T(8,128)(2,1)} %res_hbm.1, f32[8,16,16]{2,1,0:T(8,128)} %inv_hbm.1, f32[8,16,16]{2,1,0:T(8,128)} %pot_hbm.1, ...), custom_call_target="tpu_custom_call" | custom-call | bytes 3873568 | tf_op jit(solution)/shard_map/pack/pallas_call | solution.py:590
  2.8 5.5 %collective-permute-start.1 = (bf16[8,16,896]{2,1,0:T(8,128)(2,1)}, bf16[8,16,896]{2,1,0:T(8,128)(2,1)S(1)}, u32[]{:S(2)}, u32[]{:S(2)}) collective-permute-start(bf16[8,16,896]{2,1,0:T(8,128)(2,1)} %get-tuple-element.38), channel_id=1, source_target_pairs={{0,15},{1,0},{2,1},{3,2},{4,3},{5,4},{6,5},{7,6},{8,7},{9,8},{10,9... | collective-permute-start | bytes 688136 | tf_op jit(solution)/shard_map/ppermute | solution.py:91
  8.2 1.5 %collective-permute-start = (bf16[16,16,384]{2,1,0:T(8,128)(2,1)}, bf16[16,16,384]{2,1,0:T(8,128)(2,1)}, u32[]{:S(2)}, u32[]{:S(2)}) collective-permute-start(bf16[16,16,384]{2,1,0:T(8,128)(2,1)} %get-tuple-element.37), channel_id=1, source_target_pairs={{0,16},{1,17},{2,18},{3,19},{4,20},{5,21},{6,22},{7,23},{8,24},{9,... | collective-permute-start | bytes 589832 | tf_op jit(solution)/shard_map/ppermute | solution.py:91
  9.8 0.5 collective-permute-start.2
  10.3 3.8 %order_cells.2.refs_0_ = bf16[2,736,768]{2,1,0:T(8,128)(2,1)S(1)} custom-call(bf16[729,729]{1,0:T(8,128)(2,1)S(1)} %copy-done.9, s32[4,729]{1,0:T(4,128)S(1)} %get-tuple-element.39.conn_ref), custom_call_target="tpu_custom_call" | custom-call | flops 3623878656 | bytes 3335538 | tf_op jit(solution)/shard_map/order_cells/pallas_call | solution.py:590
  14.1 0.0 copy-start.2
  14.1 3.8 %order_cells.3.refs_1_ = bf16[2,736,768]{2,1,0:T(8,128)(2,1)S(1)} custom-call(bf16[729,729]{1,0:T(8,128)(2,1)S(1)} %copy-done.9, s32[4,729]{1,0:T(4,128)S(1)} %get-tuple-element.39.conn_ref), custom_call_target="tpu_custom_call" | custom-call | flops 3623878656 | bytes 3335538 | tf_op jit(solution)/shard_map/order_cells/pallas_call | solution.py:590
  17.9 1.4 %copy-done = bf16[2,736,768]{2,1,0:T(8,128)(2,1)} copy-done((bf16[2,736,768]{2,1,0:T(8,128)(2,1)}, bf16[2,736,768]{2,1,0:T(8,128)(2,1)S(1)}, u32[]{:S(2)}) %copy-start) | copy-done | bytes 2261016
  19.3 0.0 collective-permute-done.1.from_y
  19.3 1.6 %collective-permute-start.3 = (bf16[1,16,896]{2,1,0:T(8,128)(2,1)S(1)}, bf16[1,16,896]{2,1,0:T(8,128)(2,1)S(1)}, u32[]{:S(2)}, u32[]{:S(2)}) collective-permute-start(bf16[1,16,896]{2,1,0:T(8,128)(2,1)S(1)} %slice.4), channel_id=1, source_target_pairs={{0,16},{1,17},{2,18},{3,19},{4,20},{5,21},{6,22},{7,23},{8,24},{9,... | collective-permute-start | bytes 86024 | tf_op jit(solution)/shard_map/ppermute | solution.py:91
  20.9 1.2 %broadcast_in_dim.4.own_inv = f32[8,16,16,128]{3,2,1,0:T(8,128)S(1)} broadcast(f32[8,16,16]{2,1,0:T(8,128)} %inv_hbm.1), dimensions={0,1,2} | broadcast | bytes 1056768 | tf_op jit(solution)/shard_map/broadcast_in_dim | solution.py:637
  22.0 1.2 %broadcast_in_dim.5.own_pot = f32[8,16,16,128]{3,2,1,0:T(8,128)S(1)} broadcast(f32[8,16,16]{2,1,0:T(8,128)} %pot_hbm.1), dimensions={0,1,2} | broadcast | bytes 1056768 | tf_op jit(solution)/shard_map/broadcast_in_dim | solution.py:638
  23.2 2.4 %first_main.1 = (f32[4,736,256]{2,1,0:T(8,128)S(1)}, f32[2,16,16,128]{3,2,1,0:T(8,128)S(1)}, f32[2,8,16,128]{3,2,1,0:T(8,128)S(1)}) custom-call(bf16[2,8,16,16,128]{4,3,2,1,0:T(8,128)(2,1)S(1)} %copy-done.2, bf16[16,16,384]{2,1,0:T(8,128)(2,1)} %collective-permute-done.from_x, bf16[8,16,896]{2,1,0:T(8,128)(2,1)S(1)} %collective-permute-done.1.from_y, ...), custom_call_target="tpu_custom_call" | custom-call | flops 1157627904 | bytes 11501568 | tf_op jit(solution)/shard_map/first_main/pallas_call | solution.py:590
  25.6 0.0 collective-permute-done.3.corner
  25.7 1.8 %first_corner.1 = (bf16[16,16,512]{2,1,0:T(8,128)(2,1)}, f32[2,9,17,16,128]{4,3,2,1,0:T(8,128)S(1)}, bf16[2,2,17,16,128]{4,3,2,1,0:T(8,128)(2,1)S(1)}, bf16[2,9,...) custom-call(s32[1]{0:T(128)} %bitcast.even_ref, ...), custom_call_target="tpu_custom_call", output_to_operand_aliasing={{0}: (1, {})} | custom-call | flops 192937984 | bytes 15020036 | tf_op jit(solution)/shard_map/first_corner/pallas_call | solution.py:590
  27.4 0.7 collective-permute-start.4
  28.1 0.0 collective-permute-start.5
  28.1 0.8 collective-permute-start.6
  28.9 0.5 collective-permute-done.5.near.near_in
  29.4 5.2 %collective-permute-done.6.far.far_in = bf16[2,9,16,128]{3,2,1,0:T(8,128)(2,1)S(1)} collective-permute-done((bf16[2,9,16,128]{3,2,1,0:T(8,128)(2,1)S(1)}, bf16[2,9,16,128]{3,2,1,0:T(8,128)(2,1)S(1)}, u32[]{:S(2)}, u32[]{:S(2)}) %collective-permute-start.6) | collective-permute-done | bytes 73760 | tf_op jit(solution)/shard_map/ppermute | solution.py:108
  34.6 1.4 %collective-permute-start.7 = (bf16[2,2,2,16,128]{4,3,2,1,0:T(8,128)(2,1)S(1)}, bf16[2,2,2,16,128]{4,3,2,1,0:T(8,128)(2,1)S(1)}, u32[]{:S(2)}, u32[]{:S(2)}) collective-permute-start(bf16[2,2,2,16,128]{4,3,2,1,0:T(8,128)(2,1)S(1)} %corner_pack.2), channel_id=1, source_target_pairs={{0,16},{1,17},{2,18},{3,19},{4,20},{5,21},{6,22},{7,23},{8,24},{9,... | collective-permute-start | bytes 98312 | tf_op jit(solution)/shard_map/ppermute | solution.py:91
  36.0 2.8 %second_main.1 = (f32[4,736,256]{2,1,0:T(8,128)S(1)}, f32[2,9,17,16,128]{4,3,2,1,0:T(8,128)S(1)}) custom-call(s32[1]{0:T(128)} %bitcast.even_ref, bf16[2,8,16,16,128]{4,3,2,1,0:T(8,128)(2,1)S(1)} %copy-done.2, bf16[16,16,384]{2,1,0:T(8,128)(2,1)} %collective-permute-done.from_x, bf16[8,16,896]{2,1,0:T(8,128)(2,1)S(1)} %collective-permute-done.1.from_y, ...), custom_call_target="tpu_custom_call" | custom-call | flops 1157627904 | bytes 16941060 | tf_op jit(solution)/shard_map/second_main/pallas_call | solution.py:590
  38.8 0.0 collective-permute-done.7.corner_in
  38.8 0.0 copy-start.3
  38.9 2.0 %second_corner.1 = (f32[2,9,17,16,128]{4,3,2,1,0:T(8,128)S(1)}, bf16[2,2,17,16,128]{4,3,2,1,0:T(8,128)(2,1)S(1)}, bf16[2,9,16,128]{3,2,1,0:T(8,128)(2,1)S(1)}, b...) custom-call(s32[1]{0:T(128)} %bitcast.even_ref, bf16[2,8,16,16,128]{4,3,2,1,0:T(8,128)(2,1)S(1)} %copy-done.2, ...), custom_call_target="tpu_custom_call" | custom-call | flops 192937984 | bytes 17498116 | tf_op jit(solution)/shard_map/second_corner/pallas_call | solution.py:590
  40.8 1.1 %collective-permute-start.8 = (bf16[2,2,17,16,128]{4,3,2,1,0:T(8,128)(2,1)S(1)}, bf16[2,2,17,16,128]{4,3,2,1,0:T(8,128)(2,1)S(1)}, u32[]{:S(2)}, u32[]{:S(2)}) collective-permute-start(bf16[2,2,17,16,128]{4,3,2,1,0:T(8,128)(2,1)S(1)} %get-tuple-element.52), channel_id=1, source_target_pairs={{0,16},{1,17},{2,18},{3,19},{4,20},{5,21},{6,22},{7,23},{8,24},{9,... | collective-permute-start | bytes 835592 | tf_op jit(solution)/shard_map/ppermute | solution.py:91
  42.0 1.9 %turn_residents.1.turned = bf16[2,256,2560]{2,1,0:T(8,128)(2,1)S(1)} custom-call(bf16[2048,512]{1,0:T(8,128)(2,1)S(1)} %bitcast.4, bf16[16,16,512]{2,1,0:T(8,128)(2,1)} %get-tuple-element.62.res_x, bf16[8,16,896]{2,1,0:T(8,128)(2,1)S(1)} %collective-permute-done.1.from_y, bf16[1,16,896]{2,1,0:T(8,128)(2,1)S(1)} %collective-permute-done.3.corner), custom_call_target="tpu_custom_call" | custom-call | flops 578813952 | bytes 5238784 | tf_op jit(solution)/shard_map/turn_residents/pallas_call | solution.py:590
  43.8 4.6 %collective-permute-done.10.far.far_in = bf16[2,9,16,128]{3,2,1,0:T(8,128)(2,1)S(1)} collective-permute-done((bf16[2,9,16,128]{3,2,1,0:T(8,128)(2,1)S(1)}, bf16[2,9,16,128]{3,2,1,0:T(8,128)(2,1)S(1)}, u32[]{:S(2)}, u32[]{:S(2)}) %collective-permute-start.10) | collective-permute-done | bytes 73760 | tf_op jit(solution)/shard_map/ppermute | solution.py:108
  48.4 0.0 collective-permute-done.9.near.near_in
  48.4 1.0 %collective-permute-start.11 = (bf16[2,2,2,16,128]{4,3,2,1,0:T(8,128)(2,1)S(1)}, bf16[2,2,2,16,128]{4,3,2,1,0:T(8,128)(2,1)S(1)}, u32[]{:S(2)}, u32[]{:S(2)}) collective-permute-start(bf16[2,2,2,16,128]{4,3,2,1,0:T(8,128)(2,1)S(1)} %corner_pack.3), channel_id=1, source_target_pairs={{0,16},{1,17},{2,18},{3,19},{4,20},{5,21},{6,22},{7,23},{8,24},{9,... | collective-permute-start | bytes 98312 | tf_op jit(solution)/shard_map/ppermute | solution.py:91
  49.4 0.0 collective-permute-done.8.face_in
  49.4 3.0 %third_main.1 = (f32[4,736,256]{2,1,0:T(8,128)S(1)}, f32[2,9,17,16,128]{4,3,2,1,0:T(8,128)S(1)}) custom-call(s32[1]{0:T(128)} %bitcast.even_ref, bf16[2,8,16,16,128]{4,3,2,1,0:T(8,128)(2,1)S(1)} %copy-done.2, bf16[16,16,384]{2,1,0:T(8,128)(2,1)} %collective-permute-done.from_x, bf16[8,16,896]{2,1,0:T(8,128)(2,1)S(1)} %collective-permute-done.1.from_y, ...), custom_call_target="tpu_custom_call" | custom-call | flops 1157627904 | bytes 19447812 | tf_op jit(solution)/shard_map/third_main/pallas_call | solution.py:590
  52.5 0.0 collective-permute-done.11.corner_in
  52.5 3.8 %third_corner.1 = (f32[2,8,16,16,128]{4,3,2,1,0:T(8,128)}, f32[2,16,16,128]{3,2,1,0:T(8,128)S(1)}, f32[2,7,16,128]{3,2,1,0:T(8,128)S(1)}, bf16[2,16,16,128]{3,2,...) custom-call(s32[1]{0:T(128)} %bitcast.even_ref, ...), custom_call_target="tpu_custom_call" | custom-call | flops 192937984 | bytes 23633924 | tf_op jit(solution)/shard_map/third_corner/pallas_call | solution.py:590
  56.3 0.8 %margin.1 = (bf16[256,256]{1,0:T(8,128)(2,1)S(1)}, f32[256,256]{1,0:T(8,128)S(1)}) custom-call(s32[1]{0:T(128)} %bitcast.even_ref, bf16[2,256,2560]{2,1,0:T(8,128)(2,1)S(1)} %turn_residents.1.turned, bf16[160,16,256]{2,1,0:T(8,128)(2,1)S(1)} %get-tuple-element.63.rows_ref), custom_call_target="tpu_custom_call" | custom-call | flops 671088640 | bytes 4325380 | tf_op jit(solution)/shard_map/margin/pallas_call | solution.py:590
  57.1 0.1 collective-permute-start.12
  57.2 1.1 %collective-permute-start.13 = (bf16[2,16,128]{2,1,0:T(8,128)(2,1)S(1)}, bf16[2,16,128]{2,1,0:T(8,128)(2,1)S(1)}, u32[]{:S(2)}, u32[]{:S(2)}) collective-permute-start(bf16[2,16,128]{2,1,0:T(8,128)(2,1)S(1)} %get-tuple-element.67), channel_id=1, source_target_pairs={{0,16},{1,17},{2,18},{3,19},{4,20},{5,21},{6,22},{7,23},{8,24},{9,... | collective-permute-start | bytes 24584 | tf_op jit(solution)/shard_map/ppermute | solution.py:91
  58.3 2.6 %collective-permute-done.13.corner_ref = bf16[2,16,128]{2,1,0:T(8,128)(2,1)S(1)} collective-permute-done((bf16[2,16,128]{2,1,0:T(8,128)(2,1)S(1)}, bf16[2,16,128]{2,1,0:T(8,128)(2,1)S(1)}, u32[]{:S(2)}, u32[]{:S(2)}) %collective-permute-start.13) | collective-permute-done | bytes 8224 | tf_op jit(solution)/shard_map/ppermute | solution.py:91
  60.9 0.0 collective-permute-done.12.taken
  60.9 0.7 ready.1
  61.7 0.6 copy-done.6
  62.3 3.5 %all-to-all-start = ((bf16[16,32,256]{2,1,0:T(8,128)(2,1)}), bf16[16,32,256]{2,1,0:T(8,128)(2,1)S(1)}, u32[]{:S(2)}, u32[]{:S(2)}) async-start(bf16[16,32,256]{2,1,0:T(8,128)(2,1)} %bitcast.3), calls=%async_computation | async-start | bytes 524288 | tf_op jit(solution)/shard_map/all_to_all | solution.py:732
  65.9 1.9 %collective-permute-start.14 = (bf16[2,16,16,128]{3,2,1,0:T(8,128)(2,1)}, bf16[2,16,16,128]{3,2,1,0:T(8,128)(2,1)S(1)}, u32[]{:S(2)}, u32[]{:S(2)}) collective-permute-start(bf16[2,16,16,128]{3,2,1,0:T(8,128)(2,1)} %copy-done.6), channel_id=1, source_target_pairs={{0,16},{1,17},{2,18},{3,19},{4,20},{5,21},{6,22},{7,23},{8,24},{9,... | collective-permute-start | bytes 393224 | tf_op jit(solution)/shard_map/ppermute | solution.py:91
  67.7 7.1 %collective-permute-done.15.side = bf16[2,8,16,128]{3,2,1,0:T(8,128)(2,1)S(1)} collective-permute-done((bf16[2,8,16,128]{3,2,1,0:T(8,128)(2,1)S(1)}, bf16[2,8,16,128]{3,2,1,0:T(8,128)(2,1)S(1)}, u32[]{:S(2)}, u32[]{:S(2)}) %collective-permute-start.15) | collective-permute-done | bytes 65568 | tf_op jit(solution)/shard_map/ppermute | solution.py:91
  74.9 1.3 %all-to-all-done.pieces = bf16[16,32,256]{2,1,0:T(8,128)(2,1)S(1)} async-done(((bf16[16,32,256]{2,1,0:T(8,128)(2,1)}), bf16[16,32,256]{2,1,0:T(8,128)(2,1)S(1)}, u32[]{:S(2)}, u32[]{:S(2)}) %all-to-all-start) | async-done | bytes 262176 | tf_op jit(solution)/shard_map/all_to_all | solution.py:732
  76.1 0.9 %copy-done.5 = f32[2,16,16,128]{3,2,1,0:T(8,128)S(1)} copy-done((f32[2,16,16,128]{3,2,1,0:T(8,128)S(1)}, f32[2,16,16,128]{3,2,1,0:T(8,128)}, u32[]{:S(2)}) %copy-start.5) | copy-done | bytes 262168
  77.1 0.9 %copy-done.8 = f32[2,7,16,128]{3,2,1,0:T(8,128)S(1)} copy-done((f32[2,7,16,128]{3,2,1,0:T(8,128)S(1)}, f32[2,7,16,128]{3,2,1,0:T(8,128)}, u32[]{:S(2)}) %copy-start.8) | copy-done | bytes 114712
  78.0 1.4 %last.1 = (f32[2,8,16,16,128]{4,3,2,1,0:T(8,128)}, f32[32,256]{1,0:T(8,128)}) custom-call(f32[2,8,16,16,128]{4,3,2,1,0:T(8,128)} %get-tuple-element.59.old_hbm, f32[2,16,16,128]{3,2,1,0:T(8,128)S(1)} %copy-done.5, f32[2,7,16,128]{3,2,1,0:T(8,128)S(1)} %copy-done.8, ...), custom_call_target="tpu_custom_call", output_to_operand_aliasing={{0}: (0, {})} | custom-call | bytes 5062656 | tf_op jit(solution)/shard_map/last/pallas_call | solution.py:590
  (24 shorter events, 0.1 us)
Async XLA Ops:
  0.6 9.6 %copy-start.9 = (bf16[729,729]{1,0:T(8,128)(2,1)S(1)}, bf16[729,729]{1,0:T(8,128)(2,1)}, u32[]{:S(2)}) copy-start(bf16[729,729]{1,0:T(8,128)(2,1)} %matrix_ref.3) | copy-start | bytes 3188650
  2.8 16.5 %collective-permute-start.1 = (bf16[8,16,896]{2,1,0:T(8,128)(2,1)}, bf16[8,16,896]{2,1,0:T(8,128)(2,1)S(1)}, u32[]{:S(2)}, u32[]{:S(2)}) collective-permute-start(bf16[8,16,896]{2,1,0:T(8,128)(2,1)} %get-tuple-element.38), channel_id=1, source_target_pairs={{0,15},{1,0},{2,1},{3,2},{4,3},{5,4},{6,5},{7,6},{8,7},{9,8},{10,9... | collective-permute-start | bytes 688136 | tf_op jit(solution)/shard_map/ppermute | solution.py:91
  8.2 12.6 %collective-permute-start = (bf16[16,16,384]{2,1,0:T(8,128)(2,1)}, bf16[16,16,384]{2,1,0:T(8,128)(2,1)}, u32[]{:S(2)}, u32[]{:S(2)}) collective-permute-start(bf16[16,16,384]{2,1,0:T(8,128)(2,1)} %get-tuple-element.37), channel_id=1, source_target_pairs={{0,16},{1,17},{2,18},{3,19},{4,20},{5,21},{6,22},{7,23},{8,24},{9,... | collective-permute-start | bytes 589832 | tf_op jit(solution)/shard_map/ppermute | solution.py:91
  9.8 15.9 %collective-permute-start.2 = (bf16[16,16,512]{2,1,0:T(8,128)(2,1)}, bf16[16,16,512]{2,1,0:T(8,128)(2,1)}, u32[]{:S(2)}, u32[]{:S(2)}) collective-permute-start(bf16[16,16,512]{2,1,0:T(8,128)(2,1)} %get-tuple-element.42), channel_id=1, source_target_pairs={{0,16},{1,17},{2,18},{3,19},{4,20},{5,21},{6,22},{7,23},{8,24},{9,... | collective-permute-start | bytes 786440 | tf_op jit(solution)/shard_map/ppermute | solution.py:91
  14.1 9.2 %copy-start.2 = (bf16[2,8,16,16,128]{4,3,2,1,0:T(8,128)(2,1)S(1)}, bf16[2,8,16,16,128]{4,3,2,1,0:T(8,128)(2,1)}, u32[]{:S(2)}) copy-start(bf16[2,8,16,16,128]{4,3,2,1,0:T(8,128)(2,1)} %vec.11) | copy-start | bytes 3145732
  17.9 1.4 %copy-start = (bf16[2,736,768]{2,1,0:T(8,128)(2,1)}, bf16[2,736,768]{2,1,0:T(8,128)(2,1)S(1)}, u32[]{:S(2)}) copy-start(bf16[2,736,768]{2,1,0:T(8,128)(2,1)S(1)} %order_cells.3.refs_1_) | copy-start | bytes 6782980
  19.3 4.0 %copy-start.1 = (bf16[2,736,768]{2,1,0:T(8,128)(2,1)S(1)}, bf16[2,736,768]{2,1,0:T(8,128)(2,1)}, u32[]{:S(2)}) copy-start(bf16[2,736,768]{2,1,0:T(8,128)(2,1)} %copy-done) | copy-start | bytes 6782980
  19.3 6.4 %collective-permute-start.3 = (bf16[1,16,896]{2,1,0:T(8,128)(2,1)S(1)}, bf16[1,16,896]{2,1,0:T(8,128)(2,1)S(1)}, u32[]{:S(2)}, u32[]{:S(2)}) collective-permute-start(bf16[1,16,896]{2,1,0:T(8,128)(2,1)S(1)} %slice.4), channel_id=1, source_target_pairs={{0,16},{1,17},{2,18},{3,19},{4,20},{5,21},{6,22},{7,23},{8,24},{9,... | collective-permute-start | bytes 86024 | tf_op jit(solution)/shard_map/ppermute | solution.py:91
  27.4 8.6 %collective-permute-start.4 = (bf16[2,2,17,16,128]{4,3,2,1,0:T(8,128)(2,1)S(1)}, bf16[2,2,17,16,128]{4,3,2,1,0:T(8,128)(2,1)S(1)}, u32[]{:S(2)}, u32[]{:S(2)}) collective-permute-start(bf16[2,2,17,16,128]{4,3,2,1,0:T(8,128)(2,1)S(1)} %get-tuple-element.47), channel_id=1, source_target_pairs={{0,16},{1,17},{2,18},{3,19},{4,20},{5,21},{6,22},{7,23},{8,24},{9,... | collective-permute-start | bytes 835592 | tf_op jit(solution)/shard_map/ppermute | solution.py:91
  28.1 1.3 %collective-permute-start.5 = (bf16[2,9,16,128]{3,2,1,0:T(8,128)(2,1)S(1)}, bf16[2,9,16,128]{3,2,1,0:T(8,128)(2,1)S(1)}, u32[]{:S(2)}, u32[]{:S(2)}) collective-permute-start(bf16[2,9,16,128]{3,2,1,0:T(8,128)(2,1)S(1)} %get-tuple-element.48), channel_id=1, source_target_pairs={{0,1},{1,0},{2,3},{3,2},{4,5},{5,4},{6,7},{7,6},{8,9},{9,8},{10,11... | collective-permute-start | bytes 221192 | tf_op jit(solution)/shard_map/ppermute | solution.py:102
  28.1 6.5 %collective-permute-start.6 = (bf16[2,9,16,128]{3,2,1,0:T(8,128)(2,1)S(1)}, bf16[2,9,16,128]{3,2,1,0:T(8,128)(2,1)S(1)}, u32[]{:S(2)}, u32[]{:S(2)}) collective-permute-start(bf16[2,9,16,128]{3,2,1,0:T(8,128)(2,1)S(1)} %get-tuple-element.49), channel_id=1, source_target_pairs={{0,15},{1,2},{2,1},{3,4},{4,3},{5,6},{6,5},{7,8},{8,7},{9,10},{10,... | collective-permute-start | bytes 221192 | tf_op jit(solution)/shard_map/ppermute | solution.py:108
  34.6 4.2 %collective-permute-start.7 = (bf16[2,2,2,16,128]{4,3,2,1,0:T(8,128)(2,1)S(1)}, bf16[2,2,2,16,128]{4,3,2,1,0:T(8,128)(2,1)S(1)}, u32[]{:S(2)}, u32[]{:S(2)}) collective-permute-start(bf16[2,2,2,16,128]{4,3,2,1,0:T(8,128)(2,1)S(1)} %corner_pack.2), channel_id=1, source_target_pairs={{0,16},{1,17},{2,18},{3,19},{4,20},{5,21},{6,22},{7,23},{8,24},{9,... | collective-permute-start | bytes 98312 | tf_op jit(solution)/shard_map/ppermute | solution.py:91
  38.8 3.1 %copy-start.3 = (bf16[8,16,16,512]{3,2,1,0:T(8,128)(2,1)S(1)}, bf16[8,16,16,512]{3,2,1,0:T(8,128)(2,1)}, u32[]{:S(2)}) copy-start(bf16[8,16,16,512]{3,2,1,0:T(8,128)(2,1)} %res_hbm.1) | copy-start | bytes 6291460
  40.8 8.6 %collective-permute-start.8 = (bf16[2,2,17,16,128]{4,3,2,1,0:T(8,128)(2,1)S(1)}, bf16[2,2,17,16,128]{4,3,2,1,0:T(8,128)(2,1)S(1)}, u32[]{:S(2)}, u32[]{:S(2)}) collective-permute-start(bf16[2,2,17,16,128]{4,3,2,1,0:T(8,128)(2,1)S(1)} %get-tuple-element.52), channel_id=1, source_target_pairs={{0,16},{1,17},{2,18},{3,19},{4,20},{5,21},{6,22},{7,23},{8,24},{9,... | collective-permute-start | bytes 835592 | tf_op jit(solution)/shard_map/ppermute | solution.py:91
  42.0 6.5 %collective-permute-start.10 = (bf16[2,9,16,128]{3,2,1,0:T(8,128)(2,1)S(1)}, bf16[2,9,16,128]{3,2,1,0:T(8,128)(2,1)S(1)}, u32[]{:S(2)}, u32[]{:S(2)}) collective-permute-start(bf16[2,9,16,128]{3,2,1,0:T(8,128)(2,1)S(1)} %get-tuple-element.54), channel_id=1, source_target_pairs={{0,15},{1,2},{2,1},{3,4},{4,3},{5,6},{6,5},{7,8},{8,7},{9,10},{10,... | collective-permute-start | bytes 221192 | tf_op jit(solution)/shard_map/ppermute | solution.py:108
  42.0 6.5 %collective-permute-start.9 = (bf16[2,9,16,128]{3,2,1,0:T(8,128)(2,1)S(1)}, bf16[2,9,16,128]{3,2,1,0:T(8,128)(2,1)S(1)}, u32[]{:S(2)}, u32[]{:S(2)}) collective-permute-start(bf16[2,9,16,128]{3,2,1,0:T(8,128)(2,1)S(1)} %get-tuple-element.53), channel_id=1, source_target_pairs={{0,1},{1,0},{2,3},{3,2},{4,5},{5,4},{6,7},{7,6},{8,9},{9,8},{10,11... | collective-permute-start | bytes 221192 | tf_op jit(solution)/shard_map/ppermute | solution.py:102
  48.4 4.0 %collective-permute-start.11 = (bf16[2,2,2,16,128]{4,3,2,1,0:T(8,128)(2,1)S(1)}, bf16[2,2,2,16,128]{4,3,2,1,0:T(8,128)(2,1)S(1)}, u32[]{:S(2)}, u32[]{:S(2)}) collective-permute-start(bf16[2,2,2,16,128]{4,3,2,1,0:T(8,128)(2,1)S(1)} %corner_pack.3), channel_id=1, source_target_pairs={{0,16},{1,17},{2,18},{3,19},{4,20},{5,21},{6,22},{7,23},{8,24},{9,... | collective-permute-start | bytes 98312 | tf_op jit(solution)/shard_map/ppermute | solution.py:91
  56.3 0.9 %copy-start.4 = (f32[2,16,16,128]{3,2,1,0:T(8,128)}, f32[2,16,16,128]{3,2,1,0:T(8,128)S(1)}, u32[]{:S(2)}) copy-start(f32[2,16,16,128]{3,2,1,0:T(8,128)S(1)} %get-tuple-element.60.edge_x) | copy-start | bytes 786436
  56.3 5.4 %copy-start.7 = (f32[2,7,16,128]{3,2,1,0:T(8,128)}, f32[2,7,16,128]{3,2,1,0:T(8,128)S(1)}, u32[]{:S(2)}) copy-start(f32[2,7,16,128]{3,2,1,0:T(8,128)S(1)} %get-tuple-element.61.edge_y) | copy-start | bytes 344068
  57.1 3.8 %collective-permute-start.12 = (bf16[256,256]{1,0:T(8,128)(2,1)S(1)}, bf16[256,256]{1,0:T(8,128)(2,1)S(1)}, u32[]{:S(2)}, u32[]{:S(2)}) collective-permute-start(bf16[256,256]{1,0:T(8,128)(2,1)S(1)} %get-tuple-element.65), channel_id=1, source_target_pairs={{0,1},{1,0},{2,3},{3,2},{4,5},{5,4},{6,7},{7,6},{8,9},{9,8},{10,11... | collective-permute-start | bytes 393224 | tf_op jit(solution)/shard_map/ppermute | solution.py:102
  57.2 3.7 %collective-permute-start.13 = (bf16[2,16,128]{2,1,0:T(8,128)(2,1)S(1)}, bf16[2,16,128]{2,1,0:T(8,128)(2,1)S(1)}, u32[]{:S(2)}, u32[]{:S(2)}) collective-permute-start(bf16[2,16,128]{2,1,0:T(8,128)(2,1)S(1)} %get-tuple-element.67), channel_id=1, source_target_pairs={{0,16},{1,17},{2,18},{3,19},{4,20},{5,21},{6,22},{7,23},{8,24},{9,... | collective-permute-start | bytes 24584 | tf_op jit(solution)/shard_map/ppermute | solution.py:91
  61.7 0.6 copy-start.6
  62.3 13.8 %all-to-all-start = ((bf16[16,32,256]{2,1,0:T(8,128)(2,1)}), bf16[16,32,256]{2,1,0:T(8,128)(2,1)S(1)}, u32[]{:S(2)}, u32[]{:S(2)}) async-start(bf16[16,32,256]{2,1,0:T(8,128)(2,1)} %bitcast.3), calls=%async_computation | async-start | bytes 524288 | tf_op jit(solution)/shard_map/all_to_all | solution.py:732
  65.9 9.0 %collective-permute-start.14 = (bf16[2,16,16,128]{3,2,1,0:T(8,128)(2,1)}, bf16[2,16,16,128]{3,2,1,0:T(8,128)(2,1)S(1)}, u32[]{:S(2)}, u32[]{:S(2)}) collective-permute-start(bf16[2,16,16,128]{3,2,1,0:T(8,128)(2,1)} %copy-done.6), channel_id=1, source_target_pairs={{0,16},{1,17},{2,18},{3,19},{4,20},{5,21},{6,22},{7,23},{8,24},{9,... | collective-permute-start | bytes 393224 | tf_op jit(solution)/shard_map/ppermute | solution.py:91
  67.7 7.1 %collective-permute-start.15 = (bf16[2,8,16,128]{3,2,1,0:T(8,128)(2,1)S(1)}, bf16[2,8,16,128]{3,2,1,0:T(8,128)(2,1)S(1)}, u32[]{:S(2)}, u32[]{:S(2)}) collective-permute-start(bf16[2,8,16,128]{3,2,1,0:T(8,128)(2,1)S(1)} %get-tuple-element.70), channel_id=1, source_target_pairs={{0,1},{1,2},{2,3},{3,4},{4,5},{5,6},{6,7},{7,8},{8,9},{9,10},{10,1... | collective-permute-start | bytes 196616 | tf_op jit(solution)/shard_map/ppermute | solution.py:91
  76.1 1.0 %copy-start.5 = (f32[2,16,16,128]{3,2,1,0:T(8,128)S(1)}, f32[2,16,16,128]{3,2,1,0:T(8,128)}, u32[]{:S(2)}) copy-start(f32[2,16,16,128]{3,2,1,0:T(8,128)} %copy-done.4) | copy-start | bytes 786436
  77.1 0.9 %copy-start.8 = (f32[2,7,16,128]{3,2,1,0:T(8,128)S(1)}, f32[2,7,16,128]{3,2,1,0:T(8,128)}, u32[]{:S(2)}) copy-start(f32[2,7,16,128]{3,2,1,0:T(8,128)} %copy-done.7) | copy-start | bytes 344068

commit v13 on v12

--- a/solution.py
+++ b/solution.py
@@ -472,8 +472,8 @@
                  last_x, last_field, acc_in, face_in, near_in, far_in, corner_in, prod_ref, y_ref,
                  y_corner, new_ref, *refs):
     mats = refs[:n_mat]
-    out_hbm, edge_x, edge_y, face, side, corner, rows_ref = refs[n_mat : n_mat + 7]
-    part_ref, sem, acc_ref, small_ref, tail_ref = refs[n_mat + 7 :]
+    out_hbm, face_hbm, side_hbm, rows_ref = refs[n_mat : n_mat + 4]
+    part_ref, face, side, sem, acc_ref, small_ref, tail_ref = refs[n_mat + 4 :]
     nodes = Nodes(sz, vec, from_x, from_y, own_inv, own_pot, ghost_x, ghost_y, last_field)
     sums = Sums(sz, even_ref[0] == 0, acc_in, face_in, near_in, far_in, corner_in)
     u_corner, new_corner = [], []
@@ -498,10 +498,8 @@
                 rounded = value.astype(bf16)
                 if j < sz.ey:
                     face[:, j] = rounded
-                elif i < sz.ex:
-                    side[:, i] = value
                 else:
-                    corner[...] = rounded
+                    side[:, i] = rounded
                 put_row(sz.own_edges + (j if j < sz.ey else sz.ey + i), rounded)
                 continue
             at = sz.corner(i, j)
@@ -510,16 +508,16 @@
             image = inv * acc + nodes.pot(i, j) * new
             value = 2.0 * (image - center_shift * new) / half_width - old
             part_ref[:, i, j] = value
-            if i == 0:
-                edge_x[:, j] = value
-            elif j == 0:
-                edge_y[:, i - 1] = value
             put_row(i * sz.ey + j, value.astype(bf16))
         if i < sz.ex:
             copies.append(pltpu.make_async_copy(part_ref.at[:, i], out_hbm.at[:, i], sem.at[i]))
             copies[-1].start()
     for at in range(sz.own_edges + sz.ey + sz.gx, sz.edges):
         rows_ref[at] = jnp.zeros((sz.ez, sz.full), bf16)
+    copies.append(pltpu.make_async_copy(face, face_hbm, sem.at[sz.ex]))
+    copies.append(pltpu.make_async_copy(side, side_hbm, sem.at[sz.ex + 1]))
+    for copy in copies[-2:]:
+        copy.start()
     for copy in copies:
         copy.wait()
 
@@ -532,38 +530,33 @@
         out[...] = (local * norm_scale).astype(out.dtype)
 
 
-def ready_kernel(sz, keep, taken, side_ref, corner_ref, face_in, pieces, out_ref, face_out):
-    del face_in, face_out
+def pieces_kernel(keep, taken, pieces):
     rows = pieces.shape[2]
     for at in range(pieces.shape[1]):
         span = slice(at * rows, (at + 1) * rows)
         value = (keep[span] + taken[span].astype(f32)).astype(pieces.dtype)
         for copy in range(pieces.shape[0]):
             pieces[copy, at] = value
-    for i in range(sz.ex):
-        value = side_ref[:, i]
-        if i == 0:
-            value = value + corner_ref[...].astype(f32)
-        out_ref[:, i] = value.astype(out_ref.dtype)
-
-
-def last_kernel(sz, old_hbm, edge_x, edge_y, face, side, pieces, out_hbm, margin, at_x, at_y, sems):
+
+
+def last_kernel(sz, old_hbm, face, side, corner, pieces, out_hbm, margin, at_x, at_y, sems):
     del old_hbm
-    for j in range(sz.ey):
-        value = edge_x[:, j] + face[:, j].astype(f32)
-        if j == 0:
-            value = value + side[:, 0].astype(f32)
-        at_x[:, j] = value
-    for i in range(1, sz.ex):
-        at_y[:, i - 1] = edge_y[:, i - 1] + side[:, i].astype(f32)
-    copies = [
-        pltpu.make_async_copy(at_x, out_hbm.at[:, 0], sems.at[0]),
-        pltpu.make_async_copy(at_y, out_hbm.at[:, pl.ds(1, sz.ex - 1), 0], sems.at[1]),
-    ]
-    for copy in copies:
+    pairs = [(at_x, out_hbm.at[:, 0]), (at_y, out_hbm.at[:, pl.ds(1, sz.ex - 1), 0])]
+    loads = [pltpu.make_async_copy(b, a, sems.at[k]) for k, (a, b) in enumerate(pairs)]
+    stores = [pltpu.make_async_copy(a, b, sems.at[k]) for k, (a, b) in enumerate(pairs)]
+    for copy in loads:
         copy.start()
     margin[...] = sum(pieces[at].astype(f32) for at in range(pieces.shape[0]))
-    for copy in copies:
+    for copy in loads:
+        copy.wait()
+    at_x[:, 0] += side[:, 0].astype(f32) + corner[:, 0].astype(f32)
+    for j in range(sz.ey):
+        at_x[:, j] += face[:, j].astype(f32)
+    for i in range(1, sz.ex):
+        at_y[:, i - 1] += side[:, i].astype(f32)
+    for copy in stores:
+        copy.start()
+    for copy in stores:
         copy.wait()
 
 
@@ -704,42 +697,44 @@
         [products, state_grid], main_scratch,
         [parity, *state, acc, *got, y1, *mats], scalar_first=True,
     )
-    filtered, edge_x, edge_y, face, side, corner, rows = call(
+    filtered, face, side, rows = call(
         functools.partial(third_corner, sz, n_mat), "third_corner", small_flops,
         [
-            like(own, f32), like((blocks, sz.ey) + tile, f32), like((blocks, sz.ex - 1) + tile, f32),
-            like((blocks, sz.ey) + tile, bf16), like((blocks, sz.ex) + tile, f32), like(sz.edge, bf16),
+            like(own, f32), like((blocks, sz.ey) + tile, bf16), like((blocks, sz.gx) + tile, bf16),
             like((sz.edges, ez, full), bf16),
         ],
-        [pltpu.VMEM(own, f32), pltpu.SemaphoreType.DMA((sz.ex,)), pltpu.VMEM(grid, f32)] + corner_scratch,
+        [
+            pltpu.VMEM(own, f32), pltpu.VMEM((blocks, sz.ey) + tile, bf16),
+            pltpu.VMEM((blocks, sz.gx) + tile, bf16), pltpu.SemaphoreType.DMA((sz.ex + 2,)),
+            pltpu.VMEM(grid, f32),
+        ] + corner_scratch,
         [parity, *state, *ends, acc, *got, corner, prod, y1, y1_corner, y2, *mats],
-        scalar_first=True, out_hbm=1,
-    )
-    corner = send(corner, 1, 0)
+        scalar_first=True, out_hbm=3,
+    )
     give, keep = call(
         functools.partial(margin_kernel, sz, norm_scale), "margin", 2 * res_count * sz.edges * ez * full,
         [like((res_count // 2, full), bf16), like((res_count // 2, full), f32)], [],
         [parity, turned, rows], scalar_first=True,
     )
 
-    pieces, side, face = call(
-        functools.partial(ready_kernel, sz), "ready", 0,
-        [like((nx, ny // 2, res_count // ny, full), bf16), like((blocks, sz.ex) + tile, bf16), face],
-        [], [keep, send_near(give), side, corner, face], aliases={4: 2},
+    (pieces,) = call(
+        pieces_kernel, "pieces", 0, [like((nx, ny // 2, res_count // ny, full), bf16)], [],
+        [keep, send_near(give)],
     )
     pieces = pieces.reshape(nx * ny // 2, -1, full)
     groups = [[a * ny + b for a in range(nx) for b in range(c, ny, 2)] for c in range(2)]
     pieces = lax.all_to_all(pieces, ("dx", "dy"), 0, 0, axis_index_groups=groups)
 
+    side = send(side, 0, 1)
+    corner = send(side[:, sz.ex :], 1, 0)
     face = send(face, 1, 0)
-    side = send(side, 0, 1)
     filtered, margin = call(
         functools.partial(last_kernel, sz), "last", 0, [like(own, f32), like(pieces.shape[1:], f32)],
         [
             pltpu.VMEM((blocks, sz.ey) + tile, f32), pltpu.VMEM((blocks, sz.ex - 1) + tile, f32),
             pltpu.SemaphoreType.DMA((2,)),
         ],
-        [filtered, edge_x, edge_y, face, side, pieces], hbm=1, out_hbm=1, aliases={0: 0},
+        [filtered, face, side, corner, pieces], hbm=1, out_hbm=1, aliases={0: 0},
     )
     return (filtered, margin)
 

time: 80.1 us -> 80 us (level)
  local copies, waits for them, and re-layouts: 6.26 us -> 3.79 us
  Pallas kernels: 30.3 us -> 31.3 us
  waiting for transfers between devices: 21.4 us -> 22.4 us
    unnamed x20 -> x14, local copies, waits for them, and re-layouts: 3.91 us -> 1.44 us
    ppermute x3, waiting for transfers between devices: 0.52 us -> 1.86 us  [send_near(): return lax.ppermute(value, 'dy', pairs)]
    all_to_all x1, waiting for transfers between devices: 1.29 us -> 0.01 us  [body(): lax.all_to_all(pieces, ('dx', 'dy'), 0, 0, axis_index_groups=groups)]
    pallas_call x15, Pallas kernels: 30.3 us -> 31.3 us  [call(): pl.pallas_call(kernel, in_specs=specs, out_specs=out_specs, out_shape=out...]
    ppermute x11, waiting for transfers between devices: 9.74 us -> 10.7 us  [send(): return lax.ppermute(value, ('dx', 'dy'), pairs)]
where the time goes in v13:
time: 80 us; the launch traced here: 79.5 us
  Pallas kernels  31.3 us (39%)
  waiting for transfers between devices  22.4 us (28%)
  starting transfers between devices  21.1 us (26%)
  local copies, waits for them, and re-layouts  3.79 us (5%)
  between operations  1.02 us (1%)
    pallas_call x15, Pallas kernels, call(): pl.pallas_call(kernel, in_specs=specs, out_specs=out_specs, out_shape=out...  31.3 us
    ppermute x11, starting transfers between devices, send(): return lax.ppermute(value, ('dx', 'dy'), pairs)  16.7 us
    ppermute x11, waiting for transfers between devices, send(): return lax.ppermute(value, ('dx', 'dy'), pairs)  10.7 us
    ppermute x2, waiting for transfers between devices, swap_y(): far = lax.ppermute(far, 'dy', far_pairs)  9.82 us
    all_to_all x1, starting transfers between devices, body(): lax.all_to_all(pieces, ('dx', 'dy'), 0, 0, axis_index_groups=groups)  3.53 us
    ppermute x3, waiting for transfers between devices, send_near(): return lax.ppermute(value, 'dy', pairs)  1.86 us
  transfers between devices with their start and end apart: 17, of which 6 were waited for; matrix products, arithmetic and copies ran while one was open for 3% of the time, Pallas kernels for 22%

profile of v13, /device:TPU:0, one launch (start us, length us, event | category | flops | bytes accessed | tf_op | source)
XLA Modules:
  0.0 79.5 jit_solution(16150569481782915887)
XLA Ops:
  0.6 2.1 %pack.1 = (bf16[16,16,384]{2,1,0:T(8,128)(2,1)}, bf16[8,16,896]{2,1,0:T(8,128)(2,1)}, bf16[16,16,512]{2,1,0:T(8,128)(2,1)}, s32[4,729]{1,0:T(4,128)S(1)}) custom-call(bf16[2,8,16,16,128]{4,3,2,1,0:T(8,128)(2,1)} %vec.11, bf16[8,16,16,512]{3,2,1,0:T(8,128)(2,1)} %res_hbm.1, f32[8,16,16]{2,1,0:T(8,128)} %inv_hbm.1, f32[8,16,16]{2,1,0:T(8,128)} %pot_hbm.1, ...), custom_call_target="tpu_custom_call" | custom-call | bytes 3873568 | tf_op jit(solution)/shard_map/pack/pallas_call | solution.py:583
  2.8 5.5 %collective-permute-start.1 = (bf16[8,16,896]{2,1,0:T(8,128)(2,1)}, bf16[8,16,896]{2,1,0:T(8,128)(2,1)S(1)}, u32[]{:S(2)}, u32[]{:S(2)}) collective-permute-start(bf16[8,16,896]{2,1,0:T(8,128)(2,1)} %get-tuple-element.32), channel_id=1, source_target_pairs={{0,15},{1,0},{2,1},{3,2},{4,3},{5,4},{6,5},{7,6},{8,7},{9,8},{10,9... | collective-permute-start | bytes 688136 | tf_op jit(solution)/shard_map/ppermute | solution.py:91
  8.2 1.5 %collective-permute-start = (bf16[16,16,384]{2,1,0:T(8,128)(2,1)}, bf16[16,16,384]{2,1,0:T(8,128)(2,1)}, u32[]{:S(2)}, u32[]{:S(2)}) collective-permute-start(bf16[16,16,384]{2,1,0:T(8,128)(2,1)} %get-tuple-element.31), channel_id=1, source_target_pairs={{0,16},{1,17},{2,18},{3,19},{4,20},{5,21},{6,22},{7,23},{8,24},{9,... | collective-permute-start | bytes 589832 | tf_op jit(solution)/shard_map/ppermute | solution.py:91
  9.8 0.5 collective-permute-start.2
  10.3 3.8 %order_cells.2.refs_0_ = bf16[2,736,768]{2,1,0:T(8,128)(2,1)S(1)} custom-call(bf16[729,729]{1,0:T(8,128)(2,1)S(1)} %copy-done.4, s32[4,729]{1,0:T(4,128)S(1)} %get-tuple-element.33.conn_ref), custom_call_target="tpu_custom_call" | custom-call | flops 3623878656 | bytes 3335538 | tf_op jit(solution)/shard_map/order_cells/pallas_call | solution.py:583
  14.1 0.0 copy-start.2
  14.1 3.8 %order_cells.3.refs_1_ = bf16[2,736,768]{2,1,0:T(8,128)(2,1)S(1)} custom-call(bf16[729,729]{1,0:T(8,128)(2,1)S(1)} %copy-done.4, s32[4,729]{1,0:T(4,128)S(1)} %get-tuple-element.33.conn_ref), custom_call_target="tpu_custom_call" | custom-call | flops 3623878656 | bytes 3335538 | tf_op jit(solution)/shard_map/order_cells/pallas_call | solution.py:583
  17.9 1.4 %copy-done = bf16[2,736,768]{2,1,0:T(8,128)(2,1)} copy-done((bf16[2,736,768]{2,1,0:T(8,128)(2,1)}, bf16[2,736,768]{2,1,0:T(8,128)(2,1)S(1)}, u32[]{:S(2)}) %copy-start) | copy-done | bytes 2261016
  19.3 0.0 collective-permute-done.1.from_y
  19.3 1.6 %collective-permute-start.3 = (bf16[1,16,896]{2,1,0:T(8,128)(2,1)S(1)}, bf16[1,16,896]{2,1,0:T(8,128)(2,1)S(1)}, u32[]{:S(2)}, u32[]{:S(2)}) collective-permute-start(bf16[1,16,896]{2,1,0:T(8,128)(2,1)S(1)} %slice.8), channel_id=1, source_target_pairs={{0,16},{1,17},{2,18},{3,19},{4,20},{5,21},{6,22},{7,23},{8,24},{9,... | collective-permute-start | bytes 86024 | tf_op jit(solution)/shard_map/ppermute | solution.py:91
  20.9 0.0 collective-permute-done.from_x
  20.9 1.2 %broadcast_in_dim.4.own_inv = f32[8,16,16,128]{3,2,1,0:T(8,128)S(1)} broadcast(f32[8,16,16]{2,1,0:T(8,128)} %inv_hbm.1), dimensions={0,1,2} | broadcast | bytes 1056768 | tf_op jit(solution)/shard_map/broadcast_in_dim | solution.py:630
  22.1 1.2 %broadcast_in_dim.5.own_pot = f32[8,16,16,128]{3,2,1,0:T(8,128)S(1)} broadcast(f32[8,16,16]{2,1,0:T(8,128)} %pot_hbm.1), dimensions={0,1,2} | broadcast | bytes 1056768 | tf_op jit(solution)/shard_map/broadcast_in_dim | solution.py:631
  23.3 2.4 %first_main.1 = (f32[4,736,256]{2,1,0:T(8,128)S(1)}, f32[2,16,16,128]{3,2,1,0:T(8,128)S(1)}, f32[2,8,16,128]{3,2,1,0:T(8,128)S(1)}) custom-call(bf16[2,8,16,16,128]{4,3,2,1,0:T(8,128)(2,1)S(1)} %copy-done.2, bf16[16,16,384]{2,1,0:T(8,128)(2,1)} %collective-permute-done.from_x, bf16[8,16,896]{2,1,0:T(8,128)(2,1)S(1)} %collective-permute-done.1.from_y, ...), custom_call_target="tpu_custom_call" | custom-call | flops 1157627904 | bytes 11501568 | tf_op jit(solution)/shard_map/first_main/pallas_call | solution.py:583
  25.7 0.0 collective-permute-done.3.corner
  25.7 0.0 collective-permute-done.2.res_in
  25.7 1.8 %first_corner.1 = (bf16[16,16,512]{2,1,0:T(8,128)(2,1)}, f32[2,9,17,16,128]{4,3,2,1,0:T(8,128)S(1)}, bf16[2,2,17,16,128]{4,3,2,1,0:T(8,128)(2,1)S(1)}, bf16[2,9,...) custom-call(s32[1]{0:T(128)} %bitcast.even_ref, ...), custom_call_target="tpu_custom_call", output_to_operand_aliasing={{0}: (1, {})} | custom-call | flops 192937984 | bytes 15020036 | tf_op jit(solution)/shard_map/first_corner/pallas_call | solution.py:583
  27.5 0.7 collective-permute-start.4
  28.1 0.0 collective-permute-start.5
  28.1 0.7 collective-permute-start.6
  28.9 0.5 collective-permute-done.5.near.near_in
  29.4 5.2 %collective-permute-done.6.far.far_in = bf16[2,9,16,128]{3,2,1,0:T(8,128)(2,1)S(1)} collective-permute-done((bf16[2,9,16,128]{3,2,1,0:T(8,128)(2,1)S(1)}, bf16[2,9,16,128]{3,2,1,0:T(8,128)(2,1)S(1)}, u32[]{:S(2)}, u32[]{:S(2)}) %collective-permute-start.6) | collective-permute-done | bytes 73760 | tf_op jit(solution)/shard_map/ppermute | solution.py:108
  34.6 1.4 %collective-permute-start.7 = (bf16[2,2,2,16,128]{4,3,2,1,0:T(8,128)(2,1)S(1)}, bf16[2,2,2,16,128]{4,3,2,1,0:T(8,128)(2,1)S(1)}, u32[]{:S(2)}, u32[]{:S(2)}) collective-permute-start(bf16[2,2,2,16,128]{4,3,2,1,0:T(8,128)(2,1)S(1)} %corner_pack.2), channel_id=1, source_target_pairs={{0,16},{1,17},{2,18},{3,19},{4,20},{5,21},{6,22},{7,23},{8,24},{9,... | collective-permute-start | bytes 98312 | tf_op jit(solution)/shard_map/ppermute | solution.py:91
  36.0 0.0 collective-permute-done.4.face_in
  36.0 2.8 %second_main.1 = (f32[4,736,256]{2,1,0:T(8,128)S(1)}, f32[2,9,17,16,128]{4,3,2,1,0:T(8,128)S(1)}) custom-call(s32[1]{0:T(128)} %bitcast.even_ref, bf16[2,8,16,16,128]{4,3,2,1,0:T(8,128)(2,1)S(1)} %copy-done.2, bf16[16,16,384]{2,1,0:T(8,128)(2,1)} %collective-permute-done.from_x, bf16[8,16,896]{2,1,0:T(8,128)(2,1)S(1)} %collective-permute-done.1.from_y, ...), custom_call_target="tpu_custom_call" | custom-call | flops 1157627904 | bytes 16941060 | tf_op jit(solution)/shard_map/second_main/pallas_call | solution.py:583
  38.9 0.0 collective-permute-done.7.corner_in
  38.9 0.0 copy-start.3
  38.9 2.0 %second_corner.1 = (f32[2,9,17,16,128]{4,3,2,1,0:T(8,128)S(1)}, bf16[2,2,17,16,128]{4,3,2,1,0:T(8,128)(2,1)S(1)}, bf16[2,9,16,128]{3,2,1,0:T(8,128)(2,1)S(1)}, b...) custom-call(s32[1]{0:T(128)} %bitcast.even_ref, bf16[2,8,16,16,128]{4,3,2,1,0:T(8,128)(2,1)S(1)} %copy-done.2, ...), custom_call_target="tpu_custom_call" | custom-call | flops 192937984 | bytes 17498116 | tf_op jit(solution)/shard_map/second_corner/pallas_call | solution.py:583
  40.9 1.1 %collective-permute-start.8 = (bf16[2,2,17,16,128]{4,3,2,1,0:T(8,128)(2,1)S(1)}, bf16[2,2,17,16,128]{4,3,2,1,0:T(8,128)(2,1)S(1)}, u32[]{:S(2)}, u32[]{:S(2)}) collective-permute-start(bf16[2,2,17,16,128]{4,3,2,1,0:T(8,128)(2,1)S(1)} %get-tuple-element.46), channel_id=1, source_target_pairs={{0,16},{1,17},{2,18},{3,19},{4,20},{5,21},{6,22},{7,23},{8,24},{9,... | collective-permute-start | bytes 835592 | tf_op jit(solution)/shard_map/ppermute | solution.py:91
  42.0 0.0 collective-permute-start.10
  42.0 0.0 collective-permute-start.9
  42.0 1.9 %turn_residents.1.turned = bf16[2,256,2560]{2,1,0:T(8,128)(2,1)S(1)} custom-call(bf16[2048,512]{1,0:T(8,128)(2,1)S(1)} %bitcast.4, bf16[16,16,512]{2,1,0:T(8,128)(2,1)} %get-tuple-element.56.res_x, bf16[8,16,896]{2,1,0:T(8,128)(2,1)S(1)} %collective-permute-done.1.from_y, bf16[1,16,896]{2,1,0:T(8,128)(2,1)S(1)} %collective-permute-done.3.corner), custom_call_target="tpu_custom_call" | custom-call | flops 578813952 | bytes 5238784 | tf_op jit(solution)/shard_map/turn_residents/pallas_call | solution.py:583
  43.9 4.6 %collective-permute-done.10.far.far_in = bf16[2,9,16,128]{3,2,1,0:T(8,128)(2,1)S(1)} collective-permute-done((bf16[2,9,16,128]{3,2,1,0:T(8,128)(2,1)S(1)}, bf16[2,9,16,128]{3,2,1,0:T(8,128)(2,1)S(1)}, u32[]{:S(2)}, u32[]{:S(2)}) %collective-permute-start.10) | collective-permute-done | bytes 73760 | tf_op jit(solution)/shard_map/ppermute | solution.py:108
  48.5 0.0 collective-permute-done.9.near.near_in
  48.5 1.0 %collective-permute-start.11 = (bf16[2,2,2,16,128]{4,3,2,1,0:T(8,128)(2,1)S(1)}, bf16[2,2,2,16,128]{4,3,2,1,0:T(8,128)(2,1)S(1)}, u32[]{:S(2)}, u32[]{:S(2)}) collective-permute-start(bf16[2,2,2,16,128]{4,3,2,1,0:T(8,128)(2,1)S(1)} %corner_pack.3), channel_id=1, source_target_pairs={{0,16},{1,17},{2,18},{3,19},{4,20},{5,21},{6,22},{7,23},{8,24},{9,... | collective-permute-start | bytes 98312 | tf_op jit(solution)/shard_map/ppermute | solution.py:91
  49.4 0.0 collective-permute-done.8.face_in
  49.4 3.0 %third_main.1 = (f32[4,736,256]{2,1,0:T(8,128)S(1)}, f32[2,9,17,16,128]{4,3,2,1,0:T(8,128)S(1)}) custom-call(s32[1]{0:T(128)} %bitcast.even_ref, bf16[2,8,16,16,128]{4,3,2,1,0:T(8,128)(2,1)S(1)} %copy-done.2, bf16[16,16,384]{2,1,0:T(8,128)(2,1)} %collective-permute-done.from_x, bf16[8,16,896]{2,1,0:T(8,128)(2,1)S(1)} %collective-permute-done.1.from_y, ...), custom_call_target="tpu_custom_call" | custom-call | flops 1157627904 | bytes 19447812 | tf_op jit(solution)/shard_map/third_main/pallas_call | solution.py:583
  52.5 3.8 %third_corner.1 = (f32[2,8,16,16,128]{4,3,2,1,0:T(8,128)}, bf16[2,16,16,128]{3,2,1,0:T(8,128)(2,1)}, bf16[2,9,16,128]{3,2,1,0:T(8,128)(2,1)}, bf16[160,16,256]{2,1,0:T(8,128)(2,1)S(1)}) custom-call(s32[1]{0:T(128)} %bitcast.even_ref, bf16[2,8,16,16,128]{4,3,2,1,0:T(8,128)(2,1)S(1)} %copy-done.2, bf16[16,16,384]{2,1,0:T(8,128)(2,1)} %collective-permute-done.from_x, ...), custom_call_target="tpu_custom_call" | custom-call | flops 192937984 | bytes 23191556 | tf_op jit(solution)/shard_map/third_corner/pallas_call | solution.py:583
  56.4 0.8 %margin.1 = (bf16[256,256]{1,0:T(8,128)(2,1)S(1)}, f32[256,256]{1,0:T(8,128)S(1)}) custom-call(s32[1]{0:T(128)} %bitcast.even_ref, bf16[2,256,2560]{2,1,0:T(8,128)(2,1)S(1)} %turn_residents.1.turned, bf16[160,16,256]{2,1,0:T(8,128)(2,1)S(1)} %get-tuple-element.57.rows_ref), custom_call_target="tpu_custom_call" | custom-call | flops 671088640 | bytes 4325380 | tf_op jit(solution)/shard_map/margin/pallas_call | solution.py:583
  57.2 0.1 collective-permute-start.15
  57.3 1.3 %collective-permute-done.15.taken = bf16[256,256]{1,0:T(8,128)(2,1)S(1)} collective-permute-done((bf16[256,256]{1,0:T(8,128)(2,1)S(1)}, bf16[256,256]{1,0:T(8,128)(2,1)S(1)}, u32[]{:S(2)}, u32[]{:S(2)}) %collective-permute-start.15) | collective-permute-done | bytes 131104 | tf_op jit(solution)/shard_map/ppermute | solution.py:102
  58.6 0.7 pieces.1
  59.3 3.5 %all-to-all-start = ((bf16[16,32,256]{2,1,0:T(8,128)(2,1)}), bf16[16,32,256]{2,1,0:T(8,128)(2,1)S(1)}, u32[]{:S(2)}, u32[]{:S(2)}) async-start(bf16[16,32,256]{2,1,0:T(8,128)(2,1)} %bitcast.3), calls=%async_computation | async-start | bytes 524288 | tf_op jit(solution)/shard_map/all_to_all | solution.py:726
  62.9 1.9 %collective-permute-start.12 = (bf16[2,16,16,128]{3,2,1,0:T(8,128)(2,1)S(1)}, bf16[2,16,16,128]{3,2,1,0:T(8,128)(2,1)S(1)}, u32[]{:S(2)}, u32[]{:S(2)}) collective-permute-start(bf16[2,16,16,128]{3,2,1,0:T(8,128)(2,1)S(1)} %copy-done.5), channel_id=1, source_target_pairs={{0,16},{1,17},{2,18},{3,19},{4,20},{5,21},{6,22},{7,23},{8,24},{9,... | collective-permute-start | bytes 393224 | tf_op jit(solution)/shard_map/ppermute | solution.py:91
  64.8 8.5 %collective-permute-done.13.side = bf16[2,9,16,128]{3,2,1,0:T(8,128)(2,1)S(1)} collective-permute-done((bf16[2,9,16,128]{3,2,1,0:T(8,128)(2,1)S(1)}, bf16[2,9,16,128]{3,2,1,0:T(8,128)(2,1)S(1)}, u32[]{:S(2)}, u32[]{:S(2)}) %collective-permute-start.13) | collective-permute-done | bytes 73760 | tf_op jit(solution)/shard_map/ppermute | solution.py:91
  73.3 1.5 %collective-permute-start.14 = (bf16[2,1,16,128]{3,2,1,0:T(8,128)(2,1)S(1)}, bf16[2,1,16,128]{3,2,1,0:T(8,128)(2,1)S(1)}, u32[]{:S(2)}, u32[]{:S(2)}) collective-permute-start(bf16[2,1,16,128]{3,2,1,0:T(8,128)(2,1)S(1)} %slice.9), channel_id=1, source_target_pairs={{0,16},{1,17},{2,18},{3,19},{4,20},{5,21},{6,22},{7,23},{8,24},{9,... | collective-permute-start | bytes 24584 | tf_op jit(solution)/shard_map/ppermute | solution.py:91
  74.9 2.1 %collective-permute-done.14.corner = bf16[2,1,16,128]{3,2,1,0:T(8,128)(2,1)S(1)} collective-permute-done((bf16[2,1,16,128]{3,2,1,0:T(8,128)(2,1)S(1)}, bf16[2,1,16,128]{3,2,1,0:T(8,128)(2,1)S(1)}, u32[]{:S(2)}, u32[]{:S(2)}) %collective-permute-start.14) | collective-permute-done | bytes 8224 | tf_op jit(solution)/shard_map/ppermute | solution.py:91
  77.0 2.4 %last.1 = (f32[2,8,16,16,128]{4,3,2,1,0:T(8,128)}, f32[32,256]{1,0:T(8,128)}) custom-call(f32[2,8,16,16,128]{4,3,2,1,0:T(8,128)} %get-tuple-element.53.old_hbm, bf16[2,16,16,128]{3,2,1,0:T(8,128)(2,1)S(1)} %collective-permute-done.12.face, bf16[2,9,16,128]{3,2,1,0:T(8,128)(2,1)S(1)} %collective-permute-done.13.side, ...), custom_call_target="tpu_custom_call", output_to_operand_aliasing={{0}: (0, {})} | custom-call | bytes 4702208 | tf_op jit(solution)/shard_map/last/pallas_call | solution.py:583
  (19 shorter events, 0.0 us)
Async XLA Ops:
  0.6 9.6 %copy-start.4 = (bf16[729,729]{1,0:T(8,128)(2,1)S(1)}, bf16[729,729]{1,0:T(8,128)(2,1)}, u32[]{:S(2)}) copy-start(bf16[729,729]{1,0:T(8,128)(2,1)} %matrix_ref.3) | copy-start | bytes 3188650
  2.8 16.5 %collective-permute-start.1 = (bf16[8,16,896]{2,1,0:T(8,128)(2,1)}, bf16[8,16,896]{2,1,0:T(8,128)(2,1)S(1)}, u32[]{:S(2)}, u32[]{:S(2)}) collective-permute-start(bf16[8,16,896]{2,1,0:T(8,128)(2,1)} %get-tuple-element.32), channel_id=1, source_target_pairs={{0,15},{1,0},{2,1},{3,2},{4,3},{5,4},{6,5},{7,6},{8,7},{9,8},{10,9... | collective-permute-start | bytes 688136 | tf_op jit(solution)/shard_map/ppermute | solution.py:91
  8.2 12.6 %collective-permute-start = (bf16[16,16,384]{2,1,0:T(8,128)(2,1)}, bf16[16,16,384]{2,1,0:T(8,128)(2,1)}, u32[]{:S(2)}, u32[]{:S(2)}) collective-permute-start(bf16[16,16,384]{2,1,0:T(8,128)(2,1)} %get-tuple-element.31), channel_id=1, source_target_pairs={{0,16},{1,17},{2,18},{3,19},{4,20},{5,21},{6,22},{7,23},{8,24},{9,... | collective-permute-start | bytes 589832 | tf_op jit(solution)/shard_map/ppermute | solution.py:91
  9.8 15.9 %collective-permute-start.2 = (bf16[16,16,512]{2,1,0:T(8,128)(2,1)}, bf16[16,16,512]{2,1,0:T(8,128)(2,1)}, u32[]{:S(2)}, u32[]{:S(2)}) collective-permute-start(bf16[16,16,512]{2,1,0:T(8,128)(2,1)} %get-tuple-element.36), channel_id=1, source_target_pairs={{0,16},{1,17},{2,18},{3,19},{4,20},{5,21},{6,22},{7,23},{8,24},{9,... | collective-permute-start | bytes 786440 | tf_op jit(solution)/shard_map/ppermute | solution.py:91
  14.1 9.2 %copy-start.2 = (bf16[2,8,16,16,128]{4,3,2,1,0:T(8,128)(2,1)S(1)}, bf16[2,8,16,16,128]{4,3,2,1,0:T(8,128)(2,1)}, u32[]{:S(2)}) copy-start(bf16[2,8,16,16,128]{4,3,2,1,0:T(8,128)(2,1)} %vec.11) | copy-start | bytes 3145732
  17.9 1.4 %copy-start = (bf16[2,736,768]{2,1,0:T(8,128)(2,1)}, bf16[2,736,768]{2,1,0:T(8,128)(2,1)S(1)}, u32[]{:S(2)}) copy-start(bf16[2,736,768]{2,1,0:T(8,128)(2,1)S(1)} %order_cells.3.refs_1_) | copy-start | bytes 6782980
  19.3 4.0 %copy-start.1 = (bf16[2,736,768]{2,1,0:T(8,128)(2,1)S(1)}, bf16[2,736,768]{2,1,0:T(8,128)(2,1)}, u32[]{:S(2)}) copy-start(bf16[2,736,768]{2,1,0:T(8,128)(2,1)} %copy-done) | copy-start | bytes 6782980
  19.3 6.4 %collective-permute-start.3 = (bf16[1,16,896]{2,1,0:T(8,128)(2,1)S(1)}, bf16[1,16,896]{2,1,0:T(8,128)(2,1)S(1)}, u32[]{:S(2)}, u32[]{:S(2)}) collective-permute-start(bf16[1,16,896]{2,1,0:T(8,128)(2,1)S(1)} %slice.8), channel_id=1, source_target_pairs={{0,16},{1,17},{2,18},{3,19},{4,20},{5,21},{6,22},{7,23},{8,24},{9,... | collective-permute-start | bytes 86024 | tf_op jit(solution)/shard_map/ppermute | solution.py:91
  27.5 8.6 %collective-permute-start.4 = (bf16[2,2,17,16,128]{4,3,2,1,0:T(8,128)(2,1)S(1)}, bf16[2,2,17,16,128]{4,3,2,1,0:T(8,128)(2,1)S(1)}, u32[]{:S(2)}, u32[]{:S(2)}) collective-permute-start(bf16[2,2,17,16,128]{4,3,2,1,0:T(8,128)(2,1)S(1)} %get-tuple-element.41), channel_id=1, source_target_pairs={{0,16},{1,17},{2,18},{3,19},{4,20},{5,21},{6,22},{7,23},{8,24},{9,... | collective-permute-start | bytes 835592 | tf_op jit(solution)/shard_map/ppermute | solution.py:91
  28.1 1.3 %collective-permute-start.5 = (bf16[2,9,16,128]{3,2,1,0:T(8,128)(2,1)S(1)}, bf16[2,9,16,128]{3,2,1,0:T(8,128)(2,1)S(1)}, u32[]{:S(2)}, u32[]{:S(2)}) collective-permute-start(bf16[2,9,16,128]{3,2,1,0:T(8,128)(2,1)S(1)} %get-tuple-element.42), channel_id=1, source_target_pairs={{0,1},{1,0},{2,3},{3,2},{4,5},{5,4},{6,7},{7,6},{8,9},{9,8},{10,11... | collective-permute-start | bytes 221192 | tf_op jit(solution)/shard_map/ppermute | solution.py:102
  28.1 6.5 %collective-permute-start.6 = (bf16[2,9,16,128]{3,2,1,0:T(8,128)(2,1)S(1)}, bf16[2,9,16,128]{3,2,1,0:T(8,128)(2,1)S(1)}, u32[]{:S(2)}, u32[]{:S(2)}) collective-permute-start(bf16[2,9,16,128]{3,2,1,0:T(8,128)(2,1)S(1)} %get-tuple-element.43), channel_id=1, source_target_pairs={{0,15},{1,2},{2,1},{3,4},{4,3},{5,6},{6,5},{7,8},{8,7},{9,10},{10,... | collective-permute-start | bytes 221192 | tf_op jit(solution)/shard_map/ppermute | solution.py:108
  34.6 4.2 %collective-permute-start.7 = (bf16[2,2,2,16,128]{4,3,2,1,0:T(8,128)(2,1)S(1)}, bf16[2,2,2,16,128]{4,3,2,1,0:T(8,128)(2,1)S(1)}, u32[]{:S(2)}, u32[]{:S(2)}) collective-permute-start(bf16[2,2,2,16,128]{4,3,2,1,0:T(8,128)(2,1)S(1)} %corner_pack.2), channel_id=1, source_target_pairs={{0,16},{1,17},{2,18},{3,19},{4,20},{5,21},{6,22},{7,23},{8,24},{9,... | collective-permute-start | bytes 98312 | tf_op jit(solution)/shard_map/ppermute | solution.py:91
  38.9 3.1 %copy-start.3 = (bf16[8,16,16,512]{3,2,1,0:T(8,128)(2,1)S(1)}, bf16[8,16,16,512]{3,2,1,0:T(8,128)(2,1)}, u32[]{:S(2)}) copy-start(bf16[8,16,16,512]{3,2,1,0:T(8,128)(2,1)} %res_hbm.1) | copy-start | bytes 6291460
  40.9 8.6 %collective-permute-start.8 = (bf16[2,2,17,16,128]{4,3,2,1,0:T(8,128)(2,1)S(1)}, bf16[2,2,17,16,128]{4,3,2,1,0:T(8,128)(2,1)S(1)}, u32[]{:S(2)}, u32[]{:S(2)}) collective-permute-start(bf16[2,2,17,16,128]{4,3,2,1,0:T(8,128)(2,1)S(1)} %get-tuple-element.46), channel_id=1, source_target_pairs={{0,16},{1,17},{2,18},{3,19},{4,20},{5,21},{6,22},{7,23},{8,24},{9,... | collective-permute-start | bytes 835592 | tf_op jit(solution)/shard_map/ppermute | solution.py:91
  42.0 6.5 %collective-permute-start.10 = (bf16[2,9,16,128]{3,2,1,0:T(8,128)(2,1)S(1)}, bf16[2,9,16,128]{3,2,1,0:T(8,128)(2,1)S(1)}, u32[]{:S(2)}, u32[]{:S(2)}) collective-permute-start(bf16[2,9,16,128]{3,2,1,0:T(8,128)(2,1)S(1)} %get-tuple-element.48), channel_id=1, source_target_pairs={{0,15},{1,2},{2,1},{3,4},{4,3},{5,6},{6,5},{7,8},{8,7},{9,10},{10,... | collective-permute-start | bytes 221192 | tf_op jit(solution)/shard_map/ppermute | solution.py:108
  42.0 6.5 %collective-permute-start.9 = (bf16[2,9,16,128]{3,2,1,0:T(8,128)(2,1)S(1)}, bf16[2,9,16,128]{3,2,1,0:T(8,128)(2,1)S(1)}, u32[]{:S(2)}, u32[]{:S(2)}) collective-permute-start(bf16[2,9,16,128]{3,2,1,0:T(8,128)(2,1)S(1)} %get-tuple-element.47), channel_id=1, source_target_pairs={{0,1},{1,0},{2,3},{3,2},{4,5},{5,4},{6,7},{7,6},{8,9},{9,8},{10,11... | collective-permute-start | bytes 221192 | tf_op jit(solution)/shard_map/ppermute | solution.py:102
  48.5 4.0 %collective-permute-start.11 = (bf16[2,2,2,16,128]{4,3,2,1,0:T(8,128)(2,1)S(1)}, bf16[2,2,2,16,128]{4,3,2,1,0:T(8,128)(2,1)S(1)}, u32[]{:S(2)}, u32[]{:S(2)}) collective-permute-start(bf16[2,2,2,16,128]{4,3,2,1,0:T(8,128)(2,1)S(1)} %corner_pack.3), channel_id=1, source_target_pairs={{0,16},{1,17},{2,18},{3,19},{4,20},{5,21},{6,22},{7,23},{8,24},{9,... | collective-permute-start | bytes 98312 | tf_op jit(solution)/shard_map/ppermute | solution.py:91
  56.3 6.5 %copy-start.5 = (bf16[2,16,16,128]{3,2,1,0:T(8,128)(2,1)S(1)}, bf16[2,16,16,128]{3,2,1,0:T(8,128)(2,1)}, u32[]{:S(2)}) copy-start(bf16[2,16,16,128]{3,2,1,0:T(8,128)(2,1)} %get-tuple-element.54) | copy-start | bytes 393220
  56.3 8.5 %copy-start.6 = (bf16[2,9,16,128]{3,2,1,0:T(8,128)(2,1)S(1)}, bf16[2,9,16,128]{3,2,1,0:T(8,128)(2,1)}, u32[]{:S(2)}) copy-start(bf16[2,9,16,128]{3,2,1,0:T(8,128)(2,1)} %get-tuple-element.55) | copy-start | bytes 221188
  57.2 1.4 %collective-permute-start.15 = (bf16[256,256]{1,0:T(8,128)(2,1)S(1)}, bf16[256,256]{1,0:T(8,128)(2,1)S(1)}, u32[]{:S(2)}, u32[]{:S(2)}) collective-permute-start(bf16[256,256]{1,0:T(8,128)(2,1)S(1)} %get-tuple-element.59), channel_id=1, source_target_pairs={{0,1},{1,0},{2,3},{3,2},{4,5},{5,4},{6,7},{7,6},{8,9},{9,8},{10,11... | collective-permute-start | bytes 393224 | tf_op jit(solution)/shard_map/ppermute | solution.py:102
  59.3 17.7 %all-to-all-start = ((bf16[16,32,256]{2,1,0:T(8,128)(2,1)}), bf16[16,32,256]{2,1,0:T(8,128)(2,1)S(1)}, u32[]{:S(2)}, u32[]{:S(2)}) async-start(bf16[16,32,256]{2,1,0:T(8,128)(2,1)} %bitcast.3), calls=%async_computation | async-start | bytes 524288 | tf_op jit(solution)/shard_map/all_to_all | solution.py:726
  62.9 14.1 %collective-permute-start.12 = (bf16[2,16,16,128]{3,2,1,0:T(8,128)(2,1)S(1)}, bf16[2,16,16,128]{3,2,1,0:T(8,128)(2,1)S(1)}, u32[]{:S(2)}, u32[]{:S(2)}) collective-permute-start(bf16[2,16,16,128]{3,2,1,0:T(8,128)(2,1)S(1)} %copy-done.5), channel_id=1, source_target_pairs={{0,16},{1,17},{2,18},{3,19},{4,20},{5,21},{6,22},{7,23},{8,24},{9,... | collective-permute-start | bytes 393224 | tf_op jit(solution)/shard_map/ppermute | solution.py:91
  64.8 8.5 %collective-permute-start.13 = (bf16[2,9,16,128]{3,2,1,0:T(8,128)(2,1)S(1)}, bf16[2,9,16,128]{3,2,1,0:T(8,128)(2,1)S(1)}, u32[]{:S(2)}, u32[]{:S(2)}) collective-permute-start(bf16[2,9,16,128]{3,2,1,0:T(8,128)(2,1)S(1)} %copy-done.6), channel_id=1, source_target_pairs={{0,1},{1,2},{2,3},{3,4},{4,5},{5,6},{6,7},{7,8},{8,9},{9,10},{10,1... | collective-permute-start | bytes 221192 | tf_op jit(solution)/shard_map/ppermute | solution.py:91
  73.3 3.7 %collective-permute-start.14 = (bf16[2,1,16,128]{3,2,1,0:T(8,128)(2,1)S(1)}, bf16[2,1,16,128]{3,2,1,0:T(8,128)(2,1)S(1)}, u32[]{:S(2)}, u32[]{:S(2)}) collective-permute-start(bf16[2,1,16,128]{3,2,1,0:T(8,128)(2,1)S(1)} %slice.9), channel_id=1, source_target_pairs={{0,16},{1,17},{2,18},{3,19},{4,20},{5,21},{6,22},{7,23},{8,24},{9,... | collective-permute-start | bytes 24584 | tf_op jit(solution)/shard_map/ppermute | solution.py:91

commit v14 on v13

--- a/solution.py
+++ b/solution.py
@@ -468,12 +468,12 @@
     main_products(sz, prepare, u_ref, mats, rhs_ref, prod_ref)
 
 
-def third_corner(sz, n_mat, even_ref, vec, from_x, from_y, own_inv, own_pot, ghost_x, ghost_y,
+def third_corner(sz, n_mat, norm_scale, even_ref, vec, from_x, from_y, own_inv, own_pot, ghost_x, ghost_y,
                  last_x, last_field, acc_in, face_in, near_in, far_in, corner_in, prod_ref, y_ref,
-                 y_corner, new_ref, *refs):
+                 y_corner, new_ref, turned, *refs):
     mats = refs[:n_mat]
-    out_hbm, face_hbm, side_hbm, rows_ref = refs[n_mat : n_mat + 4]
-    part_ref, face, side, sem, acc_ref, small_ref, tail_ref = refs[n_mat + 4 :]
+    out_hbm, face, side, corner, give, keep = refs[n_mat : n_mat + 6]
+    part_ref, sem, acc_ref, rows_ref, small_ref, tail_ref = refs[n_mat + 6 :]
     nodes = Nodes(sz, vec, from_x, from_y, own_inv, own_pot, ghost_x, ghost_y, last_field)
     sums = Sums(sz, even_ref[0] == 0, acc_in, face_in, near_in, far_in, corner_in)
     u_corner, new_corner = [], []
@@ -498,8 +498,10 @@
                 rounded = value.astype(bf16)
                 if j < sz.ey:
                     face[:, j] = rounded
+                elif i < sz.ex:
+                    side[:, i] = value
                 else:
-                    side[:, i] = rounded
+                    corner[...] = rounded
                 put_row(sz.own_edges + (j if j < sz.ey else sz.ey + i), rounded)
                 continue
             at = sz.corner(i, j)
@@ -514,20 +516,13 @@
             copies[-1].start()
     for at in range(sz.own_edges + sz.ey + sz.gx, sz.edges):
         rows_ref[at] = jnp.zeros((sz.ez, sz.full), bf16)
-    copies.append(pltpu.make_async_copy(face, face_hbm, sem.at[sz.ex]))
-    copies.append(pltpu.make_async_copy(side, side_hbm, sem.at[sz.ex + 1]))
-    for copy in copies[-2:]:
-        copy.start()
-    for copy in copies:
-        copy.wait()
-
-
-def margin_kernel(sz, norm_scale, even_ref, turned, rows_ref, give, keep):
     rows = rows_ref[...].reshape(sz.edges * sz.ez, sz.full)
     mine = even_ref[0]
     for half, out in ((1 - mine, give), (mine, keep)):
         local = jnp.dot(turned[half], rows, preferred_element_type=f32)
         out[...] = (local * norm_scale).astype(out.dtype)
+    for copy in copies:
+        copy.wait()
 
 
 def pieces_kernel(keep, taken, pieces):
@@ -539,7 +534,16 @@
             pieces[copy, at] = value
 
 
-def last_kernel(sz, old_hbm, face, side, corner, pieces, out_hbm, margin, at_x, at_y, sems):
+def last_side_kernel(sz, side_ref, corner_ref, face_in, out_ref, face_out):
+    del face_in, face_out
+    for i in range(sz.ex):
+        value = side_ref[:, i]
+        if i == 0:
+            value = value + corner_ref[...].astype(f32)
+        out_ref[:, i] = value.astype(out_ref.dtype)
+
+
+def last_kernel(sz, old_hbm, face, side, pieces, out_hbm, margin, at_x, at_y, sems):
     del old_hbm
     pairs = [(at_x, out_hbm.at[:, 0]), (at_y, out_hbm.at[:, pl.ds(1, sz.ex - 1), 0])]
     loads = [pltpu.make_async_copy(b, a, sems.at[k]) for k, (a, b) in enumerate(pairs)]
@@ -549,7 +553,7 @@
     margin[...] = sum(pieces[at].astype(f32) for at in range(pieces.shape[0]))
     for copy in loads:
         copy.wait()
-    at_x[:, 0] += side[:, 0].astype(f32) + corner[:, 0].astype(f32)
+    at_x[:, 0] += side[:, 0].astype(f32)
     for j in range(sz.ey):
         at_x[:, j] += face[:, j].astype(f32)
     for i in range(1, sz.ex):
@@ -697,24 +701,19 @@
         [products, state_grid], main_scratch,
         [parity, *state, acc, *got, y1, *mats], scalar_first=True,
     )
-    filtered, face, side, rows = call(
-        functools.partial(third_corner, sz, n_mat), "third_corner", small_flops,
+    filtered, face, side, corner, give, keep = call(
+        functools.partial(third_corner, sz, n_mat, norm_scale), "third_corner",
+        small_flops + 2 * res_count * sz.edges * ez * full,
         [
-            like(own, f32), like((blocks, sz.ey) + tile, bf16), like((blocks, sz.gx) + tile, bf16),
-            like((sz.edges, ez, full), bf16),
+            like(own, f32), like((blocks, sz.ey) + tile, bf16), like((blocks, sz.ex) + tile, f32),
+            like(sz.edge, bf16), like((res_count // 2, full), bf16), like((res_count // 2, full), f32),
         ],
         [
-            pltpu.VMEM(own, f32), pltpu.VMEM((blocks, sz.ey) + tile, bf16),
-            pltpu.VMEM((blocks, sz.gx) + tile, bf16), pltpu.SemaphoreType.DMA((sz.ex + 2,)),
-            pltpu.VMEM(grid, f32),
+            pltpu.VMEM(own, f32), pltpu.SemaphoreType.DMA((sz.ex,)), pltpu.VMEM(grid, f32),
+            pltpu.VMEM((sz.edges, ez, full), bf16),
         ] + corner_scratch,
-        [parity, *state, *ends, acc, *got, corner, prod, y1, y1_corner, y2, *mats],
-        scalar_first=True, out_hbm=3,
-    )
-    give, keep = call(
-        functools.partial(margin_kernel, sz, norm_scale), "margin", 2 * res_count * sz.edges * ez * full,
-        [like((res_count // 2, full), bf16), like((res_count // 2, full), f32)], [],
-        [parity, turned, rows], scalar_first=True,
+        [parity, *state, *ends, acc, *got, corner, prod, y1, y1_corner, y2, turned, *mats],
+        scalar_first=True, out_hbm=1,
     )
 
     (pieces,) = call(
@@ -725,16 +724,20 @@
     groups = [[a * ny + b for a in range(nx) for b in range(c, ny, 2)] for c in range(2)]
     pieces = lax.all_to_all(pieces, ("dx", "dy"), 0, 0, axis_index_groups=groups)
 
+    corner = send(corner, 1, 0)
+    side, face = call(
+        functools.partial(last_side_kernel, sz), "last_side", 0,
+        [like((blocks, sz.ex) + tile, bf16), face], [], [side, corner, face], aliases={2: 1},
+    )
+    face = send(face, 1, 0)
     side = send(side, 0, 1)
-    corner = send(side[:, sz.ex :], 1, 0)
-    face = send(face, 1, 0)
     filtered, margin = call(
         functools.partial(last_kernel, sz), "last", 0, [like(own, f32), like(pieces.shape[1:], f32)],
         [
             pltpu.VMEM((blocks, sz.ey) + tile, f32), pltpu.VMEM((blocks, sz.ex - 1) + tile, f32),
             pltpu.SemaphoreType.DMA((2,)),
         ],
-        [filtered, face, side, corner, pieces], hbm=1, out_hbm=1, aliases={0: 0},
+        [filtered, face, side, pieces], hbm=1, out_hbm=1, aliases={0: 0},
     )
     return (filtered, margin)
 

time: 80 us -> 78.7 us (0.984)
  waiting for transfers between devices: 22.4 us -> 19.7 us
  local copies, waits for them, and re-layouts: 3.79 us -> 5.58 us
  Pallas kernels: 31.3 us -> 30.2 us
    ppermute x11, waiting for transfers between devices: 10.7 us -> 8.76 us  [send(): return lax.ppermute(value, ('dx', 'dy'), pairs)]
    unnamed x14 -> x18, local copies, waits for them, and re-layouts: 1.44 us -> 3.24 us
    pallas_call x15, Pallas kernels: 31.3 us -> 30.2 us  [call(): pl.pallas_call(kernel, in_specs=specs, out_specs=out_specs, out_shape=out...]
  transfers between devices with their start and end apart: 17 -> 17, of which waited for: 6 -> 6; matrix products, arithmetic and copies ran while one was open for 3% -> 3% of each run, Pallas kernels for 22% -> 23%
where the time goes in v14:
time: 78.7 us; the launch traced here: 78.1 us
  Pallas kernels  30.2 us (38%)
  starting transfers between devices  21.6 us (27%)
  waiting for transfers between devices  19.7 us (25%)
  local copies, waits for them, and re-layouts  5.58 us (7%)
  between operations  1.01 us (1%)
    pallas_call x15, Pallas kernels, call(): pl.pallas_call(kernel, in_specs=specs, out_specs=out_specs, out_shape=out...  30.2 us
    ppermute x11, starting transfers between devices, send(): return lax.ppermute(value, ('dx', 'dy'), pairs)  16.5 us
    ppermute x2, waiting for transfers between devices, swap_y(): far = lax.ppermute(far, 'dy', far_pairs)  9.28 us
    ppermute x11, waiting for transfers between devices, send(): return lax.ppermute(value, ('dx', 'dy'), pairs)  8.76 us
    all_to_all x1, starting transfers between devices, body(): lax.all_to_all(pieces, ('dx', 'dy'), 0, 0, axis_index_groups=groups)  3.53 us
    unnamed x18, local copies, waits for them, and re-layouts  3.24 us
    ppermute x3, waiting for transfers between devices, send_near(): return lax.ppermute(value, 'dy', pairs)  1.65 us
  transfers between devices with their start and end apart: 17, of which 6 were waited for; matrix products, arithmetic and copies ran while one was open for 3% of the time, Pallas kernels for 23%

profile of v14, /device:TPU:0, one launch (start us, length us, event | category | flops | bytes accessed | tf_op | source)
XLA Modules:
  0.0 78.1 jit_solution(14101448817360746863)
XLA Ops:
  0.6 2.1 %pack.1 = (bf16[16,16,384]{2,1,0:T(8,128)(2,1)}, bf16[8,16,896]{2,1,0:T(8,128)(2,1)}, bf16[16,16,512]{2,1,0:T(8,128)(2,1)}, s32[4,729]{1,0:T(4,128)S(1)}) custom-call(bf16[2,8,16,16,128]{4,3,2,1,0:T(8,128)(2,1)} %vec.11, bf16[8,16,16,512]{3,2,1,0:T(8,128)(2,1)} %res_hbm.1, f32[8,16,16]{2,1,0:T(8,128)} %inv_hbm.1, f32[8,16,16]{2,1,0:T(8,128)} %pot_hbm.1, ...), custom_call_target="tpu_custom_call" | custom-call | bytes 3873568 | tf_op jit(solution)/shard_map/pack/pallas_call | solution.py:587
  2.8 3.0 %collective-permute-start = (bf16[16,16,384]{2,1,0:T(8,128)(2,1)}, bf16[16,16,384]{2,1,0:T(8,128)(2,1)}, u32[]{:S(2)}, u32[]{:S(2)}) collective-permute-start(bf16[16,16,384]{2,1,0:T(8,128)(2,1)} %get-tuple-element.33), channel_id=1, source_target_pairs={{0,16},{1,17},{2,18},{3,19},{4,20},{5,21},{6,22},{7,23},{8,24},{9,... | collective-permute-start | bytes 589832 | tf_op jit(solution)/shard_map/ppermute | solution.py:91
  5.8 3.7 %collective-permute-start.1 = (bf16[8,16,896]{2,1,0:T(8,128)(2,1)}, bf16[8,16,896]{2,1,0:T(8,128)(2,1)S(1)}, u32[]{:S(2)}, u32[]{:S(2)}) collective-permute-start(bf16[8,16,896]{2,1,0:T(8,128)(2,1)} %get-tuple-element.34), channel_id=1, source_target_pairs={{0,15},{1,0},{2,1},{3,2},{4,3},{5,4},{6,5},{7,6},{8,7},{9,8},{10,9... | collective-permute-start | bytes 688136 | tf_op jit(solution)/shard_map/ppermute | solution.py:91
  9.5 0.5 collective-permute-start.2
  10.0 3.8 %order_cells.3.refs_1_ = bf16[2,736,768]{2,1,0:T(8,128)(2,1)S(1)} custom-call(bf16[729,729]{1,0:T(8,128)(2,1)S(1)} %copy-done.8, s32[4,729]{1,0:T(4,128)S(1)} %get-tuple-element.35.conn_ref), custom_call_target="tpu_custom_call" | custom-call | flops 3623878656 | bytes 3335538 | tf_op jit(solution)/shard_map/order_cells/pallas_call | solution.py:587
  13.8 0.0 copy-start.2
  13.8 3.8 %order_cells.2.refs_0_ = bf16[2,736,768]{2,1,0:T(8,128)(2,1)S(1)} custom-call(bf16[729,729]{1,0:T(8,128)(2,1)S(1)} %copy-done.8, s32[4,729]{1,0:T(4,128)S(1)} %get-tuple-element.35.conn_ref), custom_call_target="tpu_custom_call" | custom-call | flops 3623878656 | bytes 3335538 | tf_op jit(solution)/shard_map/order_cells/pallas_call | solution.py:587
  17.6 1.4 %copy-done = bf16[2,736,768]{2,1,0:T(8,128)(2,1)} copy-done((bf16[2,736,768]{2,1,0:T(8,128)(2,1)}, bf16[2,736,768]{2,1,0:T(8,128)(2,1)S(1)}, u32[]{:S(2)}) %copy-start) | copy-done | bytes 2261016
  19.0 0.0 collective-permute-done.1.from_y
  19.0 1.6 %collective-permute-start.3 = (bf16[1,16,896]{2,1,0:T(8,128)(2,1)S(1)}, bf16[1,16,896]{2,1,0:T(8,128)(2,1)S(1)}, u32[]{:S(2)}, u32[]{:S(2)}) collective-permute-start(bf16[1,16,896]{2,1,0:T(8,128)(2,1)S(1)} %slice.4), channel_id=1, source_target_pairs={{0,16},{1,17},{2,18},{3,19},{4,20},{5,21},{6,22},{7,23},{8,24},{9,... | collective-permute-start | bytes 86024 | tf_op jit(solution)/shard_map/ppermute | solution.py:91
  20.6 0.0 collective-permute-done.from_x
  20.6 1.2 %broadcast_in_dim.4.own_inv = f32[8,16,16,128]{3,2,1,0:T(8,128)S(1)} broadcast(f32[8,16,16]{2,1,0:T(8,128)} %inv_hbm.1), dimensions={0,1,2} | broadcast | bytes 1056768 | tf_op jit(solution)/shard_map/broadcast_in_dim | solution.py:634
  21.8 1.2 %broadcast_in_dim.5.own_pot = f32[8,16,16,128]{3,2,1,0:T(8,128)S(1)} broadcast(f32[8,16,16]{2,1,0:T(8,128)} %pot_hbm.1), dimensions={0,1,2} | broadcast | bytes 1056768 | tf_op jit(solution)/shard_map/broadcast_in_dim | solution.py:635
  23.0 2.4 %first_main.1 = (f32[4,736,256]{2,1,0:T(8,128)S(1)}, f32[2,16,16,128]{3,2,1,0:T(8,128)S(1)}, f32[2,8,16,128]{3,2,1,0:T(8,128)S(1)}) custom-call(bf16[2,8,16,16,128]{4,3,2,1,0:T(8,128)(2,1)S(1)} %copy-done.2, bf16[16,16,384]{2,1,0:T(8,128)(2,1)} %collective-permute-done.from_x, bf16[8,16,896]{2,1,0:T(8,128)(2,1)S(1)} %collective-permute-done.1.from_y, ...), custom_call_target="tpu_custom_call" | custom-call | flops 1157627904 | bytes 11501568 | tf_op jit(solution)/shard_map/first_main/pallas_call | solution.py:587
  25.4 1.8 %first_corner.1 = (bf16[16,16,512]{2,1,0:T(8,128)(2,1)}, f32[2,9,17,16,128]{4,3,2,1,0:T(8,128)S(1)}, bf16[2,2,17,16,128]{4,3,2,1,0:T(8,128)(2,1)S(1)}, bf16[2,9,...) custom-call(s32[1]{0:T(128)} %bitcast.even_ref, ...), custom_call_target="tpu_custom_call", output_to_operand_aliasing={{0}: (1, {})} | custom-call | flops 192937984 | bytes 15020036 | tf_op jit(solution)/shard_map/first_corner/pallas_call | solution.py:587
  27.2 0.7 collective-permute-start.4
  27.8 0.0 collective-permute-start.5
  27.9 1.0 %collective-permute-start.6 = (bf16[2,9,16,128]{3,2,1,0:T(8,128)(2,1)S(1)}, bf16[2,9,16,128]{3,2,1,0:T(8,128)(2,1)S(1)}, u32[]{:S(2)}, u32[]{:S(2)}) collective-permute-start(bf16[2,9,16,128]{3,2,1,0:T(8,128)(2,1)S(1)} %get-tuple-element.45), channel_id=1, source_target_pairs={{0,15},{1,2},{2,1},{3,4},{4,3},{5,6},{6,5},{7,8},{8,7},{9,10},{10,... | collective-permute-start | bytes 221192 | tf_op jit(solution)/shard_map/ppermute | solution.py:108
  28.8 0.3 collective-permute-done.5.near.near_in
  29.1 5.2 %collective-permute-done.6.far.far_in = bf16[2,9,16,128]{3,2,1,0:T(8,128)(2,1)S(1)} collective-permute-done((bf16[2,9,16,128]{3,2,1,0:T(8,128)(2,1)S(1)}, bf16[2,9,16,128]{3,2,1,0:T(8,128)(2,1)S(1)}, u32[]{:S(2)}, u32[]{:S(2)}) %collective-permute-start.6) | collective-permute-done | bytes 73760 | tf_op jit(solution)/shard_map/ppermute | solution.py:108
  34.3 1.4 %collective-permute-start.7 = (bf16[2,2,2,16,128]{4,3,2,1,0:T(8,128)(2,1)S(1)}, bf16[2,2,2,16,128]{4,3,2,1,0:T(8,128)(2,1)S(1)}, u32[]{:S(2)}, u32[]{:S(2)}) collective-permute-start(bf16[2,2,2,16,128]{4,3,2,1,0:T(8,128)(2,1)S(1)} %corner_pack.2), channel_id=1, source_target_pairs={{0,16},{1,17},{2,18},{3,19},{4,20},{5,21},{6,22},{7,23},{8,24},{9,... | collective-permute-start | bytes 98312 | tf_op jit(solution)/shard_map/ppermute | solution.py:91
  35.8 0.0 collective-permute-done.4.face_in
  35.8 2.8 %second_main.1 = (f32[4,736,256]{2,1,0:T(8,128)S(1)}, f32[2,9,17,16,128]{4,3,2,1,0:T(8,128)S(1)}) custom-call(s32[1]{0:T(128)} %bitcast.even_ref, bf16[2,8,16,16,128]{4,3,2,1,0:T(8,128)(2,1)S(1)} %copy-done.2, bf16[16,16,384]{2,1,0:T(8,128)(2,1)} %collective-permute-done.from_x, bf16[8,16,896]{2,1,0:T(8,128)(2,1)S(1)} %collective-permute-done.1.from_y, ...), custom_call_target="tpu_custom_call" | custom-call | flops 1157627904 | bytes 16941060 | tf_op jit(solution)/shard_map/second_main/pallas_call | solution.py:587
  38.6 0.0 collective-permute-done.7.corner_in
  38.6 0.0 copy-start.3
  38.6 2.0 %second_corner.1 = (f32[2,9,17,16,128]{4,3,2,1,0:T(8,128)S(1)}, bf16[2,2,17,16,128]{4,3,2,1,0:T(8,128)(2,1)S(1)}, bf16[2,9,16,128]{3,2,1,0:T(8,128)(2,1)S(1)}, b...) custom-call(s32[1]{0:T(128)} %bitcast.even_ref, bf16[2,8,16,16,128]{4,3,2,1,0:T(8,128)(2,1)S(1)} %copy-done.2, ...), custom_call_target="tpu_custom_call" | custom-call | flops 192937984 | bytes 17498116 | tf_op jit(solution)/shard_map/second_corner/pallas_call | solution.py:587
  40.6 1.1 %collective-permute-start.8 = (bf16[2,2,17,16,128]{4,3,2,1,0:T(8,128)(2,1)S(1)}, bf16[2,2,17,16,128]{4,3,2,1,0:T(8,128)(2,1)S(1)}, u32[]{:S(2)}, u32[]{:S(2)}) collective-permute-start(bf16[2,2,17,16,128]{4,3,2,1,0:T(8,128)(2,1)S(1)} %get-tuple-element.48), channel_id=1, source_target_pairs={{0,16},{1,17},{2,18},{3,19},{4,20},{5,21},{6,22},{7,23},{8,24},{9,... | collective-permute-start | bytes 835592 | tf_op jit(solution)/shard_map/ppermute | solution.py:91
  41.7 0.0 collective-permute-start.9
  41.7 0.5 collective-permute-start.10
  42.3 1.9 %turn_residents.1.turned = bf16[2,256,2560]{2,1,0:T(8,128)(2,1)S(1)} custom-call(bf16[2048,512]{1,0:T(8,128)(2,1)S(1)} %bitcast.4, bf16[16,16,512]{2,1,0:T(8,128)(2,1)} %get-tuple-element.55.res_x, bf16[8,16,896]{2,1,0:T(8,128)(2,1)S(1)} %collective-permute-done.1.from_y, bf16[1,16,896]{2,1,0:T(8,128)(2,1)S(1)} %collective-permute-done.3.corner), custom_call_target="tpu_custom_call" | custom-call | flops 578813952 | bytes 5238784 | tf_op jit(solution)/shard_map/turn_residents/pallas_call | solution.py:587
  44.1 4.1 %collective-permute-done.10.far.far_in = bf16[2,9,16,128]{3,2,1,0:T(8,128)(2,1)S(1)} collective-permute-done((bf16[2,9,16,128]{3,2,1,0:T(8,128)(2,1)S(1)}, bf16[2,9,16,128]{3,2,1,0:T(8,128)(2,1)S(1)}, u32[]{:S(2)}, u32[]{:S(2)}) %collective-permute-start.10) | collective-permute-done | bytes 73760 | tf_op jit(solution)/shard_map/ppermute | solution.py:108
  48.2 1.0 %collective-permute-start.11 = (bf16[2,2,2,16,128]{4,3,2,1,0:T(8,128)(2,1)S(1)}, bf16[2,2,2,16,128]{4,3,2,1,0:T(8,128)(2,1)S(1)}, u32[]{:S(2)}, u32[]{:S(2)}) collective-permute-start(bf16[2,2,2,16,128]{4,3,2,1,0:T(8,128)(2,1)S(1)} %corner_pack.3), channel_id=1, source_target_pairs={{0,16},{1,17},{2,18},{3,19},{4,20},{5,21},{6,22},{7,23},{8,24},{9,... | collective-permute-start | bytes 98312 | tf_op jit(solution)/shard_map/ppermute | solution.py:91
  49.2 3.0 %third_main.1 = (f32[4,736,256]{2,1,0:T(8,128)S(1)}, f32[2,9,17,16,128]{4,3,2,1,0:T(8,128)S(1)}) custom-call(s32[1]{0:T(128)} %bitcast.even_ref, bf16[2,8,16,16,128]{4,3,2,1,0:T(8,128)(2,1)S(1)} %copy-done.2, bf16[16,16,384]{2,1,0:T(8,128)(2,1)} %collective-permute-done.from_x, bf16[8,16,896]{2,1,0:T(8,128)(2,1)S(1)} %collective-permute-done.1.from_y, ...), custom_call_target="tpu_custom_call" | custom-call | flops 1157627904 | bytes 19447812 | tf_op jit(solution)/shard_map/third_main/pallas_call | solution.py:587
  52.2 0.0 collective-permute-done.11.corner_in
  52.2 3.6 %third_corner.1 = (f32[2,8,16,16,128]{4,3,2,1,0:T(8,128)}, bf16[2,16,16,128]{3,2,1,0:T(8,128)(2,1)S(1)}, f32[2,8,16,128]{3,2,1,0:T(8,128)S(1)}, bf16[2,16,128]{2...) custom-call(s32[1]{0:T(128)} %bitcast.even_ref, bf16[2,8,16,16,128]{4,3,2,1,0:T(8,128)(2,1)S(1)} %copy-done.2, ...), custom_call_target="tpu_custom_call" | custom-call | flops 864026624 | bytes 24961028 | tf_op jit(solution)/shard_map/third_corner/pallas_call | solution.py:587
  55.8 0.1 collective-permute-start.15
  55.9 1.3 %collective-permute-done.15.taken = bf16[256,256]{1,0:T(8,128)(2,1)S(1)} collective-permute-done((bf16[256,256]{1,0:T(8,128)(2,1)S(1)}, bf16[256,256]{1,0:T(8,128)(2,1)S(1)}, u32[]{:S(2)}, u32[]{:S(2)}) %collective-permute-start.15) | collective-permute-done | bytes 131104 | tf_op jit(solution)/shard_map/ppermute | solution.py:102
  57.3 0.7 pieces.1
  58.0 3.5 %all-to-all-start = ((bf16[16,32,256]{2,1,0:T(8,128)(2,1)}), bf16[16,32,256]{2,1,0:T(8,128)(2,1)S(1)}, u32[]{:S(2)}, u32[]{:S(2)}) async-start(bf16[16,32,256]{2,1,0:T(8,128)(2,1)} %bitcast.3), calls=%async_computation | async-start | bytes 524288 | tf_op jit(solution)/shard_map/all_to_all | solution.py:725
  61.5 1.9 %collective-permute-start.12 = (bf16[2,16,128]{2,1,0:T(8,128)(2,1)S(1)}, bf16[2,16,128]{2,1,0:T(8,128)(2,1)S(1)}, u32[]{:S(2)}, u32[]{:S(2)}) collective-permute-start(bf16[2,16,128]{2,1,0:T(8,128)(2,1)S(1)} %get-tuple-element.58), channel_id=1, source_target_pairs={{0,16},{1,17},{2,18},{3,19},{4,20},{5,21},{6,22},{7,23},{8,24},{9,... | collective-permute-start | bytes 24584 | tf_op jit(solution)/shard_map/ppermute | solution.py:91
  63.4 2.4 %collective-permute-done.12.corner_ref = bf16[2,16,128]{2,1,0:T(8,128)(2,1)S(1)} collective-permute-done((bf16[2,16,128]{2,1,0:T(8,128)(2,1)S(1)}, bf16[2,16,128]{2,1,0:T(8,128)(2,1)S(1)}, u32[]{:S(2)}, u32[]{:S(2)}) %collective-permute-start.12) | collective-permute-done | bytes 8224 | tf_op jit(solution)/shard_map/ppermute | solution.py:91
  65.8 0.9 %copy-done.5 = bf16[2,16,16,128]{3,2,1,0:T(8,128)(2,1)S(1)} copy-done((bf16[2,16,16,128]{3,2,1,0:T(8,128)(2,1)S(1)}, bf16[2,16,16,128]{3,2,1,0:T(8,128)(2,1)}, u32[]{:S(2)}) %copy-start.5) | copy-done | bytes 131096
  66.7 0.9 %copy-done.7 = f32[2,8,16,128]{3,2,1,0:T(8,128)S(1)} copy-done((f32[2,8,16,128]{3,2,1,0:T(8,128)S(1)}, f32[2,8,16,128]{3,2,1,0:T(8,128)}, u32[]{:S(2)}) %copy-start.7) | copy-done | bytes 131096
  67.6 1.6 %collective-permute-start.13 = (bf16[2,16,16,128]{3,2,1,0:T(8,128)(2,1)S(1)}, bf16[2,16,16,128]{3,2,1,0:T(8,128)(2,1)S(1)}, u32[]{:S(2)}, u32[]{:S(2)}) collective-permute-start(bf16[2,16,16,128]{3,2,1,0:T(8,128)(2,1)S(1)} %get-tuple-element.60), channel_id=1, source_target_pairs={{0,16},{1,17},{2,18},{3,19},{4,20},{5,21},{6,22},{7,23},{8,24},{9,... | collective-permute-start | bytes 393224 | tf_op jit(solution)/shard_map/ppermute | solution.py:91
  69.2 0.0 collective-permute-start.14
  69.2 6.4 %collective-permute-done.14.side = bf16[2,8,16,128]{3,2,1,0:T(8,128)(2,1)S(1)} collective-permute-done((bf16[2,8,16,128]{3,2,1,0:T(8,128)(2,1)S(1)}, bf16[2,8,16,128]{3,2,1,0:T(8,128)(2,1)S(1)}, u32[]{:S(2)}, u32[]{:S(2)}) %collective-permute-start.14) | collective-permute-done | bytes 65568 | tf_op jit(solution)/shard_map/ppermute | solution.py:91
  75.6 0.0 collective-permute-done.13.face
  75.6 2.4 %last.1 = (f32[2,8,16,16,128]{4,3,2,1,0:T(8,128)}, f32[32,256]{1,0:T(8,128)}) custom-call(f32[2,8,16,16,128]{4,3,2,1,0:T(8,128)} %get-tuple-element.56.old_hbm, bf16[2,16,16,128]{3,2,1,0:T(8,128)(2,1)S(1)} %collective-permute-done.13.face, bf16[2,8,16,128]{3,2,1,0:T(8,128)(2,1)S(1)} %collective-permute-done.14.side, ...), custom_call_target="tpu_custom_call", output_to_operand_aliasing={{0}: (0, {})} | custom-call | bytes 4685824 | tf_op jit(solution)/shard_map/last/pallas_call | solution.py:587
  (22 shorter events, 0.1 us)
Async XLA Ops:
  0.6 9.4 %copy-start.8 = (bf16[729,729]{1,0:T(8,128)(2,1)S(1)}, bf16[729,729]{1,0:T(8,128)(2,1)}, u32[]{:S(2)}) copy-start(bf16[729,729]{1,0:T(8,128)(2,1)} %matrix_ref.3) | copy-start | bytes 3188650
  2.8 17.8 %collective-permute-start = (bf16[16,16,384]{2,1,0:T(8,128)(2,1)}, bf16[16,16,384]{2,1,0:T(8,128)(2,1)}, u32[]{:S(2)}, u32[]{:S(2)}) collective-permute-start(bf16[16,16,384]{2,1,0:T(8,128)(2,1)} %get-tuple-element.33), channel_id=1, source_target_pairs={{0,16},{1,17},{2,18},{3,19},{4,20},{5,21},{6,22},{7,23},{8,24},{9,... | collective-permute-start | bytes 589832 | tf_op jit(solution)/shard_map/ppermute | solution.py:91
  5.8 13.2 %collective-permute-start.1 = (bf16[8,16,896]{2,1,0:T(8,128)(2,1)}, bf16[8,16,896]{2,1,0:T(8,128)(2,1)S(1)}, u32[]{:S(2)}, u32[]{:S(2)}) collective-permute-start(bf16[8,16,896]{2,1,0:T(8,128)(2,1)} %get-tuple-element.34), channel_id=1, source_target_pairs={{0,15},{1,0},{2,1},{3,2},{4,3},{5,4},{6,5},{7,6},{8,7},{9,8},{10,9... | collective-permute-start | bytes 688136 | tf_op jit(solution)/shard_map/ppermute | solution.py:91
  9.5 15.9 %collective-permute-start.2 = (bf16[16,16,512]{2,1,0:T(8,128)(2,1)}, bf16[16,16,512]{2,1,0:T(8,128)(2,1)}, u32[]{:S(2)}, u32[]{:S(2)}) collective-permute-start(bf16[16,16,512]{2,1,0:T(8,128)(2,1)} %get-tuple-element.38), channel_id=1, source_target_pairs={{0,16},{1,17},{2,18},{3,19},{4,20},{5,21},{6,22},{7,23},{8,24},{9,... | collective-permute-start | bytes 786440 | tf_op jit(solution)/shard_map/ppermute | solution.py:91
  13.8 9.2 %copy-start.2 = (bf16[2,8,16,16,128]{4,3,2,1,0:T(8,128)(2,1)S(1)}, bf16[2,8,16,16,128]{4,3,2,1,0:T(8,128)(2,1)}, u32[]{:S(2)}) copy-start(bf16[2,8,16,16,128]{4,3,2,1,0:T(8,128)(2,1)} %vec.11) | copy-start | bytes 3145732
  17.6 1.4 %copy-start = (bf16[2,736,768]{2,1,0:T(8,128)(2,1)}, bf16[2,736,768]{2,1,0:T(8,128)(2,1)S(1)}, u32[]{:S(2)}) copy-start(bf16[2,736,768]{2,1,0:T(8,128)(2,1)S(1)} %order_cells.2.refs_0_) | copy-start | bytes 6782980
  19.0 4.0 %copy-start.1 = (bf16[2,736,768]{2,1,0:T(8,128)(2,1)S(1)}, bf16[2,736,768]{2,1,0:T(8,128)(2,1)}, u32[]{:S(2)}) copy-start(bf16[2,736,768]{2,1,0:T(8,128)(2,1)} %copy-done) | copy-start | bytes 6782980
  19.0 6.4 %collective-permute-start.3 = (bf16[1,16,896]{2,1,0:T(8,128)(2,1)S(1)}, bf16[1,16,896]{2,1,0:T(8,128)(2,1)S(1)}, u32[]{:S(2)}, u32[]{:S(2)}) collective-permute-start(bf16[1,16,896]{2,1,0:T(8,128)(2,1)S(1)} %slice.4), channel_id=1, source_target_pairs={{0,16},{1,17},{2,18},{3,19},{4,20},{5,21},{6,22},{7,23},{8,24},{9,... | collective-permute-start | bytes 86024 | tf_op jit(solution)/shard_map/ppermute | solution.py:91
  27.2 8.6 %collective-permute-start.4 = (bf16[2,2,17,16,128]{4,3,2,1,0:T(8,128)(2,1)S(1)}, bf16[2,2,17,16,128]{4,3,2,1,0:T(8,128)(2,1)S(1)}, u32[]{:S(2)}, u32[]{:S(2)}) collective-permute-start(bf16[2,2,17,16,128]{4,3,2,1,0:T(8,128)(2,1)S(1)} %get-tuple-element.43), channel_id=1, source_target_pairs={{0,16},{1,17},{2,18},{3,19},{4,20},{5,21},{6,22},{7,23},{8,24},{9,... | collective-permute-start | bytes 835592 | tf_op jit(solution)/shard_map/ppermute | solution.py:91
  27.8 1.3 %collective-permute-start.5 = (bf16[2,9,16,128]{3,2,1,0:T(8,128)(2,1)S(1)}, bf16[2,9,16,128]{3,2,1,0:T(8,128)(2,1)S(1)}, u32[]{:S(2)}, u32[]{:S(2)}) collective-permute-start(bf16[2,9,16,128]{3,2,1,0:T(8,128)(2,1)S(1)} %get-tuple-element.44), channel_id=1, source_target_pairs={{0,1},{1,0},{2,3},{3,2},{4,5},{5,4},{6,7},{7,6},{8,9},{9,8},{10,11... | collective-permute-start | bytes 221192 | tf_op jit(solution)/shard_map/ppermute | solution.py:102
  27.9 6.5 %collective-permute-start.6 = (bf16[2,9,16,128]{3,2,1,0:T(8,128)(2,1)S(1)}, bf16[2,9,16,128]{3,2,1,0:T(8,128)(2,1)S(1)}, u32[]{:S(2)}, u32[]{:S(2)}) collective-permute-start(bf16[2,9,16,128]{3,2,1,0:T(8,128)(2,1)S(1)} %get-tuple-element.45), channel_id=1, source_target_pairs={{0,15},{1,2},{2,1},{3,4},{4,3},{5,6},{6,5},{7,8},{8,7},{9,10},{10,... | collective-permute-start | bytes 221192 | tf_op jit(solution)/shard_map/ppermute | solution.py:108
  34.3 4.3 %collective-permute-start.7 = (bf16[2,2,2,16,128]{4,3,2,1,0:T(8,128)(2,1)S(1)}, bf16[2,2,2,16,128]{4,3,2,1,0:T(8,128)(2,1)S(1)}, u32[]{:S(2)}, u32[]{:S(2)}) collective-permute-start(bf16[2,2,2,16,128]{4,3,2,1,0:T(8,128)(2,1)S(1)} %corner_pack.2), channel_id=1, source_target_pairs={{0,16},{1,17},{2,18},{3,19},{4,20},{5,21},{6,22},{7,23},{8,24},{9,... | collective-permute-start | bytes 98312 | tf_op jit(solution)/shard_map/ppermute | solution.py:91
  38.6 3.7 %copy-start.3 = (bf16[8,16,16,512]{3,2,1,0:T(8,128)(2,1)S(1)}, bf16[8,16,16,512]{3,2,1,0:T(8,128)(2,1)}, u32[]{:S(2)}) copy-start(bf16[8,16,16,512]{3,2,1,0:T(8,128)(2,1)} %res_hbm.1) | copy-start | bytes 6291460
  40.6 8.6 %collective-permute-start.8 = (bf16[2,2,17,16,128]{4,3,2,1,0:T(8,128)(2,1)S(1)}, bf16[2,2,17,16,128]{4,3,2,1,0:T(8,128)(2,1)S(1)}, u32[]{:S(2)}, u32[]{:S(2)}) collective-permute-start(bf16[2,2,17,16,128]{4,3,2,1,0:T(8,128)(2,1)S(1)} %get-tuple-element.48), channel_id=1, source_target_pairs={{0,16},{1,17},{2,18},{3,19},{4,20},{5,21},{6,22},{7,23},{8,24},{9,... | collective-permute-start | bytes 835592 | tf_op jit(solution)/shard_map/ppermute | solution.py:91
  41.7 2.4 %collective-permute-start.9 = (bf16[2,9,16,128]{3,2,1,0:T(8,128)(2,1)S(1)}, bf16[2,9,16,128]{3,2,1,0:T(8,128)(2,1)S(1)}, u32[]{:S(2)}, u32[]{:S(2)}) collective-permute-start(bf16[2,9,16,128]{3,2,1,0:T(8,128)(2,1)S(1)} %get-tuple-element.49), channel_id=1, source_target_pairs={{0,1},{1,0},{2,3},{3,2},{4,5},{5,4},{6,7},{7,6},{8,9},{9,8},{10,11... | collective-permute-start | bytes 221192 | tf_op jit(solution)/shard_map/ppermute | solution.py:102
  41.7 6.5 %collective-permute-start.10 = (bf16[2,9,16,128]{3,2,1,0:T(8,128)(2,1)S(1)}, bf16[2,9,16,128]{3,2,1,0:T(8,128)(2,1)S(1)}, u32[]{:S(2)}, u32[]{:S(2)}) collective-permute-start(bf16[2,9,16,128]{3,2,1,0:T(8,128)(2,1)S(1)} %get-tuple-element.50), channel_id=1, source_target_pairs={{0,15},{1,2},{2,1},{3,4},{4,3},{5,6},{6,5},{7,8},{8,7},{9,10},{10,... | collective-permute-start | bytes 221192 | tf_op jit(solution)/shard_map/ppermute | solution.py:108
  48.2 4.0 %collective-permute-start.11 = (bf16[2,2,2,16,128]{4,3,2,1,0:T(8,128)(2,1)S(1)}, bf16[2,2,2,16,128]{4,3,2,1,0:T(8,128)(2,1)S(1)}, u32[]{:S(2)}, u32[]{:S(2)}) collective-permute-start(bf16[2,2,2,16,128]{4,3,2,1,0:T(8,128)(2,1)S(1)} %corner_pack.3), channel_id=1, source_target_pairs={{0,16},{1,17},{2,18},{3,19},{4,20},{5,21},{6,22},{7,23},{8,24},{9,... | collective-permute-start | bytes 98312 | tf_op jit(solution)/shard_map/ppermute | solution.py:91
  55.8 2.2 %copy-start.4 = (bf16[2,16,16,128]{3,2,1,0:T(8,128)(2,1)}, bf16[2,16,16,128]{3,2,1,0:T(8,128)(2,1)S(1)}, u32[]{:S(2)}) copy-start(bf16[2,16,16,128]{3,2,1,0:T(8,128)(2,1)S(1)} %get-tuple-element.59.face_in) | copy-start | bytes 393220
  55.8 2.2 %copy-start.6 = (f32[2,8,16,128]{3,2,1,0:T(8,128)}, f32[2,8,16,128]{3,2,1,0:T(8,128)S(1)}, u32[]{:S(2)}) copy-start(f32[2,8,16,128]{3,2,1,0:T(8,128)S(1)} %get-tuple-element.57.side_ref) | copy-start | bytes 393220
  55.8 1.4 %collective-permute-start.15 = (bf16[256,256]{1,0:T(8,128)(2,1)S(1)}, bf16[256,256]{1,0:T(8,128)(2,1)S(1)}, u32[]{:S(2)}, u32[]{:S(2)}) collective-permute-start(bf16[256,256]{1,0:T(8,128)(2,1)S(1)} %get-tuple-element.63), channel_id=1, source_target_pairs={{0,1},{1,0},{2,3},{3,2},{4,5},{5,4},{6,7},{7,6},{8,9},{9,8},{10,11... | collective-permute-start | bytes 393224 | tf_op jit(solution)/shard_map/ppermute | solution.py:102
  58.0 17.6 %all-to-all-start = ((bf16[16,32,256]{2,1,0:T(8,128)(2,1)}), bf16[16,32,256]{2,1,0:T(8,128)(2,1)S(1)}, u32[]{:S(2)}, u32[]{:S(2)}) async-start(bf16[16,32,256]{2,1,0:T(8,128)(2,1)} %bitcast.3), calls=%async_computation | async-start | bytes 524288 | tf_op jit(solution)/shard_map/all_to_all | solution.py:725
  61.5 4.2 %collective-permute-start.12 = (bf16[2,16,128]{2,1,0:T(8,128)(2,1)S(1)}, bf16[2,16,128]{2,1,0:T(8,128)(2,1)S(1)}, u32[]{:S(2)}, u32[]{:S(2)}) collective-permute-start(bf16[2,16,128]{2,1,0:T(8,128)(2,1)S(1)} %get-tuple-element.58), channel_id=1, source_target_pairs={{0,16},{1,17},{2,18},{3,19},{4,20},{5,21},{6,22},{7,23},{8,24},{9,... | collective-permute-start | bytes 24584 | tf_op jit(solution)/shard_map/ppermute | solution.py:91
  65.8 0.9 %copy-start.5 = (bf16[2,16,16,128]{3,2,1,0:T(8,128)(2,1)S(1)}, bf16[2,16,16,128]{3,2,1,0:T(8,128)(2,1)}, u32[]{:S(2)}) copy-start(bf16[2,16,16,128]{3,2,1,0:T(8,128)(2,1)} %copy-done.4) | copy-start | bytes 393220
  66.7 0.9 %copy-start.7 = (f32[2,8,16,128]{3,2,1,0:T(8,128)S(1)}, f32[2,8,16,128]{3,2,1,0:T(8,128)}, u32[]{:S(2)}) copy-start(f32[2,8,16,128]{3,2,1,0:T(8,128)} %copy-done.6) | copy-start | bytes 393220
  67.6 8.0 %collective-permute-start.13 = (bf16[2,16,16,128]{3,2,1,0:T(8,128)(2,1)S(1)}, bf16[2,16,16,128]{3,2,1,0:T(8,128)(2,1)S(1)}, u32[]{:S(2)}, u32[]{:S(2)}) collective-permute-start(bf16[2,16,16,128]{3,2,1,0:T(8,128)(2,1)S(1)} %get-tuple-element.60), channel_id=1, source_target_pairs={{0,16},{1,17},{2,18},{3,19},{4,20},{5,21},{6,22},{7,23},{8,24},{9,... | collective-permute-start | bytes 393224 | tf_op jit(solution)/shard_map/ppermute | solution.py:91
  69.2 6.4 %collective-permute-start.14 = (bf16[2,8,16,128]{3,2,1,0:T(8,128)(2,1)S(1)}, bf16[2,8,16,128]{3,2,1,0:T(8,128)(2,1)S(1)}, u32[]{:S(2)}, u32[]{:S(2)}) collective-permute-start(bf16[2,8,16,128]{3,2,1,0:T(8,128)(2,1)S(1)} %get-tuple-element.61), channel_id=1, source_target_pairs={{0,1},{1,2},{2,3},{3,4},{4,5},{5,6},{6,7},{7,8},{8,9},{9,10},{10,1... | collective-permute-start | bytes 196616 | tf_op jit(solution)/shard_map/ppermute | solution.py:91

commit v15 on v14

--- a/solution.py
+++ b/solution.py
@@ -97,8 +97,8 @@
     return jnp.stack([send(value[0], -1, 0), send(value[1], 1, 0)])
 
 
-def send_near(value):
-    pairs = [(b, b + 1 if b % 2 == 0 else b - 1) for b in range(lax.axis_size("dy"))]
+def swap_bit(value, bit):
+    pairs = [(b, b ^ (1 << bit)) for b in range(lax.axis_size("dy"))]
     return lax.ppermute(value, "dy", pairs)
 
 
@@ -106,7 +106,7 @@
     ny = lax.axis_size("dy")
     far_pairs = [(b, (b - 1 if b % 2 == 0 else b + 1) % ny) for b in range(ny)]
     far = lax.ppermute(far, "dy", far_pairs)
-    return send_near(near), far
+    return swap_bit(near, 0), far
 
 
 def order_kernel(sz, first, matrix_ref, conn_ref, out_ref):
@@ -202,15 +202,23 @@
         copy.wait()
 
 
-def turn_kernel(sz, pieces, res_ref, res_x, from_y, corner, out_ref):
+def reversed_bits(value, count):
+    out = 0
+    while count > 1:
+        out, value, count = 2 * out + value % 2, value // 2, count // 2
+    return out
+
+
+def turn_kernel(sz, owners, res_ref, res_x, from_y, corner, out_ref):
     own = sz.own_edges * sz.ez
-    share = sz.res // out_ref.shape[0] // pieces
+    half = owners // 2
+    share = sz.res // owners
 
     def put(g, columns, value):
         for at in range(0, LANES, share):
-            owner = (g + at) // share
-            row = owner // 2 * share
-            out_ref[owner % 2, row : row + share, columns] = value[at : at + share]
+            place = reversed_bits((g + at) // share, owners)
+            row = place % half * share
+            out_ref[place // half, row : row + share, columns] = value[at : at + share]
 
     for g in range(0, sz.res, LANES):
         lanes = slice(g, g + LANES)
@@ -525,13 +533,10 @@
         copy.wait()
 
 
-def pieces_kernel(keep, taken, pieces):
-    rows = pieces.shape[2]
-    for at in range(pieces.shape[1]):
-        span = slice(at * rows, (at + 1) * rows)
-        value = (keep[span] + taken[span].astype(f32)).astype(pieces.dtype)
-        for copy in range(pieces.shape[0]):
-            pieces[copy, at] = value
+def halve_kernel(bit_ref, keep, taken, give, left):
+    mine = bit_ref[0]
+    give[...] = (keep[1 - mine] + taken[1 - mine].astype(f32)).astype(give.dtype)
+    left[...] = keep[mine] + taken[mine].astype(f32)
 
 
 def last_side_kernel(sz, side_ref, corner_ref, face_in, out_ref, face_out):
@@ -543,14 +548,15 @@
         out_ref[:, i] = value.astype(out_ref.dtype)
 
 
-def last_kernel(sz, old_hbm, face, side, pieces, out_hbm, margin, at_x, at_y, sems):
+def last_kernel(sz, old_hbm, face, side, *refs):
     del old_hbm
+    sums, (out_hbm, margin, at_x, at_y, sems) = refs[:-5], refs[-5:]
     pairs = [(at_x, out_hbm.at[:, 0]), (at_y, out_hbm.at[:, pl.ds(1, sz.ex - 1), 0])]
     loads = [pltpu.make_async_copy(b, a, sems.at[k]) for k, (a, b) in enumerate(pairs)]
     stores = [pltpu.make_async_copy(a, b, sems.at[k]) for k, (a, b) in enumerate(pairs)]
     for copy in loads:
         copy.start()
-    margin[...] = sum(pieces[at].astype(f32) for at in range(pieces.shape[0]))
+    margin[...] = sum(ref[...] for ref in sums)
     for copy in loads:
         copy.wait()
     at_x[:, 0] += side[:, 0].astype(f32)
@@ -678,7 +684,7 @@
         scalar_first=True, aliases={1: 0},
     )
     (turned,) = call(
-        functools.partial(turn_kernel, sz, ny // 2), "turn_residents", flops // 2,
+        functools.partial(turn_kernel, sz, ny), "turn_residents", flops // 2,
         [like((2, res_count // 2, sz.edges * ez), bf16)], [],
         [resident.reshape(-1, res_count), res_x, from_y, ghost_corner],
     )
@@ -716,13 +722,17 @@
         scalar_first=True, out_hbm=1,
     )
 
-    (pieces,) = call(
-        pieces_kernel, "pieces", 0, [like((nx, ny // 2, res_count // ny, full), bf16)], [],
-        [keep, send_near(give)],
-    )
-    pieces = pieces.reshape(nx * ny // 2, -1, full)
-    groups = [[a * ny + b for a in range(nx) for b in range(c, ny, 2)] for c in range(2)]
-    pieces = lax.all_to_all(pieces, ("dx", "dy"), 0, 0, axis_index_groups=groups)
+    taken = swap_bit(give, 0)
+    for bit in range(1, (ny - 1).bit_length()):
+        rows = keep.shape[0] // 2
+        mine = jnp.reshape((lax.axis_index("dy") >> bit) & 1, (1,)).astype(jnp.int32)
+        give, keep = call(
+            halve_kernel, "halve", 0, [like((rows, full), bf16), like((rows, full), f32)], [],
+            [mine, keep.reshape(2, rows, full), taken.reshape(2, rows, full)], scalar_first=True,
+        )
+        taken = swap_bit(give, bit)
+    keep = keep + taken.astype(f32)
+    sums = [keep] + [send(keep, steps, 0) for steps in range(1, nx)]
 
     corner = send(corner, 1, 0)
     side, face = call(
@@ -732,12 +742,12 @@
     face = send(face, 1, 0)
     side = send(side, 0, 1)
     filtered, margin = call(
-        functools.partial(last_kernel, sz), "last", 0, [like(own, f32), like(pieces.shape[1:], f32)],
+        functools.partial(last_kernel, sz), "last", 0, [like(own, f32), like(keep.shape, f32)],
         [
             pltpu.VMEM((blocks, sz.ey) + tile, f32), pltpu.VMEM((blocks, sz.ex - 1) + tile, f32),
             pltpu.SemaphoreType.DMA((2,)),
         ],
-        [filtered, face, side, pieces], hbm=1, out_hbm=1, aliases={0: 0},
+        [filtered, face, side, *sums], hbm=1, out_hbm=1, aliases={0: 0},
     )
     return (filtered, margin)
 

time: 78.7 us -> 85.8 us (1.090)
  waiting for transfers between devices: 19.7 us -> 28 us
  starting transfers between devices: 21.6 us -> 17.5 us
  local copies, waits for them, and re-layouts: 5.58 us -> 8.51 us
    ppermute x3 -> x6, waiting for transfers between devices: 1.65 us -> 10.2 us  [swap_bit(): return lax.ppermute(value, 'dy', pairs)]
    all_to_all x1 -> x0, starting transfers between devices: 3.53 us -> none  [body(): lax.all_to_all(pieces, ('dx', 'dy'), 0, 0, axis_index_groups=groups)]
    unnamed x18 -> x22, local copies, waits for them, and re-layouts: 3.24 us -> 6.16 us
    ppermute x11 -> x12, waiting for transfers between devices: 8.76 us -> 7.96 us  [send(): return lax.ppermute(value, ('dx', 'dy'), pairs)]
    ppermute x11 -> x12, starting transfers between devices: 16.5 us -> 16.5 us  [send(): return lax.ppermute(value, ('dx', 'dy'), pairs)]
    pallas_call x15 -> x17, Pallas kernels: 30.2 us -> 30.2 us  [call(): pl.pallas_call(kernel, in_specs=specs, out_specs=out_specs, out_shape=out...]
  transfers between devices with their start and end apart: 17 -> 20, of which waited for: 6 -> 8; matrix products, arithmetic and copies ran while one was open for 3% -> 3% of each run, Pallas kernels for 23% -> 21%
where the time goes in v15:
time: 85.8 us; the launch traced here: 85.3 us
  Pallas kernels  30.2 us (35%)
  waiting for transfers between devices  28 us (33%)
  starting transfers between devices  17.5 us (20%)
  local copies, waits for them, and re-layouts  8.51 us (10%)
  between operations  1.04 us (1%)
    pallas_call x17, Pallas kernels, call(): pl.pallas_call(kernel, in_specs=specs, out_specs=out_specs, out_shape=out...  30.2 us
    ppermute x12, starting transfers between devices, send(): return lax.ppermute(value, ('dx', 'dy'), pairs)  16.5 us
    ppermute x6, waiting for transfers between devices, swap_bit(): return lax.ppermute(value, 'dy', pairs)  10.2 us
    ppermute x2, waiting for transfers between devices, swap_y(): far = lax.ppermute(far, 'dy', far_pairs)  9.82 us
    ppermute x12, waiting for transfers between devices, send(): return lax.ppermute(value, ('dx', 'dy'), pairs)  7.96 us
    unnamed x22, local copies, waits for them, and re-layouts  6.16 us
  transfers between devices with their start and end apart: 20, of which 8 were waited for; matrix products, arithmetic and copies ran while one was open for 3% of the time, Pallas kernels for 21%

profile of v15, /device:TPU:0, one launch (start us, length us, event | category | flops | bytes accessed | tf_op | source)
XLA Modules:
  0.0 85.3 jit_solution(4776575232762035048)
XLA Ops:
  0.6 2.1 %pack.1 = (bf16[16,16,384]{2,1,0:T(8,128)(2,1)}, bf16[8,16,896]{2,1,0:T(8,128)(2,1)}, bf16[16,16,512]{2,1,0:T(8,128)(2,1)}, s32[4,729]{1,0:T(4,128)S(1)}) custom-call(bf16[2,8,16,16,128]{4,3,2,1,0:T(8,128)(2,1)} %vec.11, bf16[8,16,16,512]{3,2,1,0:T(8,128)(2,1)} %res_hbm.1, f32[8,16,16]{2,1,0:T(8,128)} %inv_hbm.1, f32[8,16,16]{2,1,0:T(8,128)} %pot_hbm.1, ...), custom_call_target="tpu_custom_call" | custom-call | bytes 3873568 | tf_op jit(solution)/shard_map/pack/pallas_call | solution.py:593
  2.8 5.5 %collective-permute-start.1 = (bf16[8,16,896]{2,1,0:T(8,128)(2,1)}, bf16[8,16,896]{2,1,0:T(8,128)(2,1)S(1)}, u32[]{:S(2)}, u32[]{:S(2)}) collective-permute-start(bf16[8,16,896]{2,1,0:T(8,128)(2,1)} %get-tuple-element.40), channel_id=1, source_target_pairs={{0,15},{1,0},{2,1},{3,2},{4,3},{5,4},{6,5},{7,6},{8,7},{9,8},{10,9... | collective-permute-start | bytes 688136 | tf_op jit(solution)/shard_map/ppermute | solution.py:91
  8.2 1.5 %collective-permute-start = (bf16[16,16,384]{2,1,0:T(8,128)(2,1)}, bf16[16,16,384]{2,1,0:T(8,128)(2,1)}, u32[]{:S(2)}, u32[]{:S(2)}) collective-permute-start(bf16[16,16,384]{2,1,0:T(8,128)(2,1)} %get-tuple-element.39), channel_id=1, source_target_pairs={{0,16},{1,17},{2,18},{3,19},{4,20},{5,21},{6,22},{7,23},{8,24},{9,... | collective-permute-start | bytes 589832 | tf_op jit(solution)/shard_map/ppermute | solution.py:91
  9.8 0.5 collective-permute-start.2
  10.3 3.8 %order_cells.2.refs_0_ = bf16[2,736,768]{2,1,0:T(8,128)(2,1)S(1)} custom-call(bf16[729,729]{1,0:T(8,128)(2,1)S(1)} %copy-done.10, s32[4,729]{1,0:T(4,128)S(1)} %get-tuple-element.41.conn_ref), custom_call_target="tpu_custom_call" | custom-call | flops 3623878656 | bytes 3335538 | tf_op jit(solution)/shard_map/order_cells/pallas_call | solution.py:593
  14.1 0.0 copy-start.2
  14.1 3.8 %order_cells.3.refs_1_ = bf16[2,736,768]{2,1,0:T(8,128)(2,1)S(1)} custom-call(bf16[729,729]{1,0:T(8,128)(2,1)S(1)} %copy-done.10, s32[4,729]{1,0:T(4,128)S(1)} %get-tuple-element.41.conn_ref), custom_call_target="tpu_custom_call" | custom-call | flops 3623878656 | bytes 3335538 | tf_op jit(solution)/shard_map/order_cells/pallas_call | solution.py:593
  17.9 1.4 %copy-done = bf16[2,736,768]{2,1,0:T(8,128)(2,1)} copy-done((bf16[2,736,768]{2,1,0:T(8,128)(2,1)}, bf16[2,736,768]{2,1,0:T(8,128)(2,1)S(1)}, u32[]{:S(2)}) %copy-start) | copy-done | bytes 2261016
  19.3 0.0 collective-permute-done.1.from_y
  19.3 1.6 %collective-permute-start.3 = (bf16[1,16,896]{2,1,0:T(8,128)(2,1)S(1)}, bf16[1,16,896]{2,1,0:T(8,128)(2,1)S(1)}, u32[]{:S(2)}, u32[]{:S(2)}) collective-permute-start(bf16[1,16,896]{2,1,0:T(8,128)(2,1)S(1)} %slice.4), channel_id=1, source_target_pairs={{0,16},{1,17},{2,18},{3,19},{4,20},{5,21},{6,22},{7,23},{8,24},{9,... | collective-permute-start | bytes 86024 | tf_op jit(solution)/shard_map/ppermute | solution.py:91
  20.9 0.0 collective-permute-done.from_x
  20.9 1.2 %broadcast_in_dim.4.own_inv = f32[8,16,16,128]{3,2,1,0:T(8,128)S(1)} broadcast(f32[8,16,16]{2,1,0:T(8,128)} %inv_hbm.1), dimensions={0,1,2} | broadcast | bytes 1056768 | tf_op jit(solution)/shard_map/broadcast_in_dim | solution.py:640
  22.0 1.2 %broadcast_in_dim.5.own_pot = f32[8,16,16,128]{3,2,1,0:T(8,128)S(1)} broadcast(f32[8,16,16]{2,1,0:T(8,128)} %pot_hbm.1), dimensions={0,1,2} | broadcast | bytes 1056768 | tf_op jit(solution)/shard_map/broadcast_in_dim | solution.py:641
  23.2 2.4 %first_main.1 = (f32[4,736,256]{2,1,0:T(8,128)S(1)}, f32[2,16,16,128]{3,2,1,0:T(8,128)S(1)}, f32[2,8,16,128]{3,2,1,0:T(8,128)S(1)}) custom-call(bf16[2,8,16,16,128]{4,3,2,1,0:T(8,128)(2,1)S(1)} %copy-done.2, bf16[16,16,384]{2,1,0:T(8,128)(2,1)} %collective-permute-done.from_x, bf16[8,16,896]{2,1,0:T(8,128)(2,1)S(1)} %collective-permute-done.1.from_y, ...), custom_call_target="tpu_custom_call" | custom-call | flops 1157627904 | bytes 11501568 | tf_op jit(solution)/shard_map/first_main/pallas_call | solution.py:593
  25.6 0.0 collective-permute-done.3.corner
  25.6 1.8 %first_corner.1 = (bf16[16,16,512]{2,1,0:T(8,128)(2,1)}, f32[2,9,17,16,128]{4,3,2,1,0:T(8,128)S(1)}, bf16[2,2,17,16,128]{4,3,2,1,0:T(8,128)(2,1)S(1)}, bf16[2,9,...) custom-call(s32[1]{0:T(128)} %bitcast.even_ref, ...), custom_call_target="tpu_custom_call", output_to_operand_aliasing={{0}: (1, {})} | custom-call | flops 192937984 | bytes 15020036 | tf_op jit(solution)/shard_map/first_corner/pallas_call | solution.py:593
  27.4 0.7 collective-permute-start.4
  28.1 0.7 collective-permute-start.6
  28.9 0.5 collective-permute-done.5.near.near_in
  29.4 5.2 %collective-permute-done.6.far.far_in = bf16[2,9,16,128]{3,2,1,0:T(8,128)(2,1)S(1)} collective-permute-done((bf16[2,9,16,128]{3,2,1,0:T(8,128)(2,1)S(1)}, bf16[2,9,16,128]{3,2,1,0:T(8,128)(2,1)S(1)}, u32[]{:S(2)}, u32[]{:S(2)}) %collective-permute-start.6) | collective-permute-done | bytes 73760 | tf_op jit(solution)/shard_map/ppermute | solution.py:108
  34.6 1.4 %collective-permute-start.7 = (bf16[2,2,2,16,128]{4,3,2,1,0:T(8,128)(2,1)S(1)}, bf16[2,2,2,16,128]{4,3,2,1,0:T(8,128)(2,1)S(1)}, u32[]{:S(2)}, u32[]{:S(2)}) collective-permute-start(bf16[2,2,2,16,128]{4,3,2,1,0:T(8,128)(2,1)S(1)} %corner_pack.2), channel_id=1, source_target_pairs={{0,16},{1,17},{2,18},{3,19},{4,20},{5,21},{6,22},{7,23},{8,24},{9,... | collective-permute-start | bytes 98312 | tf_op jit(solution)/shard_map/ppermute | solution.py:91
  36.0 2.8 %second_main.1 = (f32[4,736,256]{2,1,0:T(8,128)S(1)}, f32[2,9,17,16,128]{4,3,2,1,0:T(8,128)S(1)}) custom-call(s32[1]{0:T(128)} %bitcast.even_ref, bf16[2,8,16,16,128]{4,3,2,1,0:T(8,128)(2,1)S(1)} %copy-done.2, bf16[16,16,384]{2,1,0:T(8,128)(2,1)} %collective-permute-done.from_x, bf16[8,16,896]{2,1,0:T(8,128)(2,1)S(1)} %collective-permute-done.1.from_y, ...), custom_call_target="tpu_custom_call" | custom-call | flops 1157627904 | bytes 16941060 | tf_op jit(solution)/shard_map/second_main/pallas_call | solution.py:593
  38.8 0.0 copy-start.3
  38.9 2.0 %second_corner.1 = (f32[2,9,17,16,128]{4,3,2,1,0:T(8,128)S(1)}, bf16[2,2,17,16,128]{4,3,2,1,0:T(8,128)(2,1)S(1)}, bf16[2,9,16,128]{3,2,1,0:T(8,128)(2,1)S(1)}, b...) custom-call(s32[1]{0:T(128)} %bitcast.even_ref, bf16[2,8,16,16,128]{4,3,2,1,0:T(8,128)(2,1)S(1)} %copy-done.2, ...), custom_call_target="tpu_custom_call" | custom-call | flops 192937984 | bytes 17498116 | tf_op jit(solution)/shard_map/second_corner/pallas_call | solution.py:593
  40.8 1.1 %collective-permute-start.8 = (bf16[2,2,17,16,128]{4,3,2,1,0:T(8,128)(2,1)S(1)}, bf16[2,2,17,16,128]{4,3,2,1,0:T(8,128)(2,1)S(1)}, u32[]{:S(2)}, u32[]{:S(2)}) collective-permute-start(bf16[2,2,17,16,128]{4,3,2,1,0:T(8,128)(2,1)S(1)} %get-tuple-element.54), channel_id=1, source_target_pairs={{0,16},{1,17},{2,18},{3,19},{4,20},{5,21},{6,22},{7,23},{8,24},{9,... | collective-permute-start | bytes 835592 | tf_op jit(solution)/shard_map/ppermute | solution.py:91
  42.0 1.9 %turn_residents.1.turned = bf16[2,256,2560]{2,1,0:T(8,128)(2,1)S(1)} custom-call(bf16[2048,512]{1,0:T(8,128)(2,1)S(1)} %bitcast.12, bf16[16,16,512]{2,1,0:T(8,128)(2,1)} %get-tuple-element.61.res_x, bf16[8,16,896]{2,1,0:T(8,128)(2,1)S(1)} %collective-permute-done.1.from_y, bf16[1,16,896]{2,1,0:T(8,128)(2,1)S(1)} %collective-permute-done.3.corner), custom_call_target="tpu_custom_call" | custom-call | flops 578813952 | bytes 5238784 | tf_op jit(solution)/shard_map/turn_residents/pallas_call | solution.py:593
  43.8 4.6 %collective-permute-done.10.far.far_in = bf16[2,9,16,128]{3,2,1,0:T(8,128)(2,1)S(1)} collective-permute-done((bf16[2,9,16,128]{3,2,1,0:T(8,128)(2,1)S(1)}, bf16[2,9,16,128]{3,2,1,0:T(8,128)(2,1)S(1)}, u32[]{:S(2)}, u32[]{:S(2)}) %collective-permute-start.10) | collective-permute-done | bytes 73760 | tf_op jit(solution)/shard_map/ppermute | solution.py:108
  48.4 1.0 %collective-permute-start.11 = (bf16[2,2,2,16,128]{4,3,2,1,0:T(8,128)(2,1)S(1)}, bf16[2,2,2,16,128]{4,3,2,1,0:T(8,128)(2,1)S(1)}, u32[]{:S(2)}, u32[]{:S(2)}) collective-permute-start(bf16[2,2,2,16,128]{4,3,2,1,0:T(8,128)(2,1)S(1)} %corner_pack.3), channel_id=1, source_target_pairs={{0,16},{1,17},{2,18},{3,19},{4,20},{5,21},{6,22},{7,23},{8,24},{9,... | collective-permute-start | bytes 98312 | tf_op jit(solution)/shard_map/ppermute | solution.py:91
  49.4 3.0 %third_main.1 = (f32[4,736,256]{2,1,0:T(8,128)S(1)}, f32[2,9,17,16,128]{4,3,2,1,0:T(8,128)S(1)}) custom-call(s32[1]{0:T(128)} %bitcast.even_ref, bf16[2,8,16,16,128]{4,3,2,1,0:T(8,128)(2,1)S(1)} %copy-done.2, bf16[16,16,384]{2,1,0:T(8,128)(2,1)} %collective-permute-done.from_x, bf16[8,16,896]{2,1,0:T(8,128)(2,1)S(1)} %collective-permute-done.1.from_y, ...), custom_call_target="tpu_custom_call" | custom-call | flops 1157627904 | bytes 19447812 | tf_op jit(solution)/shard_map/third_main/pallas_call | solution.py:593
  52.5 4.3 %third_corner.1 = (f32[2,8,16,16,128]{4,3,2,1,0:T(8,128)}, bf16[2,16,16,128]{3,2,1,0:T(8,128)(2,1)S(1)}, f32[2,8,16,128]{3,2,1,0:T(8,128)S(1)}, bf16[2,16,128]{2...) custom-call(s32[1]{0:T(128)} %bitcast.even_ref, bf16[2,8,16,16,128]{4,3,2,1,0:T(8,128)(2,1)S(1)} %copy-done.2, ...), custom_call_target="tpu_custom_call" | custom-call | flops 864026624 | bytes 24961028 | tf_op jit(solution)/shard_map/third_corner/pallas_call | solution.py:593
  56.7 0.7 copy-done.4
  57.4 0.7 copy-done.6
  58.1 0.6 copy-done.8
  58.7 1.6 %collective-permute-done.15 = bf16[256,256]{1,0:T(8,128)(2,1)S(1)} collective-permute-done((bf16[256,256]{1,0:T(8,128)(2,1)}, bf16[256,256]{1,0:T(8,128)(2,1)S(1)}, u32[]{:S(2)}, u32[]{:S(2)}) %collective-permute-start.15) | collective-permute-done | bytes 131104 | tf_op jit(solution)/shard_map/ppermute | solution.py:102
  60.3 0.9 %copy-done.5 = f32[256,256]{1,0:T(8,128)S(1)} copy-done((f32[256,256]{1,0:T(8,128)S(1)}, f32[256,256]{1,0:T(8,128)}, u32[]{:S(2)}) %copy-start.5) | copy-done | bytes 262168
  61.3 0.1 collective-permute-start.16
  61.4 4.2 %collective-permute-done.16 = bf16[128,256]{1,0:T(8,128)(2,1)S(1)} collective-permute-done((bf16[128,256]{1,0:T(8,128)(2,1)S(1)}, bf16[128,256]{1,0:T(8,128)(2,1)S(1)}, u32[]{:S(2)}, u32[]{:S(2)}) %collective-permute-start.16) | collective-permute-done | bytes 65568 | tf_op jit(solution)/shard_map/ppermute | solution.py:102
  65.6 0.1 collective-permute-start.17
  65.7 3.9 %collective-permute-done.17 = bf16[64,256]{1,0:T(8,128)(2,1)S(1)} collective-permute-done((bf16[64,256]{1,0:T(8,128)(2,1)S(1)}, bf16[64,256]{1,0:T(8,128)(2,1)S(1)}, u32[]{:S(2)}, u32[]{:S(2)}) %collective-permute-start.17) | collective-permute-done | bytes 32800 | tf_op jit(solution)/shard_map/ppermute | solution.py:102
  69.6 0.1 collective-permute-start.18
  69.7 1.1 %collective-permute-start.12 = (bf16[2,16,128]{2,1,0:T(8,128)(2,1)S(1)}, bf16[2,16,128]{2,1,0:T(8,128)(2,1)S(1)}, u32[]{:S(2)}, u32[]{:S(2)}) collective-permute-start(bf16[2,16,128]{2,1,0:T(8,128)(2,1)S(1)} %get-tuple-element.64), channel_id=1, source_target_pairs={{0,16},{1,17},{2,18},{3,19},{4,20},{5,21},{6,22},{7,23},{8,24},{9,... | collective-permute-start | bytes 24584 | tf_op jit(solution)/shard_map/ppermute | solution.py:91
  70.8 2.6 %collective-permute-done.12.corner_ref = bf16[2,16,128]{2,1,0:T(8,128)(2,1)S(1)} collective-permute-done((bf16[2,16,128]{2,1,0:T(8,128)(2,1)S(1)}, bf16[2,16,128]{2,1,0:T(8,128)(2,1)S(1)}, u32[]{:S(2)}, u32[]{:S(2)}) %collective-permute-start.12) | collective-permute-done | bytes 8224 | tf_op jit(solution)/shard_map/ppermute | solution.py:91
  73.4 0.9 %copy-done.7 = bf16[2,16,16,128]{3,2,1,0:T(8,128)(2,1)S(1)} copy-done((bf16[2,16,16,128]{3,2,1,0:T(8,128)(2,1)S(1)}, bf16[2,16,16,128]{3,2,1,0:T(8,128)(2,1)}, u32[]{:S(2)}) %copy-start.7) | copy-done | bytes 131096
  74.3 0.9 %copy-done.9 = f32[2,8,16,128]{3,2,1,0:T(8,128)S(1)} copy-done((f32[2,8,16,128]{3,2,1,0:T(8,128)S(1)}, f32[2,8,16,128]{3,2,1,0:T(8,128)}, u32[]{:S(2)}) %copy-start.9) | copy-done | bytes 131096
  75.2 1.1 %collective-permute-start.13 = (bf16[2,16,16,128]{3,2,1,0:T(8,128)(2,1)S(1)}, bf16[2,16,16,128]{3,2,1,0:T(8,128)(2,1)S(1)}, u32[]{:S(2)}, u32[]{:S(2)}) collective-permute-start(bf16[2,16,16,128]{3,2,1,0:T(8,128)(2,1)S(1)} %get-tuple-element.66), channel_id=1, source_target_pairs={{0,16},{1,17},{2,18},{3,19},{4,20},{5,21},{6,22},{7,23},{8,24},{9,... | collective-permute-start | bytes 393224 | tf_op jit(solution)/shard_map/ppermute | solution.py:91
  76.4 1.0 %collective-permute-start.19 = (f32[32,256]{1,0:T(8,128)S(1)}, f32[32,256]{1,0:T(8,128)S(1)}, u32[]{:S(2)}, u32[]{:S(2)}) collective-permute-start(f32[32,256]{1,0:T(8,128)S(1)} %convert_add_fusion.refs_0_), channel_id=1, source_target_pairs={{0,16},{1,17},{2,18},{3,19},{4,20},{5,21},{6,22},{7,23},{8,24},{9,... | collective-permute-start | bytes 98312 | tf_op jit(solution)/shard_map/ppermute | solution.py:91
  77.4 5.3 %collective-permute-done.14.side = bf16[2,8,16,128]{3,2,1,0:T(8,128)(2,1)S(1)} collective-permute-done((bf16[2,8,16,128]{3,2,1,0:T(8,128)(2,1)S(1)}, bf16[2,8,16,128]{3,2,1,0:T(8,128)(2,1)S(1)}, u32[]{:S(2)}, u32[]{:S(2)}) %collective-permute-start.14) | collective-permute-done | bytes 65568 | tf_op jit(solution)/shard_map/ppermute | solution.py:91
  82.8 2.4 %last.1 = (f32[2,8,16,16,128]{4,3,2,1,0:T(8,128)}, f32[32,256]{1,0:T(8,128)}) custom-call(f32[2,8,16,16,128]{4,3,2,1,0:T(8,128)} %get-tuple-element.62.old_hbm, bf16[2,16,16,128]{3,2,1,0:T(8,128)(2,1)S(1)} %collective-permute-done.13.face, bf16[2,8,16,128]{3,2,1,0:T(8,128)(2,1)S(1)} %collective-permute-done.14.side, ...), custom_call_target="tpu_custom_call", output_to_operand_aliasing={{0}: (0, {})} | custom-call | bytes 4489216 | tf_op jit(solution)/shard_map/last/pallas_call | solution.py:593
  (35 shorter events, 0.1 us)
Async XLA Ops:
  0.6 9.6 %copy-start.10 = (bf16[729,729]{1,0:T(8,128)(2,1)S(1)}, bf16[729,729]{1,0:T(8,128)(2,1)}, u32[]{:S(2)}) copy-start(bf16[729,729]{1,0:T(8,128)(2,1)} %matrix_ref.3) | copy-start | bytes 3188650
  2.8 16.5 %collective-permute-start.1 = (bf16[8,16,896]{2,1,0:T(8,128)(2,1)}, bf16[8,16,896]{2,1,0:T(8,128)(2,1)S(1)}, u32[]{:S(2)}, u32[]{:S(2)}) collective-permute-start(bf16[8,16,896]{2,1,0:T(8,128)(2,1)} %get-tuple-element.40), channel_id=1, source_target_pairs={{0,15},{1,0},{2,1},{3,2},{4,3},{5,4},{6,5},{7,6},{8,7},{9,8},{10,9... | collective-permute-start | bytes 688136 | tf_op jit(solution)/shard_map/ppermute | solution.py:91
  8.2 12.6 %collective-permute-start = (bf16[16,16,384]{2,1,0:T(8,128)(2,1)}, bf16[16,16,384]{2,1,0:T(8,128)(2,1)}, u32[]{:S(2)}, u32[]{:S(2)}) collective-permute-start(bf16[16,16,384]{2,1,0:T(8,128)(2,1)} %get-tuple-element.39), channel_id=1, source_target_pairs={{0,16},{1,17},{2,18},{3,19},{4,20},{5,21},{6,22},{7,23},{8,24},{9,... | collective-permute-start | bytes 589832 | tf_op jit(solution)/shard_map/ppermute | solution.py:91
  9.8 15.9 %collective-permute-start.2 = (bf16[16,16,512]{2,1,0:T(8,128)(2,1)}, bf16[16,16,512]{2,1,0:T(8,128)(2,1)}, u32[]{:S(2)}, u32[]{:S(2)}) collective-permute-start(bf16[16,16,512]{2,1,0:T(8,128)(2,1)} %get-tuple-element.44), channel_id=1, source_target_pairs={{0,16},{1,17},{2,18},{3,19},{4,20},{5,21},{6,22},{7,23},{8,24},{9,... | collective-permute-start | bytes 786440 | tf_op jit(solution)/shard_map/ppermute | solution.py:91
  14.1 9.2 %copy-start.2 = (bf16[2,8,16,16,128]{4,3,2,1,0:T(8,128)(2,1)S(1)}, bf16[2,8,16,16,128]{4,3,2,1,0:T(8,128)(2,1)}, u32[]{:S(2)}) copy-start(bf16[2,8,16,16,128]{4,3,2,1,0:T(8,128)(2,1)} %vec.11) | copy-start | bytes 3145732
  17.9 1.4 %copy-start = (bf16[2,736,768]{2,1,0:T(8,128)(2,1)}, bf16[2,736,768]{2,1,0:T(8,128)(2,1)S(1)}, u32[]{:S(2)}) copy-start(bf16[2,736,768]{2,1,0:T(8,128)(2,1)S(1)} %order_cells.3.refs_1_) | copy-start | bytes 6782980
  19.3 4.0 %copy-start.1 = (bf16[2,736,768]{2,1,0:T(8,128)(2,1)S(1)}, bf16[2,736,768]{2,1,0:T(8,128)(2,1)}, u32[]{:S(2)}) copy-start(bf16[2,736,768]{2,1,0:T(8,128)(2,1)} %copy-done) | copy-start | bytes 6782980
  19.3 6.4 %collective-permute-start.3 = (bf16[1,16,896]{2,1,0:T(8,128)(2,1)S(1)}, bf16[1,16,896]{2,1,0:T(8,128)(2,1)S(1)}, u32[]{:S(2)}, u32[]{:S(2)}) collective-permute-start(bf16[1,16,896]{2,1,0:T(8,128)(2,1)S(1)} %slice.4), channel_id=1, source_target_pairs={{0,16},{1,17},{2,18},{3,19},{4,20},{5,21},{6,22},{7,23},{8,24},{9,... | collective-permute-start | bytes 86024 | tf_op jit(solution)/shard_map/ppermute | solution.py:91
  27.4 8.6 %collective-permute-start.4 = (bf16[2,2,17,16,128]{4,3,2,1,0:T(8,128)(2,1)S(1)}, bf16[2,2,17,16,128]{4,3,2,1,0:T(8,128)(2,1)S(1)}, u32[]{:S(2)}, u32[]{:S(2)}) collective-permute-start(bf16[2,2,17,16,128]{4,3,2,1,0:T(8,128)(2,1)S(1)} %get-tuple-element.49), channel_id=1, source_target_pairs={{0,16},{1,17},{2,18},{3,19},{4,20},{5,21},{6,22},{7,23},{8,24},{9,... | collective-permute-start | bytes 835592 | tf_op jit(solution)/shard_map/ppermute | solution.py:91
  28.1 1.3 %collective-permute-start.5 = (bf16[2,9,16,128]{3,2,1,0:T(8,128)(2,1)S(1)}, bf16[2,9,16,128]{3,2,1,0:T(8,128)(2,1)S(1)}, u32[]{:S(2)}, u32[]{:S(2)}) collective-permute-start(bf16[2,9,16,128]{3,2,1,0:T(8,128)(2,1)S(1)} %get-tuple-element.50), channel_id=1, source_target_pairs={{0,1},{1,0},{2,3},{3,2},{4,5},{5,4},{6,7},{7,6},{8,9},{9,8},{10,11... | collective-permute-start | bytes 221192 | tf_op jit(solution)/shard_map/ppermute | solution.py:102
  28.1 6.5 %collective-permute-start.6 = (bf16[2,9,16,128]{3,2,1,0:T(8,128)(2,1)S(1)}, bf16[2,9,16,128]{3,2,1,0:T(8,128)(2,1)S(1)}, u32[]{:S(2)}, u32[]{:S(2)}) collective-permute-start(bf16[2,9,16,128]{3,2,1,0:T(8,128)(2,1)S(1)} %get-tuple-element.51), channel_id=1, source_target_pairs={{0,15},{1,2},{2,1},{3,4},{4,3},{5,6},{6,5},{7,8},{8,7},{9,10},{10,... | collective-permute-start | bytes 221192 | tf_op jit(solution)/shard_map/ppermute | solution.py:108
  34.6 4.3 %collective-permute-start.7 = (bf16[2,2,2,16,128]{4,3,2,1,0:T(8,128)(2,1)S(1)}, bf16[2,2,2,16,128]{4,3,2,1,0:T(8,128)(2,1)S(1)}, u32[]{:S(2)}, u32[]{:S(2)}) collective-permute-start(bf16[2,2,2,16,128]{4,3,2,1,0:T(8,128)(2,1)S(1)} %corner_pack.2), channel_id=1, source_target_pairs={{0,16},{1,17},{2,18},{3,19},{4,20},{5,21},{6,22},{7,23},{8,24},{9,... | collective-permute-start | bytes 98312 | tf_op jit(solution)/shard_map/ppermute | solution.py:91
  38.8 3.1 %copy-start.3 = (bf16[8,16,16,512]{3,2,1,0:T(8,128)(2,1)S(1)}, bf16[8,16,16,512]{3,2,1,0:T(8,128)(2,1)}, u32[]{:S(2)}) copy-start(bf16[8,16,16,512]{3,2,1,0:T(8,128)(2,1)} %res_hbm.1) | copy-start | bytes 6291460
  40.8 8.6 %collective-permute-start.8 = (bf16[2,2,17,16,128]{4,3,2,1,0:T(8,128)(2,1)S(1)}, bf16[2,2,17,16,128]{4,3,2,1,0:T(8,128)(2,1)S(1)}, u32[]{:S(2)}, u32[]{:S(2)}) collective-permute-start(bf16[2,2,17,16,128]{4,3,2,1,0:T(8,128)(2,1)S(1)} %get-tuple-element.54), channel_id=1, source_target_pairs={{0,16},{1,17},{2,18},{3,19},{4,20},{5,21},{6,22},{7,23},{8,24},{9,... | collective-permute-start | bytes 835592 | tf_op jit(solution)/shard_map/ppermute | solution.py:91
  42.0 6.5 %collective-permute-start.10 = (bf16[2,9,16,128]{3,2,1,0:T(8,128)(2,1)S(1)}, bf16[2,9,16,128]{3,2,1,0:T(8,128)(2,1)S(1)}, u32[]{:S(2)}, u32[]{:S(2)}) collective-permute-start(bf16[2,9,16,128]{3,2,1,0:T(8,128)(2,1)S(1)} %get-tuple-element.56), channel_id=1, source_target_pairs={{0,15},{1,2},{2,1},{3,4},{4,3},{5,6},{6,5},{7,8},{8,7},{9,10},{10,... | collective-permute-start | bytes 221192 | tf_op jit(solution)/shard_map/ppermute | solution.py:108
  42.0 6.5 %collective-permute-start.9 = (bf16[2,9,16,128]{3,2,1,0:T(8,128)(2,1)S(1)}, bf16[2,9,16,128]{3,2,1,0:T(8,128)(2,1)S(1)}, u32[]{:S(2)}, u32[]{:S(2)}) collective-permute-start(bf16[2,9,16,128]{3,2,1,0:T(8,128)(2,1)S(1)} %get-tuple-element.55), channel_id=1, source_target_pairs={{0,1},{1,0},{2,3},{3,2},{4,5},{5,4},{6,7},{7,6},{8,9},{9,8},{10,11... | collective-permute-start | bytes 221192 | tf_op jit(solution)/shard_map/ppermute | solution.py:102
  48.4 4.0 %collective-permute-start.11 = (bf16[2,2,2,16,128]{4,3,2,1,0:T(8,128)(2,1)S(1)}, bf16[2,2,2,16,128]{4,3,2,1,0:T(8,128)(2,1)S(1)}, u32[]{:S(2)}, u32[]{:S(2)}) collective-permute-start(bf16[2,2,2,16,128]{4,3,2,1,0:T(8,128)(2,1)S(1)} %corner_pack.3), channel_id=1, source_target_pairs={{0,16},{1,17},{2,18},{3,19},{4,20},{5,21},{6,22},{7,23},{8,24},{9,... | collective-permute-start | bytes 98312 | tf_op jit(solution)/shard_map/ppermute | solution.py:91
  56.7 0.7 copy-start.4
  57.4 0.7 copy-start.6
  58.1 0.6 copy-start.8
  58.7 1.6 %collective-permute-start.15 = (bf16[256,256]{1,0:T(8,128)(2,1)}, bf16[256,256]{1,0:T(8,128)(2,1)S(1)}, u32[]{:S(2)}, u32[]{:S(2)}) collective-permute-start(bf16[256,256]{1,0:T(8,128)(2,1)} %get-tuple-element.69), channel_id=1, source_target_pairs={{0,1},{1,0},{2,3},{3,2},{4,5},{5,4},{6,7},{7,6},{8,9},{9,8},{10,11... | collective-permute-start | bytes 393224 | tf_op jit(solution)/shard_map/ppermute | solution.py:102
  60.3 1.0 %copy-start.5 = (f32[256,256]{1,0:T(8,128)S(1)}, f32[256,256]{1,0:T(8,128)}, u32[]{:S(2)}) copy-start(f32[256,256]{1,0:T(8,128)} %copy-done.4) | copy-start | bytes 786436
  61.3 4.3 %collective-permute-start.16 = (bf16[128,256]{1,0:T(8,128)(2,1)S(1)}, bf16[128,256]{1,0:T(8,128)(2,1)S(1)}, u32[]{:S(2)}, u32[]{:S(2)}) collective-permute-start(bf16[128,256]{1,0:T(8,128)(2,1)S(1)} %get-tuple-element.71), channel_id=1, source_target_pairs={{0,2},{1,3},{2,0},{3,1},{4,6},{5,7},{6,4},{7,5},{8,10},{9,11},{10,... | collective-permute-start | bytes 196616 | tf_op jit(solution)/shard_map/ppermute | solution.py:102
  65.6 4.0 %collective-permute-start.17 = (bf16[64,256]{1,0:T(8,128)(2,1)S(1)}, bf16[64,256]{1,0:T(8,128)(2,1)S(1)}, u32[]{:S(2)}, u32[]{:S(2)}) collective-permute-start(bf16[64,256]{1,0:T(8,128)(2,1)S(1)} %get-tuple-element.73), channel_id=1, source_target_pairs={{0,4},{1,5},{2,6},{3,7},{4,0},{5,1},{6,2},{7,3},{8,12},{9,13},{10,... | collective-permute-start | bytes 98312 | tf_op jit(solution)/shard_map/ppermute | solution.py:102
  69.6 6.7 %collective-permute-start.18 = (bf16[32,256]{1,0:T(8,128)(2,1)S(1)}, bf16[32,256]{1,0:T(8,128)(2,1)S(1)}, u32[]{:S(2)}, u32[]{:S(2)}) collective-permute-start(bf16[32,256]{1,0:T(8,128)(2,1)S(1)} %get-tuple-element.75), channel_id=1, source_target_pairs={{0,8},{1,9},{2,10},{3,11},{4,12},{5,13},{6,14},{7,15},{8,0},{9,1},... | collective-permute-start | bytes 49160 | tf_op jit(solution)/shard_map/ppermute | solution.py:102
  69.7 3.7 %collective-permute-start.12 = (bf16[2,16,128]{2,1,0:T(8,128)(2,1)S(1)}, bf16[2,16,128]{2,1,0:T(8,128)(2,1)S(1)}, u32[]{:S(2)}, u32[]{:S(2)}) collective-permute-start(bf16[2,16,128]{2,1,0:T(8,128)(2,1)S(1)} %get-tuple-element.64), channel_id=1, source_target_pairs={{0,16},{1,17},{2,18},{3,19},{4,20},{5,21},{6,22},{7,23},{8,24},{9,... | collective-permute-start | bytes 24584 | tf_op jit(solution)/shard_map/ppermute | solution.py:91
  73.4 0.9 %copy-start.7 = (bf16[2,16,16,128]{3,2,1,0:T(8,128)(2,1)S(1)}, bf16[2,16,16,128]{3,2,1,0:T(8,128)(2,1)}, u32[]{:S(2)}) copy-start(bf16[2,16,16,128]{3,2,1,0:T(8,128)(2,1)} %copy-done.6) | copy-start | bytes 393220
  74.3 0.9 %copy-start.9 = (f32[2,8,16,128]{3,2,1,0:T(8,128)S(1)}, f32[2,8,16,128]{3,2,1,0:T(8,128)}, u32[]{:S(2)}) copy-start(f32[2,8,16,128]{3,2,1,0:T(8,128)} %copy-done.8) | copy-start | bytes 393220
  75.2 7.5 %collective-permute-start.13 = (bf16[2,16,16,128]{3,2,1,0:T(8,128)(2,1)S(1)}, bf16[2,16,16,128]{3,2,1,0:T(8,128)(2,1)S(1)}, u32[]{:S(2)}, u32[]{:S(2)}) collective-permute-start(bf16[2,16,16,128]{3,2,1,0:T(8,128)(2,1)S(1)} %get-tuple-element.66), channel_id=1, source_target_pairs={{0,16},{1,17},{2,18},{3,19},{4,20},{5,21},{6,22},{7,23},{8,24},{9,... | collective-permute-start | bytes 393224 | tf_op jit(solution)/shard_map/ppermute | solution.py:91
  76.4 6.4 %collective-permute-start.14 = (bf16[2,8,16,128]{3,2,1,0:T(8,128)(2,1)S(1)}, bf16[2,8,16,128]{3,2,1,0:T(8,128)(2,1)S(1)}, u32[]{:S(2)}, u32[]{:S(2)}) collective-permute-start(bf16[2,8,16,128]{3,2,1,0:T(8,128)(2,1)S(1)} %get-tuple-element.67), channel_id=1, source_target_pairs={{0,1},{1,2},{2,3},{3,4},{4,5},{5,6},{6,7},{7,8},{8,9},{9,10},{10,1... | collective-permute-start | bytes 196616 | tf_op jit(solution)/shard_map/ppermute | solution.py:91
  76.4 6.4 %collective-permute-start.19 = (f32[32,256]{1,0:T(8,128)S(1)}, f32[32,256]{1,0:T(8,128)S(1)}, u32[]{:S(2)}, u32[]{:S(2)}) collective-permute-start(f32[32,256]{1,0:T(8,128)S(1)} %convert_add_fusion.refs_0_), channel_id=1, source_target_pairs={{0,16},{1,17},{2,18},{3,19},{4,20},{5,21},{6,22},{7,23},{8,24},{9,... | collective-permute-start | bytes 98312 | tf_op jit(solution)/shard_map/ppermute | solution.py:91

commit v16 on v14

--- a/solution.py
+++ b/solution.py
@@ -597,6 +597,10 @@
     )(*operands)
 
 
+def in_vmem(value):
+    return pltpu.with_memory_space_constraint(value, pltpu.VMEM)
+
+
 def body(vectors, resident, inv_mass, potential, cell_matrix, connectivity):
     sz = Sizes(vectors, resident, inv_mass, connectivity)
     nx, ny = lax.axis_size("dx"), lax.axis_size("dy")
@@ -663,17 +667,17 @@
         )
         return [face, near, far], swap_x(corner)
 
+    state = [vectors, *map(in_vmem, (from_x, from_y, own_inv, own_pot))]
     prod, ghost_x, ghost_y = call(
         functools.partial(first_main, sz, n_mat), "first_main", flops,
         [products, like((2, sz.ey) + tile, f32), like((2, sz.ex) + tile, f32)], main_scratch,
-        [vectors, from_x, from_y, own_inv, own_pot, *mats],
+        [*state, *mats],
     )
     res_x, acc, face, near, far, last_x, last_field = call(
         functools.partial(first_corner, sz, n_mat), "first_corner", small_flops,
         [res_x, state_grid, *messages, like(sz.edge, f32), like((2,) + tile, f32)], corner_scratch,
         [
-            parity, res_x, vectors, from_x, from_y, ghost_corner, own_inv, own_pot, ghost_x, ghost_y, prod,
-            *mats,
+            parity, res_x, *state[:3], ghost_corner, *state[3:], ghost_x, ghost_y, prod, *mats,
         ],
         scalar_first=True, aliases={1: 0},
     )
@@ -683,7 +687,7 @@
         [resident.reshape(-1, res_count), res_x, from_y, ghost_corner],
     )
     got, corner = exchange(face, near, far)
-    state = [vectors, from_x, from_y, own_inv, own_pot, ghost_x, ghost_y]
+    state += [ghost_x, ghost_y]
     ends = [last_x, last_field]
     prod, y1 = call(
         functools.partial(second_main, sz, n_mat), "second_main", flops,

time: 78.7 us -> 78.7 us (level)
  no operation moved by 1% of the time
where the time goes in v16:
time: 78.7 us; the launch traced here: 78.1 us
  Pallas kernels  30.2 us (38%)
  starting transfers between devices  21.6 us (27%)
  waiting for transfers between devices  19.7 us (25%)
  local copies, waits for them, and re-layouts  5.58 us (7%)
  between operations  1.01 us (1%)
    pallas_call x15, Pallas kernels, call(): pl.pallas_call(kernel, in_specs=specs, out_specs=out_specs, out_shape=out...  30.2 us
    ppermute x11, starting transfers between devices, send(): return lax.ppermute(value, ('dx', 'dy'), pairs)  16.5 us
    ppermute x2, waiting for transfers between devices, swap_y(): far = lax.ppermute(far, 'dy', far_pairs)  9.28 us
    ppermute x11, waiting for transfers between devices, send(): return lax.ppermute(value, ('dx', 'dy'), pairs)  8.76 us
    all_to_all x1, starting transfers between devices, body(): lax.all_to_all(pieces, ('dx', 'dy'), 0, 0, axis_index_groups=groups)  3.53 us
    unnamed x18, local copies, waits for them, and re-layouts  3.24 us
    ppermute x3, waiting for transfers between devices, send_near(): return lax.ppermute(value, 'dy', pairs)  1.65 us
  transfers between devices with their start and end apart: 17, of which 6 were waited for; matrix products, arithmetic and copies ran while one was open for 3% of the time, Pallas kernels for 23%

profile of v16, /device:TPU:0, one launch (start us, length us, event | category | flops | bytes accessed | tf_op | source)
XLA Modules:
  0.0 78.1 jit_solution(14101448817360746863)
XLA Ops:
  0.6 2.1 %pack.1 = (bf16[16,16,384]{2,1,0:T(8,128)(2,1)}, bf16[8,16,896]{2,1,0:T(8,128)(2,1)}, bf16[16,16,512]{2,1,0:T(8,128)(2,1)}, s32[4,729]{1,0:T(4,128)S(1)}) custom-call(bf16[2,8,16,16,128]{4,3,2,1,0:T(8,128)(2,1)} %vec.11, bf16[8,16,16,512]{3,2,1,0:T(8,128)(2,1)} %res_hbm.1, f32[8,16,16]{2,1,0:T(8,128)} %inv_hbm.1, f32[8,16,16]{2,1,0:T(8,128)} %pot_hbm.1, ...), custom_call_target="tpu_custom_call" | custom-call | bytes 3873568 | tf_op jit(solution)/shard_map/pack/pallas_call | solution.py:587
  2.8 3.0 %collective-permute-start = (bf16[16,16,384]{2,1,0:T(8,128)(2,1)}, bf16[16,16,384]{2,1,0:T(8,128)(2,1)}, u32[]{:S(2)}, u32[]{:S(2)}) collective-permute-start(bf16[16,16,384]{2,1,0:T(8,128)(2,1)} %get-tuple-element.33), channel_id=1, source_target_pairs={{0,16},{1,17},{2,18},{3,19},{4,20},{5,21},{6,22},{7,23},{8,24},{9,... | collective-permute-start | bytes 589832 | tf_op jit(solution)/shard_map/ppermute | solution.py:91
  5.8 3.7 %collective-permute-start.1 = (bf16[8,16,896]{2,1,0:T(8,128)(2,1)}, bf16[8,16,896]{2,1,0:T(8,128)(2,1)S(1)}, u32[]{:S(2)}, u32[]{:S(2)}) collective-permute-start(bf16[8,16,896]{2,1,0:T(8,128)(2,1)} %get-tuple-element.34), channel_id=1, source_target_pairs={{0,15},{1,0},{2,1},{3,2},{4,3},{5,4},{6,5},{7,6},{8,7},{9,8},{10,9... | collective-permute-start | bytes 688136 | tf_op jit(solution)/shard_map/ppermute | solution.py:91
  9.5 0.5 collective-permute-start.2
  10.0 3.8 %order_cells.3.refs_1_ = bf16[2,736,768]{2,1,0:T(8,128)(2,1)S(1)} custom-call(bf16[729,729]{1,0:T(8,128)(2,1)S(1)} %copy-done.8, s32[4,729]{1,0:T(4,128)S(1)} %get-tuple-element.35.conn_ref), custom_call_target="tpu_custom_call" | custom-call | flops 3623878656 | bytes 3335538 | tf_op jit(solution)/shard_map/order_cells/pallas_call | solution.py:587
  13.8 0.0 copy-start.2
  13.8 3.8 %order_cells.2.refs_0_ = bf16[2,736,768]{2,1,0:T(8,128)(2,1)S(1)} custom-call(bf16[729,729]{1,0:T(8,128)(2,1)S(1)} %copy-done.8, s32[4,729]{1,0:T(4,128)S(1)} %get-tuple-element.35.conn_ref), custom_call_target="tpu_custom_call" | custom-call | flops 3623878656 | bytes 3335538 | tf_op jit(solution)/shard_map/order_cells/pallas_call | solution.py:587
  17.6 1.4 %copy-done = bf16[2,736,768]{2,1,0:T(8,128)(2,1)} copy-done((bf16[2,736,768]{2,1,0:T(8,128)(2,1)}, bf16[2,736,768]{2,1,0:T(8,128)(2,1)S(1)}, u32[]{:S(2)}) %copy-start) | copy-done | bytes 2261016
  19.0 0.0 collective-permute-done.1.from_y
  19.0 1.6 %collective-permute-start.3 = (bf16[1,16,896]{2,1,0:T(8,128)(2,1)S(1)}, bf16[1,16,896]{2,1,0:T(8,128)(2,1)S(1)}, u32[]{:S(2)}, u32[]{:S(2)}) collective-permute-start(bf16[1,16,896]{2,1,0:T(8,128)(2,1)S(1)} %slice.4), channel_id=1, source_target_pairs={{0,16},{1,17},{2,18},{3,19},{4,20},{5,21},{6,22},{7,23},{8,24},{9,... | collective-permute-start | bytes 86024 | tf_op jit(solution)/shard_map/ppermute | solution.py:91
  20.6 0.0 collective-permute-done.from_x
  20.6 1.2 %broadcast_in_dim.4.own_inv = f32[8,16,16,128]{3,2,1,0:T(8,128)S(1)} broadcast(f32[8,16,16]{2,1,0:T(8,128)} %inv_hbm.1), dimensions={0,1,2} | broadcast | bytes 1056768 | tf_op jit(solution)/shard_map/broadcast_in_dim | solution.py:638
  21.8 1.2 %broadcast_in_dim.5.own_pot = f32[8,16,16,128]{3,2,1,0:T(8,128)S(1)} broadcast(f32[8,16,16]{2,1,0:T(8,128)} %pot_hbm.1), dimensions={0,1,2} | broadcast | bytes 1056768 | tf_op jit(solution)/shard_map/broadcast_in_dim | solution.py:639
  23.0 2.4 %first_main.1 = (f32[4,736,256]{2,1,0:T(8,128)S(1)}, f32[2,16,16,128]{3,2,1,0:T(8,128)S(1)}, f32[2,8,16,128]{3,2,1,0:T(8,128)S(1)}) custom-call(bf16[2,8,16,16,128]{4,3,2,1,0:T(8,128)(2,1)S(1)} %copy-done.2, bf16[16,16,384]{2,1,0:T(8,128)(2,1)} %collective-permute-done.from_x, bf16[8,16,896]{2,1,0:T(8,128)(2,1)S(1)} %collective-permute-done.1.from_y, ...), custom_call_target="tpu_custom_call" | custom-call | flops 1157627904 | bytes 11501568 | tf_op jit(solution)/shard_map/first_main/pallas_call | solution.py:587
  25.4 1.8 %first_corner.1 = (bf16[16,16,512]{2,1,0:T(8,128)(2,1)}, f32[2,9,17,16,128]{4,3,2,1,0:T(8,128)S(1)}, bf16[2,2,17,16,128]{4,3,2,1,0:T(8,128)(2,1)S(1)}, bf16[2,9,...) custom-call(s32[1]{0:T(128)} %bitcast.even_ref, ...), custom_call_target="tpu_custom_call", output_to_operand_aliasing={{0}: (1, {})} | custom-call | flops 192937984 | bytes 15020036 | tf_op jit(solution)/shard_map/first_corner/pallas_call | solution.py:587
  27.2 0.7 collective-permute-start.4
  27.8 0.0 collective-permute-start.5
  27.9 1.0 %collective-permute-start.6 = (bf16[2,9,16,128]{3,2,1,0:T(8,128)(2,1)S(1)}, bf16[2,9,16,128]{3,2,1,0:T(8,128)(2,1)S(1)}, u32[]{:S(2)}, u32[]{:S(2)}) collective-permute-start(bf16[2,9,16,128]{3,2,1,0:T(8,128)(2,1)S(1)} %get-tuple-element.45), channel_id=1, source_target_pairs={{0,15},{1,2},{2,1},{3,4},{4,3},{5,6},{6,5},{7,8},{8,7},{9,10},{10,... | collective-permute-start | bytes 221192 | tf_op jit(solution)/shard_map/ppermute | solution.py:108
  28.8 0.3 collective-permute-done.5.near.near_in
  29.1 5.2 %collective-permute-done.6.far.far_in = bf16[2,9,16,128]{3,2,1,0:T(8,128)(2,1)S(1)} collective-permute-done((bf16[2,9,16,128]{3,2,1,0:T(8,128)(2,1)S(1)}, bf16[2,9,16,128]{3,2,1,0:T(8,128)(2,1)S(1)}, u32[]{:S(2)}, u32[]{:S(2)}) %collective-permute-start.6) | collective-permute-done | bytes 73760 | tf_op jit(solution)/shard_map/ppermute | solution.py:108
  34.3 1.4 %collective-permute-start.7 = (bf16[2,2,2,16,128]{4,3,2,1,0:T(8,128)(2,1)S(1)}, bf16[2,2,2,16,128]{4,3,2,1,0:T(8,128)(2,1)S(1)}, u32[]{:S(2)}, u32[]{:S(2)}) collective-permute-start(bf16[2,2,2,16,128]{4,3,2,1,0:T(8,128)(2,1)S(1)} %corner_pack.2), channel_id=1, source_target_pairs={{0,16},{1,17},{2,18},{3,19},{4,20},{5,21},{6,22},{7,23},{8,24},{9,... | collective-permute-start | bytes 98312 | tf_op jit(solution)/shard_map/ppermute | solution.py:91
  35.8 0.0 collective-permute-done.4.face_in
  35.8 2.8 %second_main.1 = (f32[4,736,256]{2,1,0:T(8,128)S(1)}, f32[2,9,17,16,128]{4,3,2,1,0:T(8,128)S(1)}) custom-call(s32[1]{0:T(128)} %bitcast.even_ref, bf16[2,8,16,16,128]{4,3,2,1,0:T(8,128)(2,1)S(1)} %copy-done.2, bf16[16,16,384]{2,1,0:T(8,128)(2,1)} %collective-permute-done.from_x, bf16[8,16,896]{2,1,0:T(8,128)(2,1)S(1)} %collective-permute-done.1.from_y, ...), custom_call_target="tpu_custom_call" | custom-call | flops 1157627904 | bytes 16941060 | tf_op jit(solution)/shard_map/second_main/pallas_call | solution.py:587
  38.6 0.0 collective-permute-done.7.corner_in
  38.6 0.0 copy-start.3
  38.6 2.0 %second_corner.1 = (f32[2,9,17,16,128]{4,3,2,1,0:T(8,128)S(1)}, bf16[2,2,17,16,128]{4,3,2,1,0:T(8,128)(2,1)S(1)}, bf16[2,9,16,128]{3,2,1,0:T(8,128)(2,1)S(1)}, b...) custom-call(s32[1]{0:T(128)} %bitcast.even_ref, bf16[2,8,16,16,128]{4,3,2,1,0:T(8,128)(2,1)S(1)} %copy-done.2, ...), custom_call_target="tpu_custom_call" | custom-call | flops 192937984 | bytes 17498116 | tf_op jit(solution)/shard_map/second_corner/pallas_call | solution.py:587
  40.6 1.1 %collective-permute-start.8 = (bf16[2,2,17,16,128]{4,3,2,1,0:T(8,128)(2,1)S(1)}, bf16[2,2,17,16,128]{4,3,2,1,0:T(8,128)(2,1)S(1)}, u32[]{:S(2)}, u32[]{:S(2)}) collective-permute-start(bf16[2,2,17,16,128]{4,3,2,1,0:T(8,128)(2,1)S(1)} %get-tuple-element.48), channel_id=1, source_target_pairs={{0,16},{1,17},{2,18},{3,19},{4,20},{5,21},{6,22},{7,23},{8,24},{9,... | collective-permute-start | bytes 835592 | tf_op jit(solution)/shard_map/ppermute | solution.py:91
  41.7 0.0 collective-permute-start.9
  41.7 0.5 collective-permute-start.10
  42.3 1.9 %turn_residents.1.turned = bf16[2,256,2560]{2,1,0:T(8,128)(2,1)S(1)} custom-call(bf16[2048,512]{1,0:T(8,128)(2,1)S(1)} %bitcast.4, bf16[16,16,512]{2,1,0:T(8,128)(2,1)} %get-tuple-element.55.res_x, bf16[8,16,896]{2,1,0:T(8,128)(2,1)S(1)} %collective-permute-done.1.from_y, bf16[1,16,896]{2,1,0:T(8,128)(2,1)S(1)} %collective-permute-done.3.corner), custom_call_target="tpu_custom_call" | custom-call | flops 578813952 | bytes 5238784 | tf_op jit(solution)/shard_map/turn_residents/pallas_call | solution.py:587
  44.1 4.1 %collective-permute-done.10.far.far_in = bf16[2,9,16,128]{3,2,1,0:T(8,128)(2,1)S(1)} collective-permute-done((bf16[2,9,16,128]{3,2,1,0:T(8,128)(2,1)S(1)}, bf16[2,9,16,128]{3,2,1,0:T(8,128)(2,1)S(1)}, u32[]{:S(2)}, u32[]{:S(2)}) %collective-permute-start.10) | collective-permute-done | bytes 73760 | tf_op jit(solution)/shard_map/ppermute | solution.py:108
  48.2 1.0 %collective-permute-start.11 = (bf16[2,2,2,16,128]{4,3,2,1,0:T(8,128)(2,1)S(1)}, bf16[2,2,2,16,128]{4,3,2,1,0:T(8,128)(2,1)S(1)}, u32[]{:S(2)}, u32[]{:S(2)}) collective-permute-start(bf16[2,2,2,16,128]{4,3,2,1,0:T(8,128)(2,1)S(1)} %corner_pack.3), channel_id=1, source_target_pairs={{0,16},{1,17},{2,18},{3,19},{4,20},{5,21},{6,22},{7,23},{8,24},{9,... | collective-permute-start | bytes 98312 | tf_op jit(solution)/shard_map/ppermute | solution.py:91
  49.2 3.0 %third_main.1 = (f32[4,736,256]{2,1,0:T(8,128)S(1)}, f32[2,9,17,16,128]{4,3,2,1,0:T(8,128)S(1)}) custom-call(s32[1]{0:T(128)} %bitcast.even_ref, bf16[2,8,16,16,128]{4,3,2,1,0:T(8,128)(2,1)S(1)} %copy-done.2, bf16[16,16,384]{2,1,0:T(8,128)(2,1)} %collective-permute-done.from_x, bf16[8,16,896]{2,1,0:T(8,128)(2,1)S(1)} %collective-permute-done.1.from_y, ...), custom_call_target="tpu_custom_call" | custom-call | flops 1157627904 | bytes 19447812 | tf_op jit(solution)/shard_map/third_main/pallas_call | solution.py:587
  52.2 0.0 collective-permute-done.11.corner_in
  52.2 3.6 %third_corner.1 = (f32[2,8,16,16,128]{4,3,2,1,0:T(8,128)}, bf16[2,16,16,128]{3,2,1,0:T(8,128)(2,1)S(1)}, f32[2,8,16,128]{3,2,1,0:T(8,128)S(1)}, bf16[2,16,128]{2...) custom-call(s32[1]{0:T(128)} %bitcast.even_ref, bf16[2,8,16,16,128]{4,3,2,1,0:T(8,128)(2,1)S(1)} %copy-done.2, ...), custom_call_target="tpu_custom_call" | custom-call | flops 864026624 | bytes 24961028 | tf_op jit(solution)/shard_map/third_corner/pallas_call | solution.py:587
  55.8 0.1 collective-permute-start.15
  55.9 1.3 %collective-permute-done.15.taken = bf16[256,256]{1,0:T(8,128)(2,1)S(1)} collective-permute-done((bf16[256,256]{1,0:T(8,128)(2,1)S(1)}, bf16[256,256]{1,0:T(8,128)(2,1)S(1)}, u32[]{:S(2)}, u32[]{:S(2)}) %collective-permute-start.15) | collective-permute-done | bytes 131104 | tf_op jit(solution)/shard_map/ppermute | solution.py:102
  57.3 0.7 pieces.1
  58.0 3.5 %all-to-all-start = ((bf16[16,32,256]{2,1,0:T(8,128)(2,1)}), bf16[16,32,256]{2,1,0:T(8,128)(2,1)S(1)}, u32[]{:S(2)}, u32[]{:S(2)}) async-start(bf16[16,32,256]{2,1,0:T(8,128)(2,1)} %bitcast.3), calls=%async_computation | async-start | bytes 524288 | tf_op jit(solution)/shard_map/all_to_all | solution.py:729
  61.5 1.9 %collective-permute-start.12 = (bf16[2,16,128]{2,1,0:T(8,128)(2,1)S(1)}, bf16[2,16,128]{2,1,0:T(8,128)(2,1)S(1)}, u32[]{:S(2)}, u32[]{:S(2)}) collective-permute-start(bf16[2,16,128]{2,1,0:T(8,128)(2,1)S(1)} %get-tuple-element.58), channel_id=1, source_target_pairs={{0,16},{1,17},{2,18},{3,19},{4,20},{5,21},{6,22},{7,23},{8,24},{9,... | collective-permute-start | bytes 24584 | tf_op jit(solution)/shard_map/ppermute | solution.py:91
  63.4 2.4 %collective-permute-done.12.corner_ref = bf16[2,16,128]{2,1,0:T(8,128)(2,1)S(1)} collective-permute-done((bf16[2,16,128]{2,1,0:T(8,128)(2,1)S(1)}, bf16[2,16,128]{2,1,0:T(8,128)(2,1)S(1)}, u32[]{:S(2)}, u32[]{:S(2)}) %collective-permute-start.12) | collective-permute-done | bytes 8224 | tf_op jit(solution)/shard_map/ppermute | solution.py:91
  65.8 0.9 %copy-done.5 = bf16[2,16,16,128]{3,2,1,0:T(8,128)(2,1)S(1)} copy-done((bf16[2,16,16,128]{3,2,1,0:T(8,128)(2,1)S(1)}, bf16[2,16,16,128]{3,2,1,0:T(8,128)(2,1)}, u32[]{:S(2)}) %copy-start.5) | copy-done | bytes 131096
  66.7 0.9 %copy-done.7 = f32[2,8,16,128]{3,2,1,0:T(8,128)S(1)} copy-done((f32[2,8,16,128]{3,2,1,0:T(8,128)S(1)}, f32[2,8,16,128]{3,2,1,0:T(8,128)}, u32[]{:S(2)}) %copy-start.7) | copy-done | bytes 131096
  67.6 1.6 %collective-permute-start.13 = (bf16[2,16,16,128]{3,2,1,0:T(8,128)(2,1)S(1)}, bf16[2,16,16,128]{3,2,1,0:T(8,128)(2,1)S(1)}, u32[]{:S(2)}, u32[]{:S(2)}) collective-permute-start(bf16[2,16,16,128]{3,2,1,0:T(8,128)(2,1)S(1)} %get-tuple-element.60), channel_id=1, source_target_pairs={{0,16},{1,17},{2,18},{3,19},{4,20},{5,21},{6,22},{7,23},{8,24},{9,... | collective-permute-start | bytes 393224 | tf_op jit(solution)/shard_map/ppermute | solution.py:91
  69.2 0.0 collective-permute-start.14
  69.2 6.4 %collective-permute-done.14.side = bf16[2,8,16,128]{3,2,1,0:T(8,128)(2,1)S(1)} collective-permute-done((bf16[2,8,16,128]{3,2,1,0:T(8,128)(2,1)S(1)}, bf16[2,8,16,128]{3,2,1,0:T(8,128)(2,1)S(1)}, u32[]{:S(2)}, u32[]{:S(2)}) %collective-permute-start.14) | collective-permute-done | bytes 65568 | tf_op jit(solution)/shard_map/ppermute | solution.py:91
  75.6 0.0 collective-permute-done.13.face
  75.6 2.4 %last.1 = (f32[2,8,16,16,128]{4,3,2,1,0:T(8,128)}, f32[32,256]{1,0:T(8,128)}) custom-call(f32[2,8,16,16,128]{4,3,2,1,0:T(8,128)} %get-tuple-element.56.old_hbm, bf16[2,16,16,128]{3,2,1,0:T(8,128)(2,1)S(1)} %collective-permute-done.13.face, bf16[2,8,16,128]{3,2,1,0:T(8,128)(2,1)S(1)} %collective-permute-done.14.side, ...), custom_call_target="tpu_custom_call", output_to_operand_aliasing={{0}: (0, {})} | custom-call | bytes 4685824 | tf_op jit(solution)/shard_map/last/pallas_call | solution.py:587
  (22 shorter events, 0.1 us)
Async XLA Ops:
  0.6 9.4 %copy-start.8 = (bf16[729,729]{1,0:T(8,128)(2,1)S(1)}, bf16[729,729]{1,0:T(8,128)(2,1)}, u32[]{:S(2)}) copy-start(bf16[729,729]{1,0:T(8,128)(2,1)} %matrix_ref.3) | copy-start | bytes 3188650
  2.8 17.8 %collective-permute-start = (bf16[16,16,384]{2,1,0:T(8,128)(2,1)}, bf16[16,16,384]{2,1,0:T(8,128)(2,1)}, u32[]{:S(2)}, u32[]{:S(2)}) collective-permute-start(bf16[16,16,384]{2,1,0:T(8,128)(2,1)} %get-tuple-element.33), channel_id=1, source_target_pairs={{0,16},{1,17},{2,18},{3,19},{4,20},{5,21},{6,22},{7,23},{8,24},{9,... | collective-permute-start | bytes 589832 | tf_op jit(solution)/shard_map/ppermute | solution.py:91
  5.8 13.2 %collective-permute-start.1 = (bf16[8,16,896]{2,1,0:T(8,128)(2,1)}, bf16[8,16,896]{2,1,0:T(8,128)(2,1)S(1)}, u32[]{:S(2)}, u32[]{:S(2)}) collective-permute-start(bf16[8,16,896]{2,1,0:T(8,128)(2,1)} %get-tuple-element.34), channel_id=1, source_target_pairs={{0,15},{1,0},{2,1},{3,2},{4,3},{5,4},{6,5},{7,6},{8,7},{9,8},{10,9... | collective-permute-start | bytes 688136 | tf_op jit(solution)/shard_map/ppermute | solution.py:91
  9.5 15.9 %collective-permute-start.2 = (bf16[16,16,512]{2,1,0:T(8,128)(2,1)}, bf16[16,16,512]{2,1,0:T(8,128)(2,1)}, u32[]{:S(2)}, u32[]{:S(2)}) collective-permute-start(bf16[16,16,512]{2,1,0:T(8,128)(2,1)} %get-tuple-element.38), channel_id=1, source_target_pairs={{0,16},{1,17},{2,18},{3,19},{4,20},{5,21},{6,22},{7,23},{8,24},{9,... | collective-permute-start | bytes 786440 | tf_op jit(solution)/shard_map/ppermute | solution.py:91
  13.8 9.2 %copy-start.2 = (bf16[2,8,16,16,128]{4,3,2,1,0:T(8,128)(2,1)S(1)}, bf16[2,8,16,16,128]{4,3,2,1,0:T(8,128)(2,1)}, u32[]{:S(2)}) copy-start(bf16[2,8,16,16,128]{4,3,2,1,0:T(8,128)(2,1)} %vec.11) | copy-start | bytes 3145732
  17.6 1.4 %copy-start = (bf16[2,736,768]{2,1,0:T(8,128)(2,1)}, bf16[2,736,768]{2,1,0:T(8,128)(2,1)S(1)}, u32[]{:S(2)}) copy-start(bf16[2,736,768]{2,1,0:T(8,128)(2,1)S(1)} %order_cells.2.refs_0_) | copy-start | bytes 6782980
  19.0 4.0 %copy-start.1 = (bf16[2,736,768]{2,1,0:T(8,128)(2,1)S(1)}, bf16[2,736,768]{2,1,0:T(8,128)(2,1)}, u32[]{:S(2)}) copy-start(bf16[2,736,768]{2,1,0:T(8,128)(2,1)} %copy-done) | copy-start | bytes 6782980
  19.0 6.4 %collective-permute-start.3 = (bf16[1,16,896]{2,1,0:T(8,128)(2,1)S(1)}, bf16[1,16,896]{2,1,0:T(8,128)(2,1)S(1)}, u32[]{:S(2)}, u32[]{:S(2)}) collective-permute-start(bf16[1,16,896]{2,1,0:T(8,128)(2,1)S(1)} %slice.4), channel_id=1, source_target_pairs={{0,16},{1,17},{2,18},{3,19},{4,20},{5,21},{6,22},{7,23},{8,24},{9,... | collective-permute-start | bytes 86024 | tf_op jit(solution)/shard_map/ppermute | solution.py:91
  27.2 8.6 %collective-permute-start.4 = (bf16[2,2,17,16,128]{4,3,2,1,0:T(8,128)(2,1)S(1)}, bf16[2,2,17,16,128]{4,3,2,1,0:T(8,128)(2,1)S(1)}, u32[]{:S(2)}, u32[]{:S(2)}) collective-permute-start(bf16[2,2,17,16,128]{4,3,2,1,0:T(8,128)(2,1)S(1)} %get-tuple-element.43), channel_id=1, source_target_pairs={{0,16},{1,17},{2,18},{3,19},{4,20},{5,21},{6,22},{7,23},{8,24},{9,... | collective-permute-start | bytes 835592 | tf_op jit(solution)/shard_map/ppermute | solution.py:91
  27.8 1.3 %collective-permute-start.5 = (bf16[2,9,16,128]{3,2,1,0:T(8,128)(2,1)S(1)}, bf16[2,9,16,128]{3,2,1,0:T(8,128)(2,1)S(1)}, u32[]{:S(2)}, u32[]{:S(2)}) collective-permute-start(bf16[2,9,16,128]{3,2,1,0:T(8,128)(2,1)S(1)} %get-tuple-element.44), channel_id=1, source_target_pairs={{0,1},{1,0},{2,3},{3,2},{4,5},{5,4},{6,7},{7,6},{8,9},{9,8},{10,11... | collective-permute-start | bytes 221192 | tf_op jit(solution)/shard_map/ppermute | solution.py:102
  27.9 6.5 %collective-permute-start.6 = (bf16[2,9,16,128]{3,2,1,0:T(8,128)(2,1)S(1)}, bf16[2,9,16,128]{3,2,1,0:T(8,128)(2,1)S(1)}, u32[]{:S(2)}, u32[]{:S(2)}) collective-permute-start(bf16[2,9,16,128]{3,2,1,0:T(8,128)(2,1)S(1)} %get-tuple-element.45), channel_id=1, source_target_pairs={{0,15},{1,2},{2,1},{3,4},{4,3},{5,6},{6,5},{7,8},{8,7},{9,10},{10,... | collective-permute-start | bytes 221192 | tf_op jit(solution)/shard_map/ppermute | solution.py:108
  34.3 4.3 %collective-permute-start.7 = (bf16[2,2,2,16,128]{4,3,2,1,0:T(8,128)(2,1)S(1)}, bf16[2,2,2,16,128]{4,3,2,1,0:T(8,128)(2,1)S(1)}, u32[]{:S(2)}, u32[]{:S(2)}) collective-permute-start(bf16[2,2,2,16,128]{4,3,2,1,0:T(8,128)(2,1)S(1)} %corner_pack.2), channel_id=1, source_target_pairs={{0,16},{1,17},{2,18},{3,19},{4,20},{5,21},{6,22},{7,23},{8,24},{9,... | collective-permute-start | bytes 98312 | tf_op jit(solution)/shard_map/ppermute | solution.py:91
  38.6 3.7 %copy-start.3 = (bf16[8,16,16,512]{3,2,1,0:T(8,128)(2,1)S(1)}, bf16[8,16,16,512]{3,2,1,0:T(8,128)(2,1)}, u32[]{:S(2)}) copy-start(bf16[8,16,16,512]{3,2,1,0:T(8,128)(2,1)} %res_hbm.1) | copy-start | bytes 6291460
  40.6 8.6 %collective-permute-start.8 = (bf16[2,2,17,16,128]{4,3,2,1,0:T(8,128)(2,1)S(1)}, bf16[2,2,17,16,128]{4,3,2,1,0:T(8,128)(2,1)S(1)}, u32[]{:S(2)}, u32[]{:S(2)}) collective-permute-start(bf16[2,2,17,16,128]{4,3,2,1,0:T(8,128)(2,1)S(1)} %get-tuple-element.48), channel_id=1, source_target_pairs={{0,16},{1,17},{2,18},{3,19},{4,20},{5,21},{6,22},{7,23},{8,24},{9,... | collective-permute-start | bytes 835592 | tf_op jit(solution)/shard_map/ppermute | solution.py:91
  41.7 2.4 %collective-permute-start.9 = (bf16[2,9,16,128]{3,2,1,0:T(8,128)(2,1)S(1)}, bf16[2,9,16,128]{3,2,1,0:T(8,128)(2,1)S(1)}, u32[]{:S(2)}, u32[]{:S(2)}) collective-permute-start(bf16[2,9,16,128]{3,2,1,0:T(8,128)(2,1)S(1)} %get-tuple-element.49), channel_id=1, source_target_pairs={{0,1},{1,0},{2,3},{3,2},{4,5},{5,4},{6,7},{7,6},{8,9},{9,8},{10,11... | collective-permute-start | bytes 221192 | tf_op jit(solution)/shard_map/ppermute | solution.py:102
  41.7 6.5 %collective-permute-start.10 = (bf16[2,9,16,128]{3,2,1,0:T(8,128)(2,1)S(1)}, bf16[2,9,16,128]{3,2,1,0:T(8,128)(2,1)S(1)}, u32[]{:S(2)}, u32[]{:S(2)}) collective-permute-start(bf16[2,9,16,128]{3,2,1,0:T(8,128)(2,1)S(1)} %get-tuple-element.50), channel_id=1, source_target_pairs={{0,15},{1,2},{2,1},{3,4},{4,3},{5,6},{6,5},{7,8},{8,7},{9,10},{10,... | collective-permute-start | bytes 221192 | tf_op jit(solution)/shard_map/ppermute | solution.py:108
  48.2 4.0 %collective-permute-start.11 = (bf16[2,2,2,16,128]{4,3,2,1,0:T(8,128)(2,1)S(1)}, bf16[2,2,2,16,128]{4,3,2,1,0:T(8,128)(2,1)S(1)}, u32[]{:S(2)}, u32[]{:S(2)}) collective-permute-start(bf16[2,2,2,16,128]{4,3,2,1,0:T(8,128)(2,1)S(1)} %corner_pack.3), channel_id=1, source_target_pairs={{0,16},{1,17},{2,18},{3,19},{4,20},{5,21},{6,22},{7,23},{8,24},{9,... | collective-permute-start | bytes 98312 | tf_op jit(solution)/shard_map/ppermute | solution.py:91
  55.8 2.2 %copy-start.4 = (bf16[2,16,16,128]{3,2,1,0:T(8,128)(2,1)}, bf16[2,16,16,128]{3,2,1,0:T(8,128)(2,1)S(1)}, u32[]{:S(2)}) copy-start(bf16[2,16,16,128]{3,2,1,0:T(8,128)(2,1)S(1)} %get-tuple-element.59.face_in) | copy-start | bytes 393220
  55.8 2.2 %copy-start.6 = (f32[2,8,16,128]{3,2,1,0:T(8,128)}, f32[2,8,16,128]{3,2,1,0:T(8,128)S(1)}, u32[]{:S(2)}) copy-start(f32[2,8,16,128]{3,2,1,0:T(8,128)S(1)} %get-tuple-element.57.side_ref) | copy-start | bytes 393220
  55.8 1.4 %collective-permute-start.15 = (bf16[256,256]{1,0:T(8,128)(2,1)S(1)}, bf16[256,256]{1,0:T(8,128)(2,1)S(1)}, u32[]{:S(2)}, u32[]{:S(2)}) collective-permute-start(bf16[256,256]{1,0:T(8,128)(2,1)S(1)} %get-tuple-element.63), channel_id=1, source_target_pairs={{0,1},{1,0},{2,3},{3,2},{4,5},{5,4},{6,7},{7,6},{8,9},{9,8},{10,11... | collective-permute-start | bytes 393224 | tf_op jit(solution)/shard_map/ppermute | solution.py:102
  58.0 17.6 %all-to-all-start = ((bf16[16,32,256]{2,1,0:T(8,128)(2,1)}), bf16[16,32,256]{2,1,0:T(8,128)(2,1)S(1)}, u32[]{:S(2)}, u32[]{:S(2)}) async-start(bf16[16,32,256]{2,1,0:T(8,128)(2,1)} %bitcast.3), calls=%async_computation | async-start | bytes 524288 | tf_op jit(solution)/shard_map/all_to_all | solution.py:729
  61.5 4.2 %collective-permute-start.12 = (bf16[2,16,128]{2,1,0:T(8,128)(2,1)S(1)}, bf16[2,16,128]{2,1,0:T(8,128)(2,1)S(1)}, u32[]{:S(2)}, u32[]{:S(2)}) collective-permute-start(bf16[2,16,128]{2,1,0:T(8,128)(2,1)S(1)} %get-tuple-element.58), channel_id=1, source_target_pairs={{0,16},{1,17},{2,18},{3,19},{4,20},{5,21},{6,22},{7,23},{8,24},{9,... | collective-permute-start | bytes 24584 | tf_op jit(solution)/shard_map/ppermute | solution.py:91
  65.8 0.9 %copy-start.5 = (bf16[2,16,16,128]{3,2,1,0:T(8,128)(2,1)S(1)}, bf16[2,16,16,128]{3,2,1,0:T(8,128)(2,1)}, u32[]{:S(2)}) copy-start(bf16[2,16,16,128]{3,2,1,0:T(8,128)(2,1)} %copy-done.4) | copy-start | bytes 393220
  66.7 0.9 %copy-start.7 = (f32[2,8,16,128]{3,2,1,0:T(8,128)S(1)}, f32[2,8,16,128]{3,2,1,0:T(8,128)}, u32[]{:S(2)}) copy-start(f32[2,8,16,128]{3,2,1,0:T(8,128)} %copy-done.6) | copy-start | bytes 393220
  67.6 8.0 %collective-permute-start.13 = (bf16[2,16,16,128]{3,2,1,0:T(8,128)(2,1)S(1)}, bf16[2,16,16,128]{3,2,1,0:T(8,128)(2,1)S(1)}, u32[]{:S(2)}, u32[]{:S(2)}) collective-permute-start(bf16[2,16,16,128]{3,2,1,0:T(8,128)(2,1)S(1)} %get-tuple-element.60), channel_id=1, source_target_pairs={{0,16},{1,17},{2,18},{3,19},{4,20},{5,21},{6,22},{7,23},{8,24},{9,... | collective-permute-start | bytes 393224 | tf_op jit(solution)/shard_map/ppermute | solution.py:91
  69.2 6.4 %collective-permute-start.14 = (bf16[2,8,16,128]{3,2,1,0:T(8,128)(2,1)S(1)}, bf16[2,8,16,128]{3,2,1,0:T(8,128)(2,1)S(1)}, u32[]{:S(2)}, u32[]{:S(2)}) collective-permute-start(bf16[2,8,16,128]{3,2,1,0:T(8,128)(2,1)S(1)} %get-tuple-element.61), channel_id=1, source_target_pairs={{0,1},{1,2},{2,3},{3,4},{4,5},{5,6},{6,7},{7,8},{8,9},{9,10},{10,1... | collective-permute-start | bytes 196616 | tf_op jit(solution)/shard_map/ppermute | solution.py:91

commit v17 on v11

--- a/solution.py
+++ b/solution.py
@@ -109,12 +109,7 @@
     return send_near(near), far
 
 
-def order_kernel(sz, first, matrix_ref, conn_ref, out_ref, *load):
-    copy = None
-    if load:
-        copy = pltpu.make_async_copy(matrix_ref, *load)
-        copy.start()
-        matrix_ref = load[0]
+def order_kernel(sz, first, matrix_ref, conn_ref, out_ref):
     for slot in range(out_ref.shape[0]):
         cell = first + slot
         x0, y0, z0 = sz.origins[cell]
@@ -136,8 +131,6 @@
         index = index.astype(jnp.int32)
         row = lax.broadcasted_iota(jnp.int32, (sz.depth, sz.nodes), 0)
         pick = (row == index).astype(f32).astype(bf16)
-        if copy is not None and slot == 0:
-            copy.wait()
         half = jnp.dot(pick[: sz.rows], matrix_ref[...], preferred_element_type=f32)
         half = half.astype(bf16)
         cuts = list(range(0, sz.depth, TILE)) + [sz.depth]
@@ -209,25 +202,17 @@
         copy.wait()
 
 
-def turn_kernel(sz, pieces, res_ref, from_x, from_y, corner, out_ref):
+def turn_kernel(sz, res_ref, from_x, from_y, corner, out_ref):
     own = sz.own_edges * sz.ez
-    share = sz.res // out_ref.shape[0] // pieces
-
-    def put(g, columns, value):
-        for at in range(0, LANES, share):
-            owner = (g + at) // share
-            row = owner // 2 * share
-            out_ref[owner % 2, row : row + share, columns] = value[at : at + share]
-
     for g in range(0, sz.res, LANES):
         lanes = slice(g, g + LANES)
-        put(g, slice(0, own), res_ref[:, lanes].T)
+        out_ref[lanes, :own] = res_ref[:, lanes].T
         rest = sz.edges - sz.own_edges - sz.ey - sz.gx
         parts = [from_x[:, :, lanes], from_y[:, :, lanes], corner[:, :, lanes]]
         if rest:
             parts.append(jnp.zeros((rest, sz.ez, LANES), bf16))
         ghosts = jnp.concatenate(parts, axis=0)
-        put(g, slice(own, sz.edges * sz.ez), ghosts.reshape(-1, LANES).T)
+        out_ref[lanes, own:] = ghosts.reshape(-1, LANES).T
 
 
 def vectors_of(sz, edge):
@@ -477,8 +462,8 @@
                  last_x, last_field, acc_in, face_in, near_in, far_in, corner_in, prod_ref, y_ref,
                  y_corner, new_ref, turned, *refs):
     mats = refs[:n_mat]
-    out_hbm, edge_x, edge_y, face, side, corner, give, keep = refs[n_mat : n_mat + 8]
-    part_ref, sem, acc_ref, rows_ref, small_ref, tail_ref = refs[n_mat + 8 :]
+    out_hbm, edge_x, edge_y, face, side, corner, margin = refs[n_mat : n_mat + 7]
+    part_ref, sem, acc_ref, rows_ref, small_ref, tail_ref = refs[n_mat + 7 :]
     nodes = Nodes(sz, vec, from_x, from_y, own_inv, own_pot, ghost_x, ghost_y, last_field)
     sums = Sums(sz, even_ref[0] == 0, acc_in, face_in, near_in, far_in, corner_in)
     u_corner, new_corner = [], []
@@ -525,22 +510,12 @@
             copies[-1].start()
     for at in range(sz.own_edges + sz.ey + sz.gx, sz.edges):
         rows_ref[at] = jnp.zeros((sz.ez, sz.full), bf16)
-    rows = rows_ref[...].reshape(sz.edges * sz.ez, sz.full)
-    mine = even_ref[0]
-    for half, out in ((1 - mine, give), (mine, keep)):
-        local = jnp.dot(turned[half], rows, preferred_element_type=f32)
-        out[...] = (local * norm_scale).astype(out.dtype)
+    local = jnp.dot(
+        turned[...], rows_ref[...].reshape(sz.edges * sz.ez, sz.full), preferred_element_type=f32
+    )
+    margin[...] = (local * norm_scale).astype(bf16)
     for copy in copies:
         copy.wait()
-
-
-def pieces_kernel(keep, taken, pieces):
-    rows = pieces.shape[2]
-    for at in range(pieces.shape[1]):
-        span = slice(at * rows, (at + 1) * rows)
-        value = (keep[span] + taken[span].astype(f32)).astype(pieces.dtype)
-        for copy in range(pieces.shape[0]):
-            pieces[copy, at] = value
 
 
 def last_side_kernel(sz, side_ref, corner_ref, face_in, out_ref, face_out):
@@ -584,6 +559,9 @@
     if scalar_first:
         specs[0] = pl.BlockSpec(memory_space=pltpu.SMEM)
     out_specs = [pl.BlockSpec(memory_space=pltpu.HBM)] * out_hbm + [whole] * (len(out_shape) - out_hbm)
+    for source, target in (aliases or {}).items():
+        if source >= hbm:
+            specs[source] = out_specs[target] = pl.BlockSpec(memory_space=pl.ANY)
     out_shape = [pltpu.HBM(s.shape, s.dtype) for s in out_shape[:out_hbm]] + out_shape[out_hbm:]
     operands = [pltpu.with_memory_space_constraint(a, pltpu.HBM) for a in operands[:hbm]] + list(
         operands[hbm:]
@@ -629,8 +607,7 @@
         mats += call(
             functools.partial(order_kernel, sz, at), "order_cells", 4 * step * sz.depth**3,
             [like((step, sz.rows, sz.depth), bf16)],
-            [pltpu.VMEM(cell_matrix.shape, bf16), pltpu.SemaphoreType.DMA] if at == 0 else [],
-            [cell_matrix, conn], hbm=1 if at == 0 else 0,
+            [], [cell_matrix, conn],
         )
     own_inv = jnp.broadcast_to(inv_mass[..., None], inv_mass.shape + (width,))
     own_pot = jnp.broadcast_to(potential[..., None], inv_mass.shape + (width,))
@@ -678,8 +655,8 @@
         scalar_first=True,
     )
     (turned,) = call(
-        functools.partial(turn_kernel, sz, ny // 2), "turn_residents", flops // 2,
-        [like((2, res_count // 2, sz.edges * ez), bf16)], [],
+        functools.partial(turn_kernel, sz), "turn_residents", flops // 2,
+        [like((res_count, sz.edges * ez), bf16)], [],
         [resident.reshape(-1, res_count), from_x, from_y, ghost_corner],
     )
     got, corner = exchange(face, near, far)
@@ -701,27 +678,24 @@
         [products, state_grid], main_scratch,
         [parity, *state, acc, *got, y1, *mats], scalar_first=True,
     )
-    filtered, edge_x, edge_y, face, side, corner, give, keep = call(
+    filtered, edge_x, edge_y, face, side, corner, local = call(
         functools.partial(third_corner, sz, n_mat, norm_scale), "third_corner",
         small_flops + 2 * res_count * sz.edges * ez * full,
         [
             like(own, f32), like((blocks, sz.ey) + tile, f32), like((blocks, sz.ex - 1) + tile, f32),
             like((blocks, sz.ey) + tile, bf16), like((blocks, sz.ex) + tile, f32), like(sz.edge, bf16),
-            like((res_count // 2, full), bf16), like((res_count // 2, full), f32),
+            like((res_count, full), bf16),
         ],
         [pltpu.VMEM(own, f32), pltpu.SemaphoreType.DMA((sz.ex,)), pltpu.VMEM(grid, f32), pltpu.VMEM((sz.edges, ez, full), bf16)] + corner_scratch,
         [parity, *state, *ends, acc, *got, corner, prod, y1, y1_corner, y2, turned, *mats],
         scalar_first=True, out_hbm=1,
     )
 
-    (pieces,) = call(
-        pieces_kernel, "pieces", 0, [like((nx, ny // 2, res_count // ny, full), bf16)], [],
-        [keep, send_near(give)],
-    )
-    pieces = pieces.reshape(nx * ny // 2, -1, full)
-    groups = [[a * ny + b for a in range(nx) for b in range(c, ny, 2)] for c in range(2)]
-    pieces = lax.all_to_all(pieces, ("dx", "dy"), 0, 0, axis_index_groups=groups)
-    margin = jnp.sum(pieces.astype(f32), axis=0)
+    pieces = lax.all_to_all(local.reshape(ny, -1, full), "dy", 0, 0)
+    mine = jnp.sum(pieces.astype(f32), axis=0)
+    margin = mine
+    for steps in range(1, nx):
+        margin = margin + send(mine, steps, 0)
 
     corner = send(corner, 1, 0)
     side, face = call(

time: 71.3 us -> 70.9 us (level)
  local copies, waits for them, and re-layouts: 1.6 us -> 3.47 us
  starting transfers between devices: 21.8 us -> 20 us
  Pallas kernels: 23.6 us -> 22.3 us
  waiting for transfers between devices: 22.4 us -> 23.3 us
    all_to_all x1, waiting for transfers between devices: 0.01 us -> 6.12 us  [body(): pieces = lax.all_to_all(local.reshape(ny, -1, full), 'dy', 0, 0)]
    ppermute x10 -> x11, waiting for transfers between devices: 12 us -> 8.12 us  [send(): return lax.ppermute(value, ('dx', 'dy'), pairs)]
    unnamed x14 -> x16, local copies, waits for them, and re-layouts: 0.93 us -> 2.8 us
    ppermute x10 -> x11, starting transfers between devices: 15.3 us -> 13.5 us  [send(): return lax.ppermute(value, ('dx', 'dy'), pairs)]
    ppermute x3 -> x2, waiting for transfers between devices: 1.34 us -> 0.01 us  [send_near(): return lax.ppermute(value, 'dy', pairs)]
    pallas_call x15 -> x14, Pallas kernels: 23.6 us -> 22.3 us  [call(): pl.pallas_call(kernel, in_specs=specs, out_specs=out_specs, out_shape=out...]
  transfers between devices with their start and end apart: 16 -> 16, of which waited for: 8 -> 8; matrix products, arithmetic and copies ran while one was open for 1% -> 1% of each run, Pallas kernels for 23% -> 21%
where the time goes in v17:
time: 70.9 us; the launch traced here: 70.6 us
  waiting for transfers between devices  23.3 us (33%)
  Pallas kernels  22.3 us (31%)
  starting transfers between devices  20 us (28%)
  local copies, waits for them, and re-layouts  3.47 us (5%)
  between operations  0.84 us (1%)
    pallas_call x14, Pallas kernels, call(): pl.pallas_call(kernel, in_specs=specs, out_specs=out_specs, out_shape=out...  22.3 us
    ppermute x11, starting transfers between devices, send(): return lax.ppermute(value, ('dx', 'dy'), pairs)  13.5 us
    ppermute x2, waiting for transfers between devices, swap_y(): far = lax.ppermute(far, 'dy', far_pairs)  9.03 us
    ppermute x11, waiting for transfers between devices, send(): return lax.ppermute(value, ('dx', 'dy'), pairs)  8.12 us
    all_to_all x1, waiting for transfers between devices, body(): pieces = lax.all_to_all(local.reshape(ny, -1, full), 'dy', 0, 0)  6.12 us
    all_to_all x1, starting transfers between devices, body(): pieces = lax.all_to_all(local.reshape(ny, -1, full), 'dy', 0, 0)  3.53 us
    ppermute x2, starting transfers between devices, swap_y(): far = lax.ppermute(far, 'dy', far_pairs)  2.99 us
    unnamed x16, local copies, waits for them, and re-layouts  2.8 us
  transfers between devices with their start and end apart: 16, of which 8 were waited for; matrix products, arithmetic and copies ran while one was open for 1% of the time, Pallas kernels for 21%

profile of v17, /device:TPU:0, one launch (start us, length us, event | category | flops | bytes accessed | tf_op | source)
XLA Modules:
  0.0 70.6 jit_solution(5666193387847128278)
XLA Ops:
  0.6 0.0 copy-start.4
  0.6 2.0 %pack.1 = (bf16[16,16,896]{2,1,0:T(8,128)(2,1)S(1)}, bf16[8,16,896]{2,1,0:T(8,128)(2,1)}, s32[4,729]{1,0:T(4,128)S(1)}) custom-call(bf16[2,8,16,16,128]{4,3,2,1,0:T(8,128)(2,1)} %vec.11, bf16[8,16,16,512]{3,2,1,0:T(8,128)(2,1)} %res_hbm.1, f32[8,16,16]{2,1,0:T(8,128)} %inv_hbm.1, f32[8,16,16]{2,1,0:T(8,128)} %pot_hbm.1, s32[4,729]{1,0:T(4,128)} %bitcast.5), custom_call_target="tpu_custom_call" | custom-call | bytes 3873568 | tf_op jit(solution)/shard_map/pack/pallas_call | solution.py:569
  2.6 5.5 %collective-permute-start.1 = (bf16[8,16,896]{2,1,0:T(8,128)(2,1)}, bf16[8,16,896]{2,1,0:T(8,128)(2,1)S(1)}, u32[]{:S(2)}, u32[]{:S(2)}) collective-permute-start(bf16[8,16,896]{2,1,0:T(8,128)(2,1)} %get-tuple-element.33), channel_id=1, source_target_pairs={{0,15},{1,0},{2,1},{3,2},{4,3},{5,4},{6,5},{7,6},{8,7},{9,8},{10,9... | collective-permute-start | bytes 688136 | tf_op jit(solution)/shard_map/ppermute | solution.py:91
  8.1 1.5 %collective-permute-start = (bf16[16,16,896]{2,1,0:T(8,128)(2,1)S(1)}, bf16[16,16,896]{2,1,0:T(8,128)(2,1)S(1)}, u32[]{:S(2)}, u32[]{:S(2)}) collective-permute-start(bf16[16,16,896]{2,1,0:T(8,128)(2,1)S(1)} %get-tuple-element.32), channel_id=1, source_target_pairs={{0,16},{1,17},{2,18},{3,19},{4,20},{5,21},{6,22},{7,23},{8,24},{9,... | collective-permute-start | bytes 1376264 | tf_op jit(solution)/shard_map/ppermute | solution.py:91
  9.6 3.8 %order_cells.3.refs_1_ = bf16[2,736,768]{2,1,0:T(8,128)(2,1)S(1)} custom-call(bf16[729,729]{1,0:T(8,128)(2,1)S(1)} %copy-done.4, s32[4,729]{1,0:T(4,128)S(1)} %get-tuple-element.34.conn_ref), custom_call_target="tpu_custom_call" | custom-call | flops 3623878656 | bytes 3335538 | tf_op jit(solution)/shard_map/order_cells/pallas_call | solution.py:569
  13.4 0.0 copy-start.5
  13.4 1.2 %copy-done.5 = bf16[729,729]{1,0:T(8,128)(2,1)S(1)} copy-done((bf16[729,729]{1,0:T(8,128)(2,1)S(1)}, bf16[729,729]{1,0:T(8,128)(2,1)}, u32[]{:S(2)}) %copy-start.5) | copy-done | bytes 1062906
  14.7 3.8 %order_cells.2.refs_0_ = bf16[2,736,768]{2,1,0:T(8,128)(2,1)S(1)} custom-call(bf16[729,729]{1,0:T(8,128)(2,1)S(1)} %copy-done.5, s32[4,729]{1,0:T(4,128)S(1)} %get-tuple-element.34.conn_ref), custom_call_target="tpu_custom_call" | custom-call | flops 3623878656 | bytes 3335538 | tf_op jit(solution)/shard_map/order_cells/pallas_call | solution.py:569
  18.5 0.0 copy-start
  18.5 0.0 collective-permute-done.1.from_y
  18.5 0.6 collective-permute-start.2
  19.1 0.3 broadcast_in_dim.4.own_inv
  19.4 0.3 broadcast_in_dim.5.own_pot
  19.8 1.5 %first_main.1 = (f32[4,736,256]{2,1,0:T(8,128)S(1)}, f32[2,16,16,128]{3,2,1,0:T(8,128)S(1)}, f32[2,8,16,128]{3,2,1,0:T(8,128)S(1)}) custom-call(bf16[2,8,16,16,128]{4,3,2,1,0:T(8,128)(2,1)S(1)} %copy-done, bf16[16,16,896]{2,1,0:T(8,128)(2,1)S(1)} %collective-permute-done.from_x, bf16[8,16,896]{2,1,0:T(8,128)(2,1)S(1)} %collective-permute-done.1.from_y, ...), custom_call_target="tpu_custom_call" | custom-call | flops 1157627904 | bytes 11763712 | tf_op jit(solution)/shard_map/first_main/pallas_call | solution.py:569
  21.3 1.5 %collective-permute-done.2.corner = bf16[1,16,896]{2,1,0:T(8,128)(2,1)S(1)} collective-permute-done((bf16[1,16,896]{2,1,0:T(8,128)(2,1)S(1)}, bf16[1,16,896]{2,1,0:T(8,128)(2,1)S(1)}, u32[]{:S(2)}, u32[]{:S(2)}) %collective-permute-start.2) | collective-permute-done | bytes 28704 | tf_op jit(solution)/shard_map/ppermute | solution.py:91
  22.8 0.8 %first_corner.1 = (f32[2,9,17,16,128]{4,3,2,1,0:T(8,128)S(1)}, bf16[2,2,17,16,128]{4,3,2,1,0:T(8,128)(2,1)S(1)}, bf16[2,9,16,128]{3,2,1,0:T(8,128)(2,1)S(1)}, bf...) custom-call(s32[1]{0:T(128)} %bitcast.even_ref, ...), custom_call_target="tpu_custom_call" | custom-call | flops 192937984 | bytes 14757892 | tf_op jit(solution)/shard_map/first_corner/pallas_call | solution.py:569
  23.6 0.6 collective-permute-start.3
  24.2 0.0 collective-permute-start.4
  24.2 2.5 %collective-permute-start.5 = (bf16[2,9,16,128]{3,2,1,0:T(8,128)(2,1)S(1)}, bf16[2,9,16,128]{3,2,1,0:T(8,128)(2,1)S(1)}, u32[]{:S(2)}, u32[]{:S(2)}) collective-permute-start(bf16[2,9,16,128]{3,2,1,0:T(8,128)(2,1)S(1)} %get-tuple-element.43), channel_id=1, source_target_pairs={{0,15},{1,2},{2,1},{3,4},{4,3},{5,6},{6,5},{7,8},{8,7},{9,10},{10,... | collective-permute-start | bytes 221192 | tf_op jit(solution)/shard_map/ppermute | solution.py:108
  26.7 4.0 %collective-permute-done.5.far.far_in = bf16[2,9,16,128]{3,2,1,0:T(8,128)(2,1)S(1)} collective-permute-done((bf16[2,9,16,128]{3,2,1,0:T(8,128)(2,1)S(1)}, bf16[2,9,16,128]{3,2,1,0:T(8,128)(2,1)S(1)}, u32[]{:S(2)}, u32[]{:S(2)}) %collective-permute-start.5) | collective-permute-done | bytes 73760 | tf_op jit(solution)/shard_map/ppermute | solution.py:108
  30.7 1.5 %collective-permute-start.6 = (bf16[2,2,2,16,128]{4,3,2,1,0:T(8,128)(2,1)S(1)}, bf16[2,2,2,16,128]{4,3,2,1,0:T(8,128)(2,1)S(1)}, u32[]{:S(2)}, u32[]{:S(2)}) collective-permute-start(bf16[2,2,2,16,128]{4,3,2,1,0:T(8,128)(2,1)S(1)} %corner_pack.2), channel_id=1, source_target_pairs={{0,16},{1,17},{2,18},{3,19},{4,20},{5,21},{6,22},{7,23},{8,24},{9,... | collective-permute-start | bytes 98312 | tf_op jit(solution)/shard_map/ppermute | solution.py:91
  32.2 2.0 %second_main.1 = (f32[4,736,256]{2,1,0:T(8,128)S(1)}, f32[2,9,17,16,128]{4,3,2,1,0:T(8,128)S(1)}) custom-call(s32[1]{0:T(128)} %bitcast.even_ref, bf16[2,8,16,16,128]{4,3,2,1,0:T(8,128)(2,1)S(1)} %copy-done, bf16[16,16,896]{2,1,0:T(8,128)(2,1)S(1)} %collective-permute-done.from_x, bf16[8,16,896]{2,1,0:T(8,128)(2,1)S(1)} %collective-permute-done.1.from_y, ...), custom_call_target="tpu_custom_call" | custom-call | flops 1157627904 | bytes 17203204 | tf_op jit(solution)/shard_map/second_main/pallas_call | solution.py:569
  34.1 0.4 collective-permute-done.6.corner_in
  34.6 0.9 %second_corner.1 = (f32[2,9,17,16,128]{4,3,2,1,0:T(8,128)S(1)}, bf16[2,2,17,16,128]{4,3,2,1,0:T(8,128)(2,1)S(1)}, bf16[2,9,16,128]{3,2,1,0:T(8,128)(2,1)S(1)}, b...) custom-call(s32[1]{0:T(128)} %bitcast.even_ref, bf16[2,8,16,16,128]{4,3,2,1,0:T(8,128)(2,1)S(1)} %copy-done, ...), custom_call_target="tpu_custom_call" | custom-call | flops 192937984 | bytes 17760260 | tf_op jit(solution)/shard_map/second_corner/pallas_call | solution.py:569
  35.5 1.6 %collective-permute-start.7 = (bf16[2,2,17,16,128]{4,3,2,1,0:T(8,128)(2,1)S(1)}, bf16[2,2,17,16,128]{4,3,2,1,0:T(8,128)(2,1)S(1)}, u32[]{:S(2)}, u32[]{:S(2)}) collective-permute-start(bf16[2,2,17,16,128]{4,3,2,1,0:T(8,128)(2,1)S(1)} %get-tuple-element.46), channel_id=1, source_target_pairs={{0,16},{1,17},{2,18},{3,19},{4,20},{5,21},{6,22},{7,23},{8,24},{9,... | collective-permute-start | bytes 835592 | tf_op jit(solution)/shard_map/ppermute | solution.py:91
  37.1 0.5 collective-permute-start.9
  37.6 0.9 %turn_residents.1.turned = bf16[512,2560]{1,0:T(8,128)(2,1)S(1)} custom-call(bf16[2048,512]{1,0:T(8,128)(2,1)S(1)} %bitcast.4, bf16[16,16,896]{2,1,0:T(8,128)(2,1)S(1)} %collective-permute-done.from_x, bf16[8,16,896]{2,1,0:T(8,128)(2,1)S(1)} %collective-permute-done.1.from_y, bf16[1,16,896]{2,1,0:T(8,128)(2,1)S(1)} %collective-permute-done.2.corner), custom_call_target="tpu_custom_call" | custom-call | flops 578813952 | bytes 5435392 | tf_op jit(solution)/shard_map/turn_residents/pallas_call | solution.py:569
  38.5 0.0 collective-permute-done.8.near.near_in
  38.5 5.1 %collective-permute-done.9.far.far_in = bf16[2,9,16,128]{3,2,1,0:T(8,128)(2,1)S(1)} collective-permute-done((bf16[2,9,16,128]{3,2,1,0:T(8,128)(2,1)S(1)}, bf16[2,9,16,128]{3,2,1,0:T(8,128)(2,1)S(1)}, u32[]{:S(2)}, u32[]{:S(2)}) %collective-permute-start.9) | collective-permute-done | bytes 73760 | tf_op jit(solution)/shard_map/ppermute | solution.py:108
  43.5 0.5 collective-permute-start.10
  44.0 0.0 collective-permute-done.7.face_in
  44.0 2.1 %third_main.1 = (f32[4,736,256]{2,1,0:T(8,128)S(1)}, f32[2,9,17,16,128]{4,3,2,1,0:T(8,128)S(1)}) custom-call(s32[1]{0:T(128)} %bitcast.even_ref, bf16[2,8,16,16,128]{4,3,2,1,0:T(8,128)(2,1)S(1)} %copy-done, bf16[16,16,896]{2,1,0:T(8,128)(2,1)S(1)} %collective-permute-done.from_x, bf16[8,16,896]{2,1,0:T(8,128)(2,1)S(1)} %collective-permute-done.1.from_y, ...), custom_call_target="tpu_custom_call" | custom-call | flops 1157627904 | bytes 19709956 | tf_op jit(solution)/shard_map/third_main/pallas_call | solution.py:569
  46.1 1.3 %collective-permute-done.10.corner_in = bf16[2,2,2,16,128]{4,3,2,1,0:T(8,128)(2,1)S(1)} collective-permute-done((bf16[2,2,2,16,128]{4,3,2,1,0:T(8,128)(2,1)S(1)}, bf16[2,2,2,16,128]{4,3,2,1,0:T(8,128)(2,1)S(1)}, u32[]{:S(2)}, u32[]{:S(2)}) %collective-permute-start.10) | collective-permute-done | bytes 32800 | tf_op jit(solution)/shard_map/ppermute | solution.py:91
  47.4 3.8 %third_corner.1 = (f32[2,8,16,16,128]{4,3,2,1,0:T(8,128)}, f32[2,16,16,128]{3,2,1,0:T(8,128)S(1)}, f32[2,7,16,128]{3,2,1,0:T(8,128)S(1)}, bf16[2,16,16,128]{3,2,...) custom-call(s32[1]{0:T(128)} %bitcast.even_ref, ...), custom_call_target="tpu_custom_call" | custom-call | flops 864026624 | bytes 25468932 | tf_op jit(solution)/shard_map/third_corner/pallas_call | solution.py:569
  51.3 0.6 copy-done.2
  51.9 3.5 %all-to-all-start = ((bf16[16,32,256]{2,1,0:T(8,128)(2,1)}), bf16[16,32,256]{2,1,0:T(8,128)(2,1)S(1)}, u32[]{:S(2)}, u32[]{:S(2)}) async-start(bf16[16,32,256]{2,1,0:T(8,128)(2,1)} %bitcast.3), calls=%async_computation | async-start | bytes 524288 | tf_op jit(solution)/shard_map/all_to_all | solution.py:694
  55.4 0.6 collective-permute-start.11
  56.0 3.2 %collective-permute-done.11.corner_ref = bf16[2,16,128]{2,1,0:T(8,128)(2,1)S(1)} collective-permute-done((bf16[2,16,128]{2,1,0:T(8,128)(2,1)S(1)}, bf16[2,16,128]{2,1,0:T(8,128)(2,1)S(1)}, u32[]{:S(2)}, u32[]{:S(2)}) %collective-permute-start.11) | collective-permute-done | bytes 8224 | tf_op jit(solution)/shard_map/ppermute | solution.py:91
  59.2 0.1 collective-permute-start.13
  59.2 0.6 collective-permute-start.12
  59.8 6.1 %all-to-all-done = bf16[16,32,256]{2,1,0:T(8,128)(2,1)S(1)} async-done(((bf16[16,32,256]{2,1,0:T(8,128)(2,1)}), bf16[16,32,256]{2,1,0:T(8,128)(2,1)S(1)}, u32[]{:S(2)}, u32[]{:S(2)}) %all-to-all-start) | async-done | bytes 262176 | tf_op jit(solution)/shard_map/all_to_all | solution.py:694
  66.0 0.6 collective-permute-start.14
  66.5 0.0 collective-permute-done.13.side
  66.5 0.0 collective-permute-done.12.face
  66.5 0.9 %copy-done.3 = f32[2,7,16,128]{3,2,1,0:T(8,128)S(1)} copy-done((f32[2,7,16,128]{3,2,1,0:T(8,128)S(1)}, f32[2,7,16,128]{3,2,1,0:T(8,128)}, u32[]{:S(2)}) %copy-start.3) | copy-done | bytes 114712
  67.4 0.8 %last.1 = f32[2,8,16,16,128]{4,3,2,1,0:T(8,128)} custom-call(f32[2,8,16,16,128]{4,3,2,1,0:T(8,128)} %get-tuple-element.53.old_hbm, f32[2,16,16,128]{3,2,1,0:T(8,128)S(1)} %get-tuple-element.54.edge_x, f32[2,7,16,128]{3,2,1,0:T(8,128)S(1)} %copy-done.3, bf16[2,16,16,128]{3,2,1,0:T(8,128)(2,1)S(1)} %collective-permute-done.12.face, ...), custom_call_target="tpu_custom_call", output_to_operand_aliasing={{}: (0, {})} | custom-call | bytes 4767744 | tf_op jit(solution)/shard_map/last/pallas_call | solution.py:569
  68.2 1.7 %collective-permute-done.14 = f32[32,256]{1,0:T(8,128)S(1)} collective-permute-done((f32[32,256]{1,0:T(8,128)S(1)}, f32[32,256]{1,0:T(8,128)S(1)}, u32[]{:S(2)}, u32[]{:S(2)}) %collective-permute-start.14) | collective-permute-done | bytes 32800 | tf_op jit(solution)/shard_map/ppermute | solution.py:91
  69.9 0.6 add.8
  (19 shorter events, 0.1 us)
Async XLA Ops:
  0.6 9.0 %copy-start.4 = (bf16[729,729]{1,0:T(8,128)(2,1)S(1)}, bf16[729,729]{1,0:T(8,128)(2,1)}, u32[]{:S(2)}) copy-start(bf16[729,729]{1,0:T(8,128)(2,1)} %matrix_ref.3) | copy-start | bytes 3188650
  2.6 15.9 %collective-permute-start.1 = (bf16[8,16,896]{2,1,0:T(8,128)(2,1)}, bf16[8,16,896]{2,1,0:T(8,128)(2,1)S(1)}, u32[]{:S(2)}, u32[]{:S(2)}) collective-permute-start(bf16[8,16,896]{2,1,0:T(8,128)(2,1)} %get-tuple-element.33), channel_id=1, source_target_pairs={{0,15},{1,0},{2,1},{3,2},{4,3},{5,4},{6,5},{7,6},{8,7},{9,8},{10,9... | collective-permute-start | bytes 688136 | tf_op jit(solution)/shard_map/ppermute | solution.py:91
  8.1 11.0 %collective-permute-start = (bf16[16,16,896]{2,1,0:T(8,128)(2,1)S(1)}, bf16[16,16,896]{2,1,0:T(8,128)(2,1)S(1)}, u32[]{:S(2)}, u32[]{:S(2)}) collective-permute-start(bf16[16,16,896]{2,1,0:T(8,128)(2,1)S(1)} %get-tuple-element.32), channel_id=1, source_target_pairs={{0,16},{1,17},{2,18},{3,19},{4,20},{5,21},{6,22},{7,23},{8,24},{9,... | collective-permute-start | bytes 1376264 | tf_op jit(solution)/shard_map/ppermute | solution.py:91
  13.4 1.3 %copy-start.5 = (bf16[729,729]{1,0:T(8,128)(2,1)S(1)}, bf16[729,729]{1,0:T(8,128)(2,1)}, u32[]{:S(2)}) copy-start(bf16[729,729]{1,0:T(8,128)(2,1)} %matrix_ref.3) | copy-start | bytes 3188650
  14.7 4.4 %copy-start.6 = (f32[8,16,16]{2,1,0:T(8,128)S(1)}, f32[8,16,16]{2,1,0:T(8,128)}, u32[]{:S(2)}) copy-start(f32[8,16,16]{2,1,0:T(8,128)} %inv_hbm.1) | copy-start | bytes 24580
  14.7 4.7 %copy-start.7 = (f32[8,16,16]{2,1,0:T(8,128)S(1)}, f32[8,16,16]{2,1,0:T(8,128)}, u32[]{:S(2)}) copy-start(f32[8,16,16]{2,1,0:T(8,128)} %pot_hbm.1) | copy-start | bytes 24580
  18.5 1.3 %copy-start = (bf16[2,8,16,16,128]{4,3,2,1,0:T(8,128)(2,1)S(1)}, bf16[2,8,16,16,128]{4,3,2,1,0:T(8,128)(2,1)}, u32[]{:S(2)}) copy-start(bf16[2,8,16,16,128]{4,3,2,1,0:T(8,128)(2,1)} %vec.11) | copy-start | bytes 3145732
  18.5 4.2 %collective-permute-start.2 = (bf16[1,16,896]{2,1,0:T(8,128)(2,1)S(1)}, bf16[1,16,896]{2,1,0:T(8,128)(2,1)S(1)}, u32[]{:S(2)}, u32[]{:S(2)}) collective-permute-start(bf16[1,16,896]{2,1,0:T(8,128)(2,1)S(1)} %slice.4), channel_id=1, source_target_pairs={{0,16},{1,17},{2,18},{3,19},{4,20},{5,21},{6,22},{7,23},{8,24},{9,... | collective-permute-start | bytes 86024 | tf_op jit(solution)/shard_map/ppermute | solution.py:91
  23.6 8.6 %collective-permute-start.3 = (bf16[2,2,17,16,128]{4,3,2,1,0:T(8,128)(2,1)S(1)}, bf16[2,2,17,16,128]{4,3,2,1,0:T(8,128)(2,1)S(1)}, u32[]{:S(2)}, u32[]{:S(2)}) collective-permute-start(bf16[2,2,17,16,128]{4,3,2,1,0:T(8,128)(2,1)S(1)} %get-tuple-element.41), channel_id=1, source_target_pairs={{0,16},{1,17},{2,18},{3,19},{4,20},{5,21},{6,22},{7,23},{8,24},{9,... | collective-permute-start | bytes 835592 | tf_op jit(solution)/shard_map/ppermute | solution.py:91
  24.2 2.5 %collective-permute-start.4 = (bf16[2,9,16,128]{3,2,1,0:T(8,128)(2,1)S(1)}, bf16[2,9,16,128]{3,2,1,0:T(8,128)(2,1)S(1)}, u32[]{:S(2)}, u32[]{:S(2)}) collective-permute-start(bf16[2,9,16,128]{3,2,1,0:T(8,128)(2,1)S(1)} %get-tuple-element.42), channel_id=1, source_target_pairs={{0,1},{1,0},{2,3},{3,2},{4,5},{5,4},{6,7},{7,6},{8,9},{9,8},{10,11... | collective-permute-start | bytes 221192 | tf_op jit(solution)/shard_map/ppermute | solution.py:102
  24.2 6.5 %collective-permute-start.5 = (bf16[2,9,16,128]{3,2,1,0:T(8,128)(2,1)S(1)}, bf16[2,9,16,128]{3,2,1,0:T(8,128)(2,1)S(1)}, u32[]{:S(2)}, u32[]{:S(2)}) collective-permute-start(bf16[2,9,16,128]{3,2,1,0:T(8,128)(2,1)S(1)} %get-tuple-element.43), channel_id=1, source_target_pairs={{0,15},{1,2},{2,1},{3,4},{4,3},{5,6},{6,5},{7,8},{8,7},{9,10},{10,... | collective-permute-start | bytes 221192 | tf_op jit(solution)/shard_map/ppermute | solution.py:108
  30.7 3.9 %collective-permute-start.6 = (bf16[2,2,2,16,128]{4,3,2,1,0:T(8,128)(2,1)S(1)}, bf16[2,2,2,16,128]{4,3,2,1,0:T(8,128)(2,1)S(1)}, u32[]{:S(2)}, u32[]{:S(2)}) collective-permute-start(bf16[2,2,2,16,128]{4,3,2,1,0:T(8,128)(2,1)S(1)} %corner_pack.2), channel_id=1, source_target_pairs={{0,16},{1,17},{2,18},{3,19},{4,20},{5,21},{6,22},{7,23},{8,24},{9,... | collective-permute-start | bytes 98312 | tf_op jit(solution)/shard_map/ppermute | solution.py:91
  34.6 3.0 %copy-start.1 = (bf16[8,16,16,512]{3,2,1,0:T(8,128)(2,1)S(1)}, bf16[8,16,16,512]{3,2,1,0:T(8,128)(2,1)}, u32[]{:S(2)}) copy-start(bf16[8,16,16,512]{3,2,1,0:T(8,128)(2,1)} %res_hbm.1) | copy-start | bytes 6291460
  35.5 8.6 %collective-permute-start.7 = (bf16[2,2,17,16,128]{4,3,2,1,0:T(8,128)(2,1)S(1)}, bf16[2,2,17,16,128]{4,3,2,1,0:T(8,128)(2,1)S(1)}, u32[]{:S(2)}, u32[]{:S(2)}) collective-permute-start(bf16[2,2,17,16,128]{4,3,2,1,0:T(8,128)(2,1)S(1)} %get-tuple-element.46), channel_id=1, source_target_pairs={{0,16},{1,17},{2,18},{3,19},{4,20},{5,21},{6,22},{7,23},{8,24},{9,... | collective-permute-start | bytes 835592 | tf_op jit(solution)/shard_map/ppermute | solution.py:91
  37.0 1.4 %collective-permute-start.8 = (bf16[2,9,16,128]{3,2,1,0:T(8,128)(2,1)S(1)}, bf16[2,9,16,128]{3,2,1,0:T(8,128)(2,1)S(1)}, u32[]{:S(2)}, u32[]{:S(2)}) collective-permute-start(bf16[2,9,16,128]{3,2,1,0:T(8,128)(2,1)S(1)} %get-tuple-element.47), channel_id=1, source_target_pairs={{0,1},{1,0},{2,3},{3,2},{4,5},{5,4},{6,7},{7,6},{8,9},{9,8},{10,11... | collective-permute-start | bytes 221192 | tf_op jit(solution)/shard_map/ppermute | solution.py:102
  37.1 6.5 %collective-permute-start.9 = (bf16[2,9,16,128]{3,2,1,0:T(8,128)(2,1)S(1)}, bf16[2,9,16,128]{3,2,1,0:T(8,128)(2,1)S(1)}, u32[]{:S(2)}, u32[]{:S(2)}) collective-permute-start(bf16[2,9,16,128]{3,2,1,0:T(8,128)(2,1)S(1)} %get-tuple-element.48), channel_id=1, source_target_pairs={{0,15},{1,2},{2,1},{3,4},{4,3},{5,6},{6,5},{7,8},{8,7},{9,10},{10,... | collective-permute-start | bytes 221192 | tf_op jit(solution)/shard_map/ppermute | solution.py:108
  43.5 3.9 %collective-permute-start.10 = (bf16[2,2,2,16,128]{4,3,2,1,0:T(8,128)(2,1)S(1)}, bf16[2,2,2,16,128]{4,3,2,1,0:T(8,128)(2,1)S(1)}, u32[]{:S(2)}, u32[]{:S(2)}) collective-permute-start(bf16[2,2,2,16,128]{4,3,2,1,0:T(8,128)(2,1)S(1)} %corner_pack.3), channel_id=1, source_target_pairs={{0,16},{1,17},{2,18},{3,19},{4,20},{5,21},{6,22},{7,23},{8,24},{9,... | collective-permute-start | bytes 98312 | tf_op jit(solution)/shard_map/ppermute | solution.py:91
  51.3 0.6 copy-start.2
  51.9 14.0 %all-to-all-start = ((bf16[16,32,256]{2,1,0:T(8,128)(2,1)}), bf16[16,32,256]{2,1,0:T(8,128)(2,1)S(1)}, u32[]{:S(2)}, u32[]{:S(2)}) async-start(bf16[16,32,256]{2,1,0:T(8,128)(2,1)} %bitcast.3), calls=%async_computation | async-start | bytes 524288 | tf_op jit(solution)/shard_map/all_to_all | solution.py:694
  55.4 3.7 %collective-permute-start.11 = (bf16[2,16,128]{2,1,0:T(8,128)(2,1)S(1)}, bf16[2,16,128]{2,1,0:T(8,128)(2,1)S(1)}, u32[]{:S(2)}, u32[]{:S(2)}) collective-permute-start(bf16[2,16,128]{2,1,0:T(8,128)(2,1)S(1)} %get-tuple-element.57), channel_id=1, source_target_pairs={{0,16},{1,17},{2,18},{3,19},{4,20},{5,21},{6,22},{7,23},{8,24},{9,... | collective-permute-start | bytes 24584 | tf_op jit(solution)/shard_map/ppermute | solution.py:91
  59.2 7.4 %collective-permute-start.13 = (bf16[2,8,16,128]{3,2,1,0:T(8,128)(2,1)S(1)}, bf16[2,8,16,128]{3,2,1,0:T(8,128)(2,1)S(1)}, u32[]{:S(2)}, u32[]{:S(2)}) collective-permute-start(bf16[2,8,16,128]{3,2,1,0:T(8,128)(2,1)S(1)} %get-tuple-element.60), channel_id=1, source_target_pairs={{0,1},{1,2},{2,3},{3,4},{4,5},{5,6},{6,7},{7,8},{8,9},{9,10},{10,1... | collective-permute-start | bytes 196616 | tf_op jit(solution)/shard_map/ppermute | solution.py:91
  59.2 7.3 %collective-permute-start.12 = (bf16[2,16,16,128]{3,2,1,0:T(8,128)(2,1)S(1)}, bf16[2,16,16,128]{3,2,1,0:T(8,128)(2,1)S(1)}, u32[]{:S(2)}, u32[]{:S(2)}) collective-permute-start(bf16[2,16,16,128]{3,2,1,0:T(8,128)(2,1)S(1)} %get-tuple-element.59), channel_id=1, source_target_pairs={{0,16},{1,17},{2,18},{3,19},{4,20},{5,21},{6,22},{7,23},{8,24},{9,... | collective-permute-start | bytes 393224 | tf_op jit(solution)/shard_map/ppermute | solution.py:91
  66.0 4.0 %collective-permute-start.14 = (f32[32,256]{1,0:T(8,128)S(1)}, f32[32,256]{1,0:T(8,128)S(1)}, u32[]{:S(2)}, u32[]{:S(2)}) collective-permute-start(f32[32,256]{1,0:T(8,128)S(1)} %convert_reduce_fusion), channel_id=1, source_target_pairs={{0,16},{1,17},{2,18},{3,19},{4,20},{5,21},{6,22},{7,23},{8,24},{9,... | collective-permute-start | bytes 98312 | tf_op jit(solution)/shard_map/ppermute | solution.py:91
  66.5 0.9 %copy-start.3 = (f32[2,7,16,128]{3,2,1,0:T(8,128)S(1)}, f32[2,7,16,128]{3,2,1,0:T(8,128)}, u32[]{:S(2)}) copy-start(f32[2,7,16,128]{3,2,1,0:T(8,128)} %copy-done.2) | copy-start | bytes 344068

commit v18 on v17

--- a/solution.py
+++ b/solution.py
@@ -462,8 +462,8 @@
                  last_x, last_field, acc_in, face_in, near_in, far_in, corner_in, prod_ref, y_ref,
                  y_corner, new_ref, turned, *refs):
     mats = refs[:n_mat]
-    out_hbm, edge_x, edge_y, face, side, corner, margin = refs[n_mat : n_mat + 7]
-    part_ref, sem, acc_ref, rows_ref, small_ref, tail_ref = refs[n_mat + 7 :]
+    out_hbm, face, side, corner, margin = refs[n_mat : n_mat + 5]
+    part_ref, sem, acc_ref, rows_ref, small_ref, tail_ref = refs[n_mat + 5 :]
     nodes = Nodes(sz, vec, from_x, from_y, own_inv, own_pot, ghost_x, ghost_y, last_field)
     sums = Sums(sz, even_ref[0] == 0, acc_in, face_in, near_in, far_in, corner_in)
     u_corner, new_corner = [], []
@@ -500,10 +500,6 @@
             image = inv * acc + nodes.pot(i, j) * new
             value = 2.0 * (image - center_shift * new) / half_width - old
             part_ref[:, i, j] = value
-            if i == 0:
-                edge_x[:, j] = value
-            elif j == 0:
-                edge_y[:, i - 1] = value
             put_row(i * sz.ey + j, value.astype(bf16))
         if i < sz.ex:
             copies.append(pltpu.make_async_copy(part_ref.at[:, i], out_hbm.at[:, i], sem.at[i]))
@@ -527,22 +523,23 @@
         out_ref[:, i] = value.astype(out_ref.dtype)
 
 
-def last_kernel(sz, old_hbm, edge_x, edge_y, face, side, out_hbm, at_x, at_y, sems):
+def last_kernel(sz, old_hbm, face, side, out_hbm, at_x, at_y, sems):
     del old_hbm
+    pairs = [(at_x, out_hbm.at[:, 0]), (at_y, out_hbm.at[:, pl.ds(1, sz.ex - 1), 0])]
+    loads = [pltpu.make_async_copy(b, a, sems.at[k]) for k, (a, b) in enumerate(pairs)]
+    stores = [pltpu.make_async_copy(a, b, sems.at[k]) for k, (a, b) in enumerate(pairs)]
+    for copy in loads:
+        copy.start()
+    for copy in loads:
+        copy.wait()
+    at_x[:, 0] += side[:, 0].astype(f32)
     for j in range(sz.ey):
-        value = edge_x[:, j] + face[:, j].astype(f32)
-        if j == 0:
-            value = value + side[:, 0].astype(f32)
-        at_x[:, j] = value
+        at_x[:, j] += face[:, j].astype(f32)
     for i in range(1, sz.ex):
-        at_y[:, i - 1] = edge_y[:, i - 1] + side[:, i].astype(f32)
-    copies = [
-        pltpu.make_async_copy(at_x, out_hbm.at[:, 0], sems.at[0]),
-        pltpu.make_async_copy(at_y, out_hbm.at[:, pl.ds(1, sz.ex - 1), 0], sems.at[1]),
-    ]
-    for copy in copies:
+        at_y[:, i - 1] += side[:, i].astype(f32)
+    for copy in stores:
         copy.start()
-    for copy in copies:
+    for copy in stores:
         copy.wait()
 
 
@@ -678,11 +675,11 @@
         [products, state_grid], main_scratch,
         [parity, *state, acc, *got, y1, *mats], scalar_first=True,
     )
-    filtered, edge_x, edge_y, face, side, corner, local = call(
+    filtered, face, side, corner, local = call(
         functools.partial(third_corner, sz, n_mat, norm_scale), "third_corner",
         small_flops + 2 * res_count * sz.edges * ez * full,
         [
-            like(own, f32), like((blocks, sz.ey) + tile, f32), like((blocks, sz.ex - 1) + tile, f32),
+            like(own, f32),
             like((blocks, sz.ey) + tile, bf16), like((blocks, sz.ex) + tile, f32), like(sz.edge, bf16),
             like((res_count, full), bf16),
         ],
@@ -710,7 +707,7 @@
             pltpu.VMEM((blocks, sz.ey) + tile, f32), pltpu.VMEM((blocks, sz.ex - 1) + tile, f32),
             pltpu.SemaphoreType.DMA((2,)),
         ],
-        [filtered, edge_x, edge_y, face, side], hbm=1, out_hbm=1, aliases={0: 0},
+        [filtered, face, side], hbm=1, out_hbm=1, aliases={0: 0},
     )
     return (filtered, margin)
 

time: 70.9 us -> 70.2 us (level)
  local copies, waits for them, and re-layouts: 3.47 us -> 1.94 us
  Pallas kernels: 22.3 us -> 23.2 us
    unnamed x16 -> x12, local copies, waits for them, and re-layouts: 2.8 us -> 1.27 us
    pallas_call x14, Pallas kernels: 22.3 us -> 23.2 us  [call(): pl.pallas_call(kernel, in_specs=specs, out_specs=out_specs, out_shape=out...]
  transfers between devices with their start and end apart: 16 -> 16, of which waited for: 8 -> 8; matrix products, arithmetic and copies ran while one was open for 1% -> 1% of each run, Pallas kernels for 21% -> 23%
where the time goes in v18:
time: 70.2 us; the launch traced here: 69.9 us
  Pallas kernels  23.2 us (33%)
  waiting for transfers between devices  23.2 us (33%)
  starting transfers between devices  20 us (28%)
  local copies, waits for them, and re-layouts  1.94 us (3%)
  between operations  0.83 us (1%)
    pallas_call x14, Pallas kernels, call(): pl.pallas_call(kernel, in_specs=specs, out_specs=out_specs, out_shape=out...  23.2 us
    ppermute x11, starting transfers between devices, send(): return lax.ppermute(value, ('dx', 'dy'), pairs)  13.5 us
    ppermute x2, waiting for transfers between devices, swap_y(): far = lax.ppermute(far, 'dy', far_pairs)  9.03 us
    ppermute x11, waiting for transfers between devices, send(): return lax.ppermute(value, ('dx', 'dy'), pairs)  8.06 us
    all_to_all x1, waiting for transfers between devices, body(): pieces = lax.all_to_all(local.reshape(ny, -1, full), 'dy', 0, 0)  6.12 us
    all_to_all x1, starting transfers between devices, body(): pieces = lax.all_to_all(local.reshape(ny, -1, full), 'dy', 0, 0)  3.54 us
    ppermute x2, starting transfers between devices, swap_y(): far = lax.ppermute(far, 'dy', far_pairs)  3 us
  transfers between devices with their start and end apart: 16, of which 8 were waited for; matrix products, arithmetic and copies ran while one was open for 1% of the time, Pallas kernels for 23%

profile of v18, /device:TPU:0, one launch (start us, length us, event | category | flops | bytes accessed | tf_op | source)
XLA Modules:
  0.0 69.9 jit_solution(5073594355044135691)
XLA Ops:
  0.6 0.0 copy-start.2
  0.6 2.0 %pack.1 = (bf16[16,16,896]{2,1,0:T(8,128)(2,1)S(1)}, bf16[8,16,896]{2,1,0:T(8,128)(2,1)}, s32[4,729]{1,0:T(4,128)S(1)}) custom-call(bf16[2,8,16,16,128]{4,3,2,1,0:T(8,128)(2,1)} %vec.11, bf16[8,16,16,512]{3,2,1,0:T(8,128)(2,1)} %res_hbm.1, f32[8,16,16]{2,1,0:T(8,128)} %inv_hbm.1, f32[8,16,16]{2,1,0:T(8,128)} %pot_hbm.1, s32[4,729]{1,0:T(4,128)} %bitcast.5), custom_call_target="tpu_custom_call" | custom-call | bytes 3873568 | tf_op jit(solution)/shard_map/pack/pallas_call | solution.py:566
  2.6 5.5 %collective-permute-start.1 = (bf16[8,16,896]{2,1,0:T(8,128)(2,1)}, bf16[8,16,896]{2,1,0:T(8,128)(2,1)S(1)}, u32[]{:S(2)}, u32[]{:S(2)}) collective-permute-start(bf16[8,16,896]{2,1,0:T(8,128)(2,1)} %get-tuple-element.31), channel_id=1, source_target_pairs={{0,15},{1,0},{2,1},{3,2},{4,3},{5,4},{6,5},{7,6},{8,7},{9,8},{10,9... | collective-permute-start | bytes 688136 | tf_op jit(solution)/shard_map/ppermute | solution.py:91
  8.1 1.5 %collective-permute-start = (bf16[16,16,896]{2,1,0:T(8,128)(2,1)S(1)}, bf16[16,16,896]{2,1,0:T(8,128)(2,1)S(1)}, u32[]{:S(2)}, u32[]{:S(2)}) collective-permute-start(bf16[16,16,896]{2,1,0:T(8,128)(2,1)S(1)} %get-tuple-element.30), channel_id=1, source_target_pairs={{0,16},{1,17},{2,18},{3,19},{4,20},{5,21},{6,22},{7,23},{8,24},{9,... | collective-permute-start | bytes 1376264 | tf_op jit(solution)/shard_map/ppermute | solution.py:91
  9.6 3.8 %order_cells.3.refs_1_ = bf16[2,736,768]{2,1,0:T(8,128)(2,1)S(1)} custom-call(bf16[729,729]{1,0:T(8,128)(2,1)S(1)} %copy-done.2, s32[4,729]{1,0:T(4,128)S(1)} %get-tuple-element.32.conn_ref), custom_call_target="tpu_custom_call" | custom-call | flops 3623878656 | bytes 3335538 | tf_op jit(solution)/shard_map/order_cells/pallas_call | solution.py:566
  13.4 0.0 copy-start.3
  13.4 1.2 %copy-done.3 = bf16[729,729]{1,0:T(8,128)(2,1)S(1)} copy-done((bf16[729,729]{1,0:T(8,128)(2,1)S(1)}, bf16[729,729]{1,0:T(8,128)(2,1)}, u32[]{:S(2)}) %copy-start.3) | copy-done | bytes 1062906
  14.7 3.8 %order_cells.2.refs_0_ = bf16[2,736,768]{2,1,0:T(8,128)(2,1)S(1)} custom-call(bf16[729,729]{1,0:T(8,128)(2,1)S(1)} %copy-done.3, s32[4,729]{1,0:T(4,128)S(1)} %get-tuple-element.32.conn_ref), custom_call_target="tpu_custom_call" | custom-call | flops 3623878656 | bytes 3335538 | tf_op jit(solution)/shard_map/order_cells/pallas_call | solution.py:566
  18.5 0.0 copy-start
  18.5 0.0 collective-permute-done.1.from_y
  18.5 0.6 collective-permute-start.2
  19.1 0.3 broadcast_in_dim.4.own_inv
  19.4 0.3 broadcast_in_dim.5.own_pot
  19.8 1.5 %first_main.1 = (f32[4,736,256]{2,1,0:T(8,128)S(1)}, f32[2,16,16,128]{3,2,1,0:T(8,128)S(1)}, f32[2,8,16,128]{3,2,1,0:T(8,128)S(1)}) custom-call(bf16[2,8,16,16,128]{4,3,2,1,0:T(8,128)(2,1)S(1)} %copy-done, bf16[16,16,896]{2,1,0:T(8,128)(2,1)S(1)} %collective-permute-done.from_x, bf16[8,16,896]{2,1,0:T(8,128)(2,1)S(1)} %collective-permute-done.1.from_y, ...), custom_call_target="tpu_custom_call" | custom-call | flops 1157627904 | bytes 11763712 | tf_op jit(solution)/shard_map/first_main/pallas_call | solution.py:566
  21.3 1.5 %collective-permute-done.2.corner = bf16[1,16,896]{2,1,0:T(8,128)(2,1)S(1)} collective-permute-done((bf16[1,16,896]{2,1,0:T(8,128)(2,1)S(1)}, bf16[1,16,896]{2,1,0:T(8,128)(2,1)S(1)}, u32[]{:S(2)}, u32[]{:S(2)}) %collective-permute-start.2) | collective-permute-done | bytes 28704 | tf_op jit(solution)/shard_map/ppermute | solution.py:91
  22.8 0.9 %first_corner.1 = (f32[2,9,17,16,128]{4,3,2,1,0:T(8,128)S(1)}, bf16[2,2,17,16,128]{4,3,2,1,0:T(8,128)(2,1)S(1)}, bf16[2,9,16,128]{3,2,1,0:T(8,128)(2,1)S(1)}, bf...) custom-call(s32[1]{0:T(128)} %bitcast.even_ref, ...), custom_call_target="tpu_custom_call" | custom-call | flops 192937984 | bytes 14757892 | tf_op jit(solution)/shard_map/first_corner/pallas_call | solution.py:566
  23.6 0.6 collective-permute-start.3
  24.2 0.0 collective-permute-start.4
  24.2 2.5 %collective-permute-start.5 = (bf16[2,9,16,128]{3,2,1,0:T(8,128)(2,1)S(1)}, bf16[2,9,16,128]{3,2,1,0:T(8,128)(2,1)S(1)}, u32[]{:S(2)}, u32[]{:S(2)}) collective-permute-start(bf16[2,9,16,128]{3,2,1,0:T(8,128)(2,1)S(1)} %get-tuple-element.41), channel_id=1, source_target_pairs={{0,15},{1,2},{2,1},{3,4},{4,3},{5,6},{6,5},{7,8},{8,7},{9,10},{10,... | collective-permute-start | bytes 221192 | tf_op jit(solution)/shard_map/ppermute | solution.py:108
  26.7 0.0 collective-permute-done.4.near.near_in
  26.7 4.0 %collective-permute-done.5.far.far_in = bf16[2,9,16,128]{3,2,1,0:T(8,128)(2,1)S(1)} collective-permute-done((bf16[2,9,16,128]{3,2,1,0:T(8,128)(2,1)S(1)}, bf16[2,9,16,128]{3,2,1,0:T(8,128)(2,1)S(1)}, u32[]{:S(2)}, u32[]{:S(2)}) %collective-permute-start.5) | collective-permute-done | bytes 73760 | tf_op jit(solution)/shard_map/ppermute | solution.py:108
  30.7 1.5 %collective-permute-start.6 = (bf16[2,2,2,16,128]{4,3,2,1,0:T(8,128)(2,1)S(1)}, bf16[2,2,2,16,128]{4,3,2,1,0:T(8,128)(2,1)S(1)}, u32[]{:S(2)}, u32[]{:S(2)}) collective-permute-start(bf16[2,2,2,16,128]{4,3,2,1,0:T(8,128)(2,1)S(1)} %corner_pack.2), channel_id=1, source_target_pairs={{0,16},{1,17},{2,18},{3,19},{4,20},{5,21},{6,22},{7,23},{8,24},{9,... | collective-permute-start | bytes 98312 | tf_op jit(solution)/shard_map/ppermute | solution.py:91
  32.2 0.0 collective-permute-done.3.face_in
  32.2 2.0 %second_main.1 = (f32[4,736,256]{2,1,0:T(8,128)S(1)}, f32[2,9,17,16,128]{4,3,2,1,0:T(8,128)S(1)}) custom-call(s32[1]{0:T(128)} %bitcast.even_ref, bf16[2,8,16,16,128]{4,3,2,1,0:T(8,128)(2,1)S(1)} %copy-done, bf16[16,16,896]{2,1,0:T(8,128)(2,1)S(1)} %collective-permute-done.from_x, bf16[8,16,896]{2,1,0:T(8,128)(2,1)S(1)} %collective-permute-done.1.from_y, ...), custom_call_target="tpu_custom_call" | custom-call | flops 1157627904 | bytes 17203204 | tf_op jit(solution)/shard_map/second_main/pallas_call | solution.py:566
  34.2 0.4 collective-permute-done.6.corner_in
  34.6 0.9 %second_corner.1 = (f32[2,9,17,16,128]{4,3,2,1,0:T(8,128)S(1)}, bf16[2,2,17,16,128]{4,3,2,1,0:T(8,128)(2,1)S(1)}, bf16[2,9,16,128]{3,2,1,0:T(8,128)(2,1)S(1)}, b...) custom-call(s32[1]{0:T(128)} %bitcast.even_ref, bf16[2,8,16,16,128]{4,3,2,1,0:T(8,128)(2,1)S(1)} %copy-done, ...), custom_call_target="tpu_custom_call" | custom-call | flops 192937984 | bytes 17760260 | tf_op jit(solution)/shard_map/second_corner/pallas_call | solution.py:566
  35.5 1.6 %collective-permute-start.7 = (bf16[2,2,17,16,128]{4,3,2,1,0:T(8,128)(2,1)S(1)}, bf16[2,2,17,16,128]{4,3,2,1,0:T(8,128)(2,1)S(1)}, u32[]{:S(2)}, u32[]{:S(2)}) collective-permute-start(bf16[2,2,17,16,128]{4,3,2,1,0:T(8,128)(2,1)S(1)} %get-tuple-element.44), channel_id=1, source_target_pairs={{0,16},{1,17},{2,18},{3,19},{4,20},{5,21},{6,22},{7,23},{8,24},{9,... | collective-permute-start | bytes 835592 | tf_op jit(solution)/shard_map/ppermute | solution.py:91
  37.1 0.0 collective-permute-start.8
  37.1 0.5 collective-permute-start.9
  37.6 0.9 %turn_residents.1.turned = bf16[512,2560]{1,0:T(8,128)(2,1)S(1)} custom-call(bf16[2048,512]{1,0:T(8,128)(2,1)S(1)} %bitcast.4, bf16[16,16,896]{2,1,0:T(8,128)(2,1)S(1)} %collective-permute-done.from_x, bf16[8,16,896]{2,1,0:T(8,128)(2,1)S(1)} %collective-permute-done.1.from_y, bf16[1,16,896]{2,1,0:T(8,128)(2,1)S(1)} %collective-permute-done.2.corner), custom_call_target="tpu_custom_call" | custom-call | flops 578813952 | bytes 5435392 | tf_op jit(solution)/shard_map/turn_residents/pallas_call | solution.py:566
  38.5 0.0 collective-permute-done.8.near.near_in
  38.5 5.0 %collective-permute-done.9.far.far_in = bf16[2,9,16,128]{3,2,1,0:T(8,128)(2,1)S(1)} collective-permute-done((bf16[2,9,16,128]{3,2,1,0:T(8,128)(2,1)S(1)}, bf16[2,9,16,128]{3,2,1,0:T(8,128)(2,1)S(1)}, u32[]{:S(2)}, u32[]{:S(2)}) %collective-permute-start.9) | collective-permute-done | bytes 73760 | tf_op jit(solution)/shard_map/ppermute | solution.py:108
  43.6 0.5 collective-permute-start.10
  44.1 0.0 collective-permute-done.7.face_in
  44.1 2.1 %third_main.1 = (f32[4,736,256]{2,1,0:T(8,128)S(1)}, f32[2,9,17,16,128]{4,3,2,1,0:T(8,128)S(1)}) custom-call(s32[1]{0:T(128)} %bitcast.even_ref, bf16[2,8,16,16,128]{4,3,2,1,0:T(8,128)(2,1)S(1)} %copy-done, bf16[16,16,896]{2,1,0:T(8,128)(2,1)S(1)} %collective-permute-done.from_x, bf16[8,16,896]{2,1,0:T(8,128)(2,1)S(1)} %collective-permute-done.1.from_y, ...), custom_call_target="tpu_custom_call" | custom-call | flops 1157627904 | bytes 19709956 | tf_op jit(solution)/shard_map/third_main/pallas_call | solution.py:566
  46.1 1.3 %collective-permute-done.10.corner_in = bf16[2,2,2,16,128]{4,3,2,1,0:T(8,128)(2,1)S(1)} collective-permute-done((bf16[2,2,2,16,128]{4,3,2,1,0:T(8,128)(2,1)S(1)}, bf16[2,2,2,16,128]{4,3,2,1,0:T(8,128)(2,1)S(1)}, u32[]{:S(2)}, u32[]{:S(2)}) %collective-permute-start.10) | collective-permute-done | bytes 32800 | tf_op jit(solution)/shard_map/ppermute | solution.py:91
  47.5 3.7 %third_corner.1 = (f32[2,8,16,16,128]{4,3,2,1,0:T(8,128)}, bf16[2,16,16,128]{3,2,1,0:T(8,128)(2,1)S(1)}, f32[2,8,16,128]{3,2,1,0:T(8,128)S(1)}, bf16[2,16,128]{2,1,0:T(8,128)(2,1)S(1)}, bf16[512,256]{1,0:T(8,128)(2,1)}) custom-call(s32[1]{0:T(128)} %bitcast.even_ref, bf16[2,8,16,16,128]{4,3,2,1,0:T(8,128)(2,1)S(1)} %copy-done, ...), custom_call_target="tpu_custom_call" | custom-call | flops 864026624 | bytes 25092100 | tf_op jit(solution)/shard_map/third_corner/pallas_call | solution.py:566
  51.2 3.5 %all-to-all-start = ((bf16[16,32,256]{2,1,0:T(8,128)(2,1)}), bf16[16,32,256]{2,1,0:T(8,128)(2,1)S(1)}, u32[]{:S(2)}, u32[]{:S(2)}) async-start(bf16[16,32,256]{2,1,0:T(8,128)(2,1)} %bitcast.3), calls=%async_computation | async-start | bytes 524288 | tf_op jit(solution)/shard_map/all_to_all | solution.py:691
  54.8 0.6 collective-permute-start.11
  55.3 3.2 %collective-permute-done.11.corner_ref = bf16[2,16,128]{2,1,0:T(8,128)(2,1)S(1)} collective-permute-done((bf16[2,16,128]{2,1,0:T(8,128)(2,1)S(1)}, bf16[2,16,128]{2,1,0:T(8,128)(2,1)S(1)}, u32[]{:S(2)}, u32[]{:S(2)}) %collective-permute-start.11) | collective-permute-done | bytes 8224 | tf_op jit(solution)/shard_map/ppermute | solution.py:91
  58.5 0.1 collective-permute-start.13
  58.6 0.6 collective-permute-start.12
  59.1 6.1 %all-to-all-done = bf16[16,32,256]{2,1,0:T(8,128)(2,1)S(1)} async-done(((bf16[16,32,256]{2,1,0:T(8,128)(2,1)}), bf16[16,32,256]{2,1,0:T(8,128)(2,1)S(1)}, u32[]{:S(2)}, u32[]{:S(2)}) %all-to-all-start) | async-done | bytes 262176 | tf_op jit(solution)/shard_map/all_to_all | solution.py:691
  65.3 0.6 collective-permute-start.14
  65.9 0.0 collective-permute-done.13.side
  65.9 1.8 %last.1 = f32[2,8,16,16,128]{4,3,2,1,0:T(8,128)} custom-call(f32[2,8,16,16,128]{4,3,2,1,0:T(8,128)} %get-tuple-element.51.old_hbm, bf16[2,16,16,128]{3,2,1,0:T(8,128)(2,1)S(1)} %collective-permute-done.12.face, bf16[2,8,16,128]{3,2,1,0:T(8,128)(2,1)S(1)} %collective-permute-done.13.side), custom_call_target="tpu_custom_call", output_to_operand_aliasing={{}: (0, {})} | custom-call | bytes 4390912 | tf_op jit(solution)/shard_map/last/pallas_call | solution.py:566
  67.6 1.6 %collective-permute-done.14 = f32[32,256]{1,0:T(8,128)S(1)} collective-permute-done((f32[32,256]{1,0:T(8,128)S(1)}, f32[32,256]{1,0:T(8,128)S(1)}, u32[]{:S(2)}, u32[]{:S(2)}) %collective-permute-start.14) | collective-permute-done | bytes 32800 | tf_op jit(solution)/shard_map/ppermute | solution.py:91
  69.3 0.6 add.8
  (15 shorter events, 0.1 us)
Async XLA Ops:
  0.6 9.0 %copy-start.2 = (bf16[729,729]{1,0:T(8,128)(2,1)S(1)}, bf16[729,729]{1,0:T(8,128)(2,1)}, u32[]{:S(2)}) copy-start(bf16[729,729]{1,0:T(8,128)(2,1)} %matrix_ref.3) | copy-start | bytes 3188650
  2.6 15.9 %collective-permute-start.1 = (bf16[8,16,896]{2,1,0:T(8,128)(2,1)}, bf16[8,16,896]{2,1,0:T(8,128)(2,1)S(1)}, u32[]{:S(2)}, u32[]{:S(2)}) collective-permute-start(bf16[8,16,896]{2,1,0:T(8,128)(2,1)} %get-tuple-element.31), channel_id=1, source_target_pairs={{0,15},{1,0},{2,1},{3,2},{4,3},{5,4},{6,5},{7,6},{8,7},{9,8},{10,9... | collective-permute-start | bytes 688136 | tf_op jit(solution)/shard_map/ppermute | solution.py:91
  8.1 11.0 %collective-permute-start = (bf16[16,16,896]{2,1,0:T(8,128)(2,1)S(1)}, bf16[16,16,896]{2,1,0:T(8,128)(2,1)S(1)}, u32[]{:S(2)}, u32[]{:S(2)}) collective-permute-start(bf16[16,16,896]{2,1,0:T(8,128)(2,1)S(1)} %get-tuple-element.30), channel_id=1, source_target_pairs={{0,16},{1,17},{2,18},{3,19},{4,20},{5,21},{6,22},{7,23},{8,24},{9,... | collective-permute-start | bytes 1376264 | tf_op jit(solution)/shard_map/ppermute | solution.py:91
  13.4 1.3 %copy-start.3 = (bf16[729,729]{1,0:T(8,128)(2,1)S(1)}, bf16[729,729]{1,0:T(8,128)(2,1)}, u32[]{:S(2)}) copy-start(bf16[729,729]{1,0:T(8,128)(2,1)} %matrix_ref.3) | copy-start | bytes 3188650
  14.7 4.4 %copy-start.4 = (f32[8,16,16]{2,1,0:T(8,128)S(1)}, f32[8,16,16]{2,1,0:T(8,128)}, u32[]{:S(2)}) copy-start(f32[8,16,16]{2,1,0:T(8,128)} %inv_hbm.1) | copy-start | bytes 24580
  14.7 4.7 %copy-start.5 = (f32[8,16,16]{2,1,0:T(8,128)S(1)}, f32[8,16,16]{2,1,0:T(8,128)}, u32[]{:S(2)}) copy-start(f32[8,16,16]{2,1,0:T(8,128)} %pot_hbm.1) | copy-start | bytes 24580
  18.5 1.3 %copy-start = (bf16[2,8,16,16,128]{4,3,2,1,0:T(8,128)(2,1)S(1)}, bf16[2,8,16,16,128]{4,3,2,1,0:T(8,128)(2,1)}, u32[]{:S(2)}) copy-start(bf16[2,8,16,16,128]{4,3,2,1,0:T(8,128)(2,1)} %vec.11) | copy-start | bytes 3145732
  18.5 4.2 %collective-permute-start.2 = (bf16[1,16,896]{2,1,0:T(8,128)(2,1)S(1)}, bf16[1,16,896]{2,1,0:T(8,128)(2,1)S(1)}, u32[]{:S(2)}, u32[]{:S(2)}) collective-permute-start(bf16[1,16,896]{2,1,0:T(8,128)(2,1)S(1)} %slice.4), channel_id=1, source_target_pairs={{0,16},{1,17},{2,18},{3,19},{4,20},{5,21},{6,22},{7,23},{8,24},{9,... | collective-permute-start | bytes 86024 | tf_op jit(solution)/shard_map/ppermute | solution.py:91
  23.6 8.6 %collective-permute-start.3 = (bf16[2,2,17,16,128]{4,3,2,1,0:T(8,128)(2,1)S(1)}, bf16[2,2,17,16,128]{4,3,2,1,0:T(8,128)(2,1)S(1)}, u32[]{:S(2)}, u32[]{:S(2)}) collective-permute-start(bf16[2,2,17,16,128]{4,3,2,1,0:T(8,128)(2,1)S(1)} %get-tuple-element.39), channel_id=1, source_target_pairs={{0,16},{1,17},{2,18},{3,19},{4,20},{5,21},{6,22},{7,23},{8,24},{9,... | collective-permute-start | bytes 835592 | tf_op jit(solution)/shard_map/ppermute | solution.py:91
  24.2 2.5 %collective-permute-start.4 = (bf16[2,9,16,128]{3,2,1,0:T(8,128)(2,1)S(1)}, bf16[2,9,16,128]{3,2,1,0:T(8,128)(2,1)S(1)}, u32[]{:S(2)}, u32[]{:S(2)}) collective-permute-start(bf16[2,9,16,128]{3,2,1,0:T(8,128)(2,1)S(1)} %get-tuple-element.40), channel_id=1, source_target_pairs={{0,1},{1,0},{2,3},{3,2},{4,5},{5,4},{6,7},{7,6},{8,9},{9,8},{10,11... | collective-permute-start | bytes 221192 | tf_op jit(solution)/shard_map/ppermute | solution.py:102
  24.2 6.5 %collective-permute-start.5 = (bf16[2,9,16,128]{3,2,1,0:T(8,128)(2,1)S(1)}, bf16[2,9,16,128]{3,2,1,0:T(8,128)(2,1)S(1)}, u32[]{:S(2)}, u32[]{:S(2)}) collective-permute-start(bf16[2,9,16,128]{3,2,1,0:T(8,128)(2,1)S(1)} %get-tuple-element.41), channel_id=1, source_target_pairs={{0,15},{1,2},{2,1},{3,4},{4,3},{5,6},{6,5},{7,8},{8,7},{9,10},{10,... | collective-permute-start | bytes 221192 | tf_op jit(solution)/shard_map/ppermute | solution.py:108
  30.7 3.9 %collective-permute-start.6 = (bf16[2,2,2,16,128]{4,3,2,1,0:T(8,128)(2,1)S(1)}, bf16[2,2,2,16,128]{4,3,2,1,0:T(8,128)(2,1)S(1)}, u32[]{:S(2)}, u32[]{:S(2)}) collective-permute-start(bf16[2,2,2,16,128]{4,3,2,1,0:T(8,128)(2,1)S(1)} %corner_pack.2), channel_id=1, source_target_pairs={{0,16},{1,17},{2,18},{3,19},{4,20},{5,21},{6,22},{7,23},{8,24},{9,... | collective-permute-start | bytes 98312 | tf_op jit(solution)/shard_map/ppermute | solution.py:91
  34.6 3.0 %copy-start.1 = (bf16[8,16,16,512]{3,2,1,0:T(8,128)(2,1)S(1)}, bf16[8,16,16,512]{3,2,1,0:T(8,128)(2,1)}, u32[]{:S(2)}) copy-start(bf16[8,16,16,512]{3,2,1,0:T(8,128)(2,1)} %res_hbm.1) | copy-start | bytes 6291460
  35.5 8.6 %collective-permute-start.7 = (bf16[2,2,17,16,128]{4,3,2,1,0:T(8,128)(2,1)S(1)}, bf16[2,2,17,16,128]{4,3,2,1,0:T(8,128)(2,1)S(1)}, u32[]{:S(2)}, u32[]{:S(2)}) collective-permute-start(bf16[2,2,17,16,128]{4,3,2,1,0:T(8,128)(2,1)S(1)} %get-tuple-element.44), channel_id=1, source_target_pairs={{0,16},{1,17},{2,18},{3,19},{4,20},{5,21},{6,22},{7,23},{8,24},{9,... | collective-permute-start | bytes 835592 | tf_op jit(solution)/shard_map/ppermute | solution.py:91
  37.1 1.4 %collective-permute-start.8 = (bf16[2,9,16,128]{3,2,1,0:T(8,128)(2,1)S(1)}, bf16[2,9,16,128]{3,2,1,0:T(8,128)(2,1)S(1)}, u32[]{:S(2)}, u32[]{:S(2)}) collective-permute-start(bf16[2,9,16,128]{3,2,1,0:T(8,128)(2,1)S(1)} %get-tuple-element.45), channel_id=1, source_target_pairs={{0,1},{1,0},{2,3},{3,2},{4,5},{5,4},{6,7},{7,6},{8,9},{9,8},{10,11... | collective-permute-start | bytes 221192 | tf_op jit(solution)/shard_map/ppermute | solution.py:102
  37.1 6.5 %collective-permute-start.9 = (bf16[2,9,16,128]{3,2,1,0:T(8,128)(2,1)S(1)}, bf16[2,9,16,128]{3,2,1,0:T(8,128)(2,1)S(1)}, u32[]{:S(2)}, u32[]{:S(2)}) collective-permute-start(bf16[2,9,16,128]{3,2,1,0:T(8,128)(2,1)S(1)} %get-tuple-element.46), channel_id=1, source_target_pairs={{0,15},{1,2},{2,1},{3,4},{4,3},{5,6},{6,5},{7,8},{8,7},{9,10},{10,... | collective-permute-start | bytes 221192 | tf_op jit(solution)/shard_map/ppermute | solution.py:108
  43.6 3.9 %collective-permute-start.10 = (bf16[2,2,2,16,128]{4,3,2,1,0:T(8,128)(2,1)S(1)}, bf16[2,2,2,16,128]{4,3,2,1,0:T(8,128)(2,1)S(1)}, u32[]{:S(2)}, u32[]{:S(2)}) collective-permute-start(bf16[2,2,2,16,128]{4,3,2,1,0:T(8,128)(2,1)S(1)} %corner_pack.3), channel_id=1, source_target_pairs={{0,16},{1,17},{2,18},{3,19},{4,20},{5,21},{6,22},{7,23},{8,24},{9,... | collective-permute-start | bytes 98312 | tf_op jit(solution)/shard_map/ppermute | solution.py:91
  51.2 14.0 %all-to-all-start = ((bf16[16,32,256]{2,1,0:T(8,128)(2,1)}), bf16[16,32,256]{2,1,0:T(8,128)(2,1)S(1)}, u32[]{:S(2)}, u32[]{:S(2)}) async-start(bf16[16,32,256]{2,1,0:T(8,128)(2,1)} %bitcast.3), calls=%async_computation | async-start | bytes 524288 | tf_op jit(solution)/shard_map/all_to_all | solution.py:691
  54.8 3.7 %collective-permute-start.11 = (bf16[2,16,128]{2,1,0:T(8,128)(2,1)S(1)}, bf16[2,16,128]{2,1,0:T(8,128)(2,1)S(1)}, u32[]{:S(2)}, u32[]{:S(2)}) collective-permute-start(bf16[2,16,128]{2,1,0:T(8,128)(2,1)S(1)} %get-tuple-element.53), channel_id=1, source_target_pairs={{0,16},{1,17},{2,18},{3,19},{4,20},{5,21},{6,22},{7,23},{8,24},{9,... | collective-permute-start | bytes 24584 | tf_op jit(solution)/shard_map/ppermute | solution.py:91
  58.5 7.4 %collective-permute-start.13 = (bf16[2,8,16,128]{3,2,1,0:T(8,128)(2,1)S(1)}, bf16[2,8,16,128]{3,2,1,0:T(8,128)(2,1)S(1)}, u32[]{:S(2)}, u32[]{:S(2)}) collective-permute-start(bf16[2,8,16,128]{3,2,1,0:T(8,128)(2,1)S(1)} %get-tuple-element.56), channel_id=1, source_target_pairs={{0,1},{1,2},{2,3},{3,4},{4,5},{5,6},{6,7},{7,8},{8,9},{9,10},{10,1... | collective-permute-start | bytes 196616 | tf_op jit(solution)/shard_map/ppermute | solution.py:91
  58.6 7.3 %collective-permute-start.12 = (bf16[2,16,16,128]{3,2,1,0:T(8,128)(2,1)S(1)}, bf16[2,16,16,128]{3,2,1,0:T(8,128)(2,1)S(1)}, u32[]{:S(2)}, u32[]{:S(2)}) collective-permute-start(bf16[2,16,16,128]{3,2,1,0:T(8,128)(2,1)S(1)} %get-tuple-element.55), channel_id=1, source_target_pairs={{0,16},{1,17},{2,18},{3,19},{4,20},{5,21},{6,22},{7,23},{8,24},{9,... | collective-permute-start | bytes 393224 | tf_op jit(solution)/shard_map/ppermute | solution.py:91
  65.3 4.0 %collective-permute-start.14 = (f32[32,256]{1,0:T(8,128)S(1)}, f32[32,256]{1,0:T(8,128)S(1)}, u32[]{:S(2)}, u32[]{:S(2)}) collective-permute-start(f32[32,256]{1,0:T(8,128)S(1)} %convert_reduce_fusion), channel_id=1, source_target_pairs={{0,16},{1,17},{2,18},{3,19},{4,20},{5,21},{6,22},{7,23},{8,24},{9,... | collective-permute-start | bytes 98312 | tf_op jit(solution)/shard_map/ppermute | solution.py:91

commit v19 on v18

--- a/solution.py
+++ b/solution.py
@@ -602,7 +602,7 @@
     mats = []
     for at in range(0, sz.cells, step):
         mats += call(
-            functools.partial(order_kernel, sz, at), "order_cells", 4 * step * sz.depth**3,
+            functools.partial(order_kernel, sz, at), "order_cells", 0,
             [like((step, sz.rows, sz.depth), bf16)],
             [], [cell_matrix, conn],
         )

time: 70.2 us -> 78 us (1.11)
  waiting for transfers between devices: 23.2 us -> 16 us
  local copies, waits for them, and re-layouts: 1.94 us -> 8.93 us
  Pallas kernels: 23.2 us -> 30 us
  starting transfers between devices: 20 us -> 20.8 us
    pallas_call x14, Pallas kernels: 23.2 us -> 30 us  [call(): pl.pallas_call(kernel, in_specs=specs, out_specs=out_specs, out_shape=out...]
    unnamed x12 -> x20, local copies, waits for them, and re-layouts: 1.27 us -> 6.49 us
    ppermute x11, waiting for transfers between devices: 8.06 us -> 4.11 us  [send(): return lax.ppermute(value, ('dx', 'dy'), pairs)]
    all_to_all x1, waiting for transfers between devices: 6.12 us -> 3.28 us  [body(): pieces = lax.all_to_all(local.reshape(ny, -1, full), 'dy', 0, 0)]
    ppermute x11, starting transfers between devices: 13.5 us -> 14.9 us  [send(): return lax.ppermute(value, ('dx', 'dy'), pairs)]
    broadcast_in_dim x1, local copies, waits for them, and re-layouts: 0.33 us -> 1.27 us  [body(): own_inv = jnp.broadcast_to(inv_mass[..., None], inv_mass.shape + (width,))]
    broadcast_in_dim x1, local copies, waits for them, and re-layouts: 0.33 us -> 1.17 us  [body(): own_pot = jnp.broadcast_to(potential[..., None], inv_mass.shape + (width,))]
  transfers between devices with their start and end apart: 16 -> 16, of which waited for: 8 -> 8; matrix products, arithmetic and copies ran while one was open for 1% -> 3% of each run, Pallas kernels for 23% -> 26%
where the time goes in v19:
time: 78 us; the launch traced here: 77.3 us
  Pallas kernels  30 us (38%)
  starting transfers between devices  20.8 us (27%)
  waiting for transfers between devices  16 us (21%)
  local copies, waits for them, and re-layouts  8.93 us (11%)
  between operations  0.82 us (1%)
    pallas_call x14, Pallas kernels, call(): pl.pallas_call(kernel, in_specs=specs, out_specs=out_specs, out_shape=out...  30 us
    ppermute x11, starting transfers between devices, send(): return lax.ppermute(value, ('dx', 'dy'), pairs)  14.9 us
    ppermute x2, waiting for transfers between devices, swap_y(): far = lax.ppermute(far, 'dy', far_pairs)  8.51 us
    unnamed x20, local copies, waits for them, and re-layouts  6.49 us
    ppermute x11, waiting for transfers between devices, send(): return lax.ppermute(value, ('dx', 'dy'), pairs)  4.11 us
    all_to_all x1, starting transfers between devices, body(): pieces = lax.all_to_all(local.reshape(ny, -1, full), 'dy', 0, 0)  3.53 us
    all_to_all x1, waiting for transfers between devices, body(): pieces = lax.all_to_all(local.reshape(ny, -1, full), 'dy', 0, 0)  3.28 us
    ppermute x2, starting transfers between devices, swap_y(): far = lax.ppermute(far, 'dy', far_pairs)  2.39 us
  transfers between devices with their start and end apart: 16, of which 8 were waited for; matrix products, arithmetic and copies ran while one was open for 3% of the time, Pallas kernels for 26%

profile of v19, /device:TPU:0, one launch (start us, length us, event | category | flops | bytes accessed | tf_op | source)
XLA Modules:
  0.0 77.3 jit_solution(342228907497358756)
XLA Ops:
  0.6 2.0 %pack.1 = (bf16[16,16,896]{2,1,0:T(8,128)(2,1)}, bf16[8,16,896]{2,1,0:T(8,128)(2,1)}, s32[4,729]{1,0:T(4,128)S(1)}) custom-call(bf16[2,8,16,16,128]{4,3,2,1,0:T(8,128)(2,1)} %vec.11, bf16[8,16,16,512]{3,2,1,0:T(8,128)(2,1)} %res_hbm.1, f32[8,16,16]{2,1,0:T(8,128)} %inv_hbm.1, f32[8,16,16]{2,1,0:T(8,128)} %pot_hbm.1, s32[4,729]{1,0:T(4,128)} %bitcast.6), custom_call_target="tpu_custom_call" | custom-call | bytes 3873568 | tf_op jit(solution)/shard_map/pack/pallas_call | solution.py:566
  2.7 3.0 %collective-permute-start = (bf16[16,16,896]{2,1,0:T(8,128)(2,1)}, bf16[16,16,896]{2,1,0:T(8,128)(2,1)}, u32[]{:S(2)}, u32[]{:S(2)}) collective-permute-start(bf16[16,16,896]{2,1,0:T(8,128)(2,1)} %get-tuple-element.30), channel_id=1, source_target_pairs={{0,16},{1,17},{2,18},{3,19},{4,20},{5,21},{6,22},{7,23},{8,24},{9,... | collective-permute-start | bytes 1376264 | tf_op jit(solution)/shard_map/ppermute | solution.py:91
  5.7 3.7 %collective-permute-start.1 = (bf16[8,16,896]{2,1,0:T(8,128)(2,1)}, bf16[8,16,896]{2,1,0:T(8,128)(2,1)S(1)}, u32[]{:S(2)}, u32[]{:S(2)}) collective-permute-start(bf16[8,16,896]{2,1,0:T(8,128)(2,1)} %get-tuple-element.31), channel_id=1, source_target_pairs={{0,15},{1,0},{2,1},{3,2},{4,3},{5,4},{6,5},{7,6},{8,7},{9,8},{10,9... | collective-permute-start | bytes 688136 | tf_op jit(solution)/shard_map/ppermute | solution.py:91
  9.4 1.3 %copy-done.4 = bf16[729,729]{1,0:T(8,128)(2,1)S(1)} copy-done((bf16[729,729]{1,0:T(8,128)(2,1)S(1)}, bf16[729,729]{1,0:T(8,128)(2,1)}, u32[]{:S(2)}) %copy-start.4) | copy-done | bytes 1062906
  10.6 3.8 %order_cells.3.refs_1_ = bf16[2,736,768]{2,1,0:T(8,128)(2,1)S(1)} custom-call(bf16[729,729]{1,0:T(8,128)(2,1)S(1)} %copy-done.4, s32[4,729]{1,0:T(4,128)S(1)} %get-tuple-element.32.conn_ref), custom_call_target="tpu_custom_call" | custom-call | bytes 3335538 | tf_op jit(solution)/shard_map/order_cells/pallas_call | solution.py:566
  14.4 0.0 copy-start.2
  14.5 3.8 %order_cells.2.refs_0_ = bf16[2,736,768]{2,1,0:T(8,128)(2,1)S(1)} custom-call(bf16[729,729]{1,0:T(8,128)(2,1)S(1)} %copy-done.4, s32[4,729]{1,0:T(4,128)S(1)} %get-tuple-element.32.conn_ref), custom_call_target="tpu_custom_call" | custom-call | bytes 3335538 | tf_op jit(solution)/shard_map/order_cells/pallas_call | solution.py:566
  18.3 1.4 %copy-done = bf16[2,736,768]{2,1,0:T(8,128)(2,1)} copy-done((bf16[2,736,768]{2,1,0:T(8,128)(2,1)}, bf16[2,736,768]{2,1,0:T(8,128)(2,1)S(1)}, u32[]{:S(2)}) %copy-start) | copy-done | bytes 2261016
  19.7 0.0 collective-permute-done.1.from_y
  19.7 0.6 collective-permute-start.2
  20.2 1.3 %broadcast_in_dim.4.own_inv = f32[8,16,16,128]{3,2,1,0:T(8,128)S(1)} broadcast(f32[8,16,16]{2,1,0:T(8,128)} %inv_hbm.1), dimensions={0,1,2} | broadcast | bytes 1056768 | tf_op jit(solution)/shard_map/broadcast_in_dim | solution.py:609
  21.5 1.2 %broadcast_in_dim.5.own_pot = f32[8,16,16,128]{3,2,1,0:T(8,128)S(1)} broadcast(f32[8,16,16]{2,1,0:T(8,128)} %pot_hbm.1), dimensions={0,1,2} | broadcast | bytes 1056768 | tf_op jit(solution)/shard_map/broadcast_in_dim | solution.py:610
  22.7 2.5 %first_main.1 = (f32[4,736,256]{2,1,0:T(8,128)S(1)}, f32[2,16,16,128]{3,2,1,0:T(8,128)S(1)}, f32[2,8,16,128]{3,2,1,0:T(8,128)S(1)}) custom-call(bf16[2,8,16,16,128]{4,3,2,1,0:T(8,128)(2,1)S(1)} %copy-done.2, bf16[16,16,896]{2,1,0:T(8,128)(2,1)} %collective-permute-done.from_x, bf16[8,16,896]{2,1,0:T(8,128)(2,1)S(1)} %collective-permute-done.1.from_y, ...), custom_call_target="tpu_custom_call" | custom-call | flops 1157627904 | bytes 11763712 | tf_op jit(solution)/shard_map/first_main/pallas_call | solution.py:566
  25.2 0.0 collective-permute-done.2.corner
  25.2 1.9 %first_corner.1 = (f32[2,9,17,16,128]{4,3,2,1,0:T(8,128)S(1)}, bf16[2,2,17,16,128]{4,3,2,1,0:T(8,128)(2,1)S(1)}, bf16[2,9,16,128]{3,2,1,0:T(8,128)(2,1)S(1)}, bf...) custom-call(s32[1]{0:T(128)} %bitcast.even_ref, ...), custom_call_target="tpu_custom_call" | custom-call | flops 192937984 | bytes 14757892 | tf_op jit(solution)/shard_map/first_corner/pallas_call | solution.py:566
  27.1 1.5 %collective-permute-start.3 = (bf16[2,2,17,16,128]{4,3,2,1,0:T(8,128)(2,1)S(1)}, bf16[2,2,17,16,128]{4,3,2,1,0:T(8,128)(2,1)S(1)}, u32[]{:S(2)}, u32[]{:S(2)}) collective-permute-start(bf16[2,2,17,16,128]{4,3,2,1,0:T(8,128)(2,1)S(1)} %get-tuple-element.39), channel_id=1, source_target_pairs={{0,16},{1,17},{2,18},{3,19},{4,20},{5,21},{6,22},{7,23},{8,24},{9,... | collective-permute-start | bytes 835592 | tf_op jit(solution)/shard_map/ppermute | solution.py:91
  28.6 0.0 collective-permute-start.4
  28.6 1.2 %collective-permute-start.5 = (bf16[2,9,16,128]{3,2,1,0:T(8,128)(2,1)S(1)}, bf16[2,9,16,128]{3,2,1,0:T(8,128)(2,1)S(1)}, u32[]{:S(2)}, u32[]{:S(2)}) collective-permute-start(bf16[2,9,16,128]{3,2,1,0:T(8,128)(2,1)S(1)} %get-tuple-element.41), channel_id=1, source_target_pairs={{0,15},{1,2},{2,1},{3,4},{4,3},{5,6},{6,5},{7,8},{8,7},{9,10},{10,... | collective-permute-start | bytes 221192 | tf_op jit(solution)/shard_map/ppermute | solution.py:108
  29.7 0.1 collective-permute-done.4.near.near_in
  29.8 5.2 %collective-permute-done.5.far.far_in = bf16[2,9,16,128]{3,2,1,0:T(8,128)(2,1)S(1)} collective-permute-done((bf16[2,9,16,128]{3,2,1,0:T(8,128)(2,1)S(1)}, bf16[2,9,16,128]{3,2,1,0:T(8,128)(2,1)S(1)}, u32[]{:S(2)}, u32[]{:S(2)}) %collective-permute-start.5) | collective-permute-done | bytes 73760 | tf_op jit(solution)/shard_map/ppermute | solution.py:108
  35.0 0.6 collective-permute-start.6
  35.6 2.9 %second_main.1 = (f32[4,736,256]{2,1,0:T(8,128)S(1)}, f32[2,9,17,16,128]{4,3,2,1,0:T(8,128)S(1)}) custom-call(s32[1]{0:T(128)} %bitcast.even_ref, bf16[2,8,16,16,128]{4,3,2,1,0:T(8,128)(2,1)S(1)} %copy-done.2, bf16[16,16,896]{2,1,0:T(8,128)(2,1)} %collective-permute-done.from_x, bf16[8,16,896]{2,1,0:T(8,128)(2,1)S(1)} %collective-permute-done.1.from_y, ...), custom_call_target="tpu_custom_call" | custom-call | flops 1157627904 | bytes 17203204 | tf_op jit(solution)/shard_map/second_main/pallas_call | solution.py:566
  38.6 0.4 collective-permute-done.6.corner_in
  39.0 2.0 %second_corner.1 = (f32[2,9,17,16,128]{4,3,2,1,0:T(8,128)S(1)}, bf16[2,2,17,16,128]{4,3,2,1,0:T(8,128)(2,1)S(1)}, bf16[2,9,16,128]{3,2,1,0:T(8,128)(2,1)S(1)}, b...) custom-call(s32[1]{0:T(128)} %bitcast.even_ref, bf16[2,8,16,16,128]{4,3,2,1,0:T(8,128)(2,1)S(1)} %copy-done.2, ...), custom_call_target="tpu_custom_call" | custom-call | flops 192937984 | bytes 17760260 | tf_op jit(solution)/shard_map/second_corner/pallas_call | solution.py:566
  41.0 1.1 %collective-permute-start.7 = (bf16[2,2,17,16,128]{4,3,2,1,0:T(8,128)(2,1)S(1)}, bf16[2,2,17,16,128]{4,3,2,1,0:T(8,128)(2,1)S(1)}, u32[]{:S(2)}, u32[]{:S(2)}) collective-permute-start(bf16[2,2,17,16,128]{4,3,2,1,0:T(8,128)(2,1)S(1)} %get-tuple-element.44), channel_id=1, source_target_pairs={{0,16},{1,17},{2,18},{3,19},{4,20},{5,21},{6,22},{7,23},{8,24},{9,... | collective-permute-start | bytes 835592 | tf_op jit(solution)/shard_map/ppermute | solution.py:91
  42.1 0.0 collective-permute-start.8
  42.1 1.2 %collective-permute-start.9 = (bf16[2,9,16,128]{3,2,1,0:T(8,128)(2,1)S(1)}, bf16[2,9,16,128]{3,2,1,0:T(8,128)(2,1)S(1)}, u32[]{:S(2)}, u32[]{:S(2)}) collective-permute-start(bf16[2,9,16,128]{3,2,1,0:T(8,128)(2,1)S(1)} %get-tuple-element.46), channel_id=1, source_target_pairs={{0,15},{1,2},{2,1},{3,4},{4,3},{5,6},{6,5},{7,8},{8,7},{9,10},{10,... | collective-permute-start | bytes 221192 | tf_op jit(solution)/shard_map/ppermute | solution.py:108
  43.4 1.9 %turn_residents.1.turned = bf16[512,2560]{1,0:T(8,128)(2,1)S(1)} custom-call(bf16[2048,512]{1,0:T(8,128)(2,1)S(1)} %bitcast.4, bf16[16,16,896]{2,1,0:T(8,128)(2,1)} %collective-permute-done.from_x, bf16[8,16,896]{2,1,0:T(8,128)(2,1)S(1)} %collective-permute-done.1.from_y, bf16[1,16,896]{2,1,0:T(8,128)(2,1)S(1)} %collective-permute-done.2.corner), custom_call_target="tpu_custom_call" | custom-call | flops 578813952 | bytes 5435392 | tf_op jit(solution)/shard_map/turn_residents/pallas_call | solution.py:566
  45.3 3.3 %collective-permute-done.9.far.far_in = bf16[2,9,16,128]{3,2,1,0:T(8,128)(2,1)S(1)} collective-permute-done((bf16[2,9,16,128]{3,2,1,0:T(8,128)(2,1)S(1)}, bf16[2,9,16,128]{3,2,1,0:T(8,128)(2,1)S(1)}, u32[]{:S(2)}, u32[]{:S(2)}) %collective-permute-start.9) | collective-permute-done | bytes 73760 | tf_op jit(solution)/shard_map/ppermute | solution.py:108
  48.6 1.0 %collective-permute-start.10 = (bf16[2,2,2,16,128]{4,3,2,1,0:T(8,128)(2,1)S(1)}, bf16[2,2,2,16,128]{4,3,2,1,0:T(8,128)(2,1)S(1)}, u32[]{:S(2)}, u32[]{:S(2)}) collective-permute-start(bf16[2,2,2,16,128]{4,3,2,1,0:T(8,128)(2,1)S(1)} %corner_pack.3), channel_id=1, source_target_pairs={{0,16},{1,17},{2,18},{3,19},{4,20},{5,21},{6,22},{7,23},{8,24},{9,... | collective-permute-start | bytes 98312 | tf_op jit(solution)/shard_map/ppermute | solution.py:91
  49.6 3.1 %third_main.1 = (f32[4,736,256]{2,1,0:T(8,128)S(1)}, f32[2,9,17,16,128]{4,3,2,1,0:T(8,128)S(1)}) custom-call(s32[1]{0:T(128)} %bitcast.even_ref, bf16[2,8,16,16,128]{4,3,2,1,0:T(8,128)(2,1)S(1)} %copy-done.2, bf16[16,16,896]{2,1,0:T(8,128)(2,1)} %collective-permute-done.from_x, bf16[8,16,896]{2,1,0:T(8,128)(2,1)S(1)} %collective-permute-done.1.from_y, ...), custom_call_target="tpu_custom_call" | custom-call | flops 1157627904 | bytes 19709956 | tf_op jit(solution)/shard_map/third_main/pallas_call | solution.py:566
  52.7 4.3 %third_corner.1 = (f32[2,8,16,16,128]{4,3,2,1,0:T(8,128)}, bf16[2,16,16,128]{3,2,1,0:T(8,128)(2,1)S(1)}, f32[2,8,16,128]{3,2,1,0:T(8,128)S(1)}, bf16[2,16,128]{2,1,0:T(8,128)(2,1)S(1)}, bf16[512,256]{1,0:T(8,128)(2,1)S(1)}) custom-call(s32[1]{0:T(128)} %bitcast.even_ref, bf16[2,8,16,16,128]{4,3,2,1,0:T(8,128)(2,1)S(1)} %copy-done.2, ...), custom_call_target="tpu_custom_call" | custom-call | flops 864026624 | bytes 25092100 | tf_op jit(solution)/shard_map/third_corner/pallas_call | solution.py:566
  57.1 0.7 copy-done.5
  57.8 0.7 copy-done.6
  58.4 0.7 copy-done.8
  59.1 3.5 %all-to-all-start = ((bf16[16,32,256]{2,1,0:T(8,128)(2,1)}), bf16[16,32,256]{2,1,0:T(8,128)(2,1)S(1)}, u32[]{:S(2)}, u32[]{:S(2)}) async-start(bf16[16,32,256]{2,1,0:T(8,128)(2,1)} %bitcast.5), calls=%async_computation | async-start | bytes 524288 | tf_op jit(solution)/shard_map/all_to_all | solution.py:691
  62.6 1.1 %collective-permute-start.11 = (bf16[2,16,128]{2,1,0:T(8,128)(2,1)S(1)}, bf16[2,16,128]{2,1,0:T(8,128)(2,1)S(1)}, u32[]{:S(2)}, u32[]{:S(2)}) collective-permute-start(bf16[2,16,128]{2,1,0:T(8,128)(2,1)S(1)} %get-tuple-element.53), channel_id=1, source_target_pairs={{0,16},{1,17},{2,18},{3,19},{4,20},{5,21},{6,22},{7,23},{8,24},{9,... | collective-permute-start | bytes 24584 | tf_op jit(solution)/shard_map/ppermute | solution.py:91
  63.8 2.6 %collective-permute-done.11.corner_ref = bf16[2,16,128]{2,1,0:T(8,128)(2,1)S(1)} collective-permute-done((bf16[2,16,128]{2,1,0:T(8,128)(2,1)S(1)}, bf16[2,16,128]{2,1,0:T(8,128)(2,1)S(1)}, u32[]{:S(2)}, u32[]{:S(2)}) %collective-permute-start.11) | collective-permute-done | bytes 8224 | tf_op jit(solution)/shard_map/ppermute | solution.py:91
  66.4 0.9 %copy-done.7 = bf16[2,16,16,128]{3,2,1,0:T(8,128)(2,1)S(1)} copy-done((bf16[2,16,16,128]{3,2,1,0:T(8,128)(2,1)S(1)}, bf16[2,16,16,128]{3,2,1,0:T(8,128)(2,1)}, u32[]{:S(2)}) %copy-start.7) | copy-done | bytes 131096
  67.3 0.9 %copy-done.9 = f32[2,8,16,128]{3,2,1,0:T(8,128)S(1)} copy-done((f32[2,8,16,128]{3,2,1,0:T(8,128)S(1)}, f32[2,8,16,128]{3,2,1,0:T(8,128)}, u32[]{:S(2)}) %copy-start.9) | copy-done | bytes 131096
  68.2 0.1 collective-permute-start.13
  68.2 1.1 %collective-permute-start.12 = (bf16[2,16,16,128]{3,2,1,0:T(8,128)(2,1)S(1)}, bf16[2,16,16,128]{3,2,1,0:T(8,128)(2,1)S(1)}, u32[]{:S(2)}, u32[]{:S(2)}) collective-permute-start(bf16[2,16,16,128]{3,2,1,0:T(8,128)(2,1)S(1)} %get-tuple-element.55), channel_id=1, source_target_pairs={{0,16},{1,17},{2,18},{3,19},{4,20},{5,21},{6,22},{7,23},{8,24},{9,... | collective-permute-start | bytes 393224 | tf_op jit(solution)/shard_map/ppermute | solution.py:91
  69.4 3.3 %all-to-all-done = bf16[16,32,256]{2,1,0:T(8,128)(2,1)S(1)} async-done(((bf16[16,32,256]{2,1,0:T(8,128)(2,1)}), bf16[16,32,256]{2,1,0:T(8,128)(2,1)S(1)}, u32[]{:S(2)}, u32[]{:S(2)}) %all-to-all-start) | async-done | bytes 262176 | tf_op jit(solution)/shard_map/all_to_all | solution.py:691
  72.7 1.1 %collective-permute-start.14 = (f32[32,256]{1,0:T(8,128)S(1)}, f32[32,256]{1,0:T(8,128)S(1)}, u32[]{:S(2)}, u32[]{:S(2)}) collective-permute-start(f32[32,256]{1,0:T(8,128)S(1)} %convert_reduce_fusion), channel_id=1, source_target_pairs={{0,16},{1,17},{2,18},{3,19},{4,20},{5,21},{6,22},{7,23},{8,24},{9,... | collective-permute-start | bytes 98312 | tf_op jit(solution)/shard_map/ppermute | solution.py:91
  73.8 0.8 %collective-permute-done.13.side = bf16[2,8,16,128]{3,2,1,0:T(8,128)(2,1)S(1)} collective-permute-done((bf16[2,8,16,128]{3,2,1,0:T(8,128)(2,1)S(1)}, bf16[2,8,16,128]{3,2,1,0:T(8,128)(2,1)S(1)}, u32[]{:S(2)}, u32[]{:S(2)}) %collective-permute-start.13) | collective-permute-done | bytes 65568 | tf_op jit(solution)/shard_map/ppermute | solution.py:91
  74.6 1.8 %last.1 = f32[2,8,16,16,128]{4,3,2,1,0:T(8,128)} custom-call(f32[2,8,16,16,128]{4,3,2,1,0:T(8,128)} %get-tuple-element.51.old_hbm, bf16[2,16,16,128]{3,2,1,0:T(8,128)(2,1)S(1)} %collective-permute-done.12.face, bf16[2,8,16,128]{3,2,1,0:T(8,128)(2,1)S(1)} %collective-permute-done.13.side), custom_call_target="tpu_custom_call", output_to_operand_aliasing={{}: (0, {})} | custom-call | bytes 4390912 | tf_op jit(solution)/shard_map/last/pallas_call | solution.py:566
  76.4 0.3 collective-permute-done.14
  76.7 0.6 add.8
  (23 shorter events, 0.1 us)
Async XLA Ops:
  2.7 17.6 %collective-permute-start = (bf16[16,16,896]{2,1,0:T(8,128)(2,1)}, bf16[16,16,896]{2,1,0:T(8,128)(2,1)}, u32[]{:S(2)}, u32[]{:S(2)}) collective-permute-start(bf16[16,16,896]{2,1,0:T(8,128)(2,1)} %get-tuple-element.30), channel_id=1, source_target_pairs={{0,16},{1,17},{2,18},{3,19},{4,20},{5,21},{6,22},{7,23},{8,24},{9,... | collective-permute-start | bytes 1376264 | tf_op jit(solution)/shard_map/ppermute | solution.py:91
  5.7 14.0 %collective-permute-start.1 = (bf16[8,16,896]{2,1,0:T(8,128)(2,1)}, bf16[8,16,896]{2,1,0:T(8,128)(2,1)S(1)}, u32[]{:S(2)}, u32[]{:S(2)}) collective-permute-start(bf16[8,16,896]{2,1,0:T(8,128)(2,1)} %get-tuple-element.31), channel_id=1, source_target_pairs={{0,15},{1,0},{2,1},{3,2},{4,3},{5,4},{6,5},{7,6},{8,7},{9,8},{10,9... | collective-permute-start | bytes 688136 | tf_op jit(solution)/shard_map/ppermute | solution.py:91
  9.4 1.3 %copy-start.4 = (bf16[729,729]{1,0:T(8,128)(2,1)S(1)}, bf16[729,729]{1,0:T(8,128)(2,1)}, u32[]{:S(2)}) copy-start(bf16[729,729]{1,0:T(8,128)(2,1)} %matrix_ref.3) | copy-start | bytes 3188650
  14.4 8.3 %copy-start.2 = (bf16[2,8,16,16,128]{4,3,2,1,0:T(8,128)(2,1)S(1)}, bf16[2,8,16,16,128]{4,3,2,1,0:T(8,128)(2,1)}, u32[]{:S(2)}) copy-start(bf16[2,8,16,16,128]{4,3,2,1,0:T(8,128)(2,1)} %vec.11) | copy-start | bytes 3145732
  18.2 1.4 %copy-start = (bf16[2,736,768]{2,1,0:T(8,128)(2,1)}, bf16[2,736,768]{2,1,0:T(8,128)(2,1)S(1)}, u32[]{:S(2)}) copy-start(bf16[2,736,768]{2,1,0:T(8,128)(2,1)S(1)} %order_cells.2.refs_0_) | copy-start | bytes 6782980
  19.7 3.0 %copy-start.1 = (bf16[2,736,768]{2,1,0:T(8,128)(2,1)S(1)}, bf16[2,736,768]{2,1,0:T(8,128)(2,1)}, u32[]{:S(2)}) copy-start(bf16[2,736,768]{2,1,0:T(8,128)(2,1)} %copy-done) | copy-start | bytes 6782980
  19.7 5.5 %collective-permute-start.2 = (bf16[1,16,896]{2,1,0:T(8,128)(2,1)S(1)}, bf16[1,16,896]{2,1,0:T(8,128)(2,1)S(1)}, u32[]{:S(2)}, u32[]{:S(2)}) collective-permute-start(bf16[1,16,896]{2,1,0:T(8,128)(2,1)S(1)} %slice.4), channel_id=1, source_target_pairs={{0,16},{1,17},{2,18},{3,19},{4,20},{5,21},{6,22},{7,23},{8,24},{9,... | collective-permute-start | bytes 86024 | tf_op jit(solution)/shard_map/ppermute | solution.py:91
  27.1 8.6 %collective-permute-start.3 = (bf16[2,2,17,16,128]{4,3,2,1,0:T(8,128)(2,1)S(1)}, bf16[2,2,17,16,128]{4,3,2,1,0:T(8,128)(2,1)S(1)}, u32[]{:S(2)}, u32[]{:S(2)}) collective-permute-start(bf16[2,2,17,16,128]{4,3,2,1,0:T(8,128)(2,1)S(1)} %get-tuple-element.39), channel_id=1, source_target_pairs={{0,16},{1,17},{2,18},{3,19},{4,20},{5,21},{6,22},{7,23},{8,24},{9,... | collective-permute-start | bytes 835592 | tf_op jit(solution)/shard_map/ppermute | solution.py:91
  28.6 1.3 %collective-permute-start.4 = (bf16[2,9,16,128]{3,2,1,0:T(8,128)(2,1)S(1)}, bf16[2,9,16,128]{3,2,1,0:T(8,128)(2,1)S(1)}, u32[]{:S(2)}, u32[]{:S(2)}) collective-permute-start(bf16[2,9,16,128]{3,2,1,0:T(8,128)(2,1)S(1)} %get-tuple-element.40), channel_id=1, source_target_pairs={{0,1},{1,0},{2,3},{3,2},{4,5},{5,4},{6,7},{7,6},{8,9},{9,8},{10,11... | collective-permute-start | bytes 221192 | tf_op jit(solution)/shard_map/ppermute | solution.py:102
  28.6 6.5 %collective-permute-start.5 = (bf16[2,9,16,128]{3,2,1,0:T(8,128)(2,1)S(1)}, bf16[2,9,16,128]{3,2,1,0:T(8,128)(2,1)S(1)}, u32[]{:S(2)}, u32[]{:S(2)}) collective-permute-start(bf16[2,9,16,128]{3,2,1,0:T(8,128)(2,1)S(1)} %get-tuple-element.41), channel_id=1, source_target_pairs={{0,15},{1,2},{2,1},{3,4},{4,3},{5,6},{6,5},{7,8},{8,7},{9,10},{10,... | collective-permute-start | bytes 221192 | tf_op jit(solution)/shard_map/ppermute | solution.py:108
  35.0 3.9 %collective-permute-start.6 = (bf16[2,2,2,16,128]{4,3,2,1,0:T(8,128)(2,1)S(1)}, bf16[2,2,2,16,128]{4,3,2,1,0:T(8,128)(2,1)S(1)}, u32[]{:S(2)}, u32[]{:S(2)}) collective-permute-start(bf16[2,2,2,16,128]{4,3,2,1,0:T(8,128)(2,1)S(1)} %corner_pack.2), channel_id=1, source_target_pairs={{0,16},{1,17},{2,18},{3,19},{4,20},{5,21},{6,22},{7,23},{8,24},{9,... | collective-permute-start | bytes 98312 | tf_op jit(solution)/shard_map/ppermute | solution.py:91
  39.0 4.4 %copy-start.3 = (bf16[8,16,16,512]{3,2,1,0:T(8,128)(2,1)S(1)}, bf16[8,16,16,512]{3,2,1,0:T(8,128)(2,1)}, u32[]{:S(2)}) copy-start(bf16[8,16,16,512]{3,2,1,0:T(8,128)(2,1)} %res_hbm.1) | copy-start | bytes 6291460
  41.0 8.6 %collective-permute-start.7 = (bf16[2,2,17,16,128]{4,3,2,1,0:T(8,128)(2,1)S(1)}, bf16[2,2,17,16,128]{4,3,2,1,0:T(8,128)(2,1)S(1)}, u32[]{:S(2)}, u32[]{:S(2)}) collective-permute-start(bf16[2,2,17,16,128]{4,3,2,1,0:T(8,128)(2,1)S(1)} %get-tuple-element.44), channel_id=1, source_target_pairs={{0,16},{1,17},{2,18},{3,19},{4,20},{5,21},{6,22},{7,23},{8,24},{9,... | collective-permute-start | bytes 835592 | tf_op jit(solution)/shard_map/ppermute | solution.py:91
  42.1 3.2 %collective-permute-start.8 = (bf16[2,9,16,128]{3,2,1,0:T(8,128)(2,1)S(1)}, bf16[2,9,16,128]{3,2,1,0:T(8,128)(2,1)S(1)}, u32[]{:S(2)}, u32[]{:S(2)}) collective-permute-start(bf16[2,9,16,128]{3,2,1,0:T(8,128)(2,1)S(1)} %get-tuple-element.45), channel_id=1, source_target_pairs={{0,1},{1,0},{2,3},{3,2},{4,5},{5,4},{6,7},{7,6},{8,9},{9,8},{10,11... | collective-permute-start | bytes 221192 | tf_op jit(solution)/shard_map/ppermute | solution.py:102
  42.1 6.5 %collective-permute-start.9 = (bf16[2,9,16,128]{3,2,1,0:T(8,128)(2,1)S(1)}, bf16[2,9,16,128]{3,2,1,0:T(8,128)(2,1)S(1)}, u32[]{:S(2)}, u32[]{:S(2)}) collective-permute-start(bf16[2,9,16,128]{3,2,1,0:T(8,128)(2,1)S(1)} %get-tuple-element.46), channel_id=1, source_target_pairs={{0,15},{1,2},{2,1},{3,4},{4,3},{5,6},{6,5},{7,8},{8,7},{9,10},{10,... | collective-permute-start | bytes 221192 | tf_op jit(solution)/shard_map/ppermute | solution.py:108
  48.6 4.1 %collective-permute-start.10 = (bf16[2,2,2,16,128]{4,3,2,1,0:T(8,128)(2,1)S(1)}, bf16[2,2,2,16,128]{4,3,2,1,0:T(8,128)(2,1)S(1)}, u32[]{:S(2)}, u32[]{:S(2)}) collective-permute-start(bf16[2,2,2,16,128]{4,3,2,1,0:T(8,128)(2,1)S(1)} %corner_pack.3), channel_id=1, source_target_pairs={{0,16},{1,17},{2,18},{3,19},{4,20},{5,21},{6,22},{7,23},{8,24},{9,... | collective-permute-start | bytes 98312 | tf_op jit(solution)/shard_map/ppermute | solution.py:91
  57.1 0.7 copy-start.5
  57.8 0.7 copy-start.6
  58.4 0.7 copy-start.8
  59.1 13.5 %all-to-all-start = ((bf16[16,32,256]{2,1,0:T(8,128)(2,1)}), bf16[16,32,256]{2,1,0:T(8,128)(2,1)S(1)}, u32[]{:S(2)}, u32[]{:S(2)}) async-start(bf16[16,32,256]{2,1,0:T(8,128)(2,1)} %bitcast.5), calls=%async_computation | async-start | bytes 524288 | tf_op jit(solution)/shard_map/all_to_all | solution.py:691
  62.6 3.7 %collective-permute-start.11 = (bf16[2,16,128]{2,1,0:T(8,128)(2,1)S(1)}, bf16[2,16,128]{2,1,0:T(8,128)(2,1)S(1)}, u32[]{:S(2)}, u32[]{:S(2)}) collective-permute-start(bf16[2,16,128]{2,1,0:T(8,128)(2,1)S(1)} %get-tuple-element.53), channel_id=1, source_target_pairs={{0,16},{1,17},{2,18},{3,19},{4,20},{5,21},{6,22},{7,23},{8,24},{9,... | collective-permute-start | bytes 24584 | tf_op jit(solution)/shard_map/ppermute | solution.py:91
  66.4 0.9 %copy-start.7 = (bf16[2,16,16,128]{3,2,1,0:T(8,128)(2,1)S(1)}, bf16[2,16,16,128]{3,2,1,0:T(8,128)(2,1)}, u32[]{:S(2)}) copy-start(bf16[2,16,16,128]{3,2,1,0:T(8,128)(2,1)} %copy-done.6) | copy-start | bytes 393220
  67.3 0.9 %copy-start.9 = (f32[2,8,16,128]{3,2,1,0:T(8,128)S(1)}, f32[2,8,16,128]{3,2,1,0:T(8,128)}, u32[]{:S(2)}) copy-start(f32[2,8,16,128]{3,2,1,0:T(8,128)} %copy-done.8) | copy-start | bytes 393220
  68.2 6.4 %collective-permute-start.13 = (bf16[2,8,16,128]{3,2,1,0:T(8,128)(2,1)S(1)}, bf16[2,8,16,128]{3,2,1,0:T(8,128)(2,1)S(1)}, u32[]{:S(2)}, u32[]{:S(2)}) collective-permute-start(bf16[2,8,16,128]{3,2,1,0:T(8,128)(2,1)S(1)} %get-tuple-element.56), channel_id=1, source_target_pairs={{0,1},{1,2},{2,3},{3,4},{4,5},{5,6},{6,7},{7,8},{8,9},{9,10},{10,1... | collective-permute-start | bytes 196616 | tf_op jit(solution)/shard_map/ppermute | solution.py:91
  68.2 6.4 %collective-permute-start.12 = (bf16[2,16,16,128]{3,2,1,0:T(8,128)(2,1)S(1)}, bf16[2,16,16,128]{3,2,1,0:T(8,128)(2,1)S(1)}, u32[]{:S(2)}, u32[]{:S(2)}) collective-permute-start(bf16[2,16,16,128]{3,2,1,0:T(8,128)(2,1)S(1)} %get-tuple-element.55), channel_id=1, source_target_pairs={{0,16},{1,17},{2,18},{3,19},{4,20},{5,21},{6,22},{7,23},{8,24},{9,... | collective-permute-start | bytes 393224 | tf_op jit(solution)/shard_map/ppermute | solution.py:91
  72.7 4.0 %collective-permute-start.14 = (f32[32,256]{1,0:T(8,128)S(1)}, f32[32,256]{1,0:T(8,128)S(1)}, u32[]{:S(2)}, u32[]{:S(2)}) collective-permute-start(f32[32,256]{1,0:T(8,128)S(1)} %convert_reduce_fusion), channel_id=1, source_target_pairs={{0,16},{1,17},{2,18},{3,19},{4,20},{5,21},{6,22},{7,23},{8,24},{9,... | collective-permute-start | bytes 98312 | tf_op jit(solution)/shard_map/ppermute | solution.py:91

commit v20 on v18

--- a/solution.py
+++ b/solution.py
@@ -462,8 +462,8 @@
                  last_x, last_field, acc_in, face_in, near_in, far_in, corner_in, prod_ref, y_ref,
                  y_corner, new_ref, turned, *refs):
     mats = refs[:n_mat]
-    out_hbm, face, side, corner, margin = refs[n_mat : n_mat + 5]
-    part_ref, sem, acc_ref, rows_ref, small_ref, tail_ref = refs[n_mat + 5 :]
+    out_hbm, margin_hbm, face, side, corner = refs[n_mat : n_mat + 5]
+    part_ref, margin, sem, acc_ref, rows_ref, small_ref, tail_ref = refs[n_mat + 5 :]
     nodes = Nodes(sz, vec, from_x, from_y, own_inv, own_pot, ghost_x, ghost_y, last_field)
     sums = Sums(sz, even_ref[0] == 0, acc_in, face_in, near_in, far_in, corner_in)
     u_corner, new_corner = [], []
@@ -506,10 +506,15 @@
             copies[-1].start()
     for at in range(sz.own_edges + sz.ey + sz.gx, sz.edges):
         rows_ref[at] = jnp.zeros((sz.ez, sz.full), bf16)
-    local = jnp.dot(
-        turned[...], rows_ref[...].reshape(sz.edges * sz.ez, sz.full), preferred_element_type=f32
-    )
-    margin[...] = (local * norm_scale).astype(bf16)
+    rows = rows_ref[...].reshape(sz.edges * sz.ez, sz.full)
+    half = sz.res // 2
+    for at in range(2):
+        span = slice(at * half, (at + 1) * half)
+        local = jnp.dot(turned[span], rows, preferred_element_type=f32)
+        margin[span] = (local * norm_scale).astype(bf16)
+        span = pl.ds(at * half, half)
+        copies.append(pltpu.make_async_copy(margin.at[span], margin_hbm.at[span], sem.at[sz.ex + at]))
+        copies[-1].start()
     for copy in copies:
         copy.wait()
 
@@ -675,17 +680,16 @@
         [products, state_grid], main_scratch,
         [parity, *state, acc, *got, y1, *mats], scalar_first=True,
     )
-    filtered, face, side, corner, local = call(
+    filtered, local, face, side, corner = call(
         functools.partial(third_corner, sz, n_mat, norm_scale), "third_corner",
         small_flops + 2 * res_count * sz.edges * ez * full,
         [
-            like(own, f32),
-            like((blocks, sz.ey) + tile, bf16), like((blocks, sz.ex) + tile, f32), like(sz.edge, bf16),
-            like((res_count, full), bf16),
+            like(own, f32), like((res_count, full), bf16), like((blocks, sz.ey) + tile, bf16),
+            like((blocks, sz.ex) + tile, f32), like(sz.edge, bf16),
         ],
-        [pltpu.VMEM(own, f32), pltpu.SemaphoreType.DMA((sz.ex,)), pltpu.VMEM(grid, f32), pltpu.VMEM((sz.edges, ez, full), bf16)] + corner_scratch,
+        [pltpu.VMEM(own, f32), pltpu.VMEM((res_count, full), bf16), pltpu.SemaphoreType.DMA((sz.ex + 2,)), pltpu.VMEM(grid, f32), pltpu.VMEM((sz.edges, ez, full), bf16)] + corner_scratch,
         [parity, *state, *ends, acc, *got, corner, prod, y1, y1_corner, y2, turned, *mats],
-        scalar_first=True, out_hbm=1,
+        scalar_first=True, out_hbm=2,
     )
 
     pieces = lax.all_to_all(local.reshape(ny, -1, full), "dy", 0, 0)

time: 70.2 us -> 69.7 us (level)
  no operation moved by 1% of the time
where the time goes in v20:
time: 69.7 us; the launch traced here: 69.4 us
  waiting for transfers between devices  23.5 us (34%)
  Pallas kernels  22.7 us (33%)
  starting transfers between devices  19.8 us (28%)
  local copies, waits for them, and re-layouts  1.94 us (3%)
  between operations  0.83 us (1%)
    pallas_call x14, Pallas kernels, call(): pl.pallas_call(kernel, in_specs=specs, out_specs=out_specs, out_shape=out...  22.7 us
    ppermute x11, starting transfers between devices, send(): return lax.ppermute(value, ('dx', 'dy'), pairs)  13.2 us
    ppermute x2, waiting for transfers between devices, swap_y(): far = lax.ppermute(far, 'dy', far_pairs)  9.04 us
    ppermute x11, waiting for transfers between devices, send(): return lax.ppermute(value, ('dx', 'dy'), pairs)  8.28 us
    all_to_all x1, waiting for transfers between devices, body(): pieces = lax.all_to_all(local.reshape(ny, -1, full), 'dy', 0, 0)  6.2 us
    all_to_all x1, starting transfers between devices, body(): pieces = lax.all_to_all(local.reshape(ny, -1, full), 'dy', 0, 0)  3.54 us
    ppermute x2, starting transfers between devices, swap_y(): far = lax.ppermute(far, 'dy', far_pairs)  2.98 us
  transfers between devices with their start and end apart: 16, of which 8 were waited for; matrix products, arithmetic and copies ran while one was open for 1% of the time, Pallas kernels for 23%

profile of v20, /device:TPU:0, one launch (start us, length us, event | category | flops | bytes accessed | tf_op | source)
XLA Modules:
  0.0 69.4 jit_solution(1035191592535107273)
XLA Ops:
  0.6 0.0 copy-start.2
  0.6 2.0 %pack.1 = (bf16[16,16,896]{2,1,0:T(8,128)(2,1)S(1)}, bf16[8,16,896]{2,1,0:T(8,128)(2,1)}, s32[4,729]{1,0:T(4,128)S(1)}) custom-call(bf16[2,8,16,16,128]{4,3,2,1,0:T(8,128)(2,1)} %vec.11, bf16[8,16,16,512]{3,2,1,0:T(8,128)(2,1)} %res_hbm.1, f32[8,16,16]{2,1,0:T(8,128)} %inv_hbm.1, f32[8,16,16]{2,1,0:T(8,128)} %pot_hbm.1, s32[4,729]{1,0:T(4,128)} %bitcast.6), custom_call_target="tpu_custom_call" | custom-call | bytes 3873568 | tf_op jit(solution)/shard_map/pack/pallas_call | solution.py:571
  2.6 5.5 %collective-permute-start.1 = (bf16[8,16,896]{2,1,0:T(8,128)(2,1)}, bf16[8,16,896]{2,1,0:T(8,128)(2,1)S(1)}, u32[]{:S(2)}, u32[]{:S(2)}) collective-permute-start(bf16[8,16,896]{2,1,0:T(8,128)(2,1)} %get-tuple-element.31), channel_id=1, source_target_pairs={{0,15},{1,0},{2,1},{3,2},{4,3},{5,4},{6,5},{7,6},{8,7},{9,8},{10,9... | collective-permute-start | bytes 688136 | tf_op jit(solution)/shard_map/ppermute | solution.py:91
  8.1 1.5 %collective-permute-start = (bf16[16,16,896]{2,1,0:T(8,128)(2,1)S(1)}, bf16[16,16,896]{2,1,0:T(8,128)(2,1)S(1)}, u32[]{:S(2)}, u32[]{:S(2)}) collective-permute-start(bf16[16,16,896]{2,1,0:T(8,128)(2,1)S(1)} %get-tuple-element.30), channel_id=1, source_target_pairs={{0,16},{1,17},{2,18},{3,19},{4,20},{5,21},{6,22},{7,23},{8,24},{9,... | collective-permute-start | bytes 1376264 | tf_op jit(solution)/shard_map/ppermute | solution.py:91
  9.6 3.8 %order_cells.3.refs_1_ = bf16[2,736,768]{2,1,0:T(8,128)(2,1)S(1)} custom-call(bf16[729,729]{1,0:T(8,128)(2,1)S(1)} %copy-done.2, s32[4,729]{1,0:T(4,128)S(1)} %get-tuple-element.32.conn_ref), custom_call_target="tpu_custom_call" | custom-call | flops 3623878656 | bytes 3335538 | tf_op jit(solution)/shard_map/order_cells/pallas_call | solution.py:571
  13.4 0.0 copy-start.3
  13.4 1.2 %copy-done.3 = bf16[729,729]{1,0:T(8,128)(2,1)S(1)} copy-done((bf16[729,729]{1,0:T(8,128)(2,1)S(1)}, bf16[729,729]{1,0:T(8,128)(2,1)}, u32[]{:S(2)}) %copy-start.3) | copy-done | bytes 1062906
  14.7 3.8 %order_cells.2.refs_0_ = bf16[2,736,768]{2,1,0:T(8,128)(2,1)S(1)} custom-call(bf16[729,729]{1,0:T(8,128)(2,1)S(1)} %copy-done.3, s32[4,729]{1,0:T(4,128)S(1)} %get-tuple-element.32.conn_ref), custom_call_target="tpu_custom_call" | custom-call | flops 3623878656 | bytes 3335538 | tf_op jit(solution)/shard_map/order_cells/pallas_call | solution.py:571
  18.5 0.0 copy-start
  18.5 0.0 collective-permute-done.1.from_y
  18.5 0.6 collective-permute-start.2
  19.1 0.0 collective-permute-done.from_x
  19.1 0.3 broadcast_in_dim.4.own_inv
  19.4 0.3 broadcast_in_dim.5.own_pot
  19.8 1.5 %first_main.1 = (f32[4,736,256]{2,1,0:T(8,128)S(1)}, f32[2,16,16,128]{3,2,1,0:T(8,128)S(1)}, f32[2,8,16,128]{3,2,1,0:T(8,128)S(1)}) custom-call(bf16[2,8,16,16,128]{4,3,2,1,0:T(8,128)(2,1)S(1)} %copy-done, bf16[16,16,896]{2,1,0:T(8,128)(2,1)S(1)} %collective-permute-done.from_x, bf16[8,16,896]{2,1,0:T(8,128)(2,1)S(1)} %collective-permute-done.1.from_y, ...), custom_call_target="tpu_custom_call" | custom-call | flops 1157627904 | bytes 11763712 | tf_op jit(solution)/shard_map/first_main/pallas_call | solution.py:571
  21.2 1.5 %collective-permute-done.2.corner = bf16[1,16,896]{2,1,0:T(8,128)(2,1)S(1)} collective-permute-done((bf16[1,16,896]{2,1,0:T(8,128)(2,1)S(1)}, bf16[1,16,896]{2,1,0:T(8,128)(2,1)S(1)}, u32[]{:S(2)}, u32[]{:S(2)}) %collective-permute-start.2) | collective-permute-done | bytes 28704 | tf_op jit(solution)/shard_map/ppermute | solution.py:91
  22.7 0.8 %first_corner.1 = (f32[2,9,17,16,128]{4,3,2,1,0:T(8,128)S(1)}, bf16[2,2,17,16,128]{4,3,2,1,0:T(8,128)(2,1)S(1)}, bf16[2,9,16,128]{3,2,1,0:T(8,128)(2,1)S(1)}, bf...) custom-call(s32[1]{0:T(128)} %bitcast.even_ref, ...), custom_call_target="tpu_custom_call" | custom-call | flops 192937984 | bytes 14757892 | tf_op jit(solution)/shard_map/first_corner/pallas_call | solution.py:571
  23.6 0.5 collective-permute-start.3
  24.1 0.0 collective-permute-start.4
  24.1 2.6 %collective-permute-start.5 = (bf16[2,9,16,128]{3,2,1,0:T(8,128)(2,1)S(1)}, bf16[2,9,16,128]{3,2,1,0:T(8,128)(2,1)S(1)}, u32[]{:S(2)}, u32[]{:S(2)}) collective-permute-start(bf16[2,9,16,128]{3,2,1,0:T(8,128)(2,1)S(1)} %get-tuple-element.41), channel_id=1, source_target_pairs={{0,15},{1,2},{2,1},{3,4},{4,3},{5,6},{6,5},{7,8},{8,7},{9,10},{10,... | collective-permute-start | bytes 221192 | tf_op jit(solution)/shard_map/ppermute | solution.py:108
  26.6 0.0 collective-permute-done.4.near.near_in
  26.6 3.9 %collective-permute-done.5.far.far_in = bf16[2,9,16,128]{3,2,1,0:T(8,128)(2,1)S(1)} collective-permute-done((bf16[2,9,16,128]{3,2,1,0:T(8,128)(2,1)S(1)}, bf16[2,9,16,128]{3,2,1,0:T(8,128)(2,1)S(1)}, u32[]{:S(2)}, u32[]{:S(2)}) %collective-permute-start.5) | collective-permute-done | bytes 73760 | tf_op jit(solution)/shard_map/ppermute | solution.py:108
  30.6 1.6 %collective-permute-start.6 = (bf16[2,2,2,16,128]{4,3,2,1,0:T(8,128)(2,1)S(1)}, bf16[2,2,2,16,128]{4,3,2,1,0:T(8,128)(2,1)S(1)}, u32[]{:S(2)}, u32[]{:S(2)}) collective-permute-start(bf16[2,2,2,16,128]{4,3,2,1,0:T(8,128)(2,1)S(1)} %corner_pack.2), channel_id=1, source_target_pairs={{0,16},{1,17},{2,18},{3,19},{4,20},{5,21},{6,22},{7,23},{8,24},{9,... | collective-permute-start | bytes 98312 | tf_op jit(solution)/shard_map/ppermute | solution.py:91
  32.2 0.0 collective-permute-done.3.face_in
  32.2 1.9 %second_main.1 = (f32[4,736,256]{2,1,0:T(8,128)S(1)}, f32[2,9,17,16,128]{4,3,2,1,0:T(8,128)S(1)}) custom-call(s32[1]{0:T(128)} %bitcast.even_ref, bf16[2,8,16,16,128]{4,3,2,1,0:T(8,128)(2,1)S(1)} %copy-done, bf16[16,16,896]{2,1,0:T(8,128)(2,1)S(1)} %collective-permute-done.from_x, bf16[8,16,896]{2,1,0:T(8,128)(2,1)S(1)} %collective-permute-done.1.from_y, ...), custom_call_target="tpu_custom_call" | custom-call | flops 1157627904 | bytes 17203204 | tf_op jit(solution)/shard_map/second_main/pallas_call | solution.py:571
  34.1 0.4 collective-permute-done.6.corner_in
  34.5 0.9 %second_corner.1 = (f32[2,9,17,16,128]{4,3,2,1,0:T(8,128)S(1)}, bf16[2,2,17,16,128]{4,3,2,1,0:T(8,128)(2,1)S(1)}, bf16[2,9,16,128]{3,2,1,0:T(8,128)(2,1)S(1)}, b...) custom-call(s32[1]{0:T(128)} %bitcast.even_ref, bf16[2,8,16,16,128]{4,3,2,1,0:T(8,128)(2,1)S(1)} %copy-done, ...), custom_call_target="tpu_custom_call" | custom-call | flops 192937984 | bytes 17760260 | tf_op jit(solution)/shard_map/second_corner/pallas_call | solution.py:571
  35.4 1.7 %collective-permute-start.7 = (bf16[2,2,17,16,128]{4,3,2,1,0:T(8,128)(2,1)S(1)}, bf16[2,2,17,16,128]{4,3,2,1,0:T(8,128)(2,1)S(1)}, u32[]{:S(2)}, u32[]{:S(2)}) collective-permute-start(bf16[2,2,17,16,128]{4,3,2,1,0:T(8,128)(2,1)S(1)} %get-tuple-element.44), channel_id=1, source_target_pairs={{0,16},{1,17},{2,18},{3,19},{4,20},{5,21},{6,22},{7,23},{8,24},{9,... | collective-permute-start | bytes 835592 | tf_op jit(solution)/shard_map/ppermute | solution.py:91
  37.0 0.0 collective-permute-start.8
  37.0 0.4 collective-permute-start.9
  37.5 0.9 %turn_residents.1.turned = bf16[512,2560]{1,0:T(8,128)(2,1)S(1)} custom-call(bf16[2048,512]{1,0:T(8,128)(2,1)S(1)} %bitcast.4, bf16[16,16,896]{2,1,0:T(8,128)(2,1)S(1)} %collective-permute-done.from_x, bf16[8,16,896]{2,1,0:T(8,128)(2,1)S(1)} %collective-permute-done.1.from_y, bf16[1,16,896]{2,1,0:T(8,128)(2,1)S(1)} %collective-permute-done.2.corner), custom_call_target="tpu_custom_call" | custom-call | flops 578813952 | bytes 5435392 | tf_op jit(solution)/shard_map/turn_residents/pallas_call | solution.py:571
  38.4 5.1 %collective-permute-done.9.far.far_in = bf16[2,9,16,128]{3,2,1,0:T(8,128)(2,1)S(1)} collective-permute-done((bf16[2,9,16,128]{3,2,1,0:T(8,128)(2,1)S(1)}, bf16[2,9,16,128]{3,2,1,0:T(8,128)(2,1)S(1)}, u32[]{:S(2)}, u32[]{:S(2)}) %collective-permute-start.9) | collective-permute-done | bytes 73760 | tf_op jit(solution)/shard_map/ppermute | solution.py:108
  43.5 0.4 collective-permute-start.10
  43.9 2.1 %third_main.1 = (f32[4,736,256]{2,1,0:T(8,128)S(1)}, f32[2,9,17,16,128]{4,3,2,1,0:T(8,128)S(1)}) custom-call(s32[1]{0:T(128)} %bitcast.even_ref, bf16[2,8,16,16,128]{4,3,2,1,0:T(8,128)(2,1)S(1)} %copy-done, bf16[16,16,896]{2,1,0:T(8,128)(2,1)S(1)} %collective-permute-done.from_x, bf16[8,16,896]{2,1,0:T(8,128)(2,1)S(1)} %collective-permute-done.1.from_y, ...), custom_call_target="tpu_custom_call" | custom-call | flops 1157627904 | bytes 19709956 | tf_op jit(solution)/shard_map/third_main/pallas_call | solution.py:571
  46.0 1.4 %collective-permute-done.10.corner_in = bf16[2,2,2,16,128]{4,3,2,1,0:T(8,128)(2,1)S(1)} collective-permute-done((bf16[2,2,2,16,128]{4,3,2,1,0:T(8,128)(2,1)S(1)}, bf16[2,2,2,16,128]{4,3,2,1,0:T(8,128)(2,1)S(1)}, u32[]{:S(2)}, u32[]{:S(2)}) %collective-permute-start.10) | collective-permute-done | bytes 32800 | tf_op jit(solution)/shard_map/ppermute | solution.py:91
  47.4 3.3 %third_corner.1 = (f32[2,8,16,16,128]{4,3,2,1,0:T(8,128)}, bf16[512,256]{1,0:T(8,128)(2,1)}, bf16[2,16,16,128]{3,2,1,0:T(8,128)(2,1)S(1)}, f32[2,8,16,128]{3,2,1,0:T(8,128)S(1)}, bf16[2,16,128]{2,1,0:T(8,128)(2,1)S(1)}) custom-call(s32[1]{0:T(128)} %bitcast.even_ref, bf16[2,8,16,16,128]{4,3,2,1,0:T(8,128)(2,1)S(1)} %copy-done, ...), custom_call_target="tpu_custom_call" | custom-call | flops 864026624 | bytes 25092100 | tf_op jit(solution)/shard_map/third_corner/pallas_call | solution.py:571
  50.7 3.5 %all-to-all-start = ((bf16[16,32,256]{2,1,0:T(8,128)(2,1)}), bf16[16,32,256]{2,1,0:T(8,128)(2,1)S(1)}, u32[]{:S(2)}, u32[]{:S(2)}) async-start(bf16[16,32,256]{2,1,0:T(8,128)(2,1)} %bitcast.5), calls=%async_computation | async-start | bytes 524288 | tf_op jit(solution)/shard_map/all_to_all | solution.py:695
  54.3 0.5 collective-permute-start.11
  54.7 3.2 %collective-permute-done.11.corner_ref = bf16[2,16,128]{2,1,0:T(8,128)(2,1)S(1)} collective-permute-done((bf16[2,16,128]{2,1,0:T(8,128)(2,1)S(1)}, bf16[2,16,128]{2,1,0:T(8,128)(2,1)S(1)}, u32[]{:S(2)}, u32[]{:S(2)}) %collective-permute-start.11) | collective-permute-done | bytes 8224 | tf_op jit(solution)/shard_map/ppermute | solution.py:91
  58.0 0.1 collective-permute-start.13
  58.1 0.5 collective-permute-start.12
  58.5 6.2 %all-to-all-done = bf16[16,32,256]{2,1,0:T(8,128)(2,1)S(1)} async-done(((bf16[16,32,256]{2,1,0:T(8,128)(2,1)}), bf16[16,32,256]{2,1,0:T(8,128)(2,1)S(1)}, u32[]{:S(2)}, u32[]{:S(2)}) %all-to-all-start) | async-done | bytes 262176 | tf_op jit(solution)/shard_map/all_to_all | solution.py:695
  64.8 0.5 collective-permute-start.14
  65.3 0.0 collective-permute-done.13.side
  65.3 0.0 collective-permute-done.12.face
  65.3 1.8 %last.1 = f32[2,8,16,16,128]{4,3,2,1,0:T(8,128)} custom-call(f32[2,8,16,16,128]{4,3,2,1,0:T(8,128)} %get-tuple-element.51.old_hbm, bf16[2,16,16,128]{3,2,1,0:T(8,128)(2,1)S(1)} %collective-permute-done.12.face, bf16[2,8,16,128]{3,2,1,0:T(8,128)(2,1)S(1)} %collective-permute-done.13.side), custom_call_target="tpu_custom_call", output_to_operand_aliasing={{}: (0, {})} | custom-call | bytes 4390912 | tf_op jit(solution)/shard_map/last/pallas_call | solution.py:571
  67.0 1.7 %collective-permute-done.14 = f32[32,256]{1,0:T(8,128)S(1)} collective-permute-done((f32[32,256]{1,0:T(8,128)S(1)}, f32[32,256]{1,0:T(8,128)S(1)}, u32[]{:S(2)}, u32[]{:S(2)}) %collective-permute-start.14) | collective-permute-done | bytes 32800 | tf_op jit(solution)/shard_map/ppermute | solution.py:91
  68.8 0.6 add.8
  (15 shorter events, 0.1 us)
Async XLA Ops:
  0.6 9.0 %copy-start.2 = (bf16[729,729]{1,0:T(8,128)(2,1)S(1)}, bf16[729,729]{1,0:T(8,128)(2,1)}, u32[]{:S(2)}) copy-start(bf16[729,729]{1,0:T(8,128)(2,1)} %matrix_ref.3) | copy-start | bytes 3188650
  2.6 15.9 %collective-permute-start.1 = (bf16[8,16,896]{2,1,0:T(8,128)(2,1)}, bf16[8,16,896]{2,1,0:T(8,128)(2,1)S(1)}, u32[]{:S(2)}, u32[]{:S(2)}) collective-permute-start(bf16[8,16,896]{2,1,0:T(8,128)(2,1)} %get-tuple-element.31), channel_id=1, source_target_pairs={{0,15},{1,0},{2,1},{3,2},{4,3},{5,4},{6,5},{7,6},{8,7},{9,8},{10,9... | collective-permute-start | bytes 688136 | tf_op jit(solution)/shard_map/ppermute | solution.py:91
  8.1 11.0 %collective-permute-start = (bf16[16,16,896]{2,1,0:T(8,128)(2,1)S(1)}, bf16[16,16,896]{2,1,0:T(8,128)(2,1)S(1)}, u32[]{:S(2)}, u32[]{:S(2)}) collective-permute-start(bf16[16,16,896]{2,1,0:T(8,128)(2,1)S(1)} %get-tuple-element.30), channel_id=1, source_target_pairs={{0,16},{1,17},{2,18},{3,19},{4,20},{5,21},{6,22},{7,23},{8,24},{9,... | collective-permute-start | bytes 1376264 | tf_op jit(solution)/shard_map/ppermute | solution.py:91
  13.4 1.3 %copy-start.3 = (bf16[729,729]{1,0:T(8,128)(2,1)S(1)}, bf16[729,729]{1,0:T(8,128)(2,1)}, u32[]{:S(2)}) copy-start(bf16[729,729]{1,0:T(8,128)(2,1)} %matrix_ref.3) | copy-start | bytes 3188650
  14.7 4.4 %copy-start.4 = (f32[8,16,16]{2,1,0:T(8,128)S(1)}, f32[8,16,16]{2,1,0:T(8,128)}, u32[]{:S(2)}) copy-start(f32[8,16,16]{2,1,0:T(8,128)} %inv_hbm.1) | copy-start | bytes 24580
  14.7 4.7 %copy-start.5 = (f32[8,16,16]{2,1,0:T(8,128)S(1)}, f32[8,16,16]{2,1,0:T(8,128)}, u32[]{:S(2)}) copy-start(f32[8,16,16]{2,1,0:T(8,128)} %pot_hbm.1) | copy-start | bytes 24580
  18.5 1.3 %copy-start = (bf16[2,8,16,16,128]{4,3,2,1,0:T(8,128)(2,1)S(1)}, bf16[2,8,16,16,128]{4,3,2,1,0:T(8,128)(2,1)}, u32[]{:S(2)}) copy-start(bf16[2,8,16,16,128]{4,3,2,1,0:T(8,128)(2,1)} %vec.11) | copy-start | bytes 3145732
  18.5 4.2 %collective-permute-start.2 = (bf16[1,16,896]{2,1,0:T(8,128)(2,1)S(1)}, bf16[1,16,896]{2,1,0:T(8,128)(2,1)S(1)}, u32[]{:S(2)}, u32[]{:S(2)}) collective-permute-start(bf16[1,16,896]{2,1,0:T(8,128)(2,1)S(1)} %slice.4), channel_id=1, source_target_pairs={{0,16},{1,17},{2,18},{3,19},{4,20},{5,21},{6,22},{7,23},{8,24},{9,... | collective-permute-start | bytes 86024 | tf_op jit(solution)/shard_map/ppermute | solution.py:91
  23.6 8.6 %collective-permute-start.3 = (bf16[2,2,17,16,128]{4,3,2,1,0:T(8,128)(2,1)S(1)}, bf16[2,2,17,16,128]{4,3,2,1,0:T(8,128)(2,1)S(1)}, u32[]{:S(2)}, u32[]{:S(2)}) collective-permute-start(bf16[2,2,17,16,128]{4,3,2,1,0:T(8,128)(2,1)S(1)} %get-tuple-element.39), channel_id=1, source_target_pairs={{0,16},{1,17},{2,18},{3,19},{4,20},{5,21},{6,22},{7,23},{8,24},{9,... | collective-permute-start | bytes 835592 | tf_op jit(solution)/shard_map/ppermute | solution.py:91
  24.1 2.6 %collective-permute-start.4 = (bf16[2,9,16,128]{3,2,1,0:T(8,128)(2,1)S(1)}, bf16[2,9,16,128]{3,2,1,0:T(8,128)(2,1)S(1)}, u32[]{:S(2)}, u32[]{:S(2)}) collective-permute-start(bf16[2,9,16,128]{3,2,1,0:T(8,128)(2,1)S(1)} %get-tuple-element.40), channel_id=1, source_target_pairs={{0,1},{1,0},{2,3},{3,2},{4,5},{5,4},{6,7},{7,6},{8,9},{9,8},{10,11... | collective-permute-start | bytes 221192 | tf_op jit(solution)/shard_map/ppermute | solution.py:102
  24.1 6.5 %collective-permute-start.5 = (bf16[2,9,16,128]{3,2,1,0:T(8,128)(2,1)S(1)}, bf16[2,9,16,128]{3,2,1,0:T(8,128)(2,1)S(1)}, u32[]{:S(2)}, u32[]{:S(2)}) collective-permute-start(bf16[2,9,16,128]{3,2,1,0:T(8,128)(2,1)S(1)} %get-tuple-element.41), channel_id=1, source_target_pairs={{0,15},{1,2},{2,1},{3,4},{4,3},{5,6},{6,5},{7,8},{8,7},{9,10},{10,... | collective-permute-start | bytes 221192 | tf_op jit(solution)/shard_map/ppermute | solution.py:108
  30.6 3.9 %collective-permute-start.6 = (bf16[2,2,2,16,128]{4,3,2,1,0:T(8,128)(2,1)S(1)}, bf16[2,2,2,16,128]{4,3,2,1,0:T(8,128)(2,1)S(1)}, u32[]{:S(2)}, u32[]{:S(2)}) collective-permute-start(bf16[2,2,2,16,128]{4,3,2,1,0:T(8,128)(2,1)S(1)} %corner_pack.2), channel_id=1, source_target_pairs={{0,16},{1,17},{2,18},{3,19},{4,20},{5,21},{6,22},{7,23},{8,24},{9,... | collective-permute-start | bytes 98312 | tf_op jit(solution)/shard_map/ppermute | solution.py:91
  34.5 3.0 %copy-start.1 = (bf16[8,16,16,512]{3,2,1,0:T(8,128)(2,1)S(1)}, bf16[8,16,16,512]{3,2,1,0:T(8,128)(2,1)}, u32[]{:S(2)}) copy-start(bf16[8,16,16,512]{3,2,1,0:T(8,128)(2,1)} %res_hbm.1) | copy-start | bytes 6291460
  35.4 8.6 %collective-permute-start.7 = (bf16[2,2,17,16,128]{4,3,2,1,0:T(8,128)(2,1)S(1)}, bf16[2,2,17,16,128]{4,3,2,1,0:T(8,128)(2,1)S(1)}, u32[]{:S(2)}, u32[]{:S(2)}) collective-permute-start(bf16[2,2,17,16,128]{4,3,2,1,0:T(8,128)(2,1)S(1)} %get-tuple-element.44), channel_id=1, source_target_pairs={{0,16},{1,17},{2,18},{3,19},{4,20},{5,21},{6,22},{7,23},{8,24},{9,... | collective-permute-start | bytes 835592 | tf_op jit(solution)/shard_map/ppermute | solution.py:91
  37.0 1.3 %collective-permute-start.8 = (bf16[2,9,16,128]{3,2,1,0:T(8,128)(2,1)S(1)}, bf16[2,9,16,128]{3,2,1,0:T(8,128)(2,1)S(1)}, u32[]{:S(2)}, u32[]{:S(2)}) collective-permute-start(bf16[2,9,16,128]{3,2,1,0:T(8,128)(2,1)S(1)} %get-tuple-element.45), channel_id=1, source_target_pairs={{0,1},{1,0},{2,3},{3,2},{4,5},{5,4},{6,7},{7,6},{8,9},{9,8},{10,11... | collective-permute-start | bytes 221192 | tf_op jit(solution)/shard_map/ppermute | solution.py:102
  37.0 6.5 %collective-permute-start.9 = (bf16[2,9,16,128]{3,2,1,0:T(8,128)(2,1)S(1)}, bf16[2,9,16,128]{3,2,1,0:T(8,128)(2,1)S(1)}, u32[]{:S(2)}, u32[]{:S(2)}) collective-permute-start(bf16[2,9,16,128]{3,2,1,0:T(8,128)(2,1)S(1)} %get-tuple-element.46), channel_id=1, source_target_pairs={{0,15},{1,2},{2,1},{3,4},{4,3},{5,6},{6,5},{7,8},{8,7},{9,10},{10,... | collective-permute-start | bytes 221192 | tf_op jit(solution)/shard_map/ppermute | solution.py:108
  43.5 3.9 %collective-permute-start.10 = (bf16[2,2,2,16,128]{4,3,2,1,0:T(8,128)(2,1)S(1)}, bf16[2,2,2,16,128]{4,3,2,1,0:T(8,128)(2,1)S(1)}, u32[]{:S(2)}, u32[]{:S(2)}) collective-permute-start(bf16[2,2,2,16,128]{4,3,2,1,0:T(8,128)(2,1)S(1)} %corner_pack.3), channel_id=1, source_target_pairs={{0,16},{1,17},{2,18},{3,19},{4,20},{5,21},{6,22},{7,23},{8,24},{9,... | collective-permute-start | bytes 98312 | tf_op jit(solution)/shard_map/ppermute | solution.py:91
  50.7 14.0 %all-to-all-start = ((bf16[16,32,256]{2,1,0:T(8,128)(2,1)}), bf16[16,32,256]{2,1,0:T(8,128)(2,1)S(1)}, u32[]{:S(2)}, u32[]{:S(2)}) async-start(bf16[16,32,256]{2,1,0:T(8,128)(2,1)} %bitcast.5), calls=%async_computation | async-start | bytes 524288 | tf_op jit(solution)/shard_map/all_to_all | solution.py:695
  54.3 3.7 %collective-permute-start.11 = (bf16[2,16,128]{2,1,0:T(8,128)(2,1)S(1)}, bf16[2,16,128]{2,1,0:T(8,128)(2,1)S(1)}, u32[]{:S(2)}, u32[]{:S(2)}) collective-permute-start(bf16[2,16,128]{2,1,0:T(8,128)(2,1)S(1)} %get-tuple-element.53), channel_id=1, source_target_pairs={{0,16},{1,17},{2,18},{3,19},{4,20},{5,21},{6,22},{7,23},{8,24},{9,... | collective-permute-start | bytes 24584 | tf_op jit(solution)/shard_map/ppermute | solution.py:91
  58.0 7.3 %collective-permute-start.13 = (bf16[2,8,16,128]{3,2,1,0:T(8,128)(2,1)S(1)}, bf16[2,8,16,128]{3,2,1,0:T(8,128)(2,1)S(1)}, u32[]{:S(2)}, u32[]{:S(2)}) collective-permute-start(bf16[2,8,16,128]{3,2,1,0:T(8,128)(2,1)S(1)} %get-tuple-element.56), channel_id=1, source_target_pairs={{0,1},{1,2},{2,3},{3,4},{4,5},{5,6},{6,7},{7,8},{8,9},{9,10},{10,1... | collective-permute-start | bytes 196616 | tf_op jit(solution)/shard_map/ppermute | solution.py:91
  58.1 7.2 %collective-permute-start.12 = (bf16[2,16,16,128]{3,2,1,0:T(8,128)(2,1)S(1)}, bf16[2,16,16,128]{3,2,1,0:T(8,128)(2,1)S(1)}, u32[]{:S(2)}, u32[]{:S(2)}) collective-permute-start(bf16[2,16,16,128]{3,2,1,0:T(8,128)(2,1)S(1)} %get-tuple-element.55), channel_id=1, source_target_pairs={{0,16},{1,17},{2,18},{3,19},{4,20},{5,21},{6,22},{7,23},{8,24},{9,... | collective-permute-start | bytes 393224 | tf_op jit(solution)/shard_map/ppermute | solution.py:91
  64.8 4.0 %collective-permute-start.14 = (f32[32,256]{1,0:T(8,128)S(1)}, f32[32,256]{1,0:T(8,128)S(1)}, u32[]{:S(2)}, u32[]{:S(2)}) collective-permute-start(f32[32,256]{1,0:T(8,128)S(1)} %convert_reduce_fusion), channel_id=1, source_target_pairs={{0,16},{1,17},{2,18},{3,19},{4,20},{5,21},{6,22},{7,23},{8,24},{9,... | collective-permute-start | bytes 98312 | tf_op jit(solution)/shard_map/ppermute | solution.py:91
